TPU v7x, 32 devices: a whole 2x2x4 slice. The times are simulated.
32 devices in a mesh: tm: 8 (over z, x), space: 4 (over y, core).
Axes of the slice: x: 2, y: 2, z: 4, core: 2. Of those that a mesh axis runs over, the one named last changes fastest.
Arguments:
- snapshots: float32 [512, 16384], P('tm', 'space'), as said below
- space_factor: float32 [16384, 256], P('space'), as said below
Outputs:
- time_factor: float32 [512, 256], P('tm')
- loadings: float32 [256, 16384], P('tm', 'space')
Inputs may be any that keep to these rules, and one draw needn't show every extreme that they name: `snapshots`: entries are real values. `space_factor`: entries are real values; columns have norms between 0.05 and 1, the previous sweep's singular values.
All inputs are finite; a program needn't handle non-finite values.
Results may differ from a plain program's by a relative error of at most 0.0001.
Values sent between devices are 32-bit elements; how exact they have to be, the bound alone decides.
No kernel may reach another device: no remote copies, remote signals or barrier semaphores. Data moves between devices by JAX's collectives and lax.ppermute only.
A program may use at most 64 MiB of HBM per device.

v0:
```python
import math

import jax
import jax.numpy as jnp
from jax import lax
from jax.sharding import PartitionSpec as P

RANK = 256
NS = 2


def inner(left, right):
    return lax.dot_general(
        left,
        right,
        (((0,), (0,)), ((), ())),
        precision=lax.Precision.HIGHEST,
        preferred_element_type=jnp.float32,
    )


def matmul(left, right):
    return jnp.dot(left, right, precision=lax.Precision.HIGHEST, preferred_element_type=jnp.float32)


def polar_mixing(gram):
    identity_mat = jnp.eye(gram.shape[0], dtype=jnp.float32)
    mixing = identity_mat / jnp.sqrt(jnp.trace(gram))

    def advance(sweep, current):
        correlation = inner(current, matmul(gram, current))
        return matmul(current, 1.5 * identity_mat - 0.5 * correlation)

    return lax.fori_loop(0, NS, advance, mixing)


def on_device(snapshots, space_factor):
    projected = lax.psum(matmul(snapshots, space_factor), "space")
    devices = lax.axis_size("tm")
    block_rank = RANK // devices
    scaling = jnp.float32(math.sqrt(devices * snapshots.shape[0]))
    gram = lax.psum(inner(projected, projected), "tm")
    factor = matmul(projected, polar_mixing(gram))
    loadings = lax.psum_scatter(
        inner(lax.slice_in_dim(factor, 0, lax.axis_size("tm") * block_rank, axis=1), snapshots),
        "tm",
        scatter_dimension=0,
        tiled=True,
    )
    return (factor * scaling, loadings)


def solution(mesh):
    return jax.shard_map(
        on_device,
        mesh=mesh,
        in_specs=(P("tm", "space"), P("space", None)),
        out_specs=(P("tm", None), P("tm", "space")),
        check_vma=False,
    )
```

profile of v0, /device:TPU:8, one launch (start us, length us, event | category | flops | bytes accessed | tf_op | source)
XLA Modules:
  0.0 228.2 jit_solution(1609956039182763107)
XLA Ops:
  7.2 0.0 copy-start
  7.2 0.0 all-reduce.3.cloned.1.call-start
  7.2 1.2 copy-done
  8.4 5.1 %fusion.6 = f32[64,256]{1,0:T(8,128)} fusion(f32[64,4096]{1,0:T(8,128)S(1)} %copy-done, f32[4096,256]{1,0:T(8,128)} %param.5), kind=kOutput, calls=%fused_computation.11 | convolution fusion | flops 805306368 | bytes 5308416 | tf_op jit(solution)/shard_map/dot_general | solution.py:23
  13.5 0.0 all-reduce.3.cloned.1.call-update
  13.5 0.0 all-reduce.5.cloned.1.call-start
  13.5 32.3 %all-reduce.3.cloned.1.call-done = f32[64,256]{1,0:T(8,128)} async-done(((f32[64,256]{1,0:T(8,128)}), f32[64,256]{1,0:T(8,128)}) %all-reduce.3.cloned.1.call-update) | async-done | bytes 65552 | tf_op jit(solution)/shard_map/psum | solution.py:38
  45.8 2.0 fusion.7
  47.9 0.0 all-reduce.5.cloned.1.call-update
  47.9 0.0 reduce-scatter.2.cloned.1.call-start
  47.9 72.3 %all-reduce.5.cloned.1.call-done = f32[256,256]{1,0:T(8,128)} async-done(((f32[256,256]{1,0:T(8,128)}), f32[256,256]{1,0:T(8,128)}) %all-reduce.5.cloned.1.call-update) | async-done | bytes 262160 | tf_op jit(solution)/shard_map/psum | solution.py:42
  120.3 1.6 select_reduce_fusion
  122.6 0.1 copy.4
  122.7 0.0 copy-start.1
  122.7 4.8 %while.11 = (s32[]{:T(128)}, f32[256,256]{0,1:T(8,128)S(1)}, f32[256,256]{1,0:T(8,128)}, s32[]{:T(128)}) while((s32[]{:T(128)}, f32[256,256]{0,1:T(8,128)S(1)}, f32[256,256]{1,0:T(8,128)}, s32[]{:T(128)}) %tuple.27), condition=%wide.region_4.5_spmd.clone, body=%wide.region_3.4_spmd.clone.sunk | while | flops 604241920 | bytes 2883637 | solution.py:34
  122.8 1.4 fusion.37
  124.1 0.4 fusion.38
  124.5 0.6 convolution_bitcast_fusion.2
  125.2 1.4 fusion.37
  126.6 0.4 fusion.38
  127.0 0.6 convolution_bitcast_fusion.2
  127.6 0.0 copy-done.1
  127.6 1.0 broadcast_multiply_fusion
  128.6 5.0 %fusion.8 = f32[256,4096]{1,0:T(8,128)} fusion(f32[64,256]{1,0:T(8,128)S(1)} %get-tuple-element.43, f32[64,4096]{1,0:T(8,128)S(1)} %copy-done), kind=kOutput, calls=%fused_computation.13 | convolution fusion | flops 805306368 | bytes 5308416 | tf_op jit(solution)/shard_map/dot_general | solution.py:13
  133.6 0.0 reduce-scatter.2.cloned.1.call-update
  133.6 88.0 %reduce-scatter.2.cloned.1.call-done = f32[32,4096]{1,0:T(8,128)} async-done(((f32[256,4096]{1,0:T(8,128)}), f32[32,4096]{1,0:T(8,128)}) %reduce-scatter.2.cloned.1.call-update) | async-done | bytes 524304 | tf_op jit(solution)/shard_map/reduce_scatter | solution.py:44
  (3 shorter events, 0.1 us)
Async XLA Ops:
  7.2 1.2 copy-start
  7.2 38.7 %all-reduce.3.cloned.1.call-start = ((), (), s32[]{:S(2)}) async-start(), calls=%async_computation.1 | async-start | bytes 131072 | tf_op jit(solution)/shard_map/psum | solution.py:38
  13.5 106.8 %all-reduce.5.cloned.1.call-start = ((), (), s32[]{:S(2)}) async-start(), calls=%async_computation.2 | async-start | bytes 524288 | tf_op jit(solution)/shard_map/psum | solution.py:42
  47.9 173.7 %reduce-scatter.2.cloned.1.call-start = ((), (), s32[]{:S(2)}) async-start(), calls=%async_computation.3 | async-start | bytes 4718592 | tf_op jit(solution)/shard_map/reduce_scatter | solution.py:44
  122.7 4.8 %copy-start.1 = (f32[64,256]{1,0:T(8,128)S(1)}, f32[64,256]{1,0:T(8,128)}, u32[]{:S(2)}) copy-start(f32[64,256]{1,0:T(8,128)} %all-reduce.3.cloned.1.call-done) | copy-start | bytes 196612
Sparse Core Ops, SparseCore 0:
  13.6 32.1 all-reduce.2
  50.1 70.1 all-reduce.4
  133.8 87.8 reduce-scatter.1
where the time goes:
time: 230 us; the launch traced here: 228 us
  waiting for transfers between devices  193 us (84%)
  matrix products  17.8 us (8%)
  between operations  14.5 us (6%)
    reduce_scatter x1, waiting for transfers between devices, on_device(): lax.psum_scatter(inner(lax.slice_in_dim(factor, 0, lax.axis_size('tm') *...  88 us
    psum x1, waiting for transfers between devices, on_device(): gram = lax.psum(inner(projected, projected), 'tm')  72.3 us
    psum x1, waiting for transfers between devices, on_device(): projected = lax.psum(matmul(snapshots, space_factor), 'space')  32.3 us
    dot_general x6, matrix products, matmul(): jnp.dot(left, right, precision=lax.Precision.HIGHEST, preferred_element_t...  9.98 us
    dot_general x4, matrix products, inner(): lax.dot_general(left, right, (((0,), (0,)), ((), ())), precision=lax.Prec...  7.83 us
  transfers between devices with their start and end apart: 3, of which 3 were waited for; matrix products, arithmetic and copies ran while one was open for 0% of the time, Pallas kernels for 0%

commit v1 on v0

v1 whole, which is shorter than its diff:
```python
import math

import jax
import jax.numpy as jnp
from jax import lax
from jax.sharding import PartitionSpec as P

NS = 2


def inner(left, right):
    return lax.dot_general(
        left,
        right,
        (((0,), (0,)), ((), ())),
        precision=lax.Precision.HIGH,
        preferred_element_type=jnp.float32,
    )


def matmul(left, right):
    return jnp.dot(left, right, precision=lax.Precision.HIGH, preferred_element_type=jnp.float32)


def polar_mixing(gram):
    identity_mat = jnp.eye(gram.shape[0], dtype=jnp.float32)
    total = jnp.trace(gram)
    correlation = gram / total
    mixing = None
    for sweep in range(NS):
        update = 1.5 * identity_mat - 0.5 * correlation
        mixing = update if mixing is None else matmul(mixing, update)
        if sweep < NS - 1:
            correlation = matmul(matmul(correlation, update), update)
    return mixing / jnp.sqrt(total)


def on_device(snapshots, space_factor):
    rows, points = snapshots.shape
    rank = space_factor.shape[1]
    times, spaces = lax.axis_size("tm"), lax.axis_size("space")
    scaling = jnp.float32(math.sqrt(times * rows))

    columns = lax.all_to_all(snapshots, "tm", split_axis=1, concat_axis=0, tiled=True)

    partial = matmul(snapshots, space_factor).reshape(spaces, rows // spaces, rank)
    piece = jnp.sum(lax.all_to_all(partial, "space", 0, 0, tiled=True), axis=0)
    copies = jnp.broadcast_to(piece, (times * spaces,) + piece.shape)
    projected = lax.all_to_all(copies, ("tm", "space"), 0, 0, tiled=True).reshape(times * rows, rank)

    factor = matmul(projected, polar_mixing(inner(projected, projected)))
    own = lax.dynamic_slice_in_dim(factor, lax.axis_index("tm") * rows, rows, axis=0)
    loadings = lax.all_to_all(inner(factor, columns), "tm", split_axis=0, concat_axis=1, tiled=True)
    return (own * scaling, loadings)


def solution(mesh):
    return jax.shard_map(
        on_device,
        mesh=mesh,
        in_specs=(P("tm", "space"), P("space", None)),
        out_specs=(P("tm", None), P("tm", "space")),
        check_vma=False,
    )
```

time: 230 us -> 84.5 us (0.37)
  the two profiles are of different devices: /device:TPU:8 before, /device:TPU:0 now
where the time goes in v1:
time: 84.5 us; the launch traced here: 84.1 us
  waiting for transfers between devices  49.2 us (58%)
  starting transfers between devices  12.1 us (14%)
  matrix products  9.73 us (12%)
  blocking collectives  8.16 us (10%)
  local copies, waits for them, and re-layouts  2.95 us (3%)
  between operations  1.41 us (2%)
    all_to_all x1, waiting for transfers between devices, on_device(): lax.all_to_all(snapshots, 'tm', split_axis=1, concat_axis=0, tiled=True)  20.7 us
    all_to_all x1, waiting for transfers between devices, on_device(): lax.all_to_all(copies, ('tm', 'space'), 0, 0, tiled=True)  14.5 us
    all_to_all x1, waiting for transfers between devices, on_device(): lax.all_to_all(inner(factor, columns), 'tm', split_axis=0, concat_axis=1,...  14 us
    all_to_all x1, blocking collectives, on_device(): piece = jnp.sum(lax.all_to_all(partial, 'space', 0, 0, tiled=True), axis=0)  8.16 us
    dot_general x5, matrix products, matmul(): jnp.dot(left, right, precision=lax.Precision.HIGH, preferred_element_type...  7.11 us
    all_to_all x1, starting transfers between devices, on_device(): lax.all_to_all(copies, ('tm', 'space'), 0, 0, tiled=True)  4.9 us
    all_to_all x1, starting transfers between devices, on_device(): lax.all_to_all(inner(factor, columns), 'tm', split_axis=0, concat_axis=1,...  3.62 us
    all_to_all x1, starting transfers between devices, on_device(): lax.all_to_all(snapshots, 'tm', split_axis=1, concat_axis=0, tiled=True)  3.56 us
  transfers between devices with their start and end apart: 3, of which 3 were waited for; matrix products, arithmetic and copies ran while one was open for 8% of the time, Pallas kernels for 0%

profile of v1, /device:TPU:0, one launch (start us, length us, event | category | flops | bytes accessed | tf_op | source)
XLA Modules:
  0.0 84.1 jit_solution(7319971083602294806)
XLA Ops:
  0.6 0.0 copy-start
  0.6 3.9 %fusion.20 = f32[64,256]{1,0:T(8,128)S(1)} fusion(f32[64,4096]{1,0:T(8,128)} %param.2, f32[4096,256]{1,0:T(8,128)} %param.3), kind=kOutput, calls=%fused_computation.29 | convolution fusion | flops 402653184 | bytes 5308416 | tf_op jit(solution)/shard_map/dot_general | solution.py:22
  4.5 8.2 %all_to_all.45 = f32[4,16,256]{2,1,0:T(8,128)S(1)} all-to-all(f32[4,16,256]{2,1,0:T(8,128)S(1)} %bitcast.35), channel_id=1, replica_groups=mesh['tm'=8,'space'=4] {'space'}, dimensions={0} | all-to-all | bytes 131072 | tf_op jit(solution)/shard_map/all_to_all | solution.py:47
  12.7 0.9 %broadcast_in_dim.5 = f32[32,16,256]{2,1,0:T(8,128)} broadcast(f32[16,256]{1,0:T(8,128)S(1)} %reduce_sum.19), dimensions={1,2} | broadcast | bytes 540672 | tf_op jit(solution)/shard_map/broadcast_in_dim | solution.py:48
  13.6 4.9 %all-to-all-start.1 = ((f32[32,16,256]{2,1,0:T(8,128)}), f32[32,16,256]{2,1,0:T(8,128)S(1)}, u32[]{:S(2)}, u32[]{:S(2)}) async-start(f32[32,16,256]{2,1,0:T(8,128)} %broadcast_in_dim.5), calls=%async_computation.1 | async-start | bytes 1048576 | tf_op jit(solution)/shard_map/all_to_all | solution.py:49
  18.5 0.0 copy-done
  18.5 1.1 %copy.20 = f32[8,8,8,512]{3,2,0,1:T(8,128)} copy(f32[8,8,8,512]{3,2,1,0:T(8,128)S(1)} %bitcast.29) | data formatting | bytes 2097152 | tf_op jit(solution)/shard_map/all_to_all | solution.py:44
  19.5 14.5 %all-to-all-done.1 = f32[32,16,256]{2,1,0:T(8,128)S(1)} async-done(((f32[32,16,256]{2,1,0:T(8,128)}), f32[32,16,256]{2,1,0:T(8,128)S(1)}, u32[]{:S(2)}, u32[]{:S(2)}) %all-to-all-start.1) | async-done | bytes 524320 | tf_op jit(solution)/shard_map/all_to_all | solution.py:49
  34.0 3.6 %all-to-all-start.2 = ((f32[64,8,512]{2,0,1:T(8,128)}), f32[64,8,512]{2,0,1:T(8,128)S(1)}, u32[]{:S(2)}, u32[]{:S(2)}) async-start(f32[64,8,512]{2,0,1:T(8,128)} %bitcast.27), calls=%async_computation.2 | async-start | bytes 2097152 | tf_op jit(solution)/shard_map/all_to_all | solution.py:44
  37.6 1.2 %select_reduce_fusion = (f32[]{:T(128)}, f32[256,256]{1,0:T(8,128)S(1)}) fusion(f32[32,16,256]{2,1,0:T(8,128)S(1)} %all-to-all-done.1), kind=kOutput, calls=%fused_computation.7 | convolution fusion | flops 201523200 | bytes 786436 | tf_op jit(solution)/shard_map/dot_general | solution.py:12
  39.5 0.9 %fusion.1 = f32[256,256]{1,0:T(8,128)S(1)} fusion(f32[256,256]{1,0:T(8,128)S(1)} %get-tuple-element.3, f32[]{:T(128)} %get-tuple-element.2), kind=kOutput, calls=%fused_computation.6 | convolution fusion | flops 101056512 | bytes 524292 | tf_op jit(solution)/shard_map/dot_general | solution.py:22
  40.4 1.0 %fusion = f32[256,256]{1,0:T(8,128)S(1)} fusion(f32[256,256]{1,0:T(8,128)S(1)} %fusion.1, f32[256,256]{1,0:T(8,128)S(1)} %get-tuple-element.3, f32[]{:T(128)} %get-tuple-element.2), kind=kOutput, calls=%fused_computation.2 | convolution fusion | flops 101253120 | bytes 786436 | tf_op jit(solution)/shard_map/dot_general | solution.py:22
  41.4 0.9 %convolution_divide_fusion = f32[256,256]{1,0:T(8,128)S(1)} fusion(f32[256,256]{1,0:T(8,128)S(1)} %fusion, f32[]{:T(128)S(6)} %sqrt.3, f32[256,256]{1,0:T(8,128)S(1)} %get-tuple-element.3, f32[]{:T(128)} %get-tuple-element.2), kind=kOutput, calls=%fused_computation | convolution fusion | flops 101056512 | bytes 786440 | tf_op jit(solution)/shard_map/dot_general | solution.py:22
  42.3 0.4 fusion.21
  42.7 0.2 copy.12
  42.9 20.7 %all-to-all-done.2 = f32[64,8,512]{2,0,1:T(8,128)S(1)} async-done(((f32[64,8,512]{2,0,1:T(8,128)}), f32[64,8,512]{2,0,1:T(8,128)S(1)}, u32[]{:S(2)}, u32[]{:S(2)}) %all-to-all-start.2) | async-done | bytes 1048608 | tf_op jit(solution)/shard_map/all_to_all | solution.py:44
  63.6 1.4 %fusion.22 = f32[8,32,512]{2,1,0:T(8,128)} fusion(f32[8,32,512]{2,1,0:T(8,128)S(1)} %bitcast.33, f32[512,512,1]{1,0,2:T(8,128)S(1)} %bitcast.28), kind=kOutput, calls=%fused_computation.31 | convolution fusion | flops 402653184 | bytes 2097152 | tf_op jit(solution)/shard_map/dot_general | solution.py:12
  65.0 3.6 %all-to-all-start.3 = ((f32[8,32,512]{2,1,0:T(8,128)}), f32[8,32,512]{2,1,0:T(8,128)S(1)}, u32[]{:S(2)}, u32[]{:S(2)}) async-start(f32[8,32,512]{2,1,0:T(8,128)} %fusion.22), calls=%async_computation.3 | async-start | bytes 1048576 | tf_op jit(solution)/shard_map/all_to_all | solution.py:53
  68.6 0.6 dynamic-slice_multiply_fusion
  69.3 14.0 %all-to-all-done.3 = f32[8,32,512]{2,1,0:T(8,128)S(1)} async-done(((f32[8,32,512]{2,1,0:T(8,128)}), f32[8,32,512]{2,1,0:T(8,128)S(1)}, u32[]{:S(2)}, u32[]{:S(2)}) %all-to-all-start.3) | async-done | bytes 524320 | tf_op jit(solution)/shard_map/all_to_all | solution.py:53
  83.3 0.8 copy.18
  (1 shorter events, 0.0 us)
Async XLA Ops:
  0.6 17.8 %copy-start = (f32[64,4096]{1,0:T(8,128)S(1)}, f32[64,4096]{1,0:T(8,128)}, u32[]{:S(2)}) copy-start(f32[64,4096]{1,0:T(8,128)} %param.2) | copy-start | bytes 3145732
  13.6 20.5 %all-to-all-start.1 = ((f32[32,16,256]{2,1,0:T(8,128)}), f32[32,16,256]{2,1,0:T(8,128)S(1)}, u32[]{:S(2)}, u32[]{:S(2)}) async-start(f32[32,16,256]{2,1,0:T(8,128)} %broadcast_in_dim.5), calls=%async_computation.1 | async-start | bytes 1048576 | tf_op jit(solution)/shard_map/all_to_all | solution.py:49
  34.0 29.6 %all-to-all-start.2 = ((f32[64,8,512]{2,0,1:T(8,128)}), f32[64,8,512]{2,0,1:T(8,128)S(1)}, u32[]{:S(2)}, u32[]{:S(2)}) async-start(f32[64,8,512]{2,0,1:T(8,128)} %bitcast.27), calls=%async_computation.2 | async-start | bytes 2097152 | tf_op jit(solution)/shard_map/all_to_all | solution.py:44
  65.0 18.3 %all-to-all-start.3 = ((f32[8,32,512]{2,1,0:T(8,128)}), f32[8,32,512]{2,1,0:T(8,128)S(1)}, u32[]{:S(2)}, u32[]{:S(2)}) async-start(f32[8,32,512]{2,1,0:T(8,128)} %fusion.22), calls=%async_computation.3 | async-start | bytes 1048576 | tf_op jit(solution)/shard_map/all_to_all | solution.py:53

commit v2 on v1

--- a/solution.py
+++ b/solution.py
@@ -35,19 +35,39 @@
     return mixing / jnp.sqrt(total)
 
 
+def swap(value, axis, offset):
+    return lax.ppermute(value, axis, [(i, i ^ offset) for i in range(lax.axis_size(axis))])
+
+
+def gather_projected(partial):
+    rows, rank = partial.shape
+    times, spaces = lax.axis_size("tm"), lax.axis_size("space")
+    core = lax.axis_index("space") % 2
+    half = rows // 2
+    halves = partial.reshape(2, half, rank)
+    mine = lax.dynamic_index_in_dim(halves, core, 0, keepdims=False)
+    other = lax.dynamic_index_in_dim(halves, 1 - core, 0, keepdims=False)
+
+    terms = [mine] + [swap(other if k % 2 else mine, "space", k) for k in range(1, spaces)]
+    while len(terms) > 1:
+        terms = [a + b for a, b in zip(terms[::2], terms[1::2])]
+    piece = terms[0]
+
+    pieces = jnp.stack([piece] + [swap(piece, "tm", k) for k in range(1, times)])
+    pieces = pieces[lax.axis_index("tm") ^ jnp.arange(times)]
+    theirs = swap(pieces, "space", 1)
+    low, high = jnp.where(core == 0, pieces, theirs), jnp.where(core == 0, theirs, pieces)
+    return jnp.concatenate([low, high], axis=1).reshape(times * rows, rank)
+
+
 def on_device(snapshots, space_factor):
     rows, points = snapshots.shape
-    rank = space_factor.shape[1]
-    times, spaces = lax.axis_size("tm"), lax.axis_size("space")
+    times = lax.axis_size("tm")
     scaling = jnp.float32(math.sqrt(times * rows))
 
     columns = lax.all_to_all(snapshots, "tm", split_axis=1, concat_axis=0, tiled=True)
 
-    partial = matmul(snapshots, space_factor).reshape(spaces, rows // spaces, rank)
-    piece = jnp.sum(lax.all_to_all(partial, "space", 0, 0, tiled=True), axis=0)
-    copies = jnp.broadcast_to(piece, (times * spaces,) + piece.shape)
-    projected = lax.all_to_all(copies, ("tm", "space"), 0, 0, tiled=True).reshape(times * rows, rank)
-
+    projected = gather_projected(matmul(snapshots, space_factor))
     factor = matmul(projected, polar_mixing(inner(projected, projected)))
     own = lax.dynamic_slice_in_dim(factor, lax.axis_index("tm") * rows, rows, axis=0)
     loadings = lax.all_to_all(inner(factor, columns), "tm", split_axis=0, concat_axis=1, tiled=True)

time: 84.5 us -> 75.3 us (0.89)
  waiting for transfers between devices: 49.2 us -> 31.2 us
  starting transfers between devices: 12.1 us -> 29.1 us
  blocking collectives: 8.16 us -> 0 us
    all_to_all x1, waiting for transfers between devices: 20.7 us -> 0.01 us  [on_device(): lax.all_to_all(snapshots, 'tm', split_axis=1, concat_axis=0, tiled=True)]
    ppermute x0 -> x11, starting transfers between devices: none -> 19.3 us  [swap(): lax.ppermute(value, axis, [(i, i ^ offset) for i in range(lax.axis_size(a...]
    ppermute x0 -> x11, waiting for transfers between devices: none -> 16.8 us  [swap(): lax.ppermute(value, axis, [(i, i ^ offset) for i in range(lax.axis_size(a...]
    all_to_all x1 -> x0, waiting for transfers between devices: 14.5 us -> none  [on_device(): lax.all_to_all(copies, ('tm', 'space'), 0, 0, tiled=True)]
    all_to_all x1 -> x0, blocking collectives: 8.16 us -> none  [on_device(): piece = jnp.sum(lax.all_to_all(partial, 'space', 0, 0, tiled=True), axis=0)]
    all_to_all x1 -> x0, starting transfers between devices: 4.9 us -> none  [on_device(): lax.all_to_all(copies, ('tm', 'space'), 0, 0, tiled=True)]
    all_to_all x1, starting transfers between devices: 3.56 us -> 6.28 us  [on_device(): lax.all_to_all(snapshots, 'tm', split_axis=1, concat_axis=0, tiled=True)]
    broadcast_in_dim x1 -> x0, local copies, waits for them, and re-layouts: 0.85 us -> none  [on_device(): copies = jnp.broadcast_to(piece, (times * spaces,) + piece.shape)]
  transfers between devices with their start and end apart: 3 -> 13, of which waited for: 3 -> 5; matrix products, arithmetic and copies ran while one was open for 8% -> 9% of each run, Pallas kernels for 0% -> 0%
where the time goes in v2:
time: 75.3 us; the launch traced here: 75 us
  waiting for transfers between devices  31.2 us (41%)
  starting transfers between devices  29.1 us (39%)
  matrix products  9.73 us (13%)
  local copies, waits for them, and re-layouts  2.72 us (4%)
  between operations  1.54 us (2%)
    ppermute x11, starting transfers between devices, swap(): lax.ppermute(value, axis, [(i, i ^ offset) for i in range(lax.axis_size(a...  19.3 us
    ppermute x11, waiting for transfers between devices, swap(): lax.ppermute(value, axis, [(i, i ^ offset) for i in range(lax.axis_size(a...  16.8 us
    all_to_all x1, waiting for transfers between devices, on_device(): lax.all_to_all(inner(factor, columns), 'tm', split_axis=0, concat_axis=1,...  14.3 us
    dot_general x5, matrix products, matmul(): jnp.dot(left, right, precision=lax.Precision.HIGH, preferred_element_type...  7.11 us
    all_to_all x1, starting transfers between devices, on_device(): lax.all_to_all(snapshots, 'tm', split_axis=1, concat_axis=0, tiled=True)  6.28 us
    all_to_all x1, starting transfers between devices, on_device(): lax.all_to_all(inner(factor, columns), 'tm', split_axis=0, concat_axis=1,...  3.49 us
    dot_general x2, matrix products, inner(): lax.dot_general(left, right, (((0,), (0,)), ((), ())), precision=lax.Prec...  2.62 us
  transfers between devices with their start and end apart: 13, of which 5 were waited for; matrix products, arithmetic and copies ran while one was open for 9% of the time, Pallas kernels for 0%

profile of v2, /device:TPU:0, one launch (start us, length us, event | category | flops | bytes accessed | tf_op | source)
XLA Modules:
  0.0 75.0 jit_solution(15008943504958443668)
XLA Ops:
  0.6 0.0 copy-start
  0.7 3.9 %fusion.21 = f32[64,256]{1,0:T(8,128)S(1)} fusion(f32[64,4096]{1,0:T(8,128)} %param.2, f32[4096,256]{1,0:T(8,128)} %param.3), kind=kOutput, calls=%fused_computation.47 | convolution fusion | flops 402653184 | bytes 5308416 | tf_op jit(solution)/shard_map/dot_general | solution.py:22
  4.6 2.5 %collective-permute-start.2 = (f32[32,256]{1,0:T(8,128)S(1)}, f32[32,256]{1,0:T(8,128)S(1)}, u32[]{:S(2)}, u32[]{:S(2)}) collective-permute-start(f32[32,256]{1,0:T(8,128)S(1)} %get-tuple-element.6), channel_id=1, source_target_pairs={{0,3},{1,2},{2,1},{3,0},{4,7},{5,6},{6,5},{7,4},{8,11},{9,10},{10,... | collective-permute-start | bytes 98312 | tf_op jit(solution)/shard_map/ppermute | solution.py:39
  7.1 0.7 collective-permute-start
  7.7 0.0 collective-permute-start.1
  7.8 0.0 copy-done
  7.8 1.1 %copy.12 = f32[8,8,8,512]{3,2,0,1:T(8,128)} copy(f32[8,8,8,512]{3,2,1,0:T(8,128)S(1)} %bitcast.49) | data formatting | bytes 2097152 | tf_op jit(solution)/shard_map/all_to_all | solution.py:68
  8.9 6.3 %all-to-all-start = ((f32[64,8,512]{2,0,1:T(8,128)}), f32[64,8,512]{2,0,1:T(8,128)S(1)}, u32[]{:S(2)}, u32[]{:S(2)}) async-start(f32[64,8,512]{2,0,1:T(8,128)} %bitcast.47), calls=%async_computation | async-start | bytes 2097152 | tf_op jit(solution)/shard_map/all_to_all | solution.py:68
  15.1 0.0 collective-permute-done.2
  15.1 0.0 collective-permute-done
  15.2 0.0 collective-permute-done.1
  15.2 2.1 %collective-permute-start.3 = (f32[32,256]{1,0:T(8,128)S(1)}, f32[32,256]{1,0:T(8,128)S(1)}, u32[]{:S(2)}, u32[]{:S(2)}) collective-permute-start(f32[32,256]{1,0:T(8,128)S(1)} %get-tuple-element.3), channel_id=1, source_target_pairs={{0,4},{4,0},{8,12},{12,8},{16,20},{20,16},{24,28},{28,24},{1,5},{5... | collective-permute-start | bytes 98312 | tf_op jit(solution)/shard_map/ppermute | solution.py:39
  17.3 3.3 %collective-permute-start.8 = (f32[32,256]{1,0:T(8,128)S(1)}, f32[32,256]{1,0:T(8,128)S(1)}, u32[]{:S(2)}, u32[]{:S(2)}) collective-permute-start(f32[32,256]{1,0:T(8,128)S(1)} %get-tuple-element.3), channel_id=1, source_target_pairs={{0,24},{4,28},{8,16},{12,20},{16,8},{20,12},{24,0},{28,4},{1,25},{... | collective-permute-start | bytes 98312 | tf_op jit(solution)/shard_map/ppermute | solution.py:39
  20.5 0.0 collective-permute-start.7
  20.5 2.9 %collective-permute-start.6 = (f32[32,256]{1,0:T(8,128)S(1)}, f32[32,256]{1,0:T(8,128)S(1)}, u32[]{:S(2)}, u32[]{:S(2)}) collective-permute-start(f32[32,256]{1,0:T(8,128)S(1)} %get-tuple-element.3), channel_id=1, source_target_pairs={{0,16},{4,20},{8,24},{12,28},{16,0},{20,4},{24,8},{28,12},{1,17},{... | collective-permute-start | bytes 98312 | tf_op jit(solution)/shard_map/ppermute | solution.py:39
  23.5 0.6 collective-permute-start.5
  24.0 0.0 collective-permute-done.3
  24.0 2.4 %collective-permute-start.4 = (f32[32,256]{1,0:T(8,128)S(1)}, f32[32,256]{1,0:T(8,128)S(1)}, u32[]{:S(2)}, u32[]{:S(2)}) collective-permute-start(f32[32,256]{1,0:T(8,128)S(1)} %get-tuple-element.3), channel_id=1, source_target_pairs={{0,8},{4,12},{8,0},{12,4},{16,24},{20,28},{24,16},{28,20},{1,9},{5... | collective-permute-start | bytes 98312 | tf_op jit(solution)/shard_map/ppermute | solution.py:39
  26.4 9.1 %collective-permute-done.4 = f32[32,256]{1,0:T(8,128)S(1)} collective-permute-done((f32[32,256]{1,0:T(8,128)S(1)}, f32[32,256]{1,0:T(8,128)S(1)}, u32[]{:S(2)}, u32[]{:S(2)}) %collective-permute-start.4) | collective-permute-done | bytes 32800 | tf_op jit(solution)/shard_map/ppermute | solution.py:39
  35.5 4.8 %collective-permute-start.9 = (f32[32,256]{1,0:T(8,128)S(1)}, f32[32,256]{1,0:T(8,128)S(1)}, u32[]{:S(2)}, u32[]{:S(2)}) collective-permute-start(f32[32,256]{1,0:T(8,128)S(1)} %get-tuple-element.3), channel_id=1, source_target_pairs={{0,28},{4,24},{8,20},{12,16},{16,12},{20,8},{24,4},{28,0},{1,29},{... | collective-permute-start | bytes 98312 | tf_op jit(solution)/shard_map/ppermute | solution.py:39
  40.4 0.0 collective-permute-done.5
  40.4 5.7 %collective-permute-done.6 = f32[32,256]{1,0:T(8,128)S(1)} collective-permute-done((f32[32,256]{1,0:T(8,128)S(1)}, f32[32,256]{1,0:T(8,128)S(1)}, u32[]{:S(2)}, u32[]{:S(2)}) %collective-permute-start.6) | collective-permute-done | bytes 32800 | tf_op jit(solution)/shard_map/ppermute | solution.py:39
  46.1 0.4 collective-permute-done.7
  46.6 0.0 collective-permute-done.8
  46.6 0.0 collective-permute-done.9
  46.6 0.6 gather_fusion
  47.2 0.1 collective-permute-start.10
  47.3 1.5 %collective-permute-done.10 = f32[8,32,256]{2,1,0:T(8,128)S(1)} collective-permute-done((f32[8,32,256]{2,1,0:T(8,128)S(1)}, f32[8,32,256]{2,1,0:T(8,128)S(1)}, u32[]{:S(2)}, u32[]{:S(2)}) %collective-permute-start.10) | collective-permute-done | bytes 262176 | tf_op jit(solution)/shard_map/ppermute | solution.py:39
  48.8 1.2 %select_reduce_fusion = (f32[]{:T(128)}, f32[256,256]{1,0:T(8,128)S(1)}) fusion(f32[8,32,256]{2,1,0:T(8,128)S(1)} %get-tuple-element.5, f32[8,32,256]{2,1,0:T(8,128)S(1)} %get-tuple-element.4), kind=kOutput, calls=%fused_computation.9 | convolution fusion | flops 201654272 | bytes 786436 | tf_op jit(solution)/shard_map/dot_general | solution.py:12
  50.8 0.9 %fusion.1 = f32[256,256]{1,0:T(8,128)S(1)} fusion(f32[256,256]{1,0:T(8,128)S(1)} %get-tuple-element.9, f32[]{:T(128)} %get-tuple-element.8), kind=kOutput, calls=%fused_computation.8 | convolution fusion | flops 101056512 | bytes 524292 | tf_op jit(solution)/shard_map/dot_general | solution.py:22
  51.7 1.0 %fusion = f32[256,256]{1,0:T(8,128)S(1)} fusion(f32[256,256]{1,0:T(8,128)S(1)} %fusion.1, f32[256,256]{1,0:T(8,128)S(1)} %get-tuple-element.9, f32[]{:T(128)} %get-tuple-element.8), kind=kOutput, calls=%fused_computation.3 | convolution fusion | flops 101253120 | bytes 786436 | tf_op jit(solution)/shard_map/dot_general | solution.py:22
  52.7 0.9 %convolution_divide_fusion = f32[256,256]{1,0:T(8,128)S(1)} fusion(f32[256,256]{1,0:T(8,128)S(1)} %fusion, f32[]{:T(128)S(6)} %sqrt.3, f32[256,256]{1,0:T(8,128)S(1)} %get-tuple-element.9, f32[]{:T(128)} %get-tuple-element.8), kind=kOutput, calls=%fused_computation.1 | convolution fusion | flops 101056512 | bytes 786440 | tf_op jit(solution)/shard_map/dot_general | solution.py:22
  53.6 0.4 fusion.22
  54.0 0.2 copy.6
  54.2 0.0 all-to-all-done
  54.2 1.4 %fusion.23 = f32[8,32,512]{2,1,0:T(8,128)} fusion(f32[8,32,512]{2,1,0:T(8,128)S(1)} %bitcast.53, f32[512,512,1]{1,0,2:T(8,128)S(1)} %bitcast.48), kind=kOutput, calls=%fused_computation.49 | convolution fusion | flops 402653184 | bytes 2097152 | tf_op jit(solution)/shard_map/dot_general | solution.py:12
  55.6 3.5 %all-to-all-start.1 = ((f32[8,32,512]{2,1,0:T(8,128)}), f32[8,32,512]{2,1,0:T(8,128)S(1)}, u32[]{:S(2)}, u32[]{:S(2)}) async-start(f32[8,32,512]{2,1,0:T(8,128)} %fusion.23), calls=%async_computation.1 | async-start | bytes 1048576 | tf_op jit(solution)/shard_map/all_to_all | solution.py:73
  59.1 0.6 dynamic-slice_multiply_fusion
  59.8 14.3 %all-to-all-done.1 = f32[8,32,512]{2,1,0:T(8,128)S(1)} async-done(((f32[8,32,512]{2,1,0:T(8,128)}), f32[8,32,512]{2,1,0:T(8,128)S(1)}, u32[]{:S(2)}, u32[]{:S(2)}) %all-to-all-start.1) | async-done | bytes 524320 | tf_op jit(solution)/shard_map/all_to_all | solution.py:73
  74.1 0.8 %copy.10 = f32[8,4,8,512]{3,2,0,1:T(8,128)} copy(f32[8,4,8,512]{3,2,1,0:T(8,128)S(1)} %bitcast.51) | data formatting | bytes 1048576 | tf_op jit(solution)/shard_map/all_to_all | solution.py:73
  (13 shorter events, 0.1 us)
Async XLA Ops:
  0.6 7.1 %copy-start = (f32[64,4096]{1,0:T(8,128)S(1)}, f32[64,4096]{1,0:T(8,128)}, u32[]{:S(2)}) copy-start(f32[64,4096]{1,0:T(8,128)} %param.2) | copy-start | bytes 3145732
  4.6 10.6 %collective-permute-start.2 = (f32[32,256]{1,0:T(8,128)S(1)}, f32[32,256]{1,0:T(8,128)S(1)}, u32[]{:S(2)}, u32[]{:S(2)}) collective-permute-start(f32[32,256]{1,0:T(8,128)S(1)} %get-tuple-element.6), channel_id=1, source_target_pairs={{0,3},{1,2},{2,1},{3,0},{4,7},{5,6},{6,5},{7,4},{8,11},{9,10},{10,... | collective-permute-start | bytes 98312 | tf_op jit(solution)/shard_map/ppermute | solution.py:39
  7.1 8.1 %collective-permute-start = (f32[32,256]{1,0:T(8,128)S(1)}, f32[32,256]{1,0:T(8,128)S(1)}, u32[]{:S(2)}, u32[]{:S(2)}) collective-permute-start(f32[32,256]{1,0:T(8,128)S(1)} %get-tuple-element.6), channel_id=1, source_target_pairs={{0,1},{1,0},{2,3},{3,2},{4,5},{5,4},{6,7},{7,6},{8,9},{9,8},{10,11... | collective-permute-start | bytes 98312 | tf_op jit(solution)/shard_map/ppermute | solution.py:39
  7.7 7.4 %collective-permute-start.1 = (f32[32,256]{1,0:T(8,128)S(1)}, f32[32,256]{1,0:T(8,128)S(1)}, u32[]{:S(2)}, u32[]{:S(2)}) collective-permute-start(f32[32,256]{1,0:T(8,128)S(1)} %get-tuple-element.7), channel_id=1, source_target_pairs={{0,2},{1,3},{2,0},{3,1},{4,6},{5,7},{6,4},{7,5},{8,10},{9,11},{10,... | collective-permute-start | bytes 98312 | tf_op jit(solution)/shard_map/ppermute | solution.py:39
  8.9 45.4 %all-to-all-start = ((f32[64,8,512]{2,0,1:T(8,128)}), f32[64,8,512]{2,0,1:T(8,128)S(1)}, u32[]{:S(2)}, u32[]{:S(2)}) async-start(f32[64,8,512]{2,0,1:T(8,128)} %bitcast.47), calls=%async_computation | async-start | bytes 2097152 | tf_op jit(solution)/shard_map/all_to_all | solution.py:68
  15.2 8.8 %collective-permute-start.3 = (f32[32,256]{1,0:T(8,128)S(1)}, f32[32,256]{1,0:T(8,128)S(1)}, u32[]{:S(2)}, u32[]{:S(2)}) collective-permute-start(f32[32,256]{1,0:T(8,128)S(1)} %get-tuple-element.3), channel_id=1, source_target_pairs={{0,4},{4,0},{8,12},{12,8},{16,20},{20,16},{24,28},{28,24},{1,5},{5... | collective-permute-start | bytes 98312 | tf_op jit(solution)/shard_map/ppermute | solution.py:39
  17.3 29.3 %collective-permute-start.8 = (f32[32,256]{1,0:T(8,128)S(1)}, f32[32,256]{1,0:T(8,128)S(1)}, u32[]{:S(2)}, u32[]{:S(2)}) collective-permute-start(f32[32,256]{1,0:T(8,128)S(1)} %get-tuple-element.3), channel_id=1, source_target_pairs={{0,24},{4,28},{8,16},{12,20},{16,8},{20,12},{24,0},{28,4},{1,25},{... | collective-permute-start | bytes 98312 | tf_op jit(solution)/shard_map/ppermute | solution.py:39
  20.5 26.0 %collective-permute-start.7 = (f32[32,256]{1,0:T(8,128)S(1)}, f32[32,256]{1,0:T(8,128)S(1)}, u32[]{:S(2)}, u32[]{:S(2)}) collective-permute-start(f32[32,256]{1,0:T(8,128)S(1)} %get-tuple-element.3), channel_id=1, source_target_pairs={{0,20},{4,16},{8,28},{12,24},{16,4},{20,0},{24,12},{28,8},{1,21},{... | collective-permute-start | bytes 98312 | tf_op jit(solution)/shard_map/ppermute | solution.py:39
  20.5 25.6 %collective-permute-start.6 = (f32[32,256]{1,0:T(8,128)S(1)}, f32[32,256]{1,0:T(8,128)S(1)}, u32[]{:S(2)}, u32[]{:S(2)}) collective-permute-start(f32[32,256]{1,0:T(8,128)S(1)} %get-tuple-element.3), channel_id=1, source_target_pairs={{0,16},{4,20},{8,24},{12,28},{16,0},{20,4},{24,8},{28,12},{1,17},{... | collective-permute-start | bytes 98312 | tf_op jit(solution)/shard_map/ppermute | solution.py:39
  23.5 16.9 %collective-permute-start.5 = (f32[32,256]{1,0:T(8,128)S(1)}, f32[32,256]{1,0:T(8,128)S(1)}, u32[]{:S(2)}, u32[]{:S(2)}) collective-permute-start(f32[32,256]{1,0:T(8,128)S(1)} %get-tuple-element.3), channel_id=1, source_target_pairs={{0,12},{4,8},{8,4},{12,0},{16,28},{20,24},{24,20},{28,16},{1,13},{... | collective-permute-start | bytes 98312 | tf_op jit(solution)/shard_map/ppermute | solution.py:39
  24.0 11.5 %collective-permute-start.4 = (f32[32,256]{1,0:T(8,128)S(1)}, f32[32,256]{1,0:T(8,128)S(1)}, u32[]{:S(2)}, u32[]{:S(2)}) collective-permute-start(f32[32,256]{1,0:T(8,128)S(1)} %get-tuple-element.3), channel_id=1, source_target_pairs={{0,8},{4,12},{8,0},{12,4},{16,24},{20,28},{24,16},{28,20},{1,9},{5... | collective-permute-start | bytes 98312 | tf_op jit(solution)/shard_map/ppermute | solution.py:39
  35.5 11.0 %collective-permute-start.9 = (f32[32,256]{1,0:T(8,128)S(1)}, f32[32,256]{1,0:T(8,128)S(1)}, u32[]{:S(2)}, u32[]{:S(2)}) collective-permute-start(f32[32,256]{1,0:T(8,128)S(1)} %get-tuple-element.3), channel_id=1, source_target_pairs={{0,28},{4,24},{8,20},{12,16},{16,12},{20,8},{24,4},{28,0},{1,29},{... | collective-permute-start | bytes 98312 | tf_op jit(solution)/shard_map/ppermute | solution.py:39
  47.2 1.6 %collective-permute-start.10 = (f32[8,32,256]{2,1,0:T(8,128)S(1)}, f32[8,32,256]{2,1,0:T(8,128)S(1)}, u32[]{:S(2)}, u32[]{:S(2)}) collective-permute-start(f32[8,32,256]{2,1,0:T(8,128)S(1)} %gather_fusion), channel_id=1, source_target_pairs={{0,1},{1,0},{2,3},{3,2},{4,5},{5,4},{6,7},{7,6},{8,9},{9,8},{10,11... | collective-permute-start | bytes 786440 | tf_op jit(solution)/shard_map/ppermute | solution.py:39
  55.6 18.5 %all-to-all-start.1 = ((f32[8,32,512]{2,1,0:T(8,128)}), f32[8,32,512]{2,1,0:T(8,128)S(1)}, u32[]{:S(2)}, u32[]{:S(2)}) async-start(f32[8,32,512]{2,1,0:T(8,128)} %fusion.23), calls=%async_computation.1 | async-start | bytes 1048576 | tf_op jit(solution)/shard_map/all_to_all | solution.py:73

commit v3 on v2

v3 whole, which is shorter than its diff:
```python
import functools
import math

import jax
import jax.numpy as jnp
from jax import lax
from jax.experimental import pallas as pl
from jax.experimental.pallas import tpu as pltpu
from jax.sharding import PartitionSpec as P

VMEM_LIMIT = 48 * 1024 * 1024
ANY = pl.BlockSpec(memory_space=pl.ANY)
VMEM = pl.BlockSpec(memory_space=pltpu.VMEM)
PARAMS = pltpu.CompilerParams(vmem_limit_bytes=VMEM_LIMIT)
ROWS_BY_ROWS = (((0,), (0,)), ((), ()))
ROWS_BY_COLUMNS = (((1,), (0,)), ((), ()))


def split(value):
    high = value.astype(jnp.bfloat16)
    return high, (value - high.astype(jnp.float32)).astype(jnp.bfloat16)


def dot(left, right, dims=ROWS_BY_COLUMNS):
    return lax.dot_general(left, right, dims, preferred_element_type=jnp.float32)


def product(left, right, dims=ROWS_BY_COLUMNS):
    (left_high, left_low), (right_high, right_low) = left, right
    return dot(left_high, right_high, dims) + (
        dot(left_high, right_low, dims) + dot(left_low, right_high, dims)
    )


def project_kernel(snapshots_ref, factor_ref, partial_ref):
    rows = snapshots_ref.shape[0]
    high, low = split(snapshots_ref[...])
    factor_high, factor_low = split(factor_ref[...])
    both = dot(jnp.concatenate([high, low], axis=0), factor_high)
    term = both[:rows] + (both[rows:] + dot(high, factor_low))

    @pl.when(pl.program_id(0) == 0)
    def _():
        partial_ref[...] = term

    @pl.when(pl.program_id(0) != 0)
    def _():
        partial_ref[...] += term


def project(snapshots, space_factor):
    rows, points = snapshots.shape
    rank = space_factor.shape[1]
    depth = min(512, points)
    return pl.pallas_call(
        project_kernel,
        grid=(points // depth,),
        in_specs=[
            pl.BlockSpec((rows, depth), lambda i: (0, i)),
            pl.BlockSpec((depth, rank), lambda i: (i, 0)),
        ],
        out_specs=pl.BlockSpec((rows, rank), lambda i: (0, 0)),
        out_shape=jax.ShapeDtypeStruct((rows, rank), jnp.float32),
        compiler_params=PARAMS,
    )(snapshots, space_factor)


def cut_kernel(snapshots_ref, _, parts_ref, sems):
    parts, _, width = parts_ref.shape
    copies = [
        pltpu.make_async_copy(
            snapshots_ref.at[:, pl.ds(i * width, width)], parts_ref.at[i], sems.at[i]
        )
        for i in range(parts)
    ]
    for copy in copies:
        copy.start()
    for copy in copies:
        copy.wait()


def cut(snapshots, parts, after):
    rows, points = snapshots.shape
    if points // parts % 128:
        return snapshots.reshape(rows, parts, points // parts).transpose(1, 0, 2)
    return pl.pallas_call(
        cut_kernel,
        in_specs=[ANY, ANY],
        out_specs=ANY,
        out_shape=jax.ShapeDtypeStruct((parts, rows, points // parts), jnp.float32),
        scratch_shapes=[pltpu.SemaphoreType.DMA((parts,))],
        compiler_params=PARAMS,
    )(snapshots, after)


def mix_kernel(scaling, index_ref, low_ref, high_ref, high_t_ref, low_t_ref, own_ref):
    times, half, rank = low_ref.shape
    projected = jnp.concatenate([low_ref[...], high_ref[...]], axis=1).reshape(times * 2 * half, rank)
    high, low = split(projected)
    cross = dot(high, low, ROWS_BY_ROWS)
    gram = dot(high, high, ROWS_BY_ROWS) + (cross + cross.T)
    diagonal = lax.broadcasted_iota(jnp.int32, (rank, rank), 0) == lax.broadcasted_iota(
        jnp.int32, (rank, rank), 1
    )
    total = jnp.sum(projected * projected)
    correlation = gram / total
    correlation_split = split(correlation)
    square = product(correlation_split, correlation_split)
    tail = jnp.where(diagonal, 1.6875, 0.0) - 0.5625 * correlation + 0.0625 * square
    mixing = (jnp.where(diagonal, 2.25, 0.0) - 2.4375 * correlation) + product(split(square), split(tail))
    factor = product((high, low), split(mixing)) * lax.rsqrt(total)
    factor_high, factor_low = split(factor.T)
    high_t_ref[...] = factor_high
    low_t_ref[...] = factor_low
    rows = 2 * half
    own = jnp.zeros((rows, rank), jnp.float32)
    for i in range(times):
        own = jnp.where(index_ref[0] == i, factor[i * rows : (i + 1) * rows], own)
    own_ref[...] = own * scaling


def mix(index, low, high):
    times, half, rank = low.shape
    total = times * 2 * half
    return pl.pallas_call(
        functools.partial(mix_kernel, math.sqrt(total)),
        in_specs=[pl.BlockSpec(memory_space=pltpu.SMEM), VMEM, VMEM],
        out_specs=[VMEM] * 3,
        out_shape=[
            jax.ShapeDtypeStruct((rank, total), jnp.bfloat16),
            jax.ShapeDtypeStruct((rank, total), jnp.bfloat16),
            jax.ShapeDtypeStruct((2 * half, rank), jnp.float32),
        ],
        compiler_params=PARAMS,
    )(index, low, high)


def load_kernel(high_ref, low_ref, columns_ref, blocks_ref):
    value = product((high_ref[...], low_ref[...]), split(columns_ref[...]))
    blocks_ref[...] = value.reshape(blocks_ref.shape)


def load(high, low, columns, blocks):
    rank, _ = high.shape
    return pl.pallas_call(
        load_kernel,
        in_specs=[VMEM] * 3,
        out_specs=VMEM,
        out_shape=jax.ShapeDtypeStruct((blocks, rank // blocks, columns.shape[1]), jnp.float32),
        compiler_params=PARAMS,
    )(high, low, columns)


def swap(value, axis, offset):
    return lax.ppermute(value, axis, [(i, i ^ offset) for i in range(lax.axis_size(axis))])


def on_device(snapshots, space_factor):
    rows, points = snapshots.shape
    rank = space_factor.shape[1]
    times, spaces = lax.axis_size("tm"), lax.axis_size("space")
    index = lax.axis_index("tm")
    core = lax.axis_index("space") % 2

    halves = project(snapshots, space_factor).reshape(2, rows // 2, rank)
    mine = lax.dynamic_index_in_dim(halves, core, 0, keepdims=False)
    other = lax.dynamic_index_in_dim(halves, 1 - core, 0, keepdims=False)
    terms = [mine] + [swap(other if k % 2 else mine, "space", k) for k in range(1, spaces)]
    while len(terms) > 1:
        terms = [a + b for a, b in zip(terms[::2], terms[1::2])]
    piece = terms[0]

    received = [swap(piece, "tm", k) for k in range(1, times)]
    pieces = jnp.stack([piece] + received)[index ^ jnp.arange(times)]
    theirs = swap(pieces, "space", 1)
    low, high = jnp.where(core == 0, pieces, theirs), jnp.where(core == 0, theirs, pieces)

    columns = lax.all_to_all(cut(snapshots, times, received[0]), "tm", 0, 0, tiled=True)

    high_t, low_t, own = mix(index.reshape(1), low, high)
    blocks = load(high_t, low_t, columns.reshape(times * rows, points // times), times)
    loadings = lax.all_to_all(blocks, "tm", split_axis=0, concat_axis=0, tiled=True)
    return own, loadings.transpose(1, 0, 2).reshape(rank // times, points)


def solution(mesh):
    return jax.shard_map(
        on_device,
        mesh=mesh,
        in_specs=(P("tm", "space"), P("space", None)),
        out_specs=(P("tm", None), P("tm", "space")),
        check_vma=False,
    )
```

time: 75.3 us -> 77.2 us (1.025)
  blocking collectives: 0 us -> 21.8 us
  waiting for transfers between devices: 31.2 us -> 21 us
  matrix products: 9.73 us -> 0 us
  starting transfers between devices: 29.1 us -> 22.5 us
  Pallas kernels: 0 us -> 5.83 us
  local copies, waits for them, and re-layouts: 2.72 us -> 4.85 us
    all_to_all x0 -> x1, blocking collectives: none -> 21.8 us  [on_device(): lax.all_to_all(blocks, 'tm', split_axis=0, concat_axis=0, tiled=True)]
    all_to_all x2 -> x1, waiting for transfers between devices: 14.3 us -> 0.01 us  [on_device(): lax.all_to_all(cut(snapshots, times, received[0]), 'tm', 0, 0, tiled=True)]
    dot_general x7 -> x0, matrix products: 9.73 us -> none  [the longest x5 7.11 us: matmul(): jnp.dot(left, right, precision=lax.Precision.HIGH, preferred_element_type...]
    all_to_all x2 -> x1, starting transfers between devices: 9.77 us -> 3.57 us  [on_device(): lax.all_to_all(cut(snapshots, times, received[0]), 'tm', 0, 0, tiled=True)]
    pallas_call x0 -> x4, Pallas kernels: none -> 5.83 us  [the longest x1 2.11 us: project(): pl.pallas_call(project_kernel, grid=(points // depth,), in_specs=[pl.Bloc...]
    ppermute x11, waiting for transfers between devices: 16.8 us -> 21 us  [swap(): lax.ppermute(value, axis, [(i, i ^ offset) for i in range(lax.axis_size(a...]
    unnamed x8 -> x12, local copies, waits for them, and re-layouts: 0.03 us -> 3.44 us
    all_to_all x2 -> x0, local copies, waits for them, and re-layouts: 1.91 us -> none  [the longest x1 1.08 us: on_device(): lax.all_to_all(snapshots, 'tm', split_axis=1, concat_axis=0, tiled=True)]
  transfers between devices with their start and end apart: 13 -> 12, of which waited for: 5 -> 4; matrix products, arithmetic and copies ran while one was open for 9% -> 1% of each run, Pallas kernels for 0% -> 4%
where the time goes in v3:
time: 77.2 us; the launch traced here: 76.9 us
  starting transfers between devices  22.5 us (29%)
  blocking collectives  21.8 us (28%)
  waiting for transfers between devices  21 us (27%)
  Pallas kernels  5.83 us (8%)
  local copies, waits for them, and re-layouts  4.85 us (6%)
  between operations  0.81 us (1%)
    all_to_all x1, blocking collectives, on_device(): lax.all_to_all(blocks, 'tm', split_axis=0, concat_axis=0, tiled=True)  21.8 us
    ppermute x11, waiting for transfers between devices, swap(): lax.ppermute(value, axis, [(i, i ^ offset) for i in range(lax.axis_size(a...  21 us
    ppermute x11, starting transfers between devices, swap(): lax.ppermute(value, axis, [(i, i ^ offset) for i in range(lax.axis_size(a...  19 us
    all_to_all x1, starting transfers between devices, on_device(): lax.all_to_all(cut(snapshots, times, received[0]), 'tm', 0, 0, tiled=True)  3.57 us
    unnamed x12, local copies, waits for them, and re-layouts  3.44 us
    pallas_call x1, Pallas kernels, project(): pl.pallas_call(project_kernel, grid=(points // depth,), in_specs=[pl.Bloc...  2.11 us
    pallas_call x1, Pallas kernels, mix(): pl.pallas_call(functools.partial(mix_kernel, math.sqrt(total)), in_specs=...  2.09 us
  transfers between devices with their start and end apart: 12, of which 4 were waited for; matrix products, arithmetic and copies ran while one was open for 1% of the time, Pallas kernels for 4%

profile of v3, /device:TPU:0, one launch (start us, length us, event | category | flops | bytes accessed | tf_op | source)
XLA Modules:
  0.0 76.9 jit_solution(15701187349436288518)
XLA Ops:
  0.7 0.0 copy-start
  0.7 2.2 %copy-done = f32[4096,256]{1,0:T(8,128)S(1)} copy-done((f32[4096,256]{1,0:T(8,128)S(1)}, f32[4096,256]{1,0:T(8,128)}, u32[]{:S(2)}) %copy-start) | copy-done | bytes 4194328
  2.8 0.0 copy-start.1
  2.8 1.2 %copy-done.1 = f32[64,4096]{1,0:T(8,128)S(1)} copy-done((f32[64,4096]{1,0:T(8,128)S(1)}, f32[64,4096]{1,0:T(8,128)}, u32[]{:S(2)}) %copy-start.1) | copy-done | bytes 1048600
  4.1 0.0 copy-start.2
  4.1 2.1 %shard_map.41 = f32[64,256]{1,0:T(8,128)S(1)} custom-call(f32[64,4096]{1,0:T(8,128)S(1)} %copy-done.1, f32[4096,256]{1,0:T(8,128)S(1)} %copy-done), custom_call_target="tpu_custom_call" | custom-call | tf_op jit(solution)/shard_map/pallas_call | solution.py:55
  6.2 2.5 %collective-permute-start.2 = (f32[32,256]{1,0:T(8,128)S(1)}, f32[32,256]{1,0:T(8,128)S(1)}, u32[]{:S(2)}, u32[]{:S(2)}) collective-permute-start(f32[32,256]{1,0:T(8,128)S(1)} %get-tuple-element.12), channel_id=1, source_target_pairs={{0,3},{1,2},{2,1},{3,0},{4,7},{5,6},{6,5},{7,4},{8,11},{9,10},{10,... | collective-permute-start | bytes 98312 | tf_op jit(solution)/shard_map/ppermute | solution.py:155
  8.7 0.7 collective-permute-start
  9.4 0.0 collective-permute-start.1
  9.4 1.1 %collective-permute-done.2 = f32[32,256]{1,0:T(8,128)S(1)} collective-permute-done((f32[32,256]{1,0:T(8,128)S(1)}, f32[32,256]{1,0:T(8,128)S(1)}, u32[]{:S(2)}, u32[]{:S(2)}) %collective-permute-start.2) | collective-permute-done | bytes 32800 | tf_op jit(solution)/shard_map/ppermute | solution.py:155
  10.5 0.0 collective-permute-done
  10.5 2.8 %collective-permute-done.1 = f32[32,256]{1,0:T(8,128)S(1)} collective-permute-done((f32[32,256]{1,0:T(8,128)S(1)}, f32[32,256]{1,0:T(8,128)S(1)}, u32[]{:S(2)}, u32[]{:S(2)}) %collective-permute-start.1) | collective-permute-done | bytes 32800 | tf_op jit(solution)/shard_map/ppermute | solution.py:155
  13.3 1.6 %collective-permute-start.3 = (f32[32,256]{1,0:T(8,128)S(1)}, f32[32,256]{1,0:T(8,128)S(1)}, u32[]{:S(2)}, u32[]{:S(2)}) collective-permute-start(f32[32,256]{1,0:T(8,128)S(1)} %get-tuple-element.9), channel_id=1, source_target_pairs={{0,4},{4,0},{8,12},{12,8},{16,20},{20,16},{24,28},{28,24},{1,5},{5... | collective-permute-start | bytes 98312 | tf_op jit(solution)/shard_map/ppermute | solution.py:155
  14.8 3.6 %collective-permute-start.8 = (f32[32,256]{1,0:T(8,128)S(1)}, f32[32,256]{1,0:T(8,128)S(1)}, u32[]{:S(2)}, u32[]{:S(2)}) collective-permute-start(f32[32,256]{1,0:T(8,128)S(1)} %get-tuple-element.9), channel_id=1, source_target_pairs={{0,24},{4,28},{8,16},{12,20},{16,8},{20,12},{24,0},{28,4},{1,25},{... | collective-permute-start | bytes 98312 | tf_op jit(solution)/shard_map/ppermute | solution.py:155
  18.5 0.0 collective-permute-start.7
  18.5 2.9 %collective-permute-start.6 = (f32[32,256]{1,0:T(8,128)S(1)}, f32[32,256]{1,0:T(8,128)S(1)}, u32[]{:S(2)}, u32[]{:S(2)}) collective-permute-start(f32[32,256]{1,0:T(8,128)S(1)} %get-tuple-element.9), channel_id=1, source_target_pairs={{0,16},{4,20},{8,24},{12,28},{16,0},{20,4},{24,8},{28,12},{1,17},{... | collective-permute-start | bytes 98312 | tf_op jit(solution)/shard_map/ppermute | solution.py:155
  21.4 0.5 collective-permute-start.5
  21.8 0.0 collective-permute-done.3._
  21.8 2.5 %collective-permute-start.4 = (f32[32,256]{1,0:T(8,128)S(1)}, f32[32,256]{1,0:T(8,128)S(1)}, u32[]{:S(2)}, u32[]{:S(2)}) collective-permute-start(f32[32,256]{1,0:T(8,128)S(1)} %get-tuple-element.9), channel_id=1, source_target_pairs={{0,8},{4,12},{8,0},{12,4},{16,24},{20,28},{24,16},{28,20},{1,9},{5... | collective-permute-start | bytes 98312 | tf_op jit(solution)/shard_map/ppermute | solution.py:155
  24.3 0.0 copy-done.2
  24.3 1.0 %shard_map.43 = f32[8,64,512]{2,1,0:T(8,128)} custom-call(f32[64,4096]{1,0:T(8,128)S(1)} %copy-done.2, f32[32,256]{1,0:T(8,128)S(1)} %collective-permute-done.3._), custom_call_target="tpu_custom_call" | custom-call | tf_op jit(solution)/shard_map/pallas_call | solution.py:86
  25.4 3.6 %all-to-all-start = ((f32[8,64,512]{2,1,0:T(8,128)}), f32[8,64,512]{2,1,0:T(8,128)S(1)}, u32[]{:S(2)}, u32[]{:S(2)}) async-start(f32[8,64,512]{2,1,0:T(8,128)} %shard_map.43), calls=%async_computation | async-start | bytes 2097152 | tf_op jit(solution)/shard_map/all_to_all | solution.py:178
  29.0 0.0 collective-permute-done.4
  29.0 4.7 %collective-permute-start.9 = (f32[32,256]{1,0:T(8,128)S(1)}, f32[32,256]{1,0:T(8,128)S(1)}, u32[]{:S(2)}, u32[]{:S(2)}) collective-permute-start(f32[32,256]{1,0:T(8,128)S(1)} %get-tuple-element.9), channel_id=1, source_target_pairs={{0,28},{4,24},{8,20},{12,16},{16,12},{20,8},{24,4},{28,0},{1,29},{... | collective-permute-start | bytes 98312 | tf_op jit(solution)/shard_map/ppermute | solution.py:155
  33.7 0.0 collective-permute-done.5
  33.7 0.0 collective-permute-done.6
  33.7 0.0 collective-permute-done.7
  33.7 0.0 collective-permute-done.8
  33.8 15.6 %collective-permute-done.9 = f32[32,256]{1,0:T(8,128)S(1)} collective-permute-done((f32[32,256]{1,0:T(8,128)S(1)}, f32[32,256]{1,0:T(8,128)S(1)}, u32[]{:S(2)}, u32[]{:S(2)}) %collective-permute-start.9) | collective-permute-done | bytes 32800 | tf_op jit(solution)/shard_map/ppermute | solution.py:155
  49.3 0.6 gather_fusion
  49.9 0.1 collective-permute-start.10
  50.0 1.5 %collective-permute-done.10 = f32[8,32,256]{2,1,0:T(8,128)S(1)} collective-permute-done((f32[8,32,256]{2,1,0:T(8,128)S(1)}, f32[8,32,256]{2,1,0:T(8,128)S(1)}, u32[]{:S(2)}, u32[]{:S(2)}) %collective-permute-start.10) | collective-permute-done | bytes 262176 | tf_op jit(solution)/shard_map/ppermute | solution.py:155
  51.6 2.1 %shard_map.42 = (bf16[256,512]{1,0:T(8,128)(2,1)S(1)}, bf16[256,512]{1,0:T(8,128)(2,1)S(1)}, f32[64,256]{1,0:T(8,128)}) custom-call(s32[1]{0:T(128)} %bitcast.index_ref, f32[8,32,256]{2,1,0:T(8,128)S(1)} %get-tuple-element.11.low_ref, f32[8,32,256]{2,1,0:T(8,128)S(1)} %get-tuple-element.10.high_ref), custom_call_target="tpu_custom_call" | custom-call | tf_op jit(solution)/shard_map/pallas_call | solution.py:125
  53.6 0.0 all-to-all-done
  53.7 0.6 shard_map.44
  54.2 21.8 %all_to_all.10 = f32[8,32,512]{2,1,0:T(8,128)S(1)} all-to-all(f32[8,32,512]{2,1,0:T(8,128)S(1)} %shard_map.44), channel_id=1, replica_groups=mesh['tm'=8,'space'=4] {'tm'}, dimensions={0} | all-to-all | bytes 1048576 | tf_op jit(solution)/shard_map/all_to_all | solution.py:182
  76.1 0.8 %copy.5 = f32[8,4,8,512]{3,2,0,1:T(8,128)} copy(f32[8,4,8,512]{3,2,1,0:T(8,128)S(1)} %bitcast.30) | data formatting | bytes 1048576 | tf_op jit(solution)/shard_map/reshape | solution.py:183
  (12 shorter events, 0.1 us)
Async XLA Ops:
  0.7 2.2 %copy-start = (f32[4096,256]{1,0:T(8,128)S(1)}, f32[4096,256]{1,0:T(8,128)}, u32[]{:S(2)}) copy-start(f32[4096,256]{1,0:T(8,128)} %factor_ref.1) | copy-start | bytes 12582916
  2.8 1.2 %copy-start.1 = (f32[64,4096]{1,0:T(8,128)S(1)}, f32[64,4096]{1,0:T(8,128)}, u32[]{:S(2)}) copy-start(f32[64,4096]{1,0:T(8,128)} %snapshots_ref.3) | copy-start | bytes 3145732
  4.1 20.2 %copy-start.2 = (f32[64,4096]{1,0:T(8,128)S(1)}, f32[64,4096]{1,0:T(8,128)}, u32[]{:S(2)}) copy-start(f32[64,4096]{1,0:T(8,128)} %snapshots_ref.3) | copy-start | bytes 3145732
  6.2 4.3 %collective-permute-start.2 = (f32[32,256]{1,0:T(8,128)S(1)}, f32[32,256]{1,0:T(8,128)S(1)}, u32[]{:S(2)}, u32[]{:S(2)}) collective-permute-start(f32[32,256]{1,0:T(8,128)S(1)} %get-tuple-element.12), channel_id=1, source_target_pairs={{0,3},{1,2},{2,1},{3,0},{4,7},{5,6},{6,5},{7,4},{8,11},{9,10},{10,... | collective-permute-start | bytes 98312 | tf_op jit(solution)/shard_map/ppermute | solution.py:155
  8.7 1.8 %collective-permute-start = (f32[32,256]{1,0:T(8,128)S(1)}, f32[32,256]{1,0:T(8,128)S(1)}, u32[]{:S(2)}, u32[]{:S(2)}) collective-permute-start(f32[32,256]{1,0:T(8,128)S(1)} %get-tuple-element.12), channel_id=1, source_target_pairs={{0,1},{1,0},{2,3},{3,2},{4,5},{5,4},{6,7},{7,6},{8,9},{9,8},{10,11... | collective-permute-start | bytes 98312 | tf_op jit(solution)/shard_map/ppermute | solution.py:155
  9.4 3.9 %collective-permute-start.1 = (f32[32,256]{1,0:T(8,128)S(1)}, f32[32,256]{1,0:T(8,128)S(1)}, u32[]{:S(2)}, u32[]{:S(2)}) collective-permute-start(f32[32,256]{1,0:T(8,128)S(1)} %get-tuple-element.13), channel_id=1, source_target_pairs={{0,2},{1,3},{2,0},{3,1},{4,6},{5,7},{6,4},{7,5},{8,10},{9,11},{10,... | collective-permute-start | bytes 98312 | tf_op jit(solution)/shard_map/ppermute | solution.py:155
  13.3 8.5 %collective-permute-start.3 = (f32[32,256]{1,0:T(8,128)S(1)}, f32[32,256]{1,0:T(8,128)S(1)}, u32[]{:S(2)}, u32[]{:S(2)}) collective-permute-start(f32[32,256]{1,0:T(8,128)S(1)} %get-tuple-element.9), channel_id=1, source_target_pairs={{0,4},{4,0},{8,12},{12,8},{16,20},{20,16},{24,28},{28,24},{1,5},{5... | collective-permute-start | bytes 98312 | tf_op jit(solution)/shard_map/ppermute | solution.py:155
  14.8 18.9 %collective-permute-start.8 = (f32[32,256]{1,0:T(8,128)S(1)}, f32[32,256]{1,0:T(8,128)S(1)}, u32[]{:S(2)}, u32[]{:S(2)}) collective-permute-start(f32[32,256]{1,0:T(8,128)S(1)} %get-tuple-element.9), channel_id=1, source_target_pairs={{0,24},{4,28},{8,16},{12,20},{16,8},{20,12},{24,0},{28,4},{1,25},{... | collective-permute-start | bytes 98312 | tf_op jit(solution)/shard_map/ppermute | solution.py:155
  18.5 15.3 %collective-permute-start.7 = (f32[32,256]{1,0:T(8,128)S(1)}, f32[32,256]{1,0:T(8,128)S(1)}, u32[]{:S(2)}, u32[]{:S(2)}) collective-permute-start(f32[32,256]{1,0:T(8,128)S(1)} %get-tuple-element.9), channel_id=1, source_target_pairs={{0,20},{4,16},{8,28},{12,24},{16,4},{20,0},{24,12},{28,8},{1,21},{... | collective-permute-start | bytes 98312 | tf_op jit(solution)/shard_map/ppermute | solution.py:155
  18.5 15.2 %collective-permute-start.6 = (f32[32,256]{1,0:T(8,128)S(1)}, f32[32,256]{1,0:T(8,128)S(1)}, u32[]{:S(2)}, u32[]{:S(2)}) collective-permute-start(f32[32,256]{1,0:T(8,128)S(1)} %get-tuple-element.9), channel_id=1, source_target_pairs={{0,16},{4,20},{8,24},{12,28},{16,0},{20,4},{24,8},{28,12},{1,17},{... | collective-permute-start | bytes 98312 | tf_op jit(solution)/shard_map/ppermute | solution.py:155
  21.4 12.3 %collective-permute-start.5 = (f32[32,256]{1,0:T(8,128)S(1)}, f32[32,256]{1,0:T(8,128)S(1)}, u32[]{:S(2)}, u32[]{:S(2)}) collective-permute-start(f32[32,256]{1,0:T(8,128)S(1)} %get-tuple-element.9), channel_id=1, source_target_pairs={{0,12},{4,8},{8,4},{12,0},{16,28},{20,24},{24,20},{28,16},{1,13},{... | collective-permute-start | bytes 98312 | tf_op jit(solution)/shard_map/ppermute | solution.py:155
  21.8 7.1 %collective-permute-start.4 = (f32[32,256]{1,0:T(8,128)S(1)}, f32[32,256]{1,0:T(8,128)S(1)}, u32[]{:S(2)}, u32[]{:S(2)}) collective-permute-start(f32[32,256]{1,0:T(8,128)S(1)} %get-tuple-element.9), channel_id=1, source_target_pairs={{0,8},{4,12},{8,0},{12,4},{16,24},{20,28},{24,16},{28,20},{1,9},{5... | collective-permute-start | bytes 98312 | tf_op jit(solution)/shard_map/ppermute | solution.py:155
  25.4 28.3 %all-to-all-start = ((f32[8,64,512]{2,1,0:T(8,128)}), f32[8,64,512]{2,1,0:T(8,128)S(1)}, u32[]{:S(2)}, u32[]{:S(2)}) async-start(f32[8,64,512]{2,1,0:T(8,128)} %shard_map.43), calls=%async_computation | async-start | bytes 2097152 | tf_op jit(solution)/shard_map/all_to_all | solution.py:178
  29.0 20.4 %collective-permute-start.9 = (f32[32,256]{1,0:T(8,128)S(1)}, f32[32,256]{1,0:T(8,128)S(1)}, u32[]{:S(2)}, u32[]{:S(2)}) collective-permute-start(f32[32,256]{1,0:T(8,128)S(1)} %get-tuple-element.9), channel_id=1, source_target_pairs={{0,28},{4,24},{8,20},{12,16},{16,12},{20,8},{24,4},{28,0},{1,29},{... | collective-permute-start | bytes 98312 | tf_op jit(solution)/shard_map/ppermute | solution.py:155
  49.9 1.6 %collective-permute-start.10 = (f32[8,32,256]{2,1,0:T(8,128)S(1)}, f32[8,32,256]{2,1,0:T(8,128)S(1)}, u32[]{:S(2)}, u32[]{:S(2)}) collective-permute-start(f32[8,32,256]{2,1,0:T(8,128)S(1)} %gather_fusion), channel_id=1, source_target_pairs={{0,1},{1,0},{2,3},{3,2},{4,5},{5,4},{6,7},{7,6},{8,9},{9,8},{10,11... | collective-permute-start | bytes 786440 | tf_op jit(solution)/shard_map/ppermute | solution.py:155

commit v4 on v3

v4 whole, which is shorter than its diff:
```python
import functools
import math

import jax
import jax.numpy as jnp
from jax import lax
from jax.experimental import pallas as pl
from jax.experimental.pallas import tpu as pltpu
from jax.sharding import PartitionSpec as P

MIB = 1024 * 1024
ANY = pl.BlockSpec(memory_space=pl.ANY)
SMEM = pl.BlockSpec(memory_space=pltpu.SMEM)
VMEM = pl.BlockSpec(memory_space=pltpu.VMEM)
ROWS_BY_ROWS = (((0,), (0,)), ((), ()))
ROWS_BY_COLUMNS = (((1,), (0,)), ((), ()))
COLUMNS_BY_COLUMNS = (((1,), (1,)), ((), ()))


def params(mib=48):
    return pltpu.CompilerParams(vmem_limit_bytes=mib * MIB)


def split(value):
    high = value.astype(jnp.bfloat16)
    return high, (value - high.astype(jnp.float32)).astype(jnp.bfloat16)


def dot(left, right, dims=ROWS_BY_COLUMNS):
    return lax.dot_general(left, right, dims, preferred_element_type=jnp.float32)


def product(left, right, dims=ROWS_BY_COLUMNS):
    (left_high, left_low), (right_high, right_low) = left, right
    return dot(left_high, right_high, dims) + (
        dot(left_high, right_low, dims) + dot(left_low, right_high, dims)
    )


def project_kernel(snapshots_ref, factor_ref, partial_ref):
    rows = snapshots_ref.shape[0]
    high, low = split(snapshots_ref[...])
    factor_high, factor_low = split(factor_ref[...])
    both = dot(jnp.concatenate([high, low], axis=0), factor_high)
    term = both[:rows] + (both[rows:] + dot(high, factor_low))

    @pl.when(pl.program_id(0) == 0)
    def _():
        partial_ref[...] = term

    @pl.when(pl.program_id(0) != 0)
    def _():
        partial_ref[...] += term


def project(snapshots, space_factor):
    rows, points = snapshots.shape
    rank = space_factor.shape[1]
    depth = min(512, points)
    return pl.pallas_call(
        project_kernel,
        grid=(points // depth,),
        in_specs=[
            pl.BlockSpec((rows, depth), lambda i: (0, i)),
            pl.BlockSpec((depth, rank), lambda i: (i, 0)),
        ],
        out_specs=pl.BlockSpec((rows, rank), lambda i: (0, 0)),
        out_shape=jax.ShapeDtypeStruct((rows, rank), jnp.float32),
        compiler_params=params(60),
    )(snapshots, space_factor)


def cut_kernel(snapshots_ref, _, *refs):
    *parts, sems = refs
    width = parts[0].shape[1]
    member = lax.rem(lax.axis_index("tm"), len(parts))
    copies = []
    for k, part in enumerate(parts):
        start = pl.multiple_of((member ^ k) * width, width)
        copies.append(pltpu.make_async_copy(snapshots_ref.at[:, pl.ds(start, width)], part, sems.at[k]))
    for copy in copies:
        copy.start()
    for copy in copies:
        copy.wait()


def cut(snapshots, parts, after):
    rows, points = snapshots.shape
    return pl.pallas_call(
        cut_kernel,
        in_specs=[ANY, ANY],
        out_specs=[ANY] * parts,
        out_shape=[jax.ShapeDtypeStruct((rows, points // parts), jnp.float32)] * parts,
        scratch_shapes=[pltpu.SemaphoreType.DMA((parts,))],
        compiler_params=params(),
    )(snapshots, after)


def mix_kernel(times, group, order, index_ref, mine_ref, theirs_ref, high_t_ref, low_t_ref, own_ref):
    total_half, rank = mine_ref.shape
    half = total_half // times
    mine = mine_ref[...].reshape(times, half, rank)
    theirs = theirs_ref[...].reshape(times, half, rank)
    first = index_ref[1] == 0
    low_rows, high_rows = jnp.where(first, mine, theirs), jnp.where(first, theirs, mine)
    projected = jnp.concatenate([low_rows, high_rows], axis=1).reshape(2 * total_half, rank)
    high, low = split(projected)
    cross = dot(high, low, ROWS_BY_ROWS)
    gram = dot(high, high, ROWS_BY_ROWS) + (cross + cross.T)
    diagonal = lax.broadcasted_iota(jnp.int32, (rank, rank), 0) == lax.broadcasted_iota(
        jnp.int32, (rank, rank), 1
    )
    total = jnp.sum(projected * projected)
    correlation = gram / total
    correlation_split = split(correlation)
    square = product(correlation_split, correlation_split)
    tail = jnp.where(diagonal, 1.6875, 0.0) - 0.5625 * correlation + 0.0625 * square
    mixing = (jnp.where(diagonal, 2.25, 0.0) - 2.4375 * correlation) + product(split(square), split(tail))

    mixing_high, mixing_low = split(mixing)

    rows = 2 * half
    places = [order.index(k) for k in range(group)]
    high = jnp.concatenate([high[i * rows : (i + 1) * rows] for i in places], axis=0)
    low = jnp.concatenate([low[i * rows : (i + 1) * rows] for i in places], axis=0)
    scale = lax.rsqrt(total)
    own = product((high[:rows], low[:rows]), (mixing_high, mixing_low))
    own_ref[...] = own * (scale * math.sqrt(times * rows))
    width = rank // times
    row = lax.broadcasted_iota(jnp.int32, (rank, rank), 0)
    source = ((row // width) ^ index_ref[0]) * width + row % width
    move = jnp.where(source == lax.broadcasted_iota(jnp.int32, (rank, rank), 1), 1.0, 0.0).astype(jnp.bfloat16)
    moved = dot(move, jnp.concatenate([mixing_high, mixing_low], axis=1)).astype(jnp.bfloat16)
    turned = product((moved[:, :rank], moved[:, rank:]), (high, low), COLUMNS_BY_COLUMNS) * scale
    turned_high, turned_low = split(turned)
    high_t_ref[...] = turned_high
    low_t_ref[...] = turned_low


def mix(index, mine, theirs, times, group, order):
    total_half, rank = mine.shape
    rows = 2 * total_half // times
    return pl.pallas_call(
        functools.partial(mix_kernel, times, group, order),
        in_specs=[SMEM, VMEM, VMEM],
        out_specs=[VMEM] * 3,
        out_shape=[
            jax.ShapeDtypeStruct((rank, group * rows), jnp.bfloat16),
            jax.ShapeDtypeStruct((rank, group * rows), jnp.bfloat16),
            jax.ShapeDtypeStruct((rows, rank), jnp.float32),
        ],
        compiler_params=params(),
    )(index, mine, theirs)


def load_kernel(group, high_ref, low_ref, *refs):
    parts, blocks = refs[:group], refs[group:]
    columns = jnp.concatenate([part[...] for part in parts], axis=0)
    value = product((high_ref[...], low_ref[...]), split(columns))
    width = value.shape[0] // len(blocks)
    for i, block in enumerate(blocks):
        block[...] = value[i * width : (i + 1) * width]


def load(high, low, parts, blocks):
    rank = high.shape[0]
    columns = parts[0].shape[1]
    return pl.pallas_call(
        functools.partial(load_kernel, len(parts)),
        in_specs=[VMEM] * (2 + len(parts)),
        out_specs=[VMEM] * blocks,
        out_shape=[jax.ShapeDtypeStruct((rank // blocks, columns), jnp.float32)] * blocks,
        compiler_params=params(),
    )(high, low, *parts)


def join_kernel(group, *refs):
    *parts, out_ref = refs
    width = parts[0].shape[1]
    member = lax.rem(lax.axis_index("tm"), group)
    for k in range(group):
        value = parts[k][...]
        if k == 0:
            for term in parts[group:]:
                value = value + term[...]
        out_ref[:, pl.ds(pl.multiple_of((member ^ k) * width, width), width)] = value


def join(parts, terms):
    rows, width = parts[0].shape
    group = len(parts)
    return pl.pallas_call(
        functools.partial(join_kernel, group),
        in_specs=[VMEM] * (group + len(terms)),
        out_specs=VMEM,
        out_shape=jax.ShapeDtypeStruct((rows, group * width), jnp.float32),
        compiler_params=params(),
    )(*parts, *terms)


def swap(value, axis, offset):
    return lax.ppermute(value, axis, [(i, i ^ offset) for i in range(lax.axis_size(axis))])


def on_device(snapshots, space_factor):
    rows, points = snapshots.shape
    rank = space_factor.shape[1]
    times, spaces = lax.axis_size("tm"), lax.axis_size("space")
    group = min(4, times)
    index = lax.axis_index("tm")
    core = lax.axis_index("space") % 2

    partial = project(snapshots, space_factor)
    halves = partial.reshape(2, rows // 2, rank)
    mine = lax.dynamic_index_in_dim(halves, core, 0, keepdims=False)
    other = lax.dynamic_index_in_dim(halves, 1 - core, 0, keepdims=False)
    terms = [mine] + [swap(other if k % 2 else mine, "space", k) for k in range(1, spaces)]
    while len(terms) > 1:
        terms = [a + b for a, b in zip(terms[::2], terms[1::2])]

    pieces, *parts = lax.optimization_barrier((terms[0], *cut(snapshots, group, partial)))
    parts = [part if k == 0 else swap(part, "tm", k) for k, part in enumerate(parts)]

    order = [0]
    offsets = [1 << i for i in range(times.bit_length() - 1)]
    for offset in [o for o in offsets if o >= group] + [o for o in offsets if o < group]:
        pieces = jnp.concatenate([pieces, swap(pieces, "tm", offset)], axis=0)
        if offset < group:
            pieces, parts[offset] = lax.optimization_barrier((pieces, parts[offset]))
        order = order + [k ^ offset for k in order]
    high_t, low_t, own = mix(jnp.stack([index, core]), pieces, swap(pieces, "space", 1), times, group, order)

    blocks = load(high_t, low_t, parts, times)
    sums = []
    for k in [*range(1, group), 0]:
        sums.append([blocks[k]] + [swap(blocks[q + k], "tm", q) for q in range(group, times, group)])
    received = [swap(sum(sums[k - 1][1:], sums[k - 1][0]), "tm", k) for k in range(1, group)]
    last = sums[-1]
    return own, join([last[0], *received], last[1:])


def solution(mesh):
    return jax.shard_map(
        on_device,
        mesh=mesh,
        in_specs=(P("tm", "space"), P("space", None)),
        out_specs=(P("tm", None), P("tm", "space")),
        check_vma=False,
    )
```

time: 77.2 us -> 74.6 us (0.966)
  blocking collectives: 21.8 us -> 0 us
  waiting for transfers between devices: 21 us -> 38.9 us
  Pallas kernels: 5.83 us -> 10.5 us
  local copies, waits for them, and re-layouts: 4.85 us -> 1.62 us
    all_to_all x1 -> x0, blocking collectives: 21.8 us -> none  [on_device(): lax.all_to_all(blocks, 'tm', split_axis=0, concat_axis=0, tiled=True)]
    ppermute x11 -> x17, waiting for transfers between devices: 21 us -> 38.9 us  [swap(): lax.ppermute(value, axis, [(i, i ^ offset) for i in range(lax.axis_size(a...]
    pallas_call x1, Pallas kernels: 2.11 us -> 6.46 us  [project(): pl.pallas_call(project_kernel, grid=(points // depth,), in_specs=[pl.Bloc...]
    all_to_all x1 -> x0, starting transfers between devices: 3.57 us -> none  [on_device(): lax.all_to_all(cut(snapshots, times, received[0]), 'tm', 0, 0, tiled=True)]
    ppermute x11 -> x17, starting transfers between devices: 19 us -> 22.3 us  [swap(): lax.ppermute(value, axis, [(i, i ^ offset) for i in range(lax.axis_size(a...]
    unnamed x12 -> x4, local copies, waits for them, and re-layouts: 3.44 us -> 0.84 us
    reshape x1 -> x0, local copies, waits for them, and re-layouts: 0.83 us -> none  [on_device(): return (own, loadings.transpose(1, 0, 2).reshape(rank // times, points))]
    pallas_call x3 -> x4, Pallas kernels: 3.72 us -> 4 us  [the longest x1 2.46 us: mix(): pl.pallas_call(functools.partial(mix_kernel, times, group, order), in_spe...]
  transfers between devices with their start and end apart: 12 -> 17, of which waited for: 4 -> 12; matrix products, arithmetic and copies ran while one was open for 1% -> 0% of each run, Pallas kernels for 4% -> 3%
where the time goes in v4:
time: 74.6 us; the launch traced here: 74.2 us
  waiting for transfers between devices  38.9 us (52%)
  starting transfers between devices  22.3 us (30%)
  Pallas kernels  10.5 us (14%)
  local copies, waits for them, and re-layouts  1.62 us (2%)
  between operations  0.75 us (1%)
    ppermute x17, waiting for transfers between devices, swap(): lax.ppermute(value, axis, [(i, i ^ offset) for i in range(lax.axis_size(a...  38.9 us
    ppermute x17, starting transfers between devices, swap(): lax.ppermute(value, axis, [(i, i ^ offset) for i in range(lax.axis_size(a...  22.3 us
    pallas_call x1, Pallas kernels, project(): pl.pallas_call(project_kernel, grid=(points // depth,), in_specs=[pl.Bloc...  6.46 us
    pallas_call x1, Pallas kernels, mix(): pl.pallas_call(functools.partial(mix_kernel, times, group, order), in_spe...  2.46 us
  transfers between devices with their start and end apart: 17, of which 12 were waited for; matrix products, arithmetic and copies ran while one was open for 0% of the time, Pallas kernels for 3%

profile of v4, /device:TPU:0, one launch (start us, length us, event | category | flops | bytes accessed | tf_op | source)
XLA Modules:
  0.0 74.2 jit_solution(14102360034085390221)
XLA Ops:
  0.6 0.0 copy-start
  0.7 6.5 %shard_map.41._ = f32[64,256]{1,0:T(8,128)} custom-call(f32[64,4096]{1,0:T(8,128)} %snapshots_ref.3, f32[4096,256]{1,0:T(8,128)} %factor_ref.1), custom_call_target="tpu_custom_call" | custom-call | tf_op jit(solution)/shard_map/pallas_call | solution.py:60
  7.1 0.8 %dynamic-slice_bitcast_fusion = (f32[32,256]{1,0:T(8,128)S(1)}, f32[32,256]{1,0:T(8,128)S(1)}) fusion(f32[2,32,256]{2,1,0:T(8,128)} %bitcast.7, s32[]{:T(128)S(6)} %select_n.16, s32[]{:T(128)S(6)} %select_n.15), kind=kLoop, calls=%fused_computation.4 | loop fusion | bytes 131080 | tf_op jit(solution)/shard_map/jit(dynamic_index_in_dim)/squeeze | solution.py:216
  7.9 2.4 %collective-permute-start.2 = (f32[32,256]{1,0:T(8,128)S(1)}, f32[32,256]{1,0:T(8,128)S(1)}, u32[]{:S(2)}, u32[]{:S(2)}) collective-permute-start(f32[32,256]{1,0:T(8,128)S(1)} %get-tuple-element.50), channel_id=1, source_target_pairs={{0,3},{1,2},{2,1},{3,0},{4,7},{5,6},{6,5},{7,4},{8,11},{9,10},{10,... | collective-permute-start | bytes 98312 | tf_op jit(solution)/shard_map/ppermute | solution.py:202
  10.3 0.7 collective-permute-start
  11.0 0.0 collective-permute-start.1
  11.0 0.0 copy-done
  11.0 0.0 copy-start.1
  11.0 0.8 %copy-done.1 = f32[64,256]{1,0:T(8,128)S(1)} copy-done((f32[64,256]{1,0:T(8,128)S(1)}, f32[64,256]{1,0:T(8,128)}, u32[]{:S(2)}) %copy-start.1) | copy-done | bytes 65560
  11.9 0.1 shard_map.42
  12.0 0.1 collective-permute-done.2
  12.1 0.0 collective-permute-done
  12.1 2.8 %collective-permute-done.1 = f32[32,256]{1,0:T(8,128)S(1)} collective-permute-done((f32[32,256]{1,0:T(8,128)S(1)}, f32[32,256]{1,0:T(8,128)S(1)}, u32[]{:S(2)}, u32[]{:S(2)}) %collective-permute-start.1) | collective-permute-done | bytes 32800 | tf_op jit(solution)/shard_map/ppermute | solution.py:202
  14.9 2.7 %collective-permute-start.3 = (f32[32,256]{1,0:T(8,128)S(1)}, f32[32,256]{1,0:T(8,128)S(1)}, u32[]{:S(2)}, u32[]{:S(2)}) collective-permute-start(f32[32,256]{1,0:T(8,128)S(1)} %add_add_fusion), channel_id=1, source_target_pairs={{0,16},{4,20},{8,24},{12,28},{16,0},{20,4},{24,8},{28,12},{1,17},{... | collective-permute-start | bytes 98312 | tf_op jit(solution)/shard_map/ppermute | solution.py:202
  17.6 1.5 %collective-permute-start.5 = (f32[64,1024]{1,0:T(8,128)S(1)}, f32[64,1024]{1,0:T(8,128)S(1)}, u32[]{:S(2)}, u32[]{:S(2)}) collective-permute-start(f32[64,1024]{1,0:T(8,128)S(1)} %get-tuple-element.31), channel_id=1, source_target_pairs={{0,4},{4,0},{8,12},{12,8},{16,20},{20,16},{24,28},{28,24},{1,5},{5... | collective-permute-start | bytes 786440 | tf_op jit(solution)/shard_map/ppermute | solution.py:202
  19.1 0.7 collective-permute-done.3
  19.8 1.5 %collective-permute-start.4 = (f32[64,256]{1,0:T(8,128)S(1)}, f32[64,256]{1,0:T(8,128)S(1)}, u32[]{:S(2)}, u32[]{:S(2)}) collective-permute-start(f32[64,256]{1,0:T(8,128)S(1)} %pad_maximum_fusion.2), channel_id=1, source_target_pairs={{0,4},{4,0},{8,12},{12,8},{16,20},{20,16},{24,28},{28,24},{1,5},{5... | collective-permute-start | bytes 196616 | tf_op jit(solution)/shard_map/ppermute | solution.py:202
  21.3 1.6 %collective-permute-start.7 = (f32[64,1024]{1,0:T(8,128)S(1)}, f32[64,1024]{1,0:T(8,128)S(1)}, u32[]{:S(2)}, u32[]{:S(2)}) collective-permute-start(f32[64,1024]{1,0:T(8,128)S(1)} %get-tuple-element.33), channel_id=1, source_target_pairs={{0,8},{4,12},{8,0},{12,4},{16,24},{20,28},{24,16},{28,20},{1,9},{5... | collective-permute-start | bytes 786440 | tf_op jit(solution)/shard_map/ppermute | solution.py:202
  22.9 2.9 %collective-permute-done.4 = f32[64,256]{1,0:T(8,128)S(1)} collective-permute-done((f32[64,256]{1,0:T(8,128)S(1)}, f32[64,256]{1,0:T(8,128)S(1)}, u32[]{:S(2)}, u32[]{:S(2)}) %collective-permute-start.4) | collective-permute-done | bytes 65568 | tf_op jit(solution)/shard_map/ppermute | solution.py:202
  25.8 0.0 collective-permute-done.5.refs_1_
  25.8 1.6 %collective-permute-start.6 = (f32[128,256]{1,0:T(8,128)S(1)}, f32[128,256]{1,0:T(8,128)S(1)}, u32[]{:S(2)}, u32[]{:S(2)}) collective-permute-start(f32[128,256]{1,0:T(8,128)S(1)} %pad_maximum_fusion.1), channel_id=1, source_target_pairs={{0,8},{4,12},{8,0},{12,4},{16,24},{20,28},{24,16},{28,20},{1,9},{5... | collective-permute-start | bytes 393224 | tf_op jit(solution)/shard_map/ppermute | solution.py:202
  27.4 3.4 %collective-permute-done.6 = f32[128,256]{1,0:T(8,128)S(1)} collective-permute-done((f32[128,256]{1,0:T(8,128)S(1)}, f32[128,256]{1,0:T(8,128)S(1)}, u32[]{:S(2)}, u32[]{:S(2)}) %collective-permute-start.6) | collective-permute-done | bytes 131104 | tf_op jit(solution)/shard_map/ppermute | solution.py:202
  30.8 0.0 collective-permute-done.7.refs_2_
  30.8 0.1 collective-permute-start.8
  30.9 2.6 %collective-permute-start.9 = (f32[64,1024]{1,0:T(8,128)S(1)}, f32[64,1024]{1,0:T(8,128)S(1)}, u32[]{:S(2)}, u32[]{:S(2)}) collective-permute-start(f32[64,1024]{1,0:T(8,128)S(1)} %get-tuple-element.41), channel_id=1, source_target_pairs={{0,12},{4,8},{8,4},{12,0},{16,28},{20,24},{24,20},{28,16},{1,13},{... | collective-permute-start | bytes 786440 | tf_op jit(solution)/shard_map/ppermute | solution.py:202
  33.5 0.1 pad_add_fusion.index_ref
  33.6 0.0 collective-permute-done.8.theirs_ref
  33.6 2.5 %shard_map.43 = (bf16[256,256]{1,0:T(8,128)(2,1)S(1)}, bf16[256,256]{1,0:T(8,128)(2,1)S(1)}, f32[64,256]{1,0:T(8,128)}) custom-call(s32[2]{0:T(128)S(1)} %pad_add_fusion.index_ref, f32[256,256]{1,0:T(8,128)S(1)} %pad_maximum_fusion.mine_ref, f32[256,256]{1,0:T(8,128)S(1)} %collective-permute-done.8.theirs_ref), custom_call_target="tpu_custom_call" | custom-call | tf_op jit(solution)/shard_map/pallas_call | solution.py:143
  36.0 4.5 %collective-permute-done.9.refs_3_ = f32[64,1024]{1,0:T(8,128)S(1)} collective-permute-done((f32[64,1024]{1,0:T(8,128)S(1)}, f32[64,1024]{1,0:T(8,128)S(1)}, u32[]{:S(2)}, u32[]{:S(2)}) %collective-permute-start.9) | collective-permute-done | bytes 262176 | tf_op jit(solution)/shard_map/ppermute | solution.py:202
  40.5 0.6 shard_map.44
  41.1 1.9 %collective-permute-start.10 = (f32[32,1024]{1,0:T(8,128)S(1)}, f32[32,1024]{1,0:T(8,128)S(1)}, u32[]{:S(2)}, u32[]{:S(2)}) collective-permute-start(f32[32,1024]{1,0:T(8,128)S(1)} %get-tuple-element.44), channel_id=1, source_target_pairs={{0,16},{4,20},{8,24},{12,28},{16,0},{20,4},{24,8},{28,12},{1,17},{... | collective-permute-start | bytes 393224 | tf_op jit(solution)/shard_map/ppermute | solution.py:202
  43.0 1.1 %collective-permute-start.12 = (f32[32,1024]{1,0:T(8,128)S(1)}, f32[32,1024]{1,0:T(8,128)S(1)}, u32[]{:S(2)}, u32[]{:S(2)}) collective-permute-start(f32[32,1024]{1,0:T(8,128)S(1)} %get-tuple-element.46), channel_id=1, source_target_pairs={{0,16},{4,20},{8,24},{12,28},{16,0},{20,4},{24,8},{28,12},{1,17},{... | collective-permute-start | bytes 393224 | tf_op jit(solution)/shard_map/ppermute | solution.py:202
  44.1 1.8 %collective-permute-start.14 = (f32[32,1024]{1,0:T(8,128)S(1)}, f32[32,1024]{1,0:T(8,128)S(1)}, u32[]{:S(2)}, u32[]{:S(2)}) collective-permute-start(f32[32,1024]{1,0:T(8,128)S(1)} %get-tuple-element.48), channel_id=1, source_target_pairs={{0,16},{4,20},{8,24},{12,28},{16,0},{20,4},{24,8},{28,12},{1,17},{... | collective-permute-start | bytes 393224 | tf_op jit(solution)/shard_map/ppermute | solution.py:202
  45.9 1.1 %collective-permute-start.16 = (f32[32,1024]{1,0:T(8,128)S(1)}, f32[32,1024]{1,0:T(8,128)S(1)}, u32[]{:S(2)}, u32[]{:S(2)}) collective-permute-start(f32[32,1024]{1,0:T(8,128)S(1)} %get-tuple-element.49), channel_id=1, source_target_pairs={{0,16},{4,20},{8,24},{12,28},{16,0},{20,4},{24,8},{28,12},{1,17},{... | collective-permute-start | bytes 393224 | tf_op jit(solution)/shard_map/ppermute | solution.py:202
  47.1 12.5 %collective-permute-done.10 = f32[32,1024]{1,0:T(8,128)S(1)} collective-permute-done((f32[32,1024]{1,0:T(8,128)S(1)}, f32[32,1024]{1,0:T(8,128)S(1)}, u32[]{:S(2)}, u32[]{:S(2)}) %collective-permute-start.10) | collective-permute-done | bytes 131104 | tf_op jit(solution)/shard_map/ppermute | solution.py:202
  59.6 1.5 %collective-permute-start.11 = (f32[32,1024]{1,0:T(8,128)S(1)}, f32[32,1024]{1,0:T(8,128)S(1)}, u32[]{:S(2)}, u32[]{:S(2)}) collective-permute-start(f32[32,1024]{1,0:T(8,128)S(1)} %add.36), channel_id=1, source_target_pairs={{0,4},{4,0},{8,12},{12,8},{16,20},{20,16},{24,28},{28,24},{1,5},{5... | collective-permute-start | bytes 393224 | tf_op jit(solution)/shard_map/ppermute | solution.py:202
  61.1 1.2 %collective-permute-done.12 = f32[32,1024]{1,0:T(8,128)S(1)} collective-permute-done((f32[32,1024]{1,0:T(8,128)S(1)}, f32[32,1024]{1,0:T(8,128)S(1)}, u32[]{:S(2)}, u32[]{:S(2)}) %collective-permute-start.12) | collective-permute-done | bytes 131104 | tf_op jit(solution)/shard_map/ppermute | solution.py:202
  62.4 0.1 collective-permute-start.13
  62.5 2.8 %collective-permute-done.14 = f32[32,1024]{1,0:T(8,128)S(1)} collective-permute-done((f32[32,1024]{1,0:T(8,128)S(1)}, f32[32,1024]{1,0:T(8,128)S(1)}, u32[]{:S(2)}, u32[]{:S(2)}) %collective-permute-start.14) | collective-permute-done | bytes 131104 | tf_op jit(solution)/shard_map/ppermute | solution.py:202
  65.3 0.2 collective-permute-start.15
  65.5 1.4 %collective-permute-done.16.refs_4_ = f32[32,1024]{1,0:T(8,128)S(1)} collective-permute-done((f32[32,1024]{1,0:T(8,128)S(1)}, f32[32,1024]{1,0:T(8,128)S(1)}, u32[]{:S(2)}, u32[]{:S(2)}) %collective-permute-start.16) | collective-permute-done | bytes 131104 | tf_op jit(solution)/shard_map/ppermute | solution.py:202
  66.9 0.0 collective-permute-done.11.refs_1_
  66.9 2.8 %collective-permute-done.13.refs_2_ = f32[32,1024]{1,0:T(8,128)S(1)} collective-permute-done((f32[32,1024]{1,0:T(8,128)S(1)}, f32[32,1024]{1,0:T(8,128)S(1)}, u32[]{:S(2)}, u32[]{:S(2)}) %collective-permute-start.13) | collective-permute-done | bytes 131104 | tf_op jit(solution)/shard_map/ppermute | solution.py:202
  69.7 3.6 %collective-permute-done.15.refs_3_ = f32[32,1024]{1,0:T(8,128)S(1)} collective-permute-done((f32[32,1024]{1,0:T(8,128)S(1)}, f32[32,1024]{1,0:T(8,128)S(1)}, u32[]{:S(2)}, u32[]{:S(2)}) %collective-permute-start.15) | collective-permute-done | bytes 131104 | tf_op jit(solution)/shard_map/ppermute | solution.py:202
  73.4 0.8 %shard_map.45 = f32[32,4096]{1,0:T(8,128)} custom-call(f32[32,1024]{1,0:T(8,128)S(1)} %get-tuple-element.42.refs_0_, f32[32,1024]{1,0:T(8,128)S(1)} %collective-permute-done.11.refs_1_, f32[32,1024]{1,0:T(8,128)S(1)} %collective-permute-done.13.refs_2_, f32[32,1024]{1,0:T(8,128)S(1)} %collective-permute-done.15.refs_3_, ...), custom_call_target="tpu_custom_call" | custom-call | tf_op jit(solution)/shard_map/pallas_call | solution.py:192
  (7 shorter events, 0.1 us)
Async XLA Ops:
  0.6 10.4 %copy-start = (f32[64,4096]{1,0:T(8,128)S(1)}, f32[64,4096]{1,0:T(8,128)}, u32[]{:S(2)}) copy-start(f32[64,4096]{1,0:T(8,128)} %snapshots_ref.3) | copy-start | bytes 3145732
  7.9 4.2 %collective-permute-start.2 = (f32[32,256]{1,0:T(8,128)S(1)}, f32[32,256]{1,0:T(8,128)S(1)}, u32[]{:S(2)}, u32[]{:S(2)}) collective-permute-start(f32[32,256]{1,0:T(8,128)S(1)} %get-tuple-element.50), channel_id=1, source_target_pairs={{0,3},{1,2},{2,1},{3,0},{4,7},{5,6},{6,5},{7,4},{8,11},{9,10},{10,... | collective-permute-start | bytes 98312 | tf_op jit(solution)/shard_map/ppermute | solution.py:202
  10.3 1.8 %collective-permute-start = (f32[32,256]{1,0:T(8,128)S(1)}, f32[32,256]{1,0:T(8,128)S(1)}, u32[]{:S(2)}, u32[]{:S(2)}) collective-permute-start(f32[32,256]{1,0:T(8,128)S(1)} %get-tuple-element.50), channel_id=1, source_target_pairs={{0,1},{1,0},{2,3},{3,2},{4,5},{5,4},{6,7},{7,6},{8,9},{9,8},{10,11... | collective-permute-start | bytes 98312 | tf_op jit(solution)/shard_map/ppermute | solution.py:202
  11.0 3.9 %collective-permute-start.1 = (f32[32,256]{1,0:T(8,128)S(1)}, f32[32,256]{1,0:T(8,128)S(1)}, u32[]{:S(2)}, u32[]{:S(2)}) collective-permute-start(f32[32,256]{1,0:T(8,128)S(1)} %get-tuple-element.51), channel_id=1, source_target_pairs={{0,2},{1,3},{2,0},{3,1},{4,6},{5,7},{6,4},{7,5},{8,10},{9,11},{10,... | collective-permute-start | bytes 98312 | tf_op jit(solution)/shard_map/ppermute | solution.py:202
  11.0 0.8 %copy-start.1 = (f32[64,256]{1,0:T(8,128)S(1)}, f32[64,256]{1,0:T(8,128)}, u32[]{:S(2)}) copy-start(f32[64,256]{1,0:T(8,128)} %shard_map.41._) | copy-start | bytes 196612
  14.9 4.9 %collective-permute-start.3 = (f32[32,256]{1,0:T(8,128)S(1)}, f32[32,256]{1,0:T(8,128)S(1)}, u32[]{:S(2)}, u32[]{:S(2)}) collective-permute-start(f32[32,256]{1,0:T(8,128)S(1)} %add_add_fusion), channel_id=1, source_target_pairs={{0,16},{4,20},{8,24},{12,28},{16,0},{20,4},{24,8},{28,12},{1,17},{... | collective-permute-start | bytes 98312 | tf_op jit(solution)/shard_map/ppermute | solution.py:202
  17.6 8.2 %collective-permute-start.5 = (f32[64,1024]{1,0:T(8,128)S(1)}, f32[64,1024]{1,0:T(8,128)S(1)}, u32[]{:S(2)}, u32[]{:S(2)}) collective-permute-start(f32[64,1024]{1,0:T(8,128)S(1)} %get-tuple-element.31), channel_id=1, source_target_pairs={{0,4},{4,0},{8,12},{12,8},{16,20},{20,16},{24,28},{28,24},{1,5},{5... | collective-permute-start | bytes 786440 | tf_op jit(solution)/shard_map/ppermute | solution.py:202
  19.8 6.0 %collective-permute-start.4 = (f32[64,256]{1,0:T(8,128)S(1)}, f32[64,256]{1,0:T(8,128)S(1)}, u32[]{:S(2)}, u32[]{:S(2)}) collective-permute-start(f32[64,256]{1,0:T(8,128)S(1)} %pad_maximum_fusion.2), channel_id=1, source_target_pairs={{0,4},{4,0},{8,12},{12,8},{16,20},{20,16},{24,28},{28,24},{1,5},{5... | collective-permute-start | bytes 196616 | tf_op jit(solution)/shard_map/ppermute | solution.py:202
  21.3 9.5 %collective-permute-start.7 = (f32[64,1024]{1,0:T(8,128)S(1)}, f32[64,1024]{1,0:T(8,128)S(1)}, u32[]{:S(2)}, u32[]{:S(2)}) collective-permute-start(f32[64,1024]{1,0:T(8,128)S(1)} %get-tuple-element.33), channel_id=1, source_target_pairs={{0,8},{4,12},{8,0},{12,4},{16,24},{20,28},{24,16},{28,20},{1,9},{5... | collective-permute-start | bytes 786440 | tf_op jit(solution)/shard_map/ppermute | solution.py:202
  25.8 5.0 %collective-permute-start.6 = (f32[128,256]{1,0:T(8,128)S(1)}, f32[128,256]{1,0:T(8,128)S(1)}, u32[]{:S(2)}, u32[]{:S(2)}) collective-permute-start(f32[128,256]{1,0:T(8,128)S(1)} %pad_maximum_fusion.1), channel_id=1, source_target_pairs={{0,8},{4,12},{8,0},{12,4},{16,24},{20,28},{24,16},{28,20},{1,9},{5... | collective-permute-start | bytes 393224 | tf_op jit(solution)/shard_map/ppermute | solution.py:202
  30.8 2.7 %collective-permute-start.8 = (f32[256,256]{1,0:T(8,128)S(1)}, f32[256,256]{1,0:T(8,128)S(1)}, u32[]{:S(2)}, u32[]{:S(2)}) collective-permute-start(f32[256,256]{1,0:T(8,128)S(1)} %pad_maximum_fusion.mine_ref), channel_id=1, source_target_pairs={{0,1},{1,0},{2,3},{3,2},{4,5},{5,4},{6,7},{7,6},{8,9},{9,8},{10,11... | collective-permute-start | bytes 786440 | tf_op jit(solution)/shard_map/ppermute | solution.py:202
  30.9 9.6 %collective-permute-start.9 = (f32[64,1024]{1,0:T(8,128)S(1)}, f32[64,1024]{1,0:T(8,128)S(1)}, u32[]{:S(2)}, u32[]{:S(2)}) collective-permute-start(f32[64,1024]{1,0:T(8,128)S(1)} %get-tuple-element.41), channel_id=1, source_target_pairs={{0,12},{4,8},{8,4},{12,0},{16,28},{20,24},{24,20},{28,16},{1,13},{... | collective-permute-start | bytes 786440 | tf_op jit(solution)/shard_map/ppermute | solution.py:202
  41.1 18.4 %collective-permute-start.10 = (f32[32,1024]{1,0:T(8,128)S(1)}, f32[32,1024]{1,0:T(8,128)S(1)}, u32[]{:S(2)}, u32[]{:S(2)}) collective-permute-start(f32[32,1024]{1,0:T(8,128)S(1)} %get-tuple-element.44), channel_id=1, source_target_pairs={{0,16},{4,20},{8,24},{12,28},{16,0},{20,4},{24,8},{28,12},{1,17},{... | collective-permute-start | bytes 393224 | tf_op jit(solution)/shard_map/ppermute | solution.py:202
  43.0 19.3 %collective-permute-start.12 = (f32[32,1024]{1,0:T(8,128)S(1)}, f32[32,1024]{1,0:T(8,128)S(1)}, u32[]{:S(2)}, u32[]{:S(2)}) collective-permute-start(f32[32,1024]{1,0:T(8,128)S(1)} %get-tuple-element.46), channel_id=1, source_target_pairs={{0,16},{4,20},{8,24},{12,28},{16,0},{20,4},{24,8},{28,12},{1,17},{... | collective-permute-start | bytes 393224 | tf_op jit(solution)/shard_map/ppermute | solution.py:202
  44.1 21.1 %collective-permute-start.14 = (f32[32,1024]{1,0:T(8,128)S(1)}, f32[32,1024]{1,0:T(8,128)S(1)}, u32[]{:S(2)}, u32[]{:S(2)}) collective-permute-start(f32[32,1024]{1,0:T(8,128)S(1)} %get-tuple-element.48), channel_id=1, source_target_pairs={{0,16},{4,20},{8,24},{12,28},{16,0},{20,4},{24,8},{28,12},{1,17},{... | collective-permute-start | bytes 393224 | tf_op jit(solution)/shard_map/ppermute | solution.py:202
  45.9 21.0 %collective-permute-start.16 = (f32[32,1024]{1,0:T(8,128)S(1)}, f32[32,1024]{1,0:T(8,128)S(1)}, u32[]{:S(2)}, u32[]{:S(2)}) collective-permute-start(f32[32,1024]{1,0:T(8,128)S(1)} %get-tuple-element.49), channel_id=1, source_target_pairs={{0,16},{4,20},{8,24},{12,28},{16,0},{20,4},{24,8},{28,12},{1,17},{... | collective-permute-start | bytes 393224 | tf_op jit(solution)/shard_map/ppermute | solution.py:202
  59.6 7.4 %collective-permute-start.11 = (f32[32,1024]{1,0:T(8,128)S(1)}, f32[32,1024]{1,0:T(8,128)S(1)}, u32[]{:S(2)}, u32[]{:S(2)}) collective-permute-start(f32[32,1024]{1,0:T(8,128)S(1)} %add.36), channel_id=1, source_target_pairs={{0,4},{4,0},{8,12},{12,8},{16,20},{20,16},{24,28},{28,24},{1,5},{5... | collective-permute-start | bytes 393224 | tf_op jit(solution)/shard_map/ppermute | solution.py:202
  62.4 7.3 %collective-permute-start.13 = (f32[32,1024]{1,0:T(8,128)S(1)}, f32[32,1024]{1,0:T(8,128)S(1)}, u32[]{:S(2)}, u32[]{:S(2)}) collective-permute-start(f32[32,1024]{1,0:T(8,128)S(1)} %add.37), channel_id=1, source_target_pairs={{0,8},{4,12},{8,0},{12,4},{16,24},{20,28},{24,16},{28,20},{1,9},{5... | collective-permute-start | bytes 393224 | tf_op jit(solution)/shard_map/ppermute | solution.py:202
  65.3 8.1 %collective-permute-start.15 = (f32[32,1024]{1,0:T(8,128)S(1)}, f32[32,1024]{1,0:T(8,128)S(1)}, u32[]{:S(2)}, u32[]{:S(2)}) collective-permute-start(f32[32,1024]{1,0:T(8,128)S(1)} %add.38), channel_id=1, source_target_pairs={{0,12},{4,8},{8,4},{12,0},{16,28},{20,24},{24,20},{28,16},{1,13},{... | collective-permute-start | bytes 393224 | tf_op jit(solution)/shard_map/ppermute | solution.py:202

commit v5 on v4

--- a/solution.py
+++ b/solution.py
@@ -37,63 +37,64 @@
     )
 
 
-def project_kernel(snapshots_ref, factor_ref, partial_ref):
-    rows = snapshots_ref.shape[0]
-    high, low = split(snapshots_ref[...])
-    factor_high, factor_low = split(factor_ref[...])
-    both = dot(jnp.concatenate([high, low], axis=0), factor_high)
-    term = both[:rows] + (both[rows:] + dot(high, factor_low))
-
-    @pl.when(pl.program_id(0) == 0)
-    def _():
-        partial_ref[...] = term
-
-    @pl.when(pl.program_id(0) != 0)
-    def _():
-        partial_ref[...] += term
-
-
-def project(snapshots, space_factor):
+def project_kernel(depth, snapshots_ref, factor_ref, mine_ref, other_ref, *refs):
+    *parts, snapshots_buf, factor_buf, load_sems, part_sems = refs
+    rows, points = snapshots_ref.shape
+    half = rows // 2
+    loads = []
+    for i, start in enumerate(range(0, points, depth)):
+        span = pl.ds(start, depth)
+        loads.append(
+            (
+                pltpu.make_async_copy(snapshots_ref.at[:, span], snapshots_buf.at[:, span], load_sems.at[0, i]),
+                pltpu.make_async_copy(factor_ref.at[span, :], factor_buf.at[span, :], load_sems.at[1, i]),
+            )
+        )
+        for copy in loads[-1]:
+            copy.start()
+    width = parts[0].shape[1]
+    member = lax.rem(lax.axis_index("tm"), len(parts))
+    cuts = []
+    for k, part in enumerate(parts):
+        start = pl.multiple_of((member ^ k) * width, width)
+        cuts.append(pltpu.make_async_copy(snapshots_ref.at[:, pl.ds(start, width)], part, part_sems.at[k]))
+        cuts[-1].start()
+    value = None
+    for i, start in enumerate(range(0, points, depth)):
+        for copy in loads[i]:
+            copy.wait()
+        high, low = split(snapshots_buf[:, start : start + depth])
+        factor_high, factor_low = split(factor_buf[start : start + depth, :])
+        both = dot(jnp.concatenate([high, low], axis=0), factor_high)
+        term = both[:rows] + (both[rows:] + dot(high, factor_low))
+        value = term if value is None else value + term
+    first = lax.rem(lax.axis_index("space"), 2) == 0
+    mine_ref[...] = jnp.where(first, value[:half], value[half:])
+    other_ref[...] = jnp.where(first, value[half:], value[:half])
+    for copy in cuts:
+        copy.wait()
+
+
+def project(snapshots, space_factor, group):
     rows, points = snapshots.shape
     rank = space_factor.shape[1]
     depth = min(512, points)
-    return pl.pallas_call(
-        project_kernel,
-        grid=(points // depth,),
-        in_specs=[
-            pl.BlockSpec((rows, depth), lambda i: (0, i)),
-            pl.BlockSpec((depth, rank), lambda i: (i, 0)),
+    half = jax.ShapeDtypeStruct((rows // 2, rank), jnp.float32)
+    part = jax.ShapeDtypeStruct((rows, points // group), jnp.float32)
+    mine, other, *parts = pl.pallas_call(
+        functools.partial(project_kernel, depth),
+        in_specs=[ANY, ANY],
+        out_specs=[VMEM] * (2 + group),
+        out_shape=[half, half] + [part] * group,
+        scratch_shapes=[
+            pltpu.VMEM((rows, points), jnp.float32),
+            pltpu.VMEM((points, rank), jnp.float32),
+            pltpu.SemaphoreType.DMA((2, points // depth)),
+            pltpu.SemaphoreType.DMA((group,)),
         ],
-        out_specs=pl.BlockSpec((rows, rank), lambda i: (0, 0)),
-        out_shape=jax.ShapeDtypeStruct((rows, rank), jnp.float32),
         compiler_params=params(60),
     )(snapshots, space_factor)
-
-
-def cut_kernel(snapshots_ref, _, *refs):
-    *parts, sems = refs
-    width = parts[0].shape[1]
-    member = lax.rem(lax.axis_index("tm"), len(parts))
-    copies = []
-    for k, part in enumerate(parts):
-        start = pl.multiple_of((member ^ k) * width, width)
-        copies.append(pltpu.make_async_copy(snapshots_ref.at[:, pl.ds(start, width)], part, sems.at[k]))
-    for copy in copies:
-        copy.start()
-    for copy in copies:
-        copy.wait()
-
-
-def cut(snapshots, parts, after):
-    rows, points = snapshots.shape
-    return pl.pallas_call(
-        cut_kernel,
-        in_specs=[ANY, ANY],
-        out_specs=[ANY] * parts,
-        out_shape=[jax.ShapeDtypeStruct((rows, points // parts), jnp.float32)] * parts,
-        scratch_shapes=[pltpu.SemaphoreType.DMA((parts,))],
-        compiler_params=params(),
-    )(snapshots, after)
+    return mine, other, parts
 
 
 def mix_kernel(times, group, order, index_ref, mine_ref, theirs_ref, high_t_ref, low_t_ref, own_ref):
@@ -210,33 +211,34 @@
     index = lax.axis_index("tm")
     core = lax.axis_index("space") % 2
 
-    partial = project(snapshots, space_factor)
-    halves = partial.reshape(2, rows // 2, rank)
-    mine = lax.dynamic_index_in_dim(halves, core, 0, keepdims=False)
-    other = lax.dynamic_index_in_dim(halves, 1 - core, 0, keepdims=False)
+    mine, other, parts = project(snapshots, space_factor, group)
+    parts = [part if k == 0 else swap(part, "tm", k) for k, part in enumerate(parts)]
+
     terms = [mine] + [swap(other if k % 2 else mine, "space", k) for k in range(1, spaces)]
     while len(terms) > 1:
         terms = [a + b for a, b in zip(terms[::2], terms[1::2])]
 
-    pieces, *parts = lax.optimization_barrier((terms[0], *cut(snapshots, group, partial)))
-    parts = [part if k == 0 else swap(part, "tm", k) for k, part in enumerate(parts)]
-
-    order = [0]
+    pieces, order = terms[0], [0]
     offsets = [1 << i for i in range(times.bit_length() - 1)]
     for offset in [o for o in offsets if o >= group] + [o for o in offsets if o < group]:
         pieces = jnp.concatenate([pieces, swap(pieces, "tm", offset)], axis=0)
         if offset < group:
             pieces, parts[offset] = lax.optimization_barrier((pieces, parts[offset]))
         order = order + [k ^ offset for k in order]
-    high_t, low_t, own = mix(jnp.stack([index, core]), pieces, swap(pieces, "space", 1), times, group, order)
+    theirs, *parts = lax.optimization_barrier((swap(pieces, "space", 1), *parts))
+    high_t, low_t, own = mix(jnp.stack([index, core]), pieces, theirs, times, group, order)
 
     blocks = load(high_t, low_t, parts, times)
-    sums = []
-    for k in [*range(1, group), 0]:
-        sums.append([blocks[k]] + [swap(blocks[q + k], "tm", q) for q in range(group, times, group)])
-    received = [swap(sum(sums[k - 1][1:], sums[k - 1][0]), "tm", k) for k in range(1, group)]
-    last = sums[-1]
-    return own, join([last[0], *received], last[1:])
+    sums, arrived = {}, []
+    for i, k in enumerate(reversed(range(group))):
+        terms = [blocks[q + k] for q in range(group, times, group)]
+        if i >= 2:
+            terms, arrived[i - 2] = lax.optimization_barrier((terms, arrived[i - 2]))
+        arrived.append([swap(term, "tm", q) for term, q in zip(terms, range(group, times, group))])
+    received = []
+    for k in range(1, group):
+        received.append(swap(sum(arrived[group - 1 - k], blocks[k]), "tm", k))
+    return own, join([blocks[0], *received], arrived[-1])
 
 
 def solution(mesh):

time: 74.6 us -> 65.9 us (0.88)
  waiting for transfers between devices: 38.9 us -> 30 us
  starting transfers between devices: 22.3 us -> 25 us
  Pallas kernels: 10.5 us -> 8.06 us
  other arithmetic: 0.16 us -> 0.93 us
    ppermute x17, waiting for transfers between devices: 38.9 us -> 30 us  [swap(): lax.ppermute(value, axis, [(i, i ^ offset) for i in range(lax.axis_size(a...]
    ppermute x17, starting transfers between devices: 22.3 us -> 25 us  [swap(): lax.ppermute(value, axis, [(i, i ^ offset) for i in range(lax.axis_size(a...]
    pallas_call x2 -> x1, Pallas kernels: 6.57 us -> 4.17 us  [project(): pl.pallas_call(functools.partial(project_kernel, depth), in_specs=[ANY, A...]
    squeeze x1 -> x0, local copies, waits for them, and re-layouts: 0.78 us -> none  [on_device(): other = lax.dynamic_index_in_dim(halves, 1 - core, 0, keepdims=False)]
    add x1, other arithmetic: 0.01 us -> 0.77 us  [on_device(): terms = [a + b for a, b in zip(terms[::2], terms[1::2])]]
  transfers between devices with their start and end apart: 17 -> 17, of which waited for: 12 -> 10; matrix products, arithmetic and copies ran while one was open for 0% -> 0% of each run, Pallas kernels for 3% -> 0%
where the time goes in v5:
time: 65.9 us; the launch traced here: 65.6 us
  waiting for transfers between devices  30 us (46%)
  starting transfers between devices  25 us (38%)
  Pallas kernels  8.06 us (12%)
  local copies, waits for them, and re-layouts  0.95 us (1%)
  other arithmetic  0.93 us (1%)
  between operations  0.71 us (1%)
    ppermute x17, waiting for transfers between devices, swap(): lax.ppermute(value, axis, [(i, i ^ offset) for i in range(lax.axis_size(a...  30 us
    ppermute x17, starting transfers between devices, swap(): lax.ppermute(value, axis, [(i, i ^ offset) for i in range(lax.axis_size(a...  25 us
    pallas_call x1, Pallas kernels, project(): pl.pallas_call(functools.partial(project_kernel, depth), in_specs=[ANY, A...  4.17 us
    pallas_call x1, Pallas kernels, mix(): pl.pallas_call(functools.partial(mix_kernel, times, group, order), in_spe...  2.46 us
  transfers between devices with their start and end apart: 17, of which 10 were waited for; matrix products, arithmetic and copies ran while one was open for 0% of the time, Pallas kernels for 0%

profile of v5, /device:TPU:0, one launch (start us, length us, event | category | flops | bytes accessed | tf_op | source)
XLA Modules:
  0.0 65.6 jit_solution(2166269823554880304)
XLA Ops:
  0.6 4.2 %shard_map.41 = (f32[32,256]{1,0:T(8,128)}, f32[32,256]{1,0:T(8,128)}, f32[64,1024]{1,0:T(8,128)}, f32[64,1024]{1,0:T(8,128)}, f32[64,1024]{1,0:T(8,128)}, /*index=5*/f32[64,1024]{1,0:T(8,128)}) custom-call(f32[64,4096]{1,0:T(8,128)} %snapshots_ref.1, f32[4096,256]{1,0:T(8,128)} %factor_ref.1), custom_call_target="tpu_custom_call" | custom-call | tf_op jit(solution)/shard_map/pallas_call | solution.py:84
  4.8 3.0 %collective-permute-start.1 = (f32[32,256]{1,0:T(8,128)}, f32[32,256]{1,0:T(8,128)S(1)}, u32[]{:S(2)}, u32[]{:S(2)}) collective-permute-start(f32[32,256]{1,0:T(8,128)} %get-tuple-element.32), channel_id=1, source_target_pairs={{0,2},{1,3},{2,0},{3,1},{4,6},{5,7},{6,4},{7,5},{8,10},{9,11},{10,... | collective-permute-start | bytes 98312 | tf_op jit(solution)/shard_map/ppermute | solution.py:203
  7.8 0.0 collective-permute-start.2
  7.8 0.2 collective-permute-start
  8.0 1.9 %collective-permute-done.1 = f32[32,256]{1,0:T(8,128)S(1)} collective-permute-done((f32[32,256]{1,0:T(8,128)}, f32[32,256]{1,0:T(8,128)S(1)}, u32[]{:S(2)}, u32[]{:S(2)}) %collective-permute-start.1) | collective-permute-done | bytes 32800 | tf_op jit(solution)/shard_map/ppermute | solution.py:203
  9.9 1.5 %collective-permute-done.2 = f32[32,256]{1,0:T(8,128)S(1)} collective-permute-done((f32[32,256]{1,0:T(8,128)}, f32[32,256]{1,0:T(8,128)S(1)}, u32[]{:S(2)}, u32[]{:S(2)}) %collective-permute-start.2) | collective-permute-done | bytes 32800 | tf_op jit(solution)/shard_map/ppermute | solution.py:203
  11.5 0.0 collective-permute-done
  11.5 0.8 %add_add_fusion = f32[32,256]{1,0:T(8,128)S(1)} fusion(f32[32,256]{1,0:T(8,128)S(1)} %collective-permute-done.1, f32[32,256]{1,0:T(8,128)S(1)} %collective-permute-done.2, f32[32,256]{1,0:T(8,128)} %get-tuple-element.32, f32[32,256]{1,0:T(8,128)S(1)} %collective-permute-done), kind=kLoop, calls=%fused_computation.3 | loop fusion | flops 24576 | bytes 163840 | tf_op jit(solution)/shard_map/add | solution.py:219
  12.2 2.7 %collective-permute-start.3 = (f32[32,256]{1,0:T(8,128)S(1)}, f32[32,256]{1,0:T(8,128)S(1)}, u32[]{:S(2)}, u32[]{:S(2)}) collective-permute-start(f32[32,256]{1,0:T(8,128)S(1)} %add_add_fusion), channel_id=1, source_target_pairs={{0,16},{4,20},{8,24},{12,28},{16,0},{20,4},{24,8},{28,12},{1,17},{... | collective-permute-start | bytes 98312 | tf_op jit(solution)/shard_map/ppermute | solution.py:203
  14.9 1.5 %collective-permute-start.5 = (f32[64,1024]{1,0:T(8,128)}, f32[64,1024]{1,0:T(8,128)S(1)}, u32[]{:S(2)}, u32[]{:S(2)}) collective-permute-start(f32[64,1024]{1,0:T(8,128)} %get-tuple-element.34), channel_id=1, source_target_pairs={{0,4},{4,0},{8,12},{12,8},{16,20},{20,16},{24,28},{28,24},{1,5},{5... | collective-permute-start | bytes 786440 | tf_op jit(solution)/shard_map/ppermute | solution.py:203
  16.4 1.0 %collective-permute-done.3 = f32[32,256]{1,0:T(8,128)S(1)} collective-permute-done((f32[32,256]{1,0:T(8,128)S(1)}, f32[32,256]{1,0:T(8,128)S(1)}, u32[]{:S(2)}, u32[]{:S(2)}) %collective-permute-start.3) | collective-permute-done | bytes 32800 | tf_op jit(solution)/shard_map/ppermute | solution.py:203
  17.4 1.5 %collective-permute-start.4 = (f32[64,256]{1,0:T(8,128)S(1)}, f32[64,256]{1,0:T(8,128)S(1)}, u32[]{:S(2)}, u32[]{:S(2)}) collective-permute-start(f32[64,256]{1,0:T(8,128)S(1)} %pad_maximum_fusion.2), channel_id=1, source_target_pairs={{0,4},{4,0},{8,12},{12,8},{16,20},{20,16},{24,28},{28,24},{1,5},{5... | collective-permute-start | bytes 196616 | tf_op jit(solution)/shard_map/ppermute | solution.py:203
  18.9 1.3 %collective-permute-start.7 = (f32[64,1024]{1,0:T(8,128)}, f32[64,1024]{1,0:T(8,128)S(1)}, u32[]{:S(2)}, u32[]{:S(2)}) collective-permute-start(f32[64,1024]{1,0:T(8,128)} %get-tuple-element.36), channel_id=1, source_target_pairs={{0,8},{4,12},{8,0},{12,4},{16,24},{20,28},{24,16},{28,20},{1,9},{5... | collective-permute-start | bytes 786440 | tf_op jit(solution)/shard_map/ppermute | solution.py:203
  20.2 4.1 %collective-permute-done.4 = f32[64,256]{1,0:T(8,128)S(1)} collective-permute-done((f32[64,256]{1,0:T(8,128)S(1)}, f32[64,256]{1,0:T(8,128)S(1)}, u32[]{:S(2)}, u32[]{:S(2)}) %collective-permute-start.4) | collective-permute-done | bytes 65568 | tf_op jit(solution)/shard_map/ppermute | solution.py:203
  24.3 0.0 collective-permute-done.5.refs_1_
  24.3 1.6 %collective-permute-start.6 = (f32[128,256]{1,0:T(8,128)S(1)}, f32[128,256]{1,0:T(8,128)S(1)}, u32[]{:S(2)}, u32[]{:S(2)}) collective-permute-start(f32[128,256]{1,0:T(8,128)S(1)} %pad_maximum_fusion.1), channel_id=1, source_target_pairs={{0,8},{4,12},{8,0},{12,4},{16,24},{20,28},{24,16},{28,20},{1,9},{5... | collective-permute-start | bytes 393224 | tf_op jit(solution)/shard_map/ppermute | solution.py:203
  26.0 1.4 %collective-permute-start.9 = (f32[64,1024]{1,0:T(8,128)}, f32[64,1024]{1,0:T(8,128)S(1)}, u32[]{:S(2)}, u32[]{:S(2)}) collective-permute-start(f32[64,1024]{1,0:T(8,128)} %get-tuple-element.41), channel_id=1, source_target_pairs={{0,12},{4,8},{8,4},{12,0},{16,28},{20,24},{24,20},{28,16},{1,13},{... | collective-permute-start | bytes 786440 | tf_op jit(solution)/shard_map/ppermute | solution.py:203
  27.3 3.3 %collective-permute-done.6 = f32[128,256]{1,0:T(8,128)S(1)} collective-permute-done((f32[128,256]{1,0:T(8,128)S(1)}, f32[128,256]{1,0:T(8,128)S(1)}, u32[]{:S(2)}, u32[]{:S(2)}) %collective-permute-start.6) | collective-permute-done | bytes 131104 | tf_op jit(solution)/shard_map/ppermute | solution.py:203
  30.7 0.0 collective-permute-done.7.refs_2_
  30.7 0.1 collective-permute-start.8
  30.8 0.1 pad_add_fusion.index_ref
  30.8 4.2 %collective-permute-done.9.refs_3_ = f32[64,1024]{1,0:T(8,128)S(1)} collective-permute-done((f32[64,1024]{1,0:T(8,128)}, f32[64,1024]{1,0:T(8,128)S(1)}, u32[]{:S(2)}, u32[]{:S(2)}) %collective-permute-start.9) | collective-permute-done | bytes 262176 | tf_op jit(solution)/shard_map/ppermute | solution.py:203
  35.1 0.0 collective-permute-done.8.theirs_ref
  35.1 2.5 %shard_map.42 = (bf16[256,256]{1,0:T(8,128)(2,1)S(1)}, bf16[256,256]{1,0:T(8,128)(2,1)S(1)}, f32[64,256]{1,0:T(8,128)}) custom-call(s32[2]{0:T(128)S(1)} %pad_add_fusion.index_ref, f32[256,256]{1,0:T(8,128)S(1)} %pad_maximum_fusion.mine_ref, f32[256,256]{1,0:T(8,128)S(1)} %collective-permute-done.8.theirs_ref), custom_call_target="tpu_custom_call" | custom-call | tf_op jit(solution)/shard_map/pallas_call | solution.py:144
  37.5 0.0 copy-start
  37.5 0.9 %copy-done = f32[64,1024]{1,0:T(8,128)S(1)} copy-done((f32[64,1024]{1,0:T(8,128)S(1)}, f32[64,1024]{1,0:T(8,128)}, u32[]{:S(2)}) %copy-start) | copy-done | bytes 262168
  38.5 0.6 shard_map.43
  39.1 1.5 %collective-permute-start.10 = (f32[32,1024]{1,0:T(8,128)S(1)}, f32[32,1024]{1,0:T(8,128)S(1)}, u32[]{:S(2)}, u32[]{:S(2)}) collective-permute-start(f32[32,1024]{1,0:T(8,128)S(1)} %get-tuple-element.53), channel_id=1, source_target_pairs={{0,16},{4,20},{8,24},{12,28},{16,0},{20,4},{24,8},{28,12},{1,17},{... | collective-permute-start | bytes 393224 | tf_op jit(solution)/shard_map/ppermute | solution.py:203
  40.6 1.5 %collective-permute-start.13 = (f32[32,1024]{1,0:T(8,128)S(1)}, f32[32,1024]{1,0:T(8,128)S(1)}, u32[]{:S(2)}, u32[]{:S(2)}) collective-permute-start(f32[32,1024]{1,0:T(8,128)S(1)} %get-tuple-element.57), channel_id=1, source_target_pairs={{0,16},{4,20},{8,24},{12,28},{16,0},{20,4},{24,8},{28,12},{1,17},{... | collective-permute-start | bytes 393224 | tf_op jit(solution)/shard_map/ppermute | solution.py:203
  42.1 8.6 %collective-permute-done.10 = f32[32,1024]{1,0:T(8,128)S(1)} collective-permute-done((f32[32,1024]{1,0:T(8,128)S(1)}, f32[32,1024]{1,0:T(8,128)S(1)}, u32[]{:S(2)}, u32[]{:S(2)}) %collective-permute-start.10) | collective-permute-done | bytes 131104 | tf_op jit(solution)/shard_map/ppermute | solution.py:203
  50.7 0.0 collective-permute-start.11
  50.7 2.7 %collective-permute-start.15 = (f32[32,1024]{1,0:T(8,128)S(1)}, f32[32,1024]{1,0:T(8,128)S(1)}, u32[]{:S(2)}, u32[]{:S(2)}) collective-permute-start(f32[32,1024]{1,0:T(8,128)S(1)} %add.28), channel_id=1, source_target_pairs={{0,12},{4,8},{8,4},{12,0},{16,28},{20,24},{24,20},{28,16},{1,13},{... | collective-permute-start | bytes 393224 | tf_op jit(solution)/shard_map/ppermute | solution.py:203
  53.4 0.0 collective-permute-done.13
  53.5 1.3 %collective-permute-start.14 = (f32[32,1024]{1,0:T(8,128)S(1)}, f32[32,1024]{1,0:T(8,128)S(1)}, u32[]{:S(2)}, u32[]{:S(2)}) collective-permute-start(f32[32,1024]{1,0:T(8,128)S(1)} %add.27), channel_id=1, source_target_pairs={{0,8},{4,12},{8,0},{12,4},{16,24},{20,28},{24,16},{28,20},{1,9},{5... | collective-permute-start | bytes 393224 | tf_op jit(solution)/shard_map/ppermute | solution.py:203
  54.8 3.7 %collective-permute-start.16 = (f32[32,1024]{1,0:T(8,128)S(1)}, f32[32,1024]{1,0:T(8,128)S(1)}, u32[]{:S(2)}, u32[]{:S(2)}) collective-permute-start(f32[32,1024]{1,0:T(8,128)S(1)} %get-tuple-element.61), channel_id=1, source_target_pairs={{0,16},{4,20},{8,24},{12,28},{16,0},{20,4},{24,8},{28,12},{1,17},{... | collective-permute-start | bytes 393224 | tf_op jit(solution)/shard_map/ppermute | solution.py:203
  58.5 0.4 collective-permute-done.11
  58.9 0.9 %collective-permute-start.12 = (f32[32,1024]{1,0:T(8,128)S(1)}, f32[32,1024]{1,0:T(8,128)S(1)}, u32[]{:S(2)}, u32[]{:S(2)}) collective-permute-start(f32[32,1024]{1,0:T(8,128)S(1)} %add.26), channel_id=1, source_target_pairs={{0,4},{4,0},{8,12},{12,8},{16,20},{20,16},{24,28},{28,24},{1,5},{5... | collective-permute-start | bytes 393224 | tf_op jit(solution)/shard_map/ppermute | solution.py:203
  59.8 1.2 %collective-permute-done.15.refs_3_ = f32[32,1024]{1,0:T(8,128)S(1)} collective-permute-done((f32[32,1024]{1,0:T(8,128)S(1)}, f32[32,1024]{1,0:T(8,128)S(1)}, u32[]{:S(2)}, u32[]{:S(2)}) %collective-permute-start.15) | collective-permute-done | bytes 131104 | tf_op jit(solution)/shard_map/ppermute | solution.py:203
  61.1 3.7 %collective-permute-done.14.refs_2_ = f32[32,1024]{1,0:T(8,128)S(1)} collective-permute-done((f32[32,1024]{1,0:T(8,128)S(1)}, f32[32,1024]{1,0:T(8,128)S(1)}, u32[]{:S(2)}, u32[]{:S(2)}) %collective-permute-start.14) | collective-permute-done | bytes 131104 | tf_op jit(solution)/shard_map/ppermute | solution.py:203
  64.8 0.0 collective-permute-done.16.refs_4_
  64.8 0.0 collective-permute-done.12.refs_1_
  64.8 0.8 %shard_map.44 = f32[32,4096]{1,0:T(8,128)} custom-call(f32[32,1024]{1,0:T(8,128)S(1)} %get-tuple-element.50.refs_0_, f32[32,1024]{1,0:T(8,128)S(1)} %collective-permute-done.12.refs_1_, f32[32,1024]{1,0:T(8,128)S(1)} %collective-permute-done.14.refs_2_, f32[32,1024]{1,0:T(8,128)S(1)} %collective-permute-done.15.refs_3_, ...), custom_call_target="tpu_custom_call" | custom-call | tf_op jit(solution)/shard_map/pallas_call | solution.py:193
  (6 shorter events, 0.1 us)
Async XLA Ops:
  4.8 5.1 %collective-permute-start.1 = (f32[32,256]{1,0:T(8,128)}, f32[32,256]{1,0:T(8,128)S(1)}, u32[]{:S(2)}, u32[]{:S(2)}) collective-permute-start(f32[32,256]{1,0:T(8,128)} %get-tuple-element.32), channel_id=1, source_target_pairs={{0,2},{1,3},{2,0},{3,1},{4,6},{5,7},{6,4},{7,5},{8,10},{9,11},{10,... | collective-permute-start | bytes 98312 | tf_op jit(solution)/shard_map/ppermute | solution.py:203
  7.8 3.6 %collective-permute-start.2 = (f32[32,256]{1,0:T(8,128)}, f32[32,256]{1,0:T(8,128)S(1)}, u32[]{:S(2)}, u32[]{:S(2)}) collective-permute-start(f32[32,256]{1,0:T(8,128)} %get-tuple-element.33), channel_id=1, source_target_pairs={{0,3},{1,2},{2,1},{3,0},{4,7},{5,6},{6,5},{7,4},{8,11},{9,10},{10,... | collective-permute-start | bytes 98312 | tf_op jit(solution)/shard_map/ppermute | solution.py:203
  7.8 3.6 %collective-permute-start = (f32[32,256]{1,0:T(8,128)}, f32[32,256]{1,0:T(8,128)S(1)}, u32[]{:S(2)}, u32[]{:S(2)}) collective-permute-start(f32[32,256]{1,0:T(8,128)} %get-tuple-element.33), channel_id=1, source_target_pairs={{0,1},{1,0},{2,3},{3,2},{4,5},{5,4},{6,7},{7,6},{8,9},{9,8},{10,11... | collective-permute-start | bytes 98312 | tf_op jit(solution)/shard_map/ppermute | solution.py:203
  12.2 5.1 %collective-permute-start.3 = (f32[32,256]{1,0:T(8,128)S(1)}, f32[32,256]{1,0:T(8,128)S(1)}, u32[]{:S(2)}, u32[]{:S(2)}) collective-permute-start(f32[32,256]{1,0:T(8,128)S(1)} %add_add_fusion), channel_id=1, source_target_pairs={{0,16},{4,20},{8,24},{12,28},{16,0},{20,4},{24,8},{28,12},{1,17},{... | collective-permute-start | bytes 98312 | tf_op jit(solution)/shard_map/ppermute | solution.py:203
  14.9 9.4 %collective-permute-start.5 = (f32[64,1024]{1,0:T(8,128)}, f32[64,1024]{1,0:T(8,128)S(1)}, u32[]{:S(2)}, u32[]{:S(2)}) collective-permute-start(f32[64,1024]{1,0:T(8,128)} %get-tuple-element.34), channel_id=1, source_target_pairs={{0,4},{4,0},{8,12},{12,8},{16,20},{20,16},{24,28},{28,24},{1,5},{5... | collective-permute-start | bytes 786440 | tf_op jit(solution)/shard_map/ppermute | solution.py:203
  17.4 6.9 %collective-permute-start.4 = (f32[64,256]{1,0:T(8,128)S(1)}, f32[64,256]{1,0:T(8,128)S(1)}, u32[]{:S(2)}, u32[]{:S(2)}) collective-permute-start(f32[64,256]{1,0:T(8,128)S(1)} %pad_maximum_fusion.2), channel_id=1, source_target_pairs={{0,4},{4,0},{8,12},{12,8},{16,20},{20,16},{24,28},{28,24},{1,5},{5... | collective-permute-start | bytes 196616 | tf_op jit(solution)/shard_map/ppermute | solution.py:203
  18.9 11.8 %collective-permute-start.7 = (f32[64,1024]{1,0:T(8,128)}, f32[64,1024]{1,0:T(8,128)S(1)}, u32[]{:S(2)}, u32[]{:S(2)}) collective-permute-start(f32[64,1024]{1,0:T(8,128)} %get-tuple-element.36), channel_id=1, source_target_pairs={{0,8},{4,12},{8,0},{12,4},{16,24},{20,28},{24,16},{28,20},{1,9},{5... | collective-permute-start | bytes 786440 | tf_op jit(solution)/shard_map/ppermute | solution.py:203
  24.3 6.3 %collective-permute-start.6 = (f32[128,256]{1,0:T(8,128)S(1)}, f32[128,256]{1,0:T(8,128)S(1)}, u32[]{:S(2)}, u32[]{:S(2)}) collective-permute-start(f32[128,256]{1,0:T(8,128)S(1)} %pad_maximum_fusion.1), channel_id=1, source_target_pairs={{0,8},{4,12},{8,0},{12,4},{16,24},{20,28},{24,16},{28,20},{1,9},{5... | collective-permute-start | bytes 393224 | tf_op jit(solution)/shard_map/ppermute | solution.py:203
  26.0 9.1 %collective-permute-start.9 = (f32[64,1024]{1,0:T(8,128)}, f32[64,1024]{1,0:T(8,128)S(1)}, u32[]{:S(2)}, u32[]{:S(2)}) collective-permute-start(f32[64,1024]{1,0:T(8,128)} %get-tuple-element.41), channel_id=1, source_target_pairs={{0,12},{4,8},{8,4},{12,0},{16,28},{20,24},{24,20},{28,16},{1,13},{... | collective-permute-start | bytes 786440 | tf_op jit(solution)/shard_map/ppermute | solution.py:203
  30.7 4.4 %collective-permute-start.8 = (f32[256,256]{1,0:T(8,128)S(1)}, f32[256,256]{1,0:T(8,128)S(1)}, u32[]{:S(2)}, u32[]{:S(2)}) collective-permute-start(f32[256,256]{1,0:T(8,128)S(1)} %pad_maximum_fusion.mine_ref), channel_id=1, source_target_pairs={{0,1},{1,0},{2,3},{3,2},{4,5},{5,4},{6,7},{7,6},{8,9},{9,8},{10,11... | collective-permute-start | bytes 786440 | tf_op jit(solution)/shard_map/ppermute | solution.py:203
  37.5 0.9 %copy-start = (f32[64,1024]{1,0:T(8,128)S(1)}, f32[64,1024]{1,0:T(8,128)}, u32[]{:S(2)}) copy-start(f32[64,1024]{1,0:T(8,128)} %get-tuple-element.46.refs_0_) | copy-start | bytes 786436
  39.1 11.6 %collective-permute-start.10 = (f32[32,1024]{1,0:T(8,128)S(1)}, f32[32,1024]{1,0:T(8,128)S(1)}, u32[]{:S(2)}, u32[]{:S(2)}) collective-permute-start(f32[32,1024]{1,0:T(8,128)S(1)} %get-tuple-element.53), channel_id=1, source_target_pairs={{0,16},{4,20},{8,24},{12,28},{16,0},{20,4},{24,8},{28,12},{1,17},{... | collective-permute-start | bytes 393224 | tf_op jit(solution)/shard_map/ppermute | solution.py:203
  40.6 12.9 %collective-permute-start.13 = (f32[32,1024]{1,0:T(8,128)S(1)}, f32[32,1024]{1,0:T(8,128)S(1)}, u32[]{:S(2)}, u32[]{:S(2)}) collective-permute-start(f32[32,1024]{1,0:T(8,128)S(1)} %get-tuple-element.57), channel_id=1, source_target_pairs={{0,16},{4,20},{8,24},{12,28},{16,0},{20,4},{24,8},{28,12},{1,17},{... | collective-permute-start | bytes 393224 | tf_op jit(solution)/shard_map/ppermute | solution.py:203
  50.7 8.2 %collective-permute-start.11 = (f32[32,1024]{1,0:T(8,128)S(1)}, f32[32,1024]{1,0:T(8,128)S(1)}, u32[]{:S(2)}, u32[]{:S(2)}) collective-permute-start(f32[32,1024]{1,0:T(8,128)S(1)} %get-tuple-element.54), channel_id=1, source_target_pairs={{0,16},{4,20},{8,24},{12,28},{16,0},{20,4},{24,8},{28,12},{1,17},{... | collective-permute-start | bytes 393224 | tf_op jit(solution)/shard_map/ppermute | solution.py:203
  50.7 10.4 %collective-permute-start.15 = (f32[32,1024]{1,0:T(8,128)S(1)}, f32[32,1024]{1,0:T(8,128)S(1)}, u32[]{:S(2)}, u32[]{:S(2)}) collective-permute-start(f32[32,1024]{1,0:T(8,128)S(1)} %add.28), channel_id=1, source_target_pairs={{0,12},{4,8},{8,4},{12,0},{16,28},{20,24},{24,20},{28,16},{1,13},{... | collective-permute-start | bytes 393224 | tf_op jit(solution)/shard_map/ppermute | solution.py:203
  53.5 11.3 %collective-permute-start.14 = (f32[32,1024]{1,0:T(8,128)S(1)}, f32[32,1024]{1,0:T(8,128)S(1)}, u32[]{:S(2)}, u32[]{:S(2)}) collective-permute-start(f32[32,1024]{1,0:T(8,128)S(1)} %add.27), channel_id=1, source_target_pairs={{0,8},{4,12},{8,0},{12,4},{16,24},{20,28},{24,16},{28,20},{1,9},{5... | collective-permute-start | bytes 393224 | tf_op jit(solution)/shard_map/ppermute | solution.py:203
  54.8 10.0 %collective-permute-start.16 = (f32[32,1024]{1,0:T(8,128)S(1)}, f32[32,1024]{1,0:T(8,128)S(1)}, u32[]{:S(2)}, u32[]{:S(2)}) collective-permute-start(f32[32,1024]{1,0:T(8,128)S(1)} %get-tuple-element.61), channel_id=1, source_target_pairs={{0,16},{4,20},{8,24},{12,28},{16,0},{20,4},{24,8},{28,12},{1,17},{... | collective-permute-start | bytes 393224 | tf_op jit(solution)/shard_map/ppermute | solution.py:203
  58.9 5.9 %collective-permute-start.12 = (f32[32,1024]{1,0:T(8,128)S(1)}, f32[32,1024]{1,0:T(8,128)S(1)}, u32[]{:S(2)}, u32[]{:S(2)}) collective-permute-start(f32[32,1024]{1,0:T(8,128)S(1)} %add.26), channel_id=1, source_target_pairs={{0,4},{4,0},{8,12},{12,8},{16,20},{20,16},{24,28},{28,24},{1,5},{5... | collective-permute-start | bytes 393224 | tf_op jit(solution)/shard_map/ppermute | solution.py:203

commit v6 on v5

--- a/solution.py
+++ b/solution.py
@@ -9,7 +9,7 @@
 from jax.sharding import PartitionSpec as P
 
 MIB = 1024 * 1024
-ANY = pl.BlockSpec(memory_space=pl.ANY)
+HBM = pl.BlockSpec(memory_space=pltpu.HBM)
 SMEM = pl.BlockSpec(memory_space=pltpu.SMEM)
 VMEM = pl.BlockSpec(memory_space=pltpu.VMEM)
 ROWS_BY_ROWS = (((0,), (0,)), ((), ()))
@@ -38,31 +38,24 @@
 
 
 def project_kernel(depth, snapshots_ref, factor_ref, mine_ref, other_ref, *refs):
-    *parts, snapshots_buf, factor_buf, load_sems, part_sems = refs
+    *parts, snapshots_buf, factor_buf, sems = refs
     rows, points = snapshots_ref.shape
     half = rows // 2
-    loads = []
+    snapshots_copy = pltpu.make_async_copy(snapshots_ref, snapshots_buf, sems.at[points // depth])
+    snapshots_copy.start()
+    copies = []
     for i, start in enumerate(range(0, points, depth)):
         span = pl.ds(start, depth)
-        loads.append(
-            (
-                pltpu.make_async_copy(snapshots_ref.at[:, span], snapshots_buf.at[:, span], load_sems.at[0, i]),
-                pltpu.make_async_copy(factor_ref.at[span, :], factor_buf.at[span, :], load_sems.at[1, i]),
-            )
-        )
-        for copy in loads[-1]:
-            copy.start()
+        copies.append(pltpu.make_async_copy(factor_ref.at[span, :], factor_buf.at[span, :], sems.at[i]))
+        copies[-1].start()
+    snapshots_copy.wait()
     width = parts[0].shape[1]
     member = lax.rem(lax.axis_index("tm"), len(parts))
-    cuts = []
     for k, part in enumerate(parts):
-        start = pl.multiple_of((member ^ k) * width, width)
-        cuts.append(pltpu.make_async_copy(snapshots_ref.at[:, pl.ds(start, width)], part, part_sems.at[k]))
-        cuts[-1].start()
+        part[...] = snapshots_buf[:, pl.ds(pl.multiple_of((member ^ k) * width, width), width)]
     value = None
     for i, start in enumerate(range(0, points, depth)):
-        for copy in loads[i]:
-            copy.wait()
+        copies[i].wait()
         high, low = split(snapshots_buf[:, start : start + depth])
         factor_high, factor_low = split(factor_buf[start : start + depth, :])
         both = dot(jnp.concatenate([high, low], axis=0), factor_high)
@@ -71,8 +64,6 @@
     first = lax.rem(lax.axis_index("space"), 2) == 0
     mine_ref[...] = jnp.where(first, value[:half], value[half:])
     other_ref[...] = jnp.where(first, value[half:], value[:half])
-    for copy in cuts:
-        copy.wait()
 
 
 def project(snapshots, space_factor, group):
@@ -83,21 +74,21 @@
     part = jax.ShapeDtypeStruct((rows, points // group), jnp.float32)
     mine, other, *parts = pl.pallas_call(
         functools.partial(project_kernel, depth),
-        in_specs=[ANY, ANY],
+        in_specs=[HBM, HBM],
         out_specs=[VMEM] * (2 + group),
         out_shape=[half, half] + [part] * group,
         scratch_shapes=[
             pltpu.VMEM((rows, points), jnp.float32),
             pltpu.VMEM((points, rank), jnp.float32),
-            pltpu.SemaphoreType.DMA((2, points // depth)),
-            pltpu.SemaphoreType.DMA((group,)),
+            pltpu.SemaphoreType.DMA((points // depth + 1,)),
         ],
-        compiler_params=params(60),
+        compiler_params=params(52),
     )(snapshots, space_factor)
     return mine, other, parts
 
 
-def mix_kernel(times, group, order, index_ref, mine_ref, theirs_ref, high_t_ref, low_t_ref, own_ref):
+def load_kernel(times, group, order, index_ref, mine_ref, theirs_ref, *refs):
+    parts, own_ref, blocks = refs[:group], refs[group], refs[group + 1 :]
     total_half, rank = mine_ref.shape
     half = total_half // times
     mine = mine_ref[...].reshape(times, half, rank)
@@ -133,46 +124,26 @@
     move = jnp.where(source == lax.broadcasted_iota(jnp.int32, (rank, rank), 1), 1.0, 0.0).astype(jnp.bfloat16)
     moved = dot(move, jnp.concatenate([mixing_high, mixing_low], axis=1)).astype(jnp.bfloat16)
     turned = product((moved[:, :rank], moved[:, rank:]), (high, low), COLUMNS_BY_COLUMNS) * scale
-    turned_high, turned_low = split(turned)
-    high_t_ref[...] = turned_high
-    low_t_ref[...] = turned_low
-
-
-def mix(index, mine, theirs, times, group, order):
+    columns = jnp.concatenate([part[...] for part in parts], axis=0)
+    value = product(split(turned), split(columns))
+    for i, block in enumerate(blocks):
+        block[...] = value[i * width : (i + 1) * width]
+
+
+def load(index, mine, theirs, parts, times, order):
     total_half, rank = mine.shape
     rows = 2 * total_half // times
-    return pl.pallas_call(
-        functools.partial(mix_kernel, times, group, order),
-        in_specs=[SMEM, VMEM, VMEM],
-        out_specs=[VMEM] * 3,
-        out_shape=[
-            jax.ShapeDtypeStruct((rank, group * rows), jnp.bfloat16),
-            jax.ShapeDtypeStruct((rank, group * rows), jnp.bfloat16),
-            jax.ShapeDtypeStruct((rows, rank), jnp.float32),
-        ],
+    group = len(parts)
+    columns = parts[0].shape[1]
+    own, *blocks = pl.pallas_call(
+        functools.partial(load_kernel, times, group, order),
+        in_specs=[SMEM] + [VMEM] * (2 + group),
+        out_specs=[VMEM] * (1 + times),
+        out_shape=[jax.ShapeDtypeStruct((rows, rank), jnp.float32)]
+        + [jax.ShapeDtypeStruct((rank // times, columns), jnp.float32)] * times,
         compiler_params=params(),
-    )(index, mine, theirs)
-
-
-def load_kernel(group, high_ref, low_ref, *refs):
-    parts, blocks = refs[:group], refs[group:]
-    columns = jnp.concatenate([part[...] for part in parts], axis=0)
-    value = product((high_ref[...], low_ref[...]), split(columns))
-    width = value.shape[0] // len(blocks)
-    for i, block in enumerate(blocks):
-        block[...] = value[i * width : (i + 1) * width]
-
-
-def load(high, low, parts, blocks):
-    rank = high.shape[0]
-    columns = parts[0].shape[1]
-    return pl.pallas_call(
-        functools.partial(load_kernel, len(parts)),
-        in_specs=[VMEM] * (2 + len(parts)),
-        out_specs=[VMEM] * blocks,
-        out_shape=[jax.ShapeDtypeStruct((rank // blocks, columns), jnp.float32)] * blocks,
-        compiler_params=params(),
-    )(high, low, *parts)
+    )(index, mine, theirs, *parts)
+    return own, blocks
 
 
 def join_kernel(group, *refs):
@@ -222,14 +193,15 @@
     offsets = [1 << i for i in range(times.bit_length() - 1)]
     for offset in [o for o in offsets if o >= group] + [o for o in offsets if o < group]:
         pieces = jnp.concatenate([pieces, swap(pieces, "tm", offset)], axis=0)
-        if offset < group:
-            pieces, parts[offset] = lax.optimization_barrier((pieces, parts[offset]))
+        if len(order) == 1:
+            pieces, parts[1:-1] = lax.optimization_barrier((pieces, parts[1:-1]))
+        elif len(order) == 2:
+            pieces, parts[-1] = lax.optimization_barrier((pieces, parts[-1]))
         order = order + [k ^ offset for k in order]
-    theirs, *parts = lax.optimization_barrier((swap(pieces, "space", 1), *parts))
-    high_t, low_t, own = mix(jnp.stack([index, core]), pieces, theirs, times, group, order)
-
-    blocks = load(high_t, low_t, parts, times)
-    sums, arrived = {}, []
+    theirs = swap(pieces, "space", 1)
+
+    own, blocks = load(jnp.stack([index, core]), pieces, theirs, parts, times, order)
+    arrived = []
     for i, k in enumerate(reversed(range(group))):
         terms = [blocks[q + k] for q in range(group, times, group)]
         if i >= 2:

time: 65.9 us -> 63.5 us (0.964)
  Pallas kernels: 8.06 us -> 6.8 us
  starting transfers between devices: 25 us -> 26.2 us
  local copies, waits for them, and re-layouts: 0.95 us -> 0.02 us
  other arithmetic: 0.93 us -> 0.16 us
    pallas_call x3 -> x2, Pallas kernels: 7.21 us -> 5.96 us  [the longest x1 3.03 us: load(): pl.pallas_call(functools.partial(load_kernel, times, group, order), in_sp...]
    ppermute x17, starting transfers between devices: 25 us -> 26.2 us  [swap(): lax.ppermute(value, axis, [(i, i ^ offset) for i in range(lax.axis_size(a...]
    unnamed x2 -> x1, local copies, waits for them, and re-layouts: 0.95 us -> 0.01 us
    add x1, other arithmetic: 0.77 us -> 0.01 us  [on_device(): terms = [a + b for a, b in zip(terms[::2], terms[1::2])]]
  transfers between devices with their start and end apart: 17 -> 17, of which waited for: 10 -> 8; matrix products, arithmetic and copies ran while one was open for 0% -> 0% of each run, Pallas kernels for 0% -> 0%
where the time goes in v6:
time: 63.5 us; the launch traced here: 63.3 us
  waiting for transfers between devices  29.5 us (46%)
  starting transfers between devices  26.2 us (41%)
  Pallas kernels  6.8 us (11%)
  between operations  0.71 us (1%)
    ppermute x17, waiting for transfers between devices, swap(): lax.ppermute(value, axis, [(i, i ^ offset) for i in range(lax.axis_size(a...  29.5 us
    ppermute x17, starting transfers between devices, swap(): lax.ppermute(value, axis, [(i, i ^ offset) for i in range(lax.axis_size(a...  26.2 us
    pallas_call x1, Pallas kernels, load(): pl.pallas_call(functools.partial(load_kernel, times, group, order), in_sp...  3.03 us
    pallas_call x1, Pallas kernels, project(): pl.pallas_call(functools.partial(project_kernel, depth), in_specs=[HBM, H...  2.93 us
  transfers between devices with their start and end apart: 17, of which 8 were waited for; matrix products, arithmetic and copies ran while one was open for 0% of the time, Pallas kernels for 0%

profile of v6, /device:TPU:0, one launch (start us, length us, event | category | flops | bytes accessed | tf_op | source)
XLA Modules:
  0.0 63.3 jit_solution(4059652815184236749)
XLA Ops:
  0.6 2.9 %shard_map.41 = (f32[32,256]{1,0:T(8,128)S(1)}, f32[32,256]{1,0:T(8,128)S(1)}, f32[64,1024]{1,0:T(8,128)S(1)}, f32[64,1024]{1,0:T(8,128)S(1)}, f32[64,1024]{1,0:T(8,128)S(1)}, /*index=5*/f32[64,1024]{1,0:T(8,128)S(1)}) custom-call(f32[64,4096]{1,0:T(8,128)} %snapshots_ref.1, f32[4096,256]{1,0:T(8,128)} %factor_ref.1), custom_call_target="tpu_custom_call" | custom-call | tf_op jit(solution)/shard_map/pallas_call | solution.py:75
  3.6 3.0 %collective-permute-start.1 = (f32[32,256]{1,0:T(8,128)S(1)}, f32[32,256]{1,0:T(8,128)S(1)}, u32[]{:S(2)}, u32[]{:S(2)}) collective-permute-start(f32[32,256]{1,0:T(8,128)S(1)} %get-tuple-element.26), channel_id=1, source_target_pairs={{0,2},{1,3},{2,0},{3,1},{4,6},{5,7},{6,4},{7,5},{8,10},{9,11},{10,... | collective-permute-start | bytes 98312 | tf_op jit(solution)/shard_map/ppermute | solution.py:174
  6.6 0.0 collective-permute-start.2
  6.6 0.2 collective-permute-start
  6.8 1.9 %collective-permute-start.4 = (f32[64,1024]{1,0:T(8,128)S(1)}, f32[64,1024]{1,0:T(8,128)S(1)}, u32[]{:S(2)}, u32[]{:S(2)}) collective-permute-start(f32[64,1024]{1,0:T(8,128)S(1)} %get-tuple-element.28), channel_id=1, source_target_pairs={{0,4},{4,0},{8,12},{12,8},{16,20},{20,16},{24,28},{28,24},{1,5},{5... | collective-permute-start | bytes 786440 | tf_op jit(solution)/shard_map/ppermute | solution.py:174
  8.7 1.6 %collective-permute-start.5 = (f32[64,1024]{1,0:T(8,128)S(1)}, f32[64,1024]{1,0:T(8,128)S(1)}, u32[]{:S(2)}, u32[]{:S(2)}) collective-permute-start(f32[64,1024]{1,0:T(8,128)S(1)} %get-tuple-element.29), channel_id=1, source_target_pairs={{0,8},{4,12},{8,0},{12,4},{16,24},{20,28},{24,16},{28,20},{1,9},{5... | collective-permute-start | bytes 786440 | tf_op jit(solution)/shard_map/ppermute | solution.py:174
  10.3 0.0 collective-permute-done.1
  10.3 0.0 collective-permute-done.2
  10.3 0.0 collective-permute-done
  10.3 2.7 %collective-permute-start.3 = (f32[32,256]{1,0:T(8,128)S(1)}, f32[32,256]{1,0:T(8,128)S(1)}, u32[]{:S(2)}, u32[]{:S(2)}) collective-permute-start(f32[32,256]{1,0:T(8,128)S(1)} %add_add_fusion), channel_id=1, source_target_pairs={{0,16},{4,20},{8,24},{12,28},{16,0},{20,4},{24,8},{28,12},{1,17},{... | collective-permute-start | bytes 98312 | tf_op jit(solution)/shard_map/ppermute | solution.py:174
  13.0 2.2 %collective-permute-start.7 = (f32[64,1024]{1,0:T(8,128)S(1)}, f32[64,1024]{1,0:T(8,128)S(1)}, u32[]{:S(2)}, u32[]{:S(2)}) collective-permute-start(f32[64,1024]{1,0:T(8,128)S(1)} %get-tuple-element.31), channel_id=1, source_target_pairs={{0,12},{4,8},{8,4},{12,0},{16,28},{20,24},{24,20},{28,16},{1,13},{... | collective-permute-start | bytes 786440 | tf_op jit(solution)/shard_map/ppermute | solution.py:174
  15.2 2.5 %collective-permute-done.3 = f32[32,256]{1,0:T(8,128)S(1)} collective-permute-done((f32[32,256]{1,0:T(8,128)S(1)}, f32[32,256]{1,0:T(8,128)S(1)}, u32[]{:S(2)}, u32[]{:S(2)}) %collective-permute-start.3) | collective-permute-done | bytes 32800 | tf_op jit(solution)/shard_map/ppermute | solution.py:174
  17.7 0.0 collective-permute-done.4.refs_1_
  17.7 0.9 %collective-permute-done.5.refs_2_ = f32[64,1024]{1,0:T(8,128)S(1)} collective-permute-done((f32[64,1024]{1,0:T(8,128)S(1)}, f32[64,1024]{1,0:T(8,128)S(1)}, u32[]{:S(2)}, u32[]{:S(2)}) %collective-permute-start.5) | collective-permute-done | bytes 262176 | tf_op jit(solution)/shard_map/ppermute | solution.py:174
  18.6 0.1 collective-permute-start.6
  18.7 5.5 %collective-permute-done.6 = f32[64,256]{1,0:T(8,128)S(1)} collective-permute-done((f32[64,256]{1,0:T(8,128)S(1)}, f32[64,256]{1,0:T(8,128)S(1)}, u32[]{:S(2)}, u32[]{:S(2)}) %collective-permute-start.6) | collective-permute-done | bytes 65568 | tf_op jit(solution)/shard_map/ppermute | solution.py:174
  24.2 0.0 collective-permute-done.7.refs_3_
  24.3 1.8 %collective-permute-start.8 = (f32[128,256]{1,0:T(8,128)S(1)}, f32[128,256]{1,0:T(8,128)S(1)}, u32[]{:S(2)}, u32[]{:S(2)}) collective-permute-start(f32[128,256]{1,0:T(8,128)S(1)} %pad_maximum_fusion), channel_id=1, source_target_pairs={{0,8},{4,12},{8,0},{12,4},{16,24},{20,28},{24,16},{28,20},{1,9},{5... | collective-permute-start | bytes 393224 | tf_op jit(solution)/shard_map/ppermute | solution.py:174
  26.0 3.7 %collective-permute-done.8 = f32[128,256]{1,0:T(8,128)S(1)} collective-permute-done((f32[128,256]{1,0:T(8,128)S(1)}, f32[128,256]{1,0:T(8,128)S(1)}, u32[]{:S(2)}, u32[]{:S(2)}) %collective-permute-start.8) | collective-permute-done | bytes 131104 | tf_op jit(solution)/shard_map/ppermute | solution.py:174
  29.8 0.1 collective-permute-start.9
  29.8 0.1 pad_add_fusion.index_ref
  29.9 1.4 %collective-permute-done.9.theirs_ref = f32[256,256]{1,0:T(8,128)S(1)} collective-permute-done((f32[256,256]{1,0:T(8,128)S(1)}, f32[256,256]{1,0:T(8,128)S(1)}, u32[]{:S(2)}, u32[]{:S(2)}) %collective-permute-start.9) | collective-permute-done | bytes 262176 | tf_op jit(solution)/shard_map/ppermute | solution.py:174
  31.4 3.0 %shard_map.42 = (f32[64,256]{1,0:T(8,128)}, f32[32,1024]{1,0:T(8,128)S(1)}, f32[32,1024]{1,0:T(8,128)S(1)}, f32[32,1024]{1,0:T(8,128)S(1)}, f32[32,1024]{1,0:T(8...) custom-call(s32[2]{0:T(128)S(1)} %pad_add_fusion.index_ref, ...), custom_call_target="tpu_custom_call" | custom-call | tf_op jit(solution)/shard_map/pallas_call | solution.py:138
  34.4 2.5 %collective-permute-start.10 = (f32[32,1024]{1,0:T(8,128)S(1)}, f32[32,1024]{1,0:T(8,128)S(1)}, u32[]{:S(2)}, u32[]{:S(2)}) collective-permute-start(f32[32,1024]{1,0:T(8,128)S(1)} %get-tuple-element.41), channel_id=1, source_target_pairs={{0,16},{4,20},{8,24},{12,28},{16,0},{20,4},{24,8},{28,12},{1,17},{... | collective-permute-start | bytes 393224 | tf_op jit(solution)/shard_map/ppermute | solution.py:174
  36.9 0.4 collective-permute-start.13
  37.3 9.9 %collective-permute-done.10 = f32[32,1024]{1,0:T(8,128)S(1)} collective-permute-done((f32[32,1024]{1,0:T(8,128)S(1)}, f32[32,1024]{1,0:T(8,128)S(1)}, u32[]{:S(2)}, u32[]{:S(2)}) %collective-permute-start.10) | collective-permute-done | bytes 131104 | tf_op jit(solution)/shard_map/ppermute | solution.py:174
  47.2 0.0 collective-permute-start.11
  47.3 3.4 %collective-permute-start.15 = (f32[32,1024]{1,0:T(8,128)S(1)}, f32[32,1024]{1,0:T(8,128)S(1)}, u32[]{:S(2)}, u32[]{:S(2)}) collective-permute-start(f32[32,1024]{1,0:T(8,128)S(1)} %add.28), channel_id=1, source_target_pairs={{0,12},{4,8},{8,4},{12,0},{16,28},{20,24},{24,20},{28,16},{1,13},{... | collective-permute-start | bytes 393224 | tf_op jit(solution)/shard_map/ppermute | solution.py:174
  50.7 0.0 collective-permute-done.13
  50.7 2.2 %collective-permute-start.14 = (f32[32,1024]{1,0:T(8,128)S(1)}, f32[32,1024]{1,0:T(8,128)S(1)}, u32[]{:S(2)}, u32[]{:S(2)}) collective-permute-start(f32[32,1024]{1,0:T(8,128)S(1)} %add.27), channel_id=1, source_target_pairs={{0,8},{4,12},{8,0},{12,4},{16,24},{20,28},{24,16},{28,20},{1,9},{5... | collective-permute-start | bytes 393224 | tf_op jit(solution)/shard_map/ppermute | solution.py:174
  52.9 3.4 %collective-permute-start.16 = (f32[32,1024]{1,0:T(8,128)S(1)}, f32[32,1024]{1,0:T(8,128)S(1)}, u32[]{:S(2)}, u32[]{:S(2)}) collective-permute-start(f32[32,1024]{1,0:T(8,128)S(1)} %get-tuple-element.49), channel_id=1, source_target_pairs={{0,16},{4,20},{8,24},{12,28},{16,0},{20,4},{24,8},{28,12},{1,17},{... | collective-permute-start | bytes 393224 | tf_op jit(solution)/shard_map/ppermute | solution.py:174
  56.3 0.0 collective-permute-done.11
  56.4 0.7 %collective-permute-start.12 = (f32[32,1024]{1,0:T(8,128)S(1)}, f32[32,1024]{1,0:T(8,128)S(1)}, u32[]{:S(2)}, u32[]{:S(2)}) collective-permute-start(f32[32,1024]{1,0:T(8,128)S(1)} %add.26), channel_id=1, source_target_pairs={{0,4},{4,0},{8,12},{12,8},{16,20},{20,16},{24,28},{28,24},{1,5},{5... | collective-permute-start | bytes 393224 | tf_op jit(solution)/shard_map/ppermute | solution.py:174
  57.1 0.0 collective-permute-done.15.refs_3_
  57.1 3.7 %collective-permute-done.14.refs_2_ = f32[32,1024]{1,0:T(8,128)S(1)} collective-permute-done((f32[32,1024]{1,0:T(8,128)S(1)}, f32[32,1024]{1,0:T(8,128)S(1)}, u32[]{:S(2)}, u32[]{:S(2)}) %collective-permute-start.14) | collective-permute-done | bytes 131104 | tf_op jit(solution)/shard_map/ppermute | solution.py:174
  60.8 1.7 %collective-permute-done.16.refs_4_ = f32[32,1024]{1,0:T(8,128)S(1)} collective-permute-done((f32[32,1024]{1,0:T(8,128)S(1)}, f32[32,1024]{1,0:T(8,128)S(1)}, u32[]{:S(2)}, u32[]{:S(2)}) %collective-permute-start.16) | collective-permute-done | bytes 131104 | tf_op jit(solution)/shard_map/ppermute | solution.py:174
  62.5 0.0 collective-permute-done.12.refs_1_
  62.5 0.8 %shard_map.43 = f32[32,4096]{1,0:T(8,128)} custom-call(f32[32,1024]{1,0:T(8,128)S(1)} %get-tuple-element.38.refs_0_, f32[32,1024]{1,0:T(8,128)S(1)} %collective-permute-done.12.refs_1_, f32[32,1024]{1,0:T(8,128)S(1)} %collective-permute-done.14.refs_2_, f32[32,1024]{1,0:T(8,128)S(1)} %collective-permute-done.15.refs_3_, ...), custom_call_target="tpu_custom_call" | custom-call | tf_op jit(solution)/shard_map/pallas_call | solution.py:164
  (8 shorter events, 0.1 us)
Async XLA Ops:
  3.6 6.7 %collective-permute-start.1 = (f32[32,256]{1,0:T(8,128)S(1)}, f32[32,256]{1,0:T(8,128)S(1)}, u32[]{:S(2)}, u32[]{:S(2)}) collective-permute-start(f32[32,256]{1,0:T(8,128)S(1)} %get-tuple-element.26), channel_id=1, source_target_pairs={{0,2},{1,3},{2,0},{3,1},{4,6},{5,7},{6,4},{7,5},{8,10},{9,11},{10,... | collective-permute-start | bytes 98312 | tf_op jit(solution)/shard_map/ppermute | solution.py:174
  6.6 3.7 %collective-permute-start.2 = (f32[32,256]{1,0:T(8,128)S(1)}, f32[32,256]{1,0:T(8,128)S(1)}, u32[]{:S(2)}, u32[]{:S(2)}) collective-permute-start(f32[32,256]{1,0:T(8,128)S(1)} %get-tuple-element.27), channel_id=1, source_target_pairs={{0,3},{1,2},{2,1},{3,0},{4,7},{5,6},{6,5},{7,4},{8,11},{9,10},{10,... | collective-permute-start | bytes 98312 | tf_op jit(solution)/shard_map/ppermute | solution.py:174
  6.6 3.7 %collective-permute-start = (f32[32,256]{1,0:T(8,128)S(1)}, f32[32,256]{1,0:T(8,128)S(1)}, u32[]{:S(2)}, u32[]{:S(2)}) collective-permute-start(f32[32,256]{1,0:T(8,128)S(1)} %get-tuple-element.27), channel_id=1, source_target_pairs={{0,1},{1,0},{2,3},{3,2},{4,5},{5,4},{6,7},{7,6},{8,9},{9,8},{10,11... | collective-permute-start | bytes 98312 | tf_op jit(solution)/shard_map/ppermute | solution.py:174
  6.8 10.9 %collective-permute-start.4 = (f32[64,1024]{1,0:T(8,128)S(1)}, f32[64,1024]{1,0:T(8,128)S(1)}, u32[]{:S(2)}, u32[]{:S(2)}) collective-permute-start(f32[64,1024]{1,0:T(8,128)S(1)} %get-tuple-element.28), channel_id=1, source_target_pairs={{0,4},{4,0},{8,12},{12,8},{16,20},{20,16},{24,28},{28,24},{1,5},{5... | collective-permute-start | bytes 786440 | tf_op jit(solution)/shard_map/ppermute | solution.py:174
  8.7 9.9 %collective-permute-start.5 = (f32[64,1024]{1,0:T(8,128)S(1)}, f32[64,1024]{1,0:T(8,128)S(1)}, u32[]{:S(2)}, u32[]{:S(2)}) collective-permute-start(f32[64,1024]{1,0:T(8,128)S(1)} %get-tuple-element.29), channel_id=1, source_target_pairs={{0,8},{4,12},{8,0},{12,4},{16,24},{20,28},{24,16},{28,20},{1,9},{5... | collective-permute-start | bytes 786440 | tf_op jit(solution)/shard_map/ppermute | solution.py:174
  10.3 7.4 %collective-permute-start.3 = (f32[32,256]{1,0:T(8,128)S(1)}, f32[32,256]{1,0:T(8,128)S(1)}, u32[]{:S(2)}, u32[]{:S(2)}) collective-permute-start(f32[32,256]{1,0:T(8,128)S(1)} %add_add_fusion), channel_id=1, source_target_pairs={{0,16},{4,20},{8,24},{12,28},{16,0},{20,4},{24,8},{28,12},{1,17},{... | collective-permute-start | bytes 98312 | tf_op jit(solution)/shard_map/ppermute | solution.py:174
  13.0 11.3 %collective-permute-start.7 = (f32[64,1024]{1,0:T(8,128)S(1)}, f32[64,1024]{1,0:T(8,128)S(1)}, u32[]{:S(2)}, u32[]{:S(2)}) collective-permute-start(f32[64,1024]{1,0:T(8,128)S(1)} %get-tuple-element.31), channel_id=1, source_target_pairs={{0,12},{4,8},{8,4},{12,0},{16,28},{20,24},{24,20},{28,16},{1,13},{... | collective-permute-start | bytes 786440 | tf_op jit(solution)/shard_map/ppermute | solution.py:174
  18.6 5.6 %collective-permute-start.6 = (f32[64,256]{1,0:T(8,128)S(1)}, f32[64,256]{1,0:T(8,128)S(1)}, u32[]{:S(2)}, u32[]{:S(2)}) collective-permute-start(f32[64,256]{1,0:T(8,128)S(1)} %pad_maximum_fusion.1), channel_id=1, source_target_pairs={{0,4},{4,0},{8,12},{12,8},{16,20},{20,16},{24,28},{28,24},{1,5},{5... | collective-permute-start | bytes 196616 | tf_op jit(solution)/shard_map/ppermute | solution.py:174
  24.3 5.5 %collective-permute-start.8 = (f32[128,256]{1,0:T(8,128)S(1)}, f32[128,256]{1,0:T(8,128)S(1)}, u32[]{:S(2)}, u32[]{:S(2)}) collective-permute-start(f32[128,256]{1,0:T(8,128)S(1)} %pad_maximum_fusion), channel_id=1, source_target_pairs={{0,8},{4,12},{8,0},{12,4},{16,24},{20,28},{24,16},{28,20},{1,9},{5... | collective-permute-start | bytes 393224 | tf_op jit(solution)/shard_map/ppermute | solution.py:174
  29.8 1.6 %collective-permute-start.9 = (f32[256,256]{1,0:T(8,128)S(1)}, f32[256,256]{1,0:T(8,128)S(1)}, u32[]{:S(2)}, u32[]{:S(2)}) collective-permute-start(f32[256,256]{1,0:T(8,128)S(1)} %constant_dynamic-update-slice_fusion.mine_ref), channel_id=1, source_target_pairs={{0,1},{1,0},{2,3},{3,2},{4,5},{5,4},{6,7},{7,6},{8,9},{9,8},{10,11... | collective-permute-start | bytes 786440 | tf_op jit(solution)/shard_map/ppermute | solution.py:174
  34.4 12.9 %collective-permute-start.10 = (f32[32,1024]{1,0:T(8,128)S(1)}, f32[32,1024]{1,0:T(8,128)S(1)}, u32[]{:S(2)}, u32[]{:S(2)}) collective-permute-start(f32[32,1024]{1,0:T(8,128)S(1)} %get-tuple-element.41), channel_id=1, source_target_pairs={{0,16},{4,20},{8,24},{12,28},{16,0},{20,4},{24,8},{28,12},{1,17},{... | collective-permute-start | bytes 393224 | tf_op jit(solution)/shard_map/ppermute | solution.py:174
  36.9 13.8 %collective-permute-start.13 = (f32[32,1024]{1,0:T(8,128)S(1)}, f32[32,1024]{1,0:T(8,128)S(1)}, u32[]{:S(2)}, u32[]{:S(2)}) collective-permute-start(f32[32,1024]{1,0:T(8,128)S(1)} %get-tuple-element.45), channel_id=1, source_target_pairs={{0,16},{4,20},{8,24},{12,28},{16,0},{20,4},{24,8},{28,12},{1,17},{... | collective-permute-start | bytes 393224 | tf_op jit(solution)/shard_map/ppermute | solution.py:174
  47.2 9.1 %collective-permute-start.11 = (f32[32,1024]{1,0:T(8,128)S(1)}, f32[32,1024]{1,0:T(8,128)S(1)}, u32[]{:S(2)}, u32[]{:S(2)}) collective-permute-start(f32[32,1024]{1,0:T(8,128)S(1)} %get-tuple-element.42), channel_id=1, source_target_pairs={{0,16},{4,20},{8,24},{12,28},{16,0},{20,4},{24,8},{28,12},{1,17},{... | collective-permute-start | bytes 393224 | tf_op jit(solution)/shard_map/ppermute | solution.py:174
  47.3 9.8 %collective-permute-start.15 = (f32[32,1024]{1,0:T(8,128)S(1)}, f32[32,1024]{1,0:T(8,128)S(1)}, u32[]{:S(2)}, u32[]{:S(2)}) collective-permute-start(f32[32,1024]{1,0:T(8,128)S(1)} %add.28), channel_id=1, source_target_pairs={{0,12},{4,8},{8,4},{12,0},{16,28},{20,24},{24,20},{28,16},{1,13},{... | collective-permute-start | bytes 393224 | tf_op jit(solution)/shard_map/ppermute | solution.py:174
  50.7 10.0 %collective-permute-start.14 = (f32[32,1024]{1,0:T(8,128)S(1)}, f32[32,1024]{1,0:T(8,128)S(1)}, u32[]{:S(2)}, u32[]{:S(2)}) collective-permute-start(f32[32,1024]{1,0:T(8,128)S(1)} %add.27), channel_id=1, source_target_pairs={{0,8},{4,12},{8,0},{12,4},{16,24},{20,28},{24,16},{28,20},{1,9},{5... | collective-permute-start | bytes 393224 | tf_op jit(solution)/shard_map/ppermute | solution.py:174
  52.9 9.6 %collective-permute-start.16 = (f32[32,1024]{1,0:T(8,128)S(1)}, f32[32,1024]{1,0:T(8,128)S(1)}, u32[]{:S(2)}, u32[]{:S(2)}) collective-permute-start(f32[32,1024]{1,0:T(8,128)S(1)} %get-tuple-element.49), channel_id=1, source_target_pairs={{0,16},{4,20},{8,24},{12,28},{16,0},{20,4},{24,8},{28,12},{1,17},{... | collective-permute-start | bytes 393224 | tf_op jit(solution)/shard_map/ppermute | solution.py:174
  56.4 6.1 %collective-permute-start.12 = (f32[32,1024]{1,0:T(8,128)S(1)}, f32[32,1024]{1,0:T(8,128)S(1)}, u32[]{:S(2)}, u32[]{:S(2)}) collective-permute-start(f32[32,1024]{1,0:T(8,128)S(1)} %add.26), channel_id=1, source_target_pairs={{0,4},{4,0},{8,12},{12,8},{16,20},{20,16},{24,28},{28,24},{1,5},{5... | collective-permute-start | bytes 393224 | tf_op jit(solution)/shard_map/ppermute | solution.py:174

commit v7 on v6

v7 whole, which is shorter than its diff:
```python
import functools
import math

import jax
import jax.numpy as jnp
from jax import lax
from jax.experimental import pallas as pl
from jax.experimental.pallas import tpu as pltpu
from jax.sharding import PartitionSpec as P

MIB = 1024 * 1024
HBM = pl.BlockSpec(memory_space=pltpu.HBM)
SMEM = pl.BlockSpec(memory_space=pltpu.SMEM)
VMEM = pl.BlockSpec(memory_space=pltpu.VMEM)
FREE = pl.CostEstimate(flops=0, bytes_accessed=0, transcendentals=0)
ROWS_BY_ROWS = (((0,), (0,)), ((), ()))
ROWS_BY_COLUMNS = (((1,), (0,)), ((), ()))


def params(mib=48):
    return pltpu.CompilerParams(vmem_limit_bytes=mib * MIB)


def split(value):
    high = value.astype(jnp.bfloat16)
    return high, (value - high.astype(jnp.float32)).astype(jnp.bfloat16)


def dot(left, right, dims=ROWS_BY_COLUMNS):
    return lax.dot_general(left, right, dims, preferred_element_type=jnp.float32)


def product(left, right, dims=ROWS_BY_COLUMNS):
    (left_high, left_low), (right_high, right_low) = left, right
    return dot(left_high, right_high, dims) + (
        dot(left_high, right_low, dims) + dot(left_low, right_high, dims)
    )


def cut_kernel(snapshots_ref, parts_ref, sems):
    parts, _, width = parts_ref.shape
    copies = [
        pltpu.make_async_copy(snapshots_ref.at[:, pl.ds(i * width, width)], parts_ref.at[i], sems.at[i])
        for i in range(parts)
    ]
    for copy in copies:
        copy.start()
    for copy in copies:
        copy.wait()


def cut(snapshots, parts):
    rows, points = snapshots.shape
    width = points // parts
    if width % 128:
        return snapshots.reshape(rows, parts, width).transpose(1, 0, 2)
    return pl.pallas_call(
        cut_kernel,
        in_specs=[HBM],
        out_specs=VMEM,
        out_shape=jax.ShapeDtypeStruct((parts, rows, width), jnp.float32),
        scratch_shapes=[pltpu.SemaphoreType.DMA((parts,))],
        compiler_params=params(52),
        cost_estimate=FREE,
    )(snapshots)


def project_kernel(depth, snapshots_ref, factor_ref, mine_ref, other_ref, snapshots_buf, factor_buf, sems):
    rows, points = snapshots_ref.shape
    half = rows // 2
    snapshots_copy = pltpu.make_async_copy(snapshots_ref, snapshots_buf, sems.at[points // depth])
    snapshots_copy.start()
    copies = []
    for i, start in enumerate(range(0, points, depth)):
        span = pl.ds(start, depth)
        copies.append(pltpu.make_async_copy(factor_ref.at[span, :], factor_buf.at[span, :], sems.at[i]))
        copies[-1].start()
    snapshots_copy.wait()
    value = None
    for i, start in enumerate(range(0, points, depth)):
        copies[i].wait()
        high, low = split(snapshots_buf[:, start : start + depth])
        factor_high, factor_low = split(factor_buf[start : start + depth, :])
        both = dot(jnp.concatenate([high, low], axis=0), factor_high)
        term = both[:rows] + (both[rows:] + dot(high, factor_low))
        value = term if value is None else value + term
    first = lax.rem(lax.axis_index("space"), 2) == 0
    mine_ref[...] = jnp.where(first, value[:half], value[half:])
    other_ref[...] = jnp.where(first, value[half:], value[:half])


def project(snapshots, space_factor):
    rows, points = snapshots.shape
    rank = space_factor.shape[1]
    depth = min(512, points)
    half = jax.ShapeDtypeStruct((rows // 2, rank), jnp.float32)
    return pl.pallas_call(
        functools.partial(project_kernel, depth),
        in_specs=[HBM, HBM],
        out_specs=[VMEM] * 2,
        out_shape=[half] * 2,
        scratch_shapes=[
            pltpu.VMEM((rows, points), jnp.float32),
            pltpu.VMEM((points, rank), jnp.float32),
            pltpu.SemaphoreType.DMA((points // depth + 1,)),
        ],
        compiler_params=params(53),
        cost_estimate=FREE,
    )(snapshots, space_factor)


def mix_kernel(times, core_ref, mine_ref, theirs_ref, high_t_ref, low_t_ref, own_ref):
    total_half, rank = mine_ref.shape
    half = total_half // times
    mine = mine_ref[...].reshape(times, half, rank)
    theirs = theirs_ref[...].reshape(times, half, rank)
    first = core_ref[0] == 0
    low_rows, high_rows = jnp.where(first, mine, theirs), jnp.where(first, theirs, mine)
    projected = jnp.concatenate([low_rows, high_rows], axis=1).reshape(2 * total_half, rank)
    high, low = split(projected)
    cross = dot(high, low, ROWS_BY_ROWS)
    gram = dot(high, high, ROWS_BY_ROWS) + (cross + cross.T)
    diagonal = lax.broadcasted_iota(jnp.int32, (rank, rank), 0) == lax.broadcasted_iota(
        jnp.int32, (rank, rank), 1
    )
    total = jnp.sum(projected * projected)
    correlation = gram / total
    correlation_split = split(correlation)
    square = product(correlation_split, correlation_split)
    tail = jnp.where(diagonal, 1.6875, 0.0) - 0.5625 * correlation + 0.0625 * square
    mixing = (jnp.where(diagonal, 2.25, 0.0) - 2.4375 * correlation) + product(split(square), split(tail))
    scale = lax.rsqrt(total)
    factor = product((high, low), split(mixing)) * scale
    rows = 2 * half
    own_ref[...] = factor[:rows] * math.sqrt(times * rows)
    high_t_ref[...], low_t_ref[...] = split(factor.T)


def mix(core, mine, theirs, times):
    total_half, rank = mine.shape
    total = 2 * total_half
    return pl.pallas_call(
        functools.partial(mix_kernel, times),
        in_specs=[SMEM, VMEM, VMEM],
        out_specs=[VMEM] * 3,
        out_shape=[
            jax.ShapeDtypeStruct((rank, total), jnp.bfloat16),
            jax.ShapeDtypeStruct((rank, total), jnp.bfloat16),
            jax.ShapeDtypeStruct((total // times, rank), jnp.float32),
        ],
        compiler_params=params(),
        cost_estimate=FREE,
    )(core, mine, theirs)


def load_kernel(order, index_ref, high_ref, low_ref, columns_ref, blocks_ref):
    columns = jnp.concatenate([columns_ref[index_ref[0] ^ k] for k in order], axis=0)
    value = product((high_ref[...], low_ref[...]), split(columns))
    blocks_ref[...] = value.reshape(blocks_ref.shape)


def load(index, high, low, columns, order):
    rank, _ = high.shape
    blocks, _, width = columns.shape
    return pl.pallas_call(
        functools.partial(load_kernel, order),
        in_specs=[SMEM] + [VMEM] * 3,
        out_specs=VMEM,
        out_shape=jax.ShapeDtypeStruct((blocks, rank // blocks, width), jnp.float32),
        compiler_params=params(),
        cost_estimate=FREE,
    )(index, high, low, columns)


def swap(value, axis, offset):
    return lax.ppermute(value, axis, [(i, i ^ offset) for i in range(lax.axis_size(axis))])


def on_device(snapshots, space_factor):
    rows, points = snapshots.shape
    rank = space_factor.shape[1]
    times, spaces = lax.axis_size("tm"), lax.axis_size("space")
    index = lax.axis_index("tm")
    core = lax.axis_index("space") % 2

    snapshots, parts = lax.optimization_barrier((snapshots, cut(snapshots, times)))
    columns = lax.all_to_all(parts, "tm", 0, 0, tiled=True)

    mine, other = project(snapshots, space_factor)
    mine = mine + swap(other, "space", 1)
    for i in range(1, spaces.bit_length() - 1):
        mine = mine + swap(mine, "space", 1 << i)

    order = [0]
    for i in range(times.bit_length() - 1):
        mine = jnp.concatenate([mine, swap(mine, "tm", 1 << i)], axis=0)
        order = order + [k ^ 1 << i for k in order]
    high_t, low_t, own = mix(core.reshape(1), mine, swap(mine, "space", 1), times)

    blocks = load(index.reshape(1), high_t, low_t, columns, order)
    loadings = lax.all_to_all(blocks, "tm", 0, 0, tiled=True)
    return own, loadings.transpose(1, 0, 2).reshape(rank // times, points)


def solution(mesh):
    return jax.shard_map(
        on_device,
        mesh=mesh,
        in_specs=(P("tm", "space"), P("space", None)),
        out_specs=(P("tm", None), P("tm", "space")),
        check_vma=False,
    )
```

time: 63.5 us -> 65 us (1.024)
  blocking collectives: 0 us -> 18.2 us
  waiting for transfers between devices: 29.5 us -> 18 us
  starting transfers between devices: 26.2 us -> 19.3 us
  Pallas kernels: 6.8 us -> 7.8 us
  local copies, waits for them, and re-layouts: 0.02 us -> 0.83 us
    all_to_all x0 -> x1, blocking collectives: none -> 18.2 us  [on_device(): loadings = lax.all_to_all(blocks, 'tm', 0, 0, tiled=True)]
    ppermute x17 -> x6, starting transfers between devices: 26.2 us -> 12 us  [swap(): lax.ppermute(value, axis, [(i, i ^ offset) for i in range(lax.axis_size(a...]
    ppermute x17 -> x6, waiting for transfers between devices: 29.5 us -> 18 us  [swap(): lax.ppermute(value, axis, [(i, i ^ offset) for i in range(lax.axis_size(a...]
    all_to_all x0 -> x1, starting transfers between devices: none -> 7.26 us  [on_device(): columns = lax.all_to_all(parts, 'tm', 0, 0, tiled=True)]
    pallas_call x2 -> x3, Pallas kernels: 3.87 us -> 4.88 us  [the longest x1 2.32 us: cut(): pl.pallas_call(cut_kernel, in_specs=[HBM], out_specs=VMEM, out_shape=jax....]
    reshape x0 -> x1, local copies, waits for them, and re-layouts: none -> 0.83 us  [on_device(): return (own, loadings.transpose(1, 0, 2).reshape(rank // times, points))]
  transfers between devices with their start and end apart: 17 -> 7, of which waited for: 8 -> 6; matrix products, arithmetic and copies ran while one was open for 0% -> 0% of each run, Pallas kernels for 0% -> 8%
where the time goes in v7:
time: 65 us; the launch traced here: 64.8 us
  starting transfers between devices  19.3 us (30%)
  blocking collectives  18.2 us (28%)
  waiting for transfers between devices  18 us (28%)
  Pallas kernels  7.8 us (12%)
  local copies, waits for them, and re-layouts  0.83 us (1%)
  between operations  0.7 us (1%)
    all_to_all x1, blocking collectives, on_device(): loadings = lax.all_to_all(blocks, 'tm', 0, 0, tiled=True)  18.2 us
    ppermute x6, waiting for transfers between devices, swap(): lax.ppermute(value, axis, [(i, i ^ offset) for i in range(lax.axis_size(a...  18 us
    ppermute x6, starting transfers between devices, swap(): lax.ppermute(value, axis, [(i, i ^ offset) for i in range(lax.axis_size(a...  12 us
    all_to_all x1, starting transfers between devices, on_device(): columns = lax.all_to_all(parts, 'tm', 0, 0, tiled=True)  7.26 us
    pallas_call x1, Pallas kernels, project(): pl.pallas_call(functools.partial(project_kernel, depth), in_specs=[HBM, H...  2.93 us
    pallas_call x1, Pallas kernels, cut(): pl.pallas_call(cut_kernel, in_specs=[HBM], out_specs=VMEM, out_shape=jax....  2.32 us
    pallas_call x1, Pallas kernels, mix(): pl.pallas_call(functools.partial(mix_kernel, times), in_specs=[SMEM, VMEM...  1.98 us
  transfers between devices with their start and end apart: 7, of which 6 were waited for; matrix products, arithmetic and copies ran while one was open for 0% of the time, Pallas kernels for 8%

profile of v7, /device:TPU:0, one launch (start us, length us, event | category | flops | bytes accessed | tf_op | source)
XLA Modules:
  0.0 64.8 jit_solution(4418239975470025231)
XLA Ops:
  0.6 2.3 %shard_map.41 = f32[8,64,512]{2,1,0:T(8,128)} custom-call(f32[64,4096]{1,0:T(8,128)} %snapshots_ref.2), custom_call_target="tpu_custom_call" | custom-call | tf_op jit(solution)/shard_map/pallas_call | solution.py:57
  3.0 7.3 %all-to-all-start = ((f32[8,64,512]{2,1,0:T(8,128)}), f32[8,64,512]{2,1,0:T(8,128)S(1)}, u32[]{:S(2)}, u32[]{:S(2)}) async-start(f32[8,64,512]{2,1,0:T(8,128)} %shard_map.41), calls=%async_computation | async-start | bytes 2097152 | tf_op jit(solution)/shard_map/all_to_all | solution.py:187
  10.2 2.9 %shard_map.42 = (f32[32,256]{1,0:T(8,128)S(1)}, f32[32,256]{1,0:T(8,128)S(1)}) custom-call(f32[64,4096]{1,0:T(8,128)} %snapshots_ref.2, f32[4096,256]{1,0:T(8,128)} %factor_ref.1), custom_call_target="tpu_custom_call" | custom-call | tf_op jit(solution)/shard_map/pallas_call | solution.py:97
  13.2 0.1 collective-permute-start
  13.2 1.2 %collective-permute-done = f32[32,256]{1,0:T(8,128)S(1)} collective-permute-done((f32[32,256]{1,0:T(8,128)S(1)}, f32[32,256]{1,0:T(8,128)S(1)}, u32[]{:S(2)}, u32[]{:S(2)}) %collective-permute-start) | collective-permute-done | bytes 32800 | tf_op jit(solution)/shard_map/ppermute | solution.py:176
  14.4 1.5 %collective-permute-start.1 = (f32[32,256]{1,0:T(8,128)S(1)}, f32[32,256]{1,0:T(8,128)S(1)}, u32[]{:S(2)}, u32[]{:S(2)}) collective-permute-start(f32[32,256]{1,0:T(8,128)S(1)} %add.11), channel_id=1, source_target_pairs={{0,2},{1,3},{2,0},{3,1},{4,6},{5,7},{6,4},{7,5},{8,10},{9,11},{10,... | collective-permute-start | bytes 98312 | tf_op jit(solution)/shard_map/ppermute | solution.py:176
  16.0 2.4 %collective-permute-done.1 = f32[32,256]{1,0:T(8,128)S(1)} collective-permute-done((f32[32,256]{1,0:T(8,128)S(1)}, f32[32,256]{1,0:T(8,128)S(1)}, u32[]{:S(2)}, u32[]{:S(2)}) %collective-permute-start.1) | collective-permute-done | bytes 32800 | tf_op jit(solution)/shard_map/ppermute | solution.py:176
  18.4 2.0 %collective-permute-start.2 = (f32[32,256]{1,0:T(8,128)S(1)}, f32[32,256]{1,0:T(8,128)S(1)}, u32[]{:S(2)}, u32[]{:S(2)}) collective-permute-start(f32[32,256]{1,0:T(8,128)S(1)} %add.12), channel_id=1, source_target_pairs={{0,4},{4,0},{8,12},{12,8},{16,20},{20,16},{24,28},{28,24},{1,5},{5... | collective-permute-start | bytes 98312 | tf_op jit(solution)/shard_map/ppermute | solution.py:176
  20.4 2.3 %collective-permute-done.2 = f32[32,256]{1,0:T(8,128)S(1)} collective-permute-done((f32[32,256]{1,0:T(8,128)S(1)}, f32[32,256]{1,0:T(8,128)S(1)}, u32[]{:S(2)}, u32[]{:S(2)}) %collective-permute-start.2) | collective-permute-done | bytes 32800 | tf_op jit(solution)/shard_map/ppermute | solution.py:176
  22.7 1.9 %collective-permute-start.3 = (f32[64,256]{1,0:T(8,128)S(1)}, f32[64,256]{1,0:T(8,128)S(1)}, u32[]{:S(2)}, u32[]{:S(2)}) collective-permute-start(f32[64,256]{1,0:T(8,128)S(1)} %pad_maximum_fusion.2), channel_id=1, source_target_pairs={{0,8},{4,12},{8,0},{12,4},{16,24},{20,28},{24,16},{28,20},{1,9},{5... | collective-permute-start | bytes 196616 | tf_op jit(solution)/shard_map/ppermute | solution.py:176
  24.6 4.1 %collective-permute-done.3 = f32[64,256]{1,0:T(8,128)S(1)} collective-permute-done((f32[64,256]{1,0:T(8,128)S(1)}, f32[64,256]{1,0:T(8,128)S(1)}, u32[]{:S(2)}, u32[]{:S(2)}) %collective-permute-start.3) | collective-permute-done | bytes 65568 | tf_op jit(solution)/shard_map/ppermute | solution.py:176
  28.7 6.4 %collective-permute-start.4 = (f32[128,256]{1,0:T(8,128)S(1)}, f32[128,256]{1,0:T(8,128)S(1)}, u32[]{:S(2)}, u32[]{:S(2)}) collective-permute-start(f32[128,256]{1,0:T(8,128)S(1)} %pad_maximum_fusion.1), channel_id=1, source_target_pairs={{0,16},{4,20},{8,24},{12,28},{16,0},{20,4},{24,8},{28,12},{1,17},{... | collective-permute-start | bytes 393224 | tf_op jit(solution)/shard_map/ppermute | solution.py:176
  35.1 6.5 %collective-permute-done.4 = f32[128,256]{1,0:T(8,128)S(1)} collective-permute-done((f32[128,256]{1,0:T(8,128)S(1)}, f32[128,256]{1,0:T(8,128)S(1)}, u32[]{:S(2)}, u32[]{:S(2)}) %collective-permute-start.4) | collective-permute-done | bytes 131104 | tf_op jit(solution)/shard_map/ppermute | solution.py:176
  41.6 0.1 collective-permute-start.5
  41.7 1.5 %collective-permute-done.5.theirs_ref = f32[256,256]{1,0:T(8,128)S(1)} collective-permute-done((f32[256,256]{1,0:T(8,128)S(1)}, f32[256,256]{1,0:T(8,128)S(1)}, u32[]{:S(2)}, u32[]{:S(2)}) %collective-permute-start.5) | collective-permute-done | bytes 262176 | tf_op jit(solution)/shard_map/ppermute | solution.py:176
  43.2 2.0 %shard_map.43 = (bf16[256,512]{1,0:T(8,128)(2,1)S(1)}, bf16[256,512]{1,0:T(8,128)(2,1)S(1)}, f32[64,256]{1,0:T(8,128)}) custom-call(s32[1]{0:T(128)} %bitcast.core_ref, f32[256,256]{1,0:T(8,128)S(1)} %pad_maximum_fusion.mine_ref, f32[256,256]{1,0:T(8,128)S(1)} %collective-permute-done.5.theirs_ref), custom_call_target="tpu_custom_call" | custom-call | tf_op jit(solution)/shard_map/pallas_call | solution.py:142
  45.2 0.0 all-to-all-done.columns_ref
  45.2 0.6 shard_map.44
  45.8 18.2 %all_to_all.10 = f32[8,32,512]{2,1,0:T(8,128)S(1)} all-to-all(f32[8,32,512]{2,1,0:T(8,128)S(1)} %shard_map.44), channel_id=1, replica_groups=mesh['tm'=8,'space'=4] {'tm'}, dimensions={0} | all-to-all | bytes 1048576 | tf_op jit(solution)/shard_map/all_to_all | solution.py:201
  64.0 0.8 %copy.5 = f32[8,4,8,512]{3,2,0,1:T(8,128)} copy(f32[8,4,8,512]{3,2,1,0:T(8,128)S(1)} %bitcast.5) | data formatting | bytes 1048576 | tf_op jit(solution)/shard_map/reshape | solution.py:202
  (5 shorter events, 0.0 us)
Async XLA Ops:
  3.0 42.3 %all-to-all-start = ((f32[8,64,512]{2,1,0:T(8,128)}), f32[8,64,512]{2,1,0:T(8,128)S(1)}, u32[]{:S(2)}, u32[]{:S(2)}) async-start(f32[8,64,512]{2,1,0:T(8,128)} %shard_map.41), calls=%async_computation | async-start | bytes 2097152 | tf_op jit(solution)/shard_map/all_to_all | solution.py:187
  13.2 1.3 %collective-permute-start = (f32[32,256]{1,0:T(8,128)S(1)}, f32[32,256]{1,0:T(8,128)S(1)}, u32[]{:S(2)}, u32[]{:S(2)}) collective-permute-start(f32[32,256]{1,0:T(8,128)S(1)} %get-tuple-element.11), channel_id=1, source_target_pairs={{0,1},{1,0},{2,3},{3,2},{4,5},{5,4},{6,7},{7,6},{8,9},{9,8},{10,11... | collective-permute-start | bytes 98312 | tf_op jit(solution)/shard_map/ppermute | solution.py:176
  14.4 3.9 %collective-permute-start.1 = (f32[32,256]{1,0:T(8,128)S(1)}, f32[32,256]{1,0:T(8,128)S(1)}, u32[]{:S(2)}, u32[]{:S(2)}) collective-permute-start(f32[32,256]{1,0:T(8,128)S(1)} %add.11), channel_id=1, source_target_pairs={{0,2},{1,3},{2,0},{3,1},{4,6},{5,7},{6,4},{7,5},{8,10},{9,11},{10,... | collective-permute-start | bytes 98312 | tf_op jit(solution)/shard_map/ppermute | solution.py:176
  18.4 4.3 %collective-permute-start.2 = (f32[32,256]{1,0:T(8,128)S(1)}, f32[32,256]{1,0:T(8,128)S(1)}, u32[]{:S(2)}, u32[]{:S(2)}) collective-permute-start(f32[32,256]{1,0:T(8,128)S(1)} %add.12), channel_id=1, source_target_pairs={{0,4},{4,0},{8,12},{12,8},{16,20},{20,16},{24,28},{28,24},{1,5},{5... | collective-permute-start | bytes 98312 | tf_op jit(solution)/shard_map/ppermute | solution.py:176
  22.7 6.0 %collective-permute-start.3 = (f32[64,256]{1,0:T(8,128)S(1)}, f32[64,256]{1,0:T(8,128)S(1)}, u32[]{:S(2)}, u32[]{:S(2)}) collective-permute-start(f32[64,256]{1,0:T(8,128)S(1)} %pad_maximum_fusion.2), channel_id=1, source_target_pairs={{0,8},{4,12},{8,0},{12,4},{16,24},{20,28},{24,16},{28,20},{1,9},{5... | collective-permute-start | bytes 196616 | tf_op jit(solution)/shard_map/ppermute | solution.py:176
  28.7 12.9 %collective-permute-start.4 = (f32[128,256]{1,0:T(8,128)S(1)}, f32[128,256]{1,0:T(8,128)S(1)}, u32[]{:S(2)}, u32[]{:S(2)}) collective-permute-start(f32[128,256]{1,0:T(8,128)S(1)} %pad_maximum_fusion.1), channel_id=1, source_target_pairs={{0,16},{4,20},{8,24},{12,28},{16,0},{20,4},{24,8},{28,12},{1,17},{... | collective-permute-start | bytes 393224 | tf_op jit(solution)/shard_map/ppermute | solution.py:176
  41.6 1.6 %collective-permute-start.5 = (f32[256,256]{1,0:T(8,128)S(1)}, f32[256,256]{1,0:T(8,128)S(1)}, u32[]{:S(2)}, u32[]{:S(2)}) collective-permute-start(f32[256,256]{1,0:T(8,128)S(1)} %pad_maximum_fusion.mine_ref), channel_id=1, source_target_pairs={{0,1},{1,0},{2,3},{3,2},{4,5},{5,4},{6,7},{7,6},{8,9},{9,8},{10,11... | collective-permute-start | bytes 786440 | tf_op jit(solution)/shard_map/ppermute | solution.py:176

commit v8 on v7

--- a/solution.py
+++ b/solution.py
@@ -37,16 +37,18 @@
     )
 
 
-def cut_kernel(snapshots_ref, parts_ref, sems):
-    parts, _, width = parts_ref.shape
+def cut_kernel(step, snapshots_ref, parts_ref, buf, sems):
+    parts, rows, width = parts_ref.shape
+    spans = [pl.ds(start, step) for start in range(0, rows, step)]
     copies = [
-        pltpu.make_async_copy(snapshots_ref.at[:, pl.ds(i * width, width)], parts_ref.at[i], sems.at[i])
-        for i in range(parts)
+        pltpu.make_async_copy(snapshots_ref.at[span, :], buf.at[span, :], sems.at[i]) for i, span in enumerate(spans)
     ]
     for copy in copies:
         copy.start()
-    for copy in copies:
+    for copy, span in zip(copies, spans):
         copy.wait()
+        for i in range(parts):
+            parts_ref[i, span, :] = buf[span, i * width : (i + 1) * width]
 
 
 def cut(snapshots, parts):
@@ -54,12 +56,13 @@
     width = points // parts
     if width % 128:
         return snapshots.reshape(rows, parts, width).transpose(1, 0, 2)
-    return pl.pallas_call(
-        cut_kernel,
+    step = 8 if rows % 8 == 0 else rows
+    return pl.pallas_call(
+        functools.partial(cut_kernel, step),
         in_specs=[HBM],
         out_specs=VMEM,
         out_shape=jax.ShapeDtypeStruct((parts, rows, width), jnp.float32),
-        scratch_shapes=[pltpu.SemaphoreType.DMA((parts,))],
+        scratch_shapes=[pltpu.VMEM((rows, points), jnp.float32), pltpu.SemaphoreType.DMA((rows // step,))],
         compiler_params=params(52),
         cost_estimate=FREE,
     )(snapshots)
@@ -191,8 +194,8 @@
     for i in range(1, spaces.bit_length() - 1):
         mine = mine + swap(mine, "space", 1 << i)
 
-    order = [0]
-    for i in range(times.bit_length() - 1):
+    order, bits = [0], range(times.bit_length() - 1)
+    for i in [*bits[2:], *bits[:2]]:
         mine = jnp.concatenate([mine, swap(mine, "tm", 1 << i)], axis=0)
         order = order + [k ^ 1 << i for k in order]
     high_t, low_t, own = mix(core.reshape(1), mine, swap(mine, "space", 1), times)

time: 65 us -> 70.2 us (1.080)
  waiting for transfers between devices: 18 us -> 29 us
  starting transfers between devices: 19.3 us -> 13.3 us
    ppermute x6, waiting for transfers between devices: 18 us -> 29 us  [swap(): lax.ppermute(value, axis, [(i, i ^ offset) for i in range(lax.axis_size(a...]
    ppermute x6, starting transfers between devices: 12 us -> 6.07 us  [swap(): lax.ppermute(value, axis, [(i, i ^ offset) for i in range(lax.axis_size(a...]
  transfers between devices with their start and end apart: 7 -> 7, of which waited for: 6 -> 6; matrix products, arithmetic and copies ran while one was open for 0% -> 0% of each run, Pallas kernels for 8% -> 7%
where the time goes in v8:
time: 70.2 us; the launch traced here: 69.9 us
  waiting for transfers between devices  29 us (41%)
  blocking collectives  18.2 us (26%)
  starting transfers between devices  13.3 us (19%)
  Pallas kernels  7.81 us (11%)
  local copies, waits for them, and re-layouts  0.83 us (1%)
    ppermute x6, waiting for transfers between devices, swap(): lax.ppermute(value, axis, [(i, i ^ offset) for i in range(lax.axis_size(a...  29 us
    all_to_all x1, blocking collectives, on_device(): loadings = lax.all_to_all(blocks, 'tm', 0, 0, tiled=True)  18.2 us
    all_to_all x1, starting transfers between devices, on_device(): columns = lax.all_to_all(parts, 'tm', 0, 0, tiled=True)  7.26 us
    ppermute x6, starting transfers between devices, swap(): lax.ppermute(value, axis, [(i, i ^ offset) for i in range(lax.axis_size(a...  6.07 us
    pallas_call x1, Pallas kernels, project(): pl.pallas_call(functools.partial(project_kernel, depth), in_specs=[HBM, H...  2.92 us
    pallas_call x1, Pallas kernels, cut(): pl.pallas_call(functools.partial(cut_kernel, step), in_specs=[HBM], out_s...  2.32 us
    pallas_call x1, Pallas kernels, mix(): pl.pallas_call(functools.partial(mix_kernel, times), in_specs=[SMEM, VMEM...  1.98 us
  transfers between devices with their start and end apart: 7, of which 6 were waited for; matrix products, arithmetic and copies ran while one was open for 0% of the time, Pallas kernels for 7%

profile of v8, /device:TPU:0, one launch (start us, length us, event | category | flops | bytes accessed | tf_op | source)
XLA Modules:
  0.0 69.9 jit_solution(16054466160781861989)
XLA Ops:
  0.6 2.3 %shard_map.41 = f32[8,64,512]{2,1,0:T(8,128)} custom-call(f32[64,4096]{1,0:T(8,128)} %snapshots_ref.2), custom_call_target="tpu_custom_call" | custom-call | tf_op jit(solution)/shard_map/pallas_call | solution.py:60
  3.0 7.3 %all-to-all-start = ((f32[8,64,512]{2,1,0:T(8,128)}), f32[8,64,512]{2,1,0:T(8,128)S(1)}, u32[]{:S(2)}, u32[]{:S(2)}) async-start(f32[8,64,512]{2,1,0:T(8,128)} %shard_map.41), calls=%async_computation | async-start | bytes 2097152 | tf_op jit(solution)/shard_map/all_to_all | solution.py:190
  10.2 2.9 %shard_map.42 = (f32[32,256]{1,0:T(8,128)S(1)}, f32[32,256]{1,0:T(8,128)S(1)}) custom-call(f32[64,4096]{1,0:T(8,128)} %snapshots_ref.2, f32[4096,256]{1,0:T(8,128)} %factor_ref.1), custom_call_target="tpu_custom_call" | custom-call | tf_op jit(solution)/shard_map/pallas_call | solution.py:100
  13.2 0.1 collective-permute-start
  13.2 1.2 %collective-permute-done = f32[32,256]{1,0:T(8,128)S(1)} collective-permute-done((f32[32,256]{1,0:T(8,128)S(1)}, f32[32,256]{1,0:T(8,128)S(1)}, u32[]{:S(2)}, u32[]{:S(2)}) %collective-permute-start) | collective-permute-done | bytes 32800 | tf_op jit(solution)/shard_map/ppermute | solution.py:179
  14.4 1.5 %collective-permute-start.1 = (f32[32,256]{1,0:T(8,128)S(1)}, f32[32,256]{1,0:T(8,128)S(1)}, u32[]{:S(2)}, u32[]{:S(2)}) collective-permute-start(f32[32,256]{1,0:T(8,128)S(1)} %add.11), channel_id=1, source_target_pairs={{0,2},{1,3},{2,0},{3,1},{4,6},{5,7},{6,4},{7,5},{8,10},{9,11},{10,... | collective-permute-start | bytes 98312 | tf_op jit(solution)/shard_map/ppermute | solution.py:179
  16.0 2.4 %collective-permute-done.1 = f32[32,256]{1,0:T(8,128)S(1)} collective-permute-done((f32[32,256]{1,0:T(8,128)S(1)}, f32[32,256]{1,0:T(8,128)S(1)}, u32[]{:S(2)}, u32[]{:S(2)}) %collective-permute-start.1) | collective-permute-done | bytes 32800 | tf_op jit(solution)/shard_map/ppermute | solution.py:179
  18.4 2.9 %collective-permute-start.2 = (f32[32,256]{1,0:T(8,128)S(1)}, f32[32,256]{1,0:T(8,128)S(1)}, u32[]{:S(2)}, u32[]{:S(2)}) collective-permute-start(f32[32,256]{1,0:T(8,128)S(1)} %add.12), channel_id=1, source_target_pairs={{0,16},{4,20},{8,24},{12,28},{16,0},{20,4},{24,8},{28,12},{1,17},{... | collective-permute-start | bytes 98312 | tf_op jit(solution)/shard_map/ppermute | solution.py:179
  21.3 16.1 %collective-permute-done.2 = f32[32,256]{1,0:T(8,128)S(1)} collective-permute-done((f32[32,256]{1,0:T(8,128)S(1)}, f32[32,256]{1,0:T(8,128)S(1)}, u32[]{:S(2)}, u32[]{:S(2)}) %collective-permute-start.2) | collective-permute-done | bytes 32800 | tf_op jit(solution)/shard_map/ppermute | solution.py:179
  37.4 1.4 %collective-permute-start.3 = (f32[64,256]{1,0:T(8,128)S(1)}, f32[64,256]{1,0:T(8,128)S(1)}, u32[]{:S(2)}, u32[]{:S(2)}) collective-permute-start(f32[64,256]{1,0:T(8,128)S(1)} %pad_maximum_fusion.2), channel_id=1, source_target_pairs={{0,4},{4,0},{8,12},{12,8},{16,20},{20,16},{24,28},{28,24},{1,5},{5... | collective-permute-start | bytes 196616 | tf_op jit(solution)/shard_map/ppermute | solution.py:179
  38.8 2.8 %collective-permute-done.3 = f32[64,256]{1,0:T(8,128)S(1)} collective-permute-done((f32[64,256]{1,0:T(8,128)S(1)}, f32[64,256]{1,0:T(8,128)S(1)}, u32[]{:S(2)}, u32[]{:S(2)}) %collective-permute-start.3) | collective-permute-done | bytes 65568 | tf_op jit(solution)/shard_map/ppermute | solution.py:179
  41.7 0.1 collective-permute-start.4
  41.8 5.0 %collective-permute-done.4 = f32[128,256]{1,0:T(8,128)S(1)} collective-permute-done((f32[128,256]{1,0:T(8,128)S(1)}, f32[128,256]{1,0:T(8,128)S(1)}, u32[]{:S(2)}, u32[]{:S(2)}) %collective-permute-start.4) | collective-permute-done | bytes 131104 | tf_op jit(solution)/shard_map/ppermute | solution.py:179
  46.7 0.1 collective-permute-start.5
  46.8 1.5 %collective-permute-done.5.theirs_ref = f32[256,256]{1,0:T(8,128)S(1)} collective-permute-done((f32[256,256]{1,0:T(8,128)S(1)}, f32[256,256]{1,0:T(8,128)S(1)}, u32[]{:S(2)}, u32[]{:S(2)}) %collective-permute-start.5) | collective-permute-done | bytes 262176 | tf_op jit(solution)/shard_map/ppermute | solution.py:179
  48.3 2.0 %shard_map.43 = (bf16[256,512]{1,0:T(8,128)(2,1)S(1)}, bf16[256,512]{1,0:T(8,128)(2,1)S(1)}, f32[64,256]{1,0:T(8,128)}) custom-call(s32[1]{0:T(128)} %bitcast.core_ref, f32[256,256]{1,0:T(8,128)S(1)} %pad_maximum_fusion.mine_ref, f32[256,256]{1,0:T(8,128)S(1)} %collective-permute-done.5.theirs_ref), custom_call_target="tpu_custom_call" | custom-call | tf_op jit(solution)/shard_map/pallas_call | solution.py:145
  50.3 0.0 all-to-all-done.columns_ref
  50.3 0.6 shard_map.44
  50.9 18.2 %all_to_all.10 = f32[8,32,512]{2,1,0:T(8,128)S(1)} all-to-all(f32[8,32,512]{2,1,0:T(8,128)S(1)} %shard_map.44), channel_id=1, replica_groups=mesh['tm'=8,'space'=4] {'tm'}, dimensions={0} | all-to-all | bytes 1048576 | tf_op jit(solution)/shard_map/all_to_all | solution.py:204
  69.1 0.8 %copy.5 = f32[8,4,8,512]{3,2,0,1:T(8,128)} copy(f32[8,4,8,512]{3,2,1,0:T(8,128)S(1)} %bitcast.5) | data formatting | bytes 1048576 | tf_op jit(solution)/shard_map/reshape | solution.py:205
  (5 shorter events, 0.0 us)
Async XLA Ops:
  3.0 47.4 %all-to-all-start = ((f32[8,64,512]{2,1,0:T(8,128)}), f32[8,64,512]{2,1,0:T(8,128)S(1)}, u32[]{:S(2)}, u32[]{:S(2)}) async-start(f32[8,64,512]{2,1,0:T(8,128)} %shard_map.41), calls=%async_computation | async-start | bytes 2097152 | tf_op jit(solution)/shard_map/all_to_all | solution.py:190
  13.2 1.3 %collective-permute-start = (f32[32,256]{1,0:T(8,128)S(1)}, f32[32,256]{1,0:T(8,128)S(1)}, u32[]{:S(2)}, u32[]{:S(2)}) collective-permute-start(f32[32,256]{1,0:T(8,128)S(1)} %get-tuple-element.11), channel_id=1, source_target_pairs={{0,1},{1,0},{2,3},{3,2},{4,5},{5,4},{6,7},{7,6},{8,9},{9,8},{10,11... | collective-permute-start | bytes 98312 | tf_op jit(solution)/shard_map/ppermute | solution.py:179
  14.4 3.9 %collective-permute-start.1 = (f32[32,256]{1,0:T(8,128)S(1)}, f32[32,256]{1,0:T(8,128)S(1)}, u32[]{:S(2)}, u32[]{:S(2)}) collective-permute-start(f32[32,256]{1,0:T(8,128)S(1)} %add.11), channel_id=1, source_target_pairs={{0,2},{1,3},{2,0},{3,1},{4,6},{5,7},{6,4},{7,5},{8,10},{9,11},{10,... | collective-permute-start | bytes 98312 | tf_op jit(solution)/shard_map/ppermute | solution.py:179
  18.4 19.0 %collective-permute-start.2 = (f32[32,256]{1,0:T(8,128)S(1)}, f32[32,256]{1,0:T(8,128)S(1)}, u32[]{:S(2)}, u32[]{:S(2)}) collective-permute-start(f32[32,256]{1,0:T(8,128)S(1)} %add.12), channel_id=1, source_target_pairs={{0,16},{4,20},{8,24},{12,28},{16,0},{20,4},{24,8},{28,12},{1,17},{... | collective-permute-start | bytes 98312 | tf_op jit(solution)/shard_map/ppermute | solution.py:179
  37.4 4.3 %collective-permute-start.3 = (f32[64,256]{1,0:T(8,128)S(1)}, f32[64,256]{1,0:T(8,128)S(1)}, u32[]{:S(2)}, u32[]{:S(2)}) collective-permute-start(f32[64,256]{1,0:T(8,128)S(1)} %pad_maximum_fusion.2), channel_id=1, source_target_pairs={{0,4},{4,0},{8,12},{12,8},{16,20},{20,16},{24,28},{28,24},{1,5},{5... | collective-permute-start | bytes 196616 | tf_op jit(solution)/shard_map/ppermute | solution.py:179
  41.7 5.0 %collective-permute-start.4 = (f32[128,256]{1,0:T(8,128)S(1)}, f32[128,256]{1,0:T(8,128)S(1)}, u32[]{:S(2)}, u32[]{:S(2)}) collective-permute-start(f32[128,256]{1,0:T(8,128)S(1)} %pad_maximum_fusion.1), channel_id=1, source_target_pairs={{0,8},{4,12},{8,0},{12,4},{16,24},{20,28},{24,16},{28,20},{1,9},{5... | collective-permute-start | bytes 393224 | tf_op jit(solution)/shard_map/ppermute | solution.py:179
  46.7 1.6 %collective-permute-start.5 = (f32[256,256]{1,0:T(8,128)S(1)}, f32[256,256]{1,0:T(8,128)S(1)}, u32[]{:S(2)}, u32[]{:S(2)}) collective-permute-start(f32[256,256]{1,0:T(8,128)S(1)} %pad_maximum_fusion.mine_ref), channel_id=1, source_target_pairs={{0,1},{1,0},{2,3},{3,2},{4,5},{5,4},{6,7},{7,6},{8,9},{9,8},{10,11... | collective-permute-start | bytes 786440 | tf_op jit(solution)/shard_map/ppermute | solution.py:179

commit v9 on v6

--- a/solution.py
+++ b/solution.py
@@ -12,6 +12,7 @@
 HBM = pl.BlockSpec(memory_space=pltpu.HBM)
 SMEM = pl.BlockSpec(memory_space=pltpu.SMEM)
 VMEM = pl.BlockSpec(memory_space=pltpu.VMEM)
+FREE = pl.CostEstimate(flops=0, bytes_accessed=0, transcendentals=0)
 ROWS_BY_ROWS = (((0,), (0,)), ((), ()))
 ROWS_BY_COLUMNS = (((1,), (0,)), ((), ()))
 COLUMNS_BY_COLUMNS = (((1,), (1,)), ((), ()))
@@ -83,12 +84,12 @@
             pltpu.SemaphoreType.DMA((points // depth + 1,)),
         ],
         compiler_params=params(52),
+        cost_estimate=FREE,
     )(snapshots, space_factor)
     return mine, other, parts
 
 
-def load_kernel(times, group, order, index_ref, mine_ref, theirs_ref, *refs):
-    parts, own_ref, blocks = refs[:group], refs[group], refs[group + 1 :]
+def mix_kernel(times, order, index_ref, mine_ref, theirs_ref, high_t_ref, low_t_ref, own_ref):
     total_half, rank = mine_ref.shape
     half = total_half // times
     mine = mine_ref[...].reshape(times, half, rank)
@@ -99,19 +100,18 @@
     high, low = split(projected)
     cross = dot(high, low, ROWS_BY_ROWS)
     gram = dot(high, high, ROWS_BY_ROWS) + (cross + cross.T)
-    diagonal = lax.broadcasted_iota(jnp.int32, (rank, rank), 0) == lax.broadcasted_iota(
-        jnp.int32, (rank, rank), 1
-    )
+    row = lax.broadcasted_iota(jnp.int32, (rank, rank), 0)
+    column = lax.broadcasted_iota(jnp.int32, (rank, rank), 1)
     total = jnp.sum(projected * projected)
     correlation = gram / total
     correlation_split = split(correlation)
     square = product(correlation_split, correlation_split)
-    tail = jnp.where(diagonal, 1.6875, 0.0) - 0.5625 * correlation + 0.0625 * square
-    mixing = (jnp.where(diagonal, 2.25, 0.0) - 2.4375 * correlation) + product(split(square), split(tail))
-
+    tail = jnp.where(row == column, 1.6875, 0.0) - 0.5625 * correlation + 0.0625 * square
+    mixing = (jnp.where(row == column, 2.25, 0.0) - 2.4375 * correlation) + product(split(square), split(tail))
     mixing_high, mixing_low = split(mixing)
 
     rows = 2 * half
+    group = high_t_ref.shape[1] // rows
     places = [order.index(k) for k in range(group)]
     high = jnp.concatenate([high[i * rows : (i + 1) * rows] for i in places], axis=0)
     low = jnp.concatenate([low[i * rows : (i + 1) * rows] for i in places], axis=0)
@@ -119,55 +119,71 @@
     own = product((high[:rows], low[:rows]), (mixing_high, mixing_low))
     own_ref[...] = own * (scale * math.sqrt(times * rows))
     width = rank // times
-    row = lax.broadcasted_iota(jnp.int32, (rank, rank), 0)
     source = ((row // width) ^ index_ref[0]) * width + row % width
-    move = jnp.where(source == lax.broadcasted_iota(jnp.int32, (rank, rank), 1), 1.0, 0.0).astype(jnp.bfloat16)
+    move = jnp.where(source == column, 1.0, 0.0).astype(jnp.bfloat16)
     moved = dot(move, jnp.concatenate([mixing_high, mixing_low], axis=1)).astype(jnp.bfloat16)
     turned = product((moved[:, :rank], moved[:, rank:]), (high, low), COLUMNS_BY_COLUMNS) * scale
+    high_t_ref[...], low_t_ref[...] = split(turned)
+
+
+def mix(index, mine, theirs, times, group, order):
+    total_half, rank = mine.shape
+    rows = 2 * total_half // times
+    factor = jax.ShapeDtypeStruct((rank, group * rows), jnp.bfloat16)
+    return pl.pallas_call(
+        functools.partial(mix_kernel, times, order),
+        in_specs=[SMEM, VMEM, VMEM],
+        out_specs=[VMEM] * 3,
+        out_shape=[factor, factor, jax.ShapeDtypeStruct((rows, rank), jnp.float32)],
+        compiler_params=params(),
+        cost_estimate=FREE,
+    )(index, mine, theirs)
+
+
+def load_kernel(group, high_ref, low_ref, *refs):
+    parts, blocks = refs[:group], refs[group:]
     columns = jnp.concatenate([part[...] for part in parts], axis=0)
-    value = product(split(turned), split(columns))
+    value = product((high_ref[...], low_ref[...]), split(columns))
+    width = value.shape[0] // len(blocks)
     for i, block in enumerate(blocks):
         block[...] = value[i * width : (i + 1) * width]
 
 
-def load(index, mine, theirs, parts, times, order):
-    total_half, rank = mine.shape
-    rows = 2 * total_half // times
-    group = len(parts)
+def load(high, low, parts, blocks):
+    rank = high.shape[0]
     columns = parts[0].shape[1]
-    own, *blocks = pl.pallas_call(
-        functools.partial(load_kernel, times, group, order),
-        in_specs=[SMEM] + [VMEM] * (2 + group),
-        out_specs=[VMEM] * (1 + times),
-        out_shape=[jax.ShapeDtypeStruct((rows, rank), jnp.float32)]
-        + [jax.ShapeDtypeStruct((rank // times, columns), jnp.float32)] * times,
+    return pl.pallas_call(
+        functools.partial(load_kernel, len(parts)),
+        in_specs=[VMEM] * (2 + len(parts)),
+        out_specs=[VMEM] * blocks,
+        out_shape=[jax.ShapeDtypeStruct((rank // blocks, columns), jnp.float32)] * blocks,
         compiler_params=params(),
-    )(index, mine, theirs, *parts)
-    return own, blocks
+        cost_estimate=FREE,
+    )(high, low, *parts)
 
 
 def join_kernel(group, *refs):
-    *parts, out_ref = refs
-    width = parts[0].shape[1]
+    *terms, out_ref = refs
+    terms = terms[-group:] + terms[:-group]
+    width = terms[0].shape[1]
     member = lax.rem(lax.axis_index("tm"), group)
     for k in range(group):
-        value = parts[k][...]
-        if k == 0:
-            for term in parts[group:]:
-                value = value + term[...]
+        value = terms[k][...]
+        for term in terms[group + k :: group]:
+            value = value + term[...]
         out_ref[:, pl.ds(pl.multiple_of((member ^ k) * width, width), width)] = value
 
 
-def join(parts, terms):
-    rows, width = parts[0].shape
-    group = len(parts)
+def join(terms, group):
+    rows, width = terms[0].shape
     return pl.pallas_call(
         functools.partial(join_kernel, group),
-        in_specs=[VMEM] * (group + len(terms)),
+        in_specs=[VMEM] * len(terms),
         out_specs=VMEM,
         out_shape=jax.ShapeDtypeStruct((rows, group * width), jnp.float32),
         compiler_params=params(),
-    )(*parts, *terms)
+        cost_estimate=FREE,
+    )(*terms[group:], *terms[:group])
 
 
 def swap(value, axis, offset):
@@ -185,32 +201,26 @@
     mine, other, parts = project(snapshots, space_factor, group)
     parts = [part if k == 0 else swap(part, "tm", k) for k, part in enumerate(parts)]
 
-    terms = [mine] + [swap(other if k % 2 else mine, "space", k) for k in range(1, spaces)]
-    while len(terms) > 1:
-        terms = [a + b for a, b in zip(terms[::2], terms[1::2])]
-
-    pieces, order = terms[0], [0]
-    offsets = [1 << i for i in range(times.bit_length() - 1)]
+    mine = mine + swap(other, "space", 1)
+    for i in range(1, spaces.bit_length() - 1):
+        mine = mine + swap(mine, "space", 1 << i)
+
+    order, offsets = [0], [1 << i for i in range(times.bit_length() - 1)]
     for offset in [o for o in offsets if o >= group] + [o for o in offsets if o < group]:
-        pieces = jnp.concatenate([pieces, swap(pieces, "tm", offset)], axis=0)
-        if len(order) == 1:
-            pieces, parts[1:-1] = lax.optimization_barrier((pieces, parts[1:-1]))
-        elif len(order) == 2:
-            pieces, parts[-1] = lax.optimization_barrier((pieces, parts[-1]))
+        if offset < group:
+            mine, parts[offset] = lax.optimization_barrier((mine, parts[offset]))
+        mine = jnp.concatenate([mine, swap(mine, "tm", offset)], axis=0)
         order = order + [k ^ offset for k in order]
-    theirs = swap(pieces, "space", 1)
-
-    own, blocks = load(jnp.stack([index, core]), pieces, theirs, parts, times, order)
-    arrived = []
-    for i, k in enumerate(reversed(range(group))):
-        terms = [blocks[q + k] for q in range(group, times, group)]
-        if i >= 2:
-            terms, arrived[i - 2] = lax.optimization_barrier((terms, arrived[i - 2]))
-        arrived.append([swap(term, "tm", q) for term, q in zip(terms, range(group, times, group))])
-    received = []
-    for k in range(1, group):
-        received.append(swap(sum(arrived[group - 1 - k], blocks[k]), "tm", k))
-    return own, join([blocks[0], *received], arrived[-1])
+    theirs, parts[-1] = lax.optimization_barrier((swap(mine, "space", 1), parts[-1]))
+    high_t, low_t, own = mix(jnp.stack([index, core]), mine, theirs, times, group, order)
+
+    blocks = list(load(high_t, low_t, parts, times))
+    terms = [blocks[0]] + [None] * (times - 1)
+    for k in [*range(group, times), *range(1, group)]:
+        if 1 < k < group:
+            blocks[k], terms[k - 1] = lax.optimization_barrier((blocks[k], terms[k - 1]))
+        terms[k] = swap(blocks[k], "tm", k)
+    return own, join(terms, group)
 
 
 def solution(mesh):

time: 63.5 us -> 62.8 us (0.989)
  the two profiles are of different devices: /device:TPU:0 before, /device:TPU:8 now
where the time goes in v9:
time: 62.8 us; the launch traced here: 62.6 us
  waiting for transfers between devices  34 us (54%)
  starting transfers between devices  20.9 us (33%)
  Pallas kernels  6.82 us (11%)
  between operations  0.69 us (1%)
    ppermute x16, waiting for transfers between devices, swap(): lax.ppermute(value, axis, [(i, i ^ offset) for i in range(lax.axis_size(a...  34 us
    ppermute x16, starting transfers between devices, swap(): lax.ppermute(value, axis, [(i, i ^ offset) for i in range(lax.axis_size(a...  20.9 us
    pallas_call x1, Pallas kernels, project(): pl.pallas_call(functools.partial(project_kernel, depth), in_specs=[HBM, H...  2.93 us
    pallas_call x1, Pallas kernels, mix(): pl.pallas_call(functools.partial(mix_kernel, times, order), in_specs=[SME...  2.46 us
  transfers between devices with their start and end apart: 16, of which 12 were waited for; matrix products, arithmetic and copies ran while one was open for 0% of the time, Pallas kernels for 0%

profile of v9, /device:TPU:8, one launch (start us, length us, event | category | flops | bytes accessed | tf_op | source)
XLA Modules:
  0.0 62.6 jit_solution(913643035513700716)
XLA Ops:
  0.6 2.9 %shard_map.41 = (f32[32,256]{1,0:T(8,128)S(1)}, f32[32,256]{1,0:T(8,128)S(1)}, f32[64,1024]{1,0:T(8,128)S(1)}, f32[64,1024]{1,0:T(8,128)S(1)}, f32[64,1024]{1,0:T(8,128)S(1)}, /*index=5*/f32[64,1024]{1,0:T(8,128)S(1)}) custom-call(f32[64,4096]{1,0:T(8,128)} %snapshots_ref.1, f32[4096,256]{1,0:T(8,128)} %factor_ref.1), custom_call_target="tpu_custom_call" | custom-call | tf_op jit(solution)/shard_map/pallas_call | solution.py:76
  3.6 1.6 %collective-permute-start.3 = (f32[64,1024]{1,0:T(8,128)S(1)}, f32[64,1024]{1,0:T(8,128)S(1)}, u32[]{:S(2)}, u32[]{:S(2)}) collective-permute-start(f32[64,1024]{1,0:T(8,128)S(1)} %get-tuple-element.31), channel_id=1, source_target_pairs={{0,4},{4,0},{8,12},{12,8},{16,20},{20,16},{24,28},{28,24},{1,5},{5... | collective-permute-start | bytes 786440 | tf_op jit(solution)/shard_map/ppermute | solution.py:190
  5.1 0.0 collective-permute-start
  5.1 1.2 %collective-permute-done = f32[32,256]{1,0:T(8,128)S(1)} collective-permute-done((f32[32,256]{1,0:T(8,128)S(1)}, f32[32,256]{1,0:T(8,128)S(1)}, u32[]{:S(2)}, u32[]{:S(2)}) %collective-permute-start) | collective-permute-done | bytes 32800 | tf_op jit(solution)/shard_map/ppermute | solution.py:190
  6.3 1.5 %collective-permute-start.1 = (f32[32,256]{1,0:T(8,128)S(1)}, f32[32,256]{1,0:T(8,128)S(1)}, u32[]{:S(2)}, u32[]{:S(2)}) collective-permute-start(f32[32,256]{1,0:T(8,128)S(1)} %add.11), channel_id=1, source_target_pairs={{0,2},{1,3},{2,0},{3,1},{4,6},{5,7},{6,4},{7,5},{8,10},{9,11},{10,... | collective-permute-start | bytes 98312 | tf_op jit(solution)/shard_map/ppermute | solution.py:190
  7.9 2.4 %collective-permute-done.1 = f32[32,256]{1,0:T(8,128)S(1)} collective-permute-done((f32[32,256]{1,0:T(8,128)S(1)}, f32[32,256]{1,0:T(8,128)S(1)}, u32[]{:S(2)}, u32[]{:S(2)}) %collective-permute-start.1) | collective-permute-done | bytes 32800 | tf_op jit(solution)/shard_map/ppermute | solution.py:190
  10.3 2.6 %collective-permute-start.2 = (f32[32,256]{1,0:T(8,128)S(1)}, f32[32,256]{1,0:T(8,128)S(1)}, u32[]{:S(2)}, u32[]{:S(2)}) collective-permute-start(f32[32,256]{1,0:T(8,128)S(1)} %add.12), channel_id=1, source_target_pairs={{0,16},{4,20},{8,24},{12,28},{16,0},{20,4},{24,8},{28,12},{1,17},{... | collective-permute-start | bytes 98312 | tf_op jit(solution)/shard_map/ppermute | solution.py:190
  12.8 0.4 collective-permute-start.5
  13.3 2.2 %collective-permute-done.2 = f32[32,256]{1,0:T(8,128)S(1)} collective-permute-done((f32[32,256]{1,0:T(8,128)S(1)}, f32[32,256]{1,0:T(8,128)S(1)}, u32[]{:S(2)}, u32[]{:S(2)}) %collective-permute-start.2) | collective-permute-done | bytes 32800 | tf_op jit(solution)/shard_map/ppermute | solution.py:190
  15.5 0.0 collective-permute-done.3.refs_1_
  15.5 0.6 collective-permute-start.4
  16.1 3.7 %collective-permute-done.4 = f32[64,256]{1,0:T(8,128)S(1)} collective-permute-done((f32[64,256]{1,0:T(8,128)S(1)}, f32[64,256]{1,0:T(8,128)S(1)}, u32[]{:S(2)}, u32[]{:S(2)}) %collective-permute-start.4) | collective-permute-done | bytes 65568 | tf_op jit(solution)/shard_map/ppermute | solution.py:190
  19.8 0.6 collective-permute-done.5.refs_2_
  20.4 0.4 collective-permute-start.6
  20.9 1.5 %collective-permute-start.8 = (f32[64,1024]{1,0:T(8,128)S(1)}, f32[64,1024]{1,0:T(8,128)S(1)}, u32[]{:S(2)}, u32[]{:S(2)}) collective-permute-start(f32[64,1024]{1,0:T(8,128)S(1)} %get-tuple-element.35), channel_id=1, source_target_pairs={{0,12},{4,8},{8,4},{12,0},{16,28},{20,24},{24,20},{28,16},{1,13},{... | collective-permute-start | bytes 786440 | tf_op jit(solution)/shard_map/ppermute | solution.py:190
  22.4 4.4 %collective-permute-done.6 = f32[128,256]{1,0:T(8,128)S(1)} collective-permute-done((f32[128,256]{1,0:T(8,128)S(1)}, f32[128,256]{1,0:T(8,128)S(1)}, u32[]{:S(2)}, u32[]{:S(2)}) %collective-permute-start.6) | collective-permute-done | bytes 131104 | tf_op jit(solution)/shard_map/ppermute | solution.py:190
  26.9 0.1 collective-permute-start.7
  27.0 0.1 pad_add_fusion.index_ref
  27.1 2.8 %collective-permute-done.8.refs_3_ = f32[64,1024]{1,0:T(8,128)S(1)} collective-permute-done((f32[64,1024]{1,0:T(8,128)S(1)}, f32[64,1024]{1,0:T(8,128)S(1)}, u32[]{:S(2)}, u32[]{:S(2)}) %collective-permute-start.8) | collective-permute-done | bytes 262176 | tf_op jit(solution)/shard_map/ppermute | solution.py:190
  29.9 0.0 collective-permute-done.7.theirs_ref
  29.9 2.5 %shard_map.42 = (bf16[256,256]{1,0:T(8,128)(2,1)S(1)}, bf16[256,256]{1,0:T(8,128)(2,1)S(1)}, f32[64,256]{1,0:T(8,128)}) custom-call(s32[2]{0:T(128)S(1)} %pad_add_fusion.index_ref, f32[256,256]{1,0:T(8,128)S(1)} %constant_dynamic-update-slice_fusion.mine_ref, f32[256,256]{1,0:T(8,128)S(1)} %collective-permute-done.7.theirs_ref), custom_call_target="tpu_custom_call" | custom-call | tf_op jit(solution)/shard_map/pallas_call | solution.py:133
  32.3 0.6 shard_map.43
  32.9 1.6 %collective-permute-start.13 = (f32[32,1024]{1,0:T(8,128)S(1)}, f32[32,1024]{1,0:T(8,128)S(1)}, u32[]{:S(2)}, u32[]{:S(2)}) collective-permute-start(f32[32,1024]{1,0:T(8,128)S(1)} %get-tuple-element.50), channel_id=1, source_target_pairs={{0,4},{4,0},{8,12},{12,8},{16,20},{20,16},{24,28},{28,24},{1,5},{5... | collective-permute-start | bytes 393224 | tf_op jit(solution)/shard_map/ppermute | solution.py:190
  34.5 3.5 %collective-permute-done.13.refs_5_ = f32[32,1024]{1,0:T(8,128)S(1)} collective-permute-done((f32[32,1024]{1,0:T(8,128)S(1)}, f32[32,1024]{1,0:T(8,128)S(1)}, u32[]{:S(2)}, u32[]{:S(2)}) %collective-permute-start.13) | collective-permute-done | bytes 131104 | tf_op jit(solution)/shard_map/ppermute | solution.py:190
  38.0 1.3 %collective-permute-start.14 = (f32[32,1024]{1,0:T(8,128)S(1)}, f32[32,1024]{1,0:T(8,128)S(1)}, u32[]{:S(2)}, u32[]{:S(2)}) collective-permute-start(f32[32,1024]{1,0:T(8,128)S(1)} %get-tuple-element.53), channel_id=1, source_target_pairs={{0,8},{4,12},{8,0},{12,4},{16,24},{20,28},{24,16},{28,20},{1,9},{5... | collective-permute-start | bytes 393224 | tf_op jit(solution)/shard_map/ppermute | solution.py:190
  39.2 0.9 %collective-permute-start.9 = (f32[32,1024]{1,0:T(8,128)S(1)}, f32[32,1024]{1,0:T(8,128)S(1)}, u32[]{:S(2)}, u32[]{:S(2)}) collective-permute-start(f32[32,1024]{1,0:T(8,128)S(1)} %get-tuple-element.44), channel_id=1, source_target_pairs={{0,16},{4,20},{8,24},{12,28},{16,0},{20,4},{24,8},{28,12},{1,17},{... | collective-permute-start | bytes 393224 | tf_op jit(solution)/shard_map/ppermute | solution.py:190
  40.1 2.2 %collective-permute-start.10 = (f32[32,1024]{1,0:T(8,128)S(1)}, f32[32,1024]{1,0:T(8,128)S(1)}, u32[]{:S(2)}, u32[]{:S(2)}) collective-permute-start(f32[32,1024]{1,0:T(8,128)S(1)} %get-tuple-element.45), channel_id=1, source_target_pairs={{0,20},{4,16},{8,28},{12,24},{16,4},{20,0},{24,12},{28,8},{1,21},{... | collective-permute-start | bytes 393224 | tf_op jit(solution)/shard_map/ppermute | solution.py:190
  42.3 1.0 %collective-permute-start.11 = (f32[32,1024]{1,0:T(8,128)S(1)}, f32[32,1024]{1,0:T(8,128)S(1)}, u32[]{:S(2)}, u32[]{:S(2)}) collective-permute-start(f32[32,1024]{1,0:T(8,128)S(1)} %get-tuple-element.46), channel_id=1, source_target_pairs={{0,24},{4,28},{8,16},{12,20},{16,8},{20,12},{24,0},{28,4},{1,25},{... | collective-permute-start | bytes 393224 | tf_op jit(solution)/shard_map/ppermute | solution.py:190
  43.2 1.9 %collective-permute-start.12 = (f32[32,1024]{1,0:T(8,128)S(1)}, f32[32,1024]{1,0:T(8,128)S(1)}, u32[]{:S(2)}, u32[]{:S(2)}) collective-permute-start(f32[32,1024]{1,0:T(8,128)S(1)} %get-tuple-element.47), channel_id=1, source_target_pairs={{0,28},{4,24},{8,20},{12,16},{16,12},{20,8},{24,4},{28,0},{1,29},{... | collective-permute-start | bytes 393224 | tf_op jit(solution)/shard_map/ppermute | solution.py:190
  45.1 0.0 collective-permute-done.14.refs_6_
  45.1 3.5 %collective-permute-start.15 = (f32[32,1024]{1,0:T(8,128)S(1)}, f32[32,1024]{1,0:T(8,128)S(1)}, u32[]{:S(2)}, u32[]{:S(2)}) collective-permute-start(f32[32,1024]{1,0:T(8,128)S(1)} %get-tuple-element.55), channel_id=1, source_target_pairs={{0,12},{4,8},{8,4},{12,0},{16,28},{20,24},{24,20},{28,16},{1,13},{... | collective-permute-start | bytes 393224 | tf_op jit(solution)/shard_map/ppermute | solution.py:190
  48.6 2.1 %collective-permute-done.9.refs_0_ = f32[32,1024]{1,0:T(8,128)S(1)} collective-permute-done((f32[32,1024]{1,0:T(8,128)S(1)}, f32[32,1024]{1,0:T(8,128)S(1)}, u32[]{:S(2)}, u32[]{:S(2)}) %collective-permute-start.9) | collective-permute-done | bytes 131104 | tf_op jit(solution)/shard_map/ppermute | solution.py:190
  50.7 5.0 %collective-permute-done.10.refs_1_ = f32[32,1024]{1,0:T(8,128)S(1)} collective-permute-done((f32[32,1024]{1,0:T(8,128)S(1)}, f32[32,1024]{1,0:T(8,128)S(1)}, u32[]{:S(2)}, u32[]{:S(2)}) %collective-permute-start.10) | collective-permute-done | bytes 131104 | tf_op jit(solution)/shard_map/ppermute | solution.py:190
  55.7 4.5 %collective-permute-done.11.refs_2_ = f32[32,1024]{1,0:T(8,128)S(1)} collective-permute-done((f32[32,1024]{1,0:T(8,128)S(1)}, f32[32,1024]{1,0:T(8,128)S(1)}, u32[]{:S(2)}, u32[]{:S(2)}) %collective-permute-start.11) | collective-permute-done | bytes 131104 | tf_op jit(solution)/shard_map/ppermute | solution.py:190
  60.2 1.6 %collective-permute-done.12.refs_3_ = f32[32,1024]{1,0:T(8,128)S(1)} collective-permute-done((f32[32,1024]{1,0:T(8,128)S(1)}, f32[32,1024]{1,0:T(8,128)S(1)}, u32[]{:S(2)}, u32[]{:S(2)}) %collective-permute-start.12) | collective-permute-done | bytes 131104 | tf_op jit(solution)/shard_map/ppermute | solution.py:190
  61.8 0.0 collective-permute-done.15.refs_7_
  61.8 0.8 %shard_map.44 = f32[32,4096]{1,0:T(8,128)} custom-call(f32[32,1024]{1,0:T(8,128)S(1)} %collective-permute-done.9.refs_0_, f32[32,1024]{1,0:T(8,128)S(1)} %collective-permute-done.10.refs_1_, f32[32,1024]{1,0:T(8,128)S(1)} %collective-permute-done.11.refs_2_, f32[32,1024]{1,0:T(8,128)S(1)} %collective-permute-done.12.refs_3_, ...), custom_call_target="tpu_custom_call" | custom-call | tf_op jit(solution)/shard_map/pallas_call | solution.py:179
  (6 shorter events, 0.0 us)
Async XLA Ops:
  3.6 11.9 %collective-permute-start.3 = (f32[64,1024]{1,0:T(8,128)S(1)}, f32[64,1024]{1,0:T(8,128)S(1)}, u32[]{:S(2)}, u32[]{:S(2)}) collective-permute-start(f32[64,1024]{1,0:T(8,128)S(1)} %get-tuple-element.31), channel_id=1, source_target_pairs={{0,4},{4,0},{8,12},{12,8},{16,20},{20,16},{24,28},{28,24},{1,5},{5... | collective-permute-start | bytes 786440 | tf_op jit(solution)/shard_map/ppermute | solution.py:190
  5.1 1.2 %collective-permute-start = (f32[32,256]{1,0:T(8,128)S(1)}, f32[32,256]{1,0:T(8,128)S(1)}, u32[]{:S(2)}, u32[]{:S(2)}) collective-permute-start(f32[32,256]{1,0:T(8,128)S(1)} %get-tuple-element.30), channel_id=1, source_target_pairs={{0,1},{1,0},{2,3},{3,2},{4,5},{5,4},{6,7},{7,6},{8,9},{9,8},{10,11... | collective-permute-start | bytes 98312 | tf_op jit(solution)/shard_map/ppermute | solution.py:190
  6.3 3.9 %collective-permute-start.1 = (f32[32,256]{1,0:T(8,128)S(1)}, f32[32,256]{1,0:T(8,128)S(1)}, u32[]{:S(2)}, u32[]{:S(2)}) collective-permute-start(f32[32,256]{1,0:T(8,128)S(1)} %add.11), channel_id=1, source_target_pairs={{0,2},{1,3},{2,0},{3,1},{4,6},{5,7},{6,4},{7,5},{8,10},{9,11},{10,... | collective-permute-start | bytes 98312 | tf_op jit(solution)/shard_map/ppermute | solution.py:190
  10.3 5.2 %collective-permute-start.2 = (f32[32,256]{1,0:T(8,128)S(1)}, f32[32,256]{1,0:T(8,128)S(1)}, u32[]{:S(2)}, u32[]{:S(2)}) collective-permute-start(f32[32,256]{1,0:T(8,128)S(1)} %add.12), channel_id=1, source_target_pairs={{0,16},{4,20},{8,24},{12,28},{16,0},{20,4},{24,8},{28,12},{1,17},{... | collective-permute-start | bytes 98312 | tf_op jit(solution)/shard_map/ppermute | solution.py:190
  12.8 7.6 %collective-permute-start.5 = (f32[64,1024]{1,0:T(8,128)S(1)}, f32[64,1024]{1,0:T(8,128)S(1)}, u32[]{:S(2)}, u32[]{:S(2)}) collective-permute-start(f32[64,1024]{1,0:T(8,128)S(1)} %get-tuple-element.33), channel_id=1, source_target_pairs={{0,8},{4,12},{8,0},{12,4},{16,24},{20,28},{24,16},{28,20},{1,9},{5... | collective-permute-start | bytes 786440 | tf_op jit(solution)/shard_map/ppermute | solution.py:190
  15.5 4.3 %collective-permute-start.4 = (f32[64,256]{1,0:T(8,128)S(1)}, f32[64,256]{1,0:T(8,128)S(1)}, u32[]{:S(2)}, u32[]{:S(2)}) collective-permute-start(f32[64,256]{1,0:T(8,128)S(1)} %pad_maximum_fusion.1), channel_id=1, source_target_pairs={{0,4},{4,0},{8,12},{12,8},{16,20},{20,16},{24,28},{28,24},{1,5},{5... | collective-permute-start | bytes 196616 | tf_op jit(solution)/shard_map/ppermute | solution.py:190
  20.4 6.4 %collective-permute-start.6 = (f32[128,256]{1,0:T(8,128)S(1)}, f32[128,256]{1,0:T(8,128)S(1)}, u32[]{:S(2)}, u32[]{:S(2)}) collective-permute-start(f32[128,256]{1,0:T(8,128)S(1)} %pad_maximum_fusion), channel_id=1, source_target_pairs={{0,8},{4,12},{8,0},{12,4},{16,24},{20,28},{24,16},{28,20},{1,9},{5... | collective-permute-start | bytes 393224 | tf_op jit(solution)/shard_map/ppermute | solution.py:190
  20.9 9.0 %collective-permute-start.8 = (f32[64,1024]{1,0:T(8,128)S(1)}, f32[64,1024]{1,0:T(8,128)S(1)}, u32[]{:S(2)}, u32[]{:S(2)}) collective-permute-start(f32[64,1024]{1,0:T(8,128)S(1)} %get-tuple-element.35), channel_id=1, source_target_pairs={{0,12},{4,8},{8,4},{12,0},{16,28},{20,24},{24,20},{28,16},{1,13},{... | collective-permute-start | bytes 786440 | tf_op jit(solution)/shard_map/ppermute | solution.py:190
  26.9 3.0 %collective-permute-start.7 = (f32[256,256]{1,0:T(8,128)S(1)}, f32[256,256]{1,0:T(8,128)S(1)}, u32[]{:S(2)}, u32[]{:S(2)}) collective-permute-start(f32[256,256]{1,0:T(8,128)S(1)} %constant_dynamic-update-slice_fusion.mine_ref), channel_id=1, source_target_pairs={{0,1},{1,0},{2,3},{3,2},{4,5},{5,4},{6,7},{7,6},{8,9},{9,8},{10,11... | collective-permute-start | bytes 786440 | tf_op jit(solution)/shard_map/ppermute | solution.py:190
  32.9 5.0 %collective-permute-start.13 = (f32[32,1024]{1,0:T(8,128)S(1)}, f32[32,1024]{1,0:T(8,128)S(1)}, u32[]{:S(2)}, u32[]{:S(2)}) collective-permute-start(f32[32,1024]{1,0:T(8,128)S(1)} %get-tuple-element.50), channel_id=1, source_target_pairs={{0,4},{4,0},{8,12},{12,8},{16,20},{20,16},{24,28},{28,24},{1,5},{5... | collective-permute-start | bytes 393224 | tf_op jit(solution)/shard_map/ppermute | solution.py:190
  38.0 7.1 %collective-permute-start.14 = (f32[32,1024]{1,0:T(8,128)S(1)}, f32[32,1024]{1,0:T(8,128)S(1)}, u32[]{:S(2)}, u32[]{:S(2)}) collective-permute-start(f32[32,1024]{1,0:T(8,128)S(1)} %get-tuple-element.53), channel_id=1, source_target_pairs={{0,8},{4,12},{8,0},{12,4},{16,24},{20,28},{24,16},{28,20},{1,9},{5... | collective-permute-start | bytes 393224 | tf_op jit(solution)/shard_map/ppermute | solution.py:190
  39.2 11.4 %collective-permute-start.9 = (f32[32,1024]{1,0:T(8,128)S(1)}, f32[32,1024]{1,0:T(8,128)S(1)}, u32[]{:S(2)}, u32[]{:S(2)}) collective-permute-start(f32[32,1024]{1,0:T(8,128)S(1)} %get-tuple-element.44), channel_id=1, source_target_pairs={{0,16},{4,20},{8,24},{12,28},{16,0},{20,4},{24,8},{28,12},{1,17},{... | collective-permute-start | bytes 393224 | tf_op jit(solution)/shard_map/ppermute | solution.py:190
  40.1 15.6 %collective-permute-start.10 = (f32[32,1024]{1,0:T(8,128)S(1)}, f32[32,1024]{1,0:T(8,128)S(1)}, u32[]{:S(2)}, u32[]{:S(2)}) collective-permute-start(f32[32,1024]{1,0:T(8,128)S(1)} %get-tuple-element.45), channel_id=1, source_target_pairs={{0,20},{4,16},{8,28},{12,24},{16,4},{20,0},{24,12},{28,8},{1,21},{... | collective-permute-start | bytes 393224 | tf_op jit(solution)/shard_map/ppermute | solution.py:190
  42.3 17.9 %collective-permute-start.11 = (f32[32,1024]{1,0:T(8,128)S(1)}, f32[32,1024]{1,0:T(8,128)S(1)}, u32[]{:S(2)}, u32[]{:S(2)}) collective-permute-start(f32[32,1024]{1,0:T(8,128)S(1)} %get-tuple-element.46), channel_id=1, source_target_pairs={{0,24},{4,28},{8,16},{12,20},{16,8},{20,12},{24,0},{28,4},{1,25},{... | collective-permute-start | bytes 393224 | tf_op jit(solution)/shard_map/ppermute | solution.py:190
  43.2 18.5 %collective-permute-start.12 = (f32[32,1024]{1,0:T(8,128)S(1)}, f32[32,1024]{1,0:T(8,128)S(1)}, u32[]{:S(2)}, u32[]{:S(2)}) collective-permute-start(f32[32,1024]{1,0:T(8,128)S(1)} %get-tuple-element.47), channel_id=1, source_target_pairs={{0,28},{4,24},{8,20},{12,16},{16,12},{20,8},{24,4},{28,0},{1,29},{... | collective-permute-start | bytes 393224 | tf_op jit(solution)/shard_map/ppermute | solution.py:190
  45.1 16.7 %collective-permute-start.15 = (f32[32,1024]{1,0:T(8,128)S(1)}, f32[32,1024]{1,0:T(8,128)S(1)}, u32[]{:S(2)}, u32[]{:S(2)}) collective-permute-start(f32[32,1024]{1,0:T(8,128)S(1)} %get-tuple-element.55), channel_id=1, source_target_pairs={{0,12},{4,8},{8,4},{12,0},{16,28},{20,24},{24,20},{28,16},{1,13},{... | collective-permute-start | bytes 393224 | tf_op jit(solution)/shard_map/ppermute | solution.py:190

commit v10 on v9

--- a/solution.py
+++ b/solution.py
@@ -89,11 +89,11 @@
     return mine, other, parts
 
 
-def mix_kernel(times, order, index_ref, mine_ref, theirs_ref, high_t_ref, low_t_ref, own_ref):
-    total_half, rank = mine_ref.shape
-    half = total_half // times
-    mine = mine_ref[...].reshape(times, half, rank)
-    theirs = theirs_ref[...].reshape(times, half, rank)
+def mix_kernel(index_ref, mine_ref, theirs_ref, high_t_ref, low_t_ref, own_ref):
+    times, half, rank = mine_ref.shape
+    total_half = times * half
+    mine = jnp.stack([mine_ref[index_ref[0] ^ k] for k in range(times)])
+    theirs = jnp.stack([theirs_ref[index_ref[0] ^ k] for k in range(times)])
     first = index_ref[1] == 0
     low_rows, high_rows = jnp.where(first, mine, theirs), jnp.where(first, theirs, mine)
     projected = jnp.concatenate([low_rows, high_rows], axis=1).reshape(2 * total_half, rank)
@@ -111,10 +111,7 @@
     mixing_high, mixing_low = split(mixing)
 
     rows = 2 * half
-    group = high_t_ref.shape[1] // rows
-    places = [order.index(k) for k in range(group)]
-    high = jnp.concatenate([high[i * rows : (i + 1) * rows] for i in places], axis=0)
-    low = jnp.concatenate([low[i * rows : (i + 1) * rows] for i in places], axis=0)
+    high, low = high[: high_t_ref.shape[1]], low[: high_t_ref.shape[1]]
     scale = lax.rsqrt(total)
     own = product((high[:rows], low[:rows]), (mixing_high, mixing_low))
     own_ref[...] = own * (scale * math.sqrt(times * rows))
@@ -126,12 +123,12 @@
     high_t_ref[...], low_t_ref[...] = split(turned)
 
 
-def mix(index, mine, theirs, times, group, order):
-    total_half, rank = mine.shape
-    rows = 2 * total_half // times
+def mix(index, mine, theirs, group):
+    times, half, rank = mine.shape
+    rows = 2 * half
     factor = jax.ShapeDtypeStruct((rank, group * rows), jnp.bfloat16)
     return pl.pallas_call(
-        functools.partial(mix_kernel, times, order),
+        mix_kernel,
         in_specs=[SMEM, VMEM, VMEM],
         out_specs=[VMEM] * 3,
         out_shape=[factor, factor, jax.ShapeDtypeStruct((rows, rank), jnp.float32)],
@@ -164,7 +161,6 @@
 
 def join_kernel(group, *refs):
     *terms, out_ref = refs
-    terms = terms[-group:] + terms[:-group]
     width = terms[0].shape[1]
     member = lax.rem(lax.axis_index("tm"), group)
     for k in range(group):
@@ -183,7 +179,7 @@
         out_shape=jax.ShapeDtypeStruct((rows, group * width), jnp.float32),
         compiler_params=params(),
         cost_estimate=FREE,
-    )(*terms[group:], *terms[:group])
+    )(*terms)
 
 
 def swap(value, axis, offset):
@@ -205,20 +201,16 @@
     for i in range(1, spaces.bit_length() - 1):
         mine = mine + swap(mine, "space", 1 << i)
 
-    order, offsets = [0], [1 << i for i in range(times.bit_length() - 1)]
-    for offset in [o for o in offsets if o >= group] + [o for o in offsets if o < group]:
-        if offset < group:
-            mine, parts[offset] = lax.optimization_barrier((mine, parts[offset]))
-        mine = jnp.concatenate([mine, swap(mine, "tm", offset)], axis=0)
-        order = order + [k ^ offset for k in order]
+    mine, *parts[1:-1] = lax.optimization_barrier((mine, *parts[1:-1]))
+    mine = lax.all_to_all(jnp.broadcast_to(mine, (times, *mine.shape)), "tm", 0, 0, tiled=True)
     theirs, parts[-1] = lax.optimization_barrier((swap(mine, "space", 1), parts[-1]))
-    high_t, low_t, own = mix(jnp.stack([index, core]), mine, theirs, times, group, order)
+    high_t, low_t, own = mix(jnp.stack([index, core]), mine, theirs, group)
 
     blocks = list(load(high_t, low_t, parts, times))
     terms = [blocks[0]] + [None] * (times - 1)
     for k in [*range(group, times), *range(1, group)]:
-        if 1 < k < group:
-            blocks[k], terms[k - 1] = lax.optimization_barrier((blocks[k], terms[k - 1]))
+        if k == group - 1:
+            blocks[k], terms[1] = lax.optimization_barrier((blocks[k], terms[1]))
         terms[k] = swap(blocks[k], "tm", k)
     return own, join(terms, group)
 

time: 62.8 us -> 60.9 us (0.970)
  waiting for transfers between devices: 34 us -> 30.8 us
  local copies, waits for them, and re-layouts: 0.02 us -> 0.72 us
    ppermute x16 -> x13, waiting for transfers between devices: 34 us -> 23.7 us  [swap(): lax.ppermute(value, axis, [(i, i ^ offset) for i in range(lax.axis_size(a...]
    all_to_all x0 -> x1, waiting for transfers between devices: none -> 7.13 us  [on_device(): lax.all_to_all(jnp.broadcast_to(mine, (times, *mine.shape)), 'tm', 0, 0,...]
    all_to_all x0 -> x1, starting transfers between devices: none -> 5.32 us  [on_device(): lax.all_to_all(jnp.broadcast_to(mine, (times, *mine.shape)), 'tm', 0, 0,...]
    ppermute x16 -> x13, starting transfers between devices: 20.9 us -> 16.2 us  [swap(): lax.ppermute(value, axis, [(i, i ^ offset) for i in range(lax.axis_size(a...]
    broadcast_in_dim x0 -> x1, local copies, waits for them, and re-layouts: none -> 0.72 us  [on_device(): jnp.broadcast_to(mine, (times, *mine.shape))]
  transfers between devices with their start and end apart: 16 -> 14, of which waited for: 12 -> 10; matrix products, arithmetic and copies ran while one was open for 0% -> 0% of each run, Pallas kernels for 0% -> 0%
where the time goes in v10:
time: 60.9 us; the launch traced here: 60.6 us
  waiting for transfers between devices  30.8 us (51%)
  starting transfers between devices  21.5 us (35%)
  Pallas kernels  6.83 us (11%)
  local copies, waits for them, and re-layouts  0.72 us (1%)
  between operations  0.66 us (1%)
    ppermute x13, waiting for transfers between devices, swap(): lax.ppermute(value, axis, [(i, i ^ offset) for i in range(lax.axis_size(a...  23.7 us
    ppermute x13, starting transfers between devices, swap(): lax.ppermute(value, axis, [(i, i ^ offset) for i in range(lax.axis_size(a...  16.2 us
    all_to_all x1, waiting for transfers between devices, on_device(): lax.all_to_all(jnp.broadcast_to(mine, (times, *mine.shape)), 'tm', 0, 0,...  7.13 us
    all_to_all x1, starting transfers between devices, on_device(): lax.all_to_all(jnp.broadcast_to(mine, (times, *mine.shape)), 'tm', 0, 0,...  5.32 us
    pallas_call x1, Pallas kernels, project(): pl.pallas_call(functools.partial(project_kernel, depth), in_specs=[HBM, H...  2.93 us
    pallas_call x1, Pallas kernels, mix(): pl.pallas_call(mix_kernel, in_specs=[SMEM, VMEM, VMEM], out_specs=[VMEM]...  2.46 us
  transfers between devices with their start and end apart: 14, of which 10 were waited for; matrix products, arithmetic and copies ran while one was open for 0% of the time, Pallas kernels for 0%

profile of v10, /device:TPU:8, one launch (start us, length us, event | category | flops | bytes accessed | tf_op | source)
XLA Modules:
  0.0 60.6 jit_solution(18201183277217020075)
XLA Ops:
  0.6 2.9 %shard_map.41 = (f32[32,256]{1,0:T(8,128)S(1)}, f32[32,256]{1,0:T(8,128)S(1)}, f32[64,1024]{1,0:T(8,128)S(1)}, f32[64,1024]{1,0:T(8,128)S(1)}, f32[64,1024]{1,0:T(8,128)S(1)}, /*index=5*/f32[64,1024]{1,0:T(8,128)S(1)}) custom-call(f32[64,4096]{1,0:T(8,128)} %snapshots_ref.1, f32[4096,256]{1,0:T(8,128)} %factor_ref.1), custom_call_target="tpu_custom_call" | custom-call | tf_op jit(solution)/shard_map/pallas_call | solution.py:76
  3.6 1.6 %collective-permute-start.2 = (f32[64,1024]{1,0:T(8,128)S(1)}, f32[64,1024]{1,0:T(8,128)S(1)}, u32[]{:S(2)}, u32[]{:S(2)}) collective-permute-start(f32[64,1024]{1,0:T(8,128)S(1)} %get-tuple-element.28), channel_id=1, source_target_pairs={{0,4},{4,0},{8,12},{12,8},{16,20},{20,16},{24,28},{28,24},{1,5},{5... | collective-permute-start | bytes 786440 | tf_op jit(solution)/shard_map/ppermute | solution.py:186
  5.1 0.5 collective-permute-start.3
  5.6 0.0 collective-permute-start
  5.6 1.2 %collective-permute-done = f32[32,256]{1,0:T(8,128)S(1)} collective-permute-done((f32[32,256]{1,0:T(8,128)S(1)}, f32[32,256]{1,0:T(8,128)S(1)}, u32[]{:S(2)}, u32[]{:S(2)}) %collective-permute-start) | collective-permute-done | bytes 32800 | tf_op jit(solution)/shard_map/ppermute | solution.py:186
  6.8 1.5 %collective-permute-start.1 = (f32[32,256]{1,0:T(8,128)S(1)}, f32[32,256]{1,0:T(8,128)S(1)}, u32[]{:S(2)}, u32[]{:S(2)}) collective-permute-start(f32[32,256]{1,0:T(8,128)S(1)} %add.11), channel_id=1, source_target_pairs={{0,2},{1,3},{2,0},{3,1},{4,6},{5,7},{6,4},{7,5},{8,10},{9,11},{10,... | collective-permute-start | bytes 98312 | tf_op jit(solution)/shard_map/ppermute | solution.py:186
  8.3 2.4 %collective-permute-done.1 = f32[32,256]{1,0:T(8,128)S(1)} collective-permute-done((f32[32,256]{1,0:T(8,128)S(1)}, f32[32,256]{1,0:T(8,128)S(1)}, u32[]{:S(2)}, u32[]{:S(2)}) %collective-permute-start.1) | collective-permute-done | bytes 32800 | tf_op jit(solution)/shard_map/ppermute | solution.py:186
  10.7 1.0 %collective-permute-done.2.refs_1_ = f32[64,1024]{1,0:T(8,128)S(1)} collective-permute-done((f32[64,1024]{1,0:T(8,128)S(1)}, f32[64,1024]{1,0:T(8,128)S(1)}, u32[]{:S(2)}, u32[]{:S(2)}) %collective-permute-start.2) | collective-permute-done | bytes 262176 | tf_op jit(solution)/shard_map/ppermute | solution.py:186
  11.7 1.2 %collective-permute-done.3.refs_2_ = f32[64,1024]{1,0:T(8,128)S(1)} collective-permute-done((f32[64,1024]{1,0:T(8,128)S(1)}, f32[64,1024]{1,0:T(8,128)S(1)}, u32[]{:S(2)}, u32[]{:S(2)}) %collective-permute-start.3) | collective-permute-done | bytes 262176 | tf_op jit(solution)/shard_map/ppermute | solution.py:186
  12.9 0.7 %broadcast_in_dim.3 = f32[8,32,256]{2,1,0:T(8,128)} broadcast(f32[32,256]{1,0:T(8,128)S(1)} %add.12), dimensions={1,2} | broadcast | bytes 294912 | tf_op jit(solution)/shard_map/broadcast_in_dim | solution.py:205
  13.6 5.3 %all-to-all-start = ((f32[8,32,256]{2,1,0:T(8,128)}), f32[8,32,256]{2,1,0:T(8,128)S(1)}, u32[]{:S(2)}, u32[]{:S(2)}) async-start(f32[8,32,256]{2,1,0:T(8,128)} %broadcast_in_dim.3), calls=%async_computation | async-start | bytes 524288 | tf_op jit(solution)/shard_map/all_to_all | solution.py:205
  18.9 1.5 %collective-permute-start.5 = (f32[64,1024]{1,0:T(8,128)S(1)}, f32[64,1024]{1,0:T(8,128)S(1)}, u32[]{:S(2)}, u32[]{:S(2)}) collective-permute-start(f32[64,1024]{1,0:T(8,128)S(1)} %get-tuple-element.31), channel_id=1, source_target_pairs={{0,12},{4,8},{8,4},{12,0},{16,28},{20,24},{24,20},{28,16},{1,13},{... | collective-permute-start | bytes 786440 | tf_op jit(solution)/shard_map/ppermute | solution.py:186
  20.4 7.1 %all-to-all-done.mine_ref = f32[8,32,256]{2,1,0:T(8,128)S(1)} async-done(((f32[8,32,256]{2,1,0:T(8,128)}), f32[8,32,256]{2,1,0:T(8,128)S(1)}, u32[]{:S(2)}, u32[]{:S(2)}) %all-to-all-start) | async-done | bytes 262176 | tf_op jit(solution)/shard_map/all_to_all | solution.py:205
  27.5 0.0 collective-permute-start.4
  27.5 0.1 pad_add_fusion.index_ref
  27.6 1.8 %collective-permute-done.5.refs_3_ = f32[64,1024]{1,0:T(8,128)S(1)} collective-permute-done((f32[64,1024]{1,0:T(8,128)S(1)}, f32[64,1024]{1,0:T(8,128)S(1)}, u32[]{:S(2)}, u32[]{:S(2)}) %collective-permute-start.5) | collective-permute-done | bytes 262176 | tf_op jit(solution)/shard_map/ppermute | solution.py:186
  29.4 0.0 collective-permute-done.4.theirs_ref
  29.4 2.5 %shard_map.42 = (bf16[256,256]{1,0:T(8,128)(2,1)S(1)}, bf16[256,256]{1,0:T(8,128)(2,1)S(1)}, f32[64,256]{1,0:T(8,128)}) custom-call(s32[2]{0:T(128)S(1)} %pad_add_fusion.index_ref, f32[8,32,256]{2,1,0:T(8,128)S(1)} %all-to-all-done.mine_ref, f32[8,32,256]{2,1,0:T(8,128)S(1)} %collective-permute-done.4.theirs_ref), custom_call_target="tpu_custom_call" | custom-call | tf_op jit(solution)/shard_map/pallas_call | solution.py:130
  31.9 0.6 shard_map.43
  32.5 1.0 %collective-permute-start.6 = (f32[32,1024]{1,0:T(8,128)S(1)}, f32[32,1024]{1,0:T(8,128)S(1)}, u32[]{:S(2)}, u32[]{:S(2)}) collective-permute-start(f32[32,1024]{1,0:T(8,128)S(1)} %get-tuple-element.42), channel_id=1, source_target_pairs={{0,4},{4,0},{8,12},{12,8},{16,20},{20,16},{24,28},{28,24},{1,5},{5... | collective-permute-start | bytes 393224 | tf_op jit(solution)/shard_map/ppermute | solution.py:186
  33.4 1.4 %collective-permute-start.7 = (f32[32,1024]{1,0:T(8,128)S(1)}, f32[32,1024]{1,0:T(8,128)S(1)}, u32[]{:S(2)}, u32[]{:S(2)}) collective-permute-start(f32[32,1024]{1,0:T(8,128)S(1)} %get-tuple-element.44), channel_id=1, source_target_pairs={{0,8},{4,12},{8,0},{12,4},{16,24},{20,28},{24,16},{28,20},{1,9},{5... | collective-permute-start | bytes 393224 | tf_op jit(solution)/shard_map/ppermute | solution.py:186
  34.8 2.3 %collective-permute-start.9 = (f32[32,1024]{1,0:T(8,128)S(1)}, f32[32,1024]{1,0:T(8,128)S(1)}, u32[]{:S(2)}, u32[]{:S(2)}) collective-permute-start(f32[32,1024]{1,0:T(8,128)S(1)} %get-tuple-element.46), channel_id=1, source_target_pairs={{0,16},{4,20},{8,24},{12,28},{16,0},{20,4},{24,8},{28,12},{1,17},{... | collective-permute-start | bytes 393224 | tf_op jit(solution)/shard_map/ppermute | solution.py:186
  37.1 1.3 %collective-permute-start.10 = (f32[32,1024]{1,0:T(8,128)S(1)}, f32[32,1024]{1,0:T(8,128)S(1)}, u32[]{:S(2)}, u32[]{:S(2)}) collective-permute-start(f32[32,1024]{1,0:T(8,128)S(1)} %get-tuple-element.47), channel_id=1, source_target_pairs={{0,20},{4,16},{8,28},{12,24},{16,4},{20,0},{24,12},{28,8},{1,21},{... | collective-permute-start | bytes 393224 | tf_op jit(solution)/shard_map/ppermute | solution.py:186
  38.4 1.5 %collective-permute-start.11 = (f32[32,1024]{1,0:T(8,128)S(1)}, f32[32,1024]{1,0:T(8,128)S(1)}, u32[]{:S(2)}, u32[]{:S(2)}) collective-permute-start(f32[32,1024]{1,0:T(8,128)S(1)} %get-tuple-element.48), channel_id=1, source_target_pairs={{0,24},{4,28},{8,16},{12,20},{16,8},{20,12},{24,0},{28,4},{1,25},{... | collective-permute-start | bytes 393224 | tf_op jit(solution)/shard_map/ppermute | solution.py:186
  39.8 0.0 collective-permute-done.6.refs_1_
  39.9 0.8 %collective-permute-start.12 = (f32[32,1024]{1,0:T(8,128)S(1)}, f32[32,1024]{1,0:T(8,128)S(1)}, u32[]{:S(2)}, u32[]{:S(2)}) collective-permute-start(f32[32,1024]{1,0:T(8,128)S(1)} %get-tuple-element.49), channel_id=1, source_target_pairs={{0,28},{4,24},{8,20},{12,16},{16,12},{20,8},{24,4},{28,0},{1,29},{... | collective-permute-start | bytes 393224 | tf_op jit(solution)/shard_map/ppermute | solution.py:186
  40.7 0.0 collective-permute-done.7.refs_2_
  40.7 3.0 %collective-permute-start.8 = (f32[32,1024]{1,0:T(8,128)S(1)}, f32[32,1024]{1,0:T(8,128)S(1)}, u32[]{:S(2)}, u32[]{:S(2)}) collective-permute-start(f32[32,1024]{1,0:T(8,128)S(1)} %get-tuple-element.45), channel_id=1, source_target_pairs={{0,12},{4,8},{8,4},{12,0},{16,28},{20,24},{24,20},{28,16},{1,13},{... | collective-permute-start | bytes 393224 | tf_op jit(solution)/shard_map/ppermute | solution.py:186
  43.7 7.8 %collective-permute-done.9.refs_4_ = f32[32,1024]{1,0:T(8,128)S(1)} collective-permute-done((f32[32,1024]{1,0:T(8,128)S(1)}, f32[32,1024]{1,0:T(8,128)S(1)}, u32[]{:S(2)}, u32[]{:S(2)}) %collective-permute-start.9) | collective-permute-done | bytes 131104 | tf_op jit(solution)/shard_map/ppermute | solution.py:186
  51.4 2.8 %collective-permute-done.10.refs_5_ = f32[32,1024]{1,0:T(8,128)S(1)} collective-permute-done((f32[32,1024]{1,0:T(8,128)S(1)}, f32[32,1024]{1,0:T(8,128)S(1)}, u32[]{:S(2)}, u32[]{:S(2)}) %collective-permute-start.10) | collective-permute-done | bytes 131104 | tf_op jit(solution)/shard_map/ppermute | solution.py:186
  54.2 2.8 %collective-permute-done.11.refs_6_ = f32[32,1024]{1,0:T(8,128)S(1)} collective-permute-done((f32[32,1024]{1,0:T(8,128)S(1)}, f32[32,1024]{1,0:T(8,128)S(1)}, u32[]{:S(2)}, u32[]{:S(2)}) %collective-permute-start.11) | collective-permute-done | bytes 131104 | tf_op jit(solution)/shard_map/ppermute | solution.py:186
  57.0 2.8 %collective-permute-done.12.refs_7_ = f32[32,1024]{1,0:T(8,128)S(1)} collective-permute-done((f32[32,1024]{1,0:T(8,128)S(1)}, f32[32,1024]{1,0:T(8,128)S(1)}, u32[]{:S(2)}, u32[]{:S(2)}) %collective-permute-start.12) | collective-permute-done | bytes 131104 | tf_op jit(solution)/shard_map/ppermute | solution.py:186
  59.8 0.0 collective-permute-done.8.refs_3_
  59.8 0.8 %shard_map.44 = f32[32,4096]{1,0:T(8,128)} custom-call(f32[32,1024]{1,0:T(8,128)S(1)} %get-tuple-element.40.refs_0_, f32[32,1024]{1,0:T(8,128)S(1)} %collective-permute-done.6.refs_1_, f32[32,1024]{1,0:T(8,128)S(1)} %collective-permute-done.7.refs_2_, f32[32,1024]{1,0:T(8,128)S(1)} %collective-permute-done.8.refs_3_, ...), custom_call_target="tpu_custom_call" | custom-call | tf_op jit(solution)/shard_map/pallas_call | solution.py:175
  (2 shorter events, 0.0 us)
Async XLA Ops:
  3.6 8.1 %collective-permute-start.2 = (f32[64,1024]{1,0:T(8,128)S(1)}, f32[64,1024]{1,0:T(8,128)S(1)}, u32[]{:S(2)}, u32[]{:S(2)}) collective-permute-start(f32[64,1024]{1,0:T(8,128)S(1)} %get-tuple-element.28), channel_id=1, source_target_pairs={{0,4},{4,0},{8,12},{12,8},{16,20},{20,16},{24,28},{28,24},{1,5},{5... | collective-permute-start | bytes 786440 | tf_op jit(solution)/shard_map/ppermute | solution.py:186
  5.1 7.8 %collective-permute-start.3 = (f32[64,1024]{1,0:T(8,128)S(1)}, f32[64,1024]{1,0:T(8,128)S(1)}, u32[]{:S(2)}, u32[]{:S(2)}) collective-permute-start(f32[64,1024]{1,0:T(8,128)S(1)} %get-tuple-element.29), channel_id=1, source_target_pairs={{0,8},{4,12},{8,0},{12,4},{16,24},{20,28},{24,16},{28,20},{1,9},{5... | collective-permute-start | bytes 786440 | tf_op jit(solution)/shard_map/ppermute | solution.py:186
  5.6 1.2 %collective-permute-start = (f32[32,256]{1,0:T(8,128)S(1)}, f32[32,256]{1,0:T(8,128)S(1)}, u32[]{:S(2)}, u32[]{:S(2)}) collective-permute-start(f32[32,256]{1,0:T(8,128)S(1)} %get-tuple-element.27), channel_id=1, source_target_pairs={{0,1},{1,0},{2,3},{3,2},{4,5},{5,4},{6,7},{7,6},{8,9},{9,8},{10,11... | collective-permute-start | bytes 98312 | tf_op jit(solution)/shard_map/ppermute | solution.py:186
  6.8 3.9 %collective-permute-start.1 = (f32[32,256]{1,0:T(8,128)S(1)}, f32[32,256]{1,0:T(8,128)S(1)}, u32[]{:S(2)}, u32[]{:S(2)}) collective-permute-start(f32[32,256]{1,0:T(8,128)S(1)} %add.11), channel_id=1, source_target_pairs={{0,2},{1,3},{2,0},{3,1},{4,6},{5,7},{6,4},{7,5},{8,10},{9,11},{10,... | collective-permute-start | bytes 98312 | tf_op jit(solution)/shard_map/ppermute | solution.py:186
  13.6 13.9 %all-to-all-start = ((f32[8,32,256]{2,1,0:T(8,128)}), f32[8,32,256]{2,1,0:T(8,128)S(1)}, u32[]{:S(2)}, u32[]{:S(2)}) async-start(f32[8,32,256]{2,1,0:T(8,128)} %broadcast_in_dim.3), calls=%async_computation | async-start | bytes 524288 | tf_op jit(solution)/shard_map/all_to_all | solution.py:205
  18.9 10.5 %collective-permute-start.5 = (f32[64,1024]{1,0:T(8,128)S(1)}, f32[64,1024]{1,0:T(8,128)S(1)}, u32[]{:S(2)}, u32[]{:S(2)}) collective-permute-start(f32[64,1024]{1,0:T(8,128)S(1)} %get-tuple-element.31), channel_id=1, source_target_pairs={{0,12},{4,8},{8,4},{12,0},{16,28},{20,24},{24,20},{28,16},{1,13},{... | collective-permute-start | bytes 786440 | tf_op jit(solution)/shard_map/ppermute | solution.py:186
  27.5 1.9 %collective-permute-start.4 = (f32[8,32,256]{2,1,0:T(8,128)S(1)}, f32[8,32,256]{2,1,0:T(8,128)S(1)}, u32[]{:S(2)}, u32[]{:S(2)}) collective-permute-start(f32[8,32,256]{2,1,0:T(8,128)S(1)} %all-to-all-done.mine_ref), channel_id=1, source_target_pairs={{0,1},{1,0},{2,3},{3,2},{4,5},{5,4},{6,7},{7,6},{8,9},{9,8},{10,11... | collective-permute-start | bytes 786440 | tf_op jit(solution)/shard_map/ppermute | solution.py:186
  32.5 7.4 %collective-permute-start.6 = (f32[32,1024]{1,0:T(8,128)S(1)}, f32[32,1024]{1,0:T(8,128)S(1)}, u32[]{:S(2)}, u32[]{:S(2)}) collective-permute-start(f32[32,1024]{1,0:T(8,128)S(1)} %get-tuple-element.42), channel_id=1, source_target_pairs={{0,4},{4,0},{8,12},{12,8},{16,20},{20,16},{24,28},{28,24},{1,5},{5... | collective-permute-start | bytes 393224 | tf_op jit(solution)/shard_map/ppermute | solution.py:186
  33.4 7.2 %collective-permute-start.7 = (f32[32,1024]{1,0:T(8,128)S(1)}, f32[32,1024]{1,0:T(8,128)S(1)}, u32[]{:S(2)}, u32[]{:S(2)}) collective-permute-start(f32[32,1024]{1,0:T(8,128)S(1)} %get-tuple-element.44), channel_id=1, source_target_pairs={{0,8},{4,12},{8,0},{12,4},{16,24},{20,28},{24,16},{28,20},{1,9},{5... | collective-permute-start | bytes 393224 | tf_op jit(solution)/shard_map/ppermute | solution.py:186
  34.8 16.6 %collective-permute-start.9 = (f32[32,1024]{1,0:T(8,128)S(1)}, f32[32,1024]{1,0:T(8,128)S(1)}, u32[]{:S(2)}, u32[]{:S(2)}) collective-permute-start(f32[32,1024]{1,0:T(8,128)S(1)} %get-tuple-element.46), channel_id=1, source_target_pairs={{0,16},{4,20},{8,24},{12,28},{16,0},{20,4},{24,8},{28,12},{1,17},{... | collective-permute-start | bytes 393224 | tf_op jit(solution)/shard_map/ppermute | solution.py:186
  37.1 17.1 %collective-permute-start.10 = (f32[32,1024]{1,0:T(8,128)S(1)}, f32[32,1024]{1,0:T(8,128)S(1)}, u32[]{:S(2)}, u32[]{:S(2)}) collective-permute-start(f32[32,1024]{1,0:T(8,128)S(1)} %get-tuple-element.47), channel_id=1, source_target_pairs={{0,20},{4,16},{8,28},{12,24},{16,4},{20,0},{24,12},{28,8},{1,21},{... | collective-permute-start | bytes 393224 | tf_op jit(solution)/shard_map/ppermute | solution.py:186
  38.4 18.6 %collective-permute-start.11 = (f32[32,1024]{1,0:T(8,128)S(1)}, f32[32,1024]{1,0:T(8,128)S(1)}, u32[]{:S(2)}, u32[]{:S(2)}) collective-permute-start(f32[32,1024]{1,0:T(8,128)S(1)} %get-tuple-element.48), channel_id=1, source_target_pairs={{0,24},{4,28},{8,16},{12,20},{16,8},{20,12},{24,0},{28,4},{1,25},{... | collective-permute-start | bytes 393224 | tf_op jit(solution)/shard_map/ppermute | solution.py:186
  39.9 19.9 %collective-permute-start.12 = (f32[32,1024]{1,0:T(8,128)S(1)}, f32[32,1024]{1,0:T(8,128)S(1)}, u32[]{:S(2)}, u32[]{:S(2)}) collective-permute-start(f32[32,1024]{1,0:T(8,128)S(1)} %get-tuple-element.49), channel_id=1, source_target_pairs={{0,28},{4,24},{8,20},{12,16},{16,12},{20,8},{24,4},{28,0},{1,29},{... | collective-permute-start | bytes 393224 | tf_op jit(solution)/shard_map/ppermute | solution.py:186
  40.7 19.1 %collective-permute-start.8 = (f32[32,1024]{1,0:T(8,128)S(1)}, f32[32,1024]{1,0:T(8,128)S(1)}, u32[]{:S(2)}, u32[]{:S(2)}) collective-permute-start(f32[32,1024]{1,0:T(8,128)S(1)} %get-tuple-element.45), channel_id=1, source_target_pairs={{0,12},{4,8},{8,4},{12,0},{16,28},{20,24},{24,20},{28,16},{1,13},{... | collective-permute-start | bytes 393224 | tf_op jit(solution)/shard_map/ppermute | solution.py:186

commit v11 on v9

--- a/solution.py
+++ b/solution.py
@@ -163,15 +163,20 @@
 
 
 def join_kernel(group, *refs):
-    *terms, out_ref = refs
-    terms = terms[-group:] + terms[:-group]
+    *terms, out_ref, buf, sems = refs
     width = terms[0].shape[1]
     member = lax.rem(lax.axis_index("tm"), group)
+    copies = []
     for k in range(group):
         value = terms[k][...]
         for term in terms[group + k :: group]:
             value = value + term[...]
-        out_ref[:, pl.ds(pl.multiple_of((member ^ k) * width, width), width)] = value
+        buf[k] = value
+        span = pl.ds(pl.multiple_of((member ^ k) * width, width), width)
+        copies.append(pltpu.make_async_copy(buf.at[k], out_ref.at[:, span], sems.at[k]))
+        copies[-1].start()
+    for copy in copies:
+        copy.wait()
 
 
 def join(terms, group):
@@ -179,11 +184,12 @@
     return pl.pallas_call(
         functools.partial(join_kernel, group),
         in_specs=[VMEM] * len(terms),
-        out_specs=VMEM,
+        out_specs=HBM,
         out_shape=jax.ShapeDtypeStruct((rows, group * width), jnp.float32),
+        scratch_shapes=[pltpu.VMEM((group, rows, width), jnp.float32), pltpu.SemaphoreType.DMA((group,))],
         compiler_params=params(),
         cost_estimate=FREE,
-    )(*terms[group:], *terms[:group])
+    )(*terms)
 
 
 def swap(value, axis, offset):
@@ -205,20 +211,18 @@
     for i in range(1, spaces.bit_length() - 1):
         mine = mine + swap(mine, "space", 1 << i)
 
-    order, offsets = [0], [1 << i for i in range(times.bit_length() - 1)]
-    for offset in [o for o in offsets if o >= group] + [o for o in offsets if o < group]:
-        if offset < group:
-            mine, parts[offset] = lax.optimization_barrier((mine, parts[offset]))
-        mine = jnp.concatenate([mine, swap(mine, "tm", offset)], axis=0)
-        order = order + [k ^ offset for k in order]
-    theirs, parts[-1] = lax.optimization_barrier((swap(mine, "space", 1), parts[-1]))
-    high_t, low_t, own = mix(jnp.stack([index, core]), mine, theirs, times, group, order)
+    pair = jnp.concatenate([mine, swap(mine, "tm", 1)], axis=0)
+    pair, *parts = lax.optimization_barrier((pair, *parts))
+    offsets = [*range(group, times, 2), *range(2, group, 2)]
+    mine = jnp.concatenate([pair] + [swap(pair, "tm", k) for k in offsets], axis=0)
+    order = [k ^ i for k in [0, *offsets] for i in range(2)]
+    high_t, low_t, own = mix(jnp.stack([index, core]), mine, swap(mine, "space", 1), times, group, order)
 
     blocks = list(load(high_t, low_t, parts, times))
     terms = [blocks[0]] + [None] * (times - 1)
     for k in [*range(group, times), *range(1, group)]:
-        if 1 < k < group:
-            blocks[k], terms[k - 1] = lax.optimization_barrier((blocks[k], terms[k - 1]))
+        if k == group - 1:
+            blocks[k], terms[1] = lax.optimization_barrier((blocks[k], terms[1]))
         terms[k] = swap(blocks[k], "tm", k)
     return own, join(terms, group)
 

time: 62.8 us -> 62 us (0.987)
  waiting for transfers between devices: 34 us -> 31.3 us
  starting transfers between devices: 20.9 us -> 22.9 us
    ppermute x16 -> x17, waiting for transfers between devices: 34 us -> 31.3 us  [swap(): lax.ppermute(value, axis, [(i, i ^ offset) for i in range(lax.axis_size(a...]
    ppermute x16 -> x17, starting transfers between devices: 20.9 us -> 22.9 us  [swap(): lax.ppermute(value, axis, [(i, i ^ offset) for i in range(lax.axis_size(a...]
  transfers between devices with their start and end apart: 16 -> 17, of which waited for: 12 -> 9; matrix products, arithmetic and copies ran while one was open for 0% -> 0% of each run, Pallas kernels for 0% -> 0%
where the time goes in v11:
time: 62 us; the launch traced here: 61.8 us
  waiting for transfers between devices  31.3 us (50%)
  starting transfers between devices  22.9 us (37%)
  Pallas kernels  6.81 us (11%)
  between operations  0.73 us (1%)
    ppermute x17, waiting for transfers between devices, swap(): lax.ppermute(value, axis, [(i, i ^ offset) for i in range(lax.axis_size(a...  31.3 us
    ppermute x17, starting transfers between devices, swap(): lax.ppermute(value, axis, [(i, i ^ offset) for i in range(lax.axis_size(a...  22.9 us
    pallas_call x1, Pallas kernels, project(): pl.pallas_call(functools.partial(project_kernel, depth), in_specs=[HBM, H...  2.93 us
    pallas_call x1, Pallas kernels, mix(): pl.pallas_call(functools.partial(mix_kernel, times, order), in_specs=[SME...  2.46 us
  transfers between devices with their start and end apart: 17, of which 9 were waited for; matrix products, arithmetic and copies ran while one was open for 0% of the time, Pallas kernels for 0%

profile of v11, /device:TPU:8, one launch (start us, length us, event | category | flops | bytes accessed | tf_op | source)
XLA Modules:
  0.0 61.8 jit_solution(15394747831303956123)
XLA Ops:
  0.6 2.9 %shard_map.41 = (f32[32,256]{1,0:T(8,128)S(1)}, f32[32,256]{1,0:T(8,128)S(1)}, f32[64,1024]{1,0:T(8,128)S(1)}, f32[64,1024]{1,0:T(8,128)S(1)}, f32[64,1024]{1,0:T(8,128)S(1)}, /*index=5*/f32[64,1024]{1,0:T(8,128)S(1)}) custom-call(f32[64,4096]{1,0:T(8,128)} %snapshots_ref.1, f32[4096,256]{1,0:T(8,128)} %factor_ref.1), custom_call_target="tpu_custom_call" | custom-call | tf_op jit(solution)/shard_map/pallas_call | solution.py:76
  3.6 1.6 %collective-permute-start.3 = (f32[64,1024]{1,0:T(8,128)S(1)}, f32[64,1024]{1,0:T(8,128)S(1)}, u32[]{:S(2)}, u32[]{:S(2)}) collective-permute-start(f32[64,1024]{1,0:T(8,128)S(1)} %get-tuple-element.29), channel_id=1, source_target_pairs={{0,4},{4,0},{8,12},{12,8},{16,20},{20,16},{24,28},{28,24},{1,5},{5... | collective-permute-start | bytes 786440 | tf_op jit(solution)/shard_map/ppermute | solution.py:196
  5.1 0.5 collective-permute-start.4
  5.6 1.5 %collective-permute-start.5 = (f32[64,1024]{1,0:T(8,128)S(1)}, f32[64,1024]{1,0:T(8,128)S(1)}, u32[]{:S(2)}, u32[]{:S(2)}) collective-permute-start(f32[64,1024]{1,0:T(8,128)S(1)} %get-tuple-element.31), channel_id=1, source_target_pairs={{0,12},{4,8},{8,4},{12,0},{16,28},{20,24},{24,20},{28,16},{1,13},{... | collective-permute-start | bytes 786440 | tf_op jit(solution)/shard_map/ppermute | solution.py:196
  7.1 0.0 collective-permute-start
  7.1 1.2 %collective-permute-done = f32[32,256]{1,0:T(8,128)S(1)} collective-permute-done((f32[32,256]{1,0:T(8,128)S(1)}, f32[32,256]{1,0:T(8,128)S(1)}, u32[]{:S(2)}, u32[]{:S(2)}) %collective-permute-start) | collective-permute-done | bytes 32800 | tf_op jit(solution)/shard_map/ppermute | solution.py:196
  8.3 1.5 %collective-permute-start.1 = (f32[32,256]{1,0:T(8,128)S(1)}, f32[32,256]{1,0:T(8,128)S(1)}, u32[]{:S(2)}, u32[]{:S(2)}) collective-permute-start(f32[32,256]{1,0:T(8,128)S(1)} %add.11), channel_id=1, source_target_pairs={{0,2},{1,3},{2,0},{3,1},{4,6},{5,7},{6,4},{7,5},{8,10},{9,11},{10,... | collective-permute-start | bytes 98312 | tf_op jit(solution)/shard_map/ppermute | solution.py:196
  9.9 2.4 %collective-permute-done.1 = f32[32,256]{1,0:T(8,128)S(1)} collective-permute-done((f32[32,256]{1,0:T(8,128)S(1)}, f32[32,256]{1,0:T(8,128)S(1)}, u32[]{:S(2)}, u32[]{:S(2)}) %collective-permute-start.1) | collective-permute-done | bytes 32800 | tf_op jit(solution)/shard_map/ppermute | solution.py:196
  12.3 1.5 %collective-permute-start.2 = (f32[32,256]{1,0:T(8,128)S(1)}, f32[32,256]{1,0:T(8,128)S(1)}, u32[]{:S(2)}, u32[]{:S(2)}) collective-permute-start(f32[32,256]{1,0:T(8,128)S(1)} %add.12), channel_id=1, source_target_pairs={{0,4},{4,0},{8,12},{12,8},{16,20},{20,16},{24,28},{28,24},{1,5},{5... | collective-permute-start | bytes 98312 | tf_op jit(solution)/shard_map/ppermute | solution.py:196
  13.7 5.3 %collective-permute-done.2 = f32[32,256]{1,0:T(8,128)S(1)} collective-permute-done((f32[32,256]{1,0:T(8,128)S(1)}, f32[32,256]{1,0:T(8,128)S(1)}, u32[]{:S(2)}, u32[]{:S(2)}) %collective-permute-start.2) | collective-permute-done | bytes 32800 | tf_op jit(solution)/shard_map/ppermute | solution.py:196
  19.1 0.0 collective-permute-done.3.refs_1_
  19.1 0.0 collective-permute-done.4.refs_2_
  19.1 0.0 collective-permute-done.5.refs_3_
  19.1 0.4 collective-permute-start.8
  19.6 2.8 %collective-permute-start.7 = (f32[64,256]{1,0:T(8,128)S(1)}, f32[64,256]{1,0:T(8,128)S(1)}, u32[]{:S(2)}, u32[]{:S(2)}) collective-permute-start(f32[64,256]{1,0:T(8,128)S(1)} %pad_maximum_fusion), channel_id=1, source_target_pairs={{0,24},{4,28},{8,16},{12,20},{16,8},{20,12},{24,0},{28,4},{1,25},{... | collective-permute-start | bytes 196616 | tf_op jit(solution)/shard_map/ppermute | solution.py:196
  22.3 1.2 %collective-permute-start.6 = (f32[64,256]{1,0:T(8,128)S(1)}, f32[64,256]{1,0:T(8,128)S(1)}, u32[]{:S(2)}, u32[]{:S(2)}) collective-permute-start(f32[64,256]{1,0:T(8,128)S(1)} %pad_maximum_fusion), channel_id=1, source_target_pairs={{0,16},{4,20},{8,24},{12,28},{16,0},{20,4},{24,8},{28,12},{1,17},{... | collective-permute-start | bytes 196616 | tf_op jit(solution)/shard_map/ppermute | solution.py:196
  23.6 4.2 %collective-permute-done.6 = f32[64,256]{1,0:T(8,128)S(1)} collective-permute-done((f32[64,256]{1,0:T(8,128)S(1)}, f32[64,256]{1,0:T(8,128)S(1)}, u32[]{:S(2)}, u32[]{:S(2)}) %collective-permute-start.6) | collective-permute-done | bytes 65568 | tf_op jit(solution)/shard_map/ppermute | solution.py:196
  27.8 0.0 collective-permute-done.7
  27.8 0.0 collective-permute-done.8
  27.9 0.1 collective-permute-start.9
  27.9 0.1 pad_add_fusion.index_ref
  28.0 1.4 %collective-permute-done.9.theirs_ref = f32[256,256]{1,0:T(8,128)S(1)} collective-permute-done((f32[256,256]{1,0:T(8,128)S(1)}, f32[256,256]{1,0:T(8,128)S(1)}, u32[]{:S(2)}, u32[]{:S(2)}) %collective-permute-start.9) | collective-permute-done | bytes 262176 | tf_op jit(solution)/shard_map/ppermute | solution.py:196
  29.5 2.5 %shard_map.42 = (bf16[256,256]{1,0:T(8,128)(2,1)S(1)}, bf16[256,256]{1,0:T(8,128)(2,1)S(1)}, f32[64,256]{1,0:T(8,128)}) custom-call(s32[2]{0:T(128)S(1)} %pad_add_fusion.index_ref, f32[256,256]{1,0:T(8,128)S(1)} %constant_dynamic-update-slice_fusion.mine_ref, f32[256,256]{1,0:T(8,128)S(1)} %collective-permute-done.9.theirs_ref), custom_call_target="tpu_custom_call" | custom-call | tf_op jit(solution)/shard_map/pallas_call | solution.py:133
  31.9 0.6 shard_map.43
  32.5 1.6 %collective-permute-start.10 = (f32[32,1024]{1,0:T(8,128)S(1)}, f32[32,1024]{1,0:T(8,128)S(1)}, u32[]{:S(2)}, u32[]{:S(2)}) collective-permute-start(f32[32,1024]{1,0:T(8,128)S(1)} %get-tuple-element.42), channel_id=1, source_target_pairs={{0,4},{4,0},{8,12},{12,8},{16,20},{20,16},{24,28},{28,24},{1,5},{5... | collective-permute-start | bytes 393224 | tf_op jit(solution)/shard_map/ppermute | solution.py:196
  34.1 2.4 %collective-permute-start.11 = (f32[32,1024]{1,0:T(8,128)S(1)}, f32[32,1024]{1,0:T(8,128)S(1)}, u32[]{:S(2)}, u32[]{:S(2)}) collective-permute-start(f32[32,1024]{1,0:T(8,128)S(1)} %get-tuple-element.44), channel_id=1, source_target_pairs={{0,8},{4,12},{8,0},{12,4},{16,24},{20,28},{24,16},{28,20},{1,9},{5... | collective-permute-start | bytes 393224 | tf_op jit(solution)/shard_map/ppermute | solution.py:196
  36.5 1.0 %collective-permute-start.13 = (f32[32,1024]{1,0:T(8,128)S(1)}, f32[32,1024]{1,0:T(8,128)S(1)}, u32[]{:S(2)}, u32[]{:S(2)}) collective-permute-start(f32[32,1024]{1,0:T(8,128)S(1)} %get-tuple-element.46), channel_id=1, source_target_pairs={{0,16},{4,20},{8,24},{12,28},{16,0},{20,4},{24,8},{28,12},{1,17},{... | collective-permute-start | bytes 393224 | tf_op jit(solution)/shard_map/ppermute | solution.py:196
  37.5 1.9 %collective-permute-start.14 = (f32[32,1024]{1,0:T(8,128)S(1)}, f32[32,1024]{1,0:T(8,128)S(1)}, u32[]{:S(2)}, u32[]{:S(2)}) collective-permute-start(f32[32,1024]{1,0:T(8,128)S(1)} %get-tuple-element.47), channel_id=1, source_target_pairs={{0,20},{4,16},{8,28},{12,24},{16,4},{20,0},{24,12},{28,8},{1,21},{... | collective-permute-start | bytes 393224 | tf_op jit(solution)/shard_map/ppermute | solution.py:196
  39.4 1.5 %collective-permute-start.15 = (f32[32,1024]{1,0:T(8,128)S(1)}, f32[32,1024]{1,0:T(8,128)S(1)}, u32[]{:S(2)}, u32[]{:S(2)}) collective-permute-start(f32[32,1024]{1,0:T(8,128)S(1)} %get-tuple-element.48), channel_id=1, source_target_pairs={{0,24},{4,28},{8,16},{12,20},{16,8},{20,12},{24,0},{28,4},{1,25},{... | collective-permute-start | bytes 393224 | tf_op jit(solution)/shard_map/ppermute | solution.py:196
  40.9 0.0 collective-permute-done.10.refs_1_
  40.9 1.4 %collective-permute-start.16 = (f32[32,1024]{1,0:T(8,128)S(1)}, f32[32,1024]{1,0:T(8,128)S(1)}, u32[]{:S(2)}, u32[]{:S(2)}) collective-permute-start(f32[32,1024]{1,0:T(8,128)S(1)} %get-tuple-element.49), channel_id=1, source_target_pairs={{0,28},{4,24},{8,20},{12,16},{16,12},{20,8},{24,4},{28,0},{1,29},{... | collective-permute-start | bytes 393224 | tf_op jit(solution)/shard_map/ppermute | solution.py:196
  42.3 0.0 collective-permute-done.11.refs_2_
  42.3 2.0 %collective-permute-start.12 = (f32[32,1024]{1,0:T(8,128)S(1)}, f32[32,1024]{1,0:T(8,128)S(1)}, u32[]{:S(2)}, u32[]{:S(2)}) collective-permute-start(f32[32,1024]{1,0:T(8,128)S(1)} %get-tuple-element.45), channel_id=1, source_target_pairs={{0,12},{4,8},{8,4},{12,0},{16,28},{20,24},{24,20},{28,16},{1,13},{... | collective-permute-start | bytes 393224 | tf_op jit(solution)/shard_map/ppermute | solution.py:196
  44.3 8.3 %collective-permute-done.13.refs_4_ = f32[32,1024]{1,0:T(8,128)S(1)} collective-permute-done((f32[32,1024]{1,0:T(8,128)S(1)}, f32[32,1024]{1,0:T(8,128)S(1)}, u32[]{:S(2)}, u32[]{:S(2)}) %collective-permute-start.13) | collective-permute-done | bytes 131104 | tf_op jit(solution)/shard_map/ppermute | solution.py:196
  52.6 2.8 %collective-permute-done.14.refs_5_ = f32[32,1024]{1,0:T(8,128)S(1)} collective-permute-done((f32[32,1024]{1,0:T(8,128)S(1)}, f32[32,1024]{1,0:T(8,128)S(1)}, u32[]{:S(2)}, u32[]{:S(2)}) %collective-permute-start.14) | collective-permute-done | bytes 131104 | tf_op jit(solution)/shard_map/ppermute | solution.py:196
  55.4 3.5 %collective-permute-done.15.refs_6_ = f32[32,1024]{1,0:T(8,128)S(1)} collective-permute-done((f32[32,1024]{1,0:T(8,128)S(1)}, f32[32,1024]{1,0:T(8,128)S(1)}, u32[]{:S(2)}, u32[]{:S(2)}) %collective-permute-start.15) | collective-permute-done | bytes 131104 | tf_op jit(solution)/shard_map/ppermute | solution.py:196
  59.0 2.0 %collective-permute-done.16.refs_7_ = f32[32,1024]{1,0:T(8,128)S(1)} collective-permute-done((f32[32,1024]{1,0:T(8,128)S(1)}, f32[32,1024]{1,0:T(8,128)S(1)}, u32[]{:S(2)}, u32[]{:S(2)}) %collective-permute-start.16) | collective-permute-done | bytes 131104 | tf_op jit(solution)/shard_map/ppermute | solution.py:196
  61.0 0.0 collective-permute-done.12.refs_3_
  61.0 0.8 %shard_map.44 = f32[32,4096]{1,0:T(8,128)} custom-call(f32[32,1024]{1,0:T(8,128)S(1)} %get-tuple-element.40.refs_0_, f32[32,1024]{1,0:T(8,128)S(1)} %collective-permute-done.10.refs_1_, f32[32,1024]{1,0:T(8,128)S(1)} %collective-permute-done.11.refs_2_, f32[32,1024]{1,0:T(8,128)S(1)} %collective-permute-done.12.refs_3_, ...), custom_call_target="tpu_custom_call" | custom-call | tf_op jit(solution)/shard_map/pallas_call | solution.py:184
  (7 shorter events, 0.0 us)
Async XLA Ops:
  3.6 15.5 %collective-permute-start.3 = (f32[64,1024]{1,0:T(8,128)S(1)}, f32[64,1024]{1,0:T(8,128)S(1)}, u32[]{:S(2)}, u32[]{:S(2)}) collective-permute-start(f32[64,1024]{1,0:T(8,128)S(1)} %get-tuple-element.29), channel_id=1, source_target_pairs={{0,4},{4,0},{8,12},{12,8},{16,20},{20,16},{24,28},{28,24},{1,5},{5... | collective-permute-start | bytes 786440 | tf_op jit(solution)/shard_map/ppermute | solution.py:196
  5.1 14.0 %collective-permute-start.4 = (f32[64,1024]{1,0:T(8,128)S(1)}, f32[64,1024]{1,0:T(8,128)S(1)}, u32[]{:S(2)}, u32[]{:S(2)}) collective-permute-start(f32[64,1024]{1,0:T(8,128)S(1)} %get-tuple-element.30), channel_id=1, source_target_pairs={{0,8},{4,12},{8,0},{12,4},{16,24},{20,28},{24,16},{28,20},{1,9},{5... | collective-permute-start | bytes 786440 | tf_op jit(solution)/shard_map/ppermute | solution.py:196
  5.6 13.5 %collective-permute-start.5 = (f32[64,1024]{1,0:T(8,128)S(1)}, f32[64,1024]{1,0:T(8,128)S(1)}, u32[]{:S(2)}, u32[]{:S(2)}) collective-permute-start(f32[64,1024]{1,0:T(8,128)S(1)} %get-tuple-element.31), channel_id=1, source_target_pairs={{0,12},{4,8},{8,4},{12,0},{16,28},{20,24},{24,20},{28,16},{1,13},{... | collective-permute-start | bytes 786440 | tf_op jit(solution)/shard_map/ppermute | solution.py:196
  7.1 1.2 %collective-permute-start = (f32[32,256]{1,0:T(8,128)S(1)}, f32[32,256]{1,0:T(8,128)S(1)}, u32[]{:S(2)}, u32[]{:S(2)}) collective-permute-start(f32[32,256]{1,0:T(8,128)S(1)} %get-tuple-element.27), channel_id=1, source_target_pairs={{0,1},{1,0},{2,3},{3,2},{4,5},{5,4},{6,7},{7,6},{8,9},{9,8},{10,11... | collective-permute-start | bytes 98312 | tf_op jit(solution)/shard_map/ppermute | solution.py:196
  8.3 3.9 %collective-permute-start.1 = (f32[32,256]{1,0:T(8,128)S(1)}, f32[32,256]{1,0:T(8,128)S(1)}, u32[]{:S(2)}, u32[]{:S(2)}) collective-permute-start(f32[32,256]{1,0:T(8,128)S(1)} %add.11), channel_id=1, source_target_pairs={{0,2},{1,3},{2,0},{3,1},{4,6},{5,7},{6,4},{7,5},{8,10},{9,11},{10,... | collective-permute-start | bytes 98312 | tf_op jit(solution)/shard_map/ppermute | solution.py:196
  12.3 6.8 %collective-permute-start.2 = (f32[32,256]{1,0:T(8,128)S(1)}, f32[32,256]{1,0:T(8,128)S(1)}, u32[]{:S(2)}, u32[]{:S(2)}) collective-permute-start(f32[32,256]{1,0:T(8,128)S(1)} %add.12), channel_id=1, source_target_pairs={{0,4},{4,0},{8,12},{12,8},{16,20},{20,16},{24,28},{28,24},{1,5},{5... | collective-permute-start | bytes 98312 | tf_op jit(solution)/shard_map/ppermute | solution.py:196
  19.1 8.7 %collective-permute-start.8 = (f32[64,256]{1,0:T(8,128)S(1)}, f32[64,256]{1,0:T(8,128)S(1)}, u32[]{:S(2)}, u32[]{:S(2)}) collective-permute-start(f32[64,256]{1,0:T(8,128)S(1)} %pad_maximum_fusion), channel_id=1, source_target_pairs={{0,8},{4,12},{8,0},{12,4},{16,24},{20,28},{24,16},{28,20},{1,9},{5... | collective-permute-start | bytes 196616 | tf_op jit(solution)/shard_map/ppermute | solution.py:196
  19.6 8.3 %collective-permute-start.7 = (f32[64,256]{1,0:T(8,128)S(1)}, f32[64,256]{1,0:T(8,128)S(1)}, u32[]{:S(2)}, u32[]{:S(2)}) collective-permute-start(f32[64,256]{1,0:T(8,128)S(1)} %pad_maximum_fusion), channel_id=1, source_target_pairs={{0,24},{4,28},{8,16},{12,20},{16,8},{20,12},{24,0},{28,4},{1,25},{... | collective-permute-start | bytes 196616 | tf_op jit(solution)/shard_map/ppermute | solution.py:196
  22.3 5.5 %collective-permute-start.6 = (f32[64,256]{1,0:T(8,128)S(1)}, f32[64,256]{1,0:T(8,128)S(1)}, u32[]{:S(2)}, u32[]{:S(2)}) collective-permute-start(f32[64,256]{1,0:T(8,128)S(1)} %pad_maximum_fusion), channel_id=1, source_target_pairs={{0,16},{4,20},{8,24},{12,28},{16,0},{20,4},{24,8},{28,12},{1,17},{... | collective-permute-start | bytes 196616 | tf_op jit(solution)/shard_map/ppermute | solution.py:196
  27.9 1.6 %collective-permute-start.9 = (f32[256,256]{1,0:T(8,128)S(1)}, f32[256,256]{1,0:T(8,128)S(1)}, u32[]{:S(2)}, u32[]{:S(2)}) collective-permute-start(f32[256,256]{1,0:T(8,128)S(1)} %constant_dynamic-update-slice_fusion.mine_ref), channel_id=1, source_target_pairs={{0,1},{1,0},{2,3},{3,2},{4,5},{5,4},{6,7},{7,6},{8,9},{9,8},{10,11... | collective-permute-start | bytes 786440 | tf_op jit(solution)/shard_map/ppermute | solution.py:196
  32.5 8.4 %collective-permute-start.10 = (f32[32,1024]{1,0:T(8,128)S(1)}, f32[32,1024]{1,0:T(8,128)S(1)}, u32[]{:S(2)}, u32[]{:S(2)}) collective-permute-start(f32[32,1024]{1,0:T(8,128)S(1)} %get-tuple-element.42), channel_id=1, source_target_pairs={{0,4},{4,0},{8,12},{12,8},{16,20},{20,16},{24,28},{28,24},{1,5},{5... | collective-permute-start | bytes 393224 | tf_op jit(solution)/shard_map/ppermute | solution.py:196
  34.1 8.3 %collective-permute-start.11 = (f32[32,1024]{1,0:T(8,128)S(1)}, f32[32,1024]{1,0:T(8,128)S(1)}, u32[]{:S(2)}, u32[]{:S(2)}) collective-permute-start(f32[32,1024]{1,0:T(8,128)S(1)} %get-tuple-element.44), channel_id=1, source_target_pairs={{0,8},{4,12},{8,0},{12,4},{16,24},{20,28},{24,16},{28,20},{1,9},{5... | collective-permute-start | bytes 393224 | tf_op jit(solution)/shard_map/ppermute | solution.py:196
  36.5 16.2 %collective-permute-start.13 = (f32[32,1024]{1,0:T(8,128)S(1)}, f32[32,1024]{1,0:T(8,128)S(1)}, u32[]{:S(2)}, u32[]{:S(2)}) collective-permute-start(f32[32,1024]{1,0:T(8,128)S(1)} %get-tuple-element.46), channel_id=1, source_target_pairs={{0,16},{4,20},{8,24},{12,28},{16,0},{20,4},{24,8},{28,12},{1,17},{... | collective-permute-start | bytes 393224 | tf_op jit(solution)/shard_map/ppermute | solution.py:196
  37.5 18.0 %collective-permute-start.14 = (f32[32,1024]{1,0:T(8,128)S(1)}, f32[32,1024]{1,0:T(8,128)S(1)}, u32[]{:S(2)}, u32[]{:S(2)}) collective-permute-start(f32[32,1024]{1,0:T(8,128)S(1)} %get-tuple-element.47), channel_id=1, source_target_pairs={{0,20},{4,16},{8,28},{12,24},{16,4},{20,0},{24,12},{28,8},{1,21},{... | collective-permute-start | bytes 393224 | tf_op jit(solution)/shard_map/ppermute | solution.py:196
  39.4 19.6 %collective-permute-start.15 = (f32[32,1024]{1,0:T(8,128)S(1)}, f32[32,1024]{1,0:T(8,128)S(1)}, u32[]{:S(2)}, u32[]{:S(2)}) collective-permute-start(f32[32,1024]{1,0:T(8,128)S(1)} %get-tuple-element.48), channel_id=1, source_target_pairs={{0,24},{4,28},{8,16},{12,20},{16,8},{20,12},{24,0},{28,4},{1,25},{... | collective-permute-start | bytes 393224 | tf_op jit(solution)/shard_map/ppermute | solution.py:196
  40.9 20.1 %collective-permute-start.16 = (f32[32,1024]{1,0:T(8,128)S(1)}, f32[32,1024]{1,0:T(8,128)S(1)}, u32[]{:S(2)}, u32[]{:S(2)}) collective-permute-start(f32[32,1024]{1,0:T(8,128)S(1)} %get-tuple-element.49), channel_id=1, source_target_pairs={{0,28},{4,24},{8,20},{12,16},{16,12},{20,8},{24,4},{28,0},{1,29},{... | collective-permute-start | bytes 393224 | tf_op jit(solution)/shard_map/ppermute | solution.py:196
  42.3 18.6 %collective-permute-start.12 = (f32[32,1024]{1,0:T(8,128)S(1)}, f32[32,1024]{1,0:T(8,128)S(1)}, u32[]{:S(2)}, u32[]{:S(2)}) collective-permute-start(f32[32,1024]{1,0:T(8,128)S(1)} %get-tuple-element.45), channel_id=1, source_target_pairs={{0,12},{4,8},{8,4},{12,0},{16,28},{20,24},{24,20},{28,16},{1,13},{... | collective-permute-start | bytes 393224 | tf_op jit(solution)/shard_map/ppermute | solution.py:196

commit v12 on v11

--- a/solution.py
+++ b/solution.py
@@ -9,6 +9,7 @@
 from jax.sharding import PartitionSpec as P
 
 MIB = 1024 * 1024
+WHOLE_SHARE = 0.75
 HBM = pl.BlockSpec(memory_space=pltpu.HBM)
 SMEM = pl.BlockSpec(memory_space=pltpu.SMEM)
 VMEM = pl.BlockSpec(memory_space=pltpu.VMEM)
@@ -38,8 +39,8 @@
     )
 
 
-def project_kernel(depth, snapshots_ref, factor_ref, mine_ref, other_ref, *refs):
-    *parts, snapshots_buf, factor_buf, sems = refs
+def project_kernel(depth, group, wide, snapshots_ref, factor_ref, halves_ref, *refs):
+    *pieces, snapshots_buf, factor_buf, sems = refs
     rows, points = snapshots_ref.shape
     half = rows // 2
     snapshots_copy = pltpu.make_async_copy(snapshots_ref, snapshots_buf, sems.at[points // depth])
@@ -50,10 +51,17 @@
         copies.append(pltpu.make_async_copy(factor_ref.at[span, :], factor_buf.at[span, :], sems.at[i]))
         copies[-1].start()
     snapshots_copy.wait()
-    width = parts[0].shape[1]
-    member = lax.rem(lax.axis_index("tm"), len(parts))
+    share = points // group
+    parts, slabs = (pieces[:-1], pieces[-1]) if wide else (pieces, None)
+    member = lax.rem(lax.axis_index("tm"), group)
     for k, part in enumerate(parts):
-        part[...] = snapshots_buf[:, pl.ds(pl.multiple_of((member ^ k) * width, width), width)]
+        start = pl.multiple_of((member ^ k) * share, share)
+        part[...] = snapshots_buf[:, pl.ds(start, part.shape[1])]
+    if wide:
+        times = slabs.shape[0]
+        for i in range(times):
+            end = (i % group + 1) * share - (times - 1 - i) // group * wide
+            slabs[i] = snapshots_buf[:, end - wide : end]
     value = None
     for i, start in enumerate(range(0, points, depth)):
         copies[i].wait()
@@ -63,21 +71,23 @@
         term = both[:rows] + (both[rows:] + dot(high, factor_low))
         value = term if value is None else value + term
     first = lax.rem(lax.axis_index("space"), 2) == 0
-    mine_ref[...] = jnp.where(first, value[:half], value[half:])
-    other_ref[...] = jnp.where(first, value[half:], value[:half])
-
-
-def project(snapshots, space_factor, group):
+    halves_ref[0] = jnp.where(first, value[:half], value[half:])
+    halves_ref[1] = jnp.where(first, value[half:], value[:half])
+
+
+def project(snapshots, space_factor, group, groups, wide):
     rows, points = snapshots.shape
     rank = space_factor.shape[1]
     depth = min(512, points)
-    half = jax.ShapeDtypeStruct((rows // 2, rank), jnp.float32)
-    part = jax.ShapeDtypeStruct((rows, points // group), jnp.float32)
-    mine, other, *parts = pl.pallas_call(
-        functools.partial(project_kernel, depth),
+    narrow = points // group - groups * wide
+    pieces = [jax.ShapeDtypeStruct((rows, narrow), jnp.float32)] * (group if narrow else 0)
+    if wide:
+        pieces = [*pieces, jax.ShapeDtypeStruct((group * groups, rows, wide), jnp.float32)]
+    halves, *pieces = pl.pallas_call(
+        functools.partial(project_kernel, depth, group, wide),
         in_specs=[HBM, HBM],
-        out_specs=[VMEM] * (2 + group),
-        out_shape=[half, half] + [part] * group,
+        out_specs=[VMEM] * (1 + len(pieces)),
+        out_shape=[jax.ShapeDtypeStruct((2, rows // 2, rank), jnp.float32), *pieces],
         scratch_shapes=[
             pltpu.VMEM((rows, points), jnp.float32),
             pltpu.VMEM((points, rank), jnp.float32),
@@ -86,7 +96,7 @@
         compiler_params=params(52),
         cost_estimate=FREE,
     )(snapshots, space_factor)
-    return mine, other, parts
+    return (halves, pieces[:-1], pieces[-1:]) if wide else (halves, pieces, [])
 
 
 def mix_kernel(times, order, index_ref, mine_ref, theirs_ref, high_t_ref, low_t_ref, own_ref):
@@ -111,8 +121,7 @@
     mixing_high, mixing_low = split(mixing)
 
     rows = 2 * half
-    group = high_t_ref.shape[1] // rows
-    places = [order.index(k) for k in range(group)]
+    places = [order.index(k) for k in range(times)]
     high = jnp.concatenate([high[i * rows : (i + 1) * rows] for i in places], axis=0)
     low = jnp.concatenate([low[i * rows : (i + 1) * rows] for i in places], axis=0)
     scale = lax.rsqrt(total)
@@ -126,10 +135,10 @@
     high_t_ref[...], low_t_ref[...] = split(turned)
 
 
-def mix(index, mine, theirs, times, group, order):
+def mix(index, mine, theirs, times, order):
     total_half, rank = mine.shape
     rows = 2 * total_half // times
-    factor = jax.ShapeDtypeStruct((rank, group * rows), jnp.bfloat16)
+    factor = jax.ShapeDtypeStruct((rank, times * rows), jnp.bfloat16)
     return pl.pallas_call(
         functools.partial(mix_kernel, times, order),
         in_specs=[SMEM, VMEM, VMEM],
@@ -140,53 +149,68 @@
     )(index, mine, theirs)
 
 
-def load_kernel(group, high_ref, low_ref, *refs):
-    parts, blocks = refs[:group], refs[group:]
-    columns = jnp.concatenate([part[...] for part in parts], axis=0)
-    value = product((high_ref[...], low_ref[...]), split(columns))
-    width = value.shape[0] // len(blocks)
+def load_kernel(group, wide, index_ref, high_ref, low_ref, *refs):
+    parts, slabs, blocks = refs[:group], refs[group : group + wide], refs[group + wide :]
+    high, low = high_ref[...], low_ref[...]
+    values = []
+    if parts:
+        columns = jnp.concatenate([part[...] for part in parts], axis=0)
+        depth = columns.shape[0]
+        values.append(product((high[:, :depth], low[:, :depth]), split(columns)))
+    for slab in slabs:
+        columns = jnp.concatenate([slab[index_ref[0] ^ k] for k in range(len(blocks))], axis=0)
+        values.append(product((high, low), split(columns)))
+    rows = high.shape[0] // len(blocks)
     for i, block in enumerate(blocks):
-        block[...] = value[i * width : (i + 1) * width]
-
-
-def load(high, low, parts, blocks):
+        block[...] = jnp.concatenate([value[i * rows : (i + 1) * rows] for value in values], axis=1)
+
+
+def load(index, high, low, parts, slabs, blocks):
     rank = high.shape[0]
-    columns = parts[0].shape[1]
+    columns = sum(piece.shape[-1] for piece in [*parts[:1], *slabs])
     return pl.pallas_call(
-        functools.partial(load_kernel, len(parts)),
-        in_specs=[VMEM] * (2 + len(parts)),
+        functools.partial(load_kernel, len(parts), len(slabs)),
+        in_specs=[SMEM] + [VMEM] * (2 + len(parts) + len(slabs)),
         out_specs=[VMEM] * blocks,
         out_shape=[jax.ShapeDtypeStruct((rank // blocks, columns), jnp.float32)] * blocks,
         compiler_params=params(),
         cost_estimate=FREE,
-    )(high, low, *parts)
-
-
-def join_kernel(group, *refs):
+    )(index, high, low, *parts, *slabs)
+
+
+def join_kernel(group, wide, *refs):
     *terms, out_ref, buf, sems = refs
-    width = terms[0].shape[1]
-    member = lax.rem(lax.axis_index("tm"), group)
+    groups = len(terms) // group
+    rows, share = buf.shape[1:]
+    narrow = share - groups * wide
+    index = lax.axis_index("tm")
+    member, place = lax.rem(index, group), lax.div(index, group)
     copies = []
     for k in range(group):
-        value = terms[k][...]
-        for term in terms[group + k :: group]:
-            value = value + term[...]
-        buf[k] = value
-        span = pl.ds(pl.multiple_of((member ^ k) * width, width), width)
+        members = terms[k::group]
+        if narrow:
+            value = members[0][:, :narrow]
+            for term in members[1:]:
+                value = value + term[:, :narrow]
+            buf[k, :, :narrow] = value
+        if wide:
+            for g, term in enumerate(members):
+                buf[k, :, pl.ds(pl.multiple_of(narrow + (place ^ g) * wide, 128), wide)] = term[:, narrow:]
+        span = pl.ds(pl.multiple_of((member ^ k) * share, share), share)
         copies.append(pltpu.make_async_copy(buf.at[k], out_ref.at[:, span], sems.at[k]))
         copies[-1].start()
     for copy in copies:
         copy.wait()
 
 
-def join(terms, group):
-    rows, width = terms[0].shape
+def join(terms, group, wide, points):
+    rows = terms[0].shape[0]
     return pl.pallas_call(
-        functools.partial(join_kernel, group),
+        functools.partial(join_kernel, group, wide),
         in_specs=[VMEM] * len(terms),
         out_specs=HBM,
-        out_shape=jax.ShapeDtypeStruct((rows, group * width), jnp.float32),
-        scratch_shapes=[pltpu.VMEM((group, rows, width), jnp.float32), pltpu.SemaphoreType.DMA((group,))],
+        out_shape=jax.ShapeDtypeStruct((rows, points), jnp.float32),
+        scratch_shapes=[pltpu.VMEM((group, rows, points // group), jnp.float32), pltpu.SemaphoreType.DMA((group,))],
         compiler_params=params(),
         cost_estimate=FREE,
     )(*terms)
@@ -198,33 +222,44 @@
 
 def on_device(snapshots, space_factor):
     rows, points = snapshots.shape
-    rank = space_factor.shape[1]
     times, spaces = lax.axis_size("tm"), lax.axis_size("space")
     group = min(4, times)
+    groups = times // group
     index = lax.axis_index("tm")
     core = lax.axis_index("space") % 2
-
-    mine, other, parts = project(snapshots, space_factor, group)
+    wide = int(points // group * WHOLE_SHARE) // groups // 128 * 128
+
+    halves, parts, slabs = project(snapshots, space_factor, group, groups, wide)
+    order = [0]
+    for i in range(groups.bit_length() - 1):
+        halves = jnp.concatenate([halves, swap(halves, "tm", group << i)], axis=1)
+        order = order + [k ^ group << i for k in order]
+    if wide:
+        halves, slabs = lax.optimization_barrier((halves, slabs))
+        slabs = [lax.all_to_all(slab, "tm", 0, 0, tiled=True) for slab in slabs]
     parts = [part if k == 0 else swap(part, "tm", k) for k, part in enumerate(parts)]
 
-    mine = mine + swap(other, "space", 1)
+    mine = halves[0] + swap(halves[1], "space", 1)
     for i in range(1, spaces.bit_length() - 1):
         mine = mine + swap(mine, "space", 1 << i)
 
-    pair = jnp.concatenate([mine, swap(mine, "tm", 1)], axis=0)
-    pair, *parts = lax.optimization_barrier((pair, *parts))
-    offsets = [*range(group, times, 2), *range(2, group, 2)]
-    mine = jnp.concatenate([pair] + [swap(pair, "tm", k) for k in offsets], axis=0)
-    order = [k ^ i for k in [0, *offsets] for i in range(2)]
-    high_t, low_t, own = mix(jnp.stack([index, core]), mine, swap(mine, "space", 1), times, group, order)
-
-    blocks = list(load(high_t, low_t, parts, times))
+    for i in range(group.bit_length() - 1):
+        mine = jnp.concatenate([mine, swap(mine, "tm", 1 << i)], axis=0)
+        order = order + [k ^ 1 << i for k in order]
+        if parts:
+            mine, parts[1 << i] = lax.optimization_barrier((mine, parts[1 << i]))
+    theirs = swap(mine, "space", 1)
+    if parts:
+        theirs, parts[-1] = lax.optimization_barrier((theirs, parts[-1]))
+    high_t, low_t, own = mix(jnp.stack([index, core]), mine, theirs, times, order)
+
+    blocks = list(load(index.reshape(1), high_t, low_t, parts, slabs, times))
     terms = [blocks[0]] + [None] * (times - 1)
     for k in [*range(group, times), *range(1, group)]:
         if k == group - 1:
             blocks[k], terms[1] = lax.optimization_barrier((blocks[k], terms[1]))
         terms[k] = swap(blocks[k], "tm", k)
-    return own, join(terms, group)
+    return own, join(terms, group, wide, points)
 
 
 def solution(mesh):

time: 62 us -> 66.9 us (1.079)
  starting transfers between devices: 22.9 us -> 30.6 us
  waiting for transfers between devices: 31.3 us -> 27.1 us
  Pallas kernels: 6.81 us -> 7.56 us
    all_to_all x0 -> x1, starting transfers between devices: none -> 7.05 us  [on_device(): slabs = [lax.all_to_all(slab, 'tm', 0, 0, tiled=True) for slab in slabs]]
    ppermute x17 -> x16, waiting for transfers between devices: 31.3 us -> 27.1 us  [swap(): lax.ppermute(value, axis, [(i, i ^ offset) for i in range(lax.axis_size(a...]
    pallas_call x3, Pallas kernels: 4.35 us -> 5.06 us  [the longest x1 3.54 us: project(): pl.pallas_call(functools.partial(project_kernel, depth, group, wide), in_...]
    ppermute x17 -> x16, starting transfers between devices: 22.9 us -> 23.5 us  [swap(): lax.ppermute(value, axis, [(i, i ^ offset) for i in range(lax.axis_size(a...]
  transfers between devices with their start and end apart: 17 -> 17, of which waited for: 9 -> 12; matrix products, arithmetic and copies ran while one was open for 0% -> 0% of each run, Pallas kernels for 0% -> 4%
where the time goes in v12:
time: 66.9 us; the launch traced here: 66.1 us
  starting transfers between devices  30.6 us (46%)
  waiting for transfers between devices  27.1 us (41%)
  Pallas kernels  7.56 us (11%)
  between operations  0.69 us (1%)
    ppermute x16, waiting for transfers between devices, swap(): lax.ppermute(value, axis, [(i, i ^ offset) for i in range(lax.axis_size(a...  27.1 us
    ppermute x16, starting transfers between devices, swap(): lax.ppermute(value, axis, [(i, i ^ offset) for i in range(lax.axis_size(a...  23.5 us
    all_to_all x1, starting transfers between devices, on_device(): slabs = [lax.all_to_all(slab, 'tm', 0, 0, tiled=True) for slab in slabs]  7.05 us
    pallas_call x1, Pallas kernels, project(): pl.pallas_call(functools.partial(project_kernel, depth, group, wide), in_...  3.54 us
    pallas_call x1, Pallas kernels, mix(): pl.pallas_call(functools.partial(mix_kernel, times, order), in_specs=[SME...  2.5 us
  transfers between devices with their start and end apart: 17, of which 12 were waited for; matrix products, arithmetic and copies ran while one was open for 0% of the time, Pallas kernels for 4%

profile of v12, /device:TPU:8, one launch (start us, length us, event | category | flops | bytes accessed | tf_op | source)
XLA Modules:
  0.0 66.1 jit_solution(1120828838594402078)
XLA Ops:
  0.6 3.5 %shard_map.41 = (f32[2,32,256]{2,1,0:T(8,128)S(1)}, f32[64,256]{1,0:T(8,128)S(1)}, f32[64,256]{1,0:T(8,128)S(1)}, f32[64,256]{1,0:T(8,128)S(1)}, f32[64,256]{1,0:T(8,128)S(1)}, /*index=5*/f32[8,64,384]{2,1,0:T(8,128)}) custom-call(f32[64,4096]{1,0:T(8,128)} %snapshots_ref.1, f32[4096,256]{1,0:T(8,128)} %factor_ref.1), custom_call_target="tpu_custom_call" | custom-call | tf_op jit(solution)/shard_map/pallas_call | solution.py:86
  4.2 2.7 %collective-permute-start = (f32[2,32,256]{2,1,0:T(8,128)S(1)}, f32[2,32,256]{2,1,0:T(8,128)S(1)}, u32[]{:S(2)}, u32[]{:S(2)}) collective-permute-start(f32[2,32,256]{2,1,0:T(8,128)S(1)} %get-tuple-element.29), channel_id=1, source_target_pairs={{0,16},{4,20},{8,24},{12,28},{16,0},{20,4},{24,8},{28,12},{1,17},{... | collective-permute-start | bytes 196616 | tf_op jit(solution)/shard_map/ppermute | solution.py:220
  6.8 2.6 %collective-permute-done = f32[2,32,256]{2,1,0:T(8,128)S(1)} collective-permute-done((f32[2,32,256]{2,1,0:T(8,128)S(1)}, f32[2,32,256]{2,1,0:T(8,128)S(1)}, u32[]{:S(2)}, u32[]{:S(2)}) %collective-permute-start) | collective-permute-done | bytes 65568 | tf_op jit(solution)/shard_map/ppermute | solution.py:220
  9.5 7.1 %all-to-all-start = ((f32[8,64,384]{2,1,0:T(8,128)}), f32[8,64,384]{2,1,0:T(8,128)S(1)}, u32[]{:S(2)}, u32[]{:S(2)}) async-start(f32[8,64,384]{2,1,0:T(8,128)} %get-tuple-element.45), calls=%async_computation | async-start | bytes 1572864 | tf_op jit(solution)/shard_map/all_to_all | solution.py:239
  16.5 0.1 collective-permute-start.1
  16.6 1.2 %collective-permute-done.1 = f32[64,256]{1,0:T(8,128)S(1)} collective-permute-done((f32[64,256]{1,0:T(8,128)S(1)}, f32[64,256]{1,0:T(8,128)S(1)}, u32[]{:S(2)}, u32[]{:S(2)}) %collective-permute-start.1) | collective-permute-done | bytes 65568 | tf_op jit(solution)/shard_map/ppermute | solution.py:220
  17.9 1.6 %collective-permute-start.2 = (f32[64,256]{1,0:T(8,128)S(1)}, f32[64,256]{1,0:T(8,128)S(1)}, u32[]{:S(2)}, u32[]{:S(2)}) collective-permute-start(f32[64,256]{1,0:T(8,128)S(1)} %bitcast_add_fusion), channel_id=1, source_target_pairs={{0,2},{1,3},{2,0},{3,1},{4,6},{5,7},{6,4},{7,5},{8,10},{9,11},{10,... | collective-permute-start | bytes 196616 | tf_op jit(solution)/shard_map/ppermute | solution.py:220
  19.5 2.7 %collective-permute-done.2 = f32[64,256]{1,0:T(8,128)S(1)} collective-permute-done((f32[64,256]{1,0:T(8,128)S(1)}, f32[64,256]{1,0:T(8,128)S(1)}, u32[]{:S(2)}, u32[]{:S(2)}) %collective-permute-start.2) | collective-permute-done | bytes 65568 | tf_op jit(solution)/shard_map/ppermute | solution.py:220
  22.2 1.5 %collective-permute-start.3 = (f32[64,256]{1,0:T(8,128)S(1)}, f32[64,256]{1,0:T(8,128)S(1)}, u32[]{:S(2)}, u32[]{:S(2)}) collective-permute-start(f32[64,256]{1,0:T(8,128)S(1)} %add.12), channel_id=1, source_target_pairs={{0,4},{4,0},{8,12},{12,8},{16,20},{20,16},{24,28},{28,24},{1,5},{5... | collective-permute-start | bytes 196616 | tf_op jit(solution)/shard_map/ppermute | solution.py:220
  23.8 0.6 collective-permute-start.4
  24.3 3.9 %collective-permute-done.3 = f32[64,256]{1,0:T(8,128)S(1)} collective-permute-done((f32[64,256]{1,0:T(8,128)S(1)}, f32[64,256]{1,0:T(8,128)S(1)}, u32[]{:S(2)}, u32[]{:S(2)}) %collective-permute-start.3) | collective-permute-done | bytes 65568 | tf_op jit(solution)/shard_map/ppermute | solution.py:220
  28.2 2.2 %collective-permute-done.4.refs_1_ = f32[64,256]{1,0:T(8,128)S(1)} collective-permute-done((f32[64,256]{1,0:T(8,128)S(1)}, f32[64,256]{1,0:T(8,128)S(1)}, u32[]{:S(2)}, u32[]{:S(2)}) %collective-permute-start.4) | collective-permute-done | bytes 65568 | tf_op jit(solution)/shard_map/ppermute | solution.py:220
  30.4 0.0 collective-permute-start.5
  30.5 2.0 %collective-permute-start.6 = (f32[64,256]{1,0:T(8,128)S(1)}, f32[64,256]{1,0:T(8,128)S(1)}, u32[]{:S(2)}, u32[]{:S(2)}) collective-permute-start(f32[64,256]{1,0:T(8,128)S(1)} %get-tuple-element.34), channel_id=1, source_target_pairs={{0,8},{4,12},{8,0},{12,4},{16,24},{20,28},{24,16},{28,20},{1,9},{5... | collective-permute-start | bytes 196616 | tf_op jit(solution)/shard_map/ppermute | solution.py:220
  32.5 3.1 %collective-permute-done.5 = f32[128,256]{1,0:T(8,128)S(1)} collective-permute-done((f32[128,256]{1,0:T(8,128)S(1)}, f32[128,256]{1,0:T(8,128)S(1)}, u32[]{:S(2)}, u32[]{:S(2)}) %collective-permute-start.5) | collective-permute-done | bytes 131104 | tf_op jit(solution)/shard_map/ppermute | solution.py:220
  35.6 0.7 %collective-permute-done.6.refs_2_ = f32[64,256]{1,0:T(8,128)S(1)} collective-permute-done((f32[64,256]{1,0:T(8,128)S(1)}, f32[64,256]{1,0:T(8,128)S(1)}, u32[]{:S(2)}, u32[]{:S(2)}) %collective-permute-start.6) | collective-permute-done | bytes 65568 | tf_op jit(solution)/shard_map/ppermute | solution.py:220
  36.2 0.0 collective-permute-start.7
  36.2 2.8 %collective-permute-start.8 = (f32[64,256]{1,0:T(8,128)S(1)}, f32[64,256]{1,0:T(8,128)S(1)}, u32[]{:S(2)}, u32[]{:S(2)}) collective-permute-start(f32[64,256]{1,0:T(8,128)S(1)} %get-tuple-element.36), channel_id=1, source_target_pairs={{0,12},{4,8},{8,4},{12,0},{16,28},{20,24},{24,20},{28,16},{1,13},{... | collective-permute-start | bytes 196616 | tf_op jit(solution)/shard_map/ppermute | solution.py:220
  39.1 0.1 pad_add_fusion.index_ref
  39.2 2.7 %collective-permute-done.8.refs_3_ = f32[64,256]{1,0:T(8,128)S(1)} collective-permute-done((f32[64,256]{1,0:T(8,128)S(1)}, f32[64,256]{1,0:T(8,128)S(1)}, u32[]{:S(2)}, u32[]{:S(2)}) %collective-permute-start.8) | collective-permute-done | bytes 65568 | tf_op jit(solution)/shard_map/ppermute | solution.py:220
  41.8 0.0 collective-permute-done.7.theirs_ref
  41.9 2.5 %shard_map.42 = (bf16[256,512]{1,0:T(8,128)(2,1)S(1)}, bf16[256,512]{1,0:T(8,128)(2,1)S(1)}, f32[64,256]{1,0:T(8,128)}) custom-call(s32[2]{0:T(128)S(1)} %pad_add_fusion.index_ref, f32[256,256]{1,0:T(8,128)S(1)} %pad_maximum_fusion.mine_ref, f32[256,256]{1,0:T(8,128)S(1)} %collective-permute-done.7.theirs_ref), custom_call_target="tpu_custom_call" | custom-call | tf_op jit(solution)/shard_map/pallas_call | solution.py:142
  44.4 0.0 all-to-all-done.refs_4_
  44.4 0.7 %shard_map.43 = (f32[32,640]{1,0:T(8,128)S(1)}, f32[32,640]{1,0:T(8,128)S(1)}, f32[32,640]{1,0:T(8,128)S(1)}, f32[32,640]{1,0:T(8,128)S(1)}, f32[32,640]{1,0:T(8...) custom-call(s32[1]{0:T(128)} %bitcast.index_ref, ...), custom_call_target="tpu_custom_call" | custom-call | tf_op jit(solution)/shard_map/pallas_call | solution.py:171
  45.0 1.2 %collective-permute-start.9 = (f32[32,640]{1,0:T(8,128)S(1)}, f32[32,640]{1,0:T(8,128)S(1)}, u32[]{:S(2)}, u32[]{:S(2)}) collective-permute-start(f32[32,640]{1,0:T(8,128)S(1)} %get-tuple-element.48), channel_id=1, source_target_pairs={{0,4},{4,0},{8,12},{12,8},{16,20},{20,16},{24,28},{28,24},{1,5},{5... | collective-permute-start | bytes 245768 | tf_op jit(solution)/shard_map/ppermute | solution.py:220
  46.2 2.1 %collective-permute-start.10 = (f32[32,640]{1,0:T(8,128)S(1)}, f32[32,640]{1,0:T(8,128)S(1)}, u32[]{:S(2)}, u32[]{:S(2)}) collective-permute-start(f32[32,640]{1,0:T(8,128)S(1)} %get-tuple-element.50), channel_id=1, source_target_pairs={{0,8},{4,12},{8,0},{12,4},{16,24},{20,28},{24,16},{28,20},{1,9},{5... | collective-permute-start | bytes 245768 | tf_op jit(solution)/shard_map/ppermute | solution.py:220
  48.3 2.0 %collective-permute-start.12 = (f32[32,640]{1,0:T(8,128)S(1)}, f32[32,640]{1,0:T(8,128)S(1)}, u32[]{:S(2)}, u32[]{:S(2)}) collective-permute-start(f32[32,640]{1,0:T(8,128)S(1)} %get-tuple-element.52), channel_id=1, source_target_pairs={{0,16},{4,20},{8,24},{12,28},{16,0},{20,4},{24,8},{28,12},{1,17},{... | collective-permute-start | bytes 245768 | tf_op jit(solution)/shard_map/ppermute | solution.py:220
  50.3 1.4 %collective-permute-start.13 = (f32[32,640]{1,0:T(8,128)S(1)}, f32[32,640]{1,0:T(8,128)S(1)}, u32[]{:S(2)}, u32[]{:S(2)}) collective-permute-start(f32[32,640]{1,0:T(8,128)S(1)} %get-tuple-element.53), channel_id=1, source_target_pairs={{0,20},{4,16},{8,28},{12,24},{16,4},{20,0},{24,12},{28,8},{1,21},{... | collective-permute-start | bytes 245768 | tf_op jit(solution)/shard_map/ppermute | solution.py:220
  51.8 2.3 %collective-permute-start.14 = (f32[32,640]{1,0:T(8,128)S(1)}, f32[32,640]{1,0:T(8,128)S(1)}, u32[]{:S(2)}, u32[]{:S(2)}) collective-permute-start(f32[32,640]{1,0:T(8,128)S(1)} %get-tuple-element.54), channel_id=1, source_target_pairs={{0,24},{4,28},{8,16},{12,20},{16,8},{20,12},{24,0},{28,4},{1,25},{... | collective-permute-start | bytes 245768 | tf_op jit(solution)/shard_map/ppermute | solution.py:220
  54.0 0.0 collective-permute-done.9.refs_1_
  54.0 0.7 %collective-permute-start.15 = (f32[32,640]{1,0:T(8,128)S(1)}, f32[32,640]{1,0:T(8,128)S(1)}, u32[]{:S(2)}, u32[]{:S(2)}) collective-permute-start(f32[32,640]{1,0:T(8,128)S(1)} %get-tuple-element.55), channel_id=1, source_target_pairs={{0,28},{4,24},{8,20},{12,16},{16,12},{20,8},{24,4},{28,0},{1,29},{... | collective-permute-start | bytes 245768 | tf_op jit(solution)/shard_map/ppermute | solution.py:220
  54.7 0.0 collective-permute-done.10.refs_2_
  54.7 2.6 %collective-permute-start.11 = (f32[32,640]{1,0:T(8,128)S(1)}, f32[32,640]{1,0:T(8,128)S(1)}, u32[]{:S(2)}, u32[]{:S(2)}) collective-permute-start(f32[32,640]{1,0:T(8,128)S(1)} %get-tuple-element.51), channel_id=1, source_target_pairs={{0,12},{4,8},{8,4},{12,0},{16,28},{20,24},{24,20},{28,16},{1,13},{... | collective-permute-start | bytes 245768 | tf_op jit(solution)/shard_map/ppermute | solution.py:220
  57.3 2.8 %collective-permute-done.12.refs_4_ = f32[32,640]{1,0:T(8,128)S(1)} collective-permute-done((f32[32,640]{1,0:T(8,128)S(1)}, f32[32,640]{1,0:T(8,128)S(1)}, u32[]{:S(2)}, u32[]{:S(2)}) %collective-permute-start.12) | collective-permute-done | bytes 81952 | tf_op jit(solution)/shard_map/ppermute | solution.py:220
  60.1 1.8 %collective-permute-done.13.refs_5_ = f32[32,640]{1,0:T(8,128)S(1)} collective-permute-done((f32[32,640]{1,0:T(8,128)S(1)}, f32[32,640]{1,0:T(8,128)S(1)}, u32[]{:S(2)}, u32[]{:S(2)}) %collective-permute-start.13) | collective-permute-done | bytes 81952 | tf_op jit(solution)/shard_map/ppermute | solution.py:220
  61.8 1.7 %collective-permute-done.14.refs_6_ = f32[32,640]{1,0:T(8,128)S(1)} collective-permute-done((f32[32,640]{1,0:T(8,128)S(1)}, f32[32,640]{1,0:T(8,128)S(1)}, u32[]{:S(2)}, u32[]{:S(2)}) %collective-permute-start.14) | collective-permute-done | bytes 81952 | tf_op jit(solution)/shard_map/ppermute | solution.py:220
  63.5 1.7 %collective-permute-done.15.refs_7_ = f32[32,640]{1,0:T(8,128)S(1)} collective-permute-done((f32[32,640]{1,0:T(8,128)S(1)}, f32[32,640]{1,0:T(8,128)S(1)}, u32[]{:S(2)}, u32[]{:S(2)}) %collective-permute-start.15) | collective-permute-done | bytes 81952 | tf_op jit(solution)/shard_map/ppermute | solution.py:220
  65.2 0.0 collective-permute-done.11.refs_3_
  65.2 0.8 %shard_map.44 = f32[32,4096]{1,0:T(8,128)} custom-call(f32[32,640]{1,0:T(8,128)S(1)} %get-tuple-element.46.refs_0_, f32[32,640]{1,0:T(8,128)S(1)} %collective-permute-done.9.refs_1_, f32[32,640]{1,0:T(8,128)S(1)} %collective-permute-done.10.refs_2_, f32[32,640]{1,0:T(8,128)S(1)} %collective-permute-done.11.refs_3_, ...), custom_call_target="tpu_custom_call" | custom-call | tf_op jit(solution)/shard_map/pallas_call | solution.py:208
  (6 shorter events, 0.1 us)
Async XLA Ops:
  4.2 5.3 %collective-permute-start = (f32[2,32,256]{2,1,0:T(8,128)S(1)}, f32[2,32,256]{2,1,0:T(8,128)S(1)}, u32[]{:S(2)}, u32[]{:S(2)}) collective-permute-start(f32[2,32,256]{2,1,0:T(8,128)S(1)} %get-tuple-element.29), channel_id=1, source_target_pairs={{0,16},{4,20},{8,24},{12,28},{16,0},{20,4},{24,8},{28,12},{1,17},{... | collective-permute-start | bytes 196616 | tf_op jit(solution)/shard_map/ppermute | solution.py:220
  9.5 34.9 %all-to-all-start = ((f32[8,64,384]{2,1,0:T(8,128)}), f32[8,64,384]{2,1,0:T(8,128)S(1)}, u32[]{:S(2)}, u32[]{:S(2)}) async-start(f32[8,64,384]{2,1,0:T(8,128)} %get-tuple-element.45), calls=%async_computation | async-start | bytes 1572864 | tf_op jit(solution)/shard_map/all_to_all | solution.py:239
  16.5 1.3 %collective-permute-start.1 = (f32[64,256]{1,0:T(8,128)S(1)}, f32[64,256]{1,0:T(8,128)S(1)}, u32[]{:S(2)}, u32[]{:S(2)}) collective-permute-start(f32[64,256]{1,0:T(8,128)S(1)} %slice_bitcast_fusion), channel_id=1, source_target_pairs={{0,1},{1,0},{2,3},{3,2},{4,5},{5,4},{6,7},{7,6},{8,9},{9,8},{10,11... | collective-permute-start | bytes 196616 | tf_op jit(solution)/shard_map/ppermute | solution.py:220
  17.9 4.3 %collective-permute-start.2 = (f32[64,256]{1,0:T(8,128)S(1)}, f32[64,256]{1,0:T(8,128)S(1)}, u32[]{:S(2)}, u32[]{:S(2)}) collective-permute-start(f32[64,256]{1,0:T(8,128)S(1)} %bitcast_add_fusion), channel_id=1, source_target_pairs={{0,2},{1,3},{2,0},{3,1},{4,6},{5,7},{6,4},{7,5},{8,10},{9,11},{10,... | collective-permute-start | bytes 196616 | tf_op jit(solution)/shard_map/ppermute | solution.py:220
  22.2 6.0 %collective-permute-start.3 = (f32[64,256]{1,0:T(8,128)S(1)}, f32[64,256]{1,0:T(8,128)S(1)}, u32[]{:S(2)}, u32[]{:S(2)}) collective-permute-start(f32[64,256]{1,0:T(8,128)S(1)} %add.12), channel_id=1, source_target_pairs={{0,4},{4,0},{8,12},{12,8},{16,20},{20,16},{24,28},{28,24},{1,5},{5... | collective-permute-start | bytes 196616 | tf_op jit(solution)/shard_map/ppermute | solution.py:220
  23.8 6.7 %collective-permute-start.4 = (f32[64,256]{1,0:T(8,128)S(1)}, f32[64,256]{1,0:T(8,128)S(1)}, u32[]{:S(2)}, u32[]{:S(2)}) collective-permute-start(f32[64,256]{1,0:T(8,128)S(1)} %get-tuple-element.32), channel_id=1, source_target_pairs={{0,4},{4,0},{8,12},{12,8},{16,20},{20,16},{24,28},{28,24},{1,5},{5... | collective-permute-start | bytes 196616 | tf_op jit(solution)/shard_map/ppermute | solution.py:220
  30.4 5.1 %collective-permute-start.5 = (f32[128,256]{1,0:T(8,128)S(1)}, f32[128,256]{1,0:T(8,128)S(1)}, u32[]{:S(2)}, u32[]{:S(2)}) collective-permute-start(f32[128,256]{1,0:T(8,128)S(1)} %pad_maximum_fusion.2), channel_id=1, source_target_pairs={{0,8},{4,12},{8,0},{12,4},{16,24},{20,28},{24,16},{28,20},{1,9},{5... | collective-permute-start | bytes 393224 | tf_op jit(solution)/shard_map/ppermute | solution.py:220
  30.5 5.8 %collective-permute-start.6 = (f32[64,256]{1,0:T(8,128)S(1)}, f32[64,256]{1,0:T(8,128)S(1)}, u32[]{:S(2)}, u32[]{:S(2)}) collective-permute-start(f32[64,256]{1,0:T(8,128)S(1)} %get-tuple-element.34), channel_id=1, source_target_pairs={{0,8},{4,12},{8,0},{12,4},{16,24},{20,28},{24,16},{28,20},{1,9},{5... | collective-permute-start | bytes 196616 | tf_op jit(solution)/shard_map/ppermute | solution.py:220
  36.2 5.6 %collective-permute-start.7 = (f32[256,256]{1,0:T(8,128)S(1)}, f32[256,256]{1,0:T(8,128)S(1)}, u32[]{:S(2)}, u32[]{:S(2)}) collective-permute-start(f32[256,256]{1,0:T(8,128)S(1)} %pad_maximum_fusion.mine_ref), channel_id=1, source_target_pairs={{0,1},{1,0},{2,3},{3,2},{4,5},{5,4},{6,7},{7,6},{8,9},{9,8},{10,11... | collective-permute-start | bytes 786440 | tf_op jit(solution)/shard_map/ppermute | solution.py:220
  36.2 5.6 %collective-permute-start.8 = (f32[64,256]{1,0:T(8,128)S(1)}, f32[64,256]{1,0:T(8,128)S(1)}, u32[]{:S(2)}, u32[]{:S(2)}) collective-permute-start(f32[64,256]{1,0:T(8,128)S(1)} %get-tuple-element.36), channel_id=1, source_target_pairs={{0,12},{4,8},{8,4},{12,0},{16,28},{20,24},{24,20},{28,16},{1,13},{... | collective-permute-start | bytes 196616 | tf_op jit(solution)/shard_map/ppermute | solution.py:220
  45.0 9.0 %collective-permute-start.9 = (f32[32,640]{1,0:T(8,128)S(1)}, f32[32,640]{1,0:T(8,128)S(1)}, u32[]{:S(2)}, u32[]{:S(2)}) collective-permute-start(f32[32,640]{1,0:T(8,128)S(1)} %get-tuple-element.48), channel_id=1, source_target_pairs={{0,4},{4,0},{8,12},{12,8},{16,20},{20,16},{24,28},{28,24},{1,5},{5... | collective-permute-start | bytes 245768 | tf_op jit(solution)/shard_map/ppermute | solution.py:220
  46.2 8.5 %collective-permute-start.10 = (f32[32,640]{1,0:T(8,128)S(1)}, f32[32,640]{1,0:T(8,128)S(1)}, u32[]{:S(2)}, u32[]{:S(2)}) collective-permute-start(f32[32,640]{1,0:T(8,128)S(1)} %get-tuple-element.50), channel_id=1, source_target_pairs={{0,8},{4,12},{8,0},{12,4},{16,24},{20,28},{24,16},{28,20},{1,9},{5... | collective-permute-start | bytes 245768 | tf_op jit(solution)/shard_map/ppermute | solution.py:220
  48.3 11.8 %collective-permute-start.12 = (f32[32,640]{1,0:T(8,128)S(1)}, f32[32,640]{1,0:T(8,128)S(1)}, u32[]{:S(2)}, u32[]{:S(2)}) collective-permute-start(f32[32,640]{1,0:T(8,128)S(1)} %get-tuple-element.52), channel_id=1, source_target_pairs={{0,16},{4,20},{8,24},{12,28},{16,0},{20,4},{24,8},{28,12},{1,17},{... | collective-permute-start | bytes 245768 | tf_op jit(solution)/shard_map/ppermute | solution.py:220
  50.3 11.5 %collective-permute-start.13 = (f32[32,640]{1,0:T(8,128)S(1)}, f32[32,640]{1,0:T(8,128)S(1)}, u32[]{:S(2)}, u32[]{:S(2)}) collective-permute-start(f32[32,640]{1,0:T(8,128)S(1)} %get-tuple-element.53), channel_id=1, source_target_pairs={{0,20},{4,16},{8,28},{12,24},{16,4},{20,0},{24,12},{28,8},{1,21},{... | collective-permute-start | bytes 245768 | tf_op jit(solution)/shard_map/ppermute | solution.py:220
  51.8 11.8 %collective-permute-start.14 = (f32[32,640]{1,0:T(8,128)S(1)}, f32[32,640]{1,0:T(8,128)S(1)}, u32[]{:S(2)}, u32[]{:S(2)}) collective-permute-start(f32[32,640]{1,0:T(8,128)S(1)} %get-tuple-element.54), channel_id=1, source_target_pairs={{0,24},{4,28},{8,16},{12,20},{16,8},{20,12},{24,0},{28,4},{1,25},{... | collective-permute-start | bytes 245768 | tf_op jit(solution)/shard_map/ppermute | solution.py:220
  54.0 11.2 %collective-permute-start.15 = (f32[32,640]{1,0:T(8,128)S(1)}, f32[32,640]{1,0:T(8,128)S(1)}, u32[]{:S(2)}, u32[]{:S(2)}) collective-permute-start(f32[32,640]{1,0:T(8,128)S(1)} %get-tuple-element.55), channel_id=1, source_target_pairs={{0,28},{4,24},{8,20},{12,16},{16,12},{20,8},{24,4},{28,0},{1,29},{... | collective-permute-start | bytes 245768 | tf_op jit(solution)/shard_map/ppermute | solution.py:220
  54.7 10.5 %collective-permute-start.11 = (f32[32,640]{1,0:T(8,128)S(1)}, f32[32,640]{1,0:T(8,128)S(1)}, u32[]{:S(2)}, u32[]{:S(2)}) collective-permute-start(f32[32,640]{1,0:T(8,128)S(1)} %get-tuple-element.51), channel_id=1, source_target_pairs={{0,12},{4,8},{8,4},{12,0},{16,28},{20,24},{24,20},{28,16},{1,13},{... | collective-permute-start | bytes 245768 | tf_op jit(solution)/shard_map/ppermute | solution.py:220

commit v13 on v11

--- a/solution.py
+++ b/solution.py
@@ -211,12 +211,16 @@
     for i in range(1, spaces.bit_length() - 1):
         mine = mine + swap(mine, "space", 1 << i)
 
-    pair = jnp.concatenate([mine, swap(mine, "tm", 1)], axis=0)
-    pair, *parts = lax.optimization_barrier((pair, *parts))
-    offsets = [*range(group, times, 2), *range(2, group, 2)]
-    mine = jnp.concatenate([pair] + [swap(pair, "tm", k) for k in offsets], axis=0)
-    order = [k ^ i for k in [0, *offsets] for i in range(2)]
-    high_t, low_t, own = mix(jnp.stack([index, core]), mine, swap(mine, "space", 1), times, group, order)
+    near = group // 2
+    order = [k for k in range(times) if k % group < near]
+    mine = jnp.concatenate([mine] + [swap(mine, "tm", k) for k in order[1:]], axis=0)
+    mine, parts[1] = lax.optimization_barrier((mine, parts[1]))
+    for offset in range(near, group, near):
+        mine = jnp.concatenate([mine, swap(mine, "tm", offset)], axis=0)
+        order = order + [k ^ offset for k in order]
+    mine, parts[2] = lax.optimization_barrier((mine, parts[2]))
+    theirs, parts[3] = lax.optimization_barrier((swap(mine, "space", 1), parts[3]))
+    high_t, low_t, own = mix(jnp.stack([index, core]), mine, theirs, times, group, order)
 
     blocks = list(load(high_t, low_t, parts, times))
     terms = [blocks[0]] + [None] * (times - 1)

time: 62 us -> 60.4 us (0.974)
  waiting for transfers between devices: 31.3 us -> 30.2 us
    ppermute x17, waiting for transfers between devices: 31.3 us -> 30.2 us  [swap(): lax.ppermute(value, axis, [(i, i ^ offset) for i in range(lax.axis_size(a...]
  transfers between devices with their start and end apart: 17 -> 17, of which waited for: 9 -> 10; matrix products, arithmetic and copies ran while one was open for 0% -> 0% of each run, Pallas kernels for 0% -> 0%
where the time goes in v13:
time: 60.4 us; the launch traced here: 60.2 us
  waiting for transfers between devices  30.2 us (50%)
  starting transfers between devices  22.3 us (37%)
  Pallas kernels  6.81 us (11%)
  between operations  0.7 us (1%)
    ppermute x17, waiting for transfers between devices, swap(): lax.ppermute(value, axis, [(i, i ^ offset) for i in range(lax.axis_size(a...  30.2 us
    ppermute x17, starting transfers between devices, swap(): lax.ppermute(value, axis, [(i, i ^ offset) for i in range(lax.axis_size(a...  22.3 us
    pallas_call x1, Pallas kernels, project(): pl.pallas_call(functools.partial(project_kernel, depth), in_specs=[HBM, H...  2.93 us
    pallas_call x1, Pallas kernels, mix(): pl.pallas_call(functools.partial(mix_kernel, times, order), in_specs=[SME...  2.46 us
  transfers between devices with their start and end apart: 17, of which 10 were waited for; matrix products, arithmetic and copies ran while one was open for 0% of the time, Pallas kernels for 0%

profile of v13, /device:TPU:8, one launch (start us, length us, event | category | flops | bytes accessed | tf_op | source)
XLA Modules:
  0.0 60.2 jit_solution(13931413596907513138)
XLA Ops:
  0.6 2.9 %shard_map.41 = (f32[32,256]{1,0:T(8,128)S(1)}, f32[32,256]{1,0:T(8,128)S(1)}, f32[64,1024]{1,0:T(8,128)S(1)}, f32[64,1024]{1,0:T(8,128)S(1)}, f32[64,1024]{1,0:T(8,128)S(1)}, /*index=5*/f32[64,1024]{1,0:T(8,128)S(1)}) custom-call(f32[64,4096]{1,0:T(8,128)} %snapshots_ref.1, f32[4096,256]{1,0:T(8,128)} %factor_ref.1), custom_call_target="tpu_custom_call" | custom-call | tf_op jit(solution)/shard_map/pallas_call | solution.py:76
  3.6 1.6 %collective-permute-start.5 = (f32[64,1024]{1,0:T(8,128)S(1)}, f32[64,1024]{1,0:T(8,128)S(1)}, u32[]{:S(2)}, u32[]{:S(2)}) collective-permute-start(f32[64,1024]{1,0:T(8,128)S(1)} %get-tuple-element.29), channel_id=1, source_target_pairs={{0,4},{4,0},{8,12},{12,8},{16,20},{20,16},{24,28},{28,24},{1,5},{5... | collective-permute-start | bytes 786440 | tf_op jit(solution)/shard_map/ppermute | solution.py:196
  5.1 0.0 collective-permute-start
  5.1 1.2 %collective-permute-done = f32[32,256]{1,0:T(8,128)S(1)} collective-permute-done((f32[32,256]{1,0:T(8,128)S(1)}, f32[32,256]{1,0:T(8,128)S(1)}, u32[]{:S(2)}, u32[]{:S(2)}) %collective-permute-start) | collective-permute-done | bytes 32800 | tf_op jit(solution)/shard_map/ppermute | solution.py:196
  6.3 1.5 %collective-permute-start.1 = (f32[32,256]{1,0:T(8,128)S(1)}, f32[32,256]{1,0:T(8,128)S(1)}, u32[]{:S(2)}, u32[]{:S(2)}) collective-permute-start(f32[32,256]{1,0:T(8,128)S(1)} %add.11), channel_id=1, source_target_pairs={{0,2},{1,3},{2,0},{3,1},{4,6},{5,7},{6,4},{7,5},{8,10},{9,11},{10,... | collective-permute-start | bytes 98312 | tf_op jit(solution)/shard_map/ppermute | solution.py:196
  7.9 2.4 %collective-permute-done.1 = f32[32,256]{1,0:T(8,128)S(1)} collective-permute-done((f32[32,256]{1,0:T(8,128)S(1)}, f32[32,256]{1,0:T(8,128)S(1)}, u32[]{:S(2)}, u32[]{:S(2)}) %collective-permute-start.1) | collective-permute-done | bytes 32800 | tf_op jit(solution)/shard_map/ppermute | solution.py:196
  10.3 2.6 %collective-permute-start.4 = (f32[32,256]{1,0:T(8,128)S(1)}, f32[32,256]{1,0:T(8,128)S(1)}, u32[]{:S(2)}, u32[]{:S(2)}) collective-permute-start(f32[32,256]{1,0:T(8,128)S(1)} %add.12), channel_id=1, source_target_pairs={{0,20},{4,16},{8,28},{12,24},{16,4},{20,0},{24,12},{28,8},{1,21},{... | collective-permute-start | bytes 98312 | tf_op jit(solution)/shard_map/ppermute | solution.py:196
  12.8 0.3 collective-permute-start.3
  13.2 1.5 %collective-permute-start.2 = (f32[32,256]{1,0:T(8,128)S(1)}, f32[32,256]{1,0:T(8,128)S(1)}, u32[]{:S(2)}, u32[]{:S(2)}) collective-permute-start(f32[32,256]{1,0:T(8,128)S(1)} %add.12), channel_id=1, source_target_pairs={{0,4},{4,0},{8,12},{12,8},{16,20},{20,16},{24,28},{28,24},{1,5},{5... | collective-permute-start | bytes 98312 | tf_op jit(solution)/shard_map/ppermute | solution.py:196
  14.6 0.5 collective-permute-start.7
  15.1 0.9 %collective-permute-done.4 = f32[32,256]{1,0:T(8,128)S(1)} collective-permute-done((f32[32,256]{1,0:T(8,128)S(1)}, f32[32,256]{1,0:T(8,128)S(1)}, u32[]{:S(2)}, u32[]{:S(2)}) %collective-permute-start.4) | collective-permute-done | bytes 32800 | tf_op jit(solution)/shard_map/ppermute | solution.py:196
  16.0 1.9 %collective-permute-done.3 = f32[32,256]{1,0:T(8,128)S(1)} collective-permute-done((f32[32,256]{1,0:T(8,128)S(1)}, f32[32,256]{1,0:T(8,128)S(1)}, u32[]{:S(2)}, u32[]{:S(2)}) %collective-permute-start.3) | collective-permute-done | bytes 32800 | tf_op jit(solution)/shard_map/ppermute | solution.py:196
  17.9 0.0 collective-permute-done.2
  17.9 0.0 collective-permute-done.5.refs_1_
  17.9 0.3 collective-permute-start.6
  18.3 2.8 %collective-permute-start.9 = (f32[64,1024]{1,0:T(8,128)S(1)}, f32[64,1024]{1,0:T(8,128)S(1)}, u32[]{:S(2)}, u32[]{:S(2)}) collective-permute-start(f32[64,1024]{1,0:T(8,128)S(1)} %get-tuple-element.33), channel_id=1, source_target_pairs={{0,12},{4,8},{8,4},{12,0},{16,28},{20,24},{24,20},{28,16},{1,13},{... | collective-permute-start | bytes 786440 | tf_op jit(solution)/shard_map/ppermute | solution.py:196
  21.1 5.6 %collective-permute-done.6 = f32[128,256]{1,0:T(8,128)S(1)} collective-permute-done((f32[128,256]{1,0:T(8,128)S(1)}, f32[128,256]{1,0:T(8,128)S(1)}, u32[]{:S(2)}, u32[]{:S(2)}) %collective-permute-start.6) | collective-permute-done | bytes 131104 | tf_op jit(solution)/shard_map/ppermute | solution.py:196
  26.7 0.0 collective-permute-done.7.refs_2_
  26.7 0.1 collective-permute-start.8
  26.8 0.1 pad_add_fusion.index_ref
  26.9 3.6 %collective-permute-done.9.refs_3_ = f32[64,1024]{1,0:T(8,128)S(1)} collective-permute-done((f32[64,1024]{1,0:T(8,128)S(1)}, f32[64,1024]{1,0:T(8,128)S(1)}, u32[]{:S(2)}, u32[]{:S(2)}) %collective-permute-start.9) | collective-permute-done | bytes 262176 | tf_op jit(solution)/shard_map/ppermute | solution.py:196
  30.5 0.0 collective-permute-done.8.theirs_ref
  30.5 2.5 %shard_map.42 = (bf16[256,256]{1,0:T(8,128)(2,1)S(1)}, bf16[256,256]{1,0:T(8,128)(2,1)S(1)}, f32[64,256]{1,0:T(8,128)}) custom-call(s32[2]{0:T(128)S(1)} %pad_add_fusion.index_ref, f32[256,256]{1,0:T(8,128)S(1)} %pad_maximum_fusion.mine_ref, f32[256,256]{1,0:T(8,128)S(1)} %collective-permute-done.8.theirs_ref), custom_call_target="tpu_custom_call" | custom-call | tf_op jit(solution)/shard_map/pallas_call | solution.py:133
  32.9 0.6 shard_map.43
  33.5 0.8 %collective-permute-start.10 = (f32[32,1024]{1,0:T(8,128)S(1)}, f32[32,1024]{1,0:T(8,128)S(1)}, u32[]{:S(2)}, u32[]{:S(2)}) collective-permute-start(f32[32,1024]{1,0:T(8,128)S(1)} %get-tuple-element.44), channel_id=1, source_target_pairs={{0,4},{4,0},{8,12},{12,8},{16,20},{20,16},{24,28},{28,24},{1,5},{5... | collective-permute-start | bytes 393224 | tf_op jit(solution)/shard_map/ppermute | solution.py:196
  34.3 0.8 %collective-permute-start.11 = (f32[32,1024]{1,0:T(8,128)S(1)}, f32[32,1024]{1,0:T(8,128)S(1)}, u32[]{:S(2)}, u32[]{:S(2)}) collective-permute-start(f32[32,1024]{1,0:T(8,128)S(1)} %get-tuple-element.46), channel_id=1, source_target_pairs={{0,8},{4,12},{8,0},{12,4},{16,24},{20,28},{24,16},{28,20},{1,9},{5... | collective-permute-start | bytes 393224 | tf_op jit(solution)/shard_map/ppermute | solution.py:196
  35.1 2.6 %collective-permute-start.13 = (f32[32,1024]{1,0:T(8,128)S(1)}, f32[32,1024]{1,0:T(8,128)S(1)}, u32[]{:S(2)}, u32[]{:S(2)}) collective-permute-start(f32[32,1024]{1,0:T(8,128)S(1)} %get-tuple-element.48), channel_id=1, source_target_pairs={{0,16},{4,20},{8,24},{12,28},{16,0},{20,4},{24,8},{28,12},{1,17},{... | collective-permute-start | bytes 393224 | tf_op jit(solution)/shard_map/ppermute | solution.py:196
  37.7 0.9 %collective-permute-start.14 = (f32[32,1024]{1,0:T(8,128)S(1)}, f32[32,1024]{1,0:T(8,128)S(1)}, u32[]{:S(2)}, u32[]{:S(2)}) collective-permute-start(f32[32,1024]{1,0:T(8,128)S(1)} %get-tuple-element.49), channel_id=1, source_target_pairs={{0,20},{4,16},{8,28},{12,24},{16,4},{20,0},{24,12},{28,8},{1,21},{... | collective-permute-start | bytes 393224 | tf_op jit(solution)/shard_map/ppermute | solution.py:196
  38.7 2.4 %collective-permute-start.15 = (f32[32,1024]{1,0:T(8,128)S(1)}, f32[32,1024]{1,0:T(8,128)S(1)}, u32[]{:S(2)}, u32[]{:S(2)}) collective-permute-start(f32[32,1024]{1,0:T(8,128)S(1)} %get-tuple-element.50), channel_id=1, source_target_pairs={{0,24},{4,28},{8,16},{12,20},{16,8},{20,12},{24,0},{28,4},{1,25},{... | collective-permute-start | bytes 393224 | tf_op jit(solution)/shard_map/ppermute | solution.py:196
  41.1 0.0 collective-permute-done.10.refs_1_
  41.1 0.5 collective-permute-start.16
  41.6 0.0 collective-permute-done.11.refs_2_
  41.6 3.1 %collective-permute-start.12 = (f32[32,1024]{1,0:T(8,128)S(1)}, f32[32,1024]{1,0:T(8,128)S(1)}, u32[]{:S(2)}, u32[]{:S(2)}) collective-permute-start(f32[32,1024]{1,0:T(8,128)S(1)} %get-tuple-element.47), channel_id=1, source_target_pairs={{0,12},{4,8},{8,4},{12,0},{16,28},{20,24},{24,20},{28,16},{1,13},{... | collective-permute-start | bytes 393224 | tf_op jit(solution)/shard_map/ppermute | solution.py:196
  44.7 6.4 %collective-permute-done.13.refs_4_ = f32[32,1024]{1,0:T(8,128)S(1)} collective-permute-done((f32[32,1024]{1,0:T(8,128)S(1)}, f32[32,1024]{1,0:T(8,128)S(1)}, u32[]{:S(2)}, u32[]{:S(2)}) %collective-permute-start.13) | collective-permute-done | bytes 131104 | tf_op jit(solution)/shard_map/ppermute | solution.py:196
  51.2 2.8 %collective-permute-done.14.refs_5_ = f32[32,1024]{1,0:T(8,128)S(1)} collective-permute-done((f32[32,1024]{1,0:T(8,128)S(1)}, f32[32,1024]{1,0:T(8,128)S(1)}, u32[]{:S(2)}, u32[]{:S(2)}) %collective-permute-start.14) | collective-permute-done | bytes 131104 | tf_op jit(solution)/shard_map/ppermute | solution.py:196
  54.0 3.1 %collective-permute-done.15.refs_6_ = f32[32,1024]{1,0:T(8,128)S(1)} collective-permute-done((f32[32,1024]{1,0:T(8,128)S(1)}, f32[32,1024]{1,0:T(8,128)S(1)}, u32[]{:S(2)}, u32[]{:S(2)}) %collective-permute-start.15) | collective-permute-done | bytes 131104 | tf_op jit(solution)/shard_map/ppermute | solution.py:196
  57.0 2.3 %collective-permute-done.16.refs_7_ = f32[32,1024]{1,0:T(8,128)S(1)} collective-permute-done((f32[32,1024]{1,0:T(8,128)S(1)}, f32[32,1024]{1,0:T(8,128)S(1)}, u32[]{:S(2)}, u32[]{:S(2)}) %collective-permute-start.16) | collective-permute-done | bytes 131104 | tf_op jit(solution)/shard_map/ppermute | solution.py:196
  59.4 0.0 collective-permute-done.12.refs_3_
  59.4 0.8 %shard_map.44 = f32[32,4096]{1,0:T(8,128)} custom-call(f32[32,1024]{1,0:T(8,128)S(1)} %get-tuple-element.42.refs_0_, f32[32,1024]{1,0:T(8,128)S(1)} %collective-permute-done.10.refs_1_, f32[32,1024]{1,0:T(8,128)S(1)} %collective-permute-done.11.refs_2_, f32[32,1024]{1,0:T(8,128)S(1)} %collective-permute-done.12.refs_3_, ...), custom_call_target="tpu_custom_call" | custom-call | tf_op jit(solution)/shard_map/pallas_call | solution.py:184
  (4 shorter events, 0.0 us)
Async XLA Ops:
  3.6 14.4 %collective-permute-start.5 = (f32[64,1024]{1,0:T(8,128)S(1)}, f32[64,1024]{1,0:T(8,128)S(1)}, u32[]{:S(2)}, u32[]{:S(2)}) collective-permute-start(f32[64,1024]{1,0:T(8,128)S(1)} %get-tuple-element.29), channel_id=1, source_target_pairs={{0,4},{4,0},{8,12},{12,8},{16,20},{20,16},{24,28},{28,24},{1,5},{5... | collective-permute-start | bytes 786440 | tf_op jit(solution)/shard_map/ppermute | solution.py:196
  5.1 1.2 %collective-permute-start = (f32[32,256]{1,0:T(8,128)S(1)}, f32[32,256]{1,0:T(8,128)S(1)}, u32[]{:S(2)}, u32[]{:S(2)}) collective-permute-start(f32[32,256]{1,0:T(8,128)S(1)} %get-tuple-element.28), channel_id=1, source_target_pairs={{0,1},{1,0},{2,3},{3,2},{4,5},{5,4},{6,7},{7,6},{8,9},{9,8},{10,11... | collective-permute-start | bytes 98312 | tf_op jit(solution)/shard_map/ppermute | solution.py:196
  6.3 3.9 %collective-permute-start.1 = (f32[32,256]{1,0:T(8,128)S(1)}, f32[32,256]{1,0:T(8,128)S(1)}, u32[]{:S(2)}, u32[]{:S(2)}) collective-permute-start(f32[32,256]{1,0:T(8,128)S(1)} %add.11), channel_id=1, source_target_pairs={{0,2},{1,3},{2,0},{3,1},{4,6},{5,7},{6,4},{7,5},{8,10},{9,11},{10,... | collective-permute-start | bytes 98312 | tf_op jit(solution)/shard_map/ppermute | solution.py:196
  10.3 5.7 %collective-permute-start.4 = (f32[32,256]{1,0:T(8,128)S(1)}, f32[32,256]{1,0:T(8,128)S(1)}, u32[]{:S(2)}, u32[]{:S(2)}) collective-permute-start(f32[32,256]{1,0:T(8,128)S(1)} %add.12), channel_id=1, source_target_pairs={{0,20},{4,16},{8,28},{12,24},{16,4},{20,0},{24,12},{28,8},{1,21},{... | collective-permute-start | bytes 98312 | tf_op jit(solution)/shard_map/ppermute | solution.py:196
  12.8 5.1 %collective-permute-start.3 = (f32[32,256]{1,0:T(8,128)S(1)}, f32[32,256]{1,0:T(8,128)S(1)}, u32[]{:S(2)}, u32[]{:S(2)}) collective-permute-start(f32[32,256]{1,0:T(8,128)S(1)} %add.12), channel_id=1, source_target_pairs={{0,16},{4,20},{8,24},{12,28},{16,0},{20,4},{24,8},{28,12},{1,17},{... | collective-permute-start | bytes 98312 | tf_op jit(solution)/shard_map/ppermute | solution.py:196
  13.2 4.8 %collective-permute-start.2 = (f32[32,256]{1,0:T(8,128)S(1)}, f32[32,256]{1,0:T(8,128)S(1)}, u32[]{:S(2)}, u32[]{:S(2)}) collective-permute-start(f32[32,256]{1,0:T(8,128)S(1)} %add.12), channel_id=1, source_target_pairs={{0,4},{4,0},{8,12},{12,8},{16,20},{20,16},{24,28},{28,24},{1,5},{5... | collective-permute-start | bytes 98312 | tf_op jit(solution)/shard_map/ppermute | solution.py:196
  14.6 12.1 %collective-permute-start.7 = (f32[64,1024]{1,0:T(8,128)S(1)}, f32[64,1024]{1,0:T(8,128)S(1)}, u32[]{:S(2)}, u32[]{:S(2)}) collective-permute-start(f32[64,1024]{1,0:T(8,128)S(1)} %get-tuple-element.31), channel_id=1, source_target_pairs={{0,8},{4,12},{8,0},{12,4},{16,24},{20,28},{24,16},{28,20},{1,9},{5... | collective-permute-start | bytes 786440 | tf_op jit(solution)/shard_map/ppermute | solution.py:196
  17.9 8.8 %collective-permute-start.6 = (f32[128,256]{1,0:T(8,128)S(1)}, f32[128,256]{1,0:T(8,128)S(1)}, u32[]{:S(2)}, u32[]{:S(2)}) collective-permute-start(f32[128,256]{1,0:T(8,128)S(1)} %pad_maximum_fusion.1), channel_id=1, source_target_pairs={{0,8},{4,12},{8,0},{12,4},{16,24},{20,28},{24,16},{28,20},{1,9},{5... | collective-permute-start | bytes 393224 | tf_op jit(solution)/shard_map/ppermute | solution.py:196
  18.3 12.2 %collective-permute-start.9 = (f32[64,1024]{1,0:T(8,128)S(1)}, f32[64,1024]{1,0:T(8,128)S(1)}, u32[]{:S(2)}, u32[]{:S(2)}) collective-permute-start(f32[64,1024]{1,0:T(8,128)S(1)} %get-tuple-element.33), channel_id=1, source_target_pairs={{0,12},{4,8},{8,4},{12,0},{16,28},{20,24},{24,20},{28,16},{1,13},{... | collective-permute-start | bytes 786440 | tf_op jit(solution)/shard_map/ppermute | solution.py:196
  26.7 3.7 %collective-permute-start.8 = (f32[256,256]{1,0:T(8,128)S(1)}, f32[256,256]{1,0:T(8,128)S(1)}, u32[]{:S(2)}, u32[]{:S(2)}) collective-permute-start(f32[256,256]{1,0:T(8,128)S(1)} %pad_maximum_fusion.mine_ref), channel_id=1, source_target_pairs={{0,1},{1,0},{2,3},{3,2},{4,5},{5,4},{6,7},{7,6},{8,9},{9,8},{10,11... | collective-permute-start | bytes 786440 | tf_op jit(solution)/shard_map/ppermute | solution.py:196
  33.5 7.5 %collective-permute-start.10 = (f32[32,1024]{1,0:T(8,128)S(1)}, f32[32,1024]{1,0:T(8,128)S(1)}, u32[]{:S(2)}, u32[]{:S(2)}) collective-permute-start(f32[32,1024]{1,0:T(8,128)S(1)} %get-tuple-element.44), channel_id=1, source_target_pairs={{0,4},{4,0},{8,12},{12,8},{16,20},{20,16},{24,28},{28,24},{1,5},{5... | collective-permute-start | bytes 393224 | tf_op jit(solution)/shard_map/ppermute | solution.py:196
  34.3 7.3 %collective-permute-start.11 = (f32[32,1024]{1,0:T(8,128)S(1)}, f32[32,1024]{1,0:T(8,128)S(1)}, u32[]{:S(2)}, u32[]{:S(2)}) collective-permute-start(f32[32,1024]{1,0:T(8,128)S(1)} %get-tuple-element.46), channel_id=1, source_target_pairs={{0,8},{4,12},{8,0},{12,4},{16,24},{20,28},{24,16},{28,20},{1,9},{5... | collective-permute-start | bytes 393224 | tf_op jit(solution)/shard_map/ppermute | solution.py:196
  35.1 16.0 %collective-permute-start.13 = (f32[32,1024]{1,0:T(8,128)S(1)}, f32[32,1024]{1,0:T(8,128)S(1)}, u32[]{:S(2)}, u32[]{:S(2)}) collective-permute-start(f32[32,1024]{1,0:T(8,128)S(1)} %get-tuple-element.48), channel_id=1, source_target_pairs={{0,16},{4,20},{8,24},{12,28},{16,0},{20,4},{24,8},{28,12},{1,17},{... | collective-permute-start | bytes 393224 | tf_op jit(solution)/shard_map/ppermute | solution.py:196
  37.7 16.2 %collective-permute-start.14 = (f32[32,1024]{1,0:T(8,128)S(1)}, f32[32,1024]{1,0:T(8,128)S(1)}, u32[]{:S(2)}, u32[]{:S(2)}) collective-permute-start(f32[32,1024]{1,0:T(8,128)S(1)} %get-tuple-element.49), channel_id=1, source_target_pairs={{0,20},{4,16},{8,28},{12,24},{16,4},{20,0},{24,12},{28,8},{1,21},{... | collective-permute-start | bytes 393224 | tf_op jit(solution)/shard_map/ppermute | solution.py:196
  38.7 18.4 %collective-permute-start.15 = (f32[32,1024]{1,0:T(8,128)S(1)}, f32[32,1024]{1,0:T(8,128)S(1)}, u32[]{:S(2)}, u32[]{:S(2)}) collective-permute-start(f32[32,1024]{1,0:T(8,128)S(1)} %get-tuple-element.50), channel_id=1, source_target_pairs={{0,24},{4,28},{8,16},{12,20},{16,8},{20,12},{24,0},{28,4},{1,25},{... | collective-permute-start | bytes 393224 | tf_op jit(solution)/shard_map/ppermute | solution.py:196
  41.1 18.3 %collective-permute-start.16 = (f32[32,1024]{1,0:T(8,128)S(1)}, f32[32,1024]{1,0:T(8,128)S(1)}, u32[]{:S(2)}, u32[]{:S(2)}) collective-permute-start(f32[32,1024]{1,0:T(8,128)S(1)} %get-tuple-element.51), channel_id=1, source_target_pairs={{0,28},{4,24},{8,20},{12,16},{16,12},{20,8},{24,4},{28,0},{1,29},{... | collective-permute-start | bytes 393224 | tf_op jit(solution)/shard_map/ppermute | solution.py:196
  41.6 17.8 %collective-permute-start.12 = (f32[32,1024]{1,0:T(8,128)S(1)}, f32[32,1024]{1,0:T(8,128)S(1)}, u32[]{:S(2)}, u32[]{:S(2)}) collective-permute-start(f32[32,1024]{1,0:T(8,128)S(1)} %get-tuple-element.47), channel_id=1, source_target_pairs={{0,12},{4,8},{8,4},{12,0},{16,28},{20,24},{24,20},{28,16},{1,13},{... | collective-permute-start | bytes 393224 | tf_op jit(solution)/shard_map/ppermute | solution.py:196

commit v14 on v13

--- a/solution.py
+++ b/solution.py
@@ -214,13 +214,11 @@
     near = group // 2
     order = [k for k in range(times) if k % group < near]
     mine = jnp.concatenate([mine] + [swap(mine, "tm", k) for k in order[1:]], axis=0)
-    mine, parts[1] = lax.optimization_barrier((mine, parts[1]))
+    mine, parts = lax.optimization_barrier((mine, parts))
     for offset in range(near, group, near):
         mine = jnp.concatenate([mine, swap(mine, "tm", offset)], axis=0)
         order = order + [k ^ offset for k in order]
-    mine, parts[2] = lax.optimization_barrier((mine, parts[2]))
-    theirs, parts[3] = lax.optimization_barrier((swap(mine, "space", 1), parts[3]))
-    high_t, low_t, own = mix(jnp.stack([index, core]), mine, theirs, times, group, order)
+    high_t, low_t, own = mix(jnp.stack([index, core]), mine, swap(mine, "space", 1), times, group, order)
 
     blocks = list(load(high_t, low_t, parts, times))
     terms = [blocks[0]] + [None] * (times - 1)

time: 60.4 us -> 62.9 us (1.041)
  waiting for transfers between devices: 30.2 us -> 34 us
  starting transfers between devices: 22.3 us -> 21.1 us
    ppermute x17, waiting for transfers between devices: 30.2 us -> 34 us  [swap(): lax.ppermute(value, axis, [(i, i ^ offset) for i in range(lax.axis_size(a...]
    ppermute x17, starting transfers between devices: 22.3 us -> 21.1 us  [swap(): lax.ppermute(value, axis, [(i, i ^ offset) for i in range(lax.axis_size(a...]
  transfers between devices with their start and end apart: 17 -> 17, of which waited for: 10 -> 12; matrix products, arithmetic and copies ran while one was open for 0% -> 0% of each run, Pallas kernels for 0% -> 0%
where the time goes in v14:
time: 62.9 us; the launch traced here: 62.7 us
  waiting for transfers between devices  34 us (54%)
  starting transfers between devices  21.1 us (34%)
  Pallas kernels  6.81 us (11%)
  between operations  0.73 us (1%)
    ppermute x17, waiting for transfers between devices, swap(): lax.ppermute(value, axis, [(i, i ^ offset) for i in range(lax.axis_size(a...  34 us
    ppermute x17, starting transfers between devices, swap(): lax.ppermute(value, axis, [(i, i ^ offset) for i in range(lax.axis_size(a...  21.1 us
    pallas_call x1, Pallas kernels, project(): pl.pallas_call(functools.partial(project_kernel, depth), in_specs=[HBM, H...  2.93 us
    pallas_call x1, Pallas kernels, mix(): pl.pallas_call(functools.partial(mix_kernel, times, order), in_specs=[SME...  2.46 us
  transfers between devices with their start and end apart: 17, of which 12 were waited for; matrix products, arithmetic and copies ran while one was open for 0% of the time, Pallas kernels for 0%

profile of v14, /device:TPU:8, one launch (start us, length us, event | category | flops | bytes accessed | tf_op | source)
XLA Modules:
  0.0 62.7 jit_solution(1468923593846496007)
XLA Ops:
  0.6 2.9 %shard_map.41 = (f32[32,256]{1,0:T(8,128)S(1)}, f32[32,256]{1,0:T(8,128)S(1)}, f32[64,1024]{1,0:T(8,128)S(1)}, f32[64,1024]{1,0:T(8,128)S(1)}, f32[64,1024]{1,0:T(8,128)S(1)}, /*index=5*/f32[64,1024]{1,0:T(8,128)S(1)}) custom-call(f32[64,4096]{1,0:T(8,128)} %snapshots_ref.1, f32[4096,256]{1,0:T(8,128)} %factor_ref.1), custom_call_target="tpu_custom_call" | custom-call | tf_op jit(solution)/shard_map/pallas_call | solution.py:76
  3.6 1.6 %collective-permute-start.5 = (f32[64,1024]{1,0:T(8,128)S(1)}, f32[64,1024]{1,0:T(8,128)S(1)}, u32[]{:S(2)}, u32[]{:S(2)}) collective-permute-start(f32[64,1024]{1,0:T(8,128)S(1)} %get-tuple-element.29), channel_id=1, source_target_pairs={{0,4},{4,0},{8,12},{12,8},{16,20},{20,16},{24,28},{28,24},{1,5},{5... | collective-permute-start | bytes 786440 | tf_op jit(solution)/shard_map/ppermute | solution.py:196
  5.1 0.5 collective-permute-start.6
  5.6 1.5 %collective-permute-start.7 = (f32[64,1024]{1,0:T(8,128)S(1)}, f32[64,1024]{1,0:T(8,128)S(1)}, u32[]{:S(2)}, u32[]{:S(2)}) collective-permute-start(f32[64,1024]{1,0:T(8,128)S(1)} %get-tuple-element.31), channel_id=1, source_target_pairs={{0,12},{4,8},{8,4},{12,0},{16,28},{20,24},{24,20},{28,16},{1,13},{... | collective-permute-start | bytes 786440 | tf_op jit(solution)/shard_map/ppermute | solution.py:196
  7.1 0.0 collective-permute-start
  7.1 1.2 %collective-permute-done = f32[32,256]{1,0:T(8,128)S(1)} collective-permute-done((f32[32,256]{1,0:T(8,128)S(1)}, f32[32,256]{1,0:T(8,128)S(1)}, u32[]{:S(2)}, u32[]{:S(2)}) %collective-permute-start) | collective-permute-done | bytes 32800 | tf_op jit(solution)/shard_map/ppermute | solution.py:196
  8.3 1.5 %collective-permute-start.1 = (f32[32,256]{1,0:T(8,128)S(1)}, f32[32,256]{1,0:T(8,128)S(1)}, u32[]{:S(2)}, u32[]{:S(2)}) collective-permute-start(f32[32,256]{1,0:T(8,128)S(1)} %add.11), channel_id=1, source_target_pairs={{0,2},{1,3},{2,0},{3,1},{4,6},{5,7},{6,4},{7,5},{8,10},{9,11},{10,... | collective-permute-start | bytes 98312 | tf_op jit(solution)/shard_map/ppermute | solution.py:196
  9.9 2.4 %collective-permute-done.1 = f32[32,256]{1,0:T(8,128)S(1)} collective-permute-done((f32[32,256]{1,0:T(8,128)S(1)}, f32[32,256]{1,0:T(8,128)S(1)}, u32[]{:S(2)}, u32[]{:S(2)}) %collective-permute-start.1) | collective-permute-done | bytes 32800 | tf_op jit(solution)/shard_map/ppermute | solution.py:196
  12.3 3.5 %collective-permute-start.4 = (f32[32,256]{1,0:T(8,128)S(1)}, f32[32,256]{1,0:T(8,128)S(1)}, u32[]{:S(2)}, u32[]{:S(2)}) collective-permute-start(f32[32,256]{1,0:T(8,128)S(1)} %add.12), channel_id=1, source_target_pairs={{0,20},{4,16},{8,28},{12,24},{16,4},{20,0},{24,12},{28,8},{1,21},{... | collective-permute-start | bytes 98312 | tf_op jit(solution)/shard_map/ppermute | solution.py:196
  15.8 0.3 collective-permute-start.3
  16.1 4.4 %collective-permute-done.4 = f32[32,256]{1,0:T(8,128)S(1)} collective-permute-done((f32[32,256]{1,0:T(8,128)S(1)}, f32[32,256]{1,0:T(8,128)S(1)}, u32[]{:S(2)}, u32[]{:S(2)}) %collective-permute-start.4) | collective-permute-done | bytes 32800 | tf_op jit(solution)/shard_map/ppermute | solution.py:196
  20.5 1.5 %collective-permute-start.2 = (f32[32,256]{1,0:T(8,128)S(1)}, f32[32,256]{1,0:T(8,128)S(1)}, u32[]{:S(2)}, u32[]{:S(2)}) collective-permute-start(f32[32,256]{1,0:T(8,128)S(1)} %add.12), channel_id=1, source_target_pairs={{0,4},{4,0},{8,12},{12,8},{16,20},{20,16},{24,28},{28,24},{1,5},{5... | collective-permute-start | bytes 98312 | tf_op jit(solution)/shard_map/ppermute | solution.py:196
  22.0 0.0 collective-permute-done.3
  22.0 2.4 %collective-permute-done.2 = f32[32,256]{1,0:T(8,128)S(1)} collective-permute-done((f32[32,256]{1,0:T(8,128)S(1)}, f32[32,256]{1,0:T(8,128)S(1)}, u32[]{:S(2)}, u32[]{:S(2)}) %collective-permute-start.2) | collective-permute-done | bytes 32800 | tf_op jit(solution)/shard_map/ppermute | solution.py:196
  24.5 0.0 collective-permute-done.5.refs_1_
  24.5 0.0 collective-permute-done.6.refs_2_
  24.5 0.0 collective-permute-done.7.refs_3_
  24.5 0.1 collective-permute-start.8
  24.6 4.9 %collective-permute-done.8 = f32[128,256]{1,0:T(8,128)S(1)} collective-permute-done((f32[128,256]{1,0:T(8,128)S(1)}, f32[128,256]{1,0:T(8,128)S(1)}, u32[]{:S(2)}, u32[]{:S(2)}) %collective-permute-start.8) | collective-permute-done | bytes 131104 | tf_op jit(solution)/shard_map/ppermute | solution.py:196
  29.6 0.1 collective-permute-start.9
  29.6 0.1 pad_add_fusion.index_ref
  29.7 1.4 %collective-permute-done.9.theirs_ref = f32[256,256]{1,0:T(8,128)S(1)} collective-permute-done((f32[256,256]{1,0:T(8,128)S(1)}, f32[256,256]{1,0:T(8,128)S(1)}, u32[]{:S(2)}, u32[]{:S(2)}) %collective-permute-start.9) | collective-permute-done | bytes 262176 | tf_op jit(solution)/shard_map/ppermute | solution.py:196
  31.2 2.5 %shard_map.42 = (bf16[256,256]{1,0:T(8,128)(2,1)S(1)}, bf16[256,256]{1,0:T(8,128)(2,1)S(1)}, f32[64,256]{1,0:T(8,128)}) custom-call(s32[2]{0:T(128)S(1)} %pad_add_fusion.index_ref, f32[256,256]{1,0:T(8,128)S(1)} %constant_dynamic-update-slice_fusion.mine_ref, f32[256,256]{1,0:T(8,128)S(1)} %collective-permute-done.9.theirs_ref), custom_call_target="tpu_custom_call" | custom-call | tf_op jit(solution)/shard_map/pallas_call | solution.py:133
  33.6 0.6 shard_map.43
  34.2 1.6 %collective-permute-start.10 = (f32[32,1024]{1,0:T(8,128)S(1)}, f32[32,1024]{1,0:T(8,128)S(1)}, u32[]{:S(2)}, u32[]{:S(2)}) collective-permute-start(f32[32,1024]{1,0:T(8,128)S(1)} %get-tuple-element.42), channel_id=1, source_target_pairs={{0,4},{4,0},{8,12},{12,8},{16,20},{20,16},{24,28},{28,24},{1,5},{5... | collective-permute-start | bytes 393224 | tf_op jit(solution)/shard_map/ppermute | solution.py:196
  35.8 0.0 collective-permute-start.11
  35.8 2.0 %collective-permute-start.13 = (f32[32,1024]{1,0:T(8,128)S(1)}, f32[32,1024]{1,0:T(8,128)S(1)}, u32[]{:S(2)}, u32[]{:S(2)}) collective-permute-start(f32[32,1024]{1,0:T(8,128)S(1)} %get-tuple-element.46), channel_id=1, source_target_pairs={{0,16},{4,20},{8,24},{12,28},{16,0},{20,4},{24,8},{28,12},{1,17},{... | collective-permute-start | bytes 393224 | tf_op jit(solution)/shard_map/ppermute | solution.py:196
  37.8 0.9 %collective-permute-start.14 = (f32[32,1024]{1,0:T(8,128)S(1)}, f32[32,1024]{1,0:T(8,128)S(1)}, u32[]{:S(2)}, u32[]{:S(2)}) collective-permute-start(f32[32,1024]{1,0:T(8,128)S(1)} %get-tuple-element.47), channel_id=1, source_target_pairs={{0,20},{4,16},{8,28},{12,24},{16,4},{20,0},{24,12},{28,8},{1,21},{... | collective-permute-start | bytes 393224 | tf_op jit(solution)/shard_map/ppermute | solution.py:196
  38.7 1.0 %collective-permute-start.15 = (f32[32,1024]{1,0:T(8,128)S(1)}, f32[32,1024]{1,0:T(8,128)S(1)}, u32[]{:S(2)}, u32[]{:S(2)}) collective-permute-start(f32[32,1024]{1,0:T(8,128)S(1)} %get-tuple-element.48), channel_id=1, source_target_pairs={{0,24},{4,28},{8,16},{12,20},{16,8},{20,12},{24,0},{28,4},{1,25},{... | collective-permute-start | bytes 393224 | tf_op jit(solution)/shard_map/ppermute | solution.py:196
  39.6 0.2 collective-permute-done.10.refs_1_
  39.8 1.8 %collective-permute-start.16 = (f32[32,1024]{1,0:T(8,128)S(1)}, f32[32,1024]{1,0:T(8,128)S(1)}, u32[]{:S(2)}, u32[]{:S(2)}) collective-permute-start(f32[32,1024]{1,0:T(8,128)S(1)} %get-tuple-element.49), channel_id=1, source_target_pairs={{0,28},{4,24},{8,20},{12,16},{16,12},{20,8},{24,4},{28,0},{1,29},{... | collective-permute-start | bytes 393224 | tf_op jit(solution)/shard_map/ppermute | solution.py:196
  41.6 0.5 collective-permute-done.11.refs_2_
  42.1 3.3 %collective-permute-start.12 = (f32[32,1024]{1,0:T(8,128)S(1)}, f32[32,1024]{1,0:T(8,128)S(1)}, u32[]{:S(2)}, u32[]{:S(2)}) collective-permute-start(f32[32,1024]{1,0:T(8,128)S(1)} %get-tuple-element.45), channel_id=1, source_target_pairs={{0,12},{4,8},{8,4},{12,0},{16,28},{20,24},{24,20},{28,16},{1,13},{... | collective-permute-start | bytes 393224 | tf_op jit(solution)/shard_map/ppermute | solution.py:196
  45.4 7.6 %collective-permute-done.13.refs_4_ = f32[32,1024]{1,0:T(8,128)S(1)} collective-permute-done((f32[32,1024]{1,0:T(8,128)S(1)}, f32[32,1024]{1,0:T(8,128)S(1)}, u32[]{:S(2)}, u32[]{:S(2)}) %collective-permute-start.13) | collective-permute-done | bytes 131104 | tf_op jit(solution)/shard_map/ppermute | solution.py:196
  53.0 2.8 %collective-permute-done.14.refs_5_ = f32[32,1024]{1,0:T(8,128)S(1)} collective-permute-done((f32[32,1024]{1,0:T(8,128)S(1)}, f32[32,1024]{1,0:T(8,128)S(1)}, u32[]{:S(2)}, u32[]{:S(2)}) %collective-permute-start.14) | collective-permute-done | bytes 131104 | tf_op jit(solution)/shard_map/ppermute | solution.py:196
  55.8 4.3 %collective-permute-done.15.refs_6_ = f32[32,1024]{1,0:T(8,128)S(1)} collective-permute-done((f32[32,1024]{1,0:T(8,128)S(1)}, f32[32,1024]{1,0:T(8,128)S(1)}, u32[]{:S(2)}, u32[]{:S(2)}) %collective-permute-start.15) | collective-permute-done | bytes 131104 | tf_op jit(solution)/shard_map/ppermute | solution.py:196
  60.1 1.8 %collective-permute-done.16.refs_7_ = f32[32,1024]{1,0:T(8,128)S(1)} collective-permute-done((f32[32,1024]{1,0:T(8,128)S(1)}, f32[32,1024]{1,0:T(8,128)S(1)}, u32[]{:S(2)}, u32[]{:S(2)}) %collective-permute-start.16) | collective-permute-done | bytes 131104 | tf_op jit(solution)/shard_map/ppermute | solution.py:196
  61.9 0.0 collective-permute-done.12.refs_3_
  61.9 0.8 %shard_map.44 = f32[32,4096]{1,0:T(8,128)} custom-call(f32[32,1024]{1,0:T(8,128)S(1)} %get-tuple-element.40.refs_0_, f32[32,1024]{1,0:T(8,128)S(1)} %collective-permute-done.10.refs_1_, f32[32,1024]{1,0:T(8,128)S(1)} %collective-permute-done.11.refs_2_, f32[32,1024]{1,0:T(8,128)S(1)} %collective-permute-done.12.refs_3_, ...), custom_call_target="tpu_custom_call" | custom-call | tf_op jit(solution)/shard_map/pallas_call | solution.py:184
  (5 shorter events, 0.0 us)
Async XLA Ops:
  3.6 20.9 %collective-permute-start.5 = (f32[64,1024]{1,0:T(8,128)S(1)}, f32[64,1024]{1,0:T(8,128)S(1)}, u32[]{:S(2)}, u32[]{:S(2)}) collective-permute-start(f32[64,1024]{1,0:T(8,128)S(1)} %get-tuple-element.29), channel_id=1, source_target_pairs={{0,4},{4,0},{8,12},{12,8},{16,20},{20,16},{24,28},{28,24},{1,5},{5... | collective-permute-start | bytes 786440 | tf_op jit(solution)/shard_map/ppermute | solution.py:196
  5.1 19.4 %collective-permute-start.6 = (f32[64,1024]{1,0:T(8,128)S(1)}, f32[64,1024]{1,0:T(8,128)S(1)}, u32[]{:S(2)}, u32[]{:S(2)}) collective-permute-start(f32[64,1024]{1,0:T(8,128)S(1)} %get-tuple-element.30), channel_id=1, source_target_pairs={{0,8},{4,12},{8,0},{12,4},{16,24},{20,28},{24,16},{28,20},{1,9},{5... | collective-permute-start | bytes 786440 | tf_op jit(solution)/shard_map/ppermute | solution.py:196
  5.6 18.9 %collective-permute-start.7 = (f32[64,1024]{1,0:T(8,128)S(1)}, f32[64,1024]{1,0:T(8,128)S(1)}, u32[]{:S(2)}, u32[]{:S(2)}) collective-permute-start(f32[64,1024]{1,0:T(8,128)S(1)} %get-tuple-element.31), channel_id=1, source_target_pairs={{0,12},{4,8},{8,4},{12,0},{16,28},{20,24},{24,20},{28,16},{1,13},{... | collective-permute-start | bytes 786440 | tf_op jit(solution)/shard_map/ppermute | solution.py:196
  7.1 1.2 %collective-permute-start = (f32[32,256]{1,0:T(8,128)S(1)}, f32[32,256]{1,0:T(8,128)S(1)}, u32[]{:S(2)}, u32[]{:S(2)}) collective-permute-start(f32[32,256]{1,0:T(8,128)S(1)} %get-tuple-element.27), channel_id=1, source_target_pairs={{0,1},{1,0},{2,3},{3,2},{4,5},{5,4},{6,7},{7,6},{8,9},{9,8},{10,11... | collective-permute-start | bytes 98312 | tf_op jit(solution)/shard_map/ppermute | solution.py:196
  8.3 3.9 %collective-permute-start.1 = (f32[32,256]{1,0:T(8,128)S(1)}, f32[32,256]{1,0:T(8,128)S(1)}, u32[]{:S(2)}, u32[]{:S(2)}) collective-permute-start(f32[32,256]{1,0:T(8,128)S(1)} %add.11), channel_id=1, source_target_pairs={{0,2},{1,3},{2,0},{3,1},{4,6},{5,7},{6,4},{7,5},{8,10},{9,11},{10,... | collective-permute-start | bytes 98312 | tf_op jit(solution)/shard_map/ppermute | solution.py:196
  12.3 8.3 %collective-permute-start.4 = (f32[32,256]{1,0:T(8,128)S(1)}, f32[32,256]{1,0:T(8,128)S(1)}, u32[]{:S(2)}, u32[]{:S(2)}) collective-permute-start(f32[32,256]{1,0:T(8,128)S(1)} %add.12), channel_id=1, source_target_pairs={{0,20},{4,16},{8,28},{12,24},{16,4},{20,0},{24,12},{28,8},{1,21},{... | collective-permute-start | bytes 98312 | tf_op jit(solution)/shard_map/ppermute | solution.py:196
  15.8 6.3 %collective-permute-start.3 = (f32[32,256]{1,0:T(8,128)S(1)}, f32[32,256]{1,0:T(8,128)S(1)}, u32[]{:S(2)}, u32[]{:S(2)}) collective-permute-start(f32[32,256]{1,0:T(8,128)S(1)} %add.12), channel_id=1, source_target_pairs={{0,16},{4,20},{8,24},{12,28},{16,0},{20,4},{24,8},{28,12},{1,17},{... | collective-permute-start | bytes 98312 | tf_op jit(solution)/shard_map/ppermute | solution.py:196
  20.5 3.9 %collective-permute-start.2 = (f32[32,256]{1,0:T(8,128)S(1)}, f32[32,256]{1,0:T(8,128)S(1)}, u32[]{:S(2)}, u32[]{:S(2)}) collective-permute-start(f32[32,256]{1,0:T(8,128)S(1)} %add.12), channel_id=1, source_target_pairs={{0,4},{4,0},{8,12},{12,8},{16,20},{20,16},{24,28},{28,24},{1,5},{5... | collective-permute-start | bytes 98312 | tf_op jit(solution)/shard_map/ppermute | solution.py:196
  24.5 5.0 %collective-permute-start.8 = (f32[128,256]{1,0:T(8,128)S(1)}, f32[128,256]{1,0:T(8,128)S(1)}, u32[]{:S(2)}, u32[]{:S(2)}) collective-permute-start(f32[128,256]{1,0:T(8,128)S(1)} %pad_maximum_fusion), channel_id=1, source_target_pairs={{0,8},{4,12},{8,0},{12,4},{16,24},{20,28},{24,16},{28,20},{1,9},{5... | collective-permute-start | bytes 393224 | tf_op jit(solution)/shard_map/ppermute | solution.py:196
  29.6 1.6 %collective-permute-start.9 = (f32[256,256]{1,0:T(8,128)S(1)}, f32[256,256]{1,0:T(8,128)S(1)}, u32[]{:S(2)}, u32[]{:S(2)}) collective-permute-start(f32[256,256]{1,0:T(8,128)S(1)} %constant_dynamic-update-slice_fusion.mine_ref), channel_id=1, source_target_pairs={{0,1},{1,0},{2,3},{3,2},{4,5},{5,4},{6,7},{7,6},{8,9},{9,8},{10,11... | collective-permute-start | bytes 786440 | tf_op jit(solution)/shard_map/ppermute | solution.py:196
  34.2 5.6 %collective-permute-start.10 = (f32[32,1024]{1,0:T(8,128)S(1)}, f32[32,1024]{1,0:T(8,128)S(1)}, u32[]{:S(2)}, u32[]{:S(2)}) collective-permute-start(f32[32,1024]{1,0:T(8,128)S(1)} %get-tuple-element.42), channel_id=1, source_target_pairs={{0,4},{4,0},{8,12},{12,8},{16,20},{20,16},{24,28},{28,24},{1,5},{5... | collective-permute-start | bytes 393224 | tf_op jit(solution)/shard_map/ppermute | solution.py:196
  35.8 6.4 %collective-permute-start.11 = (f32[32,1024]{1,0:T(8,128)S(1)}, f32[32,1024]{1,0:T(8,128)S(1)}, u32[]{:S(2)}, u32[]{:S(2)}) collective-permute-start(f32[32,1024]{1,0:T(8,128)S(1)} %get-tuple-element.44), channel_id=1, source_target_pairs={{0,8},{4,12},{8,0},{12,4},{16,24},{20,28},{24,16},{28,20},{1,9},{5... | collective-permute-start | bytes 393224 | tf_op jit(solution)/shard_map/ppermute | solution.py:196
  35.8 17.3 %collective-permute-start.13 = (f32[32,1024]{1,0:T(8,128)S(1)}, f32[32,1024]{1,0:T(8,128)S(1)}, u32[]{:S(2)}, u32[]{:S(2)}) collective-permute-start(f32[32,1024]{1,0:T(8,128)S(1)} %get-tuple-element.46), channel_id=1, source_target_pairs={{0,16},{4,20},{8,24},{12,28},{16,0},{20,4},{24,8},{28,12},{1,17},{... | collective-permute-start | bytes 393224 | tf_op jit(solution)/shard_map/ppermute | solution.py:196
  37.8 18.0 %collective-permute-start.14 = (f32[32,1024]{1,0:T(8,128)S(1)}, f32[32,1024]{1,0:T(8,128)S(1)}, u32[]{:S(2)}, u32[]{:S(2)}) collective-permute-start(f32[32,1024]{1,0:T(8,128)S(1)} %get-tuple-element.47), channel_id=1, source_target_pairs={{0,20},{4,16},{8,28},{12,24},{16,4},{20,0},{24,12},{28,8},{1,21},{... | collective-permute-start | bytes 393224 | tf_op jit(solution)/shard_map/ppermute | solution.py:196
  38.7 21.4 %collective-permute-start.15 = (f32[32,1024]{1,0:T(8,128)S(1)}, f32[32,1024]{1,0:T(8,128)S(1)}, u32[]{:S(2)}, u32[]{:S(2)}) collective-permute-start(f32[32,1024]{1,0:T(8,128)S(1)} %get-tuple-element.48), channel_id=1, source_target_pairs={{0,24},{4,28},{8,16},{12,20},{16,8},{20,12},{24,0},{28,4},{1,25},{... | collective-permute-start | bytes 393224 | tf_op jit(solution)/shard_map/ppermute | solution.py:196
  39.8 22.1 %collective-permute-start.16 = (f32[32,1024]{1,0:T(8,128)S(1)}, f32[32,1024]{1,0:T(8,128)S(1)}, u32[]{:S(2)}, u32[]{:S(2)}) collective-permute-start(f32[32,1024]{1,0:T(8,128)S(1)} %get-tuple-element.49), channel_id=1, source_target_pairs={{0,28},{4,24},{8,20},{12,16},{16,12},{20,8},{24,4},{28,0},{1,29},{... | collective-permute-start | bytes 393224 | tf_op jit(solution)/shard_map/ppermute | solution.py:196
  42.1 19.7 %collective-permute-start.12 = (f32[32,1024]{1,0:T(8,128)S(1)}, f32[32,1024]{1,0:T(8,128)S(1)}, u32[]{:S(2)}, u32[]{:S(2)}) collective-permute-start(f32[32,1024]{1,0:T(8,128)S(1)} %get-tuple-element.45), channel_id=1, source_target_pairs={{0,12},{4,8},{8,4},{12,0},{16,28},{20,24},{24,20},{28,16},{1,13},{... | collective-permute-start | bytes 393224 | tf_op jit(solution)/shard_map/ppermute | solution.py:196

commit v15 on v14

--- a/solution.py
+++ b/solution.py
@@ -214,11 +214,12 @@
     near = group // 2
     order = [k for k in range(times) if k % group < near]
     mine = jnp.concatenate([mine] + [swap(mine, "tm", k) for k in order[1:]], axis=0)
-    mine, parts = lax.optimization_barrier((mine, parts))
+    mine, *parts[2:] = lax.optimization_barrier((mine, *parts[2:]))
     for offset in range(near, group, near):
         mine = jnp.concatenate([mine, swap(mine, "tm", offset)], axis=0)
         order = order + [k ^ offset for k in order]
-    high_t, low_t, own = mix(jnp.stack([index, core]), mine, swap(mine, "space", 1), times, group, order)
+    theirs, parts[1] = lax.optimization_barrier((swap(mine, "space", 1), parts[1]))
+    high_t, low_t, own = mix(jnp.stack([index, core]), mine, theirs, times, group, order)
 
     blocks = list(load(high_t, low_t, parts, times))
     terms = [blocks[0]] + [None] * (times - 1)

time: 62.9 us -> 58.7 us (0.933)
  waiting for transfers between devices: 34 us -> 29.6 us
    ppermute x17, waiting for transfers between devices: 34 us -> 29.6 us  [swap(): lax.ppermute(value, axis, [(i, i ^ offset) for i in range(lax.axis_size(a...]
  transfers between devices with their start and end apart: 17 -> 17, of which waited for: 12 -> 9; matrix products, arithmetic and copies ran while one was open for 0% -> 0% of each run, Pallas kernels for 0% -> 0%
where the time goes in v15:
time: 58.7 us; the launch traced here: 58.5 us
  waiting for transfers between devices  29.6 us (50%)
  starting transfers between devices  21.3 us (36%)
  Pallas kernels  6.81 us (12%)
  between operations  0.72 us (1%)
    ppermute x17, waiting for transfers between devices, swap(): lax.ppermute(value, axis, [(i, i ^ offset) for i in range(lax.axis_size(a...  29.6 us
    ppermute x17, starting transfers between devices, swap(): lax.ppermute(value, axis, [(i, i ^ offset) for i in range(lax.axis_size(a...  21.3 us
    pallas_call x1, Pallas kernels, project(): pl.pallas_call(functools.partial(project_kernel, depth), in_specs=[HBM, H...  2.93 us
    pallas_call x1, Pallas kernels, mix(): pl.pallas_call(functools.partial(mix_kernel, times, order), in_specs=[SME...  2.46 us
  transfers between devices with their start and end apart: 17, of which 9 were waited for; matrix products, arithmetic and copies ran while one was open for 0% of the time, Pallas kernels for 0%

profile of v15, /device:TPU:8, one launch (start us, length us, event | category | flops | bytes accessed | tf_op | source)
XLA Modules:
  0.0 58.5 jit_solution(17842492653542139067)
XLA Ops:
  0.6 2.9 %shard_map.41 = (f32[32,256]{1,0:T(8,128)S(1)}, f32[32,256]{1,0:T(8,128)S(1)}, f32[64,1024]{1,0:T(8,128)S(1)}, f32[64,1024]{1,0:T(8,128)S(1)}, f32[64,1024]{1,0:T(8,128)S(1)}, /*index=5*/f32[64,1024]{1,0:T(8,128)S(1)}) custom-call(f32[64,4096]{1,0:T(8,128)} %snapshots_ref.1, f32[4096,256]{1,0:T(8,128)} %factor_ref.1), custom_call_target="tpu_custom_call" | custom-call | tf_op jit(solution)/shard_map/pallas_call | solution.py:76
  3.6 0.1 collective-permute-start.5
  3.6 2.9 %collective-permute-start.6 = (f32[64,1024]{1,0:T(8,128)S(1)}, f32[64,1024]{1,0:T(8,128)S(1)}, u32[]{:S(2)}, u32[]{:S(2)}) collective-permute-start(f32[64,1024]{1,0:T(8,128)S(1)} %get-tuple-element.29), channel_id=1, source_target_pairs={{0,12},{4,8},{8,4},{12,0},{16,28},{20,24},{24,20},{28,16},{1,13},{... | collective-permute-start | bytes 786440 | tf_op jit(solution)/shard_map/ppermute | solution.py:196
  6.6 0.0 collective-permute-start
  6.6 1.2 %collective-permute-done = f32[32,256]{1,0:T(8,128)S(1)} collective-permute-done((f32[32,256]{1,0:T(8,128)S(1)}, f32[32,256]{1,0:T(8,128)S(1)}, u32[]{:S(2)}, u32[]{:S(2)}) %collective-permute-start) | collective-permute-done | bytes 32800 | tf_op jit(solution)/shard_map/ppermute | solution.py:196
  7.8 1.5 %collective-permute-start.1 = (f32[32,256]{1,0:T(8,128)S(1)}, f32[32,256]{1,0:T(8,128)S(1)}, u32[]{:S(2)}, u32[]{:S(2)}) collective-permute-start(f32[32,256]{1,0:T(8,128)S(1)} %add.11), channel_id=1, source_target_pairs={{0,2},{1,3},{2,0},{3,1},{4,6},{5,7},{6,4},{7,5},{8,10},{9,11},{10,... | collective-permute-start | bytes 98312 | tf_op jit(solution)/shard_map/ppermute | solution.py:196
  9.3 2.4 %collective-permute-done.1 = f32[32,256]{1,0:T(8,128)S(1)} collective-permute-done((f32[32,256]{1,0:T(8,128)S(1)}, f32[32,256]{1,0:T(8,128)S(1)}, u32[]{:S(2)}, u32[]{:S(2)}) %collective-permute-start.1) | collective-permute-done | bytes 32800 | tf_op jit(solution)/shard_map/ppermute | solution.py:196
  11.7 2.6 %collective-permute-start.4 = (f32[32,256]{1,0:T(8,128)S(1)}, f32[32,256]{1,0:T(8,128)S(1)}, u32[]{:S(2)}, u32[]{:S(2)}) collective-permute-start(f32[32,256]{1,0:T(8,128)S(1)} %add.12), channel_id=1, source_target_pairs={{0,20},{4,16},{8,28},{12,24},{16,4},{20,0},{24,12},{28,8},{1,21},{... | collective-permute-start | bytes 98312 | tf_op jit(solution)/shard_map/ppermute | solution.py:196
  14.3 0.3 collective-permute-start.3
  14.6 1.5 %collective-permute-start.2 = (f32[32,256]{1,0:T(8,128)S(1)}, f32[32,256]{1,0:T(8,128)S(1)}, u32[]{:S(2)}, u32[]{:S(2)}) collective-permute-start(f32[32,256]{1,0:T(8,128)S(1)} %add.12), channel_id=1, source_target_pairs={{0,4},{4,0},{8,12},{12,8},{16,20},{20,16},{24,28},{28,24},{1,5},{5... | collective-permute-start | bytes 98312 | tf_op jit(solution)/shard_map/ppermute | solution.py:196
  16.1 4.2 %collective-permute-done.4 = f32[32,256]{1,0:T(8,128)S(1)} collective-permute-done((f32[32,256]{1,0:T(8,128)S(1)}, f32[32,256]{1,0:T(8,128)S(1)}, u32[]{:S(2)}, u32[]{:S(2)}) %collective-permute-start.4) | collective-permute-done | bytes 32800 | tf_op jit(solution)/shard_map/ppermute | solution.py:196
  20.3 0.0 collective-permute-done.3
  20.3 0.0 collective-permute-done.2
  20.3 0.0 collective-permute-done.5.refs_2_
  20.3 0.0 collective-permute-done.6.refs_3_
  20.3 0.1 collective-permute-start.7
  20.4 1.1 %collective-permute-start.9 = (f32[64,1024]{1,0:T(8,128)S(1)}, f32[64,1024]{1,0:T(8,128)S(1)}, u32[]{:S(2)}, u32[]{:S(2)}) collective-permute-start(f32[64,1024]{1,0:T(8,128)S(1)} %get-tuple-element.31), channel_id=1, source_target_pairs={{0,4},{4,0},{8,12},{12,8},{16,20},{20,16},{24,28},{28,24},{1,5},{5... | collective-permute-start | bytes 786440 | tf_op jit(solution)/shard_map/ppermute | solution.py:196
  21.5 3.9 %collective-permute-done.7 = f32[128,256]{1,0:T(8,128)S(1)} collective-permute-done((f32[128,256]{1,0:T(8,128)S(1)}, f32[128,256]{1,0:T(8,128)S(1)}, u32[]{:S(2)}, u32[]{:S(2)}) %collective-permute-start.7) | collective-permute-done | bytes 131104 | tf_op jit(solution)/shard_map/ppermute | solution.py:196
  25.4 0.1 collective-permute-start.8
  25.5 0.1 pad_add_fusion.index_ref
  25.5 2.4 %collective-permute-done.9.refs_1_ = f32[64,1024]{1,0:T(8,128)S(1)} collective-permute-done((f32[64,1024]{1,0:T(8,128)S(1)}, f32[64,1024]{1,0:T(8,128)S(1)}, u32[]{:S(2)}, u32[]{:S(2)}) %collective-permute-start.9) | collective-permute-done | bytes 262176 | tf_op jit(solution)/shard_map/ppermute | solution.py:196
  28.0 0.0 collective-permute-done.8.theirs_ref
  28.0 2.5 %shard_map.42 = (bf16[256,256]{1,0:T(8,128)(2,1)S(1)}, bf16[256,256]{1,0:T(8,128)(2,1)S(1)}, f32[64,256]{1,0:T(8,128)}) custom-call(s32[2]{0:T(128)S(1)} %pad_add_fusion.index_ref, f32[256,256]{1,0:T(8,128)S(1)} %constant_dynamic-update-slice_fusion.mine_ref, f32[256,256]{1,0:T(8,128)S(1)} %collective-permute-done.8.theirs_ref), custom_call_target="tpu_custom_call" | custom-call | tf_op jit(solution)/shard_map/pallas_call | solution.py:133
  30.4 0.6 %shard_map.43 = (f32[32,1024]{1,0:T(8,128)S(1)}, f32[32,1024]{1,0:T(8,128)S(1)}, f32[32,1024]{1,0:T(8,128)S(1)}, f32[32,1024]{1,0:T(8,128)S(1)}, f32[32,1024]{1,...) custom-call(bf16[256,256]{1,0:T(8,128)(2,1)S(1)} %get-tuple-element.34.high_ref, ...), custom_call_target="tpu_custom_call" | custom-call | tf_op jit(solution)/shard_map/pallas_call | solution.py:155
  31.0 0.3 collective-permute-start.10
  31.4 1.7 %collective-permute-start.11 = (f32[32,1024]{1,0:T(8,128)S(1)}, f32[32,1024]{1,0:T(8,128)S(1)}, u32[]{:S(2)}, u32[]{:S(2)}) collective-permute-start(f32[32,1024]{1,0:T(8,128)S(1)} %get-tuple-element.44), channel_id=1, source_target_pairs={{0,8},{4,12},{8,0},{12,4},{16,24},{20,28},{24,16},{28,20},{1,9},{5... | collective-permute-start | bytes 393224 | tf_op jit(solution)/shard_map/ppermute | solution.py:196
  33.1 1.8 %collective-permute-start.13 = (f32[32,1024]{1,0:T(8,128)S(1)}, f32[32,1024]{1,0:T(8,128)S(1)}, u32[]{:S(2)}, u32[]{:S(2)}) collective-permute-start(f32[32,1024]{1,0:T(8,128)S(1)} %get-tuple-element.46), channel_id=1, source_target_pairs={{0,16},{4,20},{8,24},{12,28},{16,0},{20,4},{24,8},{28,12},{1,17},{... | collective-permute-start | bytes 393224 | tf_op jit(solution)/shard_map/ppermute | solution.py:196
  34.9 1.5 %collective-permute-start.14 = (f32[32,1024]{1,0:T(8,128)S(1)}, f32[32,1024]{1,0:T(8,128)S(1)}, u32[]{:S(2)}, u32[]{:S(2)}) collective-permute-start(f32[32,1024]{1,0:T(8,128)S(1)} %get-tuple-element.47), channel_id=1, source_target_pairs={{0,20},{4,16},{8,28},{12,24},{16,4},{20,0},{24,12},{28,8},{1,21},{... | collective-permute-start | bytes 393224 | tf_op jit(solution)/shard_map/ppermute | solution.py:196
  36.4 2.3 %collective-permute-start.15 = (f32[32,1024]{1,0:T(8,128)S(1)}, f32[32,1024]{1,0:T(8,128)S(1)}, u32[]{:S(2)}, u32[]{:S(2)}) collective-permute-start(f32[32,1024]{1,0:T(8,128)S(1)} %get-tuple-element.48), channel_id=1, source_target_pairs={{0,24},{4,28},{8,16},{12,20},{16,8},{20,12},{24,0},{28,4},{1,25},{... | collective-permute-start | bytes 393224 | tf_op jit(solution)/shard_map/ppermute | solution.py:196
  38.7 0.0 collective-permute-done.10.refs_1_
  38.7 0.2 collective-permute-start.16
  38.9 0.0 collective-permute-done.11.refs_2_
  38.9 3.3 %collective-permute-start.12 = (f32[32,1024]{1,0:T(8,128)S(1)}, f32[32,1024]{1,0:T(8,128)S(1)}, u32[]{:S(2)}, u32[]{:S(2)}) collective-permute-start(f32[32,1024]{1,0:T(8,128)S(1)} %get-tuple-element.45), channel_id=1, source_target_pairs={{0,12},{4,8},{8,4},{12,0},{16,28},{20,24},{24,20},{28,16},{1,13},{... | collective-permute-start | bytes 393224 | tf_op jit(solution)/shard_map/ppermute | solution.py:196
  42.3 6.9 %collective-permute-done.13.refs_4_ = f32[32,1024]{1,0:T(8,128)S(1)} collective-permute-done((f32[32,1024]{1,0:T(8,128)S(1)}, f32[32,1024]{1,0:T(8,128)S(1)}, u32[]{:S(2)}, u32[]{:S(2)}) %collective-permute-start.13) | collective-permute-done | bytes 131104 | tf_op jit(solution)/shard_map/ppermute | solution.py:196
  49.2 2.8 %collective-permute-done.14.refs_5_ = f32[32,1024]{1,0:T(8,128)S(1)} collective-permute-done((f32[32,1024]{1,0:T(8,128)S(1)}, f32[32,1024]{1,0:T(8,128)S(1)}, u32[]{:S(2)}, u32[]{:S(2)}) %collective-permute-start.14) | collective-permute-done | bytes 131104 | tf_op jit(solution)/shard_map/ppermute | solution.py:196
  52.0 2.9 %collective-permute-done.15.refs_6_ = f32[32,1024]{1,0:T(8,128)S(1)} collective-permute-done((f32[32,1024]{1,0:T(8,128)S(1)}, f32[32,1024]{1,0:T(8,128)S(1)}, u32[]{:S(2)}, u32[]{:S(2)}) %collective-permute-start.15) | collective-permute-done | bytes 131104 | tf_op jit(solution)/shard_map/ppermute | solution.py:196
  54.9 2.8 %collective-permute-done.16.refs_7_ = f32[32,1024]{1,0:T(8,128)S(1)} collective-permute-done((f32[32,1024]{1,0:T(8,128)S(1)}, f32[32,1024]{1,0:T(8,128)S(1)}, u32[]{:S(2)}, u32[]{:S(2)}) %collective-permute-start.16) | collective-permute-done | bytes 131104 | tf_op jit(solution)/shard_map/ppermute | solution.py:196
  57.7 0.0 collective-permute-done.12.refs_3_
  57.7 0.8 %shard_map.44 = f32[32,4096]{1,0:T(8,128)} custom-call(f32[32,1024]{1,0:T(8,128)S(1)} %get-tuple-element.40.refs_0_, f32[32,1024]{1,0:T(8,128)S(1)} %collective-permute-done.10.refs_1_, f32[32,1024]{1,0:T(8,128)S(1)} %collective-permute-done.11.refs_2_, f32[32,1024]{1,0:T(8,128)S(1)} %collective-permute-done.12.refs_3_, ...), custom_call_target="tpu_custom_call" | custom-call | tf_op jit(solution)/shard_map/pallas_call | solution.py:184
  (5 shorter events, 0.0 us)
Async XLA Ops:
  3.6 16.7 %collective-permute-start.5 = (f32[64,1024]{1,0:T(8,128)S(1)}, f32[64,1024]{1,0:T(8,128)S(1)}, u32[]{:S(2)}, u32[]{:S(2)}) collective-permute-start(f32[64,1024]{1,0:T(8,128)S(1)} %get-tuple-element.28), channel_id=1, source_target_pairs={{0,8},{4,12},{8,0},{12,4},{16,24},{20,28},{24,16},{28,20},{1,9},{5... | collective-permute-start | bytes 786440 | tf_op jit(solution)/shard_map/ppermute | solution.py:196
  3.6 16.7 %collective-permute-start.6 = (f32[64,1024]{1,0:T(8,128)S(1)}, f32[64,1024]{1,0:T(8,128)S(1)}, u32[]{:S(2)}, u32[]{:S(2)}) collective-permute-start(f32[64,1024]{1,0:T(8,128)S(1)} %get-tuple-element.29), channel_id=1, source_target_pairs={{0,12},{4,8},{8,4},{12,0},{16,28},{20,24},{24,20},{28,16},{1,13},{... | collective-permute-start | bytes 786440 | tf_op jit(solution)/shard_map/ppermute | solution.py:196
  6.6 1.2 %collective-permute-start = (f32[32,256]{1,0:T(8,128)S(1)}, f32[32,256]{1,0:T(8,128)S(1)}, u32[]{:S(2)}, u32[]{:S(2)}) collective-permute-start(f32[32,256]{1,0:T(8,128)S(1)} %get-tuple-element.27), channel_id=1, source_target_pairs={{0,1},{1,0},{2,3},{3,2},{4,5},{5,4},{6,7},{7,6},{8,9},{9,8},{10,11... | collective-permute-start | bytes 98312 | tf_op jit(solution)/shard_map/ppermute | solution.py:196
  7.8 3.9 %collective-permute-start.1 = (f32[32,256]{1,0:T(8,128)S(1)}, f32[32,256]{1,0:T(8,128)S(1)}, u32[]{:S(2)}, u32[]{:S(2)}) collective-permute-start(f32[32,256]{1,0:T(8,128)S(1)} %add.11), channel_id=1, source_target_pairs={{0,2},{1,3},{2,0},{3,1},{4,6},{5,7},{6,4},{7,5},{8,10},{9,11},{10,... | collective-permute-start | bytes 98312 | tf_op jit(solution)/shard_map/ppermute | solution.py:196
  11.7 8.6 %collective-permute-start.4 = (f32[32,256]{1,0:T(8,128)S(1)}, f32[32,256]{1,0:T(8,128)S(1)}, u32[]{:S(2)}, u32[]{:S(2)}) collective-permute-start(f32[32,256]{1,0:T(8,128)S(1)} %add.12), channel_id=1, source_target_pairs={{0,20},{4,16},{8,28},{12,24},{16,4},{20,0},{24,12},{28,8},{1,21},{... | collective-permute-start | bytes 98312 | tf_op jit(solution)/shard_map/ppermute | solution.py:196
  14.3 6.0 %collective-permute-start.3 = (f32[32,256]{1,0:T(8,128)S(1)}, f32[32,256]{1,0:T(8,128)S(1)}, u32[]{:S(2)}, u32[]{:S(2)}) collective-permute-start(f32[32,256]{1,0:T(8,128)S(1)} %add.12), channel_id=1, source_target_pairs={{0,16},{4,20},{8,24},{12,28},{16,0},{20,4},{24,8},{28,12},{1,17},{... | collective-permute-start | bytes 98312 | tf_op jit(solution)/shard_map/ppermute | solution.py:196
  14.6 5.7 %collective-permute-start.2 = (f32[32,256]{1,0:T(8,128)S(1)}, f32[32,256]{1,0:T(8,128)S(1)}, u32[]{:S(2)}, u32[]{:S(2)}) collective-permute-start(f32[32,256]{1,0:T(8,128)S(1)} %add.12), channel_id=1, source_target_pairs={{0,4},{4,0},{8,12},{12,8},{16,20},{20,16},{24,28},{28,24},{1,5},{5... | collective-permute-start | bytes 98312 | tf_op jit(solution)/shard_map/ppermute | solution.py:196
  20.3 5.0 %collective-permute-start.7 = (f32[128,256]{1,0:T(8,128)S(1)}, f32[128,256]{1,0:T(8,128)S(1)}, u32[]{:S(2)}, u32[]{:S(2)}) collective-permute-start(f32[128,256]{1,0:T(8,128)S(1)} %pad_maximum_fusion), channel_id=1, source_target_pairs={{0,8},{4,12},{8,0},{12,4},{16,24},{20,28},{24,16},{28,20},{1,9},{5... | collective-permute-start | bytes 393224 | tf_op jit(solution)/shard_map/ppermute | solution.py:196
  20.4 7.6 %collective-permute-start.9 = (f32[64,1024]{1,0:T(8,128)S(1)}, f32[64,1024]{1,0:T(8,128)S(1)}, u32[]{:S(2)}, u32[]{:S(2)}) collective-permute-start(f32[64,1024]{1,0:T(8,128)S(1)} %get-tuple-element.31), channel_id=1, source_target_pairs={{0,4},{4,0},{8,12},{12,8},{16,20},{20,16},{24,28},{28,24},{1,5},{5... | collective-permute-start | bytes 786440 | tf_op jit(solution)/shard_map/ppermute | solution.py:196
  25.4 2.6 %collective-permute-start.8 = (f32[256,256]{1,0:T(8,128)S(1)}, f32[256,256]{1,0:T(8,128)S(1)}, u32[]{:S(2)}, u32[]{:S(2)}) collective-permute-start(f32[256,256]{1,0:T(8,128)S(1)} %constant_dynamic-update-slice_fusion.mine_ref), channel_id=1, source_target_pairs={{0,1},{1,0},{2,3},{3,2},{4,5},{5,4},{6,7},{7,6},{8,9},{9,8},{10,11... | collective-permute-start | bytes 786440 | tf_op jit(solution)/shard_map/ppermute | solution.py:196
  31.0 7.6 %collective-permute-start.10 = (f32[32,1024]{1,0:T(8,128)S(1)}, f32[32,1024]{1,0:T(8,128)S(1)}, u32[]{:S(2)}, u32[]{:S(2)}) collective-permute-start(f32[32,1024]{1,0:T(8,128)S(1)} %get-tuple-element.42), channel_id=1, source_target_pairs={{0,4},{4,0},{8,12},{12,8},{16,20},{20,16},{24,28},{28,24},{1,5},{5... | collective-permute-start | bytes 393224 | tf_op jit(solution)/shard_map/ppermute | solution.py:196
  31.4 7.5 %collective-permute-start.11 = (f32[32,1024]{1,0:T(8,128)S(1)}, f32[32,1024]{1,0:T(8,128)S(1)}, u32[]{:S(2)}, u32[]{:S(2)}) collective-permute-start(f32[32,1024]{1,0:T(8,128)S(1)} %get-tuple-element.44), channel_id=1, source_target_pairs={{0,8},{4,12},{8,0},{12,4},{16,24},{20,28},{24,16},{28,20},{1,9},{5... | collective-permute-start | bytes 393224 | tf_op jit(solution)/shard_map/ppermute | solution.py:196
  33.1 16.1 %collective-permute-start.13 = (f32[32,1024]{1,0:T(8,128)S(1)}, f32[32,1024]{1,0:T(8,128)S(1)}, u32[]{:S(2)}, u32[]{:S(2)}) collective-permute-start(f32[32,1024]{1,0:T(8,128)S(1)} %get-tuple-element.46), channel_id=1, source_target_pairs={{0,16},{4,20},{8,24},{12,28},{16,0},{20,4},{24,8},{28,12},{1,17},{... | collective-permute-start | bytes 393224 | tf_op jit(solution)/shard_map/ppermute | solution.py:196
  34.9 17.1 %collective-permute-start.14 = (f32[32,1024]{1,0:T(8,128)S(1)}, f32[32,1024]{1,0:T(8,128)S(1)}, u32[]{:S(2)}, u32[]{:S(2)}) collective-permute-start(f32[32,1024]{1,0:T(8,128)S(1)} %get-tuple-element.47), channel_id=1, source_target_pairs={{0,20},{4,16},{8,28},{12,24},{16,4},{20,0},{24,12},{28,8},{1,21},{... | collective-permute-start | bytes 393224 | tf_op jit(solution)/shard_map/ppermute | solution.py:196
  36.4 18.5 %collective-permute-start.15 = (f32[32,1024]{1,0:T(8,128)S(1)}, f32[32,1024]{1,0:T(8,128)S(1)}, u32[]{:S(2)}, u32[]{:S(2)}) collective-permute-start(f32[32,1024]{1,0:T(8,128)S(1)} %get-tuple-element.48), channel_id=1, source_target_pairs={{0,24},{4,28},{8,16},{12,20},{16,8},{20,12},{24,0},{28,4},{1,25},{... | collective-permute-start | bytes 393224 | tf_op jit(solution)/shard_map/ppermute | solution.py:196
  38.7 19.0 %collective-permute-start.16 = (f32[32,1024]{1,0:T(8,128)S(1)}, f32[32,1024]{1,0:T(8,128)S(1)}, u32[]{:S(2)}, u32[]{:S(2)}) collective-permute-start(f32[32,1024]{1,0:T(8,128)S(1)} %get-tuple-element.49), channel_id=1, source_target_pairs={{0,28},{4,24},{8,20},{12,16},{16,12},{20,8},{24,4},{28,0},{1,29},{... | collective-permute-start | bytes 393224 | tf_op jit(solution)/shard_map/ppermute | solution.py:196
  38.9 18.8 %collective-permute-start.12 = (f32[32,1024]{1,0:T(8,128)S(1)}, f32[32,1024]{1,0:T(8,128)S(1)}, u32[]{:S(2)}, u32[]{:S(2)}) collective-permute-start(f32[32,1024]{1,0:T(8,128)S(1)} %get-tuple-element.45), channel_id=1, source_target_pairs={{0,12},{4,8},{8,4},{12,0},{16,28},{20,24},{24,20},{28,16},{1,13},{... | collective-permute-start | bytes 393224 | tf_op jit(solution)/shard_map/ppermute | solution.py:196

commit v16 on v15

--- a/solution.py
+++ b/solution.py
@@ -115,15 +115,9 @@
     places = [order.index(k) for k in range(group)]
     high = jnp.concatenate([high[i * rows : (i + 1) * rows] for i in places], axis=0)
     low = jnp.concatenate([low[i * rows : (i + 1) * rows] for i in places], axis=0)
-    scale = lax.rsqrt(total)
-    own = product((high[:rows], low[:rows]), (mixing_high, mixing_low))
-    own_ref[...] = own * (scale * math.sqrt(times * rows))
-    width = rank // times
-    source = ((row // width) ^ index_ref[0]) * width + row % width
-    move = jnp.where(source == column, 1.0, 0.0).astype(jnp.bfloat16)
-    moved = dot(move, jnp.concatenate([mixing_high, mixing_low], axis=1)).astype(jnp.bfloat16)
-    turned = product((moved[:, :rank], moved[:, rank:]), (high, low), COLUMNS_BY_COLUMNS) * scale
-    high_t_ref[...], low_t_ref[...] = split(turned)
+    factor = product((high, low), (mixing_high, mixing_low)) * lax.rsqrt(total)
+    own_ref[...] = factor[:rows] * math.sqrt(times * rows)
+    high_t_ref[...], low_t_ref[...] = split(factor.T)
 
 
 def mix(index, mine, theirs, times, group, order):
@@ -140,26 +134,39 @@
     )(index, mine, theirs)
 
 
-def load_kernel(group, high_ref, low_ref, *refs):
+def load_kernel(group, index_ref, high_ref, low_ref, *refs):
     parts, blocks = refs[:group], refs[group:]
+    times = len(blocks)
+    rank = high_ref.shape[0]
+    width = rank // times
+    if width % 16 == 0:
+        starts = [pl.multiple_of((index_ref[0] ^ k) * width, width) for k in range(times)]
+        high, low = [
+            jnp.concatenate([ref[pl.ds(start, width), :] for start in starts], axis=0) for ref in (high_ref, low_ref)
+        ]
+    else:
+        row = lax.broadcasted_iota(jnp.int32, (rank, rank), 0)
+        source = ((row // width) ^ index_ref[0]) * width + row % width
+        column = lax.broadcasted_iota(jnp.int32, row.shape, 1)
+        move = jnp.where(source == column, 1.0, 0.0).astype(jnp.bfloat16)
+        high, low = [dot(move, ref[...]).astype(jnp.bfloat16) for ref in (high_ref, low_ref)]
     columns = jnp.concatenate([part[...] for part in parts], axis=0)
-    value = product((high_ref[...], low_ref[...]), split(columns))
-    width = value.shape[0] // len(blocks)
+    value = product((high, low), split(columns))
     for i, block in enumerate(blocks):
         block[...] = value[i * width : (i + 1) * width]
 
 
-def load(high, low, parts, blocks):
+def load(index, high, low, parts, times):
     rank = high.shape[0]
     columns = parts[0].shape[1]
     return pl.pallas_call(
         functools.partial(load_kernel, len(parts)),
-        in_specs=[VMEM] * (2 + len(parts)),
-        out_specs=[VMEM] * blocks,
-        out_shape=[jax.ShapeDtypeStruct((rank // blocks, columns), jnp.float32)] * blocks,
+        in_specs=[SMEM] + [VMEM] * (2 + len(parts)),
+        out_specs=[VMEM] * times,
+        out_shape=[jax.ShapeDtypeStruct((rank // times, columns), jnp.float32)] * times,
         compiler_params=params(),
         cost_estimate=FREE,
-    )(high, low, *parts)
+    )(index, high, low, *parts)
 
 
 def join_kernel(group, *refs):
@@ -218,10 +225,11 @@
     for offset in range(near, group, near):
         mine = jnp.concatenate([mine, swap(mine, "tm", offset)], axis=0)
         order = order + [k ^ offset for k in order]
-    theirs, parts[1] = lax.optimization_barrier((swap(mine, "space", 1), parts[1]))
+    mine, parts[1] = lax.optimization_barrier((mine, parts[1]))
+    theirs = swap(mine, "space", 1)
     high_t, low_t, own = mix(jnp.stack([index, core]), mine, theirs, times, group, order)
 
-    blocks = list(load(high_t, low_t, parts, times))
+    blocks = list(load(index.reshape(1), high_t, low_t, parts, times))
     terms = [blocks[0]] + [None] * (times - 1)
     for k in [*range(group, times), *range(1, group)]:
         if k == group - 1:

time: 58.7 us -> 60.3 us (1.027)
  waiting for transfers between devices: 29.6 us -> 32.3 us
  starting transfers between devices: 21.3 us -> 20.2 us
    ppermute x17, waiting for transfers between devices: 29.6 us -> 32.3 us  [swap(): lax.ppermute(value, axis, [(i, i ^ offset) for i in range(lax.axis_size(a...]
    ppermute x17, starting transfers between devices: 21.3 us -> 20.2 us  [swap(): lax.ppermute(value, axis, [(i, i ^ offset) for i in range(lax.axis_size(a...]
  transfers between devices with their start and end apart: 17 -> 17, of which waited for: 9 -> 11; matrix products, arithmetic and copies ran while one was open for 0% -> 0% of each run, Pallas kernels for 0% -> 0%
where the time goes in v16:
time: 60.3 us; the launch traced here: 60.2 us
  waiting for transfers between devices  32.3 us (54%)
  starting transfers between devices  20.2 us (33%)
  Pallas kernels  6.88 us (11%)
  between operations  0.7 us (1%)
    ppermute x17, waiting for transfers between devices, swap(): lax.ppermute(value, axis, [(i, i ^ offset) for i in range(lax.axis_size(a...  32.3 us
    ppermute x17, starting transfers between devices, swap(): lax.ppermute(value, axis, [(i, i ^ offset) for i in range(lax.axis_size(a...  20.2 us
    pallas_call x1, Pallas kernels, project(): pl.pallas_call(functools.partial(project_kernel, depth), in_specs=[HBM, H...  2.93 us
    pallas_call x1, Pallas kernels, mix(): pl.pallas_call(functools.partial(mix_kernel, times, order), in_specs=[SME...  2.52 us
  transfers between devices with their start and end apart: 17, of which 11 were waited for; matrix products, arithmetic and copies ran while one was open for 0% of the time, Pallas kernels for 0%

profile of v16, /device:TPU:8, one launch (start us, length us, event | category | flops | bytes accessed | tf_op | source)
XLA Modules:
  0.0 60.2 jit_solution(15575029872230915371)
XLA Ops:
  0.6 2.9 %shard_map.41 = (f32[32,256]{1,0:T(8,128)S(1)}, f32[32,256]{1,0:T(8,128)S(1)}, f32[64,1024]{1,0:T(8,128)S(1)}, f32[64,1024]{1,0:T(8,128)S(1)}, f32[64,1024]{1,0:T(8,128)S(1)}, /*index=5*/f32[64,1024]{1,0:T(8,128)S(1)}) custom-call(f32[64,4096]{1,0:T(8,128)} %snapshots_ref.1, f32[4096,256]{1,0:T(8,128)} %factor_ref.1), custom_call_target="tpu_custom_call" | custom-call | tf_op jit(solution)/shard_map/pallas_call | solution.py:76
  3.6 0.1 collective-permute-start.5
  3.6 2.9 %collective-permute-start.6 = (f32[64,1024]{1,0:T(8,128)S(1)}, f32[64,1024]{1,0:T(8,128)S(1)}, u32[]{:S(2)}, u32[]{:S(2)}) collective-permute-start(f32[64,1024]{1,0:T(8,128)S(1)} %get-tuple-element.29), channel_id=1, source_target_pairs={{0,12},{4,8},{8,4},{12,0},{16,28},{20,24},{24,20},{28,16},{1,13},{... | collective-permute-start | bytes 786440 | tf_op jit(solution)/shard_map/ppermute | solution.py:203
  6.6 0.0 collective-permute-start
  6.6 1.2 %collective-permute-done = f32[32,256]{1,0:T(8,128)S(1)} collective-permute-done((f32[32,256]{1,0:T(8,128)S(1)}, f32[32,256]{1,0:T(8,128)S(1)}, u32[]{:S(2)}, u32[]{:S(2)}) %collective-permute-start) | collective-permute-done | bytes 32800 | tf_op jit(solution)/shard_map/ppermute | solution.py:203
  7.8 1.5 %collective-permute-start.1 = (f32[32,256]{1,0:T(8,128)S(1)}, f32[32,256]{1,0:T(8,128)S(1)}, u32[]{:S(2)}, u32[]{:S(2)}) collective-permute-start(f32[32,256]{1,0:T(8,128)S(1)} %add.11), channel_id=1, source_target_pairs={{0,2},{1,3},{2,0},{3,1},{4,6},{5,7},{6,4},{7,5},{8,10},{9,11},{10,... | collective-permute-start | bytes 98312 | tf_op jit(solution)/shard_map/ppermute | solution.py:203
  9.3 2.4 %collective-permute-done.1 = f32[32,256]{1,0:T(8,128)S(1)} collective-permute-done((f32[32,256]{1,0:T(8,128)S(1)}, f32[32,256]{1,0:T(8,128)S(1)}, u32[]{:S(2)}, u32[]{:S(2)}) %collective-permute-start.1) | collective-permute-done | bytes 32800 | tf_op jit(solution)/shard_map/ppermute | solution.py:203
  11.7 2.6 %collective-permute-start.4 = (f32[32,256]{1,0:T(8,128)S(1)}, f32[32,256]{1,0:T(8,128)S(1)}, u32[]{:S(2)}, u32[]{:S(2)}) collective-permute-start(f32[32,256]{1,0:T(8,128)S(1)} %add.12), channel_id=1, source_target_pairs={{0,20},{4,16},{8,28},{12,24},{16,4},{20,0},{24,12},{28,8},{1,21},{... | collective-permute-start | bytes 98312 | tf_op jit(solution)/shard_map/ppermute | solution.py:203
  14.3 0.3 collective-permute-start.3
  14.6 1.5 %collective-permute-start.2 = (f32[32,256]{1,0:T(8,128)S(1)}, f32[32,256]{1,0:T(8,128)S(1)}, u32[]{:S(2)}, u32[]{:S(2)}) collective-permute-start(f32[32,256]{1,0:T(8,128)S(1)} %add.12), channel_id=1, source_target_pairs={{0,4},{4,0},{8,12},{12,8},{16,20},{20,16},{24,28},{28,24},{1,5},{5... | collective-permute-start | bytes 98312 | tf_op jit(solution)/shard_map/ppermute | solution.py:203
  16.1 4.2 %collective-permute-done.4 = f32[32,256]{1,0:T(8,128)S(1)} collective-permute-done((f32[32,256]{1,0:T(8,128)S(1)}, f32[32,256]{1,0:T(8,128)S(1)}, u32[]{:S(2)}, u32[]{:S(2)}) %collective-permute-start.4) | collective-permute-done | bytes 32800 | tf_op jit(solution)/shard_map/ppermute | solution.py:203
  20.3 0.5 collective-permute-start.8
  20.8 0.0 collective-permute-done.3
  20.8 0.0 collective-permute-done.2
  20.8 0.0 collective-permute-done.5.refs_2_
  20.9 0.0 collective-permute-done.6.refs_3_
  20.9 0.1 collective-permute-start.7
  20.9 5.0 %collective-permute-done.7 = f32[128,256]{1,0:T(8,128)S(1)} collective-permute-done((f32[128,256]{1,0:T(8,128)S(1)}, f32[128,256]{1,0:T(8,128)S(1)}, u32[]{:S(2)}, u32[]{:S(2)}) %collective-permute-start.7) | collective-permute-done | bytes 131104 | tf_op jit(solution)/shard_map/ppermute | solution.py:203
  25.9 1.1 %collective-permute-done.8.refs_1_ = f32[64,1024]{1,0:T(8,128)S(1)} collective-permute-done((f32[64,1024]{1,0:T(8,128)S(1)}, f32[64,1024]{1,0:T(8,128)S(1)}, u32[]{:S(2)}, u32[]{:S(2)}) %collective-permute-start.8) | collective-permute-done | bytes 262176 | tf_op jit(solution)/shard_map/ppermute | solution.py:203
  27.0 0.0 collective-permute-start.9
  27.0 0.1 pad_add_fusion.index_ref
  27.1 1.5 %collective-permute-done.9.theirs_ref = f32[256,256]{1,0:T(8,128)S(1)} collective-permute-done((f32[256,256]{1,0:T(8,128)S(1)}, f32[256,256]{1,0:T(8,128)S(1)}, u32[]{:S(2)}, u32[]{:S(2)}) %collective-permute-start.9) | collective-permute-done | bytes 262176 | tf_op jit(solution)/shard_map/ppermute | solution.py:203
  28.5 2.5 %shard_map.42 = (bf16[256,256]{1,0:T(8,128)(2,1)S(1)}, bf16[256,256]{1,0:T(8,128)(2,1)S(1)}, f32[64,256]{1,0:T(8,128)}) custom-call(s32[2]{0:T(128)S(1)} %pad_add_fusion.index_ref, f32[256,256]{1,0:T(8,128)S(1)} %pad_maximum_fusion.mine_ref, f32[256,256]{1,0:T(8,128)S(1)} %collective-permute-done.9.theirs_ref), custom_call_target="tpu_custom_call" | custom-call | tf_op jit(solution)/shard_map/pallas_call | solution.py:127
  31.1 0.6 shard_map.43
  31.7 0.6 collective-permute-start.10
  32.2 0.0 collective-permute-start.11
  32.2 2.0 %collective-permute-start.13 = (f32[32,1024]{1,0:T(8,128)S(1)}, f32[32,1024]{1,0:T(8,128)S(1)}, u32[]{:S(2)}, u32[]{:S(2)}) collective-permute-start(f32[32,1024]{1,0:T(8,128)S(1)} %get-tuple-element.46), channel_id=1, source_target_pairs={{0,16},{4,20},{8,24},{12,28},{16,0},{20,4},{24,8},{28,12},{1,17},{... | collective-permute-start | bytes 393224 | tf_op jit(solution)/shard_map/ppermute | solution.py:203
  34.3 1.8 %collective-permute-start.14 = (f32[32,1024]{1,0:T(8,128)S(1)}, f32[32,1024]{1,0:T(8,128)S(1)}, u32[]{:S(2)}, u32[]{:S(2)}) collective-permute-start(f32[32,1024]{1,0:T(8,128)S(1)} %get-tuple-element.47), channel_id=1, source_target_pairs={{0,20},{4,16},{8,28},{12,24},{16,4},{20,0},{24,12},{28,8},{1,21},{... | collective-permute-start | bytes 393224 | tf_op jit(solution)/shard_map/ppermute | solution.py:203
  36.1 1.6 %collective-permute-start.15 = (f32[32,1024]{1,0:T(8,128)S(1)}, f32[32,1024]{1,0:T(8,128)S(1)}, u32[]{:S(2)}, u32[]{:S(2)}) collective-permute-start(f32[32,1024]{1,0:T(8,128)S(1)} %get-tuple-element.48), channel_id=1, source_target_pairs={{0,24},{4,28},{8,16},{12,20},{16,8},{20,12},{24,0},{28,4},{1,25},{... | collective-permute-start | bytes 393224 | tf_op jit(solution)/shard_map/ppermute | solution.py:203
  37.7 0.0 collective-permute-done.10.refs_1_
  37.7 0.3 collective-permute-start.16
  38.1 0.5 collective-permute-done.11.refs_2_
  38.6 4.3 %collective-permute-start.12 = (f32[32,1024]{1,0:T(8,128)S(1)}, f32[32,1024]{1,0:T(8,128)S(1)}, u32[]{:S(2)}, u32[]{:S(2)}) collective-permute-start(f32[32,1024]{1,0:T(8,128)S(1)} %get-tuple-element.45), channel_id=1, source_target_pairs={{0,12},{4,8},{8,4},{12,0},{16,28},{20,24},{24,20},{28,16},{1,13},{... | collective-permute-start | bytes 393224 | tf_op jit(solution)/shard_map/ppermute | solution.py:203
  42.9 6.3 %collective-permute-done.13.refs_4_ = f32[32,1024]{1,0:T(8,128)S(1)} collective-permute-done((f32[32,1024]{1,0:T(8,128)S(1)}, f32[32,1024]{1,0:T(8,128)S(1)}, u32[]{:S(2)}, u32[]{:S(2)}) %collective-permute-start.13) | collective-permute-done | bytes 131104 | tf_op jit(solution)/shard_map/ppermute | solution.py:203
  49.2 3.0 %collective-permute-done.14.refs_5_ = f32[32,1024]{1,0:T(8,128)S(1)} collective-permute-done((f32[32,1024]{1,0:T(8,128)S(1)}, f32[32,1024]{1,0:T(8,128)S(1)}, u32[]{:S(2)}, u32[]{:S(2)}) %collective-permute-start.14) | collective-permute-done | bytes 131104 | tf_op jit(solution)/shard_map/ppermute | solution.py:203
  52.1 4.4 %collective-permute-done.15.refs_6_ = f32[32,1024]{1,0:T(8,128)S(1)} collective-permute-done((f32[32,1024]{1,0:T(8,128)S(1)}, f32[32,1024]{1,0:T(8,128)S(1)}, u32[]{:S(2)}, u32[]{:S(2)}) %collective-permute-start.15) | collective-permute-done | bytes 131104 | tf_op jit(solution)/shard_map/ppermute | solution.py:203
  56.6 2.8 %collective-permute-done.16.refs_7_ = f32[32,1024]{1,0:T(8,128)S(1)} collective-permute-done((f32[32,1024]{1,0:T(8,128)S(1)}, f32[32,1024]{1,0:T(8,128)S(1)}, u32[]{:S(2)}, u32[]{:S(2)}) %collective-permute-start.16) | collective-permute-done | bytes 131104 | tf_op jit(solution)/shard_map/ppermute | solution.py:203
  59.3 0.0 collective-permute-done.12.refs_3_
  59.3 0.8 %shard_map.44 = f32[32,4096]{1,0:T(8,128)} custom-call(f32[32,1024]{1,0:T(8,128)S(1)} %get-tuple-element.40.refs_0_, f32[32,1024]{1,0:T(8,128)S(1)} %collective-permute-done.10.refs_1_, f32[32,1024]{1,0:T(8,128)S(1)} %collective-permute-done.11.refs_2_, f32[32,1024]{1,0:T(8,128)S(1)} %collective-permute-done.12.refs_3_, ...), custom_call_target="tpu_custom_call" | custom-call | tf_op jit(solution)/shard_map/pallas_call | solution.py:191
  (4 shorter events, 0.0 us)
Async XLA Ops:
  3.6 17.3 %collective-permute-start.5 = (f32[64,1024]{1,0:T(8,128)S(1)}, f32[64,1024]{1,0:T(8,128)S(1)}, u32[]{:S(2)}, u32[]{:S(2)}) collective-permute-start(f32[64,1024]{1,0:T(8,128)S(1)} %get-tuple-element.28), channel_id=1, source_target_pairs={{0,8},{4,12},{8,0},{12,4},{16,24},{20,28},{24,16},{28,20},{1,9},{5... | collective-permute-start | bytes 786440 | tf_op jit(solution)/shard_map/ppermute | solution.py:203
  3.6 17.2 %collective-permute-start.6 = (f32[64,1024]{1,0:T(8,128)S(1)}, f32[64,1024]{1,0:T(8,128)S(1)}, u32[]{:S(2)}, u32[]{:S(2)}) collective-permute-start(f32[64,1024]{1,0:T(8,128)S(1)} %get-tuple-element.29), channel_id=1, source_target_pairs={{0,12},{4,8},{8,4},{12,0},{16,28},{20,24},{24,20},{28,16},{1,13},{... | collective-permute-start | bytes 786440 | tf_op jit(solution)/shard_map/ppermute | solution.py:203
  6.6 1.2 %collective-permute-start = (f32[32,256]{1,0:T(8,128)S(1)}, f32[32,256]{1,0:T(8,128)S(1)}, u32[]{:S(2)}, u32[]{:S(2)}) collective-permute-start(f32[32,256]{1,0:T(8,128)S(1)} %get-tuple-element.27), channel_id=1, source_target_pairs={{0,1},{1,0},{2,3},{3,2},{4,5},{5,4},{6,7},{7,6},{8,9},{9,8},{10,11... | collective-permute-start | bytes 98312 | tf_op jit(solution)/shard_map/ppermute | solution.py:203
  7.8 3.9 %collective-permute-start.1 = (f32[32,256]{1,0:T(8,128)S(1)}, f32[32,256]{1,0:T(8,128)S(1)}, u32[]{:S(2)}, u32[]{:S(2)}) collective-permute-start(f32[32,256]{1,0:T(8,128)S(1)} %add.11), channel_id=1, source_target_pairs={{0,2},{1,3},{2,0},{3,1},{4,6},{5,7},{6,4},{7,5},{8,10},{9,11},{10,... | collective-permute-start | bytes 98312 | tf_op jit(solution)/shard_map/ppermute | solution.py:203
  11.7 8.6 %collective-permute-start.4 = (f32[32,256]{1,0:T(8,128)S(1)}, f32[32,256]{1,0:T(8,128)S(1)}, u32[]{:S(2)}, u32[]{:S(2)}) collective-permute-start(f32[32,256]{1,0:T(8,128)S(1)} %add.12), channel_id=1, source_target_pairs={{0,20},{4,16},{8,28},{12,24},{16,4},{20,0},{24,12},{28,8},{1,21},{... | collective-permute-start | bytes 98312 | tf_op jit(solution)/shard_map/ppermute | solution.py:203
  14.3 6.5 %collective-permute-start.3 = (f32[32,256]{1,0:T(8,128)S(1)}, f32[32,256]{1,0:T(8,128)S(1)}, u32[]{:S(2)}, u32[]{:S(2)}) collective-permute-start(f32[32,256]{1,0:T(8,128)S(1)} %add.12), channel_id=1, source_target_pairs={{0,16},{4,20},{8,24},{12,28},{16,0},{20,4},{24,8},{28,12},{1,17},{... | collective-permute-start | bytes 98312 | tf_op jit(solution)/shard_map/ppermute | solution.py:203
  14.6 6.2 %collective-permute-start.2 = (f32[32,256]{1,0:T(8,128)S(1)}, f32[32,256]{1,0:T(8,128)S(1)}, u32[]{:S(2)}, u32[]{:S(2)}) collective-permute-start(f32[32,256]{1,0:T(8,128)S(1)} %add.12), channel_id=1, source_target_pairs={{0,4},{4,0},{8,12},{12,8},{16,20},{20,16},{24,28},{28,24},{1,5},{5... | collective-permute-start | bytes 98312 | tf_op jit(solution)/shard_map/ppermute | solution.py:203
  20.3 6.7 %collective-permute-start.8 = (f32[64,1024]{1,0:T(8,128)S(1)}, f32[64,1024]{1,0:T(8,128)S(1)}, u32[]{:S(2)}, u32[]{:S(2)}) collective-permute-start(f32[64,1024]{1,0:T(8,128)S(1)} %get-tuple-element.31), channel_id=1, source_target_pairs={{0,4},{4,0},{8,12},{12,8},{16,20},{20,16},{24,28},{28,24},{1,5},{5... | collective-permute-start | bytes 786440 | tf_op jit(solution)/shard_map/ppermute | solution.py:203
  20.9 5.0 %collective-permute-start.7 = (f32[128,256]{1,0:T(8,128)S(1)}, f32[128,256]{1,0:T(8,128)S(1)}, u32[]{:S(2)}, u32[]{:S(2)}) collective-permute-start(f32[128,256]{1,0:T(8,128)S(1)} %pad_maximum_fusion.1), channel_id=1, source_target_pairs={{0,8},{4,12},{8,0},{12,4},{16,24},{20,28},{24,16},{28,20},{1,9},{5... | collective-permute-start | bytes 393224 | tf_op jit(solution)/shard_map/ppermute | solution.py:203
  27.0 1.5 %collective-permute-start.9 = (f32[256,256]{1,0:T(8,128)S(1)}, f32[256,256]{1,0:T(8,128)S(1)}, u32[]{:S(2)}, u32[]{:S(2)}) collective-permute-start(f32[256,256]{1,0:T(8,128)S(1)} %pad_maximum_fusion.mine_ref), channel_id=1, source_target_pairs={{0,1},{1,0},{2,3},{3,2},{4,5},{5,4},{6,7},{7,6},{8,9},{9,8},{10,11... | collective-permute-start | bytes 786440 | tf_op jit(solution)/shard_map/ppermute | solution.py:203
  31.7 6.1 %collective-permute-start.10 = (f32[32,1024]{1,0:T(8,128)S(1)}, f32[32,1024]{1,0:T(8,128)S(1)}, u32[]{:S(2)}, u32[]{:S(2)}) collective-permute-start(f32[32,1024]{1,0:T(8,128)S(1)} %get-tuple-element.42), channel_id=1, source_target_pairs={{0,4},{4,0},{8,12},{12,8},{16,20},{20,16},{24,28},{28,24},{1,5},{5... | collective-permute-start | bytes 393224 | tf_op jit(solution)/shard_map/ppermute | solution.py:203
  32.2 6.4 %collective-permute-start.11 = (f32[32,1024]{1,0:T(8,128)S(1)}, f32[32,1024]{1,0:T(8,128)S(1)}, u32[]{:S(2)}, u32[]{:S(2)}) collective-permute-start(f32[32,1024]{1,0:T(8,128)S(1)} %get-tuple-element.44), channel_id=1, source_target_pairs={{0,8},{4,12},{8,0},{12,4},{16,24},{20,28},{24,16},{28,20},{1,9},{5... | collective-permute-start | bytes 393224 | tf_op jit(solution)/shard_map/ppermute | solution.py:203
  32.2 17.0 %collective-permute-start.13 = (f32[32,1024]{1,0:T(8,128)S(1)}, f32[32,1024]{1,0:T(8,128)S(1)}, u32[]{:S(2)}, u32[]{:S(2)}) collective-permute-start(f32[32,1024]{1,0:T(8,128)S(1)} %get-tuple-element.46), channel_id=1, source_target_pairs={{0,16},{4,20},{8,24},{12,28},{16,0},{20,4},{24,8},{28,12},{1,17},{... | collective-permute-start | bytes 393224 | tf_op jit(solution)/shard_map/ppermute | solution.py:203
  34.3 17.9 %collective-permute-start.14 = (f32[32,1024]{1,0:T(8,128)S(1)}, f32[32,1024]{1,0:T(8,128)S(1)}, u32[]{:S(2)}, u32[]{:S(2)}) collective-permute-start(f32[32,1024]{1,0:T(8,128)S(1)} %get-tuple-element.47), channel_id=1, source_target_pairs={{0,20},{4,16},{8,28},{12,24},{16,4},{20,0},{24,12},{28,8},{1,21},{... | collective-permute-start | bytes 393224 | tf_op jit(solution)/shard_map/ppermute | solution.py:203
  36.1 20.5 %collective-permute-start.15 = (f32[32,1024]{1,0:T(8,128)S(1)}, f32[32,1024]{1,0:T(8,128)S(1)}, u32[]{:S(2)}, u32[]{:S(2)}) collective-permute-start(f32[32,1024]{1,0:T(8,128)S(1)} %get-tuple-element.48), channel_id=1, source_target_pairs={{0,24},{4,28},{8,16},{12,20},{16,8},{20,12},{24,0},{28,4},{1,25},{... | collective-permute-start | bytes 393224 | tf_op jit(solution)/shard_map/ppermute | solution.py:203
  37.7 21.6 %collective-permute-start.16 = (f32[32,1024]{1,0:T(8,128)S(1)}, f32[32,1024]{1,0:T(8,128)S(1)}, u32[]{:S(2)}, u32[]{:S(2)}) collective-permute-start(f32[32,1024]{1,0:T(8,128)S(1)} %get-tuple-element.49), channel_id=1, source_target_pairs={{0,28},{4,24},{8,20},{12,16},{16,12},{20,8},{24,4},{28,0},{1,29},{... | collective-permute-start | bytes 393224 | tf_op jit(solution)/shard_map/ppermute | solution.py:203
  38.6 20.7 %collective-permute-start.12 = (f32[32,1024]{1,0:T(8,128)S(1)}, f32[32,1024]{1,0:T(8,128)S(1)}, u32[]{:S(2)}, u32[]{:S(2)}) collective-permute-start(f32[32,1024]{1,0:T(8,128)S(1)} %get-tuple-element.45), channel_id=1, source_target_pairs={{0,12},{4,8},{8,4},{12,0},{16,28},{20,24},{24,20},{28,16},{1,13},{... | collective-permute-start | bytes 393224 | tf_op jit(solution)/shard_map/ppermute | solution.py:203

commit v17 on v15

--- a/solution.py
+++ b/solution.py
@@ -207,9 +207,10 @@
     mine, other, parts = project(snapshots, space_factor, group)
     parts = [part if k == 0 else swap(part, "tm", k) for k, part in enumerate(parts)]
 
-    mine = mine + swap(other, "space", 1)
-    for i in range(1, spaces.bit_length() - 1):
-        mine = mine + swap(mine, "space", 1 << i)
+    terms = [mine] + [swap(other if k % 2 else mine, "space", k) for k in range(1, spaces)]
+    while len(terms) > 1:
+        terms = [a + b for a, b in zip(terms[::2], terms[1::2])]
+    mine = terms[0]
 
     near = group // 2
     order = [k for k in range(times) if k % group < near]

time: 58.7 us -> 61.1 us (1.041)
  waiting for transfers between devices: 29.6 us -> 31.3 us
    ppermute x17 -> x18, waiting for transfers between devices: 29.6 us -> 31.3 us  [swap(): lax.ppermute(value, axis, [(i, i ^ offset) for i in range(lax.axis_size(a...]
    ppermute x17 -> x18, starting transfers between devices: 21.3 us -> 21.9 us  [swap(): lax.ppermute(value, axis, [(i, i ^ offset) for i in range(lax.axis_size(a...]
  transfers between devices with their start and end apart: 17 -> 18, of which waited for: 9 -> 7; matrix products, arithmetic and copies ran while one was open for 0% -> 0% of each run, Pallas kernels for 0% -> 0%
where the time goes in v17:
time: 61.1 us; the launch traced here: 60.9 us
  waiting for transfers between devices  31.3 us (51%)
  starting transfers between devices  21.9 us (36%)
  Pallas kernels  6.81 us (11%)
  between operations  0.73 us (1%)
    ppermute x18, waiting for transfers between devices, swap(): lax.ppermute(value, axis, [(i, i ^ offset) for i in range(lax.axis_size(a...  31.3 us
    ppermute x18, starting transfers between devices, swap(): lax.ppermute(value, axis, [(i, i ^ offset) for i in range(lax.axis_size(a...  21.9 us
    pallas_call x1, Pallas kernels, project(): pl.pallas_call(functools.partial(project_kernel, depth), in_specs=[HBM, H...  2.93 us
    pallas_call x1, Pallas kernels, mix(): pl.pallas_call(functools.partial(mix_kernel, times, order), in_specs=[SME...  2.46 us
  transfers between devices with their start and end apart: 18, of which 7 were waited for; matrix products, arithmetic and copies ran while one was open for 0% of the time, Pallas kernels for 0%

profile of v17, /device:TPU:8, one launch (start us, length us, event | category | flops | bytes accessed | tf_op | source)
XLA Modules:
  0.0 60.9 jit_solution(6858124750004424473)
XLA Ops:
  0.6 2.9 %shard_map.41 = (f32[32,256]{1,0:T(8,128)S(1)}, f32[32,256]{1,0:T(8,128)S(1)}, f32[64,1024]{1,0:T(8,128)S(1)}, f32[64,1024]{1,0:T(8,128)S(1)}, f32[64,1024]{1,0:T(8,128)S(1)}, /*index=5*/f32[64,1024]{1,0:T(8,128)S(1)}) custom-call(f32[64,4096]{1,0:T(8,128)} %snapshots_ref.1, f32[4096,256]{1,0:T(8,128)} %factor_ref.1), custom_call_target="tpu_custom_call" | custom-call | tf_op jit(solution)/shard_map/pallas_call | solution.py:76
  3.6 1.6 %collective-permute-start.1 = (f32[32,256]{1,0:T(8,128)S(1)}, f32[32,256]{1,0:T(8,128)S(1)}, u32[]{:S(2)}, u32[]{:S(2)}) collective-permute-start(f32[32,256]{1,0:T(8,128)S(1)} %get-tuple-element.26), channel_id=1, source_target_pairs={{0,2},{1,3},{2,0},{3,1},{4,6},{5,7},{6,4},{7,5},{8,10},{9,11},{10,... | collective-permute-start | bytes 98312 | tf_op jit(solution)/shard_map/ppermute | solution.py:196
  5.1 0.0 collective-permute-start.2
  5.2 0.6 %collective-permute-start = (f32[32,256]{1,0:T(8,128)S(1)}, f32[32,256]{1,0:T(8,128)S(1)}, u32[]{:S(2)}, u32[]{:S(2)}) collective-permute-start(f32[32,256]{1,0:T(8,128)S(1)} %get-tuple-element.27), channel_id=1, source_target_pairs={{0,1},{1,0},{2,3},{3,2},{4,5},{5,4},{6,7},{7,6},{8,9},{9,8},{10,11... | collective-permute-start | bytes 98312 | tf_op jit(solution)/shard_map/ppermute | solution.py:196
  5.8 0.0 collective-permute-start.6
  5.8 2.9 %collective-permute-start.7 = (f32[64,1024]{1,0:T(8,128)S(1)}, f32[64,1024]{1,0:T(8,128)S(1)}, u32[]{:S(2)}, u32[]{:S(2)}) collective-permute-start(f32[64,1024]{1,0:T(8,128)S(1)} %get-tuple-element.29), channel_id=1, source_target_pairs={{0,12},{4,8},{8,4},{12,0},{16,28},{20,24},{24,20},{28,16},{1,13},{... | collective-permute-start | bytes 786440 | tf_op jit(solution)/shard_map/ppermute | solution.py:196
  8.7 0.0 collective-permute-done.1
  8.7 0.0 collective-permute-done.2
  8.7 0.0 collective-permute-done
  8.8 3.4 %collective-permute-start.5 = (f32[32,256]{1,0:T(8,128)S(1)}, f32[32,256]{1,0:T(8,128)S(1)}, u32[]{:S(2)}, u32[]{:S(2)}) collective-permute-start(f32[32,256]{1,0:T(8,128)S(1)} %add_add_fusion), channel_id=1, source_target_pairs={{0,20},{4,16},{8,28},{12,24},{16,4},{20,0},{24,12},{28,8},{1,21},{... | collective-permute-start | bytes 98312 | tf_op jit(solution)/shard_map/ppermute | solution.py:196
  12.2 0.3 collective-permute-start.4
  12.5 0.7 %collective-permute-start.3 = (f32[32,256]{1,0:T(8,128)S(1)}, f32[32,256]{1,0:T(8,128)S(1)}, u32[]{:S(2)}, u32[]{:S(2)}) collective-permute-start(f32[32,256]{1,0:T(8,128)S(1)} %add_add_fusion), channel_id=1, source_target_pairs={{0,4},{4,0},{8,12},{12,8},{16,20},{20,16},{24,28},{28,24},{1,5},{5... | collective-permute-start | bytes 98312 | tf_op jit(solution)/shard_map/ppermute | solution.py:196
  13.2 9.4 %collective-permute-done.5 = f32[32,256]{1,0:T(8,128)S(1)} collective-permute-done((f32[32,256]{1,0:T(8,128)S(1)}, f32[32,256]{1,0:T(8,128)S(1)}, u32[]{:S(2)}, u32[]{:S(2)}) %collective-permute-start.5) | collective-permute-done | bytes 32800 | tf_op jit(solution)/shard_map/ppermute | solution.py:196
  22.6 0.0 collective-permute-done.4
  22.6 0.0 collective-permute-done.3
  22.7 0.0 collective-permute-done.6.refs_2_
  22.7 0.0 collective-permute-done.7.refs_3_
  22.7 0.1 collective-permute-start.8
  22.8 1.0 %collective-permute-start.10 = (f32[64,1024]{1,0:T(8,128)S(1)}, f32[64,1024]{1,0:T(8,128)S(1)}, u32[]{:S(2)}, u32[]{:S(2)}) collective-permute-start(f32[64,1024]{1,0:T(8,128)S(1)} %get-tuple-element.31), channel_id=1, source_target_pairs={{0,4},{4,0},{8,12},{12,8},{16,20},{20,16},{24,28},{28,24},{1,5},{5... | collective-permute-start | bytes 786440 | tf_op jit(solution)/shard_map/ppermute | solution.py:196
  23.8 4.0 %collective-permute-done.8 = f32[128,256]{1,0:T(8,128)S(1)} collective-permute-done((f32[128,256]{1,0:T(8,128)S(1)}, f32[128,256]{1,0:T(8,128)S(1)}, u32[]{:S(2)}, u32[]{:S(2)}) %collective-permute-start.8) | collective-permute-done | bytes 131104 | tf_op jit(solution)/shard_map/ppermute | solution.py:196
  27.7 0.1 collective-permute-start.9
  27.8 0.1 pad_add_fusion.index_ref
  27.9 1.8 %collective-permute-done.10.refs_1_ = f32[64,1024]{1,0:T(8,128)S(1)} collective-permute-done((f32[64,1024]{1,0:T(8,128)S(1)}, f32[64,1024]{1,0:T(8,128)S(1)}, u32[]{:S(2)}, u32[]{:S(2)}) %collective-permute-start.10) | collective-permute-done | bytes 262176 | tf_op jit(solution)/shard_map/ppermute | solution.py:196
  29.7 0.0 collective-permute-done.9.theirs_ref
  29.7 2.5 %shard_map.42 = (bf16[256,256]{1,0:T(8,128)(2,1)S(1)}, bf16[256,256]{1,0:T(8,128)(2,1)S(1)}, f32[64,256]{1,0:T(8,128)}) custom-call(s32[2]{0:T(128)S(1)} %pad_add_fusion.index_ref, f32[256,256]{1,0:T(8,128)S(1)} %constant_dynamic-update-slice_fusion.mine_ref, f32[256,256]{1,0:T(8,128)S(1)} %collective-permute-done.9.theirs_ref), custom_call_target="tpu_custom_call" | custom-call | tf_op jit(solution)/shard_map/pallas_call | solution.py:133
  32.1 0.6 shard_map.43
  32.7 1.2 %collective-permute-start.11 = (f32[32,1024]{1,0:T(8,128)S(1)}, f32[32,1024]{1,0:T(8,128)S(1)}, u32[]{:S(2)}, u32[]{:S(2)}) collective-permute-start(f32[32,1024]{1,0:T(8,128)S(1)} %get-tuple-element.42), channel_id=1, source_target_pairs={{0,4},{4,0},{8,12},{12,8},{16,20},{20,16},{24,28},{28,24},{1,5},{5... | collective-permute-start | bytes 393224 | tf_op jit(solution)/shard_map/ppermute | solution.py:196
  33.9 1.7 %collective-permute-start.12 = (f32[32,1024]{1,0:T(8,128)S(1)}, f32[32,1024]{1,0:T(8,128)S(1)}, u32[]{:S(2)}, u32[]{:S(2)}) collective-permute-start(f32[32,1024]{1,0:T(8,128)S(1)} %get-tuple-element.44), channel_id=1, source_target_pairs={{0,8},{4,12},{8,0},{12,4},{16,24},{20,28},{24,16},{28,20},{1,9},{5... | collective-permute-start | bytes 393224 | tf_op jit(solution)/shard_map/ppermute | solution.py:196
  35.6 1.7 %collective-permute-start.14 = (f32[32,1024]{1,0:T(8,128)S(1)}, f32[32,1024]{1,0:T(8,128)S(1)}, u32[]{:S(2)}, u32[]{:S(2)}) collective-permute-start(f32[32,1024]{1,0:T(8,128)S(1)} %get-tuple-element.46), channel_id=1, source_target_pairs={{0,16},{4,20},{8,24},{12,28},{16,0},{20,4},{24,8},{28,12},{1,17},{... | collective-permute-start | bytes 393224 | tf_op jit(solution)/shard_map/ppermute | solution.py:196
  37.3 1.5 %collective-permute-start.15 = (f32[32,1024]{1,0:T(8,128)S(1)}, f32[32,1024]{1,0:T(8,128)S(1)}, u32[]{:S(2)}, u32[]{:S(2)}) collective-permute-start(f32[32,1024]{1,0:T(8,128)S(1)} %get-tuple-element.47), channel_id=1, source_target_pairs={{0,20},{4,16},{8,28},{12,24},{16,4},{20,0},{24,12},{28,8},{1,21},{... | collective-permute-start | bytes 393224 | tf_op jit(solution)/shard_map/ppermute | solution.py:196
  38.8 1.1 %collective-permute-start.16 = (f32[32,1024]{1,0:T(8,128)S(1)}, f32[32,1024]{1,0:T(8,128)S(1)}, u32[]{:S(2)}, u32[]{:S(2)}) collective-permute-start(f32[32,1024]{1,0:T(8,128)S(1)} %get-tuple-element.48), channel_id=1, source_target_pairs={{0,24},{4,28},{8,16},{12,20},{16,8},{20,12},{24,0},{28,4},{1,25},{... | collective-permute-start | bytes 393224 | tf_op jit(solution)/shard_map/ppermute | solution.py:196
  40.0 0.0 collective-permute-done.11.refs_1_
  40.0 1.5 %collective-permute-start.17 = (f32[32,1024]{1,0:T(8,128)S(1)}, f32[32,1024]{1,0:T(8,128)S(1)}, u32[]{:S(2)}, u32[]{:S(2)}) collective-permute-start(f32[32,1024]{1,0:T(8,128)S(1)} %get-tuple-element.49), channel_id=1, source_target_pairs={{0,28},{4,24},{8,20},{12,16},{16,12},{20,8},{24,4},{28,0},{1,29},{... | collective-permute-start | bytes 393224 | tf_op jit(solution)/shard_map/ppermute | solution.py:196
  41.5 0.0 collective-permute-done.12.refs_2_
  41.5 2.5 %collective-permute-start.13 = (f32[32,1024]{1,0:T(8,128)S(1)}, f32[32,1024]{1,0:T(8,128)S(1)}, u32[]{:S(2)}, u32[]{:S(2)}) collective-permute-start(f32[32,1024]{1,0:T(8,128)S(1)} %get-tuple-element.45), channel_id=1, source_target_pairs={{0,12},{4,8},{8,4},{12,0},{16,28},{20,24},{24,20},{28,16},{1,13},{... | collective-permute-start | bytes 393224 | tf_op jit(solution)/shard_map/ppermute | solution.py:196
  43.9 7.3 %collective-permute-done.14.refs_4_ = f32[32,1024]{1,0:T(8,128)S(1)} collective-permute-done((f32[32,1024]{1,0:T(8,128)S(1)}, f32[32,1024]{1,0:T(8,128)S(1)}, u32[]{:S(2)}, u32[]{:S(2)}) %collective-permute-start.14) | collective-permute-done | bytes 131104 | tf_op jit(solution)/shard_map/ppermute | solution.py:196
  51.3 2.8 %collective-permute-done.15.refs_5_ = f32[32,1024]{1,0:T(8,128)S(1)} collective-permute-done((f32[32,1024]{1,0:T(8,128)S(1)}, f32[32,1024]{1,0:T(8,128)S(1)}, u32[]{:S(2)}, u32[]{:S(2)}) %collective-permute-start.15) | collective-permute-done | bytes 131104 | tf_op jit(solution)/shard_map/ppermute | solution.py:196
  54.1 3.1 %collective-permute-done.16.refs_6_ = f32[32,1024]{1,0:T(8,128)S(1)} collective-permute-done((f32[32,1024]{1,0:T(8,128)S(1)}, f32[32,1024]{1,0:T(8,128)S(1)}, u32[]{:S(2)}, u32[]{:S(2)}) %collective-permute-start.16) | collective-permute-done | bytes 131104 | tf_op jit(solution)/shard_map/ppermute | solution.py:196
  57.2 2.9 %collective-permute-done.17.refs_7_ = f32[32,1024]{1,0:T(8,128)S(1)} collective-permute-done((f32[32,1024]{1,0:T(8,128)S(1)}, f32[32,1024]{1,0:T(8,128)S(1)}, u32[]{:S(2)}, u32[]{:S(2)}) %collective-permute-start.17) | collective-permute-done | bytes 131104 | tf_op jit(solution)/shard_map/ppermute | solution.py:196
  60.1 0.0 collective-permute-done.13.refs_3_
  60.1 0.8 %shard_map.44 = f32[32,4096]{1,0:T(8,128)} custom-call(f32[32,1024]{1,0:T(8,128)S(1)} %get-tuple-element.40.refs_0_, f32[32,1024]{1,0:T(8,128)S(1)} %collective-permute-done.11.refs_1_, f32[32,1024]{1,0:T(8,128)S(1)} %collective-permute-done.12.refs_2_, f32[32,1024]{1,0:T(8,128)S(1)} %collective-permute-done.13.refs_3_, ...), custom_call_target="tpu_custom_call" | custom-call | tf_op jit(solution)/shard_map/pallas_call | solution.py:184
  (4 shorter events, 0.0 us)
Async XLA Ops:
  3.6 5.2 %collective-permute-start.1 = (f32[32,256]{1,0:T(8,128)S(1)}, f32[32,256]{1,0:T(8,128)S(1)}, u32[]{:S(2)}, u32[]{:S(2)}) collective-permute-start(f32[32,256]{1,0:T(8,128)S(1)} %get-tuple-element.26), channel_id=1, source_target_pairs={{0,2},{1,3},{2,0},{3,1},{4,6},{5,7},{6,4},{7,5},{8,10},{9,11},{10,... | collective-permute-start | bytes 98312 | tf_op jit(solution)/shard_map/ppermute | solution.py:196
  5.1 3.6 %collective-permute-start.2 = (f32[32,256]{1,0:T(8,128)S(1)}, f32[32,256]{1,0:T(8,128)S(1)}, u32[]{:S(2)}, u32[]{:S(2)}) collective-permute-start(f32[32,256]{1,0:T(8,128)S(1)} %get-tuple-element.27), channel_id=1, source_target_pairs={{0,3},{1,2},{2,1},{3,0},{4,7},{5,6},{6,5},{7,4},{8,11},{9,10},{10,... | collective-permute-start | bytes 98312 | tf_op jit(solution)/shard_map/ppermute | solution.py:196
  5.2 3.6 %collective-permute-start = (f32[32,256]{1,0:T(8,128)S(1)}, f32[32,256]{1,0:T(8,128)S(1)}, u32[]{:S(2)}, u32[]{:S(2)}) collective-permute-start(f32[32,256]{1,0:T(8,128)S(1)} %get-tuple-element.27), channel_id=1, source_target_pairs={{0,1},{1,0},{2,3},{3,2},{4,5},{5,4},{6,7},{7,6},{8,9},{9,8},{10,11... | collective-permute-start | bytes 98312 | tf_op jit(solution)/shard_map/ppermute | solution.py:196
  5.8 16.9 %collective-permute-start.6 = (f32[64,1024]{1,0:T(8,128)S(1)}, f32[64,1024]{1,0:T(8,128)S(1)}, u32[]{:S(2)}, u32[]{:S(2)}) collective-permute-start(f32[64,1024]{1,0:T(8,128)S(1)} %get-tuple-element.28), channel_id=1, source_target_pairs={{0,8},{4,12},{8,0},{12,4},{16,24},{20,28},{24,16},{28,20},{1,9},{5... | collective-permute-start | bytes 786440 | tf_op jit(solution)/shard_map/ppermute | solution.py:196
  5.8 16.9 %collective-permute-start.7 = (f32[64,1024]{1,0:T(8,128)S(1)}, f32[64,1024]{1,0:T(8,128)S(1)}, u32[]{:S(2)}, u32[]{:S(2)}) collective-permute-start(f32[64,1024]{1,0:T(8,128)S(1)} %get-tuple-element.29), channel_id=1, source_target_pairs={{0,12},{4,8},{8,4},{12,0},{16,28},{20,24},{24,20},{28,16},{1,13},{... | collective-permute-start | bytes 786440 | tf_op jit(solution)/shard_map/ppermute | solution.py:196
  8.8 13.9 %collective-permute-start.5 = (f32[32,256]{1,0:T(8,128)S(1)}, f32[32,256]{1,0:T(8,128)S(1)}, u32[]{:S(2)}, u32[]{:S(2)}) collective-permute-start(f32[32,256]{1,0:T(8,128)S(1)} %add_add_fusion), channel_id=1, source_target_pairs={{0,20},{4,16},{8,28},{12,24},{16,4},{20,0},{24,12},{28,8},{1,21},{... | collective-permute-start | bytes 98312 | tf_op jit(solution)/shard_map/ppermute | solution.py:196
  12.2 10.5 %collective-permute-start.4 = (f32[32,256]{1,0:T(8,128)S(1)}, f32[32,256]{1,0:T(8,128)S(1)}, u32[]{:S(2)}, u32[]{:S(2)}) collective-permute-start(f32[32,256]{1,0:T(8,128)S(1)} %add_add_fusion), channel_id=1, source_target_pairs={{0,16},{4,20},{8,24},{12,28},{16,0},{20,4},{24,8},{28,12},{1,17},{... | collective-permute-start | bytes 98312 | tf_op jit(solution)/shard_map/ppermute | solution.py:196
  12.5 10.1 %collective-permute-start.3 = (f32[32,256]{1,0:T(8,128)S(1)}, f32[32,256]{1,0:T(8,128)S(1)}, u32[]{:S(2)}, u32[]{:S(2)}) collective-permute-start(f32[32,256]{1,0:T(8,128)S(1)} %add_add_fusion), channel_id=1, source_target_pairs={{0,4},{4,0},{8,12},{12,8},{16,20},{20,16},{24,28},{28,24},{1,5},{5... | collective-permute-start | bytes 98312 | tf_op jit(solution)/shard_map/ppermute | solution.py:196
  22.7 5.0 %collective-permute-start.8 = (f32[128,256]{1,0:T(8,128)S(1)}, f32[128,256]{1,0:T(8,128)S(1)}, u32[]{:S(2)}, u32[]{:S(2)}) collective-permute-start(f32[128,256]{1,0:T(8,128)S(1)} %pad_maximum_fusion), channel_id=1, source_target_pairs={{0,8},{4,12},{8,0},{12,4},{16,24},{20,28},{24,16},{28,20},{1,9},{5... | collective-permute-start | bytes 393224 | tf_op jit(solution)/shard_map/ppermute | solution.py:196
  22.8 6.9 %collective-permute-start.10 = (f32[64,1024]{1,0:T(8,128)S(1)}, f32[64,1024]{1,0:T(8,128)S(1)}, u32[]{:S(2)}, u32[]{:S(2)}) collective-permute-start(f32[64,1024]{1,0:T(8,128)S(1)} %get-tuple-element.31), channel_id=1, source_target_pairs={{0,4},{4,0},{8,12},{12,8},{16,20},{20,16},{24,28},{28,24},{1,5},{5... | collective-permute-start | bytes 786440 | tf_op jit(solution)/shard_map/ppermute | solution.py:196
  27.7 1.9 %collective-permute-start.9 = (f32[256,256]{1,0:T(8,128)S(1)}, f32[256,256]{1,0:T(8,128)S(1)}, u32[]{:S(2)}, u32[]{:S(2)}) collective-permute-start(f32[256,256]{1,0:T(8,128)S(1)} %constant_dynamic-update-slice_fusion.mine_ref), channel_id=1, source_target_pairs={{0,1},{1,0},{2,3},{3,2},{4,5},{5,4},{6,7},{7,6},{8,9},{9,8},{10,11... | collective-permute-start | bytes 786440 | tf_op jit(solution)/shard_map/ppermute | solution.py:196
  32.7 7.3 %collective-permute-start.11 = (f32[32,1024]{1,0:T(8,128)S(1)}, f32[32,1024]{1,0:T(8,128)S(1)}, u32[]{:S(2)}, u32[]{:S(2)}) collective-permute-start(f32[32,1024]{1,0:T(8,128)S(1)} %get-tuple-element.42), channel_id=1, source_target_pairs={{0,4},{4,0},{8,12},{12,8},{16,20},{20,16},{24,28},{28,24},{1,5},{5... | collective-permute-start | bytes 393224 | tf_op jit(solution)/shard_map/ppermute | solution.py:196
  33.9 7.5 %collective-permute-start.12 = (f32[32,1024]{1,0:T(8,128)S(1)}, f32[32,1024]{1,0:T(8,128)S(1)}, u32[]{:S(2)}, u32[]{:S(2)}) collective-permute-start(f32[32,1024]{1,0:T(8,128)S(1)} %get-tuple-element.44), channel_id=1, source_target_pairs={{0,8},{4,12},{8,0},{12,4},{16,24},{20,28},{24,16},{28,20},{1,9},{5... | collective-permute-start | bytes 393224 | tf_op jit(solution)/shard_map/ppermute | solution.py:196
  35.6 15.7 %collective-permute-start.14 = (f32[32,1024]{1,0:T(8,128)S(1)}, f32[32,1024]{1,0:T(8,128)S(1)}, u32[]{:S(2)}, u32[]{:S(2)}) collective-permute-start(f32[32,1024]{1,0:T(8,128)S(1)} %get-tuple-element.46), channel_id=1, source_target_pairs={{0,16},{4,20},{8,24},{12,28},{16,0},{20,4},{24,8},{28,12},{1,17},{... | collective-permute-start | bytes 393224 | tf_op jit(solution)/shard_map/ppermute | solution.py:196
  37.3 16.8 %collective-permute-start.15 = (f32[32,1024]{1,0:T(8,128)S(1)}, f32[32,1024]{1,0:T(8,128)S(1)}, u32[]{:S(2)}, u32[]{:S(2)}) collective-permute-start(f32[32,1024]{1,0:T(8,128)S(1)} %get-tuple-element.47), channel_id=1, source_target_pairs={{0,20},{4,16},{8,28},{12,24},{16,4},{20,0},{24,12},{28,8},{1,21},{... | collective-permute-start | bytes 393224 | tf_op jit(solution)/shard_map/ppermute | solution.py:196
  38.8 18.4 %collective-permute-start.16 = (f32[32,1024]{1,0:T(8,128)S(1)}, f32[32,1024]{1,0:T(8,128)S(1)}, u32[]{:S(2)}, u32[]{:S(2)}) collective-permute-start(f32[32,1024]{1,0:T(8,128)S(1)} %get-tuple-element.48), channel_id=1, source_target_pairs={{0,24},{4,28},{8,16},{12,20},{16,8},{20,12},{24,0},{28,4},{1,25},{... | collective-permute-start | bytes 393224 | tf_op jit(solution)/shard_map/ppermute | solution.py:196
  40.0 20.1 %collective-permute-start.17 = (f32[32,1024]{1,0:T(8,128)S(1)}, f32[32,1024]{1,0:T(8,128)S(1)}, u32[]{:S(2)}, u32[]{:S(2)}) collective-permute-start(f32[32,1024]{1,0:T(8,128)S(1)} %get-tuple-element.49), channel_id=1, source_target_pairs={{0,28},{4,24},{8,20},{12,16},{16,12},{20,8},{24,4},{28,0},{1,29},{... | collective-permute-start | bytes 393224 | tf_op jit(solution)/shard_map/ppermute | solution.py:196
  41.5 18.6 %collective-permute-start.13 = (f32[32,1024]{1,0:T(8,128)S(1)}, f32[32,1024]{1,0:T(8,128)S(1)}, u32[]{:S(2)}, u32[]{:S(2)}) collective-permute-start(f32[32,1024]{1,0:T(8,128)S(1)} %get-tuple-element.45), channel_id=1, source_target_pairs={{0,12},{4,8},{8,4},{12,0},{16,28},{20,24},{24,20},{28,16},{1,13},{... | collective-permute-start | bytes 393224 | tf_op jit(solution)/shard_map/ppermute | solution.py:196

commit v18 on v17

--- a/solution.py
+++ b/solution.py
@@ -215,10 +215,11 @@
     near = group // 2
     order = [k for k in range(times) if k % group < near]
     mine = jnp.concatenate([mine] + [swap(mine, "tm", k) for k in order[1:]], axis=0)
-    mine, *parts[2:] = lax.optimization_barrier((mine, *parts[2:]))
+    mine, parts[2] = lax.optimization_barrier((mine, parts[2]))
     for offset in range(near, group, near):
         mine = jnp.concatenate([mine, swap(mine, "tm", offset)], axis=0)
         order = order + [k ^ offset for k in order]
+    mine, parts[3] = lax.optimization_barrier((mine, parts[3]))
     theirs, parts[1] = lax.optimization_barrier((swap(mine, "space", 1), parts[1]))
     high_t, low_t, own = mix(jnp.stack([index, core]), mine, theirs, times, group, order)
 

time: 61.1 us -> 59.3 us (0.971)
  starting transfers between devices: 21.9 us -> 20.5 us
    ppermute x18, starting transfers between devices: 21.9 us -> 20.5 us  [swap(): lax.ppermute(value, axis, [(i, i ^ offset) for i in range(lax.axis_size(a...]
  transfers between devices with their start and end apart: 18 -> 18, of which waited for: 7 -> 9; matrix products, arithmetic and copies ran while one was open for 0% -> 0% of each run, Pallas kernels for 0% -> 0%
where the time goes in v18:
time: 59.3 us; the launch traced here: 59 us
  waiting for transfers between devices  30.9 us (52%)
  starting transfers between devices  20.5 us (35%)
  Pallas kernels  6.81 us (11%)
  between operations  0.71 us (1%)
    ppermute x18, waiting for transfers between devices, swap(): lax.ppermute(value, axis, [(i, i ^ offset) for i in range(lax.axis_size(a...  30.9 us
    ppermute x18, starting transfers between devices, swap(): lax.ppermute(value, axis, [(i, i ^ offset) for i in range(lax.axis_size(a...  20.5 us
    pallas_call x1, Pallas kernels, project(): pl.pallas_call(functools.partial(project_kernel, depth), in_specs=[HBM, H...  2.93 us
    pallas_call x1, Pallas kernels, mix(): pl.pallas_call(functools.partial(mix_kernel, times, order), in_specs=[SME...  2.46 us
  transfers between devices with their start and end apart: 18, of which 9 were waited for; matrix products, arithmetic and copies ran while one was open for 0% of the time, Pallas kernels for 0%

profile of v18, /device:TPU:8, one launch (start us, length us, event | category | flops | bytes accessed | tf_op | source)
XLA Modules:
  0.0 59.0 jit_solution(16674912475235409316)
XLA Ops:
  0.6 2.9 %shard_map.41 = (f32[32,256]{1,0:T(8,128)S(1)}, f32[32,256]{1,0:T(8,128)S(1)}, f32[64,1024]{1,0:T(8,128)S(1)}, f32[64,1024]{1,0:T(8,128)S(1)}, f32[64,1024]{1,0:T(8,128)S(1)}, /*index=5*/f32[64,1024]{1,0:T(8,128)S(1)}) custom-call(f32[64,4096]{1,0:T(8,128)} %snapshots_ref.1, f32[4096,256]{1,0:T(8,128)} %factor_ref.1), custom_call_target="tpu_custom_call" | custom-call | tf_op jit(solution)/shard_map/pallas_call | solution.py:76
  3.6 1.6 %collective-permute-start.1 = (f32[32,256]{1,0:T(8,128)S(1)}, f32[32,256]{1,0:T(8,128)S(1)}, u32[]{:S(2)}, u32[]{:S(2)}) collective-permute-start(f32[32,256]{1,0:T(8,128)S(1)} %get-tuple-element.27), channel_id=1, source_target_pairs={{0,2},{1,3},{2,0},{3,1},{4,6},{5,7},{6,4},{7,5},{8,10},{9,11},{10,... | collective-permute-start | bytes 98312 | tf_op jit(solution)/shard_map/ppermute | solution.py:196
  5.1 0.0 collective-permute-start.2
  5.2 0.6 %collective-permute-start = (f32[32,256]{1,0:T(8,128)S(1)}, f32[32,256]{1,0:T(8,128)S(1)}, u32[]{:S(2)}, u32[]{:S(2)}) collective-permute-start(f32[32,256]{1,0:T(8,128)S(1)} %get-tuple-element.28), channel_id=1, source_target_pairs={{0,1},{1,0},{2,3},{3,2},{4,5},{5,4},{6,7},{7,6},{8,9},{9,8},{10,11... | collective-permute-start | bytes 98312 | tf_op jit(solution)/shard_map/ppermute | solution.py:196
  5.8 0.0 collective-permute-start.6
  5.8 1.8 %collective-permute-done.1 = f32[32,256]{1,0:T(8,128)S(1)} collective-permute-done((f32[32,256]{1,0:T(8,128)S(1)}, f32[32,256]{1,0:T(8,128)S(1)}, u32[]{:S(2)}, u32[]{:S(2)}) %collective-permute-start.1) | collective-permute-done | bytes 32800 | tf_op jit(solution)/shard_map/ppermute | solution.py:196
  7.5 1.0 %collective-permute-done.2 = f32[32,256]{1,0:T(8,128)S(1)} collective-permute-done((f32[32,256]{1,0:T(8,128)S(1)}, f32[32,256]{1,0:T(8,128)S(1)}, u32[]{:S(2)}, u32[]{:S(2)}) %collective-permute-start.2) | collective-permute-done | bytes 32800 | tf_op jit(solution)/shard_map/ppermute | solution.py:196
  8.6 0.0 collective-permute-done
  8.6 3.6 %collective-permute-start.5 = (f32[32,256]{1,0:T(8,128)S(1)}, f32[32,256]{1,0:T(8,128)S(1)}, u32[]{:S(2)}, u32[]{:S(2)}) collective-permute-start(f32[32,256]{1,0:T(8,128)S(1)} %add_add_fusion), channel_id=1, source_target_pairs={{0,20},{4,16},{8,28},{12,24},{16,4},{20,0},{24,12},{28,8},{1,21},{... | collective-permute-start | bytes 98312 | tf_op jit(solution)/shard_map/ppermute | solution.py:196
  12.2 0.3 collective-permute-start.4
  12.5 0.5 collective-permute-start.3
  13.0 1.4 %collective-permute-start.8 = (f32[64,1024]{1,0:T(8,128)S(1)}, f32[64,1024]{1,0:T(8,128)S(1)}, u32[]{:S(2)}, u32[]{:S(2)}) collective-permute-start(f32[64,1024]{1,0:T(8,128)S(1)} %get-tuple-element.31), channel_id=1, source_target_pairs={{0,12},{4,8},{8,4},{12,0},{16,28},{20,24},{24,20},{28,16},{1,13},{... | collective-permute-start | bytes 786440 | tf_op jit(solution)/shard_map/ppermute | solution.py:196
  14.4 3.2 %collective-permute-done.5 = f32[32,256]{1,0:T(8,128)S(1)} collective-permute-done((f32[32,256]{1,0:T(8,128)S(1)}, f32[32,256]{1,0:T(8,128)S(1)}, u32[]{:S(2)}, u32[]{:S(2)}) %collective-permute-start.5) | collective-permute-done | bytes 32800 | tf_op jit(solution)/shard_map/ppermute | solution.py:196
  17.6 0.0 collective-permute-done.4
  17.6 0.0 collective-permute-done.3
  17.6 0.0 collective-permute-done.6.refs_2_
  17.6 0.5 collective-permute-start.7
  18.1 0.7 %collective-permute-start.10 = (f32[64,1024]{1,0:T(8,128)S(1)}, f32[64,1024]{1,0:T(8,128)S(1)}, u32[]{:S(2)}, u32[]{:S(2)}) collective-permute-start(f32[64,1024]{1,0:T(8,128)S(1)} %get-tuple-element.33), channel_id=1, source_target_pairs={{0,4},{4,0},{8,12},{12,8},{16,20},{20,16},{24,28},{28,24},{1,5},{5... | collective-permute-start | bytes 786440 | tf_op jit(solution)/shard_map/ppermute | solution.py:196
  18.8 5.5 %collective-permute-done.7 = f32[128,256]{1,0:T(8,128)S(1)} collective-permute-done((f32[128,256]{1,0:T(8,128)S(1)}, f32[128,256]{1,0:T(8,128)S(1)}, u32[]{:S(2)}, u32[]{:S(2)}) %collective-permute-start.7) | collective-permute-done | bytes 131104 | tf_op jit(solution)/shard_map/ppermute | solution.py:196
  24.3 0.0 collective-permute-done.8.refs_3_
  24.3 0.1 collective-permute-start.9
  24.4 0.1 pad_add_fusion.index_ref
  24.5 3.3 %collective-permute-done.10.refs_1_ = f32[64,1024]{1,0:T(8,128)S(1)} collective-permute-done((f32[64,1024]{1,0:T(8,128)S(1)}, f32[64,1024]{1,0:T(8,128)S(1)}, u32[]{:S(2)}, u32[]{:S(2)}) %collective-permute-start.10) | collective-permute-done | bytes 262176 | tf_op jit(solution)/shard_map/ppermute | solution.py:196
  27.8 0.0 collective-permute-done.9.theirs_ref
  27.8 2.5 %shard_map.42 = (bf16[256,256]{1,0:T(8,128)(2,1)S(1)}, bf16[256,256]{1,0:T(8,128)(2,1)S(1)}, f32[64,256]{1,0:T(8,128)}) custom-call(s32[2]{0:T(128)S(1)} %pad_add_fusion.index_ref, f32[256,256]{1,0:T(8,128)S(1)} %pad_maximum_fusion.mine_ref, f32[256,256]{1,0:T(8,128)S(1)} %collective-permute-done.9.theirs_ref), custom_call_target="tpu_custom_call" | custom-call | tf_op jit(solution)/shard_map/pallas_call | solution.py:133
  30.3 0.6 shard_map.43
  30.9 0.8 %collective-permute-start.11 = (f32[32,1024]{1,0:T(8,128)S(1)}, f32[32,1024]{1,0:T(8,128)S(1)}, u32[]{:S(2)}, u32[]{:S(2)}) collective-permute-start(f32[32,1024]{1,0:T(8,128)S(1)} %get-tuple-element.44), channel_id=1, source_target_pairs={{0,4},{4,0},{8,12},{12,8},{16,20},{20,16},{24,28},{28,24},{1,5},{5... | collective-permute-start | bytes 393224 | tf_op jit(solution)/shard_map/ppermute | solution.py:196
  31.7 0.7 %collective-permute-start.12 = (f32[32,1024]{1,0:T(8,128)S(1)}, f32[32,1024]{1,0:T(8,128)S(1)}, u32[]{:S(2)}, u32[]{:S(2)}) collective-permute-start(f32[32,1024]{1,0:T(8,128)S(1)} %get-tuple-element.46), channel_id=1, source_target_pairs={{0,8},{4,12},{8,0},{12,4},{16,24},{20,28},{24,16},{28,20},{1,9},{5... | collective-permute-start | bytes 393224 | tf_op jit(solution)/shard_map/ppermute | solution.py:196
  32.4 2.4 %collective-permute-start.14 = (f32[32,1024]{1,0:T(8,128)S(1)}, f32[32,1024]{1,0:T(8,128)S(1)}, u32[]{:S(2)}, u32[]{:S(2)}) collective-permute-start(f32[32,1024]{1,0:T(8,128)S(1)} %get-tuple-element.48), channel_id=1, source_target_pairs={{0,16},{4,20},{8,24},{12,28},{16,0},{20,4},{24,8},{28,12},{1,17},{... | collective-permute-start | bytes 393224 | tf_op jit(solution)/shard_map/ppermute | solution.py:196
  34.8 0.7 %collective-permute-start.15 = (f32[32,1024]{1,0:T(8,128)S(1)}, f32[32,1024]{1,0:T(8,128)S(1)}, u32[]{:S(2)}, u32[]{:S(2)}) collective-permute-start(f32[32,1024]{1,0:T(8,128)S(1)} %get-tuple-element.49), channel_id=1, source_target_pairs={{0,20},{4,16},{8,28},{12,24},{16,4},{20,0},{24,12},{28,8},{1,21},{... | collective-permute-start | bytes 393224 | tf_op jit(solution)/shard_map/ppermute | solution.py:196
  35.5 2.7 %collective-permute-start.16 = (f32[32,1024]{1,0:T(8,128)S(1)}, f32[32,1024]{1,0:T(8,128)S(1)}, u32[]{:S(2)}, u32[]{:S(2)}) collective-permute-start(f32[32,1024]{1,0:T(8,128)S(1)} %get-tuple-element.50), channel_id=1, source_target_pairs={{0,24},{4,28},{8,16},{12,20},{16,8},{20,12},{24,0},{28,4},{1,25},{... | collective-permute-start | bytes 393224 | tf_op jit(solution)/shard_map/ppermute | solution.py:196
  38.2 0.0 collective-permute-done.11.refs_1_
  38.2 0.3 collective-permute-start.17
  38.5 0.0 collective-permute-done.12.refs_2_
  38.5 3.6 %collective-permute-start.13 = (f32[32,1024]{1,0:T(8,128)S(1)}, f32[32,1024]{1,0:T(8,128)S(1)}, u32[]{:S(2)}, u32[]{:S(2)}) collective-permute-start(f32[32,1024]{1,0:T(8,128)S(1)} %get-tuple-element.47), channel_id=1, source_target_pairs={{0,12},{4,8},{8,4},{12,0},{16,28},{20,24},{24,20},{28,16},{1,13},{... | collective-permute-start | bytes 393224 | tf_op jit(solution)/shard_map/ppermute | solution.py:196
  42.1 7.5 %collective-permute-done.14.refs_4_ = f32[32,1024]{1,0:T(8,128)S(1)} collective-permute-done((f32[32,1024]{1,0:T(8,128)S(1)}, f32[32,1024]{1,0:T(8,128)S(1)}, u32[]{:S(2)}, u32[]{:S(2)}) %collective-permute-start.14) | collective-permute-done | bytes 131104 | tf_op jit(solution)/shard_map/ppermute | solution.py:196
  49.5 2.8 %collective-permute-done.15.refs_5_ = f32[32,1024]{1,0:T(8,128)S(1)} collective-permute-done((f32[32,1024]{1,0:T(8,128)S(1)}, f32[32,1024]{1,0:T(8,128)S(1)}, u32[]{:S(2)}, u32[]{:S(2)}) %collective-permute-start.15) | collective-permute-done | bytes 131104 | tf_op jit(solution)/shard_map/ppermute | solution.py:196
  52.3 3.1 %collective-permute-done.16.refs_6_ = f32[32,1024]{1,0:T(8,128)S(1)} collective-permute-done((f32[32,1024]{1,0:T(8,128)S(1)}, f32[32,1024]{1,0:T(8,128)S(1)}, u32[]{:S(2)}, u32[]{:S(2)}) %collective-permute-start.16) | collective-permute-done | bytes 131104 | tf_op jit(solution)/shard_map/ppermute | solution.py:196
  55.5 2.7 %collective-permute-done.17.refs_7_ = f32[32,1024]{1,0:T(8,128)S(1)} collective-permute-done((f32[32,1024]{1,0:T(8,128)S(1)}, f32[32,1024]{1,0:T(8,128)S(1)}, u32[]{:S(2)}, u32[]{:S(2)}) %collective-permute-start.17) | collective-permute-done | bytes 131104 | tf_op jit(solution)/shard_map/ppermute | solution.py:196
  58.2 0.0 collective-permute-done.13.refs_3_
  58.2 0.8 %shard_map.44 = f32[32,4096]{1,0:T(8,128)} custom-call(f32[32,1024]{1,0:T(8,128)S(1)} %get-tuple-element.42.refs_0_, f32[32,1024]{1,0:T(8,128)S(1)} %collective-permute-done.11.refs_1_, f32[32,1024]{1,0:T(8,128)S(1)} %collective-permute-done.12.refs_2_, f32[32,1024]{1,0:T(8,128)S(1)} %collective-permute-done.13.refs_3_, ...), custom_call_target="tpu_custom_call" | custom-call | tf_op jit(solution)/shard_map/pallas_call | solution.py:184
  (3 shorter events, 0.0 us)
Async XLA Ops:
  3.6 4.0 %collective-permute-start.1 = (f32[32,256]{1,0:T(8,128)S(1)}, f32[32,256]{1,0:T(8,128)S(1)}, u32[]{:S(2)}, u32[]{:S(2)}) collective-permute-start(f32[32,256]{1,0:T(8,128)S(1)} %get-tuple-element.27), channel_id=1, source_target_pairs={{0,2},{1,3},{2,0},{3,1},{4,6},{5,7},{6,4},{7,5},{8,10},{9,11},{10,... | collective-permute-start | bytes 98312 | tf_op jit(solution)/shard_map/ppermute | solution.py:196
  5.1 3.4 %collective-permute-start.2 = (f32[32,256]{1,0:T(8,128)S(1)}, f32[32,256]{1,0:T(8,128)S(1)}, u32[]{:S(2)}, u32[]{:S(2)}) collective-permute-start(f32[32,256]{1,0:T(8,128)S(1)} %get-tuple-element.28), channel_id=1, source_target_pairs={{0,3},{1,2},{2,1},{3,0},{4,7},{5,6},{6,5},{7,4},{8,11},{9,10},{10,... | collective-permute-start | bytes 98312 | tf_op jit(solution)/shard_map/ppermute | solution.py:196
  5.2 3.4 %collective-permute-start = (f32[32,256]{1,0:T(8,128)S(1)}, f32[32,256]{1,0:T(8,128)S(1)}, u32[]{:S(2)}, u32[]{:S(2)}) collective-permute-start(f32[32,256]{1,0:T(8,128)S(1)} %get-tuple-element.28), channel_id=1, source_target_pairs={{0,1},{1,0},{2,3},{3,2},{4,5},{5,4},{6,7},{7,6},{8,9},{9,8},{10,11... | collective-permute-start | bytes 98312 | tf_op jit(solution)/shard_map/ppermute | solution.py:196
  5.8 11.8 %collective-permute-start.6 = (f32[64,1024]{1,0:T(8,128)S(1)}, f32[64,1024]{1,0:T(8,128)S(1)}, u32[]{:S(2)}, u32[]{:S(2)}) collective-permute-start(f32[64,1024]{1,0:T(8,128)S(1)} %get-tuple-element.29), channel_id=1, source_target_pairs={{0,8},{4,12},{8,0},{12,4},{16,24},{20,28},{24,16},{28,20},{1,9},{5... | collective-permute-start | bytes 786440 | tf_op jit(solution)/shard_map/ppermute | solution.py:196
  8.6 9.0 %collective-permute-start.5 = (f32[32,256]{1,0:T(8,128)S(1)}, f32[32,256]{1,0:T(8,128)S(1)}, u32[]{:S(2)}, u32[]{:S(2)}) collective-permute-start(f32[32,256]{1,0:T(8,128)S(1)} %add_add_fusion), channel_id=1, source_target_pairs={{0,20},{4,16},{8,28},{12,24},{16,4},{20,0},{24,12},{28,8},{1,21},{... | collective-permute-start | bytes 98312 | tf_op jit(solution)/shard_map/ppermute | solution.py:196
  12.2 5.4 %collective-permute-start.4 = (f32[32,256]{1,0:T(8,128)S(1)}, f32[32,256]{1,0:T(8,128)S(1)}, u32[]{:S(2)}, u32[]{:S(2)}) collective-permute-start(f32[32,256]{1,0:T(8,128)S(1)} %add_add_fusion), channel_id=1, source_target_pairs={{0,16},{4,20},{8,24},{12,28},{16,0},{20,4},{24,8},{28,12},{1,17},{... | collective-permute-start | bytes 98312 | tf_op jit(solution)/shard_map/ppermute | solution.py:196
  12.5 5.1 %collective-permute-start.3 = (f32[32,256]{1,0:T(8,128)S(1)}, f32[32,256]{1,0:T(8,128)S(1)}, u32[]{:S(2)}, u32[]{:S(2)}) collective-permute-start(f32[32,256]{1,0:T(8,128)S(1)} %add_add_fusion), channel_id=1, source_target_pairs={{0,4},{4,0},{8,12},{12,8},{16,20},{20,16},{24,28},{28,24},{1,5},{5... | collective-permute-start | bytes 98312 | tf_op jit(solution)/shard_map/ppermute | solution.py:196
  13.0 11.2 %collective-permute-start.8 = (f32[64,1024]{1,0:T(8,128)S(1)}, f32[64,1024]{1,0:T(8,128)S(1)}, u32[]{:S(2)}, u32[]{:S(2)}) collective-permute-start(f32[64,1024]{1,0:T(8,128)S(1)} %get-tuple-element.31), channel_id=1, source_target_pairs={{0,12},{4,8},{8,4},{12,0},{16,28},{20,24},{24,20},{28,16},{1,13},{... | collective-permute-start | bytes 786440 | tf_op jit(solution)/shard_map/ppermute | solution.py:196
  17.6 6.6 %collective-permute-start.7 = (f32[128,256]{1,0:T(8,128)S(1)}, f32[128,256]{1,0:T(8,128)S(1)}, u32[]{:S(2)}, u32[]{:S(2)}) collective-permute-start(f32[128,256]{1,0:T(8,128)S(1)} %pad_maximum_fusion.1), channel_id=1, source_target_pairs={{0,8},{4,12},{8,0},{12,4},{16,24},{20,28},{24,16},{28,20},{1,9},{5... | collective-permute-start | bytes 393224 | tf_op jit(solution)/shard_map/ppermute | solution.py:196
  18.1 9.7 %collective-permute-start.10 = (f32[64,1024]{1,0:T(8,128)S(1)}, f32[64,1024]{1,0:T(8,128)S(1)}, u32[]{:S(2)}, u32[]{:S(2)}) collective-permute-start(f32[64,1024]{1,0:T(8,128)S(1)} %get-tuple-element.33), channel_id=1, source_target_pairs={{0,4},{4,0},{8,12},{12,8},{16,20},{20,16},{24,28},{28,24},{1,5},{5... | collective-permute-start | bytes 786440 | tf_op jit(solution)/shard_map/ppermute | solution.py:196
  24.3 3.5 %collective-permute-start.9 = (f32[256,256]{1,0:T(8,128)S(1)}, f32[256,256]{1,0:T(8,128)S(1)}, u32[]{:S(2)}, u32[]{:S(2)}) collective-permute-start(f32[256,256]{1,0:T(8,128)S(1)} %pad_maximum_fusion.mine_ref), channel_id=1, source_target_pairs={{0,1},{1,0},{2,3},{3,2},{4,5},{5,4},{6,7},{7,6},{8,9},{9,8},{10,11... | collective-permute-start | bytes 786440 | tf_op jit(solution)/shard_map/ppermute | solution.py:196
  30.9 7.4 %collective-permute-start.11 = (f32[32,1024]{1,0:T(8,128)S(1)}, f32[32,1024]{1,0:T(8,128)S(1)}, u32[]{:S(2)}, u32[]{:S(2)}) collective-permute-start(f32[32,1024]{1,0:T(8,128)S(1)} %get-tuple-element.44), channel_id=1, source_target_pairs={{0,4},{4,0},{8,12},{12,8},{16,20},{20,16},{24,28},{28,24},{1,5},{5... | collective-permute-start | bytes 393224 | tf_op jit(solution)/shard_map/ppermute | solution.py:196
  31.7 6.9 %collective-permute-start.12 = (f32[32,1024]{1,0:T(8,128)S(1)}, f32[32,1024]{1,0:T(8,128)S(1)}, u32[]{:S(2)}, u32[]{:S(2)}) collective-permute-start(f32[32,1024]{1,0:T(8,128)S(1)} %get-tuple-element.46), channel_id=1, source_target_pairs={{0,8},{4,12},{8,0},{12,4},{16,24},{20,28},{24,16},{28,20},{1,9},{5... | collective-permute-start | bytes 393224 | tf_op jit(solution)/shard_map/ppermute | solution.py:196
  32.4 17.2 %collective-permute-start.14 = (f32[32,1024]{1,0:T(8,128)S(1)}, f32[32,1024]{1,0:T(8,128)S(1)}, u32[]{:S(2)}, u32[]{:S(2)}) collective-permute-start(f32[32,1024]{1,0:T(8,128)S(1)} %get-tuple-element.48), channel_id=1, source_target_pairs={{0,16},{4,20},{8,24},{12,28},{16,0},{20,4},{24,8},{28,12},{1,17},{... | collective-permute-start | bytes 393224 | tf_op jit(solution)/shard_map/ppermute | solution.py:196
  34.8 17.6 %collective-permute-start.15 = (f32[32,1024]{1,0:T(8,128)S(1)}, f32[32,1024]{1,0:T(8,128)S(1)}, u32[]{:S(2)}, u32[]{:S(2)}) collective-permute-start(f32[32,1024]{1,0:T(8,128)S(1)} %get-tuple-element.49), channel_id=1, source_target_pairs={{0,20},{4,16},{8,28},{12,24},{16,4},{20,0},{24,12},{28,8},{1,21},{... | collective-permute-start | bytes 393224 | tf_op jit(solution)/shard_map/ppermute | solution.py:196
  35.5 20.0 %collective-permute-start.16 = (f32[32,1024]{1,0:T(8,128)S(1)}, f32[32,1024]{1,0:T(8,128)S(1)}, u32[]{:S(2)}, u32[]{:S(2)}) collective-permute-start(f32[32,1024]{1,0:T(8,128)S(1)} %get-tuple-element.50), channel_id=1, source_target_pairs={{0,24},{4,28},{8,16},{12,20},{16,8},{20,12},{24,0},{28,4},{1,25},{... | collective-permute-start | bytes 393224 | tf_op jit(solution)/shard_map/ppermute | solution.py:196
  38.2 20.0 %collective-permute-start.17 = (f32[32,1024]{1,0:T(8,128)S(1)}, f32[32,1024]{1,0:T(8,128)S(1)}, u32[]{:S(2)}, u32[]{:S(2)}) collective-permute-start(f32[32,1024]{1,0:T(8,128)S(1)} %get-tuple-element.51), channel_id=1, source_target_pairs={{0,28},{4,24},{8,20},{12,16},{16,12},{20,8},{24,4},{28,0},{1,29},{... | collective-permute-start | bytes 393224 | tf_op jit(solution)/shard_map/ppermute | solution.py:196
  38.5 19.7 %collective-permute-start.13 = (f32[32,1024]{1,0:T(8,128)S(1)}, f32[32,1024]{1,0:T(8,128)S(1)}, u32[]{:S(2)}, u32[]{:S(2)}) collective-permute-start(f32[32,1024]{1,0:T(8,128)S(1)} %get-tuple-element.47), channel_id=1, source_target_pairs={{0,12},{4,8},{8,4},{12,0},{16,28},{20,24},{24,20},{28,16},{1,13},{... | collective-permute-start | bytes 393224 | tf_op jit(solution)/shard_map/ppermute | solution.py:196

commit v19 on v18

--- a/solution.py
+++ b/solution.py
@@ -89,11 +89,14 @@
     return mine, other, parts
 
 
-def mix_kernel(times, order, index_ref, mine_ref, theirs_ref, high_t_ref, low_t_ref, own_ref):
-    total_half, rank = mine_ref.shape
+def mix_kernel(times, order, index_ref, *refs):
+    *halves, high_t_ref, low_t_ref, own_ref = refs
+    rank = own_ref.shape[1]
+    mine, theirs = [jnp.concatenate([ref[...] for ref in halves[i::2]], axis=0) for i in range(2)]
+    total_half = mine.shape[0]
     half = total_half // times
-    mine = mine_ref[...].reshape(times, half, rank)
-    theirs = theirs_ref[...].reshape(times, half, rank)
+    mine = mine.reshape(times, half, rank)
+    theirs = theirs.reshape(times, half, rank)
     first = index_ref[1] == 0
     low_rows, high_rows = jnp.where(first, mine, theirs), jnp.where(first, theirs, mine)
     projected = jnp.concatenate([low_rows, high_rows], axis=1).reshape(2 * total_half, rank)
@@ -126,18 +129,19 @@
     high_t_ref[...], low_t_ref[...] = split(turned)
 
 
-def mix(index, mine, theirs, times, group, order):
-    total_half, rank = mine.shape
-    rows = 2 * total_half // times
+def mix(index, pairs, times, group, order):
+    halves = [half for pair in pairs for half in pair]
+    rank = halves[0].shape[1]
+    rows = sum(half.shape[0] for half in halves) // times
     factor = jax.ShapeDtypeStruct((rank, group * rows), jnp.bfloat16)
     return pl.pallas_call(
         functools.partial(mix_kernel, times, order),
-        in_specs=[SMEM, VMEM, VMEM],
+        in_specs=[SMEM] + [VMEM] * len(halves),
         out_specs=[VMEM] * 3,
         out_shape=[factor, factor, jax.ShapeDtypeStruct((rows, rank), jnp.float32)],
         compiler_params=params(),
         cost_estimate=FREE,
-    )(index, mine, theirs)
+    )(index, *halves)
 
 
 def load_kernel(group, high_ref, low_ref, *refs):
@@ -216,12 +220,12 @@
     order = [k for k in range(times) if k % group < near]
     mine = jnp.concatenate([mine] + [swap(mine, "tm", k) for k in order[1:]], axis=0)
     mine, parts[2] = lax.optimization_barrier((mine, parts[2]))
-    for offset in range(near, group, near):
-        mine = jnp.concatenate([mine, swap(mine, "tm", offset)], axis=0)
-        order = order + [k ^ offset for k in order]
-    mine, parts[3] = lax.optimization_barrier((mine, parts[3]))
-    theirs, parts[1] = lax.optimization_barrier((swap(mine, "space", 1), parts[1]))
-    high_t, low_t, own = mix(jnp.stack([index, core]), mine, theirs, times, group, order)
+    rest = swap(mine, "tm", near)
+    pairs = [(mine, swap(mine, "space", 1))]
+    rest, parts[1] = lax.optimization_barrier((rest, parts[1]))
+    pairs.append((rest, swap(rest, "space", 1)))
+    order = order + [k ^ near for k in order]
+    high_t, low_t, own = mix(jnp.stack([index, core]), pairs, times, group, order)
 
     blocks = list(load(high_t, low_t, parts, times))
     terms = [blocks[0]] + [None] * (times - 1)

time: 59.3 us -> 59.7 us (level)
  starting transfers between devices: 20.5 us -> 23.9 us
  waiting for transfers between devices: 30.9 us -> 27.6 us
    ppermute x18 -> x19, starting transfers between devices: 20.5 us -> 23.9 us  [swap(): lax.ppermute(value, axis, [(i, i ^ offset) for i in range(lax.axis_size(a...]
    ppermute x18 -> x19, waiting for transfers between devices: 30.9 us -> 27.6 us  [swap(): lax.ppermute(value, axis, [(i, i ^ offset) for i in range(lax.axis_size(a...]
  transfers between devices with their start and end apart: 18 -> 19, of which waited for: 9 -> 11; matrix products, arithmetic and copies ran while one was open for 0% -> 0% of each run, Pallas kernels for 0% -> 4%
where the time goes in v19:
time: 59.7 us; the launch traced here: 59 us
  waiting for transfers between devices  27.6 us (46%)
  starting transfers between devices  23.9 us (40%)
  Pallas kernels  6.81 us (11%)
  between operations  0.68 us (1%)
    ppermute x19, waiting for transfers between devices, swap(): lax.ppermute(value, axis, [(i, i ^ offset) for i in range(lax.axis_size(a...  27.6 us
    ppermute x19, starting transfers between devices, swap(): lax.ppermute(value, axis, [(i, i ^ offset) for i in range(lax.axis_size(a...  23.9 us
    pallas_call x1, Pallas kernels, project(): pl.pallas_call(functools.partial(project_kernel, depth), in_specs=[HBM, H...  2.93 us
    pallas_call x1, Pallas kernels, mix(): pl.pallas_call(functools.partial(mix_kernel, times, order), in_specs=[SME...  2.46 us
  transfers between devices with their start and end apart: 19, of which 11 were waited for; matrix products, arithmetic and copies ran while one was open for 0% of the time, Pallas kernels for 4%

profile of v19, /device:TPU:8, one launch (start us, length us, event | category | flops | bytes accessed | tf_op | source)
XLA Modules:
  0.0 59.0 jit_solution(7907062928905760516)
XLA Ops:
  0.6 2.9 %shard_map.41 = (f32[32,256]{1,0:T(8,128)S(1)}, f32[32,256]{1,0:T(8,128)S(1)}, f32[64,1024]{1,0:T(8,128)S(1)}, f32[64,1024]{1,0:T(8,128)S(1)}, f32[64,1024]{1,0:T(8,128)S(1)}, /*index=5*/f32[64,1024]{1,0:T(8,128)S(1)}) custom-call(f32[64,4096]{1,0:T(8,128)} %snapshots_ref.1, f32[4096,256]{1,0:T(8,128)} %factor_ref.1), custom_call_target="tpu_custom_call" | custom-call | tf_op jit(solution)/shard_map/pallas_call | solution.py:76
  3.6 1.6 %collective-permute-start.1 = (f32[32,256]{1,0:T(8,128)S(1)}, f32[32,256]{1,0:T(8,128)S(1)}, u32[]{:S(2)}, u32[]{:S(2)}) collective-permute-start(f32[32,256]{1,0:T(8,128)S(1)} %get-tuple-element.25), channel_id=1, source_target_pairs={{0,2},{1,3},{2,0},{3,1},{4,6},{5,7},{6,4},{7,5},{8,10},{9,11},{10,... | collective-permute-start | bytes 98312 | tf_op jit(solution)/shard_map/ppermute | solution.py:200
  5.1 0.0 collective-permute-start.2
  5.2 0.6 %collective-permute-start = (f32[32,256]{1,0:T(8,128)S(1)}, f32[32,256]{1,0:T(8,128)S(1)}, u32[]{:S(2)}, u32[]{:S(2)}) collective-permute-start(f32[32,256]{1,0:T(8,128)S(1)} %get-tuple-element.26), channel_id=1, source_target_pairs={{0,1},{1,0},{2,3},{3,2},{4,5},{5,4},{6,7},{7,6},{8,9},{9,8},{10,11... | collective-permute-start | bytes 98312 | tf_op jit(solution)/shard_map/ppermute | solution.py:200
  5.8 0.0 collective-permute-start.6
  5.8 1.8 %collective-permute-done.1 = f32[32,256]{1,0:T(8,128)S(1)} collective-permute-done((f32[32,256]{1,0:T(8,128)S(1)}, f32[32,256]{1,0:T(8,128)S(1)}, u32[]{:S(2)}, u32[]{:S(2)}) %collective-permute-start.1) | collective-permute-done | bytes 32800 | tf_op jit(solution)/shard_map/ppermute | solution.py:200
  7.5 1.0 %collective-permute-done.2 = f32[32,256]{1,0:T(8,128)S(1)} collective-permute-done((f32[32,256]{1,0:T(8,128)S(1)}, f32[32,256]{1,0:T(8,128)S(1)}, u32[]{:S(2)}, u32[]{:S(2)}) %collective-permute-start.2) | collective-permute-done | bytes 32800 | tf_op jit(solution)/shard_map/ppermute | solution.py:200
  8.6 0.0 collective-permute-done
  8.6 3.6 %collective-permute-start.5 = (f32[32,256]{1,0:T(8,128)S(1)}, f32[32,256]{1,0:T(8,128)S(1)}, u32[]{:S(2)}, u32[]{:S(2)}) collective-permute-start(f32[32,256]{1,0:T(8,128)S(1)} %add_add_fusion), channel_id=1, source_target_pairs={{0,20},{4,16},{8,28},{12,24},{16,4},{20,0},{24,12},{28,8},{1,21},{... | collective-permute-start | bytes 98312 | tf_op jit(solution)/shard_map/ppermute | solution.py:200
  12.2 0.3 collective-permute-start.4
  12.5 0.5 collective-permute-start.3
  13.0 1.5 %collective-permute-start.9 = (f32[64,1024]{1,0:T(8,128)S(1)}, f32[64,1024]{1,0:T(8,128)S(1)}, u32[]{:S(2)}, u32[]{:S(2)}) collective-permute-start(f32[64,1024]{1,0:T(8,128)S(1)} %get-tuple-element.29), channel_id=1, source_target_pairs={{0,4},{4,0},{8,12},{12,8},{16,20},{20,16},{24,28},{28,24},{1,5},{5... | collective-permute-start | bytes 786440 | tf_op jit(solution)/shard_map/ppermute | solution.py:200
  14.5 2.5 %collective-permute-done.5 = f32[32,256]{1,0:T(8,128)S(1)} collective-permute-done((f32[32,256]{1,0:T(8,128)S(1)}, f32[32,256]{1,0:T(8,128)S(1)}, u32[]{:S(2)}, u32[]{:S(2)}) %collective-permute-start.5) | collective-permute-done | bytes 32800 | tf_op jit(solution)/shard_map/ppermute | solution.py:200
  17.1 0.0 collective-permute-done.4
  17.1 0.1 collective-permute-done.3
  17.2 0.0 collective-permute-done.6.refs_2_
  17.2 0.7 %collective-permute-start.8 = (f32[128,256]{1,0:T(8,128)S(1)}, f32[128,256]{1,0:T(8,128)S(1)}, u32[]{:S(2)}, u32[]{:S(2)}) collective-permute-start(f32[128,256]{1,0:T(8,128)S(1)} %pad_maximum_fusion.refs_0_), channel_id=1, source_target_pairs={{0,8},{4,12},{8,0},{12,4},{16,24},{20,28},{24,16},{28,20},{1,9},{5... | collective-permute-start | bytes 393224 | tf_op jit(solution)/shard_map/ppermute | solution.py:200
  18.0 1.5 %collective-permute-start.11 = (f32[64,1024]{1,0:T(8,128)S(1)}, f32[64,1024]{1,0:T(8,128)S(1)}, u32[]{:S(2)}, u32[]{:S(2)}) collective-permute-start(f32[64,1024]{1,0:T(8,128)S(1)} %get-tuple-element.37), channel_id=1, source_target_pairs={{0,12},{4,8},{8,4},{12,0},{16,28},{20,24},{24,20},{28,16},{1,13},{... | collective-permute-start | bytes 786440 | tf_op jit(solution)/shard_map/ppermute | solution.py:200
  19.5 0.0 collective-permute-start.7
  19.5 3.3 %collective-permute-done.9.refs_1_ = f32[64,1024]{1,0:T(8,128)S(1)} collective-permute-done((f32[64,1024]{1,0:T(8,128)S(1)}, f32[64,1024]{1,0:T(8,128)S(1)}, u32[]{:S(2)}, u32[]{:S(2)}) %collective-permute-start.9) | collective-permute-done | bytes 262176 | tf_op jit(solution)/shard_map/ppermute | solution.py:200
  22.7 1.0 %collective-permute-done.8.refs_2_ = f32[128,256]{1,0:T(8,128)S(1)} collective-permute-done((f32[128,256]{1,0:T(8,128)S(1)}, f32[128,256]{1,0:T(8,128)S(1)}, u32[]{:S(2)}, u32[]{:S(2)}) %collective-permute-start.8) | collective-permute-done | bytes 131104 | tf_op jit(solution)/shard_map/ppermute | solution.py:200
  23.7 0.0 collective-permute-start.10
  23.8 0.1 pad_add_fusion.index_ref
  23.8 0.0 collective-permute-done.7.refs_1_
  23.8 1.3 %collective-permute-done.10.refs_3_ = f32[128,256]{1,0:T(8,128)S(1)} collective-permute-done((f32[128,256]{1,0:T(8,128)S(1)}, f32[128,256]{1,0:T(8,128)S(1)}, u32[]{:S(2)}, u32[]{:S(2)}) %collective-permute-start.10) | collective-permute-done | bytes 131104 | tf_op jit(solution)/shard_map/ppermute | solution.py:200
  25.1 2.5 %shard_map.42 = (bf16[256,256]{1,0:T(8,128)(2,1)S(1)}, bf16[256,256]{1,0:T(8,128)(2,1)S(1)}, f32[64,256]{1,0:T(8,128)}) custom-call(s32[2]{0:T(128)S(1)} %pad_add_fusion.index_ref, f32[128,256]{1,0:T(8,128)S(1)} %pad_maximum_fusion.refs_0_, f32[128,256]{1,0:T(8,128)S(1)} %collective-permute-done.7.refs_1_, f32[128,256]{1,0:T(8,128)S(1)} %collective-permute-done.8.refs_2_, ...), custom_call_target="tpu_custom_call" | custom-call | tf_op jit(solution)/shard_map/pallas_call | solution.py:137
  27.6 0.0 collective-permute-done.11.refs_3_
  27.6 0.6 shard_map.43
  28.2 0.9 %collective-permute-start.12 = (f32[32,1024]{1,0:T(8,128)S(1)}, f32[32,1024]{1,0:T(8,128)S(1)}, u32[]{:S(2)}, u32[]{:S(2)}) collective-permute-start(f32[32,1024]{1,0:T(8,128)S(1)} %get-tuple-element.40), channel_id=1, source_target_pairs={{0,4},{4,0},{8,12},{12,8},{16,20},{20,16},{24,28},{28,24},{1,5},{5... | collective-permute-start | bytes 393224 | tf_op jit(solution)/shard_map/ppermute | solution.py:200
  29.1 0.9 %collective-permute-start.13 = (f32[32,1024]{1,0:T(8,128)S(1)}, f32[32,1024]{1,0:T(8,128)S(1)}, u32[]{:S(2)}, u32[]{:S(2)}) collective-permute-start(f32[32,1024]{1,0:T(8,128)S(1)} %get-tuple-element.42), channel_id=1, source_target_pairs={{0,8},{4,12},{8,0},{12,4},{16,24},{20,28},{24,16},{28,20},{1,9},{5... | collective-permute-start | bytes 393224 | tf_op jit(solution)/shard_map/ppermute | solution.py:200
  30.1 5.5 %collective-permute-start.15 = (f32[32,1024]{1,0:T(8,128)S(1)}, f32[32,1024]{1,0:T(8,128)S(1)}, u32[]{:S(2)}, u32[]{:S(2)}) collective-permute-start(f32[32,1024]{1,0:T(8,128)S(1)} %get-tuple-element.44), channel_id=1, source_target_pairs={{0,16},{4,20},{8,24},{12,28},{16,0},{20,4},{24,8},{28,12},{1,17},{... | collective-permute-start | bytes 393224 | tf_op jit(solution)/shard_map/ppermute | solution.py:200
  35.6 0.0 collective-permute-start.16
  35.6 2.3 %collective-permute-start.17 = (f32[32,1024]{1,0:T(8,128)S(1)}, f32[32,1024]{1,0:T(8,128)S(1)}, u32[]{:S(2)}, u32[]{:S(2)}) collective-permute-start(f32[32,1024]{1,0:T(8,128)S(1)} %get-tuple-element.46), channel_id=1, source_target_pairs={{0,24},{4,28},{8,16},{12,20},{16,8},{20,12},{24,0},{28,4},{1,25},{... | collective-permute-start | bytes 393224 | tf_op jit(solution)/shard_map/ppermute | solution.py:200
  37.9 0.0 collective-permute-done.12.refs_1_
  37.9 1.4 %collective-permute-start.18 = (f32[32,1024]{1,0:T(8,128)S(1)}, f32[32,1024]{1,0:T(8,128)S(1)}, u32[]{:S(2)}, u32[]{:S(2)}) collective-permute-start(f32[32,1024]{1,0:T(8,128)S(1)} %get-tuple-element.47), channel_id=1, source_target_pairs={{0,28},{4,24},{8,20},{12,16},{16,12},{20,8},{24,4},{28,0},{1,29},{... | collective-permute-start | bytes 393224 | tf_op jit(solution)/shard_map/ppermute | solution.py:200
  39.3 0.0 collective-permute-done.13.refs_2_
  39.3 2.4 %collective-permute-start.14 = (f32[32,1024]{1,0:T(8,128)S(1)}, f32[32,1024]{1,0:T(8,128)S(1)}, u32[]{:S(2)}, u32[]{:S(2)}) collective-permute-start(f32[32,1024]{1,0:T(8,128)S(1)} %get-tuple-element.43), channel_id=1, source_target_pairs={{0,12},{4,8},{8,4},{12,0},{16,28},{20,24},{24,20},{28,16},{1,13},{... | collective-permute-start | bytes 393224 | tf_op jit(solution)/shard_map/ppermute | solution.py:200
  41.6 8.6 %collective-permute-done.15.refs_4_ = f32[32,1024]{1,0:T(8,128)S(1)} collective-permute-done((f32[32,1024]{1,0:T(8,128)S(1)}, f32[32,1024]{1,0:T(8,128)S(1)}, u32[]{:S(2)}, u32[]{:S(2)}) %collective-permute-start.15) | collective-permute-done | bytes 131104 | tf_op jit(solution)/shard_map/ppermute | solution.py:200
  50.3 2.8 %collective-permute-done.16.refs_5_ = f32[32,1024]{1,0:T(8,128)S(1)} collective-permute-done((f32[32,1024]{1,0:T(8,128)S(1)}, f32[32,1024]{1,0:T(8,128)S(1)}, u32[]{:S(2)}, u32[]{:S(2)}) %collective-permute-start.16) | collective-permute-done | bytes 131104 | tf_op jit(solution)/shard_map/ppermute | solution.py:200
  53.1 3.3 %collective-permute-done.17.refs_6_ = f32[32,1024]{1,0:T(8,128)S(1)} collective-permute-done((f32[32,1024]{1,0:T(8,128)S(1)}, f32[32,1024]{1,0:T(8,128)S(1)}, u32[]{:S(2)}, u32[]{:S(2)}) %collective-permute-start.17) | collective-permute-done | bytes 131104 | tf_op jit(solution)/shard_map/ppermute | solution.py:200
  56.4 1.8 %collective-permute-done.18.refs_7_ = f32[32,1024]{1,0:T(8,128)S(1)} collective-permute-done((f32[32,1024]{1,0:T(8,128)S(1)}, f32[32,1024]{1,0:T(8,128)S(1)}, u32[]{:S(2)}, u32[]{:S(2)}) %collective-permute-start.18) | collective-permute-done | bytes 131104 | tf_op jit(solution)/shard_map/ppermute | solution.py:200
  58.2 0.0 collective-permute-done.14.refs_3_
  58.2 0.8 %shard_map.44 = f32[32,4096]{1,0:T(8,128)} custom-call(f32[32,1024]{1,0:T(8,128)S(1)} %get-tuple-element.38.refs_0_, f32[32,1024]{1,0:T(8,128)S(1)} %collective-permute-done.12.refs_1_, f32[32,1024]{1,0:T(8,128)S(1)} %collective-permute-done.13.refs_2_, f32[32,1024]{1,0:T(8,128)S(1)} %collective-permute-done.14.refs_3_, ...), custom_call_target="tpu_custom_call" | custom-call | tf_op jit(solution)/shard_map/pallas_call | solution.py:188
  (2 shorter events, 0.0 us)
Async XLA Ops:
  3.6 4.0 %collective-permute-start.1 = (f32[32,256]{1,0:T(8,128)S(1)}, f32[32,256]{1,0:T(8,128)S(1)}, u32[]{:S(2)}, u32[]{:S(2)}) collective-permute-start(f32[32,256]{1,0:T(8,128)S(1)} %get-tuple-element.25), channel_id=1, source_target_pairs={{0,2},{1,3},{2,0},{3,1},{4,6},{5,7},{6,4},{7,5},{8,10},{9,11},{10,... | collective-permute-start | bytes 98312 | tf_op jit(solution)/shard_map/ppermute | solution.py:200
  5.1 3.4 %collective-permute-start.2 = (f32[32,256]{1,0:T(8,128)S(1)}, f32[32,256]{1,0:T(8,128)S(1)}, u32[]{:S(2)}, u32[]{:S(2)}) collective-permute-start(f32[32,256]{1,0:T(8,128)S(1)} %get-tuple-element.26), channel_id=1, source_target_pairs={{0,3},{1,2},{2,1},{3,0},{4,7},{5,6},{6,5},{7,4},{8,11},{9,10},{10,... | collective-permute-start | bytes 98312 | tf_op jit(solution)/shard_map/ppermute | solution.py:200
  5.2 3.4 %collective-permute-start = (f32[32,256]{1,0:T(8,128)S(1)}, f32[32,256]{1,0:T(8,128)S(1)}, u32[]{:S(2)}, u32[]{:S(2)}) collective-permute-start(f32[32,256]{1,0:T(8,128)S(1)} %get-tuple-element.26), channel_id=1, source_target_pairs={{0,1},{1,0},{2,3},{3,2},{4,5},{5,4},{6,7},{7,6},{8,9},{9,8},{10,11... | collective-permute-start | bytes 98312 | tf_op jit(solution)/shard_map/ppermute | solution.py:200
  5.8 11.4 %collective-permute-start.6 = (f32[64,1024]{1,0:T(8,128)S(1)}, f32[64,1024]{1,0:T(8,128)S(1)}, u32[]{:S(2)}, u32[]{:S(2)}) collective-permute-start(f32[64,1024]{1,0:T(8,128)S(1)} %get-tuple-element.27), channel_id=1, source_target_pairs={{0,8},{4,12},{8,0},{12,4},{16,24},{20,28},{24,16},{28,20},{1,9},{5... | collective-permute-start | bytes 786440 | tf_op jit(solution)/shard_map/ppermute | solution.py:200
  8.6 8.5 %collective-permute-start.5 = (f32[32,256]{1,0:T(8,128)S(1)}, f32[32,256]{1,0:T(8,128)S(1)}, u32[]{:S(2)}, u32[]{:S(2)}) collective-permute-start(f32[32,256]{1,0:T(8,128)S(1)} %add_add_fusion), channel_id=1, source_target_pairs={{0,20},{4,16},{8,28},{12,24},{16,4},{20,0},{24,12},{28,8},{1,21},{... | collective-permute-start | bytes 98312 | tf_op jit(solution)/shard_map/ppermute | solution.py:200
  12.2 4.9 %collective-permute-start.4 = (f32[32,256]{1,0:T(8,128)S(1)}, f32[32,256]{1,0:T(8,128)S(1)}, u32[]{:S(2)}, u32[]{:S(2)}) collective-permute-start(f32[32,256]{1,0:T(8,128)S(1)} %add_add_fusion), channel_id=1, source_target_pairs={{0,16},{4,20},{8,24},{12,28},{16,0},{20,4},{24,8},{28,12},{1,17},{... | collective-permute-start | bytes 98312 | tf_op jit(solution)/shard_map/ppermute | solution.py:200
  12.5 4.7 %collective-permute-start.3 = (f32[32,256]{1,0:T(8,128)S(1)}, f32[32,256]{1,0:T(8,128)S(1)}, u32[]{:S(2)}, u32[]{:S(2)}) collective-permute-start(f32[32,256]{1,0:T(8,128)S(1)} %add_add_fusion), channel_id=1, source_target_pairs={{0,4},{4,0},{8,12},{12,8},{16,20},{20,16},{24,28},{28,24},{1,5},{5... | collective-permute-start | bytes 98312 | tf_op jit(solution)/shard_map/ppermute | solution.py:200
  13.0 9.7 %collective-permute-start.9 = (f32[64,1024]{1,0:T(8,128)S(1)}, f32[64,1024]{1,0:T(8,128)S(1)}, u32[]{:S(2)}, u32[]{:S(2)}) collective-permute-start(f32[64,1024]{1,0:T(8,128)S(1)} %get-tuple-element.29), channel_id=1, source_target_pairs={{0,4},{4,0},{8,12},{12,8},{16,20},{20,16},{24,28},{28,24},{1,5},{5... | collective-permute-start | bytes 786440 | tf_op jit(solution)/shard_map/ppermute | solution.py:200
  17.2 6.5 %collective-permute-start.8 = (f32[128,256]{1,0:T(8,128)S(1)}, f32[128,256]{1,0:T(8,128)S(1)}, u32[]{:S(2)}, u32[]{:S(2)}) collective-permute-start(f32[128,256]{1,0:T(8,128)S(1)} %pad_maximum_fusion.refs_0_), channel_id=1, source_target_pairs={{0,8},{4,12},{8,0},{12,4},{16,24},{20,28},{24,16},{28,20},{1,9},{5... | collective-permute-start | bytes 393224 | tf_op jit(solution)/shard_map/ppermute | solution.py:200
  18.0 9.6 %collective-permute-start.11 = (f32[64,1024]{1,0:T(8,128)S(1)}, f32[64,1024]{1,0:T(8,128)S(1)}, u32[]{:S(2)}, u32[]{:S(2)}) collective-permute-start(f32[64,1024]{1,0:T(8,128)S(1)} %get-tuple-element.37), channel_id=1, source_target_pairs={{0,12},{4,8},{8,4},{12,0},{16,28},{20,24},{24,20},{28,16},{1,13},{... | collective-permute-start | bytes 786440 | tf_op jit(solution)/shard_map/ppermute | solution.py:200
  19.5 4.4 %collective-permute-start.7 = (f32[128,256]{1,0:T(8,128)S(1)}, f32[128,256]{1,0:T(8,128)S(1)}, u32[]{:S(2)}, u32[]{:S(2)}) collective-permute-start(f32[128,256]{1,0:T(8,128)S(1)} %pad_maximum_fusion.refs_0_), channel_id=1, source_target_pairs={{0,1},{1,0},{2,3},{3,2},{4,5},{5,4},{6,7},{7,6},{8,9},{9,8},{10,11... | collective-permute-start | bytes 393224 | tf_op jit(solution)/shard_map/ppermute | solution.py:200
  23.7 1.3 %collective-permute-start.10 = (f32[128,256]{1,0:T(8,128)S(1)}, f32[128,256]{1,0:T(8,128)S(1)}, u32[]{:S(2)}, u32[]{:S(2)}) collective-permute-start(f32[128,256]{1,0:T(8,128)S(1)} %collective-permute-done.8.refs_2_), channel_id=1, source_target_pairs={{0,1},{1,0},{2,3},{3,2},{4,5},{5,4},{6,7},{7,6},{8,9},{9,8},{10,11... | collective-permute-start | bytes 393224 | tf_op jit(solution)/shard_map/ppermute | solution.py:200
  28.2 9.7 %collective-permute-start.12 = (f32[32,1024]{1,0:T(8,128)S(1)}, f32[32,1024]{1,0:T(8,128)S(1)}, u32[]{:S(2)}, u32[]{:S(2)}) collective-permute-start(f32[32,1024]{1,0:T(8,128)S(1)} %get-tuple-element.40), channel_id=1, source_target_pairs={{0,4},{4,0},{8,12},{12,8},{16,20},{20,16},{24,28},{28,24},{1,5},{5... | collective-permute-start | bytes 393224 | tf_op jit(solution)/shard_map/ppermute | solution.py:200
  29.1 10.2 %collective-permute-start.13 = (f32[32,1024]{1,0:T(8,128)S(1)}, f32[32,1024]{1,0:T(8,128)S(1)}, u32[]{:S(2)}, u32[]{:S(2)}) collective-permute-start(f32[32,1024]{1,0:T(8,128)S(1)} %get-tuple-element.42), channel_id=1, source_target_pairs={{0,8},{4,12},{8,0},{12,4},{16,24},{20,28},{24,16},{28,20},{1,9},{5... | collective-permute-start | bytes 393224 | tf_op jit(solution)/shard_map/ppermute | solution.py:200
  30.1 20.2 %collective-permute-start.15 = (f32[32,1024]{1,0:T(8,128)S(1)}, f32[32,1024]{1,0:T(8,128)S(1)}, u32[]{:S(2)}, u32[]{:S(2)}) collective-permute-start(f32[32,1024]{1,0:T(8,128)S(1)} %get-tuple-element.44), channel_id=1, source_target_pairs={{0,16},{4,20},{8,24},{12,28},{16,0},{20,4},{24,8},{28,12},{1,17},{... | collective-permute-start | bytes 393224 | tf_op jit(solution)/shard_map/ppermute | solution.py:200
  35.6 17.5 %collective-permute-start.16 = (f32[32,1024]{1,0:T(8,128)S(1)}, f32[32,1024]{1,0:T(8,128)S(1)}, u32[]{:S(2)}, u32[]{:S(2)}) collective-permute-start(f32[32,1024]{1,0:T(8,128)S(1)} %get-tuple-element.45), channel_id=1, source_target_pairs={{0,20},{4,16},{8,28},{12,24},{16,4},{20,0},{24,12},{28,8},{1,21},{... | collective-permute-start | bytes 393224 | tf_op jit(solution)/shard_map/ppermute | solution.py:200
  35.6 20.8 %collective-permute-start.17 = (f32[32,1024]{1,0:T(8,128)S(1)}, f32[32,1024]{1,0:T(8,128)S(1)}, u32[]{:S(2)}, u32[]{:S(2)}) collective-permute-start(f32[32,1024]{1,0:T(8,128)S(1)} %get-tuple-element.46), channel_id=1, source_target_pairs={{0,24},{4,28},{8,16},{12,20},{16,8},{20,12},{24,0},{28,4},{1,25},{... | collective-permute-start | bytes 393224 | tf_op jit(solution)/shard_map/ppermute | solution.py:200
  37.9 20.3 %collective-permute-start.18 = (f32[32,1024]{1,0:T(8,128)S(1)}, f32[32,1024]{1,0:T(8,128)S(1)}, u32[]{:S(2)}, u32[]{:S(2)}) collective-permute-start(f32[32,1024]{1,0:T(8,128)S(1)} %get-tuple-element.47), channel_id=1, source_target_pairs={{0,28},{4,24},{8,20},{12,16},{16,12},{20,8},{24,4},{28,0},{1,29},{... | collective-permute-start | bytes 393224 | tf_op jit(solution)/shard_map/ppermute | solution.py:200
  39.3 18.9 %collective-permute-start.14 = (f32[32,1024]{1,0:T(8,128)S(1)}, f32[32,1024]{1,0:T(8,128)S(1)}, u32[]{:S(2)}, u32[]{:S(2)}) collective-permute-start(f32[32,1024]{1,0:T(8,128)S(1)} %get-tuple-element.43), channel_id=1, source_target_pairs={{0,12},{4,8},{8,4},{12,0},{16,28},{20,24},{24,20},{28,16},{1,13},{... | collective-permute-start | bytes 393224 | tf_op jit(solution)/shard_map/ppermute | solution.py:200

commit v20 on v19

--- a/solution.py
+++ b/solution.py
@@ -166,8 +166,9 @@
     )(high, low, *parts)
 
 
-def join_kernel(group, *refs):
+def join_kernel(group, sequence, *refs):
     *terms, out_ref, buf, sems = refs
+    terms = [terms[sequence.index(k)] for k in range(len(terms))]
     width = terms[0].shape[1]
     member = lax.rem(lax.axis_index("tm"), group)
     copies = []
@@ -183,17 +184,17 @@
         copy.wait()
 
 
-def join(terms, group):
+def join(terms, group, sequence):
     rows, width = terms[0].shape
     return pl.pallas_call(
-        functools.partial(join_kernel, group),
+        functools.partial(join_kernel, group, sequence),
         in_specs=[VMEM] * len(terms),
         out_specs=HBM,
         out_shape=jax.ShapeDtypeStruct((rows, group * width), jnp.float32),
         scratch_shapes=[pltpu.VMEM((group, rows, width), jnp.float32), pltpu.SemaphoreType.DMA((group,))],
         compiler_params=params(),
         cost_estimate=FREE,
-    )(*terms)
+    )(*[terms[k] for k in sequence])
 
 
 def swap(value, axis, offset):
@@ -219,21 +220,22 @@
     near = group // 2
     order = [k for k in range(times) if k % group < near]
     mine = jnp.concatenate([mine] + [swap(mine, "tm", k) for k in order[1:]], axis=0)
-    mine, parts[2] = lax.optimization_barrier((mine, parts[2]))
+    mine, *parts[1:3] = lax.optimization_barrier((mine, *parts[1:3]))
     rest = swap(mine, "tm", near)
     pairs = [(mine, swap(mine, "space", 1))]
-    rest, parts[1] = lax.optimization_barrier((rest, parts[1]))
     pairs.append((rest, swap(rest, "space", 1)))
     order = order + [k ^ near for k in order]
     high_t, low_t, own = mix(jnp.stack([index, core]), pairs, times, group, order)
 
     blocks = list(load(high_t, low_t, parts, times))
     terms = [blocks[0]] + [None] * (times - 1)
-    for k in [*range(group, times), *range(1, group)]:
-        if k == group - 1:
+    near, far = list(range(1, group)), list(range(group, times))
+    sequence = [*far[:2], *near[:2], *far[2:], *near[2:], 0]
+    for k in sequence[:-1]:
+        if k == near[-1]:
             blocks[k], terms[1] = lax.optimization_barrier((blocks[k], terms[1]))
         terms[k] = swap(blocks[k], "tm", k)
-    return own, join(terms, group)
+    return own, join(terms, group, sequence)
 
 
 def solution(mesh):

time: 59.7 us -> 55.9 us (0.936)
  waiting for transfers between devices: 27.6 us -> 25.2 us
  starting transfers between devices: 23.9 us -> 22.6 us
    ppermute x19, waiting for transfers between devices: 27.6 us -> 25.2 us  [swap(): lax.ppermute(value, axis, [(i, i ^ offset) for i in range(lax.axis_size(a...]
    ppermute x19, starting transfers between devices: 23.9 us -> 22.6 us  [swap(): lax.ppermute(value, axis, [(i, i ^ offset) for i in range(lax.axis_size(a...]
  transfers between devices with their start and end apart: 19 -> 19, of which waited for: 11 -> 9; matrix products, arithmetic and copies ran while one was open for 0% -> 0% of each run, Pallas kernels for 4% -> 4%
where the time goes in v20:
time: 55.9 us; the launch traced here: 55.4 us
  waiting for transfers between devices  25.2 us (45%)
  starting transfers between devices  22.6 us (40%)
  Pallas kernels  6.81 us (12%)
  between operations  0.69 us (1%)
    ppermute x19, waiting for transfers between devices, swap(): lax.ppermute(value, axis, [(i, i ^ offset) for i in range(lax.axis_size(a...  25.2 us
    ppermute x19, starting transfers between devices, swap(): lax.ppermute(value, axis, [(i, i ^ offset) for i in range(lax.axis_size(a...  22.6 us
    pallas_call x1, Pallas kernels, project(): pl.pallas_call(functools.partial(project_kernel, depth), in_specs=[HBM, H...  2.93 us
    pallas_call x1, Pallas kernels, mix(): pl.pallas_call(functools.partial(mix_kernel, times, order), in_specs=[SME...  2.46 us
  transfers between devices with their start and end apart: 19, of which 9 were waited for; matrix products, arithmetic and copies ran while one was open for 0% of the time, Pallas kernels for 4%

profile of v20, /device:TPU:8, one launch (start us, length us, event | category | flops | bytes accessed | tf_op | source)
XLA Modules:
  0.0 55.4 jit_solution(17090652951689354630)
XLA Ops:
  0.6 2.9 %shard_map.41 = (f32[32,256]{1,0:T(8,128)S(1)}, f32[32,256]{1,0:T(8,128)S(1)}, f32[64,1024]{1,0:T(8,128)S(1)}, f32[64,1024]{1,0:T(8,128)S(1)}, f32[64,1024]{1,0:T(8,128)S(1)}, /*index=5*/f32[64,1024]{1,0:T(8,128)S(1)}) custom-call(f32[64,4096]{1,0:T(8,128)} %snapshots_ref.1, f32[4096,256]{1,0:T(8,128)} %factor_ref.1), custom_call_target="tpu_custom_call" | custom-call | tf_op jit(solution)/shard_map/pallas_call | solution.py:76
  3.6 1.6 %collective-permute-start.1 = (f32[32,256]{1,0:T(8,128)S(1)}, f32[32,256]{1,0:T(8,128)S(1)}, u32[]{:S(2)}, u32[]{:S(2)}) collective-permute-start(f32[32,256]{1,0:T(8,128)S(1)} %get-tuple-element.24), channel_id=1, source_target_pairs={{0,2},{1,3},{2,0},{3,1},{4,6},{5,7},{6,4},{7,5},{8,10},{9,11},{10,... | collective-permute-start | bytes 98312 | tf_op jit(solution)/shard_map/ppermute | solution.py:201
  5.1 0.0 collective-permute-start.2
  5.2 0.6 %collective-permute-start = (f32[32,256]{1,0:T(8,128)S(1)}, f32[32,256]{1,0:T(8,128)S(1)}, u32[]{:S(2)}, u32[]{:S(2)}) collective-permute-start(f32[32,256]{1,0:T(8,128)S(1)} %get-tuple-element.25), channel_id=1, source_target_pairs={{0,1},{1,0},{2,3},{3,2},{4,5},{5,4},{6,7},{7,6},{8,9},{9,8},{10,11... | collective-permute-start | bytes 98312 | tf_op jit(solution)/shard_map/ppermute | solution.py:201
  5.8 1.5 %collective-permute-start.6 = (f32[64,1024]{1,0:T(8,128)S(1)}, f32[64,1024]{1,0:T(8,128)S(1)}, u32[]{:S(2)}, u32[]{:S(2)}) collective-permute-start(f32[64,1024]{1,0:T(8,128)S(1)} %get-tuple-element.26), channel_id=1, source_target_pairs={{0,4},{4,0},{8,12},{12,8},{16,20},{20,16},{24,28},{28,24},{1,5},{5... | collective-permute-start | bytes 786440 | tf_op jit(solution)/shard_map/ppermute | solution.py:201
  7.3 0.5 collective-permute-start.7
  7.7 0.0 collective-permute-done.1
  7.7 0.9 %collective-permute-done.2 = f32[32,256]{1,0:T(8,128)S(1)} collective-permute-done((f32[32,256]{1,0:T(8,128)S(1)}, f32[32,256]{1,0:T(8,128)S(1)}, u32[]{:S(2)}, u32[]{:S(2)}) %collective-permute-start.2) | collective-permute-done | bytes 32800 | tf_op jit(solution)/shard_map/ppermute | solution.py:201
  8.6 0.0 collective-permute-done
  8.6 3.6 %collective-permute-start.5 = (f32[32,256]{1,0:T(8,128)S(1)}, f32[32,256]{1,0:T(8,128)S(1)}, u32[]{:S(2)}, u32[]{:S(2)}) collective-permute-start(f32[32,256]{1,0:T(8,128)S(1)} %add_add_fusion), channel_id=1, source_target_pairs={{0,20},{4,16},{8,28},{12,24},{16,4},{20,0},{24,12},{28,8},{1,21},{... | collective-permute-start | bytes 98312 | tf_op jit(solution)/shard_map/ppermute | solution.py:201
  12.2 0.3 collective-permute-start.4
  12.5 0.5 collective-permute-start.3
  13.0 4.2 %collective-permute-done.5 = f32[32,256]{1,0:T(8,128)S(1)} collective-permute-done((f32[32,256]{1,0:T(8,128)S(1)}, f32[32,256]{1,0:T(8,128)S(1)}, u32[]{:S(2)}, u32[]{:S(2)}) %collective-permute-start.5) | collective-permute-done | bytes 32800 | tf_op jit(solution)/shard_map/ppermute | solution.py:201
  17.2 0.4 collective-permute-done.4
  17.6 0.0 collective-permute-done.3
  17.6 0.0 collective-permute-done.6.refs_1_
  17.6 0.0 collective-permute-done.7.refs_2_
  17.7 0.2 collective-permute-start.9
  17.9 2.4 %collective-permute-start.11 = (f32[64,1024]{1,0:T(8,128)S(1)}, f32[64,1024]{1,0:T(8,128)S(1)}, u32[]{:S(2)}, u32[]{:S(2)}) collective-permute-start(f32[64,1024]{1,0:T(8,128)S(1)} %get-tuple-element.35), channel_id=1, source_target_pairs={{0,12},{4,8},{8,4},{12,0},{16,28},{20,24},{24,20},{28,16},{1,13},{... | collective-permute-start | bytes 786440 | tf_op jit(solution)/shard_map/ppermute | solution.py:201
  20.3 0.0 collective-permute-start.8
  20.3 3.9 %collective-permute-done.9.refs_2_ = f32[128,256]{1,0:T(8,128)S(1)} collective-permute-done((f32[128,256]{1,0:T(8,128)S(1)}, f32[128,256]{1,0:T(8,128)S(1)}, u32[]{:S(2)}, u32[]{:S(2)}) %collective-permute-start.9) | collective-permute-done | bytes 131104 | tf_op jit(solution)/shard_map/ppermute | solution.py:201
  24.2 0.0 collective-permute-start.10
  24.2 0.1 pad_add_fusion.index_ref
  24.2 0.0 collective-permute-done.8.refs_1_
  24.2 1.3 %collective-permute-done.10.refs_3_ = f32[128,256]{1,0:T(8,128)S(1)} collective-permute-done((f32[128,256]{1,0:T(8,128)S(1)}, f32[128,256]{1,0:T(8,128)S(1)}, u32[]{:S(2)}, u32[]{:S(2)}) %collective-permute-start.10) | collective-permute-done | bytes 131104 | tf_op jit(solution)/shard_map/ppermute | solution.py:201
  25.5 2.5 %shard_map.42 = (bf16[256,256]{1,0:T(8,128)(2,1)S(1)}, bf16[256,256]{1,0:T(8,128)(2,1)S(1)}, f32[64,256]{1,0:T(8,128)}) custom-call(s32[2]{0:T(128)S(1)} %pad_add_fusion.index_ref, f32[128,256]{1,0:T(8,128)S(1)} %pad_maximum_fusion.refs_0_, f32[128,256]{1,0:T(8,128)S(1)} %collective-permute-done.8.refs_1_, f32[128,256]{1,0:T(8,128)S(1)} %collective-permute-done.9.refs_2_, ...), custom_call_target="tpu_custom_call" | custom-call | tf_op jit(solution)/shard_map/pallas_call | solution.py:137
  28.0 0.0 collective-permute-done.11.refs_3_
  28.0 0.6 %shard_map.43 = (f32[32,1024]{1,0:T(8,128)S(1)}, f32[32,1024]{1,0:T(8,128)S(1)}, f32[32,1024]{1,0:T(8,128)S(1)}, f32[32,1024]{1,0:T(8,128)S(1)}, f32[32,1024]{1,...) custom-call(bf16[256,256]{1,0:T(8,128)(2,1)S(1)} %get-tuple-element.30.high_ref, ...), custom_call_target="tpu_custom_call" | custom-call | tf_op jit(solution)/shard_map/pallas_call | solution.py:159
  28.6 1.1 %collective-permute-start.14 = (f32[32,1024]{1,0:T(8,128)S(1)}, f32[32,1024]{1,0:T(8,128)S(1)}, u32[]{:S(2)}, u32[]{:S(2)}) collective-permute-start(f32[32,1024]{1,0:T(8,128)S(1)} %get-tuple-element.39), channel_id=1, source_target_pairs={{0,4},{4,0},{8,12},{12,8},{16,20},{20,16},{24,28},{28,24},{1,5},{5... | collective-permute-start | bytes 393224 | tf_op jit(solution)/shard_map/ppermute | solution.py:201
  29.7 1.5 %collective-permute-start.12 = (f32[32,1024]{1,0:T(8,128)S(1)}, f32[32,1024]{1,0:T(8,128)S(1)}, u32[]{:S(2)}, u32[]{:S(2)}) collective-permute-start(f32[32,1024]{1,0:T(8,128)S(1)} %get-tuple-element.36), channel_id=1, source_target_pairs={{0,16},{4,20},{8,24},{12,28},{16,0},{20,4},{24,8},{28,12},{1,17},{... | collective-permute-start | bytes 393224 | tf_op jit(solution)/shard_map/ppermute | solution.py:201
  31.2 1.9 %collective-permute-start.13 = (f32[32,1024]{1,0:T(8,128)S(1)}, f32[32,1024]{1,0:T(8,128)S(1)}, u32[]{:S(2)}, u32[]{:S(2)}) collective-permute-start(f32[32,1024]{1,0:T(8,128)S(1)} %get-tuple-element.37), channel_id=1, source_target_pairs={{0,20},{4,16},{8,28},{12,24},{16,4},{20,0},{24,12},{28,8},{1,21},{... | collective-permute-start | bytes 393224 | tf_op jit(solution)/shard_map/ppermute | solution.py:201
  33.0 0.5 collective-permute-start.15
  33.6 1.5 %collective-permute-start.16 = (f32[32,1024]{1,0:T(8,128)S(1)}, f32[32,1024]{1,0:T(8,128)S(1)}, u32[]{:S(2)}, u32[]{:S(2)}) collective-permute-start(f32[32,1024]{1,0:T(8,128)S(1)} %get-tuple-element.42), channel_id=1, source_target_pairs={{0,24},{4,28},{8,16},{12,20},{16,8},{20,12},{24,0},{28,4},{1,25},{... | collective-permute-start | bytes 393224 | tf_op jit(solution)/shard_map/ppermute | solution.py:201
  35.1 0.0 collective-permute-done.14.refs_2_
  35.1 0.7 %collective-permute-start.17 = (f32[32,1024]{1,0:T(8,128)S(1)}, f32[32,1024]{1,0:T(8,128)S(1)}, u32[]{:S(2)}, u32[]{:S(2)}) collective-permute-start(f32[32,1024]{1,0:T(8,128)S(1)} %get-tuple-element.43), channel_id=1, source_target_pairs={{0,28},{4,24},{8,20},{12,16},{16,12},{20,8},{24,4},{28,0},{1,29},{... | collective-permute-start | bytes 393224 | tf_op jit(solution)/shard_map/ppermute | solution.py:201
  35.8 4.5 %collective-permute-done.12.refs_0_ = f32[32,1024]{1,0:T(8,128)S(1)} collective-permute-done((f32[32,1024]{1,0:T(8,128)S(1)}, f32[32,1024]{1,0:T(8,128)S(1)}, u32[]{:S(2)}, u32[]{:S(2)}) %collective-permute-start.12) | collective-permute-done | bytes 131104 | tf_op jit(solution)/shard_map/ppermute | solution.py:201
  40.3 4.1 %collective-permute-start.18 = (f32[32,1024]{1,0:T(8,128)S(1)}, f32[32,1024]{1,0:T(8,128)S(1)}, u32[]{:S(2)}, u32[]{:S(2)}) collective-permute-start(f32[32,1024]{1,0:T(8,128)S(1)} %get-tuple-element.44), channel_id=1, source_target_pairs={{0,12},{4,8},{8,4},{12,0},{16,28},{20,24},{24,20},{28,16},{1,13},{... | collective-permute-start | bytes 393224 | tf_op jit(solution)/shard_map/ppermute | solution.py:201
  44.4 3.6 %collective-permute-done.13.refs_1_ = f32[32,1024]{1,0:T(8,128)S(1)} collective-permute-done((f32[32,1024]{1,0:T(8,128)S(1)}, f32[32,1024]{1,0:T(8,128)S(1)}, u32[]{:S(2)}, u32[]{:S(2)}) %collective-permute-start.13) | collective-permute-done | bytes 131104 | tf_op jit(solution)/shard_map/ppermute | solution.py:201
  48.0 0.0 collective-permute-done.15.refs_3_
  48.0 4.4 %collective-permute-done.16.refs_4_ = f32[32,1024]{1,0:T(8,128)S(1)} collective-permute-done((f32[32,1024]{1,0:T(8,128)S(1)}, f32[32,1024]{1,0:T(8,128)S(1)}, u32[]{:S(2)}, u32[]{:S(2)}) %collective-permute-start.16) | collective-permute-done | bytes 131104 | tf_op jit(solution)/shard_map/ppermute | solution.py:201
  52.4 2.1 %collective-permute-done.17.refs_5_ = f32[32,1024]{1,0:T(8,128)S(1)} collective-permute-done((f32[32,1024]{1,0:T(8,128)S(1)}, f32[32,1024]{1,0:T(8,128)S(1)}, u32[]{:S(2)}, u32[]{:S(2)}) %collective-permute-start.17) | collective-permute-done | bytes 131104 | tf_op jit(solution)/shard_map/ppermute | solution.py:201
  54.5 0.0 collective-permute-done.18.refs_6_
  54.5 0.8 %shard_map.44 = f32[32,4096]{1,0:T(8,128)} custom-call(f32[32,1024]{1,0:T(8,128)S(1)} %collective-permute-done.12.refs_0_, f32[32,1024]{1,0:T(8,128)S(1)} %collective-permute-done.13.refs_1_, f32[32,1024]{1,0:T(8,128)S(1)} %collective-permute-done.14.refs_2_, f32[32,1024]{1,0:T(8,128)S(1)} %collective-permute-done.15.refs_3_, ...), custom_call_target="tpu_custom_call" | custom-call | tf_op jit(solution)/shard_map/pallas_call | solution.py:189
  (2 shorter events, 0.0 us)
Async XLA Ops:
  3.6 4.2 %collective-permute-start.1 = (f32[32,256]{1,0:T(8,128)S(1)}, f32[32,256]{1,0:T(8,128)S(1)}, u32[]{:S(2)}, u32[]{:S(2)}) collective-permute-start(f32[32,256]{1,0:T(8,128)S(1)} %get-tuple-element.24), channel_id=1, source_target_pairs={{0,2},{1,3},{2,0},{3,1},{4,6},{5,7},{6,4},{7,5},{8,10},{9,11},{10,... | collective-permute-start | bytes 98312 | tf_op jit(solution)/shard_map/ppermute | solution.py:201
  5.1 3.4 %collective-permute-start.2 = (f32[32,256]{1,0:T(8,128)S(1)}, f32[32,256]{1,0:T(8,128)S(1)}, u32[]{:S(2)}, u32[]{:S(2)}) collective-permute-start(f32[32,256]{1,0:T(8,128)S(1)} %get-tuple-element.25), channel_id=1, source_target_pairs={{0,3},{1,2},{2,1},{3,0},{4,7},{5,6},{6,5},{7,4},{8,11},{9,10},{10,... | collective-permute-start | bytes 98312 | tf_op jit(solution)/shard_map/ppermute | solution.py:201
  5.2 3.4 %collective-permute-start = (f32[32,256]{1,0:T(8,128)S(1)}, f32[32,256]{1,0:T(8,128)S(1)}, u32[]{:S(2)}, u32[]{:S(2)}) collective-permute-start(f32[32,256]{1,0:T(8,128)S(1)} %get-tuple-element.25), channel_id=1, source_target_pairs={{0,1},{1,0},{2,3},{3,2},{4,5},{5,4},{6,7},{7,6},{8,9},{9,8},{10,11... | collective-permute-start | bytes 98312 | tf_op jit(solution)/shard_map/ppermute | solution.py:201
  5.8 11.9 %collective-permute-start.6 = (f32[64,1024]{1,0:T(8,128)S(1)}, f32[64,1024]{1,0:T(8,128)S(1)}, u32[]{:S(2)}, u32[]{:S(2)}) collective-permute-start(f32[64,1024]{1,0:T(8,128)S(1)} %get-tuple-element.26), channel_id=1, source_target_pairs={{0,4},{4,0},{8,12},{12,8},{16,20},{20,16},{24,28},{28,24},{1,5},{5... | collective-permute-start | bytes 786440 | tf_op jit(solution)/shard_map/ppermute | solution.py:201
  7.3 10.4 %collective-permute-start.7 = (f32[64,1024]{1,0:T(8,128)S(1)}, f32[64,1024]{1,0:T(8,128)S(1)}, u32[]{:S(2)}, u32[]{:S(2)}) collective-permute-start(f32[64,1024]{1,0:T(8,128)S(1)} %get-tuple-element.27), channel_id=1, source_target_pairs={{0,8},{4,12},{8,0},{12,4},{16,24},{20,28},{24,16},{28,20},{1,9},{5... | collective-permute-start | bytes 786440 | tf_op jit(solution)/shard_map/ppermute | solution.py:201
  8.6 8.6 %collective-permute-start.5 = (f32[32,256]{1,0:T(8,128)S(1)}, f32[32,256]{1,0:T(8,128)S(1)}, u32[]{:S(2)}, u32[]{:S(2)}) collective-permute-start(f32[32,256]{1,0:T(8,128)S(1)} %add_add_fusion), channel_id=1, source_target_pairs={{0,20},{4,16},{8,28},{12,24},{16,4},{20,0},{24,12},{28,8},{1,21},{... | collective-permute-start | bytes 98312 | tf_op jit(solution)/shard_map/ppermute | solution.py:201
  12.2 5.4 %collective-permute-start.4 = (f32[32,256]{1,0:T(8,128)S(1)}, f32[32,256]{1,0:T(8,128)S(1)}, u32[]{:S(2)}, u32[]{:S(2)}) collective-permute-start(f32[32,256]{1,0:T(8,128)S(1)} %add_add_fusion), channel_id=1, source_target_pairs={{0,16},{4,20},{8,24},{12,28},{16,0},{20,4},{24,8},{28,12},{1,17},{... | collective-permute-start | bytes 98312 | tf_op jit(solution)/shard_map/ppermute | solution.py:201
  12.5 5.1 %collective-permute-start.3 = (f32[32,256]{1,0:T(8,128)S(1)}, f32[32,256]{1,0:T(8,128)S(1)}, u32[]{:S(2)}, u32[]{:S(2)}) collective-permute-start(f32[32,256]{1,0:T(8,128)S(1)} %add_add_fusion), channel_id=1, source_target_pairs={{0,4},{4,0},{8,12},{12,8},{16,20},{20,16},{24,28},{28,24},{1,5},{5... | collective-permute-start | bytes 98312 | tf_op jit(solution)/shard_map/ppermute | solution.py:201
  17.7 6.5 %collective-permute-start.9 = (f32[128,256]{1,0:T(8,128)S(1)}, f32[128,256]{1,0:T(8,128)S(1)}, u32[]{:S(2)}, u32[]{:S(2)}) collective-permute-start(f32[128,256]{1,0:T(8,128)S(1)} %pad_maximum_fusion.refs_0_), channel_id=1, source_target_pairs={{0,8},{4,12},{8,0},{12,4},{16,24},{20,28},{24,16},{28,20},{1,9},{5... | collective-permute-start | bytes 393224 | tf_op jit(solution)/shard_map/ppermute | solution.py:201
  17.9 10.1 %collective-permute-start.11 = (f32[64,1024]{1,0:T(8,128)S(1)}, f32[64,1024]{1,0:T(8,128)S(1)}, u32[]{:S(2)}, u32[]{:S(2)}) collective-permute-start(f32[64,1024]{1,0:T(8,128)S(1)} %get-tuple-element.35), channel_id=1, source_target_pairs={{0,12},{4,8},{8,4},{12,0},{16,28},{20,24},{24,20},{28,16},{1,13},{... | collective-permute-start | bytes 786440 | tf_op jit(solution)/shard_map/ppermute | solution.py:201
  20.3 3.9 %collective-permute-start.8 = (f32[128,256]{1,0:T(8,128)S(1)}, f32[128,256]{1,0:T(8,128)S(1)}, u32[]{:S(2)}, u32[]{:S(2)}) collective-permute-start(f32[128,256]{1,0:T(8,128)S(1)} %pad_maximum_fusion.refs_0_), channel_id=1, source_target_pairs={{0,1},{1,0},{2,3},{3,2},{4,5},{5,4},{6,7},{7,6},{8,9},{9,8},{10,11... | collective-permute-start | bytes 393224 | tf_op jit(solution)/shard_map/ppermute | solution.py:201
  24.2 1.3 %collective-permute-start.10 = (f32[128,256]{1,0:T(8,128)S(1)}, f32[128,256]{1,0:T(8,128)S(1)}, u32[]{:S(2)}, u32[]{:S(2)}) collective-permute-start(f32[128,256]{1,0:T(8,128)S(1)} %collective-permute-done.9.refs_2_), channel_id=1, source_target_pairs={{0,1},{1,0},{2,3},{3,2},{4,5},{5,4},{6,7},{7,6},{8,9},{9,8},{10,11... | collective-permute-start | bytes 393224 | tf_op jit(solution)/shard_map/ppermute | solution.py:201
  28.6 6.5 %collective-permute-start.14 = (f32[32,1024]{1,0:T(8,128)S(1)}, f32[32,1024]{1,0:T(8,128)S(1)}, u32[]{:S(2)}, u32[]{:S(2)}) collective-permute-start(f32[32,1024]{1,0:T(8,128)S(1)} %get-tuple-element.39), channel_id=1, source_target_pairs={{0,4},{4,0},{8,12},{12,8},{16,20},{20,16},{24,28},{28,24},{1,5},{5... | collective-permute-start | bytes 393224 | tf_op jit(solution)/shard_map/ppermute | solution.py:201
  29.7 10.6 %collective-permute-start.12 = (f32[32,1024]{1,0:T(8,128)S(1)}, f32[32,1024]{1,0:T(8,128)S(1)}, u32[]{:S(2)}, u32[]{:S(2)}) collective-permute-start(f32[32,1024]{1,0:T(8,128)S(1)} %get-tuple-element.36), channel_id=1, source_target_pairs={{0,16},{4,20},{8,24},{12,28},{16,0},{20,4},{24,8},{28,12},{1,17},{... | collective-permute-start | bytes 393224 | tf_op jit(solution)/shard_map/ppermute | solution.py:201
  31.2 16.8 %collective-permute-start.13 = (f32[32,1024]{1,0:T(8,128)S(1)}, f32[32,1024]{1,0:T(8,128)S(1)}, u32[]{:S(2)}, u32[]{:S(2)}) collective-permute-start(f32[32,1024]{1,0:T(8,128)S(1)} %get-tuple-element.37), channel_id=1, source_target_pairs={{0,20},{4,16},{8,28},{12,24},{16,4},{20,0},{24,12},{28,8},{1,21},{... | collective-permute-start | bytes 393224 | tf_op jit(solution)/shard_map/ppermute | solution.py:201
  33.0 15.0 %collective-permute-start.15 = (f32[32,1024]{1,0:T(8,128)S(1)}, f32[32,1024]{1,0:T(8,128)S(1)}, u32[]{:S(2)}, u32[]{:S(2)}) collective-permute-start(f32[32,1024]{1,0:T(8,128)S(1)} %get-tuple-element.41), channel_id=1, source_target_pairs={{0,8},{4,12},{8,0},{12,4},{16,24},{20,28},{24,16},{28,20},{1,9},{5... | collective-permute-start | bytes 393224 | tf_op jit(solution)/shard_map/ppermute | solution.py:201
  33.6 18.9 %collective-permute-start.16 = (f32[32,1024]{1,0:T(8,128)S(1)}, f32[32,1024]{1,0:T(8,128)S(1)}, u32[]{:S(2)}, u32[]{:S(2)}) collective-permute-start(f32[32,1024]{1,0:T(8,128)S(1)} %get-tuple-element.42), channel_id=1, source_target_pairs={{0,24},{4,28},{8,16},{12,20},{16,8},{20,12},{24,0},{28,4},{1,25},{... | collective-permute-start | bytes 393224 | tf_op jit(solution)/shard_map/ppermute | solution.py:201
  35.1 19.5 %collective-permute-start.17 = (f32[32,1024]{1,0:T(8,128)S(1)}, f32[32,1024]{1,0:T(8,128)S(1)}, u32[]{:S(2)}, u32[]{:S(2)}) collective-permute-start(f32[32,1024]{1,0:T(8,128)S(1)} %get-tuple-element.43), channel_id=1, source_target_pairs={{0,28},{4,24},{8,20},{12,16},{16,12},{20,8},{24,4},{28,0},{1,29},{... | collective-permute-start | bytes 393224 | tf_op jit(solution)/shard_map/ppermute | solution.py:201
  40.3 14.2 %collective-permute-start.18 = (f32[32,1024]{1,0:T(8,128)S(1)}, f32[32,1024]{1,0:T(8,128)S(1)}, u32[]{:S(2)}, u32[]{:S(2)}) collective-permute-start(f32[32,1024]{1,0:T(8,128)S(1)} %get-tuple-element.44), channel_id=1, source_target_pairs={{0,12},{4,8},{8,4},{12,0},{16,28},{20,24},{24,20},{28,16},{1,13},{... | collective-permute-start | bytes 393224 | tf_op jit(solution)/shard_map/ppermute | solution.py:201

commit v21 on v20

--- a/solution.py
+++ b/solution.py
@@ -166,12 +166,13 @@
     )(high, low, *parts)
 
 
-def join_kernel(group, sequence, *refs):
-    *terms, out_ref, buf, sems = refs
+def join_kernel(group, sequence, own_ref, *refs):
+    *terms, own_out_ref, out_ref, buf, sems = refs
     terms = [terms[sequence.index(k)] for k in range(len(terms))]
     width = terms[0].shape[1]
     member = lax.rem(lax.axis_index("tm"), group)
-    copies = []
+    copies = [pltpu.make_async_copy(own_ref, own_out_ref, sems.at[group])]
+    copies[0].start()
     for k in range(group):
         value = terms[k][...]
         for term in terms[group + k :: group]:
@@ -184,17 +185,20 @@
         copy.wait()
 
 
-def join(terms, group, sequence):
+def join(own, terms, group, sequence):
     rows, width = terms[0].shape
     return pl.pallas_call(
         functools.partial(join_kernel, group, sequence),
-        in_specs=[VMEM] * len(terms),
-        out_specs=HBM,
-        out_shape=jax.ShapeDtypeStruct((rows, group * width), jnp.float32),
-        scratch_shapes=[pltpu.VMEM((group, rows, width), jnp.float32), pltpu.SemaphoreType.DMA((group,))],
+        in_specs=[VMEM] * (1 + len(terms)),
+        out_specs=[HBM] * 2,
+        out_shape=[
+            jax.ShapeDtypeStruct(own.shape, jnp.float32),
+            jax.ShapeDtypeStruct((rows, group * width), jnp.float32),
+        ],
+        scratch_shapes=[pltpu.VMEM((group, rows, width), jnp.float32), pltpu.SemaphoreType.DMA((group + 1,))],
         compiler_params=params(),
         cost_estimate=FREE,
-    )(*[terms[k] for k in sequence])
+    )(own, *[terms[k] for k in sequence])
 
 
 def swap(value, axis, offset):
@@ -235,7 +239,7 @@
         if k == near[-1]:
             blocks[k], terms[1] = lax.optimization_barrier((blocks[k], terms[1]))
         terms[k] = swap(blocks[k], "tm", k)
-    return own, join(terms, group, sequence)
+    return tuple(join(own, terms, group, sequence))
 
 
 def solution(mesh):

time: 55.9 us -> 55.6 us (level)
  no operation moved by 1% of the time
where the time goes in v21:
time: 55.6 us; the launch traced here: 55.1 us
  waiting for transfers between devices  25.2 us (45%)
  starting transfers between devices  22.6 us (41%)
  Pallas kernels  6.51 us (12%)
  between operations  0.7 us (1%)
    ppermute x19, waiting for transfers between devices, swap(): lax.ppermute(value, axis, [(i, i ^ offset) for i in range(lax.axis_size(a...  25.2 us
    ppermute x19, starting transfers between devices, swap(): lax.ppermute(value, axis, [(i, i ^ offset) for i in range(lax.axis_size(a...  22.6 us
    pallas_call x1, Pallas kernels, project(): pl.pallas_call(functools.partial(project_kernel, depth), in_specs=[HBM, H...  2.93 us
    pallas_call x1, Pallas kernels, mix(): pl.pallas_call(functools.partial(mix_kernel, times, order), in_specs=[SME...  2.15 us
  transfers between devices with their start and end apart: 19, of which 9 were waited for; matrix products, arithmetic and copies ran while one was open for 0% of the time, Pallas kernels for 4%

profile of v21, /device:TPU:8, one launch (start us, length us, event | category | flops | bytes accessed | tf_op | source)
XLA Modules:
  0.0 55.1 jit_solution(6532535220902812048)
XLA Ops:
  0.6 2.9 %shard_map.41 = (f32[32,256]{1,0:T(8,128)S(1)}, f32[32,256]{1,0:T(8,128)S(1)}, f32[64,1024]{1,0:T(8,128)S(1)}, f32[64,1024]{1,0:T(8,128)S(1)}, f32[64,1024]{1,0:T(8,128)S(1)}, /*index=5*/f32[64,1024]{1,0:T(8,128)S(1)}) custom-call(f32[64,4096]{1,0:T(8,128)} %snapshots_ref.1, f32[4096,256]{1,0:T(8,128)} %factor_ref.1), custom_call_target="tpu_custom_call" | custom-call | tf_op jit(solution)/shard_map/pallas_call | solution.py:76
  3.6 1.6 %collective-permute-start.1 = (f32[32,256]{1,0:T(8,128)S(1)}, f32[32,256]{1,0:T(8,128)S(1)}, u32[]{:S(2)}, u32[]{:S(2)}) collective-permute-start(f32[32,256]{1,0:T(8,128)S(1)} %get-tuple-element.24), channel_id=1, source_target_pairs={{0,2},{1,3},{2,0},{3,1},{4,6},{5,7},{6,4},{7,5},{8,10},{9,11},{10,... | collective-permute-start | bytes 98312 | tf_op jit(solution)/shard_map/ppermute | solution.py:205
  5.1 0.0 collective-permute-start.2
  5.2 0.6 %collective-permute-start = (f32[32,256]{1,0:T(8,128)S(1)}, f32[32,256]{1,0:T(8,128)S(1)}, u32[]{:S(2)}, u32[]{:S(2)}) collective-permute-start(f32[32,256]{1,0:T(8,128)S(1)} %get-tuple-element.25), channel_id=1, source_target_pairs={{0,1},{1,0},{2,3},{3,2},{4,5},{5,4},{6,7},{7,6},{8,9},{9,8},{10,11... | collective-permute-start | bytes 98312 | tf_op jit(solution)/shard_map/ppermute | solution.py:205
  5.8 1.5 %collective-permute-start.6 = (f32[64,1024]{1,0:T(8,128)S(1)}, f32[64,1024]{1,0:T(8,128)S(1)}, u32[]{:S(2)}, u32[]{:S(2)}) collective-permute-start(f32[64,1024]{1,0:T(8,128)S(1)} %get-tuple-element.26), channel_id=1, source_target_pairs={{0,4},{4,0},{8,12},{12,8},{16,20},{20,16},{24,28},{28,24},{1,5},{5... | collective-permute-start | bytes 786440 | tf_op jit(solution)/shard_map/ppermute | solution.py:205
  7.3 0.5 collective-permute-start.7
  7.7 0.0 collective-permute-done.1
  7.7 0.9 %collective-permute-done.2 = f32[32,256]{1,0:T(8,128)S(1)} collective-permute-done((f32[32,256]{1,0:T(8,128)S(1)}, f32[32,256]{1,0:T(8,128)S(1)}, u32[]{:S(2)}, u32[]{:S(2)}) %collective-permute-start.2) | collective-permute-done | bytes 32800 | tf_op jit(solution)/shard_map/ppermute | solution.py:205
  8.6 0.0 collective-permute-done
  8.6 3.6 %collective-permute-start.5 = (f32[32,256]{1,0:T(8,128)S(1)}, f32[32,256]{1,0:T(8,128)S(1)}, u32[]{:S(2)}, u32[]{:S(2)}) collective-permute-start(f32[32,256]{1,0:T(8,128)S(1)} %add_add_fusion), channel_id=1, source_target_pairs={{0,20},{4,16},{8,28},{12,24},{16,4},{20,0},{24,12},{28,8},{1,21},{... | collective-permute-start | bytes 98312 | tf_op jit(solution)/shard_map/ppermute | solution.py:205
  12.2 0.3 collective-permute-start.4
  12.5 0.5 collective-permute-start.3
  13.0 4.2 %collective-permute-done.5 = f32[32,256]{1,0:T(8,128)S(1)} collective-permute-done((f32[32,256]{1,0:T(8,128)S(1)}, f32[32,256]{1,0:T(8,128)S(1)}, u32[]{:S(2)}, u32[]{:S(2)}) %collective-permute-start.5) | collective-permute-done | bytes 32800 | tf_op jit(solution)/shard_map/ppermute | solution.py:205
  17.2 0.4 collective-permute-done.4
  17.6 0.0 collective-permute-done.3
  17.6 0.0 collective-permute-done.6.refs_1_
  17.6 0.0 collective-permute-done.7.refs_2_
  17.7 0.2 collective-permute-start.9
  17.9 2.4 %collective-permute-start.11 = (f32[64,1024]{1,0:T(8,128)S(1)}, f32[64,1024]{1,0:T(8,128)S(1)}, u32[]{:S(2)}, u32[]{:S(2)}) collective-permute-start(f32[64,1024]{1,0:T(8,128)S(1)} %get-tuple-element.35), channel_id=1, source_target_pairs={{0,12},{4,8},{8,4},{12,0},{16,28},{20,24},{24,20},{28,16},{1,13},{... | collective-permute-start | bytes 786440 | tf_op jit(solution)/shard_map/ppermute | solution.py:205
  20.3 0.0 collective-permute-start.8
  20.3 3.9 %collective-permute-done.9.refs_2_ = f32[128,256]{1,0:T(8,128)S(1)} collective-permute-done((f32[128,256]{1,0:T(8,128)S(1)}, f32[128,256]{1,0:T(8,128)S(1)}, u32[]{:S(2)}, u32[]{:S(2)}) %collective-permute-start.9) | collective-permute-done | bytes 131104 | tf_op jit(solution)/shard_map/ppermute | solution.py:205
  24.2 0.0 collective-permute-start.10
  24.2 0.1 pad_add_fusion.index_ref
  24.2 0.0 collective-permute-done.8.refs_1_
  24.2 1.3 %collective-permute-done.10.refs_3_ = f32[128,256]{1,0:T(8,128)S(1)} collective-permute-done((f32[128,256]{1,0:T(8,128)S(1)}, f32[128,256]{1,0:T(8,128)S(1)}, u32[]{:S(2)}, u32[]{:S(2)}) %collective-permute-start.10) | collective-permute-done | bytes 131104 | tf_op jit(solution)/shard_map/ppermute | solution.py:205
  25.5 2.1 %shard_map.42 = (bf16[256,256]{1,0:T(8,128)(2,1)S(1)}, bf16[256,256]{1,0:T(8,128)(2,1)S(1)}, f32[64,256]{1,0:T(8,128)S(1)}) custom-call(s32[2]{0:T(128)S(1)} %pad_add_fusion.index_ref, f32[128,256]{1,0:T(8,128)S(1)} %pad_maximum_fusion.refs_0_, f32[128,256]{1,0:T(8,128)S(1)} %collective-permute-done.8.refs_1_, ...), custom_call_target="tpu_custom_call" | custom-call | tf_op jit(solution)/shard_map/pallas_call | solution.py:137
  27.7 0.0 collective-permute-done.11.refs_3_
  27.7 0.6 %shard_map.43 = (f32[32,1024]{1,0:T(8,128)S(1)}, f32[32,1024]{1,0:T(8,128)S(1)}, f32[32,1024]{1,0:T(8,128)S(1)}, f32[32,1024]{1,0:T(8,128)S(1)}, f32[32,1024]{1,...) custom-call(bf16[256,256]{1,0:T(8,128)(2,1)S(1)} %get-tuple-element.30.high_ref, ...), custom_call_target="tpu_custom_call" | custom-call | tf_op jit(solution)/shard_map/pallas_call | solution.py:159
  28.3 1.1 %collective-permute-start.14 = (f32[32,1024]{1,0:T(8,128)S(1)}, f32[32,1024]{1,0:T(8,128)S(1)}, u32[]{:S(2)}, u32[]{:S(2)}) collective-permute-start(f32[32,1024]{1,0:T(8,128)S(1)} %get-tuple-element.39), channel_id=1, source_target_pairs={{0,4},{4,0},{8,12},{12,8},{16,20},{20,16},{24,28},{28,24},{1,5},{5... | collective-permute-start | bytes 393224 | tf_op jit(solution)/shard_map/ppermute | solution.py:205
  29.4 1.8 %collective-permute-start.12 = (f32[32,1024]{1,0:T(8,128)S(1)}, f32[32,1024]{1,0:T(8,128)S(1)}, u32[]{:S(2)}, u32[]{:S(2)}) collective-permute-start(f32[32,1024]{1,0:T(8,128)S(1)} %get-tuple-element.36), channel_id=1, source_target_pairs={{0,16},{4,20},{8,24},{12,28},{16,0},{20,4},{24,8},{28,12},{1,17},{... | collective-permute-start | bytes 393224 | tf_op jit(solution)/shard_map/ppermute | solution.py:205
  31.2 1.5 %collective-permute-start.13 = (f32[32,1024]{1,0:T(8,128)S(1)}, f32[32,1024]{1,0:T(8,128)S(1)}, u32[]{:S(2)}, u32[]{:S(2)}) collective-permute-start(f32[32,1024]{1,0:T(8,128)S(1)} %get-tuple-element.37), channel_id=1, source_target_pairs={{0,20},{4,16},{8,28},{12,24},{16,4},{20,0},{24,12},{28,8},{1,21},{... | collective-permute-start | bytes 393224 | tf_op jit(solution)/shard_map/ppermute | solution.py:205
  32.7 0.8 %collective-permute-start.15 = (f32[32,1024]{1,0:T(8,128)S(1)}, f32[32,1024]{1,0:T(8,128)S(1)}, u32[]{:S(2)}, u32[]{:S(2)}) collective-permute-start(f32[32,1024]{1,0:T(8,128)S(1)} %get-tuple-element.41), channel_id=1, source_target_pairs={{0,8},{4,12},{8,0},{12,4},{16,24},{20,28},{24,16},{28,20},{1,9},{5... | collective-permute-start | bytes 393224 | tf_op jit(solution)/shard_map/ppermute | solution.py:205
  33.6 1.2 %collective-permute-start.16 = (f32[32,1024]{1,0:T(8,128)S(1)}, f32[32,1024]{1,0:T(8,128)S(1)}, u32[]{:S(2)}, u32[]{:S(2)}) collective-permute-start(f32[32,1024]{1,0:T(8,128)S(1)} %get-tuple-element.42), channel_id=1, source_target_pairs={{0,24},{4,28},{8,16},{12,20},{16,8},{20,12},{24,0},{28,4},{1,25},{... | collective-permute-start | bytes 393224 | tf_op jit(solution)/shard_map/ppermute | solution.py:205
  34.7 0.0 collective-permute-done.14.refs_2_
  34.8 1.0 %collective-permute-start.17 = (f32[32,1024]{1,0:T(8,128)S(1)}, f32[32,1024]{1,0:T(8,128)S(1)}, u32[]{:S(2)}, u32[]{:S(2)}) collective-permute-start(f32[32,1024]{1,0:T(8,128)S(1)} %get-tuple-element.43), channel_id=1, source_target_pairs={{0,28},{4,24},{8,20},{12,16},{16,12},{20,8},{24,4},{28,0},{1,29},{... | collective-permute-start | bytes 393224 | tf_op jit(solution)/shard_map/ppermute | solution.py:205
  35.8 4.5 %collective-permute-done.12.refs_0_ = f32[32,1024]{1,0:T(8,128)S(1)} collective-permute-done((f32[32,1024]{1,0:T(8,128)S(1)}, f32[32,1024]{1,0:T(8,128)S(1)}, u32[]{:S(2)}, u32[]{:S(2)}) %collective-permute-start.12) | collective-permute-done | bytes 131104 | tf_op jit(solution)/shard_map/ppermute | solution.py:205
  40.3 3.8 %collective-permute-start.18 = (f32[32,1024]{1,0:T(8,128)S(1)}, f32[32,1024]{1,0:T(8,128)S(1)}, u32[]{:S(2)}, u32[]{:S(2)}) collective-permute-start(f32[32,1024]{1,0:T(8,128)S(1)} %get-tuple-element.44), channel_id=1, source_target_pairs={{0,12},{4,8},{8,4},{12,0},{16,28},{20,24},{24,20},{28,16},{1,13},{... | collective-permute-start | bytes 393224 | tf_op jit(solution)/shard_map/ppermute | solution.py:205
  44.1 3.5 %collective-permute-done.13.refs_1_ = f32[32,1024]{1,0:T(8,128)S(1)} collective-permute-done((f32[32,1024]{1,0:T(8,128)S(1)}, f32[32,1024]{1,0:T(8,128)S(1)}, u32[]{:S(2)}, u32[]{:S(2)}) %collective-permute-start.13) | collective-permute-done | bytes 131104 | tf_op jit(solution)/shard_map/ppermute | solution.py:205
  47.7 0.0 collective-permute-done.15.refs_3_
  47.7 4.8 %collective-permute-done.16.refs_4_ = f32[32,1024]{1,0:T(8,128)S(1)} collective-permute-done((f32[32,1024]{1,0:T(8,128)S(1)}, f32[32,1024]{1,0:T(8,128)S(1)}, u32[]{:S(2)}, u32[]{:S(2)}) %collective-permute-start.16) | collective-permute-done | bytes 131104 | tf_op jit(solution)/shard_map/ppermute | solution.py:205
  52.4 1.8 %collective-permute-done.17.refs_5_ = f32[32,1024]{1,0:T(8,128)S(1)} collective-permute-done((f32[32,1024]{1,0:T(8,128)S(1)}, f32[32,1024]{1,0:T(8,128)S(1)}, u32[]{:S(2)}, u32[]{:S(2)}) %collective-permute-start.17) | collective-permute-done | bytes 131104 | tf_op jit(solution)/shard_map/ppermute | solution.py:205
  54.2 0.0 collective-permute-done.18.refs_6_
  54.2 0.8 %shard_map.44 = (f32[64,256]{1,0:T(8,128)}, f32[32,4096]{1,0:T(8,128)}) custom-call(f32[64,256]{1,0:T(8,128)S(1)} %get-tuple-element.29.own_ref, f32[32,1024]{1,0:T(8,128)S(1)} %collective-permute-done.12.refs_0_, f32[32,1024]{1,0:T(8,128)S(1)} %collective-permute-done.13.refs_1_, f32[32,1024]{1,0:T(8,128)S(1)} %collective-permute-done.14.refs_2_, ...), custom_call_target="tpu_custom_call" | custom-call | tf_op jit(solution)/shard_map/pallas_call | solution.py:190
  (2 shorter events, 0.0 us)
Async XLA Ops:
  3.6 4.2 %collective-permute-start.1 = (f32[32,256]{1,0:T(8,128)S(1)}, f32[32,256]{1,0:T(8,128)S(1)}, u32[]{:S(2)}, u32[]{:S(2)}) collective-permute-start(f32[32,256]{1,0:T(8,128)S(1)} %get-tuple-element.24), channel_id=1, source_target_pairs={{0,2},{1,3},{2,0},{3,1},{4,6},{5,7},{6,4},{7,5},{8,10},{9,11},{10,... | collective-permute-start | bytes 98312 | tf_op jit(solution)/shard_map/ppermute | solution.py:205
  5.1 3.4 %collective-permute-start.2 = (f32[32,256]{1,0:T(8,128)S(1)}, f32[32,256]{1,0:T(8,128)S(1)}, u32[]{:S(2)}, u32[]{:S(2)}) collective-permute-start(f32[32,256]{1,0:T(8,128)S(1)} %get-tuple-element.25), channel_id=1, source_target_pairs={{0,3},{1,2},{2,1},{3,0},{4,7},{5,6},{6,5},{7,4},{8,11},{9,10},{10,... | collective-permute-start | bytes 98312 | tf_op jit(solution)/shard_map/ppermute | solution.py:205
  5.2 3.4 %collective-permute-start = (f32[32,256]{1,0:T(8,128)S(1)}, f32[32,256]{1,0:T(8,128)S(1)}, u32[]{:S(2)}, u32[]{:S(2)}) collective-permute-start(f32[32,256]{1,0:T(8,128)S(1)} %get-tuple-element.25), channel_id=1, source_target_pairs={{0,1},{1,0},{2,3},{3,2},{4,5},{5,4},{6,7},{7,6},{8,9},{9,8},{10,11... | collective-permute-start | bytes 98312 | tf_op jit(solution)/shard_map/ppermute | solution.py:205
  5.8 11.9 %collective-permute-start.6 = (f32[64,1024]{1,0:T(8,128)S(1)}, f32[64,1024]{1,0:T(8,128)S(1)}, u32[]{:S(2)}, u32[]{:S(2)}) collective-permute-start(f32[64,1024]{1,0:T(8,128)S(1)} %get-tuple-element.26), channel_id=1, source_target_pairs={{0,4},{4,0},{8,12},{12,8},{16,20},{20,16},{24,28},{28,24},{1,5},{5... | collective-permute-start | bytes 786440 | tf_op jit(solution)/shard_map/ppermute | solution.py:205
  7.3 10.4 %collective-permute-start.7 = (f32[64,1024]{1,0:T(8,128)S(1)}, f32[64,1024]{1,0:T(8,128)S(1)}, u32[]{:S(2)}, u32[]{:S(2)}) collective-permute-start(f32[64,1024]{1,0:T(8,128)S(1)} %get-tuple-element.27), channel_id=1, source_target_pairs={{0,8},{4,12},{8,0},{12,4},{16,24},{20,28},{24,16},{28,20},{1,9},{5... | collective-permute-start | bytes 786440 | tf_op jit(solution)/shard_map/ppermute | solution.py:205
  8.6 8.6 %collective-permute-start.5 = (f32[32,256]{1,0:T(8,128)S(1)}, f32[32,256]{1,0:T(8,128)S(1)}, u32[]{:S(2)}, u32[]{:S(2)}) collective-permute-start(f32[32,256]{1,0:T(8,128)S(1)} %add_add_fusion), channel_id=1, source_target_pairs={{0,20},{4,16},{8,28},{12,24},{16,4},{20,0},{24,12},{28,8},{1,21},{... | collective-permute-start | bytes 98312 | tf_op jit(solution)/shard_map/ppermute | solution.py:205
  12.2 5.4 %collective-permute-start.4 = (f32[32,256]{1,0:T(8,128)S(1)}, f32[32,256]{1,0:T(8,128)S(1)}, u32[]{:S(2)}, u32[]{:S(2)}) collective-permute-start(f32[32,256]{1,0:T(8,128)S(1)} %add_add_fusion), channel_id=1, source_target_pairs={{0,16},{4,20},{8,24},{12,28},{16,0},{20,4},{24,8},{28,12},{1,17},{... | collective-permute-start | bytes 98312 | tf_op jit(solution)/shard_map/ppermute | solution.py:205
  12.5 5.1 %collective-permute-start.3 = (f32[32,256]{1,0:T(8,128)S(1)}, f32[32,256]{1,0:T(8,128)S(1)}, u32[]{:S(2)}, u32[]{:S(2)}) collective-permute-start(f32[32,256]{1,0:T(8,128)S(1)} %add_add_fusion), channel_id=1, source_target_pairs={{0,4},{4,0},{8,12},{12,8},{16,20},{20,16},{24,28},{28,24},{1,5},{5... | collective-permute-start | bytes 98312 | tf_op jit(solution)/shard_map/ppermute | solution.py:205
  17.7 6.5 %collective-permute-start.9 = (f32[128,256]{1,0:T(8,128)S(1)}, f32[128,256]{1,0:T(8,128)S(1)}, u32[]{:S(2)}, u32[]{:S(2)}) collective-permute-start(f32[128,256]{1,0:T(8,128)S(1)} %pad_maximum_fusion.refs_0_), channel_id=1, source_target_pairs={{0,8},{4,12},{8,0},{12,4},{16,24},{20,28},{24,16},{28,20},{1,9},{5... | collective-permute-start | bytes 393224 | tf_op jit(solution)/shard_map/ppermute | solution.py:205
  17.9 9.8 %collective-permute-start.11 = (f32[64,1024]{1,0:T(8,128)S(1)}, f32[64,1024]{1,0:T(8,128)S(1)}, u32[]{:S(2)}, u32[]{:S(2)}) collective-permute-start(f32[64,1024]{1,0:T(8,128)S(1)} %get-tuple-element.35), channel_id=1, source_target_pairs={{0,12},{4,8},{8,4},{12,0},{16,28},{20,24},{24,20},{28,16},{1,13},{... | collective-permute-start | bytes 786440 | tf_op jit(solution)/shard_map/ppermute | solution.py:205
  20.3 3.9 %collective-permute-start.8 = (f32[128,256]{1,0:T(8,128)S(1)}, f32[128,256]{1,0:T(8,128)S(1)}, u32[]{:S(2)}, u32[]{:S(2)}) collective-permute-start(f32[128,256]{1,0:T(8,128)S(1)} %pad_maximum_fusion.refs_0_), channel_id=1, source_target_pairs={{0,1},{1,0},{2,3},{3,2},{4,5},{5,4},{6,7},{7,6},{8,9},{9,8},{10,11... | collective-permute-start | bytes 393224 | tf_op jit(solution)/shard_map/ppermute | solution.py:205
  24.2 1.3 %collective-permute-start.10 = (f32[128,256]{1,0:T(8,128)S(1)}, f32[128,256]{1,0:T(8,128)S(1)}, u32[]{:S(2)}, u32[]{:S(2)}) collective-permute-start(f32[128,256]{1,0:T(8,128)S(1)} %collective-permute-done.9.refs_2_), channel_id=1, source_target_pairs={{0,1},{1,0},{2,3},{3,2},{4,5},{5,4},{6,7},{7,6},{8,9},{9,8},{10,11... | collective-permute-start | bytes 393224 | tf_op jit(solution)/shard_map/ppermute | solution.py:205
  28.3 6.5 %collective-permute-start.14 = (f32[32,1024]{1,0:T(8,128)S(1)}, f32[32,1024]{1,0:T(8,128)S(1)}, u32[]{:S(2)}, u32[]{:S(2)}) collective-permute-start(f32[32,1024]{1,0:T(8,128)S(1)} %get-tuple-element.39), channel_id=1, source_target_pairs={{0,4},{4,0},{8,12},{12,8},{16,20},{20,16},{24,28},{28,24},{1,5},{5... | collective-permute-start | bytes 393224 | tf_op jit(solution)/shard_map/ppermute | solution.py:205
  29.4 10.9 %collective-permute-start.12 = (f32[32,1024]{1,0:T(8,128)S(1)}, f32[32,1024]{1,0:T(8,128)S(1)}, u32[]{:S(2)}, u32[]{:S(2)}) collective-permute-start(f32[32,1024]{1,0:T(8,128)S(1)} %get-tuple-element.36), channel_id=1, source_target_pairs={{0,16},{4,20},{8,24},{12,28},{16,0},{20,4},{24,8},{28,12},{1,17},{... | collective-permute-start | bytes 393224 | tf_op jit(solution)/shard_map/ppermute | solution.py:205
  31.2 16.5 %collective-permute-start.13 = (f32[32,1024]{1,0:T(8,128)S(1)}, f32[32,1024]{1,0:T(8,128)S(1)}, u32[]{:S(2)}, u32[]{:S(2)}) collective-permute-start(f32[32,1024]{1,0:T(8,128)S(1)} %get-tuple-element.37), channel_id=1, source_target_pairs={{0,20},{4,16},{8,28},{12,24},{16,4},{20,0},{24,12},{28,8},{1,21},{... | collective-permute-start | bytes 393224 | tf_op jit(solution)/shard_map/ppermute | solution.py:205
  32.7 15.0 %collective-permute-start.15 = (f32[32,1024]{1,0:T(8,128)S(1)}, f32[32,1024]{1,0:T(8,128)S(1)}, u32[]{:S(2)}, u32[]{:S(2)}) collective-permute-start(f32[32,1024]{1,0:T(8,128)S(1)} %get-tuple-element.41), channel_id=1, source_target_pairs={{0,8},{4,12},{8,0},{12,4},{16,24},{20,28},{24,16},{28,20},{1,9},{5... | collective-permute-start | bytes 393224 | tf_op jit(solution)/shard_map/ppermute | solution.py:205
  33.6 18.9 %collective-permute-start.16 = (f32[32,1024]{1,0:T(8,128)S(1)}, f32[32,1024]{1,0:T(8,128)S(1)}, u32[]{:S(2)}, u32[]{:S(2)}) collective-permute-start(f32[32,1024]{1,0:T(8,128)S(1)} %get-tuple-element.42), channel_id=1, source_target_pairs={{0,24},{4,28},{8,16},{12,20},{16,8},{20,12},{24,0},{28,4},{1,25},{... | collective-permute-start | bytes 393224 | tf_op jit(solution)/shard_map/ppermute | solution.py:205
  34.8 19.5 %collective-permute-start.17 = (f32[32,1024]{1,0:T(8,128)S(1)}, f32[32,1024]{1,0:T(8,128)S(1)}, u32[]{:S(2)}, u32[]{:S(2)}) collective-permute-start(f32[32,1024]{1,0:T(8,128)S(1)} %get-tuple-element.43), channel_id=1, source_target_pairs={{0,28},{4,24},{8,20},{12,16},{16,12},{20,8},{24,4},{28,0},{1,29},{... | collective-permute-start | bytes 393224 | tf_op jit(solution)/shard_map/ppermute | solution.py:205
  40.3 13.9 %collective-permute-start.18 = (f32[32,1024]{1,0:T(8,128)S(1)}, f32[32,1024]{1,0:T(8,128)S(1)}, u32[]{:S(2)}, u32[]{:S(2)}) collective-permute-start(f32[32,1024]{1,0:T(8,128)S(1)} %get-tuple-element.44), channel_id=1, source_target_pairs={{0,12},{4,8},{8,4},{12,0},{16,28},{20,24},{24,20},{28,16},{1,13},{... | collective-permute-start | bytes 393224 | tf_op jit(solution)/shard_map/ppermute | solution.py:205

commit v22 on v21

--- a/solution.py
+++ b/solution.py
@@ -38,10 +38,9 @@
     )
 
 
-def project_kernel(depth, snapshots_ref, factor_ref, mine_ref, other_ref, *refs):
+def project_kernel(depth, snapshots_ref, factor_ref, partial_ref, *refs):
     *parts, snapshots_buf, factor_buf, sems = refs
     rows, points = snapshots_ref.shape
-    half = rows // 2
     snapshots_copy = pltpu.make_async_copy(snapshots_ref, snapshots_buf, sems.at[points // depth])
     snapshots_copy.start()
     copies = []
@@ -62,22 +61,19 @@
         both = dot(jnp.concatenate([high, low], axis=0), factor_high)
         term = both[:rows] + (both[rows:] + dot(high, factor_low))
         value = term if value is None else value + term
-    first = lax.rem(lax.axis_index("space"), 2) == 0
-    mine_ref[...] = jnp.where(first, value[:half], value[half:])
-    other_ref[...] = jnp.where(first, value[half:], value[:half])
+    partial_ref[...] = value
 
 
 def project(snapshots, space_factor, group):
     rows, points = snapshots.shape
     rank = space_factor.shape[1]
     depth = min(512, points)
-    half = jax.ShapeDtypeStruct((rows // 2, rank), jnp.float32)
     part = jax.ShapeDtypeStruct((rows, points // group), jnp.float32)
-    mine, other, *parts = pl.pallas_call(
+    partial, *parts = pl.pallas_call(
         functools.partial(project_kernel, depth),
         in_specs=[HBM, HBM],
-        out_specs=[VMEM] * (2 + group),
-        out_shape=[half, half] + [part] * group,
+        out_specs=[VMEM] * (1 + group),
+        out_shape=[jax.ShapeDtypeStruct((rows, rank), jnp.float32)] + [part] * group,
         scratch_shapes=[
             pltpu.VMEM((rows, points), jnp.float32),
             pltpu.VMEM((points, rank), jnp.float32),
@@ -86,20 +82,15 @@
         compiler_params=params(52),
         cost_estimate=FREE,
     )(snapshots, space_factor)
-    return mine, other, parts
+    return partial, parts
 
 
 def mix_kernel(times, order, index_ref, *refs):
     *halves, high_t_ref, low_t_ref, own_ref = refs
     rank = own_ref.shape[1]
     mine, theirs = [jnp.concatenate([ref[...] for ref in halves[i::2]], axis=0) for i in range(2)]
-    total_half = mine.shape[0]
-    half = total_half // times
-    mine = mine.reshape(times, half, rank)
-    theirs = theirs.reshape(times, half, rank)
     first = index_ref[1] == 0
-    low_rows, high_rows = jnp.where(first, mine, theirs), jnp.where(first, theirs, mine)
-    projected = jnp.concatenate([low_rows, high_rows], axis=1).reshape(2 * total_half, rank)
+    projected = jnp.concatenate([jnp.where(first, mine, theirs), jnp.where(first, theirs, mine)], axis=0)
     high, low = split(projected)
     cross = dot(high, low, ROWS_BY_ROWS)
     gram = dot(high, high, ROWS_BY_ROWS) + (cross + cross.T)
@@ -113,7 +104,7 @@
     mixing = (jnp.where(row == column, 2.25, 0.0) - 2.4375 * correlation) + product(split(square), split(tail))
     mixing_high, mixing_low = split(mixing)
 
-    rows = 2 * half
+    rows = own_ref.shape[0]
     group = high_t_ref.shape[1] // rows
     places = [order.index(k) for k in range(group)]
     high = jnp.concatenate([high[i * rows : (i + 1) * rows] for i in places], axis=0)
@@ -205,6 +196,17 @@
     return lax.ppermute(value, axis, [(i, i ^ offset) for i in range(lax.axis_size(axis))])
 
 
+def swap_by_core(value, offset, other_offset):
+    spaces = lax.axis_size("space")
+    pairs = []
+    for t in range(lax.axis_size("tm")):
+        for s in range(spaces):
+            step = other_offset if s % 2 else offset
+            if step:
+                pairs.append((t * spaces + s, (t ^ step) * spaces + s))
+    return lax.ppermute(value, ("tm", "space"), pairs)
+
+
 def on_device(snapshots, space_factor):
     rows, points = snapshots.shape
     rank = space_factor.shape[1]
@@ -213,23 +215,29 @@
     index = lax.axis_index("tm")
     core = lax.axis_index("space") % 2
 
-    mine, other, parts = project(snapshots, space_factor, group)
-    parts = [part if k == 0 else swap(part, "tm", k) for k, part in enumerate(parts)]
-
-    terms = [mine] + [swap(other if k % 2 else mine, "space", k) for k in range(1, spaces)]
+    partial, parts = project(snapshots, space_factor, group)
+    parts[1:3] = [swap(parts[k], "tm", k) for k in (1, 2)]
+
+    terms = [partial] + [swap(partial, "space", k) for k in range(1, spaces)]
     while len(terms) > 1:
         terms = [a + b for a, b in zip(terms[::2], terms[1::2])]
-    mine = terms[0]
-
-    near = group // 2
-    order = [k for k in range(times) if k % group < near]
-    mine = jnp.concatenate([mine] + [swap(mine, "tm", k) for k in order[1:]], axis=0)
-    mine, *parts[1:3] = lax.optimization_barrier((mine, *parts[1:3]))
-    rest = swap(mine, "tm", near)
-    pairs = [(mine, swap(mine, "space", 1))]
-    pairs.append((rest, swap(rest, "space", 1)))
-    order = order + [k ^ near for k in order]
-    high_t, low_t, own = mix(jnp.stack([index, core]), pairs, times, group, order)
+    projected = terms[0]
+    projected, *parts[1:3] = lax.optimization_barrier((projected, *parts[1:3]))
+
+    offsets = [*range(group, times), *range(1, group), 0]
+    orders = offsets[: times - group : 2] + offsets[times - group :: 2], offsets[1 : times - group : 2] + offsets[times - group + 1 :: 2]
+    mine = [swap_by_core(projected, a, b) for a, b in zip(*orders)]
+    mine[0], parts[3] = lax.optimization_barrier((mine[0], parts[3]))
+    parts[3] = swap(parts[3], "tm", 3)
+    for i in range(2):
+        if orders[i][-1] == 0:
+            mine[-1] = jnp.where(core == i, projected, mine[-1])
+    middle = len(mine) // 2
+    pairs = []
+    for half in (mine[:middle], mine[middle:]):
+        half = jnp.concatenate(half, axis=0)
+        pairs.append((half, swap(half, "space", 1)))
+    high_t, low_t, own = mix(jnp.stack([index, core]), pairs, times, group, orders[0] + orders[1])
 
     blocks = list(load(high_t, low_t, parts, times))
     terms = [blocks[0]] + [None] * (times - 1)

time: 55.6 us -> 65.2 us (1.17)
  starting transfers between devices: 22.6 us -> 30.3 us
  waiting for transfers between devices: 25.2 us -> 27.1 us
    ppermute x0 -> x4, starting transfers between devices: none -> 6.91 us  [swap_by_core(): return lax.ppermute(value, ('tm', 'space'), pairs)]
    ppermute x0 -> x4, waiting for transfers between devices: none -> 3.81 us  [swap_by_core(): return lax.ppermute(value, ('tm', 'space'), pairs)]
    ppermute x19 -> x15, waiting for transfers between devices: 25.2 us -> 23.3 us  [swap(): lax.ppermute(value, axis, [(i, i ^ offset) for i in range(lax.axis_size(a...]
    ppermute x19 -> x15, starting transfers between devices: 22.6 us -> 23.4 us  [swap(): lax.ppermute(value, axis, [(i, i ^ offset) for i in range(lax.axis_size(a...]
  transfers between devices with their start and end apart: 19 -> 19, of which waited for: 9 -> 11; matrix products, arithmetic and copies ran while one was open for 0% -> 0% of each run, Pallas kernels for 4% -> 3%
where the time goes in v22:
time: 65.2 us; the launch traced here: 64.8 us
  starting transfers between devices  30.3 us (46%)
  waiting for transfers between devices  27.1 us (42%)
  Pallas kernels  6.52 us (10%)
  between operations  0.71 us (1%)
    ppermute x15, starting transfers between devices, swap(): lax.ppermute(value, axis, [(i, i ^ offset) for i in range(lax.axis_size(a...  23.4 us
    ppermute x15, waiting for transfers between devices, swap(): lax.ppermute(value, axis, [(i, i ^ offset) for i in range(lax.axis_size(a...  23.3 us
    ppermute x4, starting transfers between devices, swap_by_core(): return lax.ppermute(value, ('tm', 'space'), pairs)  6.91 us
    ppermute x4, waiting for transfers between devices, swap_by_core(): return lax.ppermute(value, ('tm', 'space'), pairs)  3.81 us
    pallas_call x1, Pallas kernels, project(): pl.pallas_call(functools.partial(project_kernel, depth), in_specs=[HBM, H...  2.93 us
    pallas_call x1, Pallas kernels, mix(): pl.pallas_call(functools.partial(mix_kernel, times, order), in_specs=[SME...  2.15 us
  transfers between devices with their start and end apart: 19, of which 11 were waited for; matrix products, arithmetic and copies ran while one was open for 0% of the time, Pallas kernels for 3%

profile of v22, /device:TPU:8, one launch (start us, length us, event | category | flops | bytes accessed | tf_op | source)
XLA Modules:
  0.0 64.8 jit_solution(7630690024989867364)
XLA Ops:
  0.6 2.9 %shard_map.41 = (f32[64,256]{1,0:T(8,128)S(1)}, f32[64,1024]{1,0:T(8,128)S(1)}, f32[64,1024]{1,0:T(8,128)S(1)}, f32[64,1024]{1,0:T(8,128)S(1)}, f32[64,1024]{1,0:T(8,128)S(1)}) custom-call(f32[64,4096]{1,0:T(8,128)} %snapshots_ref.1, f32[4096,256]{1,0:T(8,128)} %factor_ref.1), custom_call_target="tpu_custom_call" | custom-call | tf_op jit(solution)/shard_map/pallas_call | solution.py:72
  3.6 1.0 %collective-permute-start.2 = (f32[64,256]{1,0:T(8,128)S(1)}, f32[64,256]{1,0:T(8,128)S(1)}, u32[]{:S(2)}, u32[]{:S(2)}) collective-permute-start(f32[64,256]{1,0:T(8,128)S(1)} %get-tuple-element.25), channel_id=1, source_target_pairs={{0,3},{1,2},{2,1},{3,0},{4,7},{5,6},{6,5},{7,4},{8,11},{9,10},{10,... | collective-permute-start | bytes 196616 | tf_op jit(solution)/shard_map/ppermute | solution.py:196
  4.6 0.6 collective-permute-start.1
  5.2 0.3 collective-permute-start
  5.5 1.5 %collective-permute-start.3 = (f32[64,1024]{1,0:T(8,128)S(1)}, f32[64,1024]{1,0:T(8,128)S(1)}, u32[]{:S(2)}, u32[]{:S(2)}) collective-permute-start(f32[64,1024]{1,0:T(8,128)S(1)} %get-tuple-element.26), channel_id=1, source_target_pairs={{0,4},{4,0},{8,12},{12,8},{16,20},{20,16},{24,28},{28,24},{1,5},{5... | collective-permute-start | bytes 786440 | tf_op jit(solution)/shard_map/ppermute | solution.py:196
  7.0 0.5 collective-permute-start.4
  7.4 0.5 collective-permute-done.2
  7.9 1.5 %collective-permute-done.1 = f32[64,256]{1,0:T(8,128)S(1)} collective-permute-done((f32[64,256]{1,0:T(8,128)S(1)}, f32[64,256]{1,0:T(8,128)S(1)}, u32[]{:S(2)}, u32[]{:S(2)}) %collective-permute-start.1) | collective-permute-done | bytes 65568 | tf_op jit(solution)/shard_map/ppermute | solution.py:196
  9.4 0.0 collective-permute-done
  9.5 4.5 %collective-permute-done.3.refs_1_ = f32[64,1024]{1,0:T(8,128)S(1)} collective-permute-done((f32[64,1024]{1,0:T(8,128)S(1)}, f32[64,1024]{1,0:T(8,128)S(1)}, u32[]{:S(2)}, u32[]{:S(2)}) %collective-permute-start.3) | collective-permute-done | bytes 262176 | tf_op jit(solution)/shard_map/ppermute | solution.py:196
  13.9 1.2 %collective-permute-done.4.refs_2_ = f32[64,1024]{1,0:T(8,128)S(1)} collective-permute-done((f32[64,1024]{1,0:T(8,128)S(1)}, f32[64,1024]{1,0:T(8,128)S(1)}, u32[]{:S(2)}, u32[]{:S(2)}) %collective-permute-start.4) | collective-permute-done | bytes 262176 | tf_op jit(solution)/shard_map/ppermute | solution.py:196
  15.2 2.6 %collective-permute-start.5 = (f32[64,256]{1,0:T(8,128)S(1)}, f32[64,256]{1,0:T(8,128)S(1)}, u32[]{:S(2)}, u32[]{:S(2)}) collective-permute-start(f32[64,256]{1,0:T(8,128)S(1)} %add_add_fusion), channel_id=1, source_target_pairs={{0,16},{1,21},{2,18},{3,23},{4,20},{5,17},{6,22},{7,19},{8,24},{9,... | collective-permute-start | bytes 196616 | tf_op jit(solution)/shard_map/ppermute | solution.py:207
  17.8 2.3 %collective-permute-start.9 = (f32[64,256]{1,0:T(8,128)S(1)}, f32[64,256]{1,0:T(8,128)S(1)}, u32[]{:S(2)}, u32[]{:S(2)}) collective-permute-start(f32[64,256]{1,0:T(8,128)S(1)} %add_add_fusion), channel_id=1, source_target_pairs={{0,12},{2,14},{4,8},{6,10},{8,4},{10,6},{12,0},{14,2},{16,28},{18,... | collective-permute-start | bytes 196616 | tf_op jit(solution)/shard_map/ppermute | solution.py:207
  20.1 1.6 %collective-permute-start.8 = (f32[64,256]{1,0:T(8,128)S(1)}, f32[64,256]{1,0:T(8,128)S(1)}, u32[]{:S(2)}, u32[]{:S(2)}) collective-permute-start(f32[64,256]{1,0:T(8,128)S(1)} %add_add_fusion), channel_id=1, source_target_pairs={{0,4},{1,9},{2,6},{3,11},{4,0},{5,13},{6,2},{7,15},{8,12},{9,1},{1... | collective-permute-start | bytes 196616 | tf_op jit(solution)/shard_map/ppermute | solution.py:207
  21.6 0.5 collective-permute-start.6
  22.1 0.0 collective-permute-done.5
  22.1 3.8 %collective-permute-done.6 = f32[64,256]{1,0:T(8,128)S(1)} collective-permute-done((f32[64,256]{1,0:T(8,128)S(1)}, f32[64,256]{1,0:T(8,128)S(1)}, u32[]{:S(2)}, u32[]{:S(2)}) %collective-permute-start.6) | collective-permute-done | bytes 65568 | tf_op jit(solution)/shard_map/ppermute | solution.py:207
  25.9 0.0 collective-permute-start.7
  25.9 3.4 %collective-permute-start.11 = (f32[64,1024]{1,0:T(8,128)S(1)}, f32[64,1024]{1,0:T(8,128)S(1)}, u32[]{:S(2)}, u32[]{:S(2)}) collective-permute-start(f32[64,1024]{1,0:T(8,128)S(1)} %get-tuple-element.37), channel_id=1, source_target_pairs={{0,12},{4,8},{8,4},{12,0},{16,28},{20,24},{24,20},{28,16},{1,13},{... | collective-permute-start | bytes 786440 | tf_op jit(solution)/shard_map/ppermute | solution.py:196
  29.3 0.0 collective-permute-done.9
  29.3 0.0 collective-permute-done.8
  29.4 0.2 collective-permute-start.10
  29.6 0.1 pad_add_fusion.index_ref
  29.7 0.0 collective-permute-done.7.refs_1_
  29.7 1.1 %collective-permute-done.10.refs_3_ = f32[128,256]{1,0:T(8,128)S(1)} collective-permute-done((f32[128,256]{1,0:T(8,128)S(1)}, f32[128,256]{1,0:T(8,128)S(1)}, u32[]{:S(2)}, u32[]{:S(2)}) %collective-permute-start.10) | collective-permute-done | bytes 131104 | tf_op jit(solution)/shard_map/ppermute | solution.py:196
  30.8 2.1 %shard_map.42 = (bf16[256,256]{1,0:T(8,128)(2,1)S(1)}, bf16[256,256]{1,0:T(8,128)(2,1)S(1)}, f32[64,256]{1,0:T(8,128)S(1)}) custom-call(s32[2]{0:T(128)S(1)} %pad_add_fusion.index_ref, f32[128,256]{1,0:T(8,128)S(1)} %constant_dynamic-update-slice_fusion.refs_0_, f32[128,256]{1,0:T(8,128)S(1)} %collective-permute-done.7.refs_1_, ...), custom_call_target="tpu_custom_call" | custom-call | tf_op jit(solution)/shard_map/pallas_call | solution.py:128
  32.9 3.3 %collective-permute-done.11.refs_3_ = f32[64,1024]{1,0:T(8,128)S(1)} collective-permute-done((f32[64,1024]{1,0:T(8,128)S(1)}, f32[64,1024]{1,0:T(8,128)S(1)}, u32[]{:S(2)}, u32[]{:S(2)}) %collective-permute-start.11) | collective-permute-done | bytes 262176 | tf_op jit(solution)/shard_map/ppermute | solution.py:196
  36.2 0.6 shard_map.43
  36.8 1.6 %collective-permute-start.14 = (f32[32,1024]{1,0:T(8,128)S(1)}, f32[32,1024]{1,0:T(8,128)S(1)}, u32[]{:S(2)}, u32[]{:S(2)}) collective-permute-start(f32[32,1024]{1,0:T(8,128)S(1)} %get-tuple-element.41), channel_id=1, source_target_pairs={{0,4},{4,0},{8,12},{12,8},{16,20},{20,16},{24,28},{28,24},{1,5},{5... | collective-permute-start | bytes 393224 | tf_op jit(solution)/shard_map/ppermute | solution.py:196
  38.4 0.5 collective-permute-start.12
  38.9 2.4 %collective-permute-start.13 = (f32[32,1024]{1,0:T(8,128)S(1)}, f32[32,1024]{1,0:T(8,128)S(1)}, u32[]{:S(2)}, u32[]{:S(2)}) collective-permute-start(f32[32,1024]{1,0:T(8,128)S(1)} %get-tuple-element.39), channel_id=1, source_target_pairs={{0,20},{4,16},{8,28},{12,24},{16,4},{20,0},{24,12},{28,8},{1,21},{... | collective-permute-start | bytes 393224 | tf_op jit(solution)/shard_map/ppermute | solution.py:196
  41.3 2.7 %collective-permute-start.15 = (f32[32,1024]{1,0:T(8,128)S(1)}, f32[32,1024]{1,0:T(8,128)S(1)}, u32[]{:S(2)}, u32[]{:S(2)}) collective-permute-start(f32[32,1024]{1,0:T(8,128)S(1)} %get-tuple-element.43), channel_id=1, source_target_pairs={{0,8},{4,12},{8,0},{12,4},{16,24},{20,28},{24,16},{28,20},{1,9},{5... | collective-permute-start | bytes 393224 | tf_op jit(solution)/shard_map/ppermute | solution.py:196
  44.0 0.0 collective-permute-start.16
  44.0 0.0 collective-permute-done.14.refs_2_
  44.0 2.0 %collective-permute-start.17 = (f32[32,1024]{1,0:T(8,128)S(1)}, f32[32,1024]{1,0:T(8,128)S(1)}, u32[]{:S(2)}, u32[]{:S(2)}) collective-permute-start(f32[32,1024]{1,0:T(8,128)S(1)} %get-tuple-element.45), channel_id=1, source_target_pairs={{0,28},{4,24},{8,20},{12,16},{16,12},{20,8},{24,4},{28,0},{1,29},{... | collective-permute-start | bytes 393224 | tf_op jit(solution)/shard_map/ppermute | solution.py:196
  46.0 3.0 %collective-permute-done.12.refs_0_ = f32[32,1024]{1,0:T(8,128)S(1)} collective-permute-done((f32[32,1024]{1,0:T(8,128)S(1)}, f32[32,1024]{1,0:T(8,128)S(1)}, u32[]{:S(2)}, u32[]{:S(2)}) %collective-permute-start.12) | collective-permute-done | bytes 131104 | tf_op jit(solution)/shard_map/ppermute | solution.py:196
  49.0 6.8 %collective-permute-start.18 = (f32[32,1024]{1,0:T(8,128)S(1)}, f32[32,1024]{1,0:T(8,128)S(1)}, u32[]{:S(2)}, u32[]{:S(2)}) collective-permute-start(f32[32,1024]{1,0:T(8,128)S(1)} %get-tuple-element.46), channel_id=1, source_target_pairs={{0,12},{4,8},{8,4},{12,0},{16,28},{20,24},{24,20},{28,16},{1,13},{... | collective-permute-start | bytes 393224 | tf_op jit(solution)/shard_map/ppermute | solution.py:196
  55.8 0.5 collective-permute-done.13.refs_1_
  56.3 0.0 collective-permute-done.15.refs_3_
  56.3 4.9 %collective-permute-done.16.refs_4_ = f32[32,1024]{1,0:T(8,128)S(1)} collective-permute-done((f32[32,1024]{1,0:T(8,128)S(1)}, f32[32,1024]{1,0:T(8,128)S(1)}, u32[]{:S(2)}, u32[]{:S(2)}) %collective-permute-start.16) | collective-permute-done | bytes 131104 | tf_op jit(solution)/shard_map/ppermute | solution.py:196
  61.3 2.7 %collective-permute-done.17.refs_5_ = f32[32,1024]{1,0:T(8,128)S(1)} collective-permute-done((f32[32,1024]{1,0:T(8,128)S(1)}, f32[32,1024]{1,0:T(8,128)S(1)}, u32[]{:S(2)}, u32[]{:S(2)}) %collective-permute-start.17) | collective-permute-done | bytes 131104 | tf_op jit(solution)/shard_map/ppermute | solution.py:196
  64.0 0.0 collective-permute-done.18.refs_6_
  64.0 0.8 %shard_map.44 = (f32[64,256]{1,0:T(8,128)}, f32[32,4096]{1,0:T(8,128)}) custom-call(f32[64,256]{1,0:T(8,128)S(1)} %get-tuple-element.31.own_ref, f32[32,1024]{1,0:T(8,128)S(1)} %collective-permute-done.12.refs_0_, f32[32,1024]{1,0:T(8,128)S(1)} %collective-permute-done.13.refs_1_, f32[32,1024]{1,0:T(8,128)S(1)} %collective-permute-done.14.refs_2_, ...), custom_call_target="tpu_custom_call" | custom-call | tf_op jit(solution)/shard_map/pallas_call | solution.py:181
  (5 shorter events, 0.0 us)
Async XLA Ops:
  3.6 4.4 %collective-permute-start.2 = (f32[64,256]{1,0:T(8,128)S(1)}, f32[64,256]{1,0:T(8,128)S(1)}, u32[]{:S(2)}, u32[]{:S(2)}) collective-permute-start(f32[64,256]{1,0:T(8,128)S(1)} %get-tuple-element.25), channel_id=1, source_target_pairs={{0,3},{1,2},{2,1},{3,0},{4,7},{5,6},{6,5},{7,4},{8,11},{9,10},{10,... | collective-permute-start | bytes 196616 | tf_op jit(solution)/shard_map/ppermute | solution.py:196
  4.6 4.8 %collective-permute-start.1 = (f32[64,256]{1,0:T(8,128)S(1)}, f32[64,256]{1,0:T(8,128)S(1)}, u32[]{:S(2)}, u32[]{:S(2)}) collective-permute-start(f32[64,256]{1,0:T(8,128)S(1)} %get-tuple-element.25), channel_id=1, source_target_pairs={{0,2},{1,3},{2,0},{3,1},{4,6},{5,7},{6,4},{7,5},{8,10},{9,11},{10,... | collective-permute-start | bytes 196616 | tf_op jit(solution)/shard_map/ppermute | solution.py:196
  5.2 4.2 %collective-permute-start = (f32[64,256]{1,0:T(8,128)S(1)}, f32[64,256]{1,0:T(8,128)S(1)}, u32[]{:S(2)}, u32[]{:S(2)}) collective-permute-start(f32[64,256]{1,0:T(8,128)S(1)} %get-tuple-element.25), channel_id=1, source_target_pairs={{0,1},{1,0},{2,3},{3,2},{4,5},{5,4},{6,7},{7,6},{8,9},{9,8},{10,11... | collective-permute-start | bytes 196616 | tf_op jit(solution)/shard_map/ppermute | solution.py:196
  5.5 8.5 %collective-permute-start.3 = (f32[64,1024]{1,0:T(8,128)S(1)}, f32[64,1024]{1,0:T(8,128)S(1)}, u32[]{:S(2)}, u32[]{:S(2)}) collective-permute-start(f32[64,1024]{1,0:T(8,128)S(1)} %get-tuple-element.26), channel_id=1, source_target_pairs={{0,4},{4,0},{8,12},{12,8},{16,20},{20,16},{24,28},{28,24},{1,5},{5... | collective-permute-start | bytes 786440 | tf_op jit(solution)/shard_map/ppermute | solution.py:196
  7.0 8.2 %collective-permute-start.4 = (f32[64,1024]{1,0:T(8,128)S(1)}, f32[64,1024]{1,0:T(8,128)S(1)}, u32[]{:S(2)}, u32[]{:S(2)}) collective-permute-start(f32[64,1024]{1,0:T(8,128)S(1)} %get-tuple-element.27), channel_id=1, source_target_pairs={{0,8},{4,12},{8,0},{12,4},{16,24},{20,28},{24,16},{28,20},{1,9},{5... | collective-permute-start | bytes 786440 | tf_op jit(solution)/shard_map/ppermute | solution.py:196
  15.2 6.9 %collective-permute-start.5 = (f32[64,256]{1,0:T(8,128)S(1)}, f32[64,256]{1,0:T(8,128)S(1)}, u32[]{:S(2)}, u32[]{:S(2)}) collective-permute-start(f32[64,256]{1,0:T(8,128)S(1)} %add_add_fusion), channel_id=1, source_target_pairs={{0,16},{1,21},{2,18},{3,23},{4,20},{5,17},{6,22},{7,19},{8,24},{9,... | collective-permute-start | bytes 196616 | tf_op jit(solution)/shard_map/ppermute | solution.py:207
  17.8 11.6 %collective-permute-start.9 = (f32[64,256]{1,0:T(8,128)S(1)}, f32[64,256]{1,0:T(8,128)S(1)}, u32[]{:S(2)}, u32[]{:S(2)}) collective-permute-start(f32[64,256]{1,0:T(8,128)S(1)} %add_add_fusion), channel_id=1, source_target_pairs={{0,12},{2,14},{4,8},{6,10},{8,4},{10,6},{12,0},{14,2},{16,28},{18,... | collective-permute-start | bytes 196616 | tf_op jit(solution)/shard_map/ppermute | solution.py:207
  20.1 9.3 %collective-permute-start.8 = (f32[64,256]{1,0:T(8,128)S(1)}, f32[64,256]{1,0:T(8,128)S(1)}, u32[]{:S(2)}, u32[]{:S(2)}) collective-permute-start(f32[64,256]{1,0:T(8,128)S(1)} %add_add_fusion), channel_id=1, source_target_pairs={{0,4},{1,9},{2,6},{3,11},{4,0},{5,13},{6,2},{7,15},{8,12},{9,1},{1... | collective-permute-start | bytes 196616 | tf_op jit(solution)/shard_map/ppermute | solution.py:207
  21.6 4.3 %collective-permute-start.6 = (f32[64,256]{1,0:T(8,128)S(1)}, f32[64,256]{1,0:T(8,128)S(1)}, u32[]{:S(2)}, u32[]{:S(2)}) collective-permute-start(f32[64,256]{1,0:T(8,128)S(1)} %add_add_fusion), channel_id=1, source_target_pairs={{0,24},{1,29},{2,26},{3,31},{4,28},{5,25},{6,30},{7,27},{8,16},{9,... | collective-permute-start | bytes 196616 | tf_op jit(solution)/shard_map/ppermute | solution.py:207
  25.9 3.8 %collective-permute-start.7 = (f32[128,256]{1,0:T(8,128)S(1)}, f32[128,256]{1,0:T(8,128)S(1)}, u32[]{:S(2)}, u32[]{:S(2)}) collective-permute-start(f32[128,256]{1,0:T(8,128)S(1)} %constant_dynamic-update-slice_fusion.refs_0_), channel_id=1, source_target_pairs={{0,1},{1,0},{2,3},{3,2},{4,5},{5,4},{6,7},{7,6},{8,9},{9,8},{10,11... | collective-permute-start | bytes 393224 | tf_op jit(solution)/shard_map/ppermute | solution.py:196
  25.9 10.3 %collective-permute-start.11 = (f32[64,1024]{1,0:T(8,128)S(1)}, f32[64,1024]{1,0:T(8,128)S(1)}, u32[]{:S(2)}, u32[]{:S(2)}) collective-permute-start(f32[64,1024]{1,0:T(8,128)S(1)} %get-tuple-element.37), channel_id=1, source_target_pairs={{0,12},{4,8},{8,4},{12,0},{16,28},{20,24},{24,20},{28,16},{1,13},{... | collective-permute-start | bytes 786440 | tf_op jit(solution)/shard_map/ppermute | solution.py:196
  29.4 1.4 %collective-permute-start.10 = (f32[128,256]{1,0:T(8,128)S(1)}, f32[128,256]{1,0:T(8,128)S(1)}, u32[]{:S(2)}, u32[]{:S(2)}) collective-permute-start(f32[128,256]{1,0:T(8,128)S(1)} %pad_maximum_fusion.refs_2_), channel_id=1, source_target_pairs={{0,1},{1,0},{2,3},{3,2},{4,5},{5,4},{6,7},{7,6},{8,9},{9,8},{10,11... | collective-permute-start | bytes 393224 | tf_op jit(solution)/shard_map/ppermute | solution.py:196
  36.8 7.1 %collective-permute-start.14 = (f32[32,1024]{1,0:T(8,128)S(1)}, f32[32,1024]{1,0:T(8,128)S(1)}, u32[]{:S(2)}, u32[]{:S(2)}) collective-permute-start(f32[32,1024]{1,0:T(8,128)S(1)} %get-tuple-element.41), channel_id=1, source_target_pairs={{0,4},{4,0},{8,12},{12,8},{16,20},{20,16},{24,28},{28,24},{1,5},{5... | collective-permute-start | bytes 393224 | tf_op jit(solution)/shard_map/ppermute | solution.py:196
  38.4 10.6 %collective-permute-start.12 = (f32[32,1024]{1,0:T(8,128)S(1)}, f32[32,1024]{1,0:T(8,128)S(1)}, u32[]{:S(2)}, u32[]{:S(2)}) collective-permute-start(f32[32,1024]{1,0:T(8,128)S(1)} %get-tuple-element.38), channel_id=1, source_target_pairs={{0,16},{4,20},{8,24},{12,28},{16,0},{20,4},{24,8},{28,12},{1,17},{... | collective-permute-start | bytes 393224 | tf_op jit(solution)/shard_map/ppermute | solution.py:196
  38.9 17.4 %collective-permute-start.13 = (f32[32,1024]{1,0:T(8,128)S(1)}, f32[32,1024]{1,0:T(8,128)S(1)}, u32[]{:S(2)}, u32[]{:S(2)}) collective-permute-start(f32[32,1024]{1,0:T(8,128)S(1)} %get-tuple-element.39), channel_id=1, source_target_pairs={{0,20},{4,16},{8,28},{12,24},{16,4},{20,0},{24,12},{28,8},{1,21},{... | collective-permute-start | bytes 393224 | tf_op jit(solution)/shard_map/ppermute | solution.py:196
  41.3 15.0 %collective-permute-start.15 = (f32[32,1024]{1,0:T(8,128)S(1)}, f32[32,1024]{1,0:T(8,128)S(1)}, u32[]{:S(2)}, u32[]{:S(2)}) collective-permute-start(f32[32,1024]{1,0:T(8,128)S(1)} %get-tuple-element.43), channel_id=1, source_target_pairs={{0,8},{4,12},{8,0},{12,4},{16,24},{20,28},{24,16},{28,20},{1,9},{5... | collective-permute-start | bytes 393224 | tf_op jit(solution)/shard_map/ppermute | solution.py:196
  44.0 17.3 %collective-permute-start.16 = (f32[32,1024]{1,0:T(8,128)S(1)}, f32[32,1024]{1,0:T(8,128)S(1)}, u32[]{:S(2)}, u32[]{:S(2)}) collective-permute-start(f32[32,1024]{1,0:T(8,128)S(1)} %get-tuple-element.44), channel_id=1, source_target_pairs={{0,24},{4,28},{8,16},{12,20},{16,8},{20,12},{24,0},{28,4},{1,25},{... | collective-permute-start | bytes 393224 | tf_op jit(solution)/shard_map/ppermute | solution.py:196
  44.0 20.0 %collective-permute-start.17 = (f32[32,1024]{1,0:T(8,128)S(1)}, f32[32,1024]{1,0:T(8,128)S(1)}, u32[]{:S(2)}, u32[]{:S(2)}) collective-permute-start(f32[32,1024]{1,0:T(8,128)S(1)} %get-tuple-element.45), channel_id=1, source_target_pairs={{0,28},{4,24},{8,20},{12,16},{16,12},{20,8},{24,4},{28,0},{1,29},{... | collective-permute-start | bytes 393224 | tf_op jit(solution)/shard_map/ppermute | solution.py:196
  49.0 15.0 %collective-permute-start.18 = (f32[32,1024]{1,0:T(8,128)S(1)}, f32[32,1024]{1,0:T(8,128)S(1)}, u32[]{:S(2)}, u32[]{:S(2)}) collective-permute-start(f32[32,1024]{1,0:T(8,128)S(1)} %get-tuple-element.46), channel_id=1, source_target_pairs={{0,12},{4,8},{8,4},{12,0},{16,28},{20,24},{24,20},{28,16},{1,13},{... | collective-permute-start | bytes 393224 | tf_op jit(solution)/shard_map/ppermute | solution.py:196

commit v23 on v21

--- a/solution.py
+++ b/solution.py
@@ -234,7 +234,7 @@
     blocks = list(load(high_t, low_t, parts, times))
     terms = [blocks[0]] + [None] * (times - 1)
     near, far = list(range(1, group)), list(range(group, times))
-    sequence = [*far[:2], *near[:2], *far[2:], *near[2:], 0]
+    sequence = [*far, *near, 0]
     for k in sequence[:-1]:
         if k == near[-1]:
             blocks[k], terms[1] = lax.optimization_barrier((blocks[k], terms[1]))

time: 55.6 us -> 56.3 us (1.013)
  starting transfers between devices: 22.6 us -> 24.5 us
  waiting for transfers between devices: 25.2 us -> 23.5 us
    ppermute x19, starting transfers between devices: 22.6 us -> 24.5 us  [swap(): lax.ppermute(value, axis, [(i, i ^ offset) for i in range(lax.axis_size(a...]
    ppermute x19, waiting for transfers between devices: 25.2 us -> 23.5 us  [swap(): lax.ppermute(value, axis, [(i, i ^ offset) for i in range(lax.axis_size(a...]
  transfers between devices with their start and end apart: 19 -> 19, of which waited for: 9 -> 8; matrix products, arithmetic and copies ran while one was open for 0% -> 0% of each run, Pallas kernels for 4% -> 4%
where the time goes in v23:
time: 56.3 us; the launch traced here: 55.2 us
  starting transfers between devices  24.5 us (44%)
  waiting for transfers between devices  23.5 us (42%)
  Pallas kernels  6.51 us (12%)
  between operations  0.7 us (1%)
    ppermute x19, starting transfers between devices, swap(): lax.ppermute(value, axis, [(i, i ^ offset) for i in range(lax.axis_size(a...  24.5 us
    ppermute x19, waiting for transfers between devices, swap(): lax.ppermute(value, axis, [(i, i ^ offset) for i in range(lax.axis_size(a...  23.5 us
    pallas_call x1, Pallas kernels, project(): pl.pallas_call(functools.partial(project_kernel, depth), in_specs=[HBM, H...  2.93 us
    pallas_call x1, Pallas kernels, mix(): pl.pallas_call(functools.partial(mix_kernel, times, order), in_specs=[SME...  2.15 us
  transfers between devices with their start and end apart: 19, of which 8 were waited for; matrix products, arithmetic and copies ran while one was open for 0% of the time, Pallas kernels for 4%

profile of v23, /device:TPU:8, one launch (start us, length us, event | category | flops | bytes accessed | tf_op | source)
XLA Modules:
  0.0 55.2 jit_solution(15035031018771314394)
XLA Ops:
  0.6 2.9 %shard_map.41 = (f32[32,256]{1,0:T(8,128)S(1)}, f32[32,256]{1,0:T(8,128)S(1)}, f32[64,1024]{1,0:T(8,128)S(1)}, f32[64,1024]{1,0:T(8,128)S(1)}, f32[64,1024]{1,0:T(8,128)S(1)}, /*index=5*/f32[64,1024]{1,0:T(8,128)S(1)}) custom-call(f32[64,4096]{1,0:T(8,128)} %snapshots_ref.1, f32[4096,256]{1,0:T(8,128)} %factor_ref.1), custom_call_target="tpu_custom_call" | custom-call | tf_op jit(solution)/shard_map/pallas_call | solution.py:76
  3.6 1.6 %collective-permute-start.1 = (f32[32,256]{1,0:T(8,128)S(1)}, f32[32,256]{1,0:T(8,128)S(1)}, u32[]{:S(2)}, u32[]{:S(2)}) collective-permute-start(f32[32,256]{1,0:T(8,128)S(1)} %get-tuple-element.24), channel_id=1, source_target_pairs={{0,2},{1,3},{2,0},{3,1},{4,6},{5,7},{6,4},{7,5},{8,10},{9,11},{10,... | collective-permute-start | bytes 98312 | tf_op jit(solution)/shard_map/ppermute | solution.py:205
  5.1 0.0 collective-permute-start.2
  5.2 0.6 %collective-permute-start = (f32[32,256]{1,0:T(8,128)S(1)}, f32[32,256]{1,0:T(8,128)S(1)}, u32[]{:S(2)}, u32[]{:S(2)}) collective-permute-start(f32[32,256]{1,0:T(8,128)S(1)} %get-tuple-element.25), channel_id=1, source_target_pairs={{0,1},{1,0},{2,3},{3,2},{4,5},{5,4},{6,7},{7,6},{8,9},{9,8},{10,11... | collective-permute-start | bytes 98312 | tf_op jit(solution)/shard_map/ppermute | solution.py:205
  5.8 1.5 %collective-permute-start.6 = (f32[64,1024]{1,0:T(8,128)S(1)}, f32[64,1024]{1,0:T(8,128)S(1)}, u32[]{:S(2)}, u32[]{:S(2)}) collective-permute-start(f32[64,1024]{1,0:T(8,128)S(1)} %get-tuple-element.26), channel_id=1, source_target_pairs={{0,4},{4,0},{8,12},{12,8},{16,20},{20,16},{24,28},{28,24},{1,5},{5... | collective-permute-start | bytes 786440 | tf_op jit(solution)/shard_map/ppermute | solution.py:205
  7.3 0.5 collective-permute-start.7
  7.7 0.0 collective-permute-done.1
  7.7 0.9 %collective-permute-done.2 = f32[32,256]{1,0:T(8,128)S(1)} collective-permute-done((f32[32,256]{1,0:T(8,128)S(1)}, f32[32,256]{1,0:T(8,128)S(1)}, u32[]{:S(2)}, u32[]{:S(2)}) %collective-permute-start.2) | collective-permute-done | bytes 32800 | tf_op jit(solution)/shard_map/ppermute | solution.py:205
  8.6 0.0 collective-permute-done
  8.6 3.6 %collective-permute-start.5 = (f32[32,256]{1,0:T(8,128)S(1)}, f32[32,256]{1,0:T(8,128)S(1)}, u32[]{:S(2)}, u32[]{:S(2)}) collective-permute-start(f32[32,256]{1,0:T(8,128)S(1)} %add_add_fusion), channel_id=1, source_target_pairs={{0,20},{4,16},{8,28},{12,24},{16,4},{20,0},{24,12},{28,8},{1,21},{... | collective-permute-start | bytes 98312 | tf_op jit(solution)/shard_map/ppermute | solution.py:205
  12.2 0.3 collective-permute-start.4
  12.5 0.5 collective-permute-start.3
  13.0 4.2 %collective-permute-done.5 = f32[32,256]{1,0:T(8,128)S(1)} collective-permute-done((f32[32,256]{1,0:T(8,128)S(1)}, f32[32,256]{1,0:T(8,128)S(1)}, u32[]{:S(2)}, u32[]{:S(2)}) %collective-permute-start.5) | collective-permute-done | bytes 32800 | tf_op jit(solution)/shard_map/ppermute | solution.py:205
  17.2 0.4 collective-permute-done.4
  17.6 0.0 collective-permute-done.3
  17.6 0.0 collective-permute-done.6.refs_1_
  17.6 0.0 collective-permute-done.7.refs_2_
  17.7 0.2 collective-permute-start.9
  17.9 2.4 %collective-permute-start.11 = (f32[64,1024]{1,0:T(8,128)S(1)}, f32[64,1024]{1,0:T(8,128)S(1)}, u32[]{:S(2)}, u32[]{:S(2)}) collective-permute-start(f32[64,1024]{1,0:T(8,128)S(1)} %get-tuple-element.35), channel_id=1, source_target_pairs={{0,12},{4,8},{8,4},{12,0},{16,28},{20,24},{24,20},{28,16},{1,13},{... | collective-permute-start | bytes 786440 | tf_op jit(solution)/shard_map/ppermute | solution.py:205
  20.3 0.0 collective-permute-start.8
  20.3 3.9 %collective-permute-done.9.refs_2_ = f32[128,256]{1,0:T(8,128)S(1)} collective-permute-done((f32[128,256]{1,0:T(8,128)S(1)}, f32[128,256]{1,0:T(8,128)S(1)}, u32[]{:S(2)}, u32[]{:S(2)}) %collective-permute-start.9) | collective-permute-done | bytes 131104 | tf_op jit(solution)/shard_map/ppermute | solution.py:205
  24.2 0.0 collective-permute-start.10
  24.2 0.1 pad_add_fusion.index_ref
  24.2 0.0 collective-permute-done.8.refs_1_
  24.2 1.3 %collective-permute-done.10.refs_3_ = f32[128,256]{1,0:T(8,128)S(1)} collective-permute-done((f32[128,256]{1,0:T(8,128)S(1)}, f32[128,256]{1,0:T(8,128)S(1)}, u32[]{:S(2)}, u32[]{:S(2)}) %collective-permute-start.10) | collective-permute-done | bytes 131104 | tf_op jit(solution)/shard_map/ppermute | solution.py:205
  25.5 2.1 %shard_map.42 = (bf16[256,256]{1,0:T(8,128)(2,1)S(1)}, bf16[256,256]{1,0:T(8,128)(2,1)S(1)}, f32[64,256]{1,0:T(8,128)S(1)}) custom-call(s32[2]{0:T(128)S(1)} %pad_add_fusion.index_ref, f32[128,256]{1,0:T(8,128)S(1)} %pad_maximum_fusion.refs_0_, f32[128,256]{1,0:T(8,128)S(1)} %collective-permute-done.8.refs_1_, ...), custom_call_target="tpu_custom_call" | custom-call | tf_op jit(solution)/shard_map/pallas_call | solution.py:137
  27.7 0.0 collective-permute-done.11.refs_3_
  27.7 0.6 %shard_map.43 = (f32[32,1024]{1,0:T(8,128)S(1)}, f32[32,1024]{1,0:T(8,128)S(1)}, f32[32,1024]{1,0:T(8,128)S(1)}, f32[32,1024]{1,0:T(8,128)S(1)}, f32[32,1024]{1,...) custom-call(bf16[256,256]{1,0:T(8,128)(2,1)S(1)} %get-tuple-element.30.high_ref, ...), custom_call_target="tpu_custom_call" | custom-call | tf_op jit(solution)/shard_map/pallas_call | solution.py:159
  28.3 1.1 %collective-permute-start.16 = (f32[32,1024]{1,0:T(8,128)S(1)}, f32[32,1024]{1,0:T(8,128)S(1)}, u32[]{:S(2)}, u32[]{:S(2)}) collective-permute-start(f32[32,1024]{1,0:T(8,128)S(1)} %get-tuple-element.41), channel_id=1, source_target_pairs={{0,4},{4,0},{8,12},{12,8},{16,20},{20,16},{24,28},{28,24},{1,5},{5... | collective-permute-start | bytes 393224 | tf_op jit(solution)/shard_map/ppermute | solution.py:205
  29.4 1.8 %collective-permute-start.12 = (f32[32,1024]{1,0:T(8,128)S(1)}, f32[32,1024]{1,0:T(8,128)S(1)}, u32[]{:S(2)}, u32[]{:S(2)}) collective-permute-start(f32[32,1024]{1,0:T(8,128)S(1)} %get-tuple-element.36), channel_id=1, source_target_pairs={{0,16},{4,20},{8,24},{12,28},{16,0},{20,4},{24,8},{28,12},{1,17},{... | collective-permute-start | bytes 393224 | tf_op jit(solution)/shard_map/ppermute | solution.py:205
  31.2 1.5 %collective-permute-start.13 = (f32[32,1024]{1,0:T(8,128)S(1)}, f32[32,1024]{1,0:T(8,128)S(1)}, u32[]{:S(2)}, u32[]{:S(2)}) collective-permute-start(f32[32,1024]{1,0:T(8,128)S(1)} %get-tuple-element.37), channel_id=1, source_target_pairs={{0,20},{4,16},{8,28},{12,24},{16,4},{20,0},{24,12},{28,8},{1,21},{... | collective-permute-start | bytes 393224 | tf_op jit(solution)/shard_map/ppermute | solution.py:205
  32.7 1.2 %collective-permute-start.14 = (f32[32,1024]{1,0:T(8,128)S(1)}, f32[32,1024]{1,0:T(8,128)S(1)}, u32[]{:S(2)}, u32[]{:S(2)}) collective-permute-start(f32[32,1024]{1,0:T(8,128)S(1)} %get-tuple-element.38), channel_id=1, source_target_pairs={{0,24},{4,28},{8,16},{12,20},{16,8},{20,12},{24,0},{28,4},{1,25},{... | collective-permute-start | bytes 393224 | tf_op jit(solution)/shard_map/ppermute | solution.py:205
  33.9 1.4 %collective-permute-start.15 = (f32[32,1024]{1,0:T(8,128)S(1)}, f32[32,1024]{1,0:T(8,128)S(1)}, u32[]{:S(2)}, u32[]{:S(2)}) collective-permute-start(f32[32,1024]{1,0:T(8,128)S(1)} %get-tuple-element.39), channel_id=1, source_target_pairs={{0,28},{4,24},{8,20},{12,16},{16,12},{20,8},{24,4},{28,0},{1,29},{... | collective-permute-start | bytes 393224 | tf_op jit(solution)/shard_map/ppermute | solution.py:205
  35.3 0.0 collective-permute-done.16.refs_4_
  35.3 2.3 %collective-permute-start.17 = (f32[32,1024]{1,0:T(8,128)S(1)}, f32[32,1024]{1,0:T(8,128)S(1)}, u32[]{:S(2)}, u32[]{:S(2)}) collective-permute-start(f32[32,1024]{1,0:T(8,128)S(1)} %get-tuple-element.43), channel_id=1, source_target_pairs={{0,8},{4,12},{8,0},{12,4},{16,24},{20,28},{24,16},{28,20},{1,9},{5... | collective-permute-start | bytes 393224 | tf_op jit(solution)/shard_map/ppermute | solution.py:205
  37.6 7.3 %collective-permute-done.12.refs_0_ = f32[32,1024]{1,0:T(8,128)S(1)} collective-permute-done((f32[32,1024]{1,0:T(8,128)S(1)}, f32[32,1024]{1,0:T(8,128)S(1)}, u32[]{:S(2)}, u32[]{:S(2)}) %collective-permute-start.12) | collective-permute-done | bytes 131104 | tf_op jit(solution)/shard_map/ppermute | solution.py:205
  44.9 3.9 %collective-permute-start.18 = (f32[32,1024]{1,0:T(8,128)S(1)}, f32[32,1024]{1,0:T(8,128)S(1)}, u32[]{:S(2)}, u32[]{:S(2)}) collective-permute-start(f32[32,1024]{1,0:T(8,128)S(1)} %get-tuple-element.44), channel_id=1, source_target_pairs={{0,12},{4,8},{8,4},{12,0},{16,28},{20,24},{24,20},{28,16},{1,13},{... | collective-permute-start | bytes 393224 | tf_op jit(solution)/shard_map/ppermute | solution.py:205
  48.7 0.0 collective-permute-done.13.refs_1_
  48.8 3.7 %collective-permute-done.14.refs_2_ = f32[32,1024]{1,0:T(8,128)S(1)} collective-permute-done((f32[32,1024]{1,0:T(8,128)S(1)}, f32[32,1024]{1,0:T(8,128)S(1)}, u32[]{:S(2)}, u32[]{:S(2)}) %collective-permute-start.14) | collective-permute-done | bytes 131104 | tf_op jit(solution)/shard_map/ppermute | solution.py:205
  52.4 1.9 %collective-permute-done.15.refs_3_ = f32[32,1024]{1,0:T(8,128)S(1)} collective-permute-done((f32[32,1024]{1,0:T(8,128)S(1)}, f32[32,1024]{1,0:T(8,128)S(1)}, u32[]{:S(2)}, u32[]{:S(2)}) %collective-permute-start.15) | collective-permute-done | bytes 131104 | tf_op jit(solution)/shard_map/ppermute | solution.py:205
  54.4 0.0 collective-permute-done.17.refs_5_
  54.4 0.0 collective-permute-done.18.refs_6_
  54.4 0.8 %shard_map.44 = (f32[64,256]{1,0:T(8,128)}, f32[32,4096]{1,0:T(8,128)}) custom-call(f32[64,256]{1,0:T(8,128)S(1)} %get-tuple-element.29.own_ref, f32[32,1024]{1,0:T(8,128)S(1)} %collective-permute-done.12.refs_0_, f32[32,1024]{1,0:T(8,128)S(1)} %collective-permute-done.13.refs_1_, f32[32,1024]{1,0:T(8,128)S(1)} %collective-permute-done.14.refs_2_, ...), custom_call_target="tpu_custom_call" | custom-call | tf_op jit(solution)/shard_map/pallas_call | solution.py:190
  (2 shorter events, 0.0 us)
Async XLA Ops:
  3.6 4.2 %collective-permute-start.1 = (f32[32,256]{1,0:T(8,128)S(1)}, f32[32,256]{1,0:T(8,128)S(1)}, u32[]{:S(2)}, u32[]{:S(2)}) collective-permute-start(f32[32,256]{1,0:T(8,128)S(1)} %get-tuple-element.24), channel_id=1, source_target_pairs={{0,2},{1,3},{2,0},{3,1},{4,6},{5,7},{6,4},{7,5},{8,10},{9,11},{10,... | collective-permute-start | bytes 98312 | tf_op jit(solution)/shard_map/ppermute | solution.py:205
  5.1 3.4 %collective-permute-start.2 = (f32[32,256]{1,0:T(8,128)S(1)}, f32[32,256]{1,0:T(8,128)S(1)}, u32[]{:S(2)}, u32[]{:S(2)}) collective-permute-start(f32[32,256]{1,0:T(8,128)S(1)} %get-tuple-element.25), channel_id=1, source_target_pairs={{0,3},{1,2},{2,1},{3,0},{4,7},{5,6},{6,5},{7,4},{8,11},{9,10},{10,... | collective-permute-start | bytes 98312 | tf_op jit(solution)/shard_map/ppermute | solution.py:205
  5.2 3.4 %collective-permute-start = (f32[32,256]{1,0:T(8,128)S(1)}, f32[32,256]{1,0:T(8,128)S(1)}, u32[]{:S(2)}, u32[]{:S(2)}) collective-permute-start(f32[32,256]{1,0:T(8,128)S(1)} %get-tuple-element.25), channel_id=1, source_target_pairs={{0,1},{1,0},{2,3},{3,2},{4,5},{5,4},{6,7},{7,6},{8,9},{9,8},{10,11... | collective-permute-start | bytes 98312 | tf_op jit(solution)/shard_map/ppermute | solution.py:205
  5.8 11.9 %collective-permute-start.6 = (f32[64,1024]{1,0:T(8,128)S(1)}, f32[64,1024]{1,0:T(8,128)S(1)}, u32[]{:S(2)}, u32[]{:S(2)}) collective-permute-start(f32[64,1024]{1,0:T(8,128)S(1)} %get-tuple-element.26), channel_id=1, source_target_pairs={{0,4},{4,0},{8,12},{12,8},{16,20},{20,16},{24,28},{28,24},{1,5},{5... | collective-permute-start | bytes 786440 | tf_op jit(solution)/shard_map/ppermute | solution.py:205
  7.3 10.4 %collective-permute-start.7 = (f32[64,1024]{1,0:T(8,128)S(1)}, f32[64,1024]{1,0:T(8,128)S(1)}, u32[]{:S(2)}, u32[]{:S(2)}) collective-permute-start(f32[64,1024]{1,0:T(8,128)S(1)} %get-tuple-element.27), channel_id=1, source_target_pairs={{0,8},{4,12},{8,0},{12,4},{16,24},{20,28},{24,16},{28,20},{1,9},{5... | collective-permute-start | bytes 786440 | tf_op jit(solution)/shard_map/ppermute | solution.py:205
  8.6 8.6 %collective-permute-start.5 = (f32[32,256]{1,0:T(8,128)S(1)}, f32[32,256]{1,0:T(8,128)S(1)}, u32[]{:S(2)}, u32[]{:S(2)}) collective-permute-start(f32[32,256]{1,0:T(8,128)S(1)} %add_add_fusion), channel_id=1, source_target_pairs={{0,20},{4,16},{8,28},{12,24},{16,4},{20,0},{24,12},{28,8},{1,21},{... | collective-permute-start | bytes 98312 | tf_op jit(solution)/shard_map/ppermute | solution.py:205
  12.2 5.4 %collective-permute-start.4 = (f32[32,256]{1,0:T(8,128)S(1)}, f32[32,256]{1,0:T(8,128)S(1)}, u32[]{:S(2)}, u32[]{:S(2)}) collective-permute-start(f32[32,256]{1,0:T(8,128)S(1)} %add_add_fusion), channel_id=1, source_target_pairs={{0,16},{4,20},{8,24},{12,28},{16,0},{20,4},{24,8},{28,12},{1,17},{... | collective-permute-start | bytes 98312 | tf_op jit(solution)/shard_map/ppermute | solution.py:205
  12.5 5.1 %collective-permute-start.3 = (f32[32,256]{1,0:T(8,128)S(1)}, f32[32,256]{1,0:T(8,128)S(1)}, u32[]{:S(2)}, u32[]{:S(2)}) collective-permute-start(f32[32,256]{1,0:T(8,128)S(1)} %add_add_fusion), channel_id=1, source_target_pairs={{0,4},{4,0},{8,12},{12,8},{16,20},{20,16},{24,28},{28,24},{1,5},{5... | collective-permute-start | bytes 98312 | tf_op jit(solution)/shard_map/ppermute | solution.py:205
  17.7 6.5 %collective-permute-start.9 = (f32[128,256]{1,0:T(8,128)S(1)}, f32[128,256]{1,0:T(8,128)S(1)}, u32[]{:S(2)}, u32[]{:S(2)}) collective-permute-start(f32[128,256]{1,0:T(8,128)S(1)} %pad_maximum_fusion.refs_0_), channel_id=1, source_target_pairs={{0,8},{4,12},{8,0},{12,4},{16,24},{20,28},{24,16},{28,20},{1,9},{5... | collective-permute-start | bytes 393224 | tf_op jit(solution)/shard_map/ppermute | solution.py:205
  17.9 9.8 %collective-permute-start.11 = (f32[64,1024]{1,0:T(8,128)S(1)}, f32[64,1024]{1,0:T(8,128)S(1)}, u32[]{:S(2)}, u32[]{:S(2)}) collective-permute-start(f32[64,1024]{1,0:T(8,128)S(1)} %get-tuple-element.35), channel_id=1, source_target_pairs={{0,12},{4,8},{8,4},{12,0},{16,28},{20,24},{24,20},{28,16},{1,13},{... | collective-permute-start | bytes 786440 | tf_op jit(solution)/shard_map/ppermute | solution.py:205
  20.3 3.9 %collective-permute-start.8 = (f32[128,256]{1,0:T(8,128)S(1)}, f32[128,256]{1,0:T(8,128)S(1)}, u32[]{:S(2)}, u32[]{:S(2)}) collective-permute-start(f32[128,256]{1,0:T(8,128)S(1)} %pad_maximum_fusion.refs_0_), channel_id=1, source_target_pairs={{0,1},{1,0},{2,3},{3,2},{4,5},{5,4},{6,7},{7,6},{8,9},{9,8},{10,11... | collective-permute-start | bytes 393224 | tf_op jit(solution)/shard_map/ppermute | solution.py:205
  24.2 1.3 %collective-permute-start.10 = (f32[128,256]{1,0:T(8,128)S(1)}, f32[128,256]{1,0:T(8,128)S(1)}, u32[]{:S(2)}, u32[]{:S(2)}) collective-permute-start(f32[128,256]{1,0:T(8,128)S(1)} %collective-permute-done.9.refs_2_), channel_id=1, source_target_pairs={{0,1},{1,0},{2,3},{3,2},{4,5},{5,4},{6,7},{7,6},{8,9},{9,8},{10,11... | collective-permute-start | bytes 393224 | tf_op jit(solution)/shard_map/ppermute | solution.py:205
  28.3 7.0 %collective-permute-start.16 = (f32[32,1024]{1,0:T(8,128)S(1)}, f32[32,1024]{1,0:T(8,128)S(1)}, u32[]{:S(2)}, u32[]{:S(2)}) collective-permute-start(f32[32,1024]{1,0:T(8,128)S(1)} %get-tuple-element.41), channel_id=1, source_target_pairs={{0,4},{4,0},{8,12},{12,8},{16,20},{20,16},{24,28},{28,24},{1,5},{5... | collective-permute-start | bytes 393224 | tf_op jit(solution)/shard_map/ppermute | solution.py:205
  29.4 15.5 %collective-permute-start.12 = (f32[32,1024]{1,0:T(8,128)S(1)}, f32[32,1024]{1,0:T(8,128)S(1)}, u32[]{:S(2)}, u32[]{:S(2)}) collective-permute-start(f32[32,1024]{1,0:T(8,128)S(1)} %get-tuple-element.36), channel_id=1, source_target_pairs={{0,16},{4,20},{8,24},{12,28},{16,0},{20,4},{24,8},{28,12},{1,17},{... | collective-permute-start | bytes 393224 | tf_op jit(solution)/shard_map/ppermute | solution.py:205
  31.2 17.6 %collective-permute-start.13 = (f32[32,1024]{1,0:T(8,128)S(1)}, f32[32,1024]{1,0:T(8,128)S(1)}, u32[]{:S(2)}, u32[]{:S(2)}) collective-permute-start(f32[32,1024]{1,0:T(8,128)S(1)} %get-tuple-element.37), channel_id=1, source_target_pairs={{0,20},{4,16},{8,28},{12,24},{16,4},{20,0},{24,12},{28,8},{1,21},{... | collective-permute-start | bytes 393224 | tf_op jit(solution)/shard_map/ppermute | solution.py:205
  32.7 19.7 %collective-permute-start.14 = (f32[32,1024]{1,0:T(8,128)S(1)}, f32[32,1024]{1,0:T(8,128)S(1)}, u32[]{:S(2)}, u32[]{:S(2)}) collective-permute-start(f32[32,1024]{1,0:T(8,128)S(1)} %get-tuple-element.38), channel_id=1, source_target_pairs={{0,24},{4,28},{8,16},{12,20},{16,8},{20,12},{24,0},{28,4},{1,25},{... | collective-permute-start | bytes 393224 | tf_op jit(solution)/shard_map/ppermute | solution.py:205
  33.9 20.5 %collective-permute-start.15 = (f32[32,1024]{1,0:T(8,128)S(1)}, f32[32,1024]{1,0:T(8,128)S(1)}, u32[]{:S(2)}, u32[]{:S(2)}) collective-permute-start(f32[32,1024]{1,0:T(8,128)S(1)} %get-tuple-element.39), channel_id=1, source_target_pairs={{0,28},{4,24},{8,20},{12,16},{16,12},{20,8},{24,4},{28,0},{1,29},{... | collective-permute-start | bytes 393224 | tf_op jit(solution)/shard_map/ppermute | solution.py:205
  35.3 19.1 %collective-permute-start.17 = (f32[32,1024]{1,0:T(8,128)S(1)}, f32[32,1024]{1,0:T(8,128)S(1)}, u32[]{:S(2)}, u32[]{:S(2)}) collective-permute-start(f32[32,1024]{1,0:T(8,128)S(1)} %get-tuple-element.43), channel_id=1, source_target_pairs={{0,8},{4,12},{8,0},{12,4},{16,24},{20,28},{24,16},{28,20},{1,9},{5... | collective-permute-start | bytes 393224 | tf_op jit(solution)/shard_map/ppermute | solution.py:205
  44.9 9.5 %collective-permute-start.18 = (f32[32,1024]{1,0:T(8,128)S(1)}, f32[32,1024]{1,0:T(8,128)S(1)}, u32[]{:S(2)}, u32[]{:S(2)}) collective-permute-start(f32[32,1024]{1,0:T(8,128)S(1)} %get-tuple-element.44), channel_id=1, source_target_pairs={{0,12},{4,8},{8,4},{12,0},{16,28},{20,24},{24,20},{28,16},{1,13},{... | collective-permute-start | bytes 393224 | tf_op jit(solution)/shard_map/ppermute | solution.py:205

commit v24 on v21

--- a/solution.py
+++ b/solution.py
@@ -33,23 +33,30 @@
 
 def product(left, right, dims=ROWS_BY_COLUMNS):
     (left_high, left_low), (right_high, right_low) = left, right
-    return dot(left_high, right_high, dims) + (
-        dot(left_high, right_low, dims) + dot(left_low, right_high, dims)
-    )
+    rows = left_high.shape[0]
+    both = dot(jnp.concatenate([left_high, left_low], axis=0), right_high, dims)
+    return both[:rows] + (both[rows:] + dot(left_high, right_low, dims))
 
 
 def project_kernel(depth, snapshots_ref, factor_ref, mine_ref, other_ref, *refs):
     *parts, snapshots_buf, factor_buf, sems = refs
     rows, points = snapshots_ref.shape
     half = rows // 2
-    snapshots_copy = pltpu.make_async_copy(snapshots_ref, snapshots_buf, sems.at[points // depth])
-    snapshots_copy.start()
+    count = sems.shape[0] - points // depth
+    snapshots_copies = []
+    for i in range(count):
+        span = pl.ds(i * (rows // count), rows // count)
+        snapshots_copies.append(
+            pltpu.make_async_copy(snapshots_ref.at[span, :], snapshots_buf.at[span, :], sems.at[points // depth + i])
+        )
+        snapshots_copies[-1].start()
     copies = []
     for i, start in enumerate(range(0, points, depth)):
         span = pl.ds(start, depth)
         copies.append(pltpu.make_async_copy(factor_ref.at[span, :], factor_buf.at[span, :], sems.at[i]))
         copies[-1].start()
-    snapshots_copy.wait()
+    for copy in snapshots_copies:
+        copy.wait()
     width = parts[0].shape[1]
     member = lax.rem(lax.axis_index("tm"), len(parts))
     for k, part in enumerate(parts):
@@ -70,7 +77,8 @@
 def project(snapshots, space_factor, group):
     rows, points = snapshots.shape
     rank = space_factor.shape[1]
-    depth = min(512, points)
+    depth = min(256, points)
+    count = 4 if rows % 32 == 0 else 1
     half = jax.ShapeDtypeStruct((rows // 2, rank), jnp.float32)
     part = jax.ShapeDtypeStruct((rows, points // group), jnp.float32)
     mine, other, *parts = pl.pallas_call(
@@ -81,7 +89,7 @@
         scratch_shapes=[
             pltpu.VMEM((rows, points), jnp.float32),
             pltpu.VMEM((points, rank), jnp.float32),
-            pltpu.SemaphoreType.DMA((points // depth + 1,)),
+            pltpu.SemaphoreType.DMA((points // depth + count,)),
         ],
         compiler_params=params(52),
         cost_estimate=FREE,

time: 55.6 us -> 55.7 us (level)
  no operation moved by 1% of the time
where the time goes in v24:
time: 55.7 us; the launch traced here: 55.1 us
  waiting for transfers between devices  25.2 us (45%)
  starting transfers between devices  22.6 us (41%)
  Pallas kernels  6.57 us (12%)
  between operations  0.7 us (1%)
    ppermute x19, waiting for transfers between devices, swap(): lax.ppermute(value, axis, [(i, i ^ offset) for i in range(lax.axis_size(a...  25.2 us
    ppermute x19, starting transfers between devices, swap(): lax.ppermute(value, axis, [(i, i ^ offset) for i in range(lax.axis_size(a...  22.6 us
    pallas_call x1, Pallas kernels, project(): pl.pallas_call(functools.partial(project_kernel, depth), in_specs=[HBM, H...  3.06 us
    pallas_call x1, Pallas kernels, mix(): pl.pallas_call(functools.partial(mix_kernel, times, order), in_specs=[SME...  2.08 us
  transfers between devices with their start and end apart: 19, of which 9 were waited for; matrix products, arithmetic and copies ran while one was open for 0% of the time, Pallas kernels for 4%

profile of v24, /device:TPU:8, one launch (start us, length us, event | category | flops | bytes accessed | tf_op | source)
XLA Modules:
  0.0 55.1 jit_solution(16309431592953419648)
XLA Ops:
  0.6 3.1 %shard_map.41 = (f32[32,256]{1,0:T(8,128)S(1)}, f32[32,256]{1,0:T(8,128)S(1)}, f32[64,1024]{1,0:T(8,128)S(1)}, f32[64,1024]{1,0:T(8,128)S(1)}, f32[64,1024]{1,0:T(8,128)S(1)}, /*index=5*/f32[64,1024]{1,0:T(8,128)S(1)}) custom-call(f32[64,4096]{1,0:T(8,128)} %snapshots_ref.1, f32[4096,256]{1,0:T(8,128)} %factor_ref.1), custom_call_target="tpu_custom_call" | custom-call | tf_op jit(solution)/shard_map/pallas_call | solution.py:84
  3.7 1.6 %collective-permute-start.1 = (f32[32,256]{1,0:T(8,128)S(1)}, f32[32,256]{1,0:T(8,128)S(1)}, u32[]{:S(2)}, u32[]{:S(2)}) collective-permute-start(f32[32,256]{1,0:T(8,128)S(1)} %get-tuple-element.24), channel_id=1, source_target_pairs={{0,2},{1,3},{2,0},{3,1},{4,6},{5,7},{6,4},{7,5},{8,10},{9,11},{10,... | collective-permute-start | bytes 98312 | tf_op jit(solution)/shard_map/ppermute | solution.py:213
  5.3 0.0 collective-permute-start.2
  5.3 0.6 %collective-permute-start = (f32[32,256]{1,0:T(8,128)S(1)}, f32[32,256]{1,0:T(8,128)S(1)}, u32[]{:S(2)}, u32[]{:S(2)}) collective-permute-start(f32[32,256]{1,0:T(8,128)S(1)} %get-tuple-element.25), channel_id=1, source_target_pairs={{0,1},{1,0},{2,3},{3,2},{4,5},{5,4},{6,7},{7,6},{8,9},{9,8},{10,11... | collective-permute-start | bytes 98312 | tf_op jit(solution)/shard_map/ppermute | solution.py:213
  5.9 1.5 %collective-permute-start.6 = (f32[64,1024]{1,0:T(8,128)S(1)}, f32[64,1024]{1,0:T(8,128)S(1)}, u32[]{:S(2)}, u32[]{:S(2)}) collective-permute-start(f32[64,1024]{1,0:T(8,128)S(1)} %get-tuple-element.26), channel_id=1, source_target_pairs={{0,4},{4,0},{8,12},{12,8},{16,20},{20,16},{24,28},{28,24},{1,5},{5... | collective-permute-start | bytes 786440 | tf_op jit(solution)/shard_map/ppermute | solution.py:213
  7.4 0.5 collective-permute-start.7
  7.8 0.0 collective-permute-done.1
  7.9 0.9 %collective-permute-done.2 = f32[32,256]{1,0:T(8,128)S(1)} collective-permute-done((f32[32,256]{1,0:T(8,128)S(1)}, f32[32,256]{1,0:T(8,128)S(1)}, u32[]{:S(2)}, u32[]{:S(2)}) %collective-permute-start.2) | collective-permute-done | bytes 32800 | tf_op jit(solution)/shard_map/ppermute | solution.py:213
  8.7 0.0 collective-permute-done
  8.7 3.6 %collective-permute-start.5 = (f32[32,256]{1,0:T(8,128)S(1)}, f32[32,256]{1,0:T(8,128)S(1)}, u32[]{:S(2)}, u32[]{:S(2)}) collective-permute-start(f32[32,256]{1,0:T(8,128)S(1)} %add_add_fusion), channel_id=1, source_target_pairs={{0,20},{4,16},{8,28},{12,24},{16,4},{20,0},{24,12},{28,8},{1,21},{... | collective-permute-start | bytes 98312 | tf_op jit(solution)/shard_map/ppermute | solution.py:213
  12.3 0.3 collective-permute-start.4
  12.6 0.5 collective-permute-start.3
  13.2 4.2 %collective-permute-done.5 = f32[32,256]{1,0:T(8,128)S(1)} collective-permute-done((f32[32,256]{1,0:T(8,128)S(1)}, f32[32,256]{1,0:T(8,128)S(1)}, u32[]{:S(2)}, u32[]{:S(2)}) %collective-permute-start.5) | collective-permute-done | bytes 32800 | tf_op jit(solution)/shard_map/ppermute | solution.py:213
  17.4 0.4 collective-permute-done.4
  17.8 0.0 collective-permute-done.3
  17.8 0.0 collective-permute-done.6.refs_1_
  17.8 0.0 collective-permute-done.7.refs_2_
  17.8 0.2 collective-permute-start.9
  18.0 2.4 %collective-permute-start.11 = (f32[64,1024]{1,0:T(8,128)S(1)}, f32[64,1024]{1,0:T(8,128)S(1)}, u32[]{:S(2)}, u32[]{:S(2)}) collective-permute-start(f32[64,1024]{1,0:T(8,128)S(1)} %get-tuple-element.35), channel_id=1, source_target_pairs={{0,12},{4,8},{8,4},{12,0},{16,28},{20,24},{24,20},{28,16},{1,13},{... | collective-permute-start | bytes 786440 | tf_op jit(solution)/shard_map/ppermute | solution.py:213
  20.4 0.0 collective-permute-start.8
  20.4 3.9 %collective-permute-done.9.refs_2_ = f32[128,256]{1,0:T(8,128)S(1)} collective-permute-done((f32[128,256]{1,0:T(8,128)S(1)}, f32[128,256]{1,0:T(8,128)S(1)}, u32[]{:S(2)}, u32[]{:S(2)}) %collective-permute-start.9) | collective-permute-done | bytes 131104 | tf_op jit(solution)/shard_map/ppermute | solution.py:213
  24.3 0.0 collective-permute-start.10
  24.3 0.1 pad_add_fusion.index_ref
  24.4 0.0 collective-permute-done.8.refs_1_
  24.4 1.3 %collective-permute-done.10.refs_3_ = f32[128,256]{1,0:T(8,128)S(1)} collective-permute-done((f32[128,256]{1,0:T(8,128)S(1)}, f32[128,256]{1,0:T(8,128)S(1)}, u32[]{:S(2)}, u32[]{:S(2)}) %collective-permute-start.10) | collective-permute-done | bytes 131104 | tf_op jit(solution)/shard_map/ppermute | solution.py:213
  25.6 2.1 %shard_map.42 = (bf16[256,256]{1,0:T(8,128)(2,1)S(1)}, bf16[256,256]{1,0:T(8,128)(2,1)S(1)}, f32[64,256]{1,0:T(8,128)S(1)}) custom-call(s32[2]{0:T(128)S(1)} %pad_add_fusion.index_ref, f32[128,256]{1,0:T(8,128)S(1)} %pad_maximum_fusion.refs_0_, f32[128,256]{1,0:T(8,128)S(1)} %collective-permute-done.8.refs_1_, ...), custom_call_target="tpu_custom_call" | custom-call | tf_op jit(solution)/shard_map/pallas_call | solution.py:145
  27.7 0.0 collective-permute-done.11.refs_3_
  27.7 0.6 %shard_map.43 = (f32[32,1024]{1,0:T(8,128)S(1)}, f32[32,1024]{1,0:T(8,128)S(1)}, f32[32,1024]{1,0:T(8,128)S(1)}, f32[32,1024]{1,0:T(8,128)S(1)}, f32[32,1024]{1,...) custom-call(bf16[256,256]{1,0:T(8,128)(2,1)S(1)} %get-tuple-element.30.high_ref, ...), custom_call_target="tpu_custom_call" | custom-call | tf_op jit(solution)/shard_map/pallas_call | solution.py:167
  28.3 1.2 %collective-permute-start.14 = (f32[32,1024]{1,0:T(8,128)S(1)}, f32[32,1024]{1,0:T(8,128)S(1)}, u32[]{:S(2)}, u32[]{:S(2)}) collective-permute-start(f32[32,1024]{1,0:T(8,128)S(1)} %get-tuple-element.39), channel_id=1, source_target_pairs={{0,4},{4,0},{8,12},{12,8},{16,20},{20,16},{24,28},{28,24},{1,5},{5... | collective-permute-start | bytes 393224 | tf_op jit(solution)/shard_map/ppermute | solution.py:213
  29.5 1.8 %collective-permute-start.12 = (f32[32,1024]{1,0:T(8,128)S(1)}, f32[32,1024]{1,0:T(8,128)S(1)}, u32[]{:S(2)}, u32[]{:S(2)}) collective-permute-start(f32[32,1024]{1,0:T(8,128)S(1)} %get-tuple-element.36), channel_id=1, source_target_pairs={{0,16},{4,20},{8,24},{12,28},{16,0},{20,4},{24,8},{28,12},{1,17},{... | collective-permute-start | bytes 393224 | tf_op jit(solution)/shard_map/ppermute | solution.py:213
  31.3 1.5 %collective-permute-start.13 = (f32[32,1024]{1,0:T(8,128)S(1)}, f32[32,1024]{1,0:T(8,128)S(1)}, u32[]{:S(2)}, u32[]{:S(2)}) collective-permute-start(f32[32,1024]{1,0:T(8,128)S(1)} %get-tuple-element.37), channel_id=1, source_target_pairs={{0,20},{4,16},{8,28},{12,24},{16,4},{20,0},{24,12},{28,8},{1,21},{... | collective-permute-start | bytes 393224 | tf_op jit(solution)/shard_map/ppermute | solution.py:213
  32.8 0.9 %collective-permute-start.15 = (f32[32,1024]{1,0:T(8,128)S(1)}, f32[32,1024]{1,0:T(8,128)S(1)}, u32[]{:S(2)}, u32[]{:S(2)}) collective-permute-start(f32[32,1024]{1,0:T(8,128)S(1)} %get-tuple-element.41), channel_id=1, source_target_pairs={{0,8},{4,12},{8,0},{12,4},{16,24},{20,28},{24,16},{28,20},{1,9},{5... | collective-permute-start | bytes 393224 | tf_op jit(solution)/shard_map/ppermute | solution.py:213
  33.7 1.2 %collective-permute-start.16 = (f32[32,1024]{1,0:T(8,128)S(1)}, f32[32,1024]{1,0:T(8,128)S(1)}, u32[]{:S(2)}, u32[]{:S(2)}) collective-permute-start(f32[32,1024]{1,0:T(8,128)S(1)} %get-tuple-element.42), channel_id=1, source_target_pairs={{0,24},{4,28},{8,16},{12,20},{16,8},{20,12},{24,0},{28,4},{1,25},{... | collective-permute-start | bytes 393224 | tf_op jit(solution)/shard_map/ppermute | solution.py:213
  34.9 0.0 collective-permute-done.14.refs_2_
  34.9 1.1 %collective-permute-start.17 = (f32[32,1024]{1,0:T(8,128)S(1)}, f32[32,1024]{1,0:T(8,128)S(1)}, u32[]{:S(2)}, u32[]{:S(2)}) collective-permute-start(f32[32,1024]{1,0:T(8,128)S(1)} %get-tuple-element.43), channel_id=1, source_target_pairs={{0,28},{4,24},{8,20},{12,16},{16,12},{20,8},{24,4},{28,0},{1,29},{... | collective-permute-start | bytes 393224 | tf_op jit(solution)/shard_map/ppermute | solution.py:213
  35.9 4.5 %collective-permute-done.12.refs_0_ = f32[32,1024]{1,0:T(8,128)S(1)} collective-permute-done((f32[32,1024]{1,0:T(8,128)S(1)}, f32[32,1024]{1,0:T(8,128)S(1)}, u32[]{:S(2)}, u32[]{:S(2)}) %collective-permute-start.12) | collective-permute-done | bytes 131104 | tf_op jit(solution)/shard_map/ppermute | solution.py:213
  40.5 3.7 %collective-permute-start.18 = (f32[32,1024]{1,0:T(8,128)S(1)}, f32[32,1024]{1,0:T(8,128)S(1)}, u32[]{:S(2)}, u32[]{:S(2)}) collective-permute-start(f32[32,1024]{1,0:T(8,128)S(1)} %get-tuple-element.44), channel_id=1, source_target_pairs={{0,12},{4,8},{8,4},{12,0},{16,28},{20,24},{24,20},{28,16},{1,13},{... | collective-permute-start | bytes 393224 | tf_op jit(solution)/shard_map/ppermute | solution.py:213
  44.2 3.6 %collective-permute-done.13.refs_1_ = f32[32,1024]{1,0:T(8,128)S(1)} collective-permute-done((f32[32,1024]{1,0:T(8,128)S(1)}, f32[32,1024]{1,0:T(8,128)S(1)}, u32[]{:S(2)}, u32[]{:S(2)}) %collective-permute-start.13) | collective-permute-done | bytes 131104 | tf_op jit(solution)/shard_map/ppermute | solution.py:213
  47.7 0.0 collective-permute-done.15.refs_3_
  47.8 4.8 %collective-permute-done.16.refs_4_ = f32[32,1024]{1,0:T(8,128)S(1)} collective-permute-done((f32[32,1024]{1,0:T(8,128)S(1)}, f32[32,1024]{1,0:T(8,128)S(1)}, u32[]{:S(2)}, u32[]{:S(2)}) %collective-permute-start.16) | collective-permute-done | bytes 131104 | tf_op jit(solution)/shard_map/ppermute | solution.py:213
  52.5 1.8 %collective-permute-done.17.refs_5_ = f32[32,1024]{1,0:T(8,128)S(1)} collective-permute-done((f32[32,1024]{1,0:T(8,128)S(1)}, f32[32,1024]{1,0:T(8,128)S(1)}, u32[]{:S(2)}, u32[]{:S(2)}) %collective-permute-start.17) | collective-permute-done | bytes 131104 | tf_op jit(solution)/shard_map/ppermute | solution.py:213
  54.3 0.0 collective-permute-done.18.refs_6_
  54.3 0.8 %shard_map.44 = (f32[64,256]{1,0:T(8,128)}, f32[32,4096]{1,0:T(8,128)}) custom-call(f32[64,256]{1,0:T(8,128)S(1)} %get-tuple-element.29.own_ref, f32[32,1024]{1,0:T(8,128)S(1)} %collective-permute-done.12.refs_0_, f32[32,1024]{1,0:T(8,128)S(1)} %collective-permute-done.13.refs_1_, f32[32,1024]{1,0:T(8,128)S(1)} %collective-permute-done.14.refs_2_, ...), custom_call_target="tpu_custom_call" | custom-call | tf_op jit(solution)/shard_map/pallas_call | solution.py:198
  (2 shorter events, 0.0 us)
Async XLA Ops:
  3.7 4.2 %collective-permute-start.1 = (f32[32,256]{1,0:T(8,128)S(1)}, f32[32,256]{1,0:T(8,128)S(1)}, u32[]{:S(2)}, u32[]{:S(2)}) collective-permute-start(f32[32,256]{1,0:T(8,128)S(1)} %get-tuple-element.24), channel_id=1, source_target_pairs={{0,2},{1,3},{2,0},{3,1},{4,6},{5,7},{6,4},{7,5},{8,10},{9,11},{10,... | collective-permute-start | bytes 98312 | tf_op jit(solution)/shard_map/ppermute | solution.py:213
  5.3 3.4 %collective-permute-start.2 = (f32[32,256]{1,0:T(8,128)S(1)}, f32[32,256]{1,0:T(8,128)S(1)}, u32[]{:S(2)}, u32[]{:S(2)}) collective-permute-start(f32[32,256]{1,0:T(8,128)S(1)} %get-tuple-element.25), channel_id=1, source_target_pairs={{0,3},{1,2},{2,1},{3,0},{4,7},{5,6},{6,5},{7,4},{8,11},{9,10},{10,... | collective-permute-start | bytes 98312 | tf_op jit(solution)/shard_map/ppermute | solution.py:213
  5.3 3.4 %collective-permute-start = (f32[32,256]{1,0:T(8,128)S(1)}, f32[32,256]{1,0:T(8,128)S(1)}, u32[]{:S(2)}, u32[]{:S(2)}) collective-permute-start(f32[32,256]{1,0:T(8,128)S(1)} %get-tuple-element.25), channel_id=1, source_target_pairs={{0,1},{1,0},{2,3},{3,2},{4,5},{5,4},{6,7},{7,6},{8,9},{9,8},{10,11... | collective-permute-start | bytes 98312 | tf_op jit(solution)/shard_map/ppermute | solution.py:213
  5.9 11.9 %collective-permute-start.6 = (f32[64,1024]{1,0:T(8,128)S(1)}, f32[64,1024]{1,0:T(8,128)S(1)}, u32[]{:S(2)}, u32[]{:S(2)}) collective-permute-start(f32[64,1024]{1,0:T(8,128)S(1)} %get-tuple-element.26), channel_id=1, source_target_pairs={{0,4},{4,0},{8,12},{12,8},{16,20},{20,16},{24,28},{28,24},{1,5},{5... | collective-permute-start | bytes 786440 | tf_op jit(solution)/shard_map/ppermute | solution.py:213
  7.4 10.4 %collective-permute-start.7 = (f32[64,1024]{1,0:T(8,128)S(1)}, f32[64,1024]{1,0:T(8,128)S(1)}, u32[]{:S(2)}, u32[]{:S(2)}) collective-permute-start(f32[64,1024]{1,0:T(8,128)S(1)} %get-tuple-element.27), channel_id=1, source_target_pairs={{0,8},{4,12},{8,0},{12,4},{16,24},{20,28},{24,16},{28,20},{1,9},{5... | collective-permute-start | bytes 786440 | tf_op jit(solution)/shard_map/ppermute | solution.py:213
  8.7 8.6 %collective-permute-start.5 = (f32[32,256]{1,0:T(8,128)S(1)}, f32[32,256]{1,0:T(8,128)S(1)}, u32[]{:S(2)}, u32[]{:S(2)}) collective-permute-start(f32[32,256]{1,0:T(8,128)S(1)} %add_add_fusion), channel_id=1, source_target_pairs={{0,20},{4,16},{8,28},{12,24},{16,4},{20,0},{24,12},{28,8},{1,21},{... | collective-permute-start | bytes 98312 | tf_op jit(solution)/shard_map/ppermute | solution.py:213
  12.3 5.4 %collective-permute-start.4 = (f32[32,256]{1,0:T(8,128)S(1)}, f32[32,256]{1,0:T(8,128)S(1)}, u32[]{:S(2)}, u32[]{:S(2)}) collective-permute-start(f32[32,256]{1,0:T(8,128)S(1)} %add_add_fusion), channel_id=1, source_target_pairs={{0,16},{4,20},{8,24},{12,28},{16,0},{20,4},{24,8},{28,12},{1,17},{... | collective-permute-start | bytes 98312 | tf_op jit(solution)/shard_map/ppermute | solution.py:213
  12.6 5.1 %collective-permute-start.3 = (f32[32,256]{1,0:T(8,128)S(1)}, f32[32,256]{1,0:T(8,128)S(1)}, u32[]{:S(2)}, u32[]{:S(2)}) collective-permute-start(f32[32,256]{1,0:T(8,128)S(1)} %add_add_fusion), channel_id=1, source_target_pairs={{0,4},{4,0},{8,12},{12,8},{16,20},{20,16},{24,28},{28,24},{1,5},{5... | collective-permute-start | bytes 98312 | tf_op jit(solution)/shard_map/ppermute | solution.py:213
  17.8 6.5 %collective-permute-start.9 = (f32[128,256]{1,0:T(8,128)S(1)}, f32[128,256]{1,0:T(8,128)S(1)}, u32[]{:S(2)}, u32[]{:S(2)}) collective-permute-start(f32[128,256]{1,0:T(8,128)S(1)} %pad_maximum_fusion.refs_0_), channel_id=1, source_target_pairs={{0,8},{4,12},{8,0},{12,4},{16,24},{20,28},{24,16},{28,20},{1,9},{5... | collective-permute-start | bytes 393224 | tf_op jit(solution)/shard_map/ppermute | solution.py:213
  18.0 9.7 %collective-permute-start.11 = (f32[64,1024]{1,0:T(8,128)S(1)}, f32[64,1024]{1,0:T(8,128)S(1)}, u32[]{:S(2)}, u32[]{:S(2)}) collective-permute-start(f32[64,1024]{1,0:T(8,128)S(1)} %get-tuple-element.35), channel_id=1, source_target_pairs={{0,12},{4,8},{8,4},{12,0},{16,28},{20,24},{24,20},{28,16},{1,13},{... | collective-permute-start | bytes 786440 | tf_op jit(solution)/shard_map/ppermute | solution.py:213
  20.4 3.9 %collective-permute-start.8 = (f32[128,256]{1,0:T(8,128)S(1)}, f32[128,256]{1,0:T(8,128)S(1)}, u32[]{:S(2)}, u32[]{:S(2)}) collective-permute-start(f32[128,256]{1,0:T(8,128)S(1)} %pad_maximum_fusion.refs_0_), channel_id=1, source_target_pairs={{0,1},{1,0},{2,3},{3,2},{4,5},{5,4},{6,7},{7,6},{8,9},{9,8},{10,11... | collective-permute-start | bytes 393224 | tf_op jit(solution)/shard_map/ppermute | solution.py:213
  24.3 1.3 %collective-permute-start.10 = (f32[128,256]{1,0:T(8,128)S(1)}, f32[128,256]{1,0:T(8,128)S(1)}, u32[]{:S(2)}, u32[]{:S(2)}) collective-permute-start(f32[128,256]{1,0:T(8,128)S(1)} %collective-permute-done.9.refs_2_), channel_id=1, source_target_pairs={{0,1},{1,0},{2,3},{3,2},{4,5},{5,4},{6,7},{7,6},{8,9},{9,8},{10,11... | collective-permute-start | bytes 393224 | tf_op jit(solution)/shard_map/ppermute | solution.py:213
  28.3 6.5 %collective-permute-start.14 = (f32[32,1024]{1,0:T(8,128)S(1)}, f32[32,1024]{1,0:T(8,128)S(1)}, u32[]{:S(2)}, u32[]{:S(2)}) collective-permute-start(f32[32,1024]{1,0:T(8,128)S(1)} %get-tuple-element.39), channel_id=1, source_target_pairs={{0,4},{4,0},{8,12},{12,8},{16,20},{20,16},{24,28},{28,24},{1,5},{5... | collective-permute-start | bytes 393224 | tf_op jit(solution)/shard_map/ppermute | solution.py:213
  29.5 10.9 %collective-permute-start.12 = (f32[32,1024]{1,0:T(8,128)S(1)}, f32[32,1024]{1,0:T(8,128)S(1)}, u32[]{:S(2)}, u32[]{:S(2)}) collective-permute-start(f32[32,1024]{1,0:T(8,128)S(1)} %get-tuple-element.36), channel_id=1, source_target_pairs={{0,16},{4,20},{8,24},{12,28},{16,0},{20,4},{24,8},{28,12},{1,17},{... | collective-permute-start | bytes 393224 | tf_op jit(solution)/shard_map/ppermute | solution.py:213
  31.3 16.5 %collective-permute-start.13 = (f32[32,1024]{1,0:T(8,128)S(1)}, f32[32,1024]{1,0:T(8,128)S(1)}, u32[]{:S(2)}, u32[]{:S(2)}) collective-permute-start(f32[32,1024]{1,0:T(8,128)S(1)} %get-tuple-element.37), channel_id=1, source_target_pairs={{0,20},{4,16},{8,28},{12,24},{16,4},{20,0},{24,12},{28,8},{1,21},{... | collective-permute-start | bytes 393224 | tf_op jit(solution)/shard_map/ppermute | solution.py:213
  32.8 15.0 %collective-permute-start.15 = (f32[32,1024]{1,0:T(8,128)S(1)}, f32[32,1024]{1,0:T(8,128)S(1)}, u32[]{:S(2)}, u32[]{:S(2)}) collective-permute-start(f32[32,1024]{1,0:T(8,128)S(1)} %get-tuple-element.41), channel_id=1, source_target_pairs={{0,8},{4,12},{8,0},{12,4},{16,24},{20,28},{24,16},{28,20},{1,9},{5... | collective-permute-start | bytes 393224 | tf_op jit(solution)/shard_map/ppermute | solution.py:213
  33.7 18.8 %collective-permute-start.16 = (f32[32,1024]{1,0:T(8,128)S(1)}, f32[32,1024]{1,0:T(8,128)S(1)}, u32[]{:S(2)}, u32[]{:S(2)}) collective-permute-start(f32[32,1024]{1,0:T(8,128)S(1)} %get-tuple-element.42), channel_id=1, source_target_pairs={{0,24},{4,28},{8,16},{12,20},{16,8},{20,12},{24,0},{28,4},{1,25},{... | collective-permute-start | bytes 393224 | tf_op jit(solution)/shard_map/ppermute | solution.py:213
  34.9 19.4 %collective-permute-start.17 = (f32[32,1024]{1,0:T(8,128)S(1)}, f32[32,1024]{1,0:T(8,128)S(1)}, u32[]{:S(2)}, u32[]{:S(2)}) collective-permute-start(f32[32,1024]{1,0:T(8,128)S(1)} %get-tuple-element.43), channel_id=1, source_target_pairs={{0,28},{4,24},{8,20},{12,16},{16,12},{20,8},{24,4},{28,0},{1,29},{... | collective-permute-start | bytes 393224 | tf_op jit(solution)/shard_map/ppermute | solution.py:213
  40.5 13.8 %collective-permute-start.18 = (f32[32,1024]{1,0:T(8,128)S(1)}, f32[32,1024]{1,0:T(8,128)S(1)}, u32[]{:S(2)}, u32[]{:S(2)}) collective-permute-start(f32[32,1024]{1,0:T(8,128)S(1)} %get-tuple-element.44), channel_id=1, source_target_pairs={{0,12},{4,8},{8,4},{12,0},{16,28},{20,24},{24,20},{28,16},{1,13},{... | collective-permute-start | bytes 393224 | tf_op jit(solution)/shard_map/ppermute | solution.py:213

commit v25 on v20

--- a/solution.py
+++ b/solution.py
@@ -33,9 +33,9 @@
 
 def product(left, right, dims=ROWS_BY_COLUMNS):
     (left_high, left_low), (right_high, right_low) = left, right
-    return dot(left_high, right_high, dims) + (
-        dot(left_high, right_low, dims) + dot(left_low, right_high, dims)
-    )
+    rows = left_high.shape[0]
+    both = dot(jnp.concatenate([left_high, left_low], axis=0), right_high, dims)
+    return both[:rows] + (both[rows:] + dot(left_high, right_low, dims))
 
 
 def project_kernel(depth, snapshots_ref, factor_ref, mine_ref, other_ref, *refs):
@@ -166,35 +166,53 @@
     )(high, low, *parts)
 
 
-def join_kernel(group, sequence, *refs):
-    *terms, out_ref, buf, sems = refs
-    terms = [terms[sequence.index(k)] for k in range(len(terms))]
-    width = terms[0].shape[1]
+def join_kernel(group, members, count, *refs):
+    *refs, out_ref, buf, sems = refs
+    terms = refs[:count]
+    width = buf.shape[2]
     member = lax.rem(lax.axis_index("tm"), group)
     copies = []
-    for k in range(group):
-        value = terms[k][...]
-        for term in terms[group + k :: group]:
+    if len(refs) > count + 1:
+        own_ref, own_out_ref = refs[count:]
+        copies.append(pltpu.make_async_copy(own_ref, own_out_ref, sems.at[len(members)]))
+        copies[0].start()
+    for i, k in enumerate(members):
+        value = terms[i][...]
+        for term in terms[i + len(members) :: len(members)]:
             value = value + term[...]
-        buf[k] = value
+        buf[i] = value
         span = pl.ds(pl.multiple_of((member ^ k) * width, width), width)
-        copies.append(pltpu.make_async_copy(buf.at[k], out_ref.at[:, span], sems.at[k]))
+        copies.append(pltpu.make_async_copy(buf.at[i], out_ref.at[:, span], sems.at[i]))
         copies[-1].start()
     for copy in copies:
         copy.wait()
 
 
-def join(terms, group, sequence):
+def join(own, terms, group):
     rows, width = terms[0].shape
-    return pl.pallas_call(
-        functools.partial(join_kernel, group, sequence),
-        in_specs=[VMEM] * len(terms),
-        out_specs=HBM,
-        out_shape=jax.ShapeDtypeStruct((rows, group * width), jnp.float32),
-        scratch_shapes=[pltpu.VMEM((group, rows, width), jnp.float32), pltpu.SemaphoreType.DMA((group,))],
-        compiler_params=params(),
-        cost_estimate=FREE,
-    )(*[terms[k] for k in sequence])
+    loadings = jax.ShapeDtypeStruct((rows, group * width), jnp.float32)
+
+    def call(members, value, spec, out_shape, aliases):
+        firsts = reversed(range(0, len(terms), group))
+        picked = [terms[first + k] for first in firsts for k in members]
+        return pl.pallas_call(
+            functools.partial(join_kernel, group, members, len(picked)),
+            in_specs=[VMEM] * len(picked) + [spec],
+            out_specs=[HBM] * len(out_shape),
+            out_shape=out_shape,
+            scratch_shapes=[
+                pltpu.VMEM((len(members), rows, width), jnp.float32),
+                pltpu.SemaphoreType.DMA((len(members) + 1,)),
+            ],
+            input_output_aliases={len(picked): 0} if aliases else {},
+            compiler_params=params(),
+            cost_estimate=FREE,
+        )(*picked, value)
+
+    half = group // 2
+    own_shape = jax.ShapeDtypeStruct(own.shape, jnp.float32)
+    own, loaded = call(range(half), own, VMEM, [own_shape, loadings], False)
+    return own, call(range(half, group), loaded, HBM, [loadings], True)[0]
 
 
 def swap(value, axis, offset):
@@ -235,7 +253,7 @@
         if k == near[-1]:
             blocks[k], terms[1] = lax.optimization_barrier((blocks[k], terms[1]))
         terms[k] = swap(blocks[k], "tm", k)
-    return own, join(terms, group, sequence)
+    return join(own, terms, group)
 
 
 def solution(mesh):

time: 55.9 us -> 56.1 us (level)
  waiting for transfers between devices: 25.2 us -> 22.7 us
  starting transfers between devices: 22.6 us -> 24.5 us
    ppermute x19, waiting for transfers between devices: 25.2 us -> 22.7 us  [swap(): lax.ppermute(value, axis, [(i, i ^ offset) for i in range(lax.axis_size(a...]
    ppermute x19, starting transfers between devices: 22.6 us -> 24.5 us  [swap(): lax.ppermute(value, axis, [(i, i ^ offset) for i in range(lax.axis_size(a...]
    pallas_call x1 -> x2, Pallas kernels: 0.83 us -> 1.49 us  [call(): pl.pallas_call(functools.partial(join_kernel, group, members, len(picked)...]
  transfers between devices with their start and end apart: 19 -> 19, of which waited for: 9 -> 8; matrix products, arithmetic and copies ran while one was open for 0% -> 0% of each run, Pallas kernels for 4% -> 5%
where the time goes in v25:
time: 56.1 us; the launch traced here: 55.1 us
  starting transfers between devices  24.5 us (44%)
  waiting for transfers between devices  22.7 us (40%)
  Pallas kernels  7.07 us (13%)
  between operations  0.71 us (1%)
    ppermute x19, starting transfers between devices, swap(): lax.ppermute(value, axis, [(i, i ^ offset) for i in range(lax.axis_size(a...  24.5 us
    ppermute x19, waiting for transfers between devices, swap(): lax.ppermute(value, axis, [(i, i ^ offset) for i in range(lax.axis_size(a...  22.7 us
    pallas_call x1, Pallas kernels, project(): pl.pallas_call(functools.partial(project_kernel, depth), in_specs=[HBM, H...  2.93 us
    pallas_call x1, Pallas kernels, mix(): pl.pallas_call(functools.partial(mix_kernel, times, order), in_specs=[SME...  2.08 us
    pallas_call x2, Pallas kernels, call(): pl.pallas_call(functools.partial(join_kernel, group, members, len(picked)...  1.49 us
  transfers between devices with their start and end apart: 19, of which 8 were waited for; matrix products, arithmetic and copies ran while one was open for 0% of the time, Pallas kernels for 5%

profile of v25, /device:TPU:8, one launch (start us, length us, event | category | flops | bytes accessed | tf_op | source)
XLA Modules:
  0.0 55.1 jit_solution(2984636846700511163)
XLA Ops:
  0.6 2.9 %shard_map.41 = (f32[32,256]{1,0:T(8,128)S(1)}, f32[32,256]{1,0:T(8,128)S(1)}, f32[64,1024]{1,0:T(8,128)S(1)}, f32[64,1024]{1,0:T(8,128)S(1)}, f32[64,1024]{1,0:T(8,128)S(1)}, /*index=5*/f32[64,1024]{1,0:T(8,128)S(1)}) custom-call(f32[64,4096]{1,0:T(8,128)} %snapshots_ref.1, f32[4096,256]{1,0:T(8,128)} %factor_ref.1), custom_call_target="tpu_custom_call" | custom-call | tf_op jit(solution)/shard_map/pallas_call | solution.py:76
  3.6 1.6 %collective-permute-start.1 = (f32[32,256]{1,0:T(8,128)S(1)}, f32[32,256]{1,0:T(8,128)S(1)}, u32[]{:S(2)}, u32[]{:S(2)}) collective-permute-start(f32[32,256]{1,0:T(8,128)S(1)} %get-tuple-element.26), channel_id=1, source_target_pairs={{0,2},{1,3},{2,0},{3,1},{4,6},{5,7},{6,4},{7,5},{8,10},{9,11},{10,... | collective-permute-start | bytes 98312 | tf_op jit(solution)/shard_map/ppermute | solution.py:219
  5.1 0.0 collective-permute-start.2
  5.2 0.6 %collective-permute-start = (f32[32,256]{1,0:T(8,128)S(1)}, f32[32,256]{1,0:T(8,128)S(1)}, u32[]{:S(2)}, u32[]{:S(2)}) collective-permute-start(f32[32,256]{1,0:T(8,128)S(1)} %get-tuple-element.27), channel_id=1, source_target_pairs={{0,1},{1,0},{2,3},{3,2},{4,5},{5,4},{6,7},{7,6},{8,9},{9,8},{10,11... | collective-permute-start | bytes 98312 | tf_op jit(solution)/shard_map/ppermute | solution.py:219
  5.8 1.5 %collective-permute-start.6 = (f32[64,1024]{1,0:T(8,128)S(1)}, f32[64,1024]{1,0:T(8,128)S(1)}, u32[]{:S(2)}, u32[]{:S(2)}) collective-permute-start(f32[64,1024]{1,0:T(8,128)S(1)} %get-tuple-element.28), channel_id=1, source_target_pairs={{0,4},{4,0},{8,12},{12,8},{16,20},{20,16},{24,28},{28,24},{1,5},{5... | collective-permute-start | bytes 786440 | tf_op jit(solution)/shard_map/ppermute | solution.py:219
  7.3 0.5 collective-permute-start.7
  7.7 0.0 collective-permute-done.1
  7.7 0.9 %collective-permute-done.2 = f32[32,256]{1,0:T(8,128)S(1)} collective-permute-done((f32[32,256]{1,0:T(8,128)S(1)}, f32[32,256]{1,0:T(8,128)S(1)}, u32[]{:S(2)}, u32[]{:S(2)}) %collective-permute-start.2) | collective-permute-done | bytes 32800 | tf_op jit(solution)/shard_map/ppermute | solution.py:219
  8.6 0.0 collective-permute-done
  8.6 3.6 %collective-permute-start.5 = (f32[32,256]{1,0:T(8,128)S(1)}, f32[32,256]{1,0:T(8,128)S(1)}, u32[]{:S(2)}, u32[]{:S(2)}) collective-permute-start(f32[32,256]{1,0:T(8,128)S(1)} %add_add_fusion), channel_id=1, source_target_pairs={{0,20},{4,16},{8,28},{12,24},{16,4},{20,0},{24,12},{28,8},{1,21},{... | collective-permute-start | bytes 98312 | tf_op jit(solution)/shard_map/ppermute | solution.py:219
  12.2 0.3 collective-permute-start.4
  12.5 0.5 collective-permute-start.3
  13.0 4.2 %collective-permute-done.5 = f32[32,256]{1,0:T(8,128)S(1)} collective-permute-done((f32[32,256]{1,0:T(8,128)S(1)}, f32[32,256]{1,0:T(8,128)S(1)}, u32[]{:S(2)}, u32[]{:S(2)}) %collective-permute-start.5) | collective-permute-done | bytes 32800 | tf_op jit(solution)/shard_map/ppermute | solution.py:219
  17.2 0.4 collective-permute-done.4
  17.6 0.0 collective-permute-done.3
  17.6 0.0 collective-permute-done.6.refs_1_
  17.6 0.0 collective-permute-done.7.refs_2_
  17.7 0.2 collective-permute-start.9
  17.9 2.4 %collective-permute-start.11 = (f32[64,1024]{1,0:T(8,128)S(1)}, f32[64,1024]{1,0:T(8,128)S(1)}, u32[]{:S(2)}, u32[]{:S(2)}) collective-permute-start(f32[64,1024]{1,0:T(8,128)S(1)} %get-tuple-element.36), channel_id=1, source_target_pairs={{0,12},{4,8},{8,4},{12,0},{16,28},{20,24},{24,20},{28,16},{1,13},{... | collective-permute-start | bytes 786440 | tf_op jit(solution)/shard_map/ppermute | solution.py:219
  20.3 0.0 collective-permute-start.8
  20.3 3.9 %collective-permute-done.9.refs_2_ = f32[128,256]{1,0:T(8,128)S(1)} collective-permute-done((f32[128,256]{1,0:T(8,128)S(1)}, f32[128,256]{1,0:T(8,128)S(1)}, u32[]{:S(2)}, u32[]{:S(2)}) %collective-permute-start.9) | collective-permute-done | bytes 131104 | tf_op jit(solution)/shard_map/ppermute | solution.py:219
  24.2 0.0 collective-permute-start.10
  24.2 0.1 pad_add_fusion.index_ref
  24.2 0.0 collective-permute-done.8.refs_1_
  24.2 1.3 %collective-permute-done.10.refs_3_ = f32[128,256]{1,0:T(8,128)S(1)} collective-permute-done((f32[128,256]{1,0:T(8,128)S(1)}, f32[128,256]{1,0:T(8,128)S(1)}, u32[]{:S(2)}, u32[]{:S(2)}) %collective-permute-start.10) | collective-permute-done | bytes 131104 | tf_op jit(solution)/shard_map/ppermute | solution.py:219
  25.5 2.1 %shard_map.42 = (bf16[256,256]{1,0:T(8,128)(2,1)S(1)}, bf16[256,256]{1,0:T(8,128)(2,1)S(1)}, f32[64,256]{1,0:T(8,128)S(1)}) custom-call(s32[2]{0:T(128)S(1)} %pad_add_fusion.index_ref, f32[128,256]{1,0:T(8,128)S(1)} %pad_maximum_fusion.refs_0_, f32[128,256]{1,0:T(8,128)S(1)} %collective-permute-done.8.refs_1_, ...), custom_call_target="tpu_custom_call" | custom-call | tf_op jit(solution)/shard_map/pallas_call | solution.py:137
  27.6 0.0 collective-permute-done.11.refs_3_
  27.6 0.6 %shard_map.43 = (f32[32,1024]{1,0:T(8,128)S(1)}, f32[32,1024]{1,0:T(8,128)S(1)}, f32[32,1024]{1,0:T(8,128)S(1)}, f32[32,1024]{1,0:T(8,128)S(1)}, f32[32,1024]{1,...) custom-call(bf16[256,256]{1,0:T(8,128)(2,1)S(1)} %get-tuple-element.31.high_ref, ...), custom_call_target="tpu_custom_call" | custom-call | tf_op jit(solution)/shard_map/pallas_call | solution.py:159
  28.2 1.2 %collective-permute-start.14 = (f32[32,1024]{1,0:T(8,128)S(1)}, f32[32,1024]{1,0:T(8,128)S(1)}, u32[]{:S(2)}, u32[]{:S(2)}) collective-permute-start(f32[32,1024]{1,0:T(8,128)S(1)} %get-tuple-element.41), channel_id=1, source_target_pairs={{0,4},{4,0},{8,12},{12,8},{16,20},{20,16},{24,28},{28,24},{1,5},{5... | collective-permute-start | bytes 393224 | tf_op jit(solution)/shard_map/ppermute | solution.py:219
  29.4 1.8 %collective-permute-start.12 = (f32[32,1024]{1,0:T(8,128)S(1)}, f32[32,1024]{1,0:T(8,128)S(1)}, u32[]{:S(2)}, u32[]{:S(2)}) collective-permute-start(f32[32,1024]{1,0:T(8,128)S(1)} %get-tuple-element.37), channel_id=1, source_target_pairs={{0,16},{4,20},{8,24},{12,28},{16,0},{20,4},{24,8},{28,12},{1,17},{... | collective-permute-start | bytes 393224 | tf_op jit(solution)/shard_map/ppermute | solution.py:219
  31.2 1.5 %collective-permute-start.13 = (f32[32,1024]{1,0:T(8,128)S(1)}, f32[32,1024]{1,0:T(8,128)S(1)}, u32[]{:S(2)}, u32[]{:S(2)}) collective-permute-start(f32[32,1024]{1,0:T(8,128)S(1)} %get-tuple-element.38), channel_id=1, source_target_pairs={{0,20},{4,16},{8,28},{12,24},{16,4},{20,0},{24,12},{28,8},{1,21},{... | collective-permute-start | bytes 393224 | tf_op jit(solution)/shard_map/ppermute | solution.py:219
  32.6 1.2 %collective-permute-start.15 = (f32[32,1024]{1,0:T(8,128)S(1)}, f32[32,1024]{1,0:T(8,128)S(1)}, u32[]{:S(2)}, u32[]{:S(2)}) collective-permute-start(f32[32,1024]{1,0:T(8,128)S(1)} %get-tuple-element.45), channel_id=1, source_target_pairs={{0,24},{4,28},{8,16},{12,20},{16,8},{20,12},{24,0},{28,4},{1,25},{... | collective-permute-start | bytes 393224 | tf_op jit(solution)/shard_map/ppermute | solution.py:219
  33.9 1.4 %collective-permute-start.16 = (f32[32,1024]{1,0:T(8,128)S(1)}, f32[32,1024]{1,0:T(8,128)S(1)}, u32[]{:S(2)}, u32[]{:S(2)}) collective-permute-start(f32[32,1024]{1,0:T(8,128)S(1)} %get-tuple-element.46), channel_id=1, source_target_pairs={{0,28},{4,24},{8,20},{12,16},{16,12},{20,8},{24,4},{28,0},{1,29},{... | collective-permute-start | bytes 393224 | tf_op jit(solution)/shard_map/ppermute | solution.py:219
  35.2 0.0 collective-permute-done.14.refs_3_
  35.2 2.3 %collective-permute-start.17 = (f32[32,1024]{1,0:T(8,128)S(1)}, f32[32,1024]{1,0:T(8,128)S(1)}, u32[]{:S(2)}, u32[]{:S(2)}) collective-permute-start(f32[32,1024]{1,0:T(8,128)S(1)} %get-tuple-element.47), channel_id=1, source_target_pairs={{0,8},{4,12},{8,0},{12,4},{16,24},{20,28},{24,16},{28,20},{1,9},{5... | collective-permute-start | bytes 393224 | tf_op jit(solution)/shard_map/ppermute | solution.py:219
  37.6 7.2 %collective-permute-done.12.refs_0_ = f32[32,1024]{1,0:T(8,128)S(1)} collective-permute-done((f32[32,1024]{1,0:T(8,128)S(1)}, f32[32,1024]{1,0:T(8,128)S(1)}, u32[]{:S(2)}, u32[]{:S(2)}) %collective-permute-start.12) | collective-permute-done | bytes 131104 | tf_op jit(solution)/shard_map/ppermute | solution.py:219
  44.8 3.9 %collective-permute-start.18 = (f32[32,1024]{1,0:T(8,128)S(1)}, f32[32,1024]{1,0:T(8,128)S(1)}, u32[]{:S(2)}, u32[]{:S(2)}) collective-permute-start(f32[32,1024]{1,0:T(8,128)S(1)} %get-tuple-element.48), channel_id=1, source_target_pairs={{0,12},{4,8},{8,4},{12,0},{16,28},{20,24},{24,20},{28,16},{1,13},{... | collective-permute-start | bytes 393224 | tf_op jit(solution)/shard_map/ppermute | solution.py:219
  48.7 0.0 collective-permute-done.13.refs_1_
  48.7 0.7 %shard_map.44 = (f32[64,256]{1,0:T(8,128)}, f32[32,4096]{1,0:T(8,128)}) custom-call(f32[32,1024]{1,0:T(8,128)S(1)} %collective-permute-done.12.refs_0_, f32[32,1024]{1,0:T(8,128)S(1)} %collective-permute-done.13.refs_1_, f32[32,1024]{1,0:T(8,128)S(1)} %get-tuple-element.39.refs_2_, f32[32,1024]{1,0:T(8,128)S(1)} %collective-permute-done.14.refs_3_, ...), custom_call_target="tpu_custom_call" | custom-call | tf_op jit(solution)/shard_map/pallas_call | solution.py:198
  49.4 2.9 %collective-permute-done.15.refs_0_ = f32[32,1024]{1,0:T(8,128)S(1)} collective-permute-done((f32[32,1024]{1,0:T(8,128)S(1)}, f32[32,1024]{1,0:T(8,128)S(1)}, u32[]{:S(2)}, u32[]{:S(2)}) %collective-permute-start.15) | collective-permute-done | bytes 131104 | tf_op jit(solution)/shard_map/ppermute | solution.py:219
  52.4 1.9 %collective-permute-done.16.refs_1_ = f32[32,1024]{1,0:T(8,128)S(1)} collective-permute-done((f32[32,1024]{1,0:T(8,128)S(1)}, f32[32,1024]{1,0:T(8,128)S(1)}, u32[]{:S(2)}, u32[]{:S(2)}) %collective-permute-start.16) | collective-permute-done | bytes 131104 | tf_op jit(solution)/shard_map/ppermute | solution.py:219
  54.3 0.0 collective-permute-done.17.refs_2_
  54.3 0.0 collective-permute-done.18.refs_3_
  54.3 0.7 %shard_map.45 = f32[32,4096]{1,0:T(8,128)} custom-call(f32[32,1024]{1,0:T(8,128)S(1)} %collective-permute-done.15.refs_0_, f32[32,1024]{1,0:T(8,128)S(1)} %collective-permute-done.16.refs_1_, f32[32,1024]{1,0:T(8,128)S(1)} %collective-permute-done.17.refs_2_, f32[32,1024]{1,0:T(8,128)S(1)} %collective-permute-done.18.refs_3_, ...), custom_call_target="tpu_custom_call", output_to_operand_aliasing={{}: (4, {})} | custom-call | tf_op jit(solution)/shard_map/pallas_call | solution.py:198
  (2 shorter events, 0.0 us)
Async XLA Ops:
  3.6 4.2 %collective-permute-start.1 = (f32[32,256]{1,0:T(8,128)S(1)}, f32[32,256]{1,0:T(8,128)S(1)}, u32[]{:S(2)}, u32[]{:S(2)}) collective-permute-start(f32[32,256]{1,0:T(8,128)S(1)} %get-tuple-element.26), channel_id=1, source_target_pairs={{0,2},{1,3},{2,0},{3,1},{4,6},{5,7},{6,4},{7,5},{8,10},{9,11},{10,... | collective-permute-start | bytes 98312 | tf_op jit(solution)/shard_map/ppermute | solution.py:219
  5.1 3.4 %collective-permute-start.2 = (f32[32,256]{1,0:T(8,128)S(1)}, f32[32,256]{1,0:T(8,128)S(1)}, u32[]{:S(2)}, u32[]{:S(2)}) collective-permute-start(f32[32,256]{1,0:T(8,128)S(1)} %get-tuple-element.27), channel_id=1, source_target_pairs={{0,3},{1,2},{2,1},{3,0},{4,7},{5,6},{6,5},{7,4},{8,11},{9,10},{10,... | collective-permute-start | bytes 98312 | tf_op jit(solution)/shard_map/ppermute | solution.py:219
  5.2 3.4 %collective-permute-start = (f32[32,256]{1,0:T(8,128)S(1)}, f32[32,256]{1,0:T(8,128)S(1)}, u32[]{:S(2)}, u32[]{:S(2)}) collective-permute-start(f32[32,256]{1,0:T(8,128)S(1)} %get-tuple-element.27), channel_id=1, source_target_pairs={{0,1},{1,0},{2,3},{3,2},{4,5},{5,4},{6,7},{7,6},{8,9},{9,8},{10,11... | collective-permute-start | bytes 98312 | tf_op jit(solution)/shard_map/ppermute | solution.py:219
  5.8 11.9 %collective-permute-start.6 = (f32[64,1024]{1,0:T(8,128)S(1)}, f32[64,1024]{1,0:T(8,128)S(1)}, u32[]{:S(2)}, u32[]{:S(2)}) collective-permute-start(f32[64,1024]{1,0:T(8,128)S(1)} %get-tuple-element.28), channel_id=1, source_target_pairs={{0,4},{4,0},{8,12},{12,8},{16,20},{20,16},{24,28},{28,24},{1,5},{5... | collective-permute-start | bytes 786440 | tf_op jit(solution)/shard_map/ppermute | solution.py:219
  7.3 10.4 %collective-permute-start.7 = (f32[64,1024]{1,0:T(8,128)S(1)}, f32[64,1024]{1,0:T(8,128)S(1)}, u32[]{:S(2)}, u32[]{:S(2)}) collective-permute-start(f32[64,1024]{1,0:T(8,128)S(1)} %get-tuple-element.29), channel_id=1, source_target_pairs={{0,8},{4,12},{8,0},{12,4},{16,24},{20,28},{24,16},{28,20},{1,9},{5... | collective-permute-start | bytes 786440 | tf_op jit(solution)/shard_map/ppermute | solution.py:219
  8.6 8.6 %collective-permute-start.5 = (f32[32,256]{1,0:T(8,128)S(1)}, f32[32,256]{1,0:T(8,128)S(1)}, u32[]{:S(2)}, u32[]{:S(2)}) collective-permute-start(f32[32,256]{1,0:T(8,128)S(1)} %add_add_fusion), channel_id=1, source_target_pairs={{0,20},{4,16},{8,28},{12,24},{16,4},{20,0},{24,12},{28,8},{1,21},{... | collective-permute-start | bytes 98312 | tf_op jit(solution)/shard_map/ppermute | solution.py:219
  12.2 5.4 %collective-permute-start.4 = (f32[32,256]{1,0:T(8,128)S(1)}, f32[32,256]{1,0:T(8,128)S(1)}, u32[]{:S(2)}, u32[]{:S(2)}) collective-permute-start(f32[32,256]{1,0:T(8,128)S(1)} %add_add_fusion), channel_id=1, source_target_pairs={{0,16},{4,20},{8,24},{12,28},{16,0},{20,4},{24,8},{28,12},{1,17},{... | collective-permute-start | bytes 98312 | tf_op jit(solution)/shard_map/ppermute | solution.py:219
  12.5 5.1 %collective-permute-start.3 = (f32[32,256]{1,0:T(8,128)S(1)}, f32[32,256]{1,0:T(8,128)S(1)}, u32[]{:S(2)}, u32[]{:S(2)}) collective-permute-start(f32[32,256]{1,0:T(8,128)S(1)} %add_add_fusion), channel_id=1, source_target_pairs={{0,4},{4,0},{8,12},{12,8},{16,20},{20,16},{24,28},{28,24},{1,5},{5... | collective-permute-start | bytes 98312 | tf_op jit(solution)/shard_map/ppermute | solution.py:219
  17.7 6.5 %collective-permute-start.9 = (f32[128,256]{1,0:T(8,128)S(1)}, f32[128,256]{1,0:T(8,128)S(1)}, u32[]{:S(2)}, u32[]{:S(2)}) collective-permute-start(f32[128,256]{1,0:T(8,128)S(1)} %pad_maximum_fusion.refs_0_), channel_id=1, source_target_pairs={{0,8},{4,12},{8,0},{12,4},{16,24},{20,28},{24,16},{28,20},{1,9},{5... | collective-permute-start | bytes 393224 | tf_op jit(solution)/shard_map/ppermute | solution.py:219
  17.9 9.7 %collective-permute-start.11 = (f32[64,1024]{1,0:T(8,128)S(1)}, f32[64,1024]{1,0:T(8,128)S(1)}, u32[]{:S(2)}, u32[]{:S(2)}) collective-permute-start(f32[64,1024]{1,0:T(8,128)S(1)} %get-tuple-element.36), channel_id=1, source_target_pairs={{0,12},{4,8},{8,4},{12,0},{16,28},{20,24},{24,20},{28,16},{1,13},{... | collective-permute-start | bytes 786440 | tf_op jit(solution)/shard_map/ppermute | solution.py:219
  20.3 3.9 %collective-permute-start.8 = (f32[128,256]{1,0:T(8,128)S(1)}, f32[128,256]{1,0:T(8,128)S(1)}, u32[]{:S(2)}, u32[]{:S(2)}) collective-permute-start(f32[128,256]{1,0:T(8,128)S(1)} %pad_maximum_fusion.refs_0_), channel_id=1, source_target_pairs={{0,1},{1,0},{2,3},{3,2},{4,5},{5,4},{6,7},{7,6},{8,9},{9,8},{10,11... | collective-permute-start | bytes 393224 | tf_op jit(solution)/shard_map/ppermute | solution.py:219
  24.2 1.3 %collective-permute-start.10 = (f32[128,256]{1,0:T(8,128)S(1)}, f32[128,256]{1,0:T(8,128)S(1)}, u32[]{:S(2)}, u32[]{:S(2)}) collective-permute-start(f32[128,256]{1,0:T(8,128)S(1)} %collective-permute-done.9.refs_2_), channel_id=1, source_target_pairs={{0,1},{1,0},{2,3},{3,2},{4,5},{5,4},{6,7},{7,6},{8,9},{9,8},{10,11... | collective-permute-start | bytes 393224 | tf_op jit(solution)/shard_map/ppermute | solution.py:219
  28.2 7.1 %collective-permute-start.14 = (f32[32,1024]{1,0:T(8,128)S(1)}, f32[32,1024]{1,0:T(8,128)S(1)}, u32[]{:S(2)}, u32[]{:S(2)}) collective-permute-start(f32[32,1024]{1,0:T(8,128)S(1)} %get-tuple-element.41), channel_id=1, source_target_pairs={{0,4},{4,0},{8,12},{12,8},{16,20},{20,16},{24,28},{28,24},{1,5},{5... | collective-permute-start | bytes 393224 | tf_op jit(solution)/shard_map/ppermute | solution.py:219
  29.4 15.4 %collective-permute-start.12 = (f32[32,1024]{1,0:T(8,128)S(1)}, f32[32,1024]{1,0:T(8,128)S(1)}, u32[]{:S(2)}, u32[]{:S(2)}) collective-permute-start(f32[32,1024]{1,0:T(8,128)S(1)} %get-tuple-element.37), channel_id=1, source_target_pairs={{0,16},{4,20},{8,24},{12,28},{16,0},{20,4},{24,8},{28,12},{1,17},{... | collective-permute-start | bytes 393224 | tf_op jit(solution)/shard_map/ppermute | solution.py:219
  31.2 17.5 %collective-permute-start.13 = (f32[32,1024]{1,0:T(8,128)S(1)}, f32[32,1024]{1,0:T(8,128)S(1)}, u32[]{:S(2)}, u32[]{:S(2)}) collective-permute-start(f32[32,1024]{1,0:T(8,128)S(1)} %get-tuple-element.38), channel_id=1, source_target_pairs={{0,20},{4,16},{8,28},{12,24},{16,4},{20,0},{24,12},{28,8},{1,21},{... | collective-permute-start | bytes 393224 | tf_op jit(solution)/shard_map/ppermute | solution.py:219
  32.6 19.7 %collective-permute-start.15 = (f32[32,1024]{1,0:T(8,128)S(1)}, f32[32,1024]{1,0:T(8,128)S(1)}, u32[]{:S(2)}, u32[]{:S(2)}) collective-permute-start(f32[32,1024]{1,0:T(8,128)S(1)} %get-tuple-element.45), channel_id=1, source_target_pairs={{0,24},{4,28},{8,16},{12,20},{16,8},{20,12},{24,0},{28,4},{1,25},{... | collective-permute-start | bytes 393224 | tf_op jit(solution)/shard_map/ppermute | solution.py:219
  33.9 20.5 %collective-permute-start.16 = (f32[32,1024]{1,0:T(8,128)S(1)}, f32[32,1024]{1,0:T(8,128)S(1)}, u32[]{:S(2)}, u32[]{:S(2)}) collective-permute-start(f32[32,1024]{1,0:T(8,128)S(1)} %get-tuple-element.46), channel_id=1, source_target_pairs={{0,28},{4,24},{8,20},{12,16},{16,12},{20,8},{24,4},{28,0},{1,29},{... | collective-permute-start | bytes 393224 | tf_op jit(solution)/shard_map/ppermute | solution.py:219
  35.2 19.1 %collective-permute-start.17 = (f32[32,1024]{1,0:T(8,128)S(1)}, f32[32,1024]{1,0:T(8,128)S(1)}, u32[]{:S(2)}, u32[]{:S(2)}) collective-permute-start(f32[32,1024]{1,0:T(8,128)S(1)} %get-tuple-element.47), channel_id=1, source_target_pairs={{0,8},{4,12},{8,0},{12,4},{16,24},{20,28},{24,16},{28,20},{1,9},{5... | collective-permute-start | bytes 393224 | tf_op jit(solution)/shard_map/ppermute | solution.py:219
  44.8 9.5 %collective-permute-start.18 = (f32[32,1024]{1,0:T(8,128)S(1)}, f32[32,1024]{1,0:T(8,128)S(1)}, u32[]{:S(2)}, u32[]{:S(2)}) collective-permute-start(f32[32,1024]{1,0:T(8,128)S(1)} %get-tuple-element.48), channel_id=1, source_target_pairs={{0,12},{4,8},{8,4},{12,0},{16,28},{20,24},{24,20},{28,16},{1,13},{... | collective-permute-start | bytes 393224 | tf_op jit(solution)/shard_map/ppermute | solution.py:219

commit v26 on v21

--- a/solution.py
+++ b/solution.py
@@ -33,9 +33,9 @@
 
 def product(left, right, dims=ROWS_BY_COLUMNS):
     (left_high, left_low), (right_high, right_low) = left, right
-    return dot(left_high, right_high, dims) + (
-        dot(left_high, right_low, dims) + dot(left_low, right_high, dims)
-    )
+    rows = left_high.shape[0]
+    both = dot(jnp.concatenate([left_high, left_low], axis=0), right_high, dims)
+    return both[:rows] + (both[rows:] + dot(left_high, right_low, dims))
 
 
 def project_kernel(depth, snapshots_ref, factor_ref, mine_ref, other_ref, *refs):

time: 55.6 us -> 55.5 us (level)
  no operation moved by 1% of the time
where the time goes in v26:
time: 55.5 us; the launch traced here: 55 us
  waiting for transfers between devices  25.2 us (45%)
  starting transfers between devices  22.6 us (41%)
  Pallas kernels  6.43 us (12%)
  between operations  0.7 us (1%)
    ppermute x19, waiting for transfers between devices, swap(): lax.ppermute(value, axis, [(i, i ^ offset) for i in range(lax.axis_size(a...  25.2 us
    ppermute x19, starting transfers between devices, swap(): lax.ppermute(value, axis, [(i, i ^ offset) for i in range(lax.axis_size(a...  22.6 us
    pallas_call x1, Pallas kernels, project(): pl.pallas_call(functools.partial(project_kernel, depth), in_specs=[HBM, H...  2.93 us
    pallas_call x1, Pallas kernels, mix(): pl.pallas_call(functools.partial(mix_kernel, times, order), in_specs=[SME...  2.08 us
  transfers between devices with their start and end apart: 19, of which 9 were waited for; matrix products, arithmetic and copies ran while one was open for 0% of the time, Pallas kernels for 4%

profile of v26, /device:TPU:8, one launch (start us, length us, event | category | flops | bytes accessed | tf_op | source)
XLA Modules:
  0.0 55.0 jit_solution(7474471054228293216)
XLA Ops:
  0.6 2.9 %shard_map.41 = (f32[32,256]{1,0:T(8,128)S(1)}, f32[32,256]{1,0:T(8,128)S(1)}, f32[64,1024]{1,0:T(8,128)S(1)}, f32[64,1024]{1,0:T(8,128)S(1)}, f32[64,1024]{1,0:T(8,128)S(1)}, /*index=5*/f32[64,1024]{1,0:T(8,128)S(1)}) custom-call(f32[64,4096]{1,0:T(8,128)} %snapshots_ref.1, f32[4096,256]{1,0:T(8,128)} %factor_ref.1), custom_call_target="tpu_custom_call" | custom-call | tf_op jit(solution)/shard_map/pallas_call | solution.py:76
  3.6 1.6 %collective-permute-start.1 = (f32[32,256]{1,0:T(8,128)S(1)}, f32[32,256]{1,0:T(8,128)S(1)}, u32[]{:S(2)}, u32[]{:S(2)}) collective-permute-start(f32[32,256]{1,0:T(8,128)S(1)} %get-tuple-element.24), channel_id=1, source_target_pairs={{0,2},{1,3},{2,0},{3,1},{4,6},{5,7},{6,4},{7,5},{8,10},{9,11},{10,... | collective-permute-start | bytes 98312 | tf_op jit(solution)/shard_map/ppermute | solution.py:205
  5.1 0.0 collective-permute-start.2
  5.2 0.6 %collective-permute-start = (f32[32,256]{1,0:T(8,128)S(1)}, f32[32,256]{1,0:T(8,128)S(1)}, u32[]{:S(2)}, u32[]{:S(2)}) collective-permute-start(f32[32,256]{1,0:T(8,128)S(1)} %get-tuple-element.25), channel_id=1, source_target_pairs={{0,1},{1,0},{2,3},{3,2},{4,5},{5,4},{6,7},{7,6},{8,9},{9,8},{10,11... | collective-permute-start | bytes 98312 | tf_op jit(solution)/shard_map/ppermute | solution.py:205
  5.8 1.5 %collective-permute-start.6 = (f32[64,1024]{1,0:T(8,128)S(1)}, f32[64,1024]{1,0:T(8,128)S(1)}, u32[]{:S(2)}, u32[]{:S(2)}) collective-permute-start(f32[64,1024]{1,0:T(8,128)S(1)} %get-tuple-element.26), channel_id=1, source_target_pairs={{0,4},{4,0},{8,12},{12,8},{16,20},{20,16},{24,28},{28,24},{1,5},{5... | collective-permute-start | bytes 786440 | tf_op jit(solution)/shard_map/ppermute | solution.py:205
  7.3 0.5 collective-permute-start.7
  7.7 0.0 collective-permute-done.1
  7.7 0.9 %collective-permute-done.2 = f32[32,256]{1,0:T(8,128)S(1)} collective-permute-done((f32[32,256]{1,0:T(8,128)S(1)}, f32[32,256]{1,0:T(8,128)S(1)}, u32[]{:S(2)}, u32[]{:S(2)}) %collective-permute-start.2) | collective-permute-done | bytes 32800 | tf_op jit(solution)/shard_map/ppermute | solution.py:205
  8.6 0.0 collective-permute-done
  8.6 3.6 %collective-permute-start.5 = (f32[32,256]{1,0:T(8,128)S(1)}, f32[32,256]{1,0:T(8,128)S(1)}, u32[]{:S(2)}, u32[]{:S(2)}) collective-permute-start(f32[32,256]{1,0:T(8,128)S(1)} %add_add_fusion), channel_id=1, source_target_pairs={{0,20},{4,16},{8,28},{12,24},{16,4},{20,0},{24,12},{28,8},{1,21},{... | collective-permute-start | bytes 98312 | tf_op jit(solution)/shard_map/ppermute | solution.py:205
  12.2 0.3 collective-permute-start.4
  12.5 0.5 collective-permute-start.3
  13.0 4.2 %collective-permute-done.5 = f32[32,256]{1,0:T(8,128)S(1)} collective-permute-done((f32[32,256]{1,0:T(8,128)S(1)}, f32[32,256]{1,0:T(8,128)S(1)}, u32[]{:S(2)}, u32[]{:S(2)}) %collective-permute-start.5) | collective-permute-done | bytes 32800 | tf_op jit(solution)/shard_map/ppermute | solution.py:205
  17.2 0.4 collective-permute-done.4
  17.6 0.0 collective-permute-done.3
  17.6 0.0 collective-permute-done.6.refs_1_
  17.6 0.0 collective-permute-done.7.refs_2_
  17.7 0.2 collective-permute-start.9
  17.9 2.4 %collective-permute-start.11 = (f32[64,1024]{1,0:T(8,128)S(1)}, f32[64,1024]{1,0:T(8,128)S(1)}, u32[]{:S(2)}, u32[]{:S(2)}) collective-permute-start(f32[64,1024]{1,0:T(8,128)S(1)} %get-tuple-element.35), channel_id=1, source_target_pairs={{0,12},{4,8},{8,4},{12,0},{16,28},{20,24},{24,20},{28,16},{1,13},{... | collective-permute-start | bytes 786440 | tf_op jit(solution)/shard_map/ppermute | solution.py:205
  20.3 0.0 collective-permute-start.8
  20.3 3.9 %collective-permute-done.9.refs_2_ = f32[128,256]{1,0:T(8,128)S(1)} collective-permute-done((f32[128,256]{1,0:T(8,128)S(1)}, f32[128,256]{1,0:T(8,128)S(1)}, u32[]{:S(2)}, u32[]{:S(2)}) %collective-permute-start.9) | collective-permute-done | bytes 131104 | tf_op jit(solution)/shard_map/ppermute | solution.py:205
  24.2 0.0 collective-permute-start.10
  24.2 0.1 pad_add_fusion.index_ref
  24.2 0.0 collective-permute-done.8.refs_1_
  24.2 1.3 %collective-permute-done.10.refs_3_ = f32[128,256]{1,0:T(8,128)S(1)} collective-permute-done((f32[128,256]{1,0:T(8,128)S(1)}, f32[128,256]{1,0:T(8,128)S(1)}, u32[]{:S(2)}, u32[]{:S(2)}) %collective-permute-start.10) | collective-permute-done | bytes 131104 | tf_op jit(solution)/shard_map/ppermute | solution.py:205
  25.5 2.1 %shard_map.42 = (bf16[256,256]{1,0:T(8,128)(2,1)S(1)}, bf16[256,256]{1,0:T(8,128)(2,1)S(1)}, f32[64,256]{1,0:T(8,128)S(1)}) custom-call(s32[2]{0:T(128)S(1)} %pad_add_fusion.index_ref, f32[128,256]{1,0:T(8,128)S(1)} %pad_maximum_fusion.refs_0_, f32[128,256]{1,0:T(8,128)S(1)} %collective-permute-done.8.refs_1_, ...), custom_call_target="tpu_custom_call" | custom-call | tf_op jit(solution)/shard_map/pallas_call | solution.py:137
  27.6 0.0 collective-permute-done.11.refs_3_
  27.6 0.6 %shard_map.43 = (f32[32,1024]{1,0:T(8,128)S(1)}, f32[32,1024]{1,0:T(8,128)S(1)}, f32[32,1024]{1,0:T(8,128)S(1)}, f32[32,1024]{1,0:T(8,128)S(1)}, f32[32,1024]{1,...) custom-call(bf16[256,256]{1,0:T(8,128)(2,1)S(1)} %get-tuple-element.30.high_ref, ...), custom_call_target="tpu_custom_call" | custom-call | tf_op jit(solution)/shard_map/pallas_call | solution.py:159
  28.2 1.2 %collective-permute-start.14 = (f32[32,1024]{1,0:T(8,128)S(1)}, f32[32,1024]{1,0:T(8,128)S(1)}, u32[]{:S(2)}, u32[]{:S(2)}) collective-permute-start(f32[32,1024]{1,0:T(8,128)S(1)} %get-tuple-element.39), channel_id=1, source_target_pairs={{0,4},{4,0},{8,12},{12,8},{16,20},{20,16},{24,28},{28,24},{1,5},{5... | collective-permute-start | bytes 393224 | tf_op jit(solution)/shard_map/ppermute | solution.py:205
  29.4 1.8 %collective-permute-start.12 = (f32[32,1024]{1,0:T(8,128)S(1)}, f32[32,1024]{1,0:T(8,128)S(1)}, u32[]{:S(2)}, u32[]{:S(2)}) collective-permute-start(f32[32,1024]{1,0:T(8,128)S(1)} %get-tuple-element.36), channel_id=1, source_target_pairs={{0,16},{4,20},{8,24},{12,28},{16,0},{20,4},{24,8},{28,12},{1,17},{... | collective-permute-start | bytes 393224 | tf_op jit(solution)/shard_map/ppermute | solution.py:205
  31.2 1.5 %collective-permute-start.13 = (f32[32,1024]{1,0:T(8,128)S(1)}, f32[32,1024]{1,0:T(8,128)S(1)}, u32[]{:S(2)}, u32[]{:S(2)}) collective-permute-start(f32[32,1024]{1,0:T(8,128)S(1)} %get-tuple-element.37), channel_id=1, source_target_pairs={{0,20},{4,16},{8,28},{12,24},{16,4},{20,0},{24,12},{28,8},{1,21},{... | collective-permute-start | bytes 393224 | tf_op jit(solution)/shard_map/ppermute | solution.py:205
  32.6 0.9 %collective-permute-start.15 = (f32[32,1024]{1,0:T(8,128)S(1)}, f32[32,1024]{1,0:T(8,128)S(1)}, u32[]{:S(2)}, u32[]{:S(2)}) collective-permute-start(f32[32,1024]{1,0:T(8,128)S(1)} %get-tuple-element.41), channel_id=1, source_target_pairs={{0,8},{4,12},{8,0},{12,4},{16,24},{20,28},{24,16},{28,20},{1,9},{5... | collective-permute-start | bytes 393224 | tf_op jit(solution)/shard_map/ppermute | solution.py:205
  33.6 1.2 %collective-permute-start.16 = (f32[32,1024]{1,0:T(8,128)S(1)}, f32[32,1024]{1,0:T(8,128)S(1)}, u32[]{:S(2)}, u32[]{:S(2)}) collective-permute-start(f32[32,1024]{1,0:T(8,128)S(1)} %get-tuple-element.42), channel_id=1, source_target_pairs={{0,24},{4,28},{8,16},{12,20},{16,8},{20,12},{24,0},{28,4},{1,25},{... | collective-permute-start | bytes 393224 | tf_op jit(solution)/shard_map/ppermute | solution.py:205
  34.7 0.0 collective-permute-done.14.refs_2_
  34.7 1.1 %collective-permute-start.17 = (f32[32,1024]{1,0:T(8,128)S(1)}, f32[32,1024]{1,0:T(8,128)S(1)}, u32[]{:S(2)}, u32[]{:S(2)}) collective-permute-start(f32[32,1024]{1,0:T(8,128)S(1)} %get-tuple-element.43), channel_id=1, source_target_pairs={{0,28},{4,24},{8,20},{12,16},{16,12},{20,8},{24,4},{28,0},{1,29},{... | collective-permute-start | bytes 393224 | tf_op jit(solution)/shard_map/ppermute | solution.py:205
  35.8 4.5 %collective-permute-done.12.refs_0_ = f32[32,1024]{1,0:T(8,128)S(1)} collective-permute-done((f32[32,1024]{1,0:T(8,128)S(1)}, f32[32,1024]{1,0:T(8,128)S(1)}, u32[]{:S(2)}, u32[]{:S(2)}) %collective-permute-start.12) | collective-permute-done | bytes 131104 | tf_op jit(solution)/shard_map/ppermute | solution.py:205
  40.3 3.7 %collective-permute-start.18 = (f32[32,1024]{1,0:T(8,128)S(1)}, f32[32,1024]{1,0:T(8,128)S(1)}, u32[]{:S(2)}, u32[]{:S(2)}) collective-permute-start(f32[32,1024]{1,0:T(8,128)S(1)} %get-tuple-element.44), channel_id=1, source_target_pairs={{0,12},{4,8},{8,4},{12,0},{16,28},{20,24},{24,20},{28,16},{1,13},{... | collective-permute-start | bytes 393224 | tf_op jit(solution)/shard_map/ppermute | solution.py:205
  44.1 3.6 %collective-permute-done.13.refs_1_ = f32[32,1024]{1,0:T(8,128)S(1)} collective-permute-done((f32[32,1024]{1,0:T(8,128)S(1)}, f32[32,1024]{1,0:T(8,128)S(1)}, u32[]{:S(2)}, u32[]{:S(2)}) %collective-permute-start.13) | collective-permute-done | bytes 131104 | tf_op jit(solution)/shard_map/ppermute | solution.py:205
  47.6 0.0 collective-permute-done.15.refs_3_
  47.6 4.8 %collective-permute-done.16.refs_4_ = f32[32,1024]{1,0:T(8,128)S(1)} collective-permute-done((f32[32,1024]{1,0:T(8,128)S(1)}, f32[32,1024]{1,0:T(8,128)S(1)}, u32[]{:S(2)}, u32[]{:S(2)}) %collective-permute-start.16) | collective-permute-done | bytes 131104 | tf_op jit(solution)/shard_map/ppermute | solution.py:205
  52.4 1.8 %collective-permute-done.17.refs_5_ = f32[32,1024]{1,0:T(8,128)S(1)} collective-permute-done((f32[32,1024]{1,0:T(8,128)S(1)}, f32[32,1024]{1,0:T(8,128)S(1)}, u32[]{:S(2)}, u32[]{:S(2)}) %collective-permute-start.17) | collective-permute-done | bytes 131104 | tf_op jit(solution)/shard_map/ppermute | solution.py:205
  54.1 0.0 collective-permute-done.18.refs_6_
  54.1 0.8 %shard_map.44 = (f32[64,256]{1,0:T(8,128)}, f32[32,4096]{1,0:T(8,128)}) custom-call(f32[64,256]{1,0:T(8,128)S(1)} %get-tuple-element.29.own_ref, f32[32,1024]{1,0:T(8,128)S(1)} %collective-permute-done.12.refs_0_, f32[32,1024]{1,0:T(8,128)S(1)} %collective-permute-done.13.refs_1_, f32[32,1024]{1,0:T(8,128)S(1)} %collective-permute-done.14.refs_2_, ...), custom_call_target="tpu_custom_call" | custom-call | tf_op jit(solution)/shard_map/pallas_call | solution.py:190
  (2 shorter events, 0.0 us)
Async XLA Ops:
  3.6 4.2 %collective-permute-start.1 = (f32[32,256]{1,0:T(8,128)S(1)}, f32[32,256]{1,0:T(8,128)S(1)}, u32[]{:S(2)}, u32[]{:S(2)}) collective-permute-start(f32[32,256]{1,0:T(8,128)S(1)} %get-tuple-element.24), channel_id=1, source_target_pairs={{0,2},{1,3},{2,0},{3,1},{4,6},{5,7},{6,4},{7,5},{8,10},{9,11},{10,... | collective-permute-start | bytes 98312 | tf_op jit(solution)/shard_map/ppermute | solution.py:205
  5.1 3.4 %collective-permute-start.2 = (f32[32,256]{1,0:T(8,128)S(1)}, f32[32,256]{1,0:T(8,128)S(1)}, u32[]{:S(2)}, u32[]{:S(2)}) collective-permute-start(f32[32,256]{1,0:T(8,128)S(1)} %get-tuple-element.25), channel_id=1, source_target_pairs={{0,3},{1,2},{2,1},{3,0},{4,7},{5,6},{6,5},{7,4},{8,11},{9,10},{10,... | collective-permute-start | bytes 98312 | tf_op jit(solution)/shard_map/ppermute | solution.py:205
  5.2 3.4 %collective-permute-start = (f32[32,256]{1,0:T(8,128)S(1)}, f32[32,256]{1,0:T(8,128)S(1)}, u32[]{:S(2)}, u32[]{:S(2)}) collective-permute-start(f32[32,256]{1,0:T(8,128)S(1)} %get-tuple-element.25), channel_id=1, source_target_pairs={{0,1},{1,0},{2,3},{3,2},{4,5},{5,4},{6,7},{7,6},{8,9},{9,8},{10,11... | collective-permute-start | bytes 98312 | tf_op jit(solution)/shard_map/ppermute | solution.py:205
  5.8 11.9 %collective-permute-start.6 = (f32[64,1024]{1,0:T(8,128)S(1)}, f32[64,1024]{1,0:T(8,128)S(1)}, u32[]{:S(2)}, u32[]{:S(2)}) collective-permute-start(f32[64,1024]{1,0:T(8,128)S(1)} %get-tuple-element.26), channel_id=1, source_target_pairs={{0,4},{4,0},{8,12},{12,8},{16,20},{20,16},{24,28},{28,24},{1,5},{5... | collective-permute-start | bytes 786440 | tf_op jit(solution)/shard_map/ppermute | solution.py:205
  7.3 10.4 %collective-permute-start.7 = (f32[64,1024]{1,0:T(8,128)S(1)}, f32[64,1024]{1,0:T(8,128)S(1)}, u32[]{:S(2)}, u32[]{:S(2)}) collective-permute-start(f32[64,1024]{1,0:T(8,128)S(1)} %get-tuple-element.27), channel_id=1, source_target_pairs={{0,8},{4,12},{8,0},{12,4},{16,24},{20,28},{24,16},{28,20},{1,9},{5... | collective-permute-start | bytes 786440 | tf_op jit(solution)/shard_map/ppermute | solution.py:205
  8.6 8.6 %collective-permute-start.5 = (f32[32,256]{1,0:T(8,128)S(1)}, f32[32,256]{1,0:T(8,128)S(1)}, u32[]{:S(2)}, u32[]{:S(2)}) collective-permute-start(f32[32,256]{1,0:T(8,128)S(1)} %add_add_fusion), channel_id=1, source_target_pairs={{0,20},{4,16},{8,28},{12,24},{16,4},{20,0},{24,12},{28,8},{1,21},{... | collective-permute-start | bytes 98312 | tf_op jit(solution)/shard_map/ppermute | solution.py:205
  12.2 5.4 %collective-permute-start.4 = (f32[32,256]{1,0:T(8,128)S(1)}, f32[32,256]{1,0:T(8,128)S(1)}, u32[]{:S(2)}, u32[]{:S(2)}) collective-permute-start(f32[32,256]{1,0:T(8,128)S(1)} %add_add_fusion), channel_id=1, source_target_pairs={{0,16},{4,20},{8,24},{12,28},{16,0},{20,4},{24,8},{28,12},{1,17},{... | collective-permute-start | bytes 98312 | tf_op jit(solution)/shard_map/ppermute | solution.py:205
  12.5 5.1 %collective-permute-start.3 = (f32[32,256]{1,0:T(8,128)S(1)}, f32[32,256]{1,0:T(8,128)S(1)}, u32[]{:S(2)}, u32[]{:S(2)}) collective-permute-start(f32[32,256]{1,0:T(8,128)S(1)} %add_add_fusion), channel_id=1, source_target_pairs={{0,4},{4,0},{8,12},{12,8},{16,20},{20,16},{24,28},{28,24},{1,5},{5... | collective-permute-start | bytes 98312 | tf_op jit(solution)/shard_map/ppermute | solution.py:205
  17.7 6.5 %collective-permute-start.9 = (f32[128,256]{1,0:T(8,128)S(1)}, f32[128,256]{1,0:T(8,128)S(1)}, u32[]{:S(2)}, u32[]{:S(2)}) collective-permute-start(f32[128,256]{1,0:T(8,128)S(1)} %pad_maximum_fusion.refs_0_), channel_id=1, source_target_pairs={{0,8},{4,12},{8,0},{12,4},{16,24},{20,28},{24,16},{28,20},{1,9},{5... | collective-permute-start | bytes 393224 | tf_op jit(solution)/shard_map/ppermute | solution.py:205
  17.9 9.7 %collective-permute-start.11 = (f32[64,1024]{1,0:T(8,128)S(1)}, f32[64,1024]{1,0:T(8,128)S(1)}, u32[]{:S(2)}, u32[]{:S(2)}) collective-permute-start(f32[64,1024]{1,0:T(8,128)S(1)} %get-tuple-element.35), channel_id=1, source_target_pairs={{0,12},{4,8},{8,4},{12,0},{16,28},{20,24},{24,20},{28,16},{1,13},{... | collective-permute-start | bytes 786440 | tf_op jit(solution)/shard_map/ppermute | solution.py:205
  20.3 3.9 %collective-permute-start.8 = (f32[128,256]{1,0:T(8,128)S(1)}, f32[128,256]{1,0:T(8,128)S(1)}, u32[]{:S(2)}, u32[]{:S(2)}) collective-permute-start(f32[128,256]{1,0:T(8,128)S(1)} %pad_maximum_fusion.refs_0_), channel_id=1, source_target_pairs={{0,1},{1,0},{2,3},{3,2},{4,5},{5,4},{6,7},{7,6},{8,9},{9,8},{10,11... | collective-permute-start | bytes 393224 | tf_op jit(solution)/shard_map/ppermute | solution.py:205
  24.2 1.3 %collective-permute-start.10 = (f32[128,256]{1,0:T(8,128)S(1)}, f32[128,256]{1,0:T(8,128)S(1)}, u32[]{:S(2)}, u32[]{:S(2)}) collective-permute-start(f32[128,256]{1,0:T(8,128)S(1)} %collective-permute-done.9.refs_2_), channel_id=1, source_target_pairs={{0,1},{1,0},{2,3},{3,2},{4,5},{5,4},{6,7},{7,6},{8,9},{9,8},{10,11... | collective-permute-start | bytes 393224 | tf_op jit(solution)/shard_map/ppermute | solution.py:205
  28.2 6.5 %collective-permute-start.14 = (f32[32,1024]{1,0:T(8,128)S(1)}, f32[32,1024]{1,0:T(8,128)S(1)}, u32[]{:S(2)}, u32[]{:S(2)}) collective-permute-start(f32[32,1024]{1,0:T(8,128)S(1)} %get-tuple-element.39), channel_id=1, source_target_pairs={{0,4},{4,0},{8,12},{12,8},{16,20},{20,16},{24,28},{28,24},{1,5},{5... | collective-permute-start | bytes 393224 | tf_op jit(solution)/shard_map/ppermute | solution.py:205
  29.4 10.9 %collective-permute-start.12 = (f32[32,1024]{1,0:T(8,128)S(1)}, f32[32,1024]{1,0:T(8,128)S(1)}, u32[]{:S(2)}, u32[]{:S(2)}) collective-permute-start(f32[32,1024]{1,0:T(8,128)S(1)} %get-tuple-element.36), channel_id=1, source_target_pairs={{0,16},{4,20},{8,24},{12,28},{16,0},{20,4},{24,8},{28,12},{1,17},{... | collective-permute-start | bytes 393224 | tf_op jit(solution)/shard_map/ppermute | solution.py:205
  31.2 16.5 %collective-permute-start.13 = (f32[32,1024]{1,0:T(8,128)S(1)}, f32[32,1024]{1,0:T(8,128)S(1)}, u32[]{:S(2)}, u32[]{:S(2)}) collective-permute-start(f32[32,1024]{1,0:T(8,128)S(1)} %get-tuple-element.37), channel_id=1, source_target_pairs={{0,20},{4,16},{8,28},{12,24},{16,4},{20,0},{24,12},{28,8},{1,21},{... | collective-permute-start | bytes 393224 | tf_op jit(solution)/shard_map/ppermute | solution.py:205
  32.6 15.0 %collective-permute-start.15 = (f32[32,1024]{1,0:T(8,128)S(1)}, f32[32,1024]{1,0:T(8,128)S(1)}, u32[]{:S(2)}, u32[]{:S(2)}) collective-permute-start(f32[32,1024]{1,0:T(8,128)S(1)} %get-tuple-element.41), channel_id=1, source_target_pairs={{0,8},{4,12},{8,0},{12,4},{16,24},{20,28},{24,16},{28,20},{1,9},{5... | collective-permute-start | bytes 393224 | tf_op jit(solution)/shard_map/ppermute | solution.py:205
  33.6 18.8 %collective-permute-start.16 = (f32[32,1024]{1,0:T(8,128)S(1)}, f32[32,1024]{1,0:T(8,128)S(1)}, u32[]{:S(2)}, u32[]{:S(2)}) collective-permute-start(f32[32,1024]{1,0:T(8,128)S(1)} %get-tuple-element.42), channel_id=1, source_target_pairs={{0,24},{4,28},{8,16},{12,20},{16,8},{20,12},{24,0},{28,4},{1,25},{... | collective-permute-start | bytes 393224 | tf_op jit(solution)/shard_map/ppermute | solution.py:205
  34.7 19.4 %collective-permute-start.17 = (f32[32,1024]{1,0:T(8,128)S(1)}, f32[32,1024]{1,0:T(8,128)S(1)}, u32[]{:S(2)}, u32[]{:S(2)}) collective-permute-start(f32[32,1024]{1,0:T(8,128)S(1)} %get-tuple-element.43), channel_id=1, source_target_pairs={{0,28},{4,24},{8,20},{12,16},{16,12},{20,8},{24,4},{28,0},{1,29},{... | collective-permute-start | bytes 393224 | tf_op jit(solution)/shard_map/ppermute | solution.py:205
  40.3 13.8 %collective-permute-start.18 = (f32[32,1024]{1,0:T(8,128)S(1)}, f32[32,1024]{1,0:T(8,128)S(1)}, u32[]{:S(2)}, u32[]{:S(2)}) collective-permute-start(f32[32,1024]{1,0:T(8,128)S(1)} %get-tuple-element.44), channel_id=1, source_target_pairs={{0,12},{4,8},{8,4},{12,0},{16,28},{20,24},{24,20},{28,16},{1,13},{... | collective-permute-start | bytes 393224 | tf_op jit(solution)/shard_map/ppermute | solution.py:205

commit v27 on v21

--- a/solution.py
+++ b/solution.py
@@ -222,7 +222,7 @@
     mine = terms[0]
 
     near = group // 2
-    order = [k for k in range(times) if k % group < near]
+    order = [0] + [k for k in [*range(group, times), *range(1, group)] if k % group < near]
     mine = jnp.concatenate([mine] + [swap(mine, "tm", k) for k in order[1:]], axis=0)
     mine, *parts[1:3] = lax.optimization_barrier((mine, *parts[1:3]))
     rest = swap(mine, "tm", near)

time: 55.6 us -> 55.8 us (level)
  starting transfers between devices: 22.6 us -> 23.6 us
  waiting for transfers between devices: 25.2 us -> 24.6 us
    ppermute x19, starting transfers between devices: 22.6 us -> 23.6 us  [swap(): lax.ppermute(value, axis, [(i, i ^ offset) for i in range(lax.axis_size(a...]
    ppermute x19, waiting for transfers between devices: 25.2 us -> 24.6 us  [swap(): lax.ppermute(value, axis, [(i, i ^ offset) for i in range(lax.axis_size(a...]
  transfers between devices with their start and end apart: 19 -> 19, of which waited for: 9 -> 11; matrix products, arithmetic and copies ran while one was open for 0% -> 0% of each run, Pallas kernels for 4% -> 4%
where the time goes in v27:
time: 55.8 us; the launch traced here: 55.5 us
  waiting for transfers between devices  24.6 us (44%)
  starting transfers between devices  23.6 us (42%)
  Pallas kernels  6.5 us (12%)
  between operations  0.69 us (1%)
    ppermute x19, waiting for transfers between devices, swap(): lax.ppermute(value, axis, [(i, i ^ offset) for i in range(lax.axis_size(a...  24.6 us
    ppermute x19, starting transfers between devices, swap(): lax.ppermute(value, axis, [(i, i ^ offset) for i in range(lax.axis_size(a...  23.6 us
    pallas_call x1, Pallas kernels, project(): pl.pallas_call(functools.partial(project_kernel, depth), in_specs=[HBM, H...  2.93 us
    pallas_call x1, Pallas kernels, mix(): pl.pallas_call(functools.partial(mix_kernel, times, order), in_specs=[SME...  2.14 us
  transfers between devices with their start and end apart: 19, of which 11 were waited for; matrix products, arithmetic and copies ran while one was open for 0% of the time, Pallas kernels for 4%

profile of v27, /device:TPU:8, one launch (start us, length us, event | category | flops | bytes accessed | tf_op | source)
XLA Modules:
  0.0 55.5 jit_solution(7262532978106491939)
XLA Ops:
  0.6 2.9 %shard_map.41 = (f32[32,256]{1,0:T(8,128)S(1)}, f32[32,256]{1,0:T(8,128)S(1)}, f32[64,1024]{1,0:T(8,128)S(1)}, f32[64,1024]{1,0:T(8,128)S(1)}, f32[64,1024]{1,0:T(8,128)S(1)}, /*index=5*/f32[64,1024]{1,0:T(8,128)S(1)}) custom-call(f32[64,4096]{1,0:T(8,128)} %snapshots_ref.1, f32[4096,256]{1,0:T(8,128)} %factor_ref.1), custom_call_target="tpu_custom_call" | custom-call | tf_op jit(solution)/shard_map/pallas_call | solution.py:76
  3.6 1.6 %collective-permute-start.1 = (f32[32,256]{1,0:T(8,128)S(1)}, f32[32,256]{1,0:T(8,128)S(1)}, u32[]{:S(2)}, u32[]{:S(2)}) collective-permute-start(f32[32,256]{1,0:T(8,128)S(1)} %get-tuple-element.24), channel_id=1, source_target_pairs={{0,2},{1,3},{2,0},{3,1},{4,6},{5,7},{6,4},{7,5},{8,10},{9,11},{10,... | collective-permute-start | bytes 98312 | tf_op jit(solution)/shard_map/ppermute | solution.py:205
  5.1 0.0 collective-permute-start.2
  5.2 0.6 %collective-permute-start = (f32[32,256]{1,0:T(8,128)S(1)}, f32[32,256]{1,0:T(8,128)S(1)}, u32[]{:S(2)}, u32[]{:S(2)}) collective-permute-start(f32[32,256]{1,0:T(8,128)S(1)} %get-tuple-element.25), channel_id=1, source_target_pairs={{0,1},{1,0},{2,3},{3,2},{4,5},{5,4},{6,7},{7,6},{8,9},{9,8},{10,11... | collective-permute-start | bytes 98312 | tf_op jit(solution)/shard_map/ppermute | solution.py:205
  5.8 1.5 %collective-permute-start.6 = (f32[64,1024]{1,0:T(8,128)S(1)}, f32[64,1024]{1,0:T(8,128)S(1)}, u32[]{:S(2)}, u32[]{:S(2)}) collective-permute-start(f32[64,1024]{1,0:T(8,128)S(1)} %get-tuple-element.26), channel_id=1, source_target_pairs={{0,4},{4,0},{8,12},{12,8},{16,20},{20,16},{24,28},{28,24},{1,5},{5... | collective-permute-start | bytes 786440 | tf_op jit(solution)/shard_map/ppermute | solution.py:205
  7.3 0.5 collective-permute-start.7
  7.7 0.0 collective-permute-done.1
  7.7 0.9 %collective-permute-done.2 = f32[32,256]{1,0:T(8,128)S(1)} collective-permute-done((f32[32,256]{1,0:T(8,128)S(1)}, f32[32,256]{1,0:T(8,128)S(1)}, u32[]{:S(2)}, u32[]{:S(2)}) %collective-permute-start.2) | collective-permute-done | bytes 32800 | tf_op jit(solution)/shard_map/ppermute | solution.py:205
  8.6 0.0 collective-permute-done
  8.6 1.6 %collective-permute-start.5 = (f32[32,256]{1,0:T(8,128)S(1)}, f32[32,256]{1,0:T(8,128)S(1)}, u32[]{:S(2)}, u32[]{:S(2)}) collective-permute-start(f32[32,256]{1,0:T(8,128)S(1)} %add_add_fusion), channel_id=1, source_target_pairs={{0,4},{4,0},{8,12},{12,8},{16,20},{20,16},{24,28},{28,24},{1,5},{5... | collective-permute-start | bytes 98312 | tf_op jit(solution)/shard_map/ppermute | solution.py:205
  10.1 2.6 %collective-permute-start.4 = (f32[32,256]{1,0:T(8,128)S(1)}, f32[32,256]{1,0:T(8,128)S(1)}, u32[]{:S(2)}, u32[]{:S(2)}) collective-permute-start(f32[32,256]{1,0:T(8,128)S(1)} %add_add_fusion), channel_id=1, source_target_pairs={{0,20},{4,16},{8,28},{12,24},{16,4},{20,0},{24,12},{28,8},{1,21},{... | collective-permute-start | bytes 98312 | tf_op jit(solution)/shard_map/ppermute | solution.py:205
  12.7 0.3 collective-permute-start.3
  13.0 1.6 %collective-permute-done.5 = f32[32,256]{1,0:T(8,128)S(1)} collective-permute-done((f32[32,256]{1,0:T(8,128)S(1)}, f32[32,256]{1,0:T(8,128)S(1)}, u32[]{:S(2)}, u32[]{:S(2)}) %collective-permute-start.5) | collective-permute-done | bytes 32800 | tf_op jit(solution)/shard_map/ppermute | solution.py:205
  14.7 2.6 %collective-permute-done.4 = f32[32,256]{1,0:T(8,128)S(1)} collective-permute-done((f32[32,256]{1,0:T(8,128)S(1)}, f32[32,256]{1,0:T(8,128)S(1)}, u32[]{:S(2)}, u32[]{:S(2)}) %collective-permute-start.4) | collective-permute-done | bytes 32800 | tf_op jit(solution)/shard_map/ppermute | solution.py:205
  17.2 0.4 collective-permute-done.3
  17.6 0.0 collective-permute-done.6.refs_1_
  17.6 0.0 collective-permute-done.7.refs_2_
  17.6 0.7 %collective-permute-start.9 = (f32[128,256]{1,0:T(8,128)S(1)}, f32[128,256]{1,0:T(8,128)S(1)}, u32[]{:S(2)}, u32[]{:S(2)}) collective-permute-start(f32[128,256]{1,0:T(8,128)S(1)} %pad_maximum_fusion.refs_0_), channel_id=1, source_target_pairs={{0,8},{4,12},{8,0},{12,4},{16,24},{20,28},{24,16},{28,20},{1,9},{5... | collective-permute-start | bytes 393224 | tf_op jit(solution)/shard_map/ppermute | solution.py:205
  18.4 2.2 %collective-permute-start.11 = (f32[64,1024]{1,0:T(8,128)S(1)}, f32[64,1024]{1,0:T(8,128)S(1)}, u32[]{:S(2)}, u32[]{:S(2)}) collective-permute-start(f32[64,1024]{1,0:T(8,128)S(1)} %get-tuple-element.35), channel_id=1, source_target_pairs={{0,12},{4,8},{8,4},{12,0},{16,28},{20,24},{24,20},{28,16},{1,13},{... | collective-permute-start | bytes 786440 | tf_op jit(solution)/shard_map/ppermute | solution.py:205
  20.6 0.0 collective-permute-start.8
  20.6 3.6 %collective-permute-done.9.refs_2_ = f32[128,256]{1,0:T(8,128)S(1)} collective-permute-done((f32[128,256]{1,0:T(8,128)S(1)}, f32[128,256]{1,0:T(8,128)S(1)}, u32[]{:S(2)}, u32[]{:S(2)}) %collective-permute-start.9) | collective-permute-done | bytes 131104 | tf_op jit(solution)/shard_map/ppermute | solution.py:205
  24.1 0.0 collective-permute-start.10
  24.2 0.1 pad_add_fusion.index_ref
  24.2 0.0 collective-permute-done.8.refs_1_
  24.2 1.3 %collective-permute-done.10.refs_3_ = f32[128,256]{1,0:T(8,128)S(1)} collective-permute-done((f32[128,256]{1,0:T(8,128)S(1)}, f32[128,256]{1,0:T(8,128)S(1)}, u32[]{:S(2)}, u32[]{:S(2)}) %collective-permute-start.10) | collective-permute-done | bytes 131104 | tf_op jit(solution)/shard_map/ppermute | solution.py:205
  25.5 2.1 %shard_map.42 = (bf16[256,256]{1,0:T(8,128)(2,1)S(1)}, bf16[256,256]{1,0:T(8,128)(2,1)S(1)}, f32[64,256]{1,0:T(8,128)S(1)}) custom-call(s32[2]{0:T(128)S(1)} %pad_add_fusion.index_ref, f32[128,256]{1,0:T(8,128)S(1)} %pad_maximum_fusion.refs_0_, f32[128,256]{1,0:T(8,128)S(1)} %collective-permute-done.8.refs_1_, ...), custom_call_target="tpu_custom_call" | custom-call | tf_op jit(solution)/shard_map/pallas_call | solution.py:137
  27.6 0.5 collective-permute-done.11.refs_3_
  28.1 0.6 %shard_map.43 = (f32[32,1024]{1,0:T(8,128)S(1)}, f32[32,1024]{1,0:T(8,128)S(1)}, f32[32,1024]{1,0:T(8,128)S(1)}, f32[32,1024]{1,0:T(8,128)S(1)}, f32[32,1024]{1,...) custom-call(bf16[256,256]{1,0:T(8,128)(2,1)S(1)} %get-tuple-element.30.high_ref, ...), custom_call_target="tpu_custom_call" | custom-call | tf_op jit(solution)/shard_map/pallas_call | solution.py:159
  28.7 1.0 %collective-permute-start.14 = (f32[32,1024]{1,0:T(8,128)S(1)}, f32[32,1024]{1,0:T(8,128)S(1)}, u32[]{:S(2)}, u32[]{:S(2)}) collective-permute-start(f32[32,1024]{1,0:T(8,128)S(1)} %get-tuple-element.39), channel_id=1, source_target_pairs={{0,4},{4,0},{8,12},{12,8},{16,20},{20,16},{24,28},{28,24},{1,5},{5... | collective-permute-start | bytes 393224 | tf_op jit(solution)/shard_map/ppermute | solution.py:205
  29.7 1.1 %collective-permute-start.12 = (f32[32,1024]{1,0:T(8,128)S(1)}, f32[32,1024]{1,0:T(8,128)S(1)}, u32[]{:S(2)}, u32[]{:S(2)}) collective-permute-start(f32[32,1024]{1,0:T(8,128)S(1)} %get-tuple-element.36), channel_id=1, source_target_pairs={{0,16},{4,20},{8,24},{12,28},{16,0},{20,4},{24,8},{28,12},{1,17},{... | collective-permute-start | bytes 393224 | tf_op jit(solution)/shard_map/ppermute | solution.py:205
  30.8 2.4 %collective-permute-start.13 = (f32[32,1024]{1,0:T(8,128)S(1)}, f32[32,1024]{1,0:T(8,128)S(1)}, u32[]{:S(2)}, u32[]{:S(2)}) collective-permute-start(f32[32,1024]{1,0:T(8,128)S(1)} %get-tuple-element.37), channel_id=1, source_target_pairs={{0,20},{4,16},{8,28},{12,24},{16,4},{20,0},{24,12},{28,8},{1,21},{... | collective-permute-start | bytes 393224 | tf_op jit(solution)/shard_map/ppermute | solution.py:205
  33.2 0.4 collective-permute-start.15
  33.6 1.4 %collective-permute-start.16 = (f32[32,1024]{1,0:T(8,128)S(1)}, f32[32,1024]{1,0:T(8,128)S(1)}, u32[]{:S(2)}, u32[]{:S(2)}) collective-permute-start(f32[32,1024]{1,0:T(8,128)S(1)} %get-tuple-element.42), channel_id=1, source_target_pairs={{0,24},{4,28},{8,16},{12,20},{16,8},{20,12},{24,0},{28,4},{1,25},{... | collective-permute-start | bytes 393224 | tf_op jit(solution)/shard_map/ppermute | solution.py:205
  34.9 0.0 collective-permute-done.14.refs_2_
  34.9 1.5 %collective-permute-start.17 = (f32[32,1024]{1,0:T(8,128)S(1)}, f32[32,1024]{1,0:T(8,128)S(1)}, u32[]{:S(2)}, u32[]{:S(2)}) collective-permute-start(f32[32,1024]{1,0:T(8,128)S(1)} %get-tuple-element.43), channel_id=1, source_target_pairs={{0,28},{4,24},{8,20},{12,16},{16,12},{20,8},{24,4},{28,0},{1,29},{... | collective-permute-start | bytes 393224 | tf_op jit(solution)/shard_map/ppermute | solution.py:205
  36.4 3.7 %collective-permute-done.12.refs_0_ = f32[32,1024]{1,0:T(8,128)S(1)} collective-permute-done((f32[32,1024]{1,0:T(8,128)S(1)}, f32[32,1024]{1,0:T(8,128)S(1)}, u32[]{:S(2)}, u32[]{:S(2)}) %collective-permute-start.12) | collective-permute-done | bytes 131104 | tf_op jit(solution)/shard_map/ppermute | solution.py:205
  40.2 4.4 %collective-permute-start.18 = (f32[32,1024]{1,0:T(8,128)S(1)}, f32[32,1024]{1,0:T(8,128)S(1)}, u32[]{:S(2)}, u32[]{:S(2)}) collective-permute-start(f32[32,1024]{1,0:T(8,128)S(1)} %get-tuple-element.44), channel_id=1, source_target_pairs={{0,12},{4,8},{8,4},{12,0},{16,28},{20,24},{24,20},{28,16},{1,13},{... | collective-permute-start | bytes 393224 | tf_op jit(solution)/shard_map/ppermute | solution.py:205
  44.6 3.1 %collective-permute-done.13.refs_1_ = f32[32,1024]{1,0:T(8,128)S(1)} collective-permute-done((f32[32,1024]{1,0:T(8,128)S(1)}, f32[32,1024]{1,0:T(8,128)S(1)}, u32[]{:S(2)}, u32[]{:S(2)}) %collective-permute-start.13) | collective-permute-done | bytes 131104 | tf_op jit(solution)/shard_map/ppermute | solution.py:205
  47.7 0.0 collective-permute-done.15.refs_3_
  47.7 5.2 %collective-permute-done.16.refs_4_ = f32[32,1024]{1,0:T(8,128)S(1)} collective-permute-done((f32[32,1024]{1,0:T(8,128)S(1)}, f32[32,1024]{1,0:T(8,128)S(1)}, u32[]{:S(2)}, u32[]{:S(2)}) %collective-permute-start.16) | collective-permute-done | bytes 131104 | tf_op jit(solution)/shard_map/ppermute | solution.py:205
  52.9 1.8 %collective-permute-done.17.refs_5_ = f32[32,1024]{1,0:T(8,128)S(1)} collective-permute-done((f32[32,1024]{1,0:T(8,128)S(1)}, f32[32,1024]{1,0:T(8,128)S(1)}, u32[]{:S(2)}, u32[]{:S(2)}) %collective-permute-start.17) | collective-permute-done | bytes 131104 | tf_op jit(solution)/shard_map/ppermute | solution.py:205
  54.7 0.0 collective-permute-done.18.refs_6_
  54.7 0.8 %shard_map.44 = (f32[64,256]{1,0:T(8,128)}, f32[32,4096]{1,0:T(8,128)}) custom-call(f32[64,256]{1,0:T(8,128)S(1)} %get-tuple-element.29.own_ref, f32[32,1024]{1,0:T(8,128)S(1)} %collective-permute-done.12.refs_0_, f32[32,1024]{1,0:T(8,128)S(1)} %collective-permute-done.13.refs_1_, f32[32,1024]{1,0:T(8,128)S(1)} %collective-permute-done.14.refs_2_, ...), custom_call_target="tpu_custom_call" | custom-call | tf_op jit(solution)/shard_map/pallas_call | solution.py:190
  (2 shorter events, 0.0 us)
Async XLA Ops:
  3.6 4.2 %collective-permute-start.1 = (f32[32,256]{1,0:T(8,128)S(1)}, f32[32,256]{1,0:T(8,128)S(1)}, u32[]{:S(2)}, u32[]{:S(2)}) collective-permute-start(f32[32,256]{1,0:T(8,128)S(1)} %get-tuple-element.24), channel_id=1, source_target_pairs={{0,2},{1,3},{2,0},{3,1},{4,6},{5,7},{6,4},{7,5},{8,10},{9,11},{10,... | collective-permute-start | bytes 98312 | tf_op jit(solution)/shard_map/ppermute | solution.py:205
  5.1 3.4 %collective-permute-start.2 = (f32[32,256]{1,0:T(8,128)S(1)}, f32[32,256]{1,0:T(8,128)S(1)}, u32[]{:S(2)}, u32[]{:S(2)}) collective-permute-start(f32[32,256]{1,0:T(8,128)S(1)} %get-tuple-element.25), channel_id=1, source_target_pairs={{0,3},{1,2},{2,1},{3,0},{4,7},{5,6},{6,5},{7,4},{8,11},{9,10},{10,... | collective-permute-start | bytes 98312 | tf_op jit(solution)/shard_map/ppermute | solution.py:205
  5.2 3.4 %collective-permute-start = (f32[32,256]{1,0:T(8,128)S(1)}, f32[32,256]{1,0:T(8,128)S(1)}, u32[]{:S(2)}, u32[]{:S(2)}) collective-permute-start(f32[32,256]{1,0:T(8,128)S(1)} %get-tuple-element.25), channel_id=1, source_target_pairs={{0,1},{1,0},{2,3},{3,2},{4,5},{5,4},{6,7},{7,6},{8,9},{9,8},{10,11... | collective-permute-start | bytes 98312 | tf_op jit(solution)/shard_map/ppermute | solution.py:205
  5.8 11.9 %collective-permute-start.6 = (f32[64,1024]{1,0:T(8,128)S(1)}, f32[64,1024]{1,0:T(8,128)S(1)}, u32[]{:S(2)}, u32[]{:S(2)}) collective-permute-start(f32[64,1024]{1,0:T(8,128)S(1)} %get-tuple-element.26), channel_id=1, source_target_pairs={{0,4},{4,0},{8,12},{12,8},{16,20},{20,16},{24,28},{28,24},{1,5},{5... | collective-permute-start | bytes 786440 | tf_op jit(solution)/shard_map/ppermute | solution.py:205
  7.3 10.4 %collective-permute-start.7 = (f32[64,1024]{1,0:T(8,128)S(1)}, f32[64,1024]{1,0:T(8,128)S(1)}, u32[]{:S(2)}, u32[]{:S(2)}) collective-permute-start(f32[64,1024]{1,0:T(8,128)S(1)} %get-tuple-element.27), channel_id=1, source_target_pairs={{0,8},{4,12},{8,0},{12,4},{16,24},{20,28},{24,16},{28,20},{1,9},{5... | collective-permute-start | bytes 786440 | tf_op jit(solution)/shard_map/ppermute | solution.py:205
  8.6 6.1 %collective-permute-start.5 = (f32[32,256]{1,0:T(8,128)S(1)}, f32[32,256]{1,0:T(8,128)S(1)}, u32[]{:S(2)}, u32[]{:S(2)}) collective-permute-start(f32[32,256]{1,0:T(8,128)S(1)} %add_add_fusion), channel_id=1, source_target_pairs={{0,4},{4,0},{8,12},{12,8},{16,20},{20,16},{24,28},{28,24},{1,5},{5... | collective-permute-start | bytes 98312 | tf_op jit(solution)/shard_map/ppermute | solution.py:205
  10.1 7.1 %collective-permute-start.4 = (f32[32,256]{1,0:T(8,128)S(1)}, f32[32,256]{1,0:T(8,128)S(1)}, u32[]{:S(2)}, u32[]{:S(2)}) collective-permute-start(f32[32,256]{1,0:T(8,128)S(1)} %add_add_fusion), channel_id=1, source_target_pairs={{0,20},{4,16},{8,28},{12,24},{16,4},{20,0},{24,12},{28,8},{1,21},{... | collective-permute-start | bytes 98312 | tf_op jit(solution)/shard_map/ppermute | solution.py:205
  12.7 4.9 %collective-permute-start.3 = (f32[32,256]{1,0:T(8,128)S(1)}, f32[32,256]{1,0:T(8,128)S(1)}, u32[]{:S(2)}, u32[]{:S(2)}) collective-permute-start(f32[32,256]{1,0:T(8,128)S(1)} %add_add_fusion), channel_id=1, source_target_pairs={{0,16},{4,20},{8,24},{12,28},{16,0},{20,4},{24,8},{28,12},{1,17},{... | collective-permute-start | bytes 98312 | tf_op jit(solution)/shard_map/ppermute | solution.py:205
  17.6 6.5 %collective-permute-start.9 = (f32[128,256]{1,0:T(8,128)S(1)}, f32[128,256]{1,0:T(8,128)S(1)}, u32[]{:S(2)}, u32[]{:S(2)}) collective-permute-start(f32[128,256]{1,0:T(8,128)S(1)} %pad_maximum_fusion.refs_0_), channel_id=1, source_target_pairs={{0,8},{4,12},{8,0},{12,4},{16,24},{20,28},{24,16},{28,20},{1,9},{5... | collective-permute-start | bytes 393224 | tf_op jit(solution)/shard_map/ppermute | solution.py:205
  18.4 9.8 %collective-permute-start.11 = (f32[64,1024]{1,0:T(8,128)S(1)}, f32[64,1024]{1,0:T(8,128)S(1)}, u32[]{:S(2)}, u32[]{:S(2)}) collective-permute-start(f32[64,1024]{1,0:T(8,128)S(1)} %get-tuple-element.35), channel_id=1, source_target_pairs={{0,12},{4,8},{8,4},{12,0},{16,28},{20,24},{24,20},{28,16},{1,13},{... | collective-permute-start | bytes 786440 | tf_op jit(solution)/shard_map/ppermute | solution.py:205
  20.6 3.7 %collective-permute-start.8 = (f32[128,256]{1,0:T(8,128)S(1)}, f32[128,256]{1,0:T(8,128)S(1)}, u32[]{:S(2)}, u32[]{:S(2)}) collective-permute-start(f32[128,256]{1,0:T(8,128)S(1)} %pad_maximum_fusion.refs_0_), channel_id=1, source_target_pairs={{0,1},{1,0},{2,3},{3,2},{4,5},{5,4},{6,7},{7,6},{8,9},{9,8},{10,11... | collective-permute-start | bytes 393224 | tf_op jit(solution)/shard_map/ppermute | solution.py:205
  24.1 1.3 %collective-permute-start.10 = (f32[128,256]{1,0:T(8,128)S(1)}, f32[128,256]{1,0:T(8,128)S(1)}, u32[]{:S(2)}, u32[]{:S(2)}) collective-permute-start(f32[128,256]{1,0:T(8,128)S(1)} %collective-permute-done.9.refs_2_), channel_id=1, source_target_pairs={{0,1},{1,0},{2,3},{3,2},{4,5},{5,4},{6,7},{7,6},{8,9},{9,8},{10,11... | collective-permute-start | bytes 393224 | tf_op jit(solution)/shard_map/ppermute | solution.py:205
  28.7 6.2 %collective-permute-start.14 = (f32[32,1024]{1,0:T(8,128)S(1)}, f32[32,1024]{1,0:T(8,128)S(1)}, u32[]{:S(2)}, u32[]{:S(2)}) collective-permute-start(f32[32,1024]{1,0:T(8,128)S(1)} %get-tuple-element.39), channel_id=1, source_target_pairs={{0,4},{4,0},{8,12},{12,8},{16,20},{20,16},{24,28},{28,24},{1,5},{5... | collective-permute-start | bytes 393224 | tf_op jit(solution)/shard_map/ppermute | solution.py:205
  29.7 10.5 %collective-permute-start.12 = (f32[32,1024]{1,0:T(8,128)S(1)}, f32[32,1024]{1,0:T(8,128)S(1)}, u32[]{:S(2)}, u32[]{:S(2)}) collective-permute-start(f32[32,1024]{1,0:T(8,128)S(1)} %get-tuple-element.36), channel_id=1, source_target_pairs={{0,16},{4,20},{8,24},{12,28},{16,0},{20,4},{24,8},{28,12},{1,17},{... | collective-permute-start | bytes 393224 | tf_op jit(solution)/shard_map/ppermute | solution.py:205
  30.8 16.9 %collective-permute-start.13 = (f32[32,1024]{1,0:T(8,128)S(1)}, f32[32,1024]{1,0:T(8,128)S(1)}, u32[]{:S(2)}, u32[]{:S(2)}) collective-permute-start(f32[32,1024]{1,0:T(8,128)S(1)} %get-tuple-element.37), channel_id=1, source_target_pairs={{0,20},{4,16},{8,28},{12,24},{16,4},{20,0},{24,12},{28,8},{1,21},{... | collective-permute-start | bytes 393224 | tf_op jit(solution)/shard_map/ppermute | solution.py:205
  33.2 14.5 %collective-permute-start.15 = (f32[32,1024]{1,0:T(8,128)S(1)}, f32[32,1024]{1,0:T(8,128)S(1)}, u32[]{:S(2)}, u32[]{:S(2)}) collective-permute-start(f32[32,1024]{1,0:T(8,128)S(1)} %get-tuple-element.41), channel_id=1, source_target_pairs={{0,8},{4,12},{8,0},{12,4},{16,24},{20,28},{24,16},{28,20},{1,9},{5... | collective-permute-start | bytes 393224 | tf_op jit(solution)/shard_map/ppermute | solution.py:205
  33.6 19.4 %collective-permute-start.16 = (f32[32,1024]{1,0:T(8,128)S(1)}, f32[32,1024]{1,0:T(8,128)S(1)}, u32[]{:S(2)}, u32[]{:S(2)}) collective-permute-start(f32[32,1024]{1,0:T(8,128)S(1)} %get-tuple-element.42), channel_id=1, source_target_pairs={{0,24},{4,28},{8,16},{12,20},{16,8},{20,12},{24,0},{28,4},{1,25},{... | collective-permute-start | bytes 393224 | tf_op jit(solution)/shard_map/ppermute | solution.py:205
  34.9 19.8 %collective-permute-start.17 = (f32[32,1024]{1,0:T(8,128)S(1)}, f32[32,1024]{1,0:T(8,128)S(1)}, u32[]{:S(2)}, u32[]{:S(2)}) collective-permute-start(f32[32,1024]{1,0:T(8,128)S(1)} %get-tuple-element.43), channel_id=1, source_target_pairs={{0,28},{4,24},{8,20},{12,16},{16,12},{20,8},{24,4},{28,0},{1,29},{... | collective-permute-start | bytes 393224 | tf_op jit(solution)/shard_map/ppermute | solution.py:205
  40.2 14.5 %collective-permute-start.18 = (f32[32,1024]{1,0:T(8,128)S(1)}, f32[32,1024]{1,0:T(8,128)S(1)}, u32[]{:S(2)}, u32[]{:S(2)}) collective-permute-start(f32[32,1024]{1,0:T(8,128)S(1)} %get-tuple-element.44), channel_id=1, source_target_pairs={{0,12},{4,8},{8,4},{12,0},{16,28},{20,24},{24,20},{28,16},{1,13},{... | collective-permute-start | bytes 393224 | tf_op jit(solution)/shard_map/ppermute | solution.py:205

commit v28 on v26

--- a/solution.py
+++ b/solution.py
@@ -144,26 +144,39 @@
     )(index, *halves)
 
 
-def load_kernel(group, high_ref, low_ref, *refs):
-    parts, blocks = refs[:group], refs[group:]
+def load_kernel(group, start, stop, high_ref, low_ref, *refs):
+    parts, refs = refs[: stop - start], refs[stop - start :]
+    depth = high_ref.shape[1] // group
+    span = slice(start * depth, stop * depth)
     columns = jnp.concatenate([part[...] for part in parts], axis=0)
-    value = product((high_ref[...], low_ref[...]), split(columns))
+    value = product((high_ref[:, span], low_ref[:, span]), split(columns))
+    if start == 0:
+        refs[0][...] = value
+        return
+    sum_ref, *blocks = refs
     width = value.shape[0] // len(blocks)
     for i, block in enumerate(blocks):
-        block[...] = value[i * width : (i + 1) * width]
+        rows = slice(i * width, (i + 1) * width)
+        block[...] = sum_ref[rows] + value[rows]
 
 
 def load(high, low, parts, blocks):
     rank = high.shape[0]
+    group = len(parts)
     columns = parts[0].shape[1]
-    return pl.pallas_call(
-        functools.partial(load_kernel, len(parts)),
-        in_specs=[VMEM] * (2 + len(parts)),
-        out_specs=[VMEM] * blocks,
-        out_shape=[jax.ShapeDtypeStruct((rank // blocks, columns), jnp.float32)] * blocks,
-        compiler_params=params(),
-        cost_estimate=FREE,
-    )(high, low, *parts)
+
+    def call(start, stop, out_shape, *sums):
+        return pl.pallas_call(
+            functools.partial(load_kernel, group, start, stop),
+            in_specs=[VMEM] * (2 + stop - start + len(sums)),
+            out_specs=[VMEM] * len(out_shape),
+            out_shape=out_shape,
+            compiler_params=params(),
+            cost_estimate=FREE,
+        )(high, low, *parts[start:stop], *sums)
+
+    early = call(0, group - 1, [jax.ShapeDtypeStruct((rank, columns), jnp.float32)])
+    return call(group - 1, group, [jax.ShapeDtypeStruct((rank // blocks, columns), jnp.float32)] * blocks, *early)
 
 
 def join_kernel(group, sequence, own_ref, *refs):

time: 55.5 us -> 56.1 us (1.011)
  Pallas kernels: 6.43 us -> 7.02 us
    pallas_call x1 -> x2, Pallas kernels: 0.58 us -> 1.17 us  [call(): pl.pallas_call(functools.partial(load_kernel, group, start, stop), in_spe...]
  transfers between devices with their start and end apart: 19 -> 19, of which waited for: 9 -> 9; matrix products, arithmetic and copies ran while one was open for 0% -> 0% of each run, Pallas kernels for 4% -> 5%
where the time goes in v28:
time: 56.1 us; the launch traced here: 55.6 us
  waiting for transfers between devices  25.5 us (45%)
  starting transfers between devices  22.3 us (40%)
  Pallas kernels  7.02 us (13%)
  between operations  0.71 us (1%)
    ppermute x19, waiting for transfers between devices, swap(): lax.ppermute(value, axis, [(i, i ^ offset) for i in range(lax.axis_size(a...  25.5 us
    ppermute x19, starting transfers between devices, swap(): lax.ppermute(value, axis, [(i, i ^ offset) for i in range(lax.axis_size(a...  22.3 us
    pallas_call x1, Pallas kernels, project(): pl.pallas_call(functools.partial(project_kernel, depth), in_specs=[HBM, H...  2.93 us
    pallas_call x1, Pallas kernels, mix(): pl.pallas_call(functools.partial(mix_kernel, times, order), in_specs=[SME...  2.08 us
    pallas_call x2, Pallas kernels, call(): pl.pallas_call(functools.partial(load_kernel, group, start, stop), in_spe...  1.17 us
  transfers between devices with their start and end apart: 19, of which 9 were waited for; matrix products, arithmetic and copies ran while one was open for 0% of the time, Pallas kernels for 5%

profile of v28, /device:TPU:8, one launch (start us, length us, event | category | flops | bytes accessed | tf_op | source)
XLA Modules:
  0.0 55.6 jit_solution(1106454731240309740)
XLA Ops:
  0.6 2.9 %shard_map.41 = (f32[32,256]{1,0:T(8,128)S(1)}, f32[32,256]{1,0:T(8,128)S(1)}, f32[64,1024]{1,0:T(8,128)S(1)}, f32[64,1024]{1,0:T(8,128)S(1)}, f32[64,1024]{1,0:T(8,128)S(1)}, /*index=5*/f32[64,1024]{1,0:T(8,128)S(1)}) custom-call(f32[64,4096]{1,0:T(8,128)} %snapshots_ref.1, f32[4096,256]{1,0:T(8,128)} %factor_ref.1), custom_call_target="tpu_custom_call" | custom-call | tf_op jit(solution)/shard_map/pallas_call | solution.py:76
  3.6 1.6 %collective-permute-start.1 = (f32[32,256]{1,0:T(8,128)S(1)}, f32[32,256]{1,0:T(8,128)S(1)}, u32[]{:S(2)}, u32[]{:S(2)}) collective-permute-start(f32[32,256]{1,0:T(8,128)S(1)} %get-tuple-element.24), channel_id=1, source_target_pairs={{0,2},{1,3},{2,0},{3,1},{4,6},{5,7},{6,4},{7,5},{8,10},{9,11},{10,... | collective-permute-start | bytes 98312 | tf_op jit(solution)/shard_map/ppermute | solution.py:218
  5.1 0.0 collective-permute-start.2
  5.2 0.6 %collective-permute-start = (f32[32,256]{1,0:T(8,128)S(1)}, f32[32,256]{1,0:T(8,128)S(1)}, u32[]{:S(2)}, u32[]{:S(2)}) collective-permute-start(f32[32,256]{1,0:T(8,128)S(1)} %get-tuple-element.25), channel_id=1, source_target_pairs={{0,1},{1,0},{2,3},{3,2},{4,5},{5,4},{6,7},{7,6},{8,9},{9,8},{10,11... | collective-permute-start | bytes 98312 | tf_op jit(solution)/shard_map/ppermute | solution.py:218
  5.8 1.5 %collective-permute-start.6 = (f32[64,1024]{1,0:T(8,128)S(1)}, f32[64,1024]{1,0:T(8,128)S(1)}, u32[]{:S(2)}, u32[]{:S(2)}) collective-permute-start(f32[64,1024]{1,0:T(8,128)S(1)} %get-tuple-element.26), channel_id=1, source_target_pairs={{0,4},{4,0},{8,12},{12,8},{16,20},{20,16},{24,28},{28,24},{1,5},{5... | collective-permute-start | bytes 786440 | tf_op jit(solution)/shard_map/ppermute | solution.py:218
  7.3 0.5 collective-permute-start.7
  7.7 0.0 collective-permute-done.1
  7.7 0.9 %collective-permute-done.2 = f32[32,256]{1,0:T(8,128)S(1)} collective-permute-done((f32[32,256]{1,0:T(8,128)S(1)}, f32[32,256]{1,0:T(8,128)S(1)}, u32[]{:S(2)}, u32[]{:S(2)}) %collective-permute-start.2) | collective-permute-done | bytes 32800 | tf_op jit(solution)/shard_map/ppermute | solution.py:218
  8.6 0.0 collective-permute-done
  8.6 3.6 %collective-permute-start.5 = (f32[32,256]{1,0:T(8,128)S(1)}, f32[32,256]{1,0:T(8,128)S(1)}, u32[]{:S(2)}, u32[]{:S(2)}) collective-permute-start(f32[32,256]{1,0:T(8,128)S(1)} %add_add_fusion), channel_id=1, source_target_pairs={{0,20},{4,16},{8,28},{12,24},{16,4},{20,0},{24,12},{28,8},{1,21},{... | collective-permute-start | bytes 98312 | tf_op jit(solution)/shard_map/ppermute | solution.py:218
  12.2 0.3 collective-permute-start.4
  12.5 0.5 collective-permute-start.3
  13.0 4.2 %collective-permute-done.5 = f32[32,256]{1,0:T(8,128)S(1)} collective-permute-done((f32[32,256]{1,0:T(8,128)S(1)}, f32[32,256]{1,0:T(8,128)S(1)}, u32[]{:S(2)}, u32[]{:S(2)}) %collective-permute-start.5) | collective-permute-done | bytes 32800 | tf_op jit(solution)/shard_map/ppermute | solution.py:218
  17.2 0.4 collective-permute-done.4
  17.6 0.0 collective-permute-done.3
  17.6 0.0 collective-permute-done.6.refs_1_
  17.6 0.0 collective-permute-done.7.refs_2_
  17.7 0.2 collective-permute-start.9
  17.9 2.4 %collective-permute-start.11 = (f32[64,1024]{1,0:T(8,128)S(1)}, f32[64,1024]{1,0:T(8,128)S(1)}, u32[]{:S(2)}, u32[]{:S(2)}) collective-permute-start(f32[64,1024]{1,0:T(8,128)S(1)} %get-tuple-element.32), channel_id=1, source_target_pairs={{0,12},{4,8},{8,4},{12,0},{16,28},{20,24},{24,20},{28,16},{1,13},{... | collective-permute-start | bytes 786440 | tf_op jit(solution)/shard_map/ppermute | solution.py:218
  20.3 0.0 collective-permute-start.8
  20.3 3.9 %collective-permute-done.9.refs_2_ = f32[128,256]{1,0:T(8,128)S(1)} collective-permute-done((f32[128,256]{1,0:T(8,128)S(1)}, f32[128,256]{1,0:T(8,128)S(1)}, u32[]{:S(2)}, u32[]{:S(2)}) %collective-permute-start.9) | collective-permute-done | bytes 131104 | tf_op jit(solution)/shard_map/ppermute | solution.py:218
  24.2 0.0 collective-permute-start.10
  24.2 0.1 pad_add_fusion.index_ref
  24.2 0.0 collective-permute-done.8.refs_1_
  24.2 1.3 %collective-permute-done.10.refs_3_ = f32[128,256]{1,0:T(8,128)S(1)} collective-permute-done((f32[128,256]{1,0:T(8,128)S(1)}, f32[128,256]{1,0:T(8,128)S(1)}, u32[]{:S(2)}, u32[]{:S(2)}) %collective-permute-start.10) | collective-permute-done | bytes 131104 | tf_op jit(solution)/shard_map/ppermute | solution.py:218
  25.5 2.1 %shard_map.42 = (bf16[256,256]{1,0:T(8,128)(2,1)S(1)}, bf16[256,256]{1,0:T(8,128)(2,1)S(1)}, f32[64,256]{1,0:T(8,128)S(1)}) custom-call(s32[2]{0:T(128)S(1)} %pad_add_fusion.index_ref, f32[128,256]{1,0:T(8,128)S(1)} %pad_maximum_fusion.refs_0_, f32[128,256]{1,0:T(8,128)S(1)} %collective-permute-done.8.refs_1_, ...), custom_call_target="tpu_custom_call" | custom-call | tf_op jit(solution)/shard_map/pallas_call | solution.py:137
  27.6 0.6 %shard_map.43.refs_1_ = f32[256,1024]{1,0:T(8,128)S(1)} custom-call(bf16[256,256]{1,0:T(8,128)(2,1)S(1)} %get-tuple-element.30.high_ref, bf16[256,256]{1,0:T(8,128)(2,1)S(1)} %get-tuple-element.31.low_ref, f32[64,1024]{1,0:T(8,128)S(1)} %get-tuple-element.33.refs_0_, f32[64,1024]{1,0:T(8,128)S(1)} %collective-permute-done.6.refs_1_, ...), custom_call_target="tpu_custom_call" | custom-call | tf_op jit(solution)/shard_map/pallas_call | solution.py:169
  28.2 0.0 collective-permute-done.11.refs_0_
  28.2 0.6 %shard_map.44 = (f32[32,1024]{1,0:T(8,128)S(1)}, f32[32,1024]{1,0:T(8,128)S(1)}, f32[32,1024]{1,0:T(8,128)S(1)}, f32[32,1024]{1,0:T(8,128)S(1)}, f32[32,1024]{1,...) custom-call(bf16[256,256]{1,0:T(8,128)(2,1)S(1)} %get-tuple-element.30.high_ref, ...), custom_call_target="tpu_custom_call" | custom-call | tf_op jit(solution)/shard_map/pallas_call | solution.py:169
  28.8 1.1 %collective-permute-start.14 = (f32[32,1024]{1,0:T(8,128)S(1)}, f32[32,1024]{1,0:T(8,128)S(1)}, u32[]{:S(2)}, u32[]{:S(2)}) collective-permute-start(f32[32,1024]{1,0:T(8,128)S(1)} %get-tuple-element.39), channel_id=1, source_target_pairs={{0,4},{4,0},{8,12},{12,8},{16,20},{20,16},{24,28},{28,24},{1,5},{5... | collective-permute-start | bytes 393224 | tf_op jit(solution)/shard_map/ppermute | solution.py:218
  29.9 1.3 %collective-permute-start.12 = (f32[32,1024]{1,0:T(8,128)S(1)}, f32[32,1024]{1,0:T(8,128)S(1)}, u32[]{:S(2)}, u32[]{:S(2)}) collective-permute-start(f32[32,1024]{1,0:T(8,128)S(1)} %get-tuple-element.36), channel_id=1, source_target_pairs={{0,16},{4,20},{8,24},{12,28},{16,0},{20,4},{24,8},{28,12},{1,17},{... | collective-permute-start | bytes 393224 | tf_op jit(solution)/shard_map/ppermute | solution.py:218
  31.2 2.1 %collective-permute-start.13 = (f32[32,1024]{1,0:T(8,128)S(1)}, f32[32,1024]{1,0:T(8,128)S(1)}, u32[]{:S(2)}, u32[]{:S(2)}) collective-permute-start(f32[32,1024]{1,0:T(8,128)S(1)} %get-tuple-element.37), channel_id=1, source_target_pairs={{0,20},{4,16},{8,28},{12,24},{16,4},{20,0},{24,12},{28,8},{1,21},{... | collective-permute-start | bytes 393224 | tf_op jit(solution)/shard_map/ppermute | solution.py:218
  33.2 0.3 collective-permute-start.15
  33.6 1.7 %collective-permute-start.16 = (f32[32,1024]{1,0:T(8,128)S(1)}, f32[32,1024]{1,0:T(8,128)S(1)}, u32[]{:S(2)}, u32[]{:S(2)}) collective-permute-start(f32[32,1024]{1,0:T(8,128)S(1)} %get-tuple-element.42), channel_id=1, source_target_pairs={{0,24},{4,28},{8,16},{12,20},{16,8},{20,12},{24,0},{28,4},{1,25},{... | collective-permute-start | bytes 393224 | tf_op jit(solution)/shard_map/ppermute | solution.py:218
  35.3 0.0 collective-permute-done.14.refs_2_
  35.3 0.5 collective-permute-start.17
  35.8 4.6 %collective-permute-done.12.refs_0_ = f32[32,1024]{1,0:T(8,128)S(1)} collective-permute-done((f32[32,1024]{1,0:T(8,128)S(1)}, f32[32,1024]{1,0:T(8,128)S(1)}, u32[]{:S(2)}, u32[]{:S(2)}) %collective-permute-start.12) | collective-permute-done | bytes 131104 | tf_op jit(solution)/shard_map/ppermute | solution.py:218
  40.4 4.0 %collective-permute-start.18 = (f32[32,1024]{1,0:T(8,128)S(1)}, f32[32,1024]{1,0:T(8,128)S(1)}, u32[]{:S(2)}, u32[]{:S(2)}) collective-permute-start(f32[32,1024]{1,0:T(8,128)S(1)} %get-tuple-element.44), channel_id=1, source_target_pairs={{0,12},{4,8},{8,4},{12,0},{16,28},{20,24},{24,20},{28,16},{1,13},{... | collective-permute-start | bytes 393224 | tf_op jit(solution)/shard_map/ppermute | solution.py:218
  44.4 3.8 %collective-permute-done.13.refs_1_ = f32[32,1024]{1,0:T(8,128)S(1)} collective-permute-done((f32[32,1024]{1,0:T(8,128)S(1)}, f32[32,1024]{1,0:T(8,128)S(1)}, u32[]{:S(2)}, u32[]{:S(2)}) %collective-permute-start.13) | collective-permute-done | bytes 131104 | tf_op jit(solution)/shard_map/ppermute | solution.py:218
  48.2 0.0 collective-permute-done.15.refs_3_
  48.2 4.4 %collective-permute-done.16.refs_4_ = f32[32,1024]{1,0:T(8,128)S(1)} collective-permute-done((f32[32,1024]{1,0:T(8,128)S(1)}, f32[32,1024]{1,0:T(8,128)S(1)}, u32[]{:S(2)}, u32[]{:S(2)}) %collective-permute-start.16) | collective-permute-done | bytes 131104 | tf_op jit(solution)/shard_map/ppermute | solution.py:218
  52.6 2.2 %collective-permute-done.17.refs_5_ = f32[32,1024]{1,0:T(8,128)S(1)} collective-permute-done((f32[32,1024]{1,0:T(8,128)S(1)}, f32[32,1024]{1,0:T(8,128)S(1)}, u32[]{:S(2)}, u32[]{:S(2)}) %collective-permute-start.17) | collective-permute-done | bytes 131104 | tf_op jit(solution)/shard_map/ppermute | solution.py:218
  54.7 0.0 collective-permute-done.18.refs_6_
  54.7 0.8 %shard_map.45 = (f32[64,256]{1,0:T(8,128)}, f32[32,4096]{1,0:T(8,128)}) custom-call(f32[64,256]{1,0:T(8,128)S(1)} %get-tuple-element.29.own_ref, f32[32,1024]{1,0:T(8,128)S(1)} %collective-permute-done.12.refs_0_, f32[32,1024]{1,0:T(8,128)S(1)} %collective-permute-done.13.refs_1_, f32[32,1024]{1,0:T(8,128)S(1)} %collective-permute-done.14.refs_2_, ...), custom_call_target="tpu_custom_call" | custom-call | tf_op jit(solution)/shard_map/pallas_call | solution.py:203
  (2 shorter events, 0.0 us)
Async XLA Ops:
  3.6 4.2 %collective-permute-start.1 = (f32[32,256]{1,0:T(8,128)S(1)}, f32[32,256]{1,0:T(8,128)S(1)}, u32[]{:S(2)}, u32[]{:S(2)}) collective-permute-start(f32[32,256]{1,0:T(8,128)S(1)} %get-tuple-element.24), channel_id=1, source_target_pairs={{0,2},{1,3},{2,0},{3,1},{4,6},{5,7},{6,4},{7,5},{8,10},{9,11},{10,... | collective-permute-start | bytes 98312 | tf_op jit(solution)/shard_map/ppermute | solution.py:218
  5.1 3.4 %collective-permute-start.2 = (f32[32,256]{1,0:T(8,128)S(1)}, f32[32,256]{1,0:T(8,128)S(1)}, u32[]{:S(2)}, u32[]{:S(2)}) collective-permute-start(f32[32,256]{1,0:T(8,128)S(1)} %get-tuple-element.25), channel_id=1, source_target_pairs={{0,3},{1,2},{2,1},{3,0},{4,7},{5,6},{6,5},{7,4},{8,11},{9,10},{10,... | collective-permute-start | bytes 98312 | tf_op jit(solution)/shard_map/ppermute | solution.py:218
  5.2 3.4 %collective-permute-start = (f32[32,256]{1,0:T(8,128)S(1)}, f32[32,256]{1,0:T(8,128)S(1)}, u32[]{:S(2)}, u32[]{:S(2)}) collective-permute-start(f32[32,256]{1,0:T(8,128)S(1)} %get-tuple-element.25), channel_id=1, source_target_pairs={{0,1},{1,0},{2,3},{3,2},{4,5},{5,4},{6,7},{7,6},{8,9},{9,8},{10,11... | collective-permute-start | bytes 98312 | tf_op jit(solution)/shard_map/ppermute | solution.py:218
  5.8 11.9 %collective-permute-start.6 = (f32[64,1024]{1,0:T(8,128)S(1)}, f32[64,1024]{1,0:T(8,128)S(1)}, u32[]{:S(2)}, u32[]{:S(2)}) collective-permute-start(f32[64,1024]{1,0:T(8,128)S(1)} %get-tuple-element.26), channel_id=1, source_target_pairs={{0,4},{4,0},{8,12},{12,8},{16,20},{20,16},{24,28},{28,24},{1,5},{5... | collective-permute-start | bytes 786440 | tf_op jit(solution)/shard_map/ppermute | solution.py:218
  7.3 10.4 %collective-permute-start.7 = (f32[64,1024]{1,0:T(8,128)S(1)}, f32[64,1024]{1,0:T(8,128)S(1)}, u32[]{:S(2)}, u32[]{:S(2)}) collective-permute-start(f32[64,1024]{1,0:T(8,128)S(1)} %get-tuple-element.27), channel_id=1, source_target_pairs={{0,8},{4,12},{8,0},{12,4},{16,24},{20,28},{24,16},{28,20},{1,9},{5... | collective-permute-start | bytes 786440 | tf_op jit(solution)/shard_map/ppermute | solution.py:218
  8.6 8.6 %collective-permute-start.5 = (f32[32,256]{1,0:T(8,128)S(1)}, f32[32,256]{1,0:T(8,128)S(1)}, u32[]{:S(2)}, u32[]{:S(2)}) collective-permute-start(f32[32,256]{1,0:T(8,128)S(1)} %add_add_fusion), channel_id=1, source_target_pairs={{0,20},{4,16},{8,28},{12,24},{16,4},{20,0},{24,12},{28,8},{1,21},{... | collective-permute-start | bytes 98312 | tf_op jit(solution)/shard_map/ppermute | solution.py:218
  12.2 5.4 %collective-permute-start.4 = (f32[32,256]{1,0:T(8,128)S(1)}, f32[32,256]{1,0:T(8,128)S(1)}, u32[]{:S(2)}, u32[]{:S(2)}) collective-permute-start(f32[32,256]{1,0:T(8,128)S(1)} %add_add_fusion), channel_id=1, source_target_pairs={{0,16},{4,20},{8,24},{12,28},{16,0},{20,4},{24,8},{28,12},{1,17},{... | collective-permute-start | bytes 98312 | tf_op jit(solution)/shard_map/ppermute | solution.py:218
  12.5 5.1 %collective-permute-start.3 = (f32[32,256]{1,0:T(8,128)S(1)}, f32[32,256]{1,0:T(8,128)S(1)}, u32[]{:S(2)}, u32[]{:S(2)}) collective-permute-start(f32[32,256]{1,0:T(8,128)S(1)} %add_add_fusion), channel_id=1, source_target_pairs={{0,4},{4,0},{8,12},{12,8},{16,20},{20,16},{24,28},{28,24},{1,5},{5... | collective-permute-start | bytes 98312 | tf_op jit(solution)/shard_map/ppermute | solution.py:218
  17.7 6.5 %collective-permute-start.9 = (f32[128,256]{1,0:T(8,128)S(1)}, f32[128,256]{1,0:T(8,128)S(1)}, u32[]{:S(2)}, u32[]{:S(2)}) collective-permute-start(f32[128,256]{1,0:T(8,128)S(1)} %pad_maximum_fusion.refs_0_), channel_id=1, source_target_pairs={{0,8},{4,12},{8,0},{12,4},{16,24},{20,28},{24,16},{28,20},{1,9},{5... | collective-permute-start | bytes 393224 | tf_op jit(solution)/shard_map/ppermute | solution.py:218
  17.9 10.3 %collective-permute-start.11 = (f32[64,1024]{1,0:T(8,128)S(1)}, f32[64,1024]{1,0:T(8,128)S(1)}, u32[]{:S(2)}, u32[]{:S(2)}) collective-permute-start(f32[64,1024]{1,0:T(8,128)S(1)} %get-tuple-element.32), channel_id=1, source_target_pairs={{0,12},{4,8},{8,4},{12,0},{16,28},{20,24},{24,20},{28,16},{1,13},{... | collective-permute-start | bytes 786440 | tf_op jit(solution)/shard_map/ppermute | solution.py:218
  20.3 3.9 %collective-permute-start.8 = (f32[128,256]{1,0:T(8,128)S(1)}, f32[128,256]{1,0:T(8,128)S(1)}, u32[]{:S(2)}, u32[]{:S(2)}) collective-permute-start(f32[128,256]{1,0:T(8,128)S(1)} %pad_maximum_fusion.refs_0_), channel_id=1, source_target_pairs={{0,1},{1,0},{2,3},{3,2},{4,5},{5,4},{6,7},{7,6},{8,9},{9,8},{10,11... | collective-permute-start | bytes 393224 | tf_op jit(solution)/shard_map/ppermute | solution.py:218
  24.2 1.3 %collective-permute-start.10 = (f32[128,256]{1,0:T(8,128)S(1)}, f32[128,256]{1,0:T(8,128)S(1)}, u32[]{:S(2)}, u32[]{:S(2)}) collective-permute-start(f32[128,256]{1,0:T(8,128)S(1)} %collective-permute-done.9.refs_2_), channel_id=1, source_target_pairs={{0,1},{1,0},{2,3},{3,2},{4,5},{5,4},{6,7},{7,6},{8,9},{9,8},{10,11... | collective-permute-start | bytes 393224 | tf_op jit(solution)/shard_map/ppermute | solution.py:218
  28.8 6.5 %collective-permute-start.14 = (f32[32,1024]{1,0:T(8,128)S(1)}, f32[32,1024]{1,0:T(8,128)S(1)}, u32[]{:S(2)}, u32[]{:S(2)}) collective-permute-start(f32[32,1024]{1,0:T(8,128)S(1)} %get-tuple-element.39), channel_id=1, source_target_pairs={{0,4},{4,0},{8,12},{12,8},{16,20},{20,16},{24,28},{28,24},{1,5},{5... | collective-permute-start | bytes 393224 | tf_op jit(solution)/shard_map/ppermute | solution.py:218
  29.9 10.5 %collective-permute-start.12 = (f32[32,1024]{1,0:T(8,128)S(1)}, f32[32,1024]{1,0:T(8,128)S(1)}, u32[]{:S(2)}, u32[]{:S(2)}) collective-permute-start(f32[32,1024]{1,0:T(8,128)S(1)} %get-tuple-element.36), channel_id=1, source_target_pairs={{0,16},{4,20},{8,24},{12,28},{16,0},{20,4},{24,8},{28,12},{1,17},{... | collective-permute-start | bytes 393224 | tf_op jit(solution)/shard_map/ppermute | solution.py:218
  31.2 17.0 %collective-permute-start.13 = (f32[32,1024]{1,0:T(8,128)S(1)}, f32[32,1024]{1,0:T(8,128)S(1)}, u32[]{:S(2)}, u32[]{:S(2)}) collective-permute-start(f32[32,1024]{1,0:T(8,128)S(1)} %get-tuple-element.37), channel_id=1, source_target_pairs={{0,20},{4,16},{8,28},{12,24},{16,4},{20,0},{24,12},{28,8},{1,21},{... | collective-permute-start | bytes 393224 | tf_op jit(solution)/shard_map/ppermute | solution.py:218
  33.2 15.0 %collective-permute-start.15 = (f32[32,1024]{1,0:T(8,128)S(1)}, f32[32,1024]{1,0:T(8,128)S(1)}, u32[]{:S(2)}, u32[]{:S(2)}) collective-permute-start(f32[32,1024]{1,0:T(8,128)S(1)} %get-tuple-element.41), channel_id=1, source_target_pairs={{0,8},{4,12},{8,0},{12,4},{16,24},{20,28},{24,16},{28,20},{1,9},{5... | collective-permute-start | bytes 393224 | tf_op jit(solution)/shard_map/ppermute | solution.py:218
  33.6 19.0 %collective-permute-start.16 = (f32[32,1024]{1,0:T(8,128)S(1)}, f32[32,1024]{1,0:T(8,128)S(1)}, u32[]{:S(2)}, u32[]{:S(2)}) collective-permute-start(f32[32,1024]{1,0:T(8,128)S(1)} %get-tuple-element.42), channel_id=1, source_target_pairs={{0,24},{4,28},{8,16},{12,20},{16,8},{20,12},{24,0},{28,4},{1,25},{... | collective-permute-start | bytes 393224 | tf_op jit(solution)/shard_map/ppermute | solution.py:218
  35.3 19.5 %collective-permute-start.17 = (f32[32,1024]{1,0:T(8,128)S(1)}, f32[32,1024]{1,0:T(8,128)S(1)}, u32[]{:S(2)}, u32[]{:S(2)}) collective-permute-start(f32[32,1024]{1,0:T(8,128)S(1)} %get-tuple-element.43), channel_id=1, source_target_pairs={{0,28},{4,24},{8,20},{12,16},{16,12},{20,8},{24,4},{28,0},{1,29},{... | collective-permute-start | bytes 393224 | tf_op jit(solution)/shard_map/ppermute | solution.py:218
  40.4 14.3 %collective-permute-start.18 = (f32[32,1024]{1,0:T(8,128)S(1)}, f32[32,1024]{1,0:T(8,128)S(1)}, u32[]{:S(2)}, u32[]{:S(2)}) collective-permute-start(f32[32,1024]{1,0:T(8,128)S(1)} %get-tuple-element.44), channel_id=1, source_target_pairs={{0,12},{4,8},{8,4},{12,0},{16,28},{20,24},{24,20},{28,16},{1,13},{... | collective-permute-start | bytes 393224 | tf_op jit(solution)/shard_map/ppermute | solution.py:218

commit v29 on v23

--- a/solution.py
+++ b/solution.py
@@ -234,7 +234,7 @@
     blocks = list(load(high_t, low_t, parts, times))
     terms = [blocks[0]] + [None] * (times - 1)
     near, far = list(range(1, group)), list(range(group, times))
-    sequence = [*far, *near, 0]
+    sequence = [*far[:3], *near[:2], *far[3:], *near[2:], 0]
     for k in sequence[:-1]:
         if k == near[-1]:
             blocks[k], terms[1] = lax.optimization_barrier((blocks[k], terms[1]))

time: 56.3 us -> 55.6 us (0.988); the launches traced: 55.2 us -> 55.1 us
  starting transfers between devices: 24.5 us -> 23.5 us
  waiting for transfers between devices: 23.5 us -> 24.3 us
    ppermute x19, starting transfers between devices: 24.5 us -> 23.5 us  [swap(): lax.ppermute(value, axis, [(i, i ^ offset) for i in range(lax.axis_size(a...]
    ppermute x19, waiting for transfers between devices: 23.5 us -> 24.3 us  [swap(): lax.ppermute(value, axis, [(i, i ^ offset) for i in range(lax.axis_size(a...]
  transfers between devices with their start and end apart: 19 -> 19, of which waited for: 8 -> 9; matrix products, arithmetic and copies ran while one was open for 0% -> 0% of each run, Pallas kernels for 4% -> 4%
where the time goes in v29:
time: 55.6 us; the launch traced here: 55.1 us
  waiting for transfers between devices  24.3 us (44%)
  starting transfers between devices  23.5 us (42%)
  Pallas kernels  6.51 us (12%)
  between operations  0.7 us (1%)
    ppermute x19, waiting for transfers between devices, swap(): lax.ppermute(value, axis, [(i, i ^ offset) for i in range(lax.axis_size(a...  24.3 us
    ppermute x19, starting transfers between devices, swap(): lax.ppermute(value, axis, [(i, i ^ offset) for i in range(lax.axis_size(a...  23.5 us
    pallas_call x1, Pallas kernels, project(): pl.pallas_call(functools.partial(project_kernel, depth), in_specs=[HBM, H...  2.93 us
    pallas_call x1, Pallas kernels, mix(): pl.pallas_call(functools.partial(mix_kernel, times, order), in_specs=[SME...  2.15 us
  transfers between devices with their start and end apart: 19, of which 9 were waited for; matrix products, arithmetic and copies ran while one was open for 0% of the time, Pallas kernels for 4%

profile of v29, /device:TPU:8, one launch (start us, length us, event | category | flops | bytes accessed | tf_op | source)
XLA Modules:
  0.0 55.1 jit_solution(13208158934625567940)
XLA Ops:
  0.6 2.9 %shard_map.41 = (f32[32,256]{1,0:T(8,128)S(1)}, f32[32,256]{1,0:T(8,128)S(1)}, f32[64,1024]{1,0:T(8,128)S(1)}, f32[64,1024]{1,0:T(8,128)S(1)}, f32[64,1024]{1,0:T(8,128)S(1)}, /*index=5*/f32[64,1024]{1,0:T(8,128)S(1)}) custom-call(f32[64,4096]{1,0:T(8,128)} %snapshots_ref.1, f32[4096,256]{1,0:T(8,128)} %factor_ref.1), custom_call_target="tpu_custom_call" | custom-call | tf_op jit(solution)/shard_map/pallas_call | solution.py:76
  3.6 1.6 %collective-permute-start.1 = (f32[32,256]{1,0:T(8,128)S(1)}, f32[32,256]{1,0:T(8,128)S(1)}, u32[]{:S(2)}, u32[]{:S(2)}) collective-permute-start(f32[32,256]{1,0:T(8,128)S(1)} %get-tuple-element.24), channel_id=1, source_target_pairs={{0,2},{1,3},{2,0},{3,1},{4,6},{5,7},{6,4},{7,5},{8,10},{9,11},{10,... | collective-permute-start | bytes 98312 | tf_op jit(solution)/shard_map/ppermute | solution.py:205
  5.1 0.0 collective-permute-start.2
  5.2 0.6 %collective-permute-start = (f32[32,256]{1,0:T(8,128)S(1)}, f32[32,256]{1,0:T(8,128)S(1)}, u32[]{:S(2)}, u32[]{:S(2)}) collective-permute-start(f32[32,256]{1,0:T(8,128)S(1)} %get-tuple-element.25), channel_id=1, source_target_pairs={{0,1},{1,0},{2,3},{3,2},{4,5},{5,4},{6,7},{7,6},{8,9},{9,8},{10,11... | collective-permute-start | bytes 98312 | tf_op jit(solution)/shard_map/ppermute | solution.py:205
  5.8 1.5 %collective-permute-start.6 = (f32[64,1024]{1,0:T(8,128)S(1)}, f32[64,1024]{1,0:T(8,128)S(1)}, u32[]{:S(2)}, u32[]{:S(2)}) collective-permute-start(f32[64,1024]{1,0:T(8,128)S(1)} %get-tuple-element.26), channel_id=1, source_target_pairs={{0,4},{4,0},{8,12},{12,8},{16,20},{20,16},{24,28},{28,24},{1,5},{5... | collective-permute-start | bytes 786440 | tf_op jit(solution)/shard_map/ppermute | solution.py:205
  7.3 0.5 collective-permute-start.7
  7.7 0.0 collective-permute-done.1
  7.7 0.9 %collective-permute-done.2 = f32[32,256]{1,0:T(8,128)S(1)} collective-permute-done((f32[32,256]{1,0:T(8,128)S(1)}, f32[32,256]{1,0:T(8,128)S(1)}, u32[]{:S(2)}, u32[]{:S(2)}) %collective-permute-start.2) | collective-permute-done | bytes 32800 | tf_op jit(solution)/shard_map/ppermute | solution.py:205
  8.6 0.0 collective-permute-done
  8.6 3.6 %collective-permute-start.5 = (f32[32,256]{1,0:T(8,128)S(1)}, f32[32,256]{1,0:T(8,128)S(1)}, u32[]{:S(2)}, u32[]{:S(2)}) collective-permute-start(f32[32,256]{1,0:T(8,128)S(1)} %add_add_fusion), channel_id=1, source_target_pairs={{0,20},{4,16},{8,28},{12,24},{16,4},{20,0},{24,12},{28,8},{1,21},{... | collective-permute-start | bytes 98312 | tf_op jit(solution)/shard_map/ppermute | solution.py:205
  12.2 0.3 collective-permute-start.4
  12.5 0.5 collective-permute-start.3
  13.0 4.2 %collective-permute-done.5 = f32[32,256]{1,0:T(8,128)S(1)} collective-permute-done((f32[32,256]{1,0:T(8,128)S(1)}, f32[32,256]{1,0:T(8,128)S(1)}, u32[]{:S(2)}, u32[]{:S(2)}) %collective-permute-start.5) | collective-permute-done | bytes 32800 | tf_op jit(solution)/shard_map/ppermute | solution.py:205
  17.2 0.4 collective-permute-done.4
  17.6 0.0 collective-permute-done.3
  17.6 0.0 collective-permute-done.6.refs_1_
  17.6 0.0 collective-permute-done.7.refs_2_
  17.7 0.2 collective-permute-start.9
  17.9 2.4 %collective-permute-start.11 = (f32[64,1024]{1,0:T(8,128)S(1)}, f32[64,1024]{1,0:T(8,128)S(1)}, u32[]{:S(2)}, u32[]{:S(2)}) collective-permute-start(f32[64,1024]{1,0:T(8,128)S(1)} %get-tuple-element.35), channel_id=1, source_target_pairs={{0,12},{4,8},{8,4},{12,0},{16,28},{20,24},{24,20},{28,16},{1,13},{... | collective-permute-start | bytes 786440 | tf_op jit(solution)/shard_map/ppermute | solution.py:205
  20.3 0.0 collective-permute-start.8
  20.3 3.9 %collective-permute-done.9.refs_2_ = f32[128,256]{1,0:T(8,128)S(1)} collective-permute-done((f32[128,256]{1,0:T(8,128)S(1)}, f32[128,256]{1,0:T(8,128)S(1)}, u32[]{:S(2)}, u32[]{:S(2)}) %collective-permute-start.9) | collective-permute-done | bytes 131104 | tf_op jit(solution)/shard_map/ppermute | solution.py:205
  24.2 0.0 collective-permute-start.10
  24.2 0.1 pad_add_fusion.index_ref
  24.2 0.0 collective-permute-done.8.refs_1_
  24.2 1.3 %collective-permute-done.10.refs_3_ = f32[128,256]{1,0:T(8,128)S(1)} collective-permute-done((f32[128,256]{1,0:T(8,128)S(1)}, f32[128,256]{1,0:T(8,128)S(1)}, u32[]{:S(2)}, u32[]{:S(2)}) %collective-permute-start.10) | collective-permute-done | bytes 131104 | tf_op jit(solution)/shard_map/ppermute | solution.py:205
  25.5 2.1 %shard_map.42 = (bf16[256,256]{1,0:T(8,128)(2,1)S(1)}, bf16[256,256]{1,0:T(8,128)(2,1)S(1)}, f32[64,256]{1,0:T(8,128)S(1)}) custom-call(s32[2]{0:T(128)S(1)} %pad_add_fusion.index_ref, f32[128,256]{1,0:T(8,128)S(1)} %pad_maximum_fusion.refs_0_, f32[128,256]{1,0:T(8,128)S(1)} %collective-permute-done.8.refs_1_, ...), custom_call_target="tpu_custom_call" | custom-call | tf_op jit(solution)/shard_map/pallas_call | solution.py:137
  27.7 0.0 collective-permute-done.11.refs_3_
  27.7 0.6 %shard_map.43 = (f32[32,1024]{1,0:T(8,128)S(1)}, f32[32,1024]{1,0:T(8,128)S(1)}, f32[32,1024]{1,0:T(8,128)S(1)}, f32[32,1024]{1,0:T(8,128)S(1)}, f32[32,1024]{1,...) custom-call(bf16[256,256]{1,0:T(8,128)(2,1)S(1)} %get-tuple-element.30.high_ref, ...), custom_call_target="tpu_custom_call" | custom-call | tf_op jit(solution)/shard_map/pallas_call | solution.py:159
  28.3 1.1 %collective-permute-start.15 = (f32[32,1024]{1,0:T(8,128)S(1)}, f32[32,1024]{1,0:T(8,128)S(1)}, u32[]{:S(2)}, u32[]{:S(2)}) collective-permute-start(f32[32,1024]{1,0:T(8,128)S(1)} %get-tuple-element.40), channel_id=1, source_target_pairs={{0,4},{4,0},{8,12},{12,8},{16,20},{20,16},{24,28},{28,24},{1,5},{5... | collective-permute-start | bytes 393224 | tf_op jit(solution)/shard_map/ppermute | solution.py:205
  29.4 1.8 %collective-permute-start.12 = (f32[32,1024]{1,0:T(8,128)S(1)}, f32[32,1024]{1,0:T(8,128)S(1)}, u32[]{:S(2)}, u32[]{:S(2)}) collective-permute-start(f32[32,1024]{1,0:T(8,128)S(1)} %get-tuple-element.36), channel_id=1, source_target_pairs={{0,16},{4,20},{8,24},{12,28},{16,0},{20,4},{24,8},{28,12},{1,17},{... | collective-permute-start | bytes 393224 | tf_op jit(solution)/shard_map/ppermute | solution.py:205
  31.2 1.5 %collective-permute-start.13 = (f32[32,1024]{1,0:T(8,128)S(1)}, f32[32,1024]{1,0:T(8,128)S(1)}, u32[]{:S(2)}, u32[]{:S(2)}) collective-permute-start(f32[32,1024]{1,0:T(8,128)S(1)} %get-tuple-element.37), channel_id=1, source_target_pairs={{0,20},{4,16},{8,28},{12,24},{16,4},{20,0},{24,12},{28,8},{1,21},{... | collective-permute-start | bytes 393224 | tf_op jit(solution)/shard_map/ppermute | solution.py:205
  32.7 1.2 %collective-permute-start.14 = (f32[32,1024]{1,0:T(8,128)S(1)}, f32[32,1024]{1,0:T(8,128)S(1)}, u32[]{:S(2)}, u32[]{:S(2)}) collective-permute-start(f32[32,1024]{1,0:T(8,128)S(1)} %get-tuple-element.38), channel_id=1, source_target_pairs={{0,24},{4,28},{8,16},{12,20},{16,8},{20,12},{24,0},{28,4},{1,25},{... | collective-permute-start | bytes 393224 | tf_op jit(solution)/shard_map/ppermute | solution.py:205
  33.9 1.8 %collective-permute-start.16 = (f32[32,1024]{1,0:T(8,128)S(1)}, f32[32,1024]{1,0:T(8,128)S(1)}, u32[]{:S(2)}, u32[]{:S(2)}) collective-permute-start(f32[32,1024]{1,0:T(8,128)S(1)} %get-tuple-element.42), channel_id=1, source_target_pairs={{0,8},{4,12},{8,0},{12,4},{16,24},{20,28},{24,16},{28,20},{1,9},{5... | collective-permute-start | bytes 393224 | tf_op jit(solution)/shard_map/ppermute | solution.py:205
  35.6 0.0 collective-permute-done.15.refs_3_
  35.6 1.0 %collective-permute-start.17 = (f32[32,1024]{1,0:T(8,128)S(1)}, f32[32,1024]{1,0:T(8,128)S(1)}, u32[]{:S(2)}, u32[]{:S(2)}) collective-permute-start(f32[32,1024]{1,0:T(8,128)S(1)} %get-tuple-element.43), channel_id=1, source_target_pairs={{0,28},{4,24},{8,20},{12,16},{16,12},{20,8},{24,4},{28,0},{1,29},{... | collective-permute-start | bytes 393224 | tf_op jit(solution)/shard_map/ppermute | solution.py:205
  36.7 6.5 %collective-permute-done.12.refs_0_ = f32[32,1024]{1,0:T(8,128)S(1)} collective-permute-done((f32[32,1024]{1,0:T(8,128)S(1)}, f32[32,1024]{1,0:T(8,128)S(1)}, u32[]{:S(2)}, u32[]{:S(2)}) %collective-permute-start.12) | collective-permute-done | bytes 131104 | tf_op jit(solution)/shard_map/ppermute | solution.py:205
  43.2 3.8 %collective-permute-start.18 = (f32[32,1024]{1,0:T(8,128)S(1)}, f32[32,1024]{1,0:T(8,128)S(1)}, u32[]{:S(2)}, u32[]{:S(2)}) collective-permute-start(f32[32,1024]{1,0:T(8,128)S(1)} %get-tuple-element.44), channel_id=1, source_target_pairs={{0,12},{4,8},{8,4},{12,0},{16,28},{20,24},{24,20},{28,16},{1,13},{... | collective-permute-start | bytes 393224 | tf_op jit(solution)/shard_map/ppermute | solution.py:205
  47.0 0.6 %collective-permute-done.13.refs_1_ = f32[32,1024]{1,0:T(8,128)S(1)} collective-permute-done((f32[32,1024]{1,0:T(8,128)S(1)}, f32[32,1024]{1,0:T(8,128)S(1)}, u32[]{:S(2)}, u32[]{:S(2)}) %collective-permute-start.13) | collective-permute-done | bytes 131104 | tf_op jit(solution)/shard_map/ppermute | solution.py:205
  47.7 4.8 %collective-permute-done.14.refs_2_ = f32[32,1024]{1,0:T(8,128)S(1)} collective-permute-done((f32[32,1024]{1,0:T(8,128)S(1)}, f32[32,1024]{1,0:T(8,128)S(1)}, u32[]{:S(2)}, u32[]{:S(2)}) %collective-permute-start.14) | collective-permute-done | bytes 131104 | tf_op jit(solution)/shard_map/ppermute | solution.py:205
  52.4 0.0 collective-permute-done.16.refs_4_
  52.5 1.8 %collective-permute-done.17.refs_5_ = f32[32,1024]{1,0:T(8,128)S(1)} collective-permute-done((f32[32,1024]{1,0:T(8,128)S(1)}, f32[32,1024]{1,0:T(8,128)S(1)}, u32[]{:S(2)}, u32[]{:S(2)}) %collective-permute-start.17) | collective-permute-done | bytes 131104 | tf_op jit(solution)/shard_map/ppermute | solution.py:205
  54.3 0.0 collective-permute-done.18.refs_6_
  54.3 0.8 %shard_map.44 = (f32[64,256]{1,0:T(8,128)}, f32[32,4096]{1,0:T(8,128)}) custom-call(f32[64,256]{1,0:T(8,128)S(1)} %get-tuple-element.29.own_ref, f32[32,1024]{1,0:T(8,128)S(1)} %collective-permute-done.12.refs_0_, f32[32,1024]{1,0:T(8,128)S(1)} %collective-permute-done.13.refs_1_, f32[32,1024]{1,0:T(8,128)S(1)} %collective-permute-done.14.refs_2_, ...), custom_call_target="tpu_custom_call" | custom-call | tf_op jit(solution)/shard_map/pallas_call | solution.py:190
  (2 shorter events, 0.0 us)
Async XLA Ops:
  3.6 4.2 %collective-permute-start.1 = (f32[32,256]{1,0:T(8,128)S(1)}, f32[32,256]{1,0:T(8,128)S(1)}, u32[]{:S(2)}, u32[]{:S(2)}) collective-permute-start(f32[32,256]{1,0:T(8,128)S(1)} %get-tuple-element.24), channel_id=1, source_target_pairs={{0,2},{1,3},{2,0},{3,1},{4,6},{5,7},{6,4},{7,5},{8,10},{9,11},{10,... | collective-permute-start | bytes 98312 | tf_op jit(solution)/shard_map/ppermute | solution.py:205
  5.1 3.4 %collective-permute-start.2 = (f32[32,256]{1,0:T(8,128)S(1)}, f32[32,256]{1,0:T(8,128)S(1)}, u32[]{:S(2)}, u32[]{:S(2)}) collective-permute-start(f32[32,256]{1,0:T(8,128)S(1)} %get-tuple-element.25), channel_id=1, source_target_pairs={{0,3},{1,2},{2,1},{3,0},{4,7},{5,6},{6,5},{7,4},{8,11},{9,10},{10,... | collective-permute-start | bytes 98312 | tf_op jit(solution)/shard_map/ppermute | solution.py:205
  5.2 3.4 %collective-permute-start = (f32[32,256]{1,0:T(8,128)S(1)}, f32[32,256]{1,0:T(8,128)S(1)}, u32[]{:S(2)}, u32[]{:S(2)}) collective-permute-start(f32[32,256]{1,0:T(8,128)S(1)} %get-tuple-element.25), channel_id=1, source_target_pairs={{0,1},{1,0},{2,3},{3,2},{4,5},{5,4},{6,7},{7,6},{8,9},{9,8},{10,11... | collective-permute-start | bytes 98312 | tf_op jit(solution)/shard_map/ppermute | solution.py:205
  5.8 11.9 %collective-permute-start.6 = (f32[64,1024]{1,0:T(8,128)S(1)}, f32[64,1024]{1,0:T(8,128)S(1)}, u32[]{:S(2)}, u32[]{:S(2)}) collective-permute-start(f32[64,1024]{1,0:T(8,128)S(1)} %get-tuple-element.26), channel_id=1, source_target_pairs={{0,4},{4,0},{8,12},{12,8},{16,20},{20,16},{24,28},{28,24},{1,5},{5... | collective-permute-start | bytes 786440 | tf_op jit(solution)/shard_map/ppermute | solution.py:205
  7.3 10.4 %collective-permute-start.7 = (f32[64,1024]{1,0:T(8,128)S(1)}, f32[64,1024]{1,0:T(8,128)S(1)}, u32[]{:S(2)}, u32[]{:S(2)}) collective-permute-start(f32[64,1024]{1,0:T(8,128)S(1)} %get-tuple-element.27), channel_id=1, source_target_pairs={{0,8},{4,12},{8,0},{12,4},{16,24},{20,28},{24,16},{28,20},{1,9},{5... | collective-permute-start | bytes 786440 | tf_op jit(solution)/shard_map/ppermute | solution.py:205
  8.6 8.6 %collective-permute-start.5 = (f32[32,256]{1,0:T(8,128)S(1)}, f32[32,256]{1,0:T(8,128)S(1)}, u32[]{:S(2)}, u32[]{:S(2)}) collective-permute-start(f32[32,256]{1,0:T(8,128)S(1)} %add_add_fusion), channel_id=1, source_target_pairs={{0,20},{4,16},{8,28},{12,24},{16,4},{20,0},{24,12},{28,8},{1,21},{... | collective-permute-start | bytes 98312 | tf_op jit(solution)/shard_map/ppermute | solution.py:205
  12.2 5.4 %collective-permute-start.4 = (f32[32,256]{1,0:T(8,128)S(1)}, f32[32,256]{1,0:T(8,128)S(1)}, u32[]{:S(2)}, u32[]{:S(2)}) collective-permute-start(f32[32,256]{1,0:T(8,128)S(1)} %add_add_fusion), channel_id=1, source_target_pairs={{0,16},{4,20},{8,24},{12,28},{16,0},{20,4},{24,8},{28,12},{1,17},{... | collective-permute-start | bytes 98312 | tf_op jit(solution)/shard_map/ppermute | solution.py:205
  12.5 5.1 %collective-permute-start.3 = (f32[32,256]{1,0:T(8,128)S(1)}, f32[32,256]{1,0:T(8,128)S(1)}, u32[]{:S(2)}, u32[]{:S(2)}) collective-permute-start(f32[32,256]{1,0:T(8,128)S(1)} %add_add_fusion), channel_id=1, source_target_pairs={{0,4},{4,0},{8,12},{12,8},{16,20},{20,16},{24,28},{28,24},{1,5},{5... | collective-permute-start | bytes 98312 | tf_op jit(solution)/shard_map/ppermute | solution.py:205
  17.7 6.5 %collective-permute-start.9 = (f32[128,256]{1,0:T(8,128)S(1)}, f32[128,256]{1,0:T(8,128)S(1)}, u32[]{:S(2)}, u32[]{:S(2)}) collective-permute-start(f32[128,256]{1,0:T(8,128)S(1)} %pad_maximum_fusion.refs_0_), channel_id=1, source_target_pairs={{0,8},{4,12},{8,0},{12,4},{16,24},{20,28},{24,16},{28,20},{1,9},{5... | collective-permute-start | bytes 393224 | tf_op jit(solution)/shard_map/ppermute | solution.py:205
  17.9 9.8 %collective-permute-start.11 = (f32[64,1024]{1,0:T(8,128)S(1)}, f32[64,1024]{1,0:T(8,128)S(1)}, u32[]{:S(2)}, u32[]{:S(2)}) collective-permute-start(f32[64,1024]{1,0:T(8,128)S(1)} %get-tuple-element.35), channel_id=1, source_target_pairs={{0,12},{4,8},{8,4},{12,0},{16,28},{20,24},{24,20},{28,16},{1,13},{... | collective-permute-start | bytes 786440 | tf_op jit(solution)/shard_map/ppermute | solution.py:205
  20.3 3.9 %collective-permute-start.8 = (f32[128,256]{1,0:T(8,128)S(1)}, f32[128,256]{1,0:T(8,128)S(1)}, u32[]{:S(2)}, u32[]{:S(2)}) collective-permute-start(f32[128,256]{1,0:T(8,128)S(1)} %pad_maximum_fusion.refs_0_), channel_id=1, source_target_pairs={{0,1},{1,0},{2,3},{3,2},{4,5},{5,4},{6,7},{7,6},{8,9},{9,8},{10,11... | collective-permute-start | bytes 393224 | tf_op jit(solution)/shard_map/ppermute | solution.py:205
  24.2 1.3 %collective-permute-start.10 = (f32[128,256]{1,0:T(8,128)S(1)}, f32[128,256]{1,0:T(8,128)S(1)}, u32[]{:S(2)}, u32[]{:S(2)}) collective-permute-start(f32[128,256]{1,0:T(8,128)S(1)} %collective-permute-done.9.refs_2_), channel_id=1, source_target_pairs={{0,1},{1,0},{2,3},{3,2},{4,5},{5,4},{6,7},{7,6},{8,9},{9,8},{10,11... | collective-permute-start | bytes 393224 | tf_op jit(solution)/shard_map/ppermute | solution.py:205
  28.3 7.4 %collective-permute-start.15 = (f32[32,1024]{1,0:T(8,128)S(1)}, f32[32,1024]{1,0:T(8,128)S(1)}, u32[]{:S(2)}, u32[]{:S(2)}) collective-permute-start(f32[32,1024]{1,0:T(8,128)S(1)} %get-tuple-element.40), channel_id=1, source_target_pairs={{0,4},{4,0},{8,12},{12,8},{16,20},{20,16},{24,28},{28,24},{1,5},{5... | collective-permute-start | bytes 393224 | tf_op jit(solution)/shard_map/ppermute | solution.py:205
  29.4 13.8 %collective-permute-start.12 = (f32[32,1024]{1,0:T(8,128)S(1)}, f32[32,1024]{1,0:T(8,128)S(1)}, u32[]{:S(2)}, u32[]{:S(2)}) collective-permute-start(f32[32,1024]{1,0:T(8,128)S(1)} %get-tuple-element.36), channel_id=1, source_target_pairs={{0,16},{4,20},{8,24},{12,28},{16,0},{20,4},{24,8},{28,12},{1,17},{... | collective-permute-start | bytes 393224 | tf_op jit(solution)/shard_map/ppermute | solution.py:205
  31.2 16.5 %collective-permute-start.13 = (f32[32,1024]{1,0:T(8,128)S(1)}, f32[32,1024]{1,0:T(8,128)S(1)}, u32[]{:S(2)}, u32[]{:S(2)}) collective-permute-start(f32[32,1024]{1,0:T(8,128)S(1)} %get-tuple-element.37), channel_id=1, source_target_pairs={{0,20},{4,16},{8,28},{12,24},{16,4},{20,0},{24,12},{28,8},{1,21},{... | collective-permute-start | bytes 393224 | tf_op jit(solution)/shard_map/ppermute | solution.py:205
  32.7 19.7 %collective-permute-start.14 = (f32[32,1024]{1,0:T(8,128)S(1)}, f32[32,1024]{1,0:T(8,128)S(1)}, u32[]{:S(2)}, u32[]{:S(2)}) collective-permute-start(f32[32,1024]{1,0:T(8,128)S(1)} %get-tuple-element.38), channel_id=1, source_target_pairs={{0,24},{4,28},{8,16},{12,20},{16,8},{20,12},{24,0},{28,4},{1,25},{... | collective-permute-start | bytes 393224 | tf_op jit(solution)/shard_map/ppermute | solution.py:205
  33.9 18.6 %collective-permute-start.16 = (f32[32,1024]{1,0:T(8,128)S(1)}, f32[32,1024]{1,0:T(8,128)S(1)}, u32[]{:S(2)}, u32[]{:S(2)}) collective-permute-start(f32[32,1024]{1,0:T(8,128)S(1)} %get-tuple-element.42), channel_id=1, source_target_pairs={{0,8},{4,12},{8,0},{12,4},{16,24},{20,28},{24,16},{28,20},{1,9},{5... | collective-permute-start | bytes 393224 | tf_op jit(solution)/shard_map/ppermute | solution.py:205
  35.6 18.6 %collective-permute-start.17 = (f32[32,1024]{1,0:T(8,128)S(1)}, f32[32,1024]{1,0:T(8,128)S(1)}, u32[]{:S(2)}, u32[]{:S(2)}) collective-permute-start(f32[32,1024]{1,0:T(8,128)S(1)} %get-tuple-element.43), channel_id=1, source_target_pairs={{0,28},{4,24},{8,20},{12,16},{16,12},{20,8},{24,4},{28,0},{1,29},{... | collective-permute-start | bytes 393224 | tf_op jit(solution)/shard_map/ppermute | solution.py:205
  43.2 11.0 %collective-permute-start.18 = (f32[32,1024]{1,0:T(8,128)S(1)}, f32[32,1024]{1,0:T(8,128)S(1)}, u32[]{:S(2)}, u32[]{:S(2)}) collective-permute-start(f32[32,1024]{1,0:T(8,128)S(1)} %get-tuple-element.44), channel_id=1, source_target_pairs={{0,12},{4,8},{8,4},{12,0},{16,28},{20,24},{24,20},{28,16},{1,13},{... | collective-permute-start | bytes 393224 | tf_op jit(solution)/shard_map/ppermute | solution.py:205
